TPU v7x, 32 devices: a whole 2x2x4 slice. The times are simulated.
32 devices in a mesh: context: 16 (over z, y, core), tensor: 2 (over x).
Axes of the slice: x: 2, y: 2, z: 4, core: 2. Of those that a mesh axis runs over, the one named last changes fastest.
Arguments:
- hidden_rows: bfloat16 [2048, 4096], P(('context', 'tensor')), may hold values from -6 to 6
- norm_gain: bfloat16 [4096], replicated, may hold values from 0.25 to 1.75
- w_qkv: bfloat16 [4096, 1536], P('context', 'tensor')
- w_out: bfloat16 [1024, 4096], P('tensor', 'context'), may hold values from -0.1875 to 0.1875
- doc_lengths: int32 [16], replicated, may hold values from 1 to 512, 2048 in all
- span_order: int32 [32], replicated, may hold values from 0 to 31, each once
Outputs:
- attended: bfloat16 [2048, 4096], P(('context', 'tensor'))
Inputs may be any that keep to these rules, and one draw needn't show every extreme that they name: `doc_lengths`: the lengths sum to 2048; the longest is exactly 512. `span_order`: each initial span appears once.
All inputs are finite; a program needn't handle non-finite values.
Results may differ from a plain program's by a relative error of at most 0.02.
The roundings to bfloat16 on the way count: a program that leaves them out, or rounds other values in their place, can miss the bound.
Values may be sent and summed in bfloat16 or wider, within the bound.
No kernel may reach another device: no remote copies, remote signals or barrier semaphores. Data moves between devices by JAX's collectives and lax.ppermute only.
A program may use at most 64 MiB of HBM per device.

v0:
```python
import jax
import jax.numpy as jnp
from jax import lax
from jax.sharding import PartitionSpec as P

HD = 128
QH_DEV = 4
SPAN = 64


rope_theta = 500000.0


def locate(layout_rows, span_order, doc_ends):
    span_index = layout_rows // SPAN
    matches = span_index[:, None] == jnp.arange(span_order.shape[0], dtype=jnp.int32)[None, :]
    source_span = jnp.sum(jnp.where(matches, span_order[None, :], 0), axis=1)
    initial = source_span * SPAN + layout_rows % SPAN
    document = jnp.sum((initial[:, None] >= doc_ends[None, :]).astype(jnp.int32), axis=1)
    doc_start = jnp.max(
        jnp.where(doc_ends[None, :] <= initial[:, None], doc_ends[None, :], 0), axis=1
    )
    return (initial, document, initial - doc_start)


def rotate(values, position):
    half = values.shape[-1] // 2
    freq = rope_theta ** (-(jnp.arange(half, dtype=jnp.float32) * 2.0 / values.shape[-1]))
    angle = position.astype(jnp.float32)[:, None, None] * freq[None, None, :]
    cosine = jnp.cos(angle)
    sine = jnp.sin(angle)
    first_half = values[..., :half]
    second_half = values[..., half:]
    return jnp.concatenate(
        [first_half * cosine - second_half * sine, second_half * cosine + first_half * sine],
        axis=-1,
    )


def per_device(hidden_rows, norm_gain, w_qkv, w_out, doc_lengths, span_order):
    doc_ends = jnp.cumsum(doc_lengths)
    wide = hidden_rows.astype(jnp.float32)
    meansq = jnp.mean(wide * wide, axis=-1, keepdims=True)
    normed = (wide * lax.rsqrt(meansq + 1e-05) * norm_gain.astype(jnp.float32)[None, :]).astype(
        jnp.bfloat16
    )
    normed_all = lax.all_gather(normed, "tensor", axis=0, tiled=True)
    tokens_here = normed_all.shape[0]
    head_cols = QH_DEV * HD
    qkv = jnp.dot(
        normed_all,
        lax.all_gather(w_qkv, "context", axis=0, tiled=True),
        preferred_element_type=jnp.float32,
    )
    first_layout = lax.axis_index("context") * tokens_here
    query_rows = first_layout + jnp.arange(tokens_here, dtype=jnp.int32)
    query_orig, query_doc, query_pos = locate(query_rows, span_order, doc_ends)
    queries = rotate(qkv[:, :head_cols].reshape(tokens_here, QH_DEV, HD), query_pos).astype(
        jnp.bfloat16
    )
    keys = rotate(qkv[:, head_cols : head_cols + HD].reshape(tokens_here, 1, HD), query_pos)
    keys = keys.reshape(tokens_here, HD).astype(jnp.bfloat16)
    values = qkv[:, head_cols + HD :].astype(jnp.bfloat16)
    scale = 1.0 / HD**0.5
    key_block = lax.all_gather(keys, "context", axis=0, tiled=True)
    value_block = lax.all_gather(values, "context", axis=0, tiled=True)
    count = key_block.shape[0]
    key_rows = jnp.arange(count, dtype=jnp.int32)
    key_orig, key_doc, unused_pos = locate(key_rows, span_order, doc_ends)
    allowed = (key_doc[None, :] == query_doc[:, None]) & (key_orig[None, :] <= query_orig[:, None])
    top_old = jnp.full((tokens_here, QH_DEV), -1e30, jnp.float32)
    scores = (
        jnp.einsum("qhd,kd->qhk", queries, key_block, preferred_element_type=jnp.float32) * scale
    )
    scores = jnp.where(allowed[:, None, :], scores, -1e30)
    top_new = jnp.maximum(top_old, jnp.max(scores, axis=-1))
    expo = jnp.where(allowed[:, None, :], jnp.exp(scores - top_new[..., None]), 0.0)
    total_new = jnp.sum(expo, axis=-1)
    product = jnp.einsum(
        "qhk,kd->qhd", expo.astype(jnp.bfloat16), value_block, preferred_element_type=jnp.float32
    )
    mixed = (product / total_new[..., None]).astype(jnp.bfloat16).reshape(tokens_here, head_cols)
    partial_sums = jnp.dot(
        mixed,
        lax.all_gather(w_out, "context", axis=1, tiled=True),
        preferred_element_type=jnp.float32,
    )
    return lax.psum_scatter(
        partial_sums.astype(jnp.bfloat16), "tensor", scatter_dimension=0, tiled=True
    )


def solution(mesh):
    placed = (
        P(("context", "tensor"), None),
        P(),
        P("context", "tensor"),
        P("tensor", "context"),
        P(),
        P(),
    )
    return jax.shard_map(
        per_device,
        mesh=mesh,
        in_specs=placed,
        out_specs=P(("context", "tensor"), None),
        check_vma=False,
    )
```

profile of v0, /device:TPU:1, one launch (start us, length us, event | category | flops | bytes accessed | tf_op | source)
XLA Modules:
  0.0 186.8 jit_solution(13998784792903277921)
XLA Ops:
  6.5 0.7 convert_element_type.41
  7.2 1.2 fusion.12
  8.5 2.0 %fusion.14 = bf16[64,4096]{1,0:T(8,128)(2,1)} fusion(bf16[64,4096]{1,0:T(8,128)(2,1)} %param.6, f32[4096]{0:T(1024)S(1)} %convert_element_type.41, f32[64]{0:T(128)S(1)} %add_rsqrt_fusion), kind=kLoop, calls=%fused_computation.14 | loop fusion | flops 1048576 | bytes 1065216 | tf_op jit(solution)/shard_map/convert_element_type | solution.py:44
  10.6 0.7 all-gather.7.cloned.1.call-update
  11.4 0.7 all-gather.9.cloned.1.call-update
  12.1 0.7 copy.19
  12.9 0.1 reduce
  13.0 0.7 select_reduce_fusion.1
  13.9 0.8 select_reduce_fusion
  14.8 0.3 multiply_cosine_fusion
  15.1 0.3 compare_and_fusion
  15.4 18.7 %all-gather.5.cloned.1.call-done = bf16[128,4096]{1,0:T(8,128)(2,1)} async-done(((bf16[64,4096]{1,0:T(8,128)(2,1)}), bf16[128,4096]{1,0:T(8,128)(2,1)}) %all-gather.5.cloned.1.call-update) | async-done | bytes 1048592 | tf_op jit(solution)/shard_map/all_gather | solution.py:47
  34.1 64.6 %all-gather.7.cloned.1.call-done = bf16[4096,768]{1,0:T(8,128)(2,1)} async-done(((bf16[256,768]{1,0:T(8,128)(2,1)}), bf16[4096,768]{1,0:T(8,128)(2,1)}) %all-gather.7.cloned.1.call-update) | async-done | bytes 6291472 | tf_op jit(solution)/shard_map/all_gather | solution.py:52
  98.7 4.1 %fusion.43 = f32[128,768]{1,0:T(8,128)S(1)} fusion(bf16[128,4096]{1,0:T(8,128)(2,1)} %all-gather.5.cloned.1.call-done, bf16[4096,768]{1,0:T(8,128)(2,1)} %all-gather.7.cloned.1.call-done), kind=kOutput, calls=%fused_computation.73 | convolution fusion | flops 805306368 | bytes 7733248 | tf_op jit(solution)/shard_map/dot_general | solution.py:50
  103.0 0.2 fusion.26
  103.3 0.2 fusion.42
  103.5 21.4 %all-gather = bf16[2048,1,128]{0,2,1:T(8,128)(2,1)S(1)} all-gather(bf16[128,1,128]{0,2,1:T(8,128)(2,1)S(1)} %pad_maximum_fusion), channel_id=2, replica_groups=mesh['context'=16,'tensor'=2] {'context'}, dimensions={0}, use_global_device_ids=true | all-gather | bytes 557056 | tf_op jit(solution)/shard_map/all_gather | solution.py:65
  124.9 1.1 fusion
  126.0 20.0 %all_gather.18 = bf16[2048,128]{1,0:T(8,128)(2,1)S(1)} all-gather(bf16[128,128]{1,0:T(8,128)(2,1)S(1)} %slice.41), channel_id=1, replica_groups=mesh['context'=16,'tensor'=2] {'context'}, dimensions={0}, use_global_device_ids=true | all-gather | bytes 557056 | tf_op jit(solution)/shard_map/all_gather | solution.py:66
  146.0 1.3 fusion.1
  147.3 1.4 fusion.9
  148.7 8.4 %all-gather.9.cloned.1.call-done = bf16[512,4096]{1,0:T(8,128)(2,1)} async-done(((bf16[512,256]{1,0:T(8,128)(2,1)}), bf16[512,4096]{1,0:T(8,128)(2,1)}) %all-gather.9.cloned.1.call-update) | async-done | bytes 4194320 | tf_op jit(solution)/shard_map/all_gather | solution.py:85
  157.1 3.9 %convolution_convert_fusion = bf16[128,4096]{1,0:T(8,128)(2,1)} fusion(bf16[128,512]{0,1:T(8,128)(2,1)S(1)} %bitcast.18, bf16[512,4096]{1,0:T(8,128)(2,1)} %all-gather.9.cloned.1.call-done), kind=kOutput, calls=%fused_computation | convolution fusion | flops 537395200 | bytes 5373952 | tf_op jit(solution)/shard_map/dot_general | solution.py:83
  161.0 19.3 %reduce-scatter.2.cloned.1.call-done = bf16[64,4096]{1,0:T(8,128)(2,1)} async-done(((bf16[128,4096]{1,0:T(8,128)(2,1)}), bf16[64,4096]{1,0:T(8,128)(2,1)}) %reduce-scatter.2.cloned.1.call-update) | async-done | bytes 524304 | tf_op jit(solution)/shard_map/reduce_scatter | solution.py:88
  (24 shorter events, 0.7 us)
Async XLA Ops:
  6.5 27.6 %all-gather.5.cloned.1.call-start = ((), (), s32[]{:S(2)}) async-start(), calls=%async_computation.1 | async-start | bytes 1572864 | tf_op jit(solution)/shard_map/all_gather | solution.py:47
  10.6 88.1 %all-gather.7.cloned.1.call-start = ((), (), s32[]{:S(2)}) async-start(), calls=%async_computation.2 | async-start | bytes 6684672 | tf_op jit(solution)/shard_map/all_gather | solution.py:52
  11.3 145.8 %all-gather.9.cloned.1.call-start = ((), (), s32[]{:S(2)}) async-start(), calls=%async_computation.3 | async-start | bytes 4456448 | tf_op jit(solution)/shard_map/all_gather | solution.py:85
  12.0 168.3 %reduce-scatter.2.cloned.1.call-start = ((), (), s32[]{:S(2)}) async-start(), calls=%async_computation.4 | async-start | bytes 1572864 | tf_op jit(solution)/shard_map/reduce_scatter | solution.py:88
Sparse Core Ops, SparseCore 0:
  10.7 23.3 all-gather.4
  36.4 62.2 all-gather.6
  100.8 56.1 all-gather.8
  161.1 19.1 reduce-scatter.1
where the time goes:
time: 188 us; the launch traced here: 187 us
  waiting for transfers between devices  112 us (60%)
  blocking collectives  41.4 us (22%)
  between operations  13.3 us (7%)
  matrix products  10.5 us (6%)
  other arithmetic  8.03 us (4%)
    all_gather x1, waiting for transfers between devices, per_device(): lax.all_gather(w_qkv, 'context', axis=0, tiled=True)  64.6 us
    all_gather x1, blocking collectives, per_device(): key_block = lax.all_gather(keys, 'context', axis=0, tiled=True)  21.4 us
    all_gather x1, blocking collectives, per_device(): value_block = lax.all_gather(values, 'context', axis=0, tiled=True)  20 us
    reduce_scatter x1, waiting for transfers between devices, per_device(): lax.psum_scatter(partial_sums.astype(jnp.bfloat16), 'tensor', scatter_dim...  19.3 us
    all_gather x1, waiting for transfers between devices, per_device(): normed_all = lax.all_gather(normed, 'tensor', axis=0, tiled=True)  18.7 us
    all_gather x1, waiting for transfers between devices, per_device(): lax.all_gather(w_out, 'context', axis=1, tiled=True)  8.39 us
    dot_general x1, matrix products, per_device(): jnp.dot(normed_all, lax.all_gather(w_qkv, 'context', axis=0, tiled=True),...  4.1 us
    dot_general x1, matrix products, per_device(): jnp.dot(mixed, lax.all_gather(w_out, 'context', axis=1, tiled=True), pref...  3.92 us
  transfers between devices with their start and end apart: 4, of which 4 were waited for; matrix products, arithmetic and copies ran while one was open for 6% of the time, Pallas kernels for 0%

commit v1 on v0

v1 whole, which is shorter than its diff:
```python
import functools

import jax
import jax.numpy as jnp
from jax import lax
from jax.experimental import pallas as pl
from jax.experimental.pallas import tpu as pltpu
from jax.sharding import PartitionSpec as P

HD = 128
QH_DEV = 4
SPAN = 64
HEAD_COLS = QH_DEV * HD
VMEM_LIMIT = 48 * 1024 * 1024

rope_theta = 500000.0


def ring_of_chips(count):
    wide = 1
    while (wide * 2) * (wide * 2) <= count:
        wide *= 2
    tall = count // wide
    if wide < 2:
        return list(range(count))
    ring = [(z, 0) for z in range(tall)]
    for z in range(tall - 1, -1, -1):
        row = list(range(1, wide))
        ring += [(z, y) for y in (row if (tall - 1 - z) % 2 == 0 else row[::-1])]
    if (tall - 1) % 2 == 0 or wide == 2:
        return [z * wide + y for z, y in ring]
    return [z * wide + y for z, y in ring]


def locate(layout_rows, span_order, doc_ends):
    span_index = layout_rows // SPAN
    matches = span_index[:, None] == jnp.arange(span_order.shape[0], dtype=jnp.int32)[None, :]
    source_span = jnp.sum(jnp.where(matches, span_order[None, :], 0), axis=1)
    initial = source_span * SPAN + layout_rows % SPAN
    doc_start = jnp.max(
        jnp.where(doc_ends[None, :] <= initial[:, None], doc_ends[None, :], 0), axis=1
    )
    return (initial, doc_start)


def vmem_specs(count):
    return [pl.BlockSpec(memory_space=pltpu.VMEM)] * count


def compute_params():
    return pltpu.CompilerParams(vmem_limit_bytes=VMEM_LIMIT)


def norm_kernel(place, chips, where_ref, hidden_ref, gain_ref, own_ref, other_ref):
    at, core = where_ref[0], where_ref[1]
    wide = hidden_ref[...].astype(jnp.float32)
    meansq = jnp.mean(wide * wide, axis=-1, keepdims=True)
    normed = (wide * lax.rsqrt(meansq + 1e-05) * gain_ref[...].astype(jnp.float32)).astype(
        jnp.bfloat16
    )
    block = own_ref.shape[2]
    for chip in range(chips):
        slot = lax.rem(place[chip] + chips - at, chips)
        first = normed[:, (2 * chip) * block : (2 * chip + 1) * block]
        second = normed[:, (2 * chip + 1) * block : (2 * chip + 2) * block]

        @pl.when(core == 0)
        def _():
            own_ref[slot] = first
            other_ref[slot] = second

        @pl.when(core != 0)
        def _():
            own_ref[slot] = second
            other_ref[slot] = first


def take_ring(refs, chips):
    refs = list(refs)
    if chips % 2:
        return [(ref,) for ref in refs]
    half = chips // 2
    return [(r,) for r in refs[:half]] + [tuple(refs[half : half + 2])] + [
        (r,) for r in refs[half + 2 :]
    ]


def project_kernel(chips, groups, *refs):
    rows_refs, refs = refs[:groups], refs[groups:]
    weight_refs, (mine_ref, theirs_ref) = refs[:-2], refs[-2:]
    weights = take_ring(weight_refs, chips)
    total = None
    for slot in range(chips):
        rows = jnp.concatenate([ref[slot] for ref in rows_refs], axis=0)
        start = 0
        for ref in weights[slot]:
            depth = ref.shape[0]
            part = jnp.dot(
                rows[:, start : start + depth], ref[...], preferred_element_type=jnp.float32
            )
            total = part if total is None else total + part
            start += depth
    half = mine_ref.shape[0]
    mine_ref[...] = total[:half]
    theirs_ref[...] = total[half:]


def turn(values, cosine, sine):
    return values * cosine + pltpu.roll(values, HD // 2, 1) * sine


def keys_kernel(mine_ref, theirs_ref, cosine_ref, sine_ref, out_ref):
    total = mine_ref[...] + theirs_ref[...]
    out_ref[:, :HD] = turn(total[:, :HD], cosine_ref[...], sine_ref[...]).astype(jnp.bfloat16)
    out_ref[:, HD:] = total[:, HD:].astype(jnp.bfloat16)


def attend_kernel(mine_ref, theirs_ref, cosine_ref, sine_ref, low_ref, high_ref, orig_ref, *refs):
    block_refs, (out_ref, keys_ref, values_ref) = refs[:-3], refs[-3:]
    start = 0
    for ref in block_refs:
        keys_ref[start : start + ref.shape[0], :] = ref[:, :HD]
        values_ref[start : start + ref.shape[0], :] = ref[:, HD:]
        start += ref.shape[0]
    keys = keys_ref[...]
    values = values_ref[...]
    orig = orig_ref[...]
    allowed = (orig >= low_ref[...]) & (orig <= high_ref[...])
    scale = 1.0 / HD**0.5
    for head in range(QH_DEV):
        columns = slice(head * HD, (head + 1) * HD)
        query = turn(
            mine_ref[:, columns] + theirs_ref[:, columns], cosine_ref[...], sine_ref[...]
        ).astype(jnp.bfloat16)
        scores = lax.dot_general(
            query, keys, (((1,), (1,)), ((), ())), preferred_element_type=jnp.float32
        )
        scores = jnp.where(allowed, scores * scale, -1e30)
        top = jnp.max(scores, axis=-1, keepdims=True)
        expo = jnp.where(allowed, jnp.exp(scores - top), 0.0)
        total = jnp.sum(expo, axis=-1, keepdims=True)
        product = jnp.dot(expo.astype(jnp.bfloat16), values, preferred_element_type=jnp.float32)
        out_ref[:, columns] = (product / total).astype(jnp.bfloat16)


def output_kernel(chips, groups, mine_ref, theirs_ref, *refs):
    weight_refs, out_refs = refs[:-groups], refs[-groups:]
    weights = take_ring(weight_refs, chips)
    mixed = jnp.concatenate([mine_ref[...], theirs_ref[...]], axis=0)
    rows = mixed.shape[0] // groups
    for slot in range(chips):
        start, total = 0, None
        for ref in weights[slot]:
            depth = ref.shape[0]
            part = jnp.dot(
                mixed[:, start : start + depth], ref[...], preferred_element_type=jnp.float32
            )
            total = part if total is None else total + part
            start += depth
        total = total.astype(jnp.bfloat16)
        for group in range(groups):
            out_refs[group][slot] = total[group * rows : (group + 1) * rows]


def sum_kernel(place, chips, groups, where_ref, *refs):
    part_refs, out_ref = refs[:groups], refs[groups]
    at, core = where_ref[0], where_ref[1]
    block = part_refs[0].shape[2]
    half = groups // 2

    def added(part, slot):
        total = part_refs[part * half][slot].astype(jnp.float32)
        for ref in part_refs[part * half + 1 : (part + 1) * half]:
            total += ref[slot].astype(jnp.float32)
        return total.astype(jnp.bfloat16)

    for chip in range(chips):
        slot = lax.rem(place[chip] + chips - at, chips)
        first = slice((2 * chip) * block, (2 * chip + 1) * block)
        second = slice((2 * chip + 1) * block, (2 * chip + 2) * block)

        @pl.when(core == 0)
        def _():
            out_ref[:, first] = added(0, slot)
            out_ref[:, second] = added(1, slot)

        @pl.when(core != 0)
        def _():
            out_ref[:, first] = added(1, slot)
            out_ref[:, second] = added(0, slot)


def per_device(n_context, n_tensor, hidden_rows, norm_gain, w_qkv, w_out, doc_lengths, span_order):
    chips = n_context // 2
    ring = ring_of_chips(chips)
    place = [ring.index(chip) for chip in range(chips)]
    groups = 2 * n_tensor
    rows_here, width = hidden_rows.shape
    tokens_here = rows_here * n_tensor
    block = width // n_context
    context = lax.axis_index("context")
    tensor = lax.axis_index("tensor")
    core = context % 2
    at = jnp.sum(
        jnp.where(jnp.arange(chips) == context // 2, jnp.asarray(place, jnp.int32), 0)
    ).astype(jnp.int32)
    where = jnp.stack([at, core]).astype(jnp.int32)

    ahead = [
        (ring[i] * 2 + k, ring[(i + 1) % chips] * 2 + k) for i in range(chips) for k in range(2)
    ]
    back = [(b, a) for a, b in ahead]
    sibling = [(c, c ^ 1) for c in range(n_context)]

    def ring_gather(mine):
        up, down = mine, mine
        behind, before = [], []
        for _ in range((chips - 1) // 2):
            up = lax.ppermute(up, "context", ahead)
            down = lax.ppermute(down, "context", back)
            behind.append(up)
            before.append(down)
        middle = []
        if chips % 2 == 0:
            half = mine.shape[0] // 2
            middle = [
                lax.ppermute(up[:half], "context", ahead),
                lax.ppermute(down[half:], "context", back),
            ]
        return [mine] + before + middle + behind[::-1]

    def member(e, d):
        return [
            (c * n_tensor + t, (c ^ e) * n_tensor + (t - d) % n_tensor)
            for c in range(n_context)
            for t in range(n_tensor)
        ]

    keys_blocks = ring_gather(w_qkv[:, HEAD_COLS:])
    query_blocks = ring_gather(w_qkv[:, :HEAD_COLS])
    out_blocks = ring_gather(w_out)

    smem = pl.BlockSpec(memory_space=pltpu.SMEM)
    normed_shape = jax.ShapeDtypeStruct((chips, rows_here, block), jnp.bfloat16)
    normed_own, normed_other = pl.pallas_call(
        functools.partial(norm_kernel, place, chips),
        out_shape=[normed_shape] * 2,
        in_specs=[smem] + vmem_specs(2),
        out_specs=vmem_specs(2),
        compiler_params=compute_params(),
        name="norm",
    )(where, hidden_rows, norm_gain[None, :])
    normed = []
    for e in range(2):
        for d in range(n_tensor):
            rows = normed_own if e == 0 else normed_other
            if e or d:
                rows = lax.ppermute(rows, ("context", "tensor"), member(e, d))
            normed.append(rows)

    def project(blocks, name):
        columns = blocks[0].shape[1]
        mine, theirs = pl.pallas_call(
            functools.partial(project_kernel, chips, groups),
            out_shape=[jax.ShapeDtypeStruct((tokens_here, columns), jnp.float32)] * 2,
            in_specs=vmem_specs(groups + len(blocks)),
            out_specs=vmem_specs(2),
            compiler_params=compute_params(),
            name=name,
        )(*normed, *blocks)
        return mine, lax.ppermute(theirs, "context", sibling)

    doc_ends = jnp.cumsum(doc_lengths)
    inside = (
        (tensor + jnp.arange(n_tensor, dtype=jnp.int32)) % n_tensor * rows_here
    )[:, None] + jnp.arange(rows_here, dtype=jnp.int32)[None, :]
    inside = inside.reshape(-1)
    query_orig, query_start = locate(context * tokens_here + inside, span_order, doc_ends)
    half = HD // 2
    freq = rope_theta ** (-(jnp.arange(half, dtype=jnp.float32) * 2.0 / HD))
    angle = (query_orig - query_start).astype(jnp.float32)[:, None] * freq[None, :]
    cosine, sine = jnp.cos(angle), jnp.sin(angle)
    cosine = jnp.concatenate([cosine, cosine], axis=1)
    sine = jnp.concatenate([-sine, sine], axis=1)
    chip_of_slot = jnp.sum(
        jnp.where(
            ((jnp.arange(chips) + at) % chips)[:, None] == jnp.arange(chips)[None, :],
            jnp.asarray(ring, jnp.int32)[None, :],
            0,
        ),
        axis=1,
    ).astype(jnp.int32)
    owner = jnp.concatenate([chip_of_slot * 2 + core, chip_of_slot * 2 + (1 - core)])
    key_rows = (owner[:, None] * tokens_here + inside[None, :]).reshape(-1).astype(jnp.int32)
    key_orig, _ = locate(key_rows, span_order, doc_ends)

    mine, theirs = project(keys_blocks, "project_keys")
    kv = pl.pallas_call(
        keys_kernel,
        out_shape=jax.ShapeDtypeStruct((tokens_here, 2 * HD), jnp.bfloat16),
        in_specs=vmem_specs(4),
        out_specs=vmem_specs(1)[0],
        compiler_params=compute_params(),
        name="keys",
    )(mine, theirs, cosine, sine)
    kv_blocks = ring_gather(kv)
    kv_blocks = kv_blocks + [lax.ppermute(b, "context", sibling) for b in kv_blocks]

    mine, theirs = project(query_blocks, "project_queries")
    count = n_context * tokens_here
    mixed = pl.pallas_call(
        attend_kernel,
        out_shape=jax.ShapeDtypeStruct((tokens_here, HEAD_COLS), jnp.bfloat16),
        in_specs=vmem_specs(7 + len(kv_blocks)),
        out_specs=vmem_specs(1)[0],
        scratch_shapes=[pltpu.VMEM((count, HD), jnp.bfloat16)] * 2,
        compiler_params=compute_params(),
        name="attend",
    )(
        mine,
        theirs,
        cosine,
        sine,
        query_start[:, None],
        query_orig[:, None],
        key_orig[None, :],
        *kv_blocks,
    )
    mixed_theirs = lax.ppermute(mixed, "context", sibling)

    out_block = w_out.shape[1]
    parts = pl.pallas_call(
        functools.partial(output_kernel, chips, groups),
        out_shape=[jax.ShapeDtypeStruct((chips, rows_here, out_block), jnp.bfloat16)] * groups,
        in_specs=vmem_specs(2 + len(out_blocks)),
        out_specs=vmem_specs(groups),
        compiler_params=compute_params(),
        name="output",
    )(mixed, mixed_theirs, *out_blocks)
    arrived = []
    for e in range(2):
        for d in range(n_tensor):
            part = parts[e * n_tensor + d]
            if e or d:
                part = lax.ppermute(part, ("context", "tensor"), member(e, -d))
            arrived.append(part)
    return pl.pallas_call(
        functools.partial(sum_kernel, place, chips, groups),
        out_shape=jax.ShapeDtypeStruct((rows_here, n_context * out_block), jnp.bfloat16),
        in_specs=[smem] + vmem_specs(groups),
        out_specs=vmem_specs(1)[0],
        compiler_params=compute_params(),
        name="sum",
    )(where, *arrived)


def solution(mesh):
    placed = (
        P(("context", "tensor"), None),
        P(),
        P("context", "tensor"),
        P("tensor", "context"),
        P(),
        P(),
    )
    return jax.shard_map(
        functools.partial(per_device, mesh.shape["context"], mesh.shape["tensor"]),
        mesh=mesh,
        in_specs=placed,
        out_specs=P(("context", "tensor"), None),
        check_vma=False,
    )
```

time: 188 us -> 114 us (0.61)
  waiting for transfers between devices: 112 us -> 42.7 us
  starting transfers between devices: 0.12 us -> 50.3 us
  blocking collectives: 41.4 us -> 0 us
  between operations: 13.3 us -> 0.52 us
  matrix products: 10.5 us -> 0 us
  Pallas kernels: 0 us -> 7.85 us
  local copies, waits for them, and re-layouts: 1.15 us -> 8.54 us
  other arithmetic: 8.03 us -> 3.89 us
    all_gather x3 -> x0, waiting for transfers between devices: 91.7 us -> none  [the longest x1 64.6 us: per_device(): lax.all_gather(w_qkv, 'context', axis=0, tiled=True)]
    ppermute x0 -> x50, starting transfers between devices: none -> 50.3 us  [the longest x12 14.4 us: ring_gather(): down = lax.ppermute(down, 'context', back)]
    ppermute x0 -> x50, waiting for transfers between devices: none -> 42.7 us  [the longest x12 18 us: ring_gather(): down = lax.ppermute(down, 'context', back)]
    all_gather x2 -> x0, blocking collectives: 41.4 us -> none  [the longest x1 21.4 us: per_device(): key_block = lax.all_gather(keys, 'context', axis=0, tiled=True)]
    reduce_scatter x1 -> x0, waiting for transfers between devices: 19.3 us -> none  [per_device(): lax.psum_scatter(partial_sums.astype(jnp.bfloat16), 'tensor', scatter_dim...]
    dot_general x4 -> x0, matrix products: 10.5 us -> none  [the longest x1 4.1 us: per_device(): jnp.dot(normed_all, lax.all_gather(w_qkv, 'context', axis=0, tiled=True),...]
    pallas_call x0 -> x7, Pallas kernels: none -> 7.85 us  [the longest x1 2.74 us: per_device(): pl.pallas_call(attend_kernel, out_shape=jax.ShapeDtypeStruct((tokens_here...]
    unnamed x1 -> x76, local copies, waits for them, and re-layouts: 0.09 us -> 6.7 us
  transfers between devices with their start and end apart: 4 -> 50, of which waited for: 4 -> 13; matrix products, arithmetic and copies ran while one was open for 6% -> 4% of each run, Pallas kernels for 0% -> 4%
where the time goes in v1:
time: 114 us
  starting transfers between devices  50.3 us (44%)
  waiting for transfers between devices  42.7 us (37%)
  local copies, waits for them, and re-layouts  8.54 us (7%)
  Pallas kernels  7.85 us (7%)
  other arithmetic  3.89 us (3%)
    ppermute x12, waiting for transfers between devices, ring_gather(): down = lax.ppermute(down, 'context', back)  18 us
    ppermute x12, starting transfers between devices, ring_gather(): down = lax.ppermute(down, 'context', back)  14.4 us
    ppermute x9, starting transfers between devices, per_device(): lax.ppermute(b, 'context', sibling)  10.9 us
    ppermute x3, waiting for transfers between devices, per_device(): part = lax.ppermute(part, ('context', 'tensor'), member(e, -d))  10.8 us
    ppermute x12, waiting for transfers between devices, ring_gather(): up = lax.ppermute(up, 'context', ahead)  7.99 us
    unnamed x76, local copies, waits for them, and re-layouts  6.7 us
    ppermute x2, starting transfers between devices, project(): return (mine, lax.ppermute(theirs, 'context', sibling))  6.57 us
    ppermute x12, starting transfers between devices, ring_gather(): up = lax.ppermute(up, 'context', ahead)  5.32 us
  transfers between devices with their start and end apart: 50, of which 13 were waited for; matrix products, arithmetic and copies ran while one was open for 4% of the time, Pallas kernels for 4%

profile of v1, /device:TPU:1, one launch (start us, length us, event | category | flops | bytes accessed | tf_op | source)
XLA Modules:
  0.0 113.8 jit_solution(10724760210887133122)
XLA Ops:
  4.7 2.6 %collective-permute-start.2 = (bf16[8,64,256]{2,1,0:T(8,128)(2,1)S(1)}, bf16[8,64,256]{2,1,0:T(8,128)(2,1)S(1)}, u32[]{:S(2)}, u32[]{:S(2)}) collective-permute-start(bf16[8,64,256]{2,1,0:T(8,128)(2,1)S(1)} %get-tuple-element.16), channel_id=1, source_target_pairs={{0,3},{1,2},{2,1},{3,0},{4,7},{5,6},{6,5},{7,4},{8,11},{9,10},{10,... | collective-permute-start | bytes 786440 | tf_op jit(solution)/shard_map/ppermute | solution.py:258
  13.8 6.6 %collective-permute-done.13.refs_6_ = bf16[256,256]{1,0:T(8,128)(2,1)S(1)} collective-permute-done((bf16[256,256]{1,0:T(8,128)(2,1)S(1)}, bf16[256,256]{1,0:T(8,128)(2,1)S(1)}, u32[]{:S(2)}, u32[]{:S(2)}) %collective-permute-start.13) | collective-permute-done | bytes 131104 | tf_op jit(solution)/shard_map/ppermute | solution.py:220
  21.9 2.3 %collective-permute-done.14.refs_7_ = bf16[256,256]{1,0:T(8,128)(2,1)S(1)} collective-permute-done((bf16[256,256]{1,0:T(8,128)(2,1)S(1)}, bf16[256,256]{1,0:T(8,128)(2,1)S(1)}, u32[]{:S(2)}, u32[]{:S(2)}) %collective-permute-start.14) | collective-permute-done | bytes 131104 | tf_op jit(solution)/shard_map/ppermute | solution.py:220
  27.6 3.7 %collective-permute-done.refs_1_ = bf16[8,64,256]{2,1,0:T(8,128)(2,1)S(1)} collective-permute-done((bf16[8,64,256]{2,1,0:T(8,128)(2,1)S(1)}, bf16[8,64,256]{2,1,0:T(8,128)(2,1)S(1)}, u32[]{:S(2)}, u32[]{:S(2)}) %collective-permute-start) | collective-permute-done | bytes 262176 | tf_op jit(solution)/shard_map/ppermute | solution.py:258
  36.4 5.9 %collective-permute-start.20 = (f32[128,256]{1,0:T(8,128)S(1)}, f32[128,256]{1,0:T(8,128)S(1)}, u32[]{:S(2)}, u32[]{:S(2)}) collective-permute-start(f32[128,256]{1,0:T(8,128)S(1)} %get-tuple-element.20), channel_id=1, source_target_pairs={{0,2},{2,0},{4,6},{6,4},{8,10},{10,8},{12,14},{14,12},{16,18},{18,... | collective-permute-start | bytes 393224 | tf_op jit(solution)/shard_map/ppermute | solution.py:271
  43.5 1.4 %collective-permute-start.21 = (bf16[128,256]{1,0:T(8,128)(2,1)S(1)}, bf16[128,256]{1,0:T(8,128)(2,1)S(1)}, u32[]{:S(2)}, u32[]{:S(2)}) collective-permute-start(bf16[128,256]{1,0:T(8,128)(2,1)S(1)} %keys.1.refs_0_), channel_id=1, source_target_pairs={{8,0},{10,2},{16,8},{18,10},{24,16},{26,18},{28,24},{30,26},{20,28... | collective-permute-start | bytes 196616 | tf_op jit(solution)/shard_map/ppermute | solution.py:220
  49.3 4.5 %collective-permute-done.24.refs_8_ = bf16[128,256]{1,0:T(8,128)(2,1)S(1)} collective-permute-done((bf16[128,256]{1,0:T(8,128)(2,1)S(1)}, bf16[128,256]{1,0:T(8,128)(2,1)S(1)}, u32[]{:S(2)}, u32[]{:S(2)}) %collective-permute-start.24) | collective-permute-done | bytes 65568 | tf_op jit(solution)/shard_map/ppermute | solution.py:219
  54.0 6.4 %collective-permute-done.22.refs_2_ = bf16[128,256]{1,0:T(8,128)(2,1)S(1)} collective-permute-done((bf16[128,256]{1,0:T(8,128)(2,1)S(1)}, bf16[128,256]{1,0:T(8,128)(2,1)S(1)}, u32[]{:S(2)}, u32[]{:S(2)}) %collective-permute-start.22) | collective-permute-done | bytes 65568 | tf_op jit(solution)/shard_map/ppermute | solution.py:220
  61.1 3.2 %collective-permute-done.25.refs_7_ = bf16[128,256]{1,0:T(8,128)(2,1)S(1)} collective-permute-done((bf16[128,256]{1,0:T(8,128)(2,1)S(1)}, bf16[128,256]{1,0:T(8,128)(2,1)S(1)}, u32[]{:S(2)}, u32[]{:S(2)}) %collective-permute-start.25) | collective-permute-done | bytes 65568 | tf_op jit(solution)/shard_map/ppermute | solution.py:219
  64.4 1.4 %collective-permute-start.23 = (bf16[128,256]{1,0:T(8,128)(2,1)S(1)}, bf16[128,256]{1,0:T(8,128)(2,1)S(1)}, u32[]{:S(2)}, u32[]{:S(2)}) collective-permute-start(bf16[128,256]{1,0:T(8,128)(2,1)S(1)} %collective-permute-done.22.refs_2_), channel_id=1, source_target_pairs={{8,0},{10,2},{16,8},{18,10},{24,16},{26,18},{28,24},{30,26},{20,28... | collective-permute-start | bytes 196616 | tf_op jit(solution)/shard_map/ppermute | solution.py:220
  67.5 4.1 %collective-permute-start.29 = (bf16[128,256]{1,0:T(8,128)(2,1)S(1)}, bf16[128,256]{1,0:T(8,128)(2,1)S(1)}, u32[]{:S(2)}, u32[]{:S(2)}) collective-permute-start(bf16[128,256]{1,0:T(8,128)(2,1)S(1)} %keys.1.refs_0_), channel_id=1, source_target_pairs={{0,2},{2,0},{4,6},{6,4},{8,10},{10,8},{12,14},{14,12},{16,18},{18,... | collective-permute-start | bytes 196616 | tf_op jit(solution)/shard_map/ppermute | solution.py:307
  71.7 1.9 %collective-permute-start.37 = (bf16[128,256]{1,0:T(8,128)(2,1)S(1)}, bf16[128,256]{1,0:T(8,128)(2,1)S(1)}, u32[]{:S(2)}, u32[]{:S(2)}) collective-permute-start(bf16[128,256]{1,0:T(8,128)(2,1)S(1)} %collective-permute-done.24.refs_8_), channel_id=1, source_target_pairs={{0,2},{2,0},{4,6},{6,4},{8,10},{10,8},{12,14},{14,12},{16,18},{18,... | collective-permute-start | bytes 196616 | tf_op jit(solution)/shard_map/ppermute | solution.py:307
  73.6 1.4 %collective-permute-start.31 = (bf16[128,256]{1,0:T(8,128)(2,1)S(1)}, bf16[128,256]{1,0:T(8,128)(2,1)S(1)}, u32[]{:S(2)}, u32[]{:S(2)}) collective-permute-start(bf16[128,256]{1,0:T(8,128)(2,1)S(1)} %collective-permute-done.22.refs_2_), channel_id=1, source_target_pairs={{0,2},{2,0},{4,6},{6,4},{8,10},{10,8},{12,14},{14,12},{16,18},{18,... | collective-permute-start | bytes 196616 | tf_op jit(solution)/shard_map/ppermute | solution.py:307
  75.0 1.6 %collective-permute-start.36 = (bf16[128,256]{1,0:T(8,128)(2,1)S(1)}, bf16[128,256]{1,0:T(8,128)(2,1)S(1)}, u32[]{:S(2)}, u32[]{:S(2)}) collective-permute-start(bf16[128,256]{1,0:T(8,128)(2,1)S(1)} %collective-permute-done.25.refs_7_), channel_id=1, source_target_pairs={{0,2},{2,0},{4,6},{6,4},{8,10},{10,8},{12,14},{14,12},{16,18},{18,... | collective-permute-start | bytes 196616 | tf_op jit(solution)/shard_map/ppermute | solution.py:307
  77.9 1.5 %project_queries.1 = (f32[128,512]{1,0:T(8,128)S(1)}, f32[128,512]{1,0:T(8,128)}) custom-call(bf16[8,64,256]{2,1,0:T(8,128)(2,1)S(1)} %get-tuple-element.15.refs_0_, bf16[8,64,256]{2,1,0:T(8,128)(2,1)S(1)} %collective-permute-done.refs_1_, bf16[8,64,256]{2,1,0:T(8,128)(2,1)S(1)} %collective-permute-done.1.refs_2_, ...), custom_call_target="tpu_custom_call" | custom-call | tf_op jit(solution)/shard_map/project_queries/pallas_call | solution.py:263
  80.6 1.7 %collective-permute-start.44 = (bf16[512,256]{1,0:T(8,128)(2,1)S(1)}, bf16[512,256]{1,0:T(8,128)(2,1)S(1)}, u32[]{:S(2)}, u32[]{:S(2)}) collective-permute-start(bf16[512,256]{1,0:T(8,128)(2,1)S(1)} %collective-permute-done.43.refs_7_), channel_id=1, source_target_pairs={{0,8},{2,10},{8,16},{10,18},{16,24},{18,26},{24,28},{26,30},{28,20... | collective-permute-start | bytes 786440 | tf_op jit(solution)/shard_map/ppermute | solution.py:219
  83.0 1.7 %collective-permute-start.27 = (bf16[64,256]{1,0:T(8,128)(2,1)}, bf16[64,256]{1,0:T(8,128)(2,1)S(1)}, u32[]{:S(2)}, u32[]{:S(2)}) collective-permute-start(bf16[64,256]{1,0:T(8,128)(2,1)} %slice.44), channel_id=1, source_target_pairs={{0,8},{2,10},{8,16},{10,18},{16,24},{18,26},{24,28},{26,30},{28,20... | collective-permute-start | bytes 98312 | tf_op jit(solution)/shard_map/ppermute | solution.py:227
  86.8 1.5 %collective-permute-done.41.refs_3_ = bf16[512,256]{1,0:T(8,128)(2,1)S(1)} collective-permute-done((bf16[512,256]{1,0:T(8,128)(2,1)S(1)}, bf16[512,256]{1,0:T(8,128)(2,1)S(1)}, u32[]{:S(2)}, u32[]{:S(2)}) %collective-permute-start.41) | collective-permute-done | bytes 262176 | tf_op jit(solution)/shard_map/ppermute | solution.py:220
  91.1 1.8 %collective-permute-start.45 = (bf16[256,256]{1,0:T(8,128)(2,1)S(1)}, bf16[256,256]{1,0:T(8,128)(2,1)S(1)}, u32[]{:S(2)}, u32[]{:S(2)}) collective-permute-start(bf16[256,256]{1,0:T(8,128)(2,1)S(1)} %slice.46), channel_id=1, source_target_pairs={{0,8},{2,10},{8,16},{10,18},{16,24},{18,26},{24,28},{26,30},{28,20... | collective-permute-start | bytes 393224 | tf_op jit(solution)/shard_map/ppermute | solution.py:227
  93.0 2.7 %attend.1.mine_ref = bf16[128,512]{1,0:T(8,128)(2,1)S(1)} custom-call(f32[128,512]{1,0:T(8,128)S(1)} %get-tuple-element.17.mine_ref, f32[128,512]{1,0:T(8,128)S(1)} %collective-permute-done.11.theirs_ref, f32[128,128]{1,0:T(8,128)S(1)} %get-tuple-element.34.cosine_ref, f32[128,128]{1,0:T(8,128)S(1)} %get-tuple-element.35.sine_ref, ...), custom_call_target="tpu_custom_call" | custom-call | tf_op jit(solution)/shard_map/attend/pallas_call | solution.py:311
  98.9 1.5 %collective-permute-start.48 = (bf16[8,64,256]{2,1,0:T(8,128)(2,1)S(1)}, bf16[8,64,256]{2,1,0:T(8,128)(2,1)S(1)}, u32[]{:S(2)}, u32[]{:S(2)}) collective-permute-start(bf16[8,64,256]{2,1,0:T(8,128)(2,1)S(1)} %get-tuple-element.23), channel_id=1, source_target_pairs={{0,2},{1,3},{2,0},{3,1},{4,6},{5,7},{6,4},{7,5},{8,10},{9,11},{10,... | collective-permute-start | bytes 786440 | tf_op jit(solution)/shard_map/ppermute | solution.py:345
  101.5 3.7 %collective-permute-done.47.refs_1_ = bf16[8,64,256]{2,1,0:T(8,128)(2,1)S(1)} collective-permute-done((bf16[8,64,256]{2,1,0:T(8,128)(2,1)S(1)}, bf16[8,64,256]{2,1,0:T(8,128)(2,1)S(1)}, u32[]{:S(2)}, u32[]{:S(2)}) %collective-permute-start.47) | collective-permute-done | bytes 262176 | tf_op jit(solution)/shard_map/ppermute | solution.py:345
  105.2 7.1 %collective-permute-done.49.refs_3_ = bf16[8,64,256]{2,1,0:T(8,128)(2,1)S(1)} collective-permute-done((bf16[8,64,256]{2,1,0:T(8,128)(2,1)S(1)}, bf16[8,64,256]{2,1,0:T(8,128)(2,1)S(1)}, u32[]{:S(2)}, u32[]{:S(2)}) %collective-permute-start.49) | collective-permute-done | bytes 262176 | tf_op jit(solution)/shard_map/ppermute | solution.py:345
  112.2 1.5 %sum.1 = bf16[64,4096]{1,0:T(8,128)(2,1)} custom-call(s32[2]{0:T(128)S(1)} %pad_add_fusion.where_ref, bf16[8,64,256]{2,1,0:T(8,128)(2,1)S(1)} %get-tuple-element.21.refs_0_, bf16[8,64,256]{2,1,0:T(8,128)(2,1)S(1)} %collective-permute-done.47.refs_1_, bf16[8,64,256]{2,1,0:T(8,128)(2,1)S(1)} %collective-permute-done.48.refs_2_, ...), custom_call_target="tpu_custom_call" | custom-call | tf_op jit(solution)/shard_map/sum/pallas_call | solution.py:347
  (199 shorter events, 41.4 us)
Async XLA Ops:
  4.5 27.8 %collective-permute-start.1 = (bf16[8,64,256]{2,1,0:T(8,128)(2,1)S(1)}, bf16[8,64,256]{2,1,0:T(8,128)(2,1)S(1)}, u32[]{:S(2)}, u32[]{:S(2)}) collective-permute-start(bf16[8,64,256]{2,1,0:T(8,128)(2,1)S(1)} %get-tuple-element.16), channel_id=1, source_target_pairs={{0,2},{1,3},{2,0},{3,1},{4,6},{5,7},{6,4},{7,5},{8,10},{9,11},{10,... | collective-permute-start | bytes 786440 | tf_op jit(solution)/shard_map/ppermute | solution.py:258
  4.7 28.3 %collective-permute-start.2 = (bf16[8,64,256]{2,1,0:T(8,128)(2,1)S(1)}, bf16[8,64,256]{2,1,0:T(8,128)(2,1)S(1)}, u32[]{:S(2)}, u32[]{:S(2)}) collective-permute-start(bf16[8,64,256]{2,1,0:T(8,128)(2,1)S(1)} %get-tuple-element.16), channel_id=1, source_target_pairs={{0,3},{1,2},{2,1},{3,0},{4,7},{5,6},{6,5},{7,4},{8,11},{9,10},{10,... | collective-permute-start | bytes 786440 | tf_op jit(solution)/shard_map/ppermute | solution.py:258
  8.8 25.5 %collective-permute-start.3 = (bf16[256,512]{1,0:T(8,128)(2,1)S(1)}, bf16[256,512]{1,0:T(8,128)(2,1)S(1)}, u32[]{:S(2)}, u32[]{:S(2)}) collective-permute-start(bf16[256,512]{1,0:T(8,128)(2,1)S(1)} %slice.30.refs_4_), channel_id=1, source_target_pairs={{8,0},{10,2},{16,8},{18,10},{24,16},{26,18},{28,24},{30,26},{20,28... | collective-permute-start | bytes 786440 | tf_op jit(solution)/shard_map/ppermute | solution.py:220
  12.0 8.4 %collective-permute-start.13 = (bf16[256,256]{1,0:T(8,128)(2,1)S(1)}, bf16[256,256]{1,0:T(8,128)(2,1)S(1)}, u32[]{:S(2)}, u32[]{:S(2)}) collective-permute-start(bf16[256,256]{1,0:T(8,128)(2,1)S(1)} %collective-permute-done.12.refs_5_), channel_id=1, source_target_pairs={{8,0},{10,2},{16,8},{18,10},{24,16},{26,18},{28,24},{30,26},{20,28... | collective-permute-start | bytes 393224 | tf_op jit(solution)/shard_map/ppermute | solution.py:220
  13.2 8.4 %collective-permute-start.16 = (bf16[256,256]{1,0:T(8,128)(2,1)S(1)}, bf16[256,256]{1,0:T(8,128)(2,1)S(1)}, u32[]{:S(2)}, u32[]{:S(2)}) collective-permute-start(bf16[256,256]{1,0:T(8,128)(2,1)S(1)} %collective-permute-done.15.refs_12_), channel_id=1, source_target_pairs={{0,8},{2,10},{8,16},{10,18},{16,24},{18,26},{24,28},{26,30},{28,20... | collective-permute-start | bytes 393224 | tf_op jit(solution)/shard_map/ppermute | solution.py:219
  24.2 10.3 %collective-permute-start.6 = (bf16[256,512]{1,0:T(8,128)(2,1)S(1)}, bf16[256,512]{1,0:T(8,128)(2,1)S(1)}, u32[]{:S(2)}, u32[]{:S(2)}) collective-permute-start(bf16[256,512]{1,0:T(8,128)(2,1)S(1)} %slice.30.refs_4_), channel_id=1, source_target_pairs={{0,8},{2,10},{8,16},{10,18},{16,24},{18,26},{24,28},{26,30},{28,20... | collective-permute-start | bytes 786440 | tf_op jit(solution)/shard_map/ppermute | solution.py:219
  33.0 12.0 %collective-permute-start.39 = (bf16[512,256]{1,0:T(8,128)(2,1)S(1)}, bf16[512,256]{1,0:T(8,128)(2,1)S(1)}, u32[]{:S(2)}, u32[]{:S(2)}) collective-permute-start(bf16[512,256]{1,0:T(8,128)(2,1)S(1)} %copy-done.1), channel_id=1, source_target_pairs={{8,0},{10,2},{16,8},{18,10},{24,16},{26,18},{28,24},{30,26},{20,28... | collective-permute-start | bytes 786440 | tf_op jit(solution)/shard_map/ppermute | solution.py:220
  34.3 13.4 %collective-permute-start.42 = (bf16[512,256]{1,0:T(8,128)(2,1)S(1)}, bf16[512,256]{1,0:T(8,128)(2,1)S(1)}, u32[]{:S(2)}, u32[]{:S(2)}) collective-permute-start(bf16[512,256]{1,0:T(8,128)(2,1)S(1)} %copy-done.1), channel_id=1, source_target_pairs={{0,8},{2,10},{8,16},{10,18},{16,24},{18,26},{24,28},{26,30},{28,20... | collective-permute-start | bytes 786440 | tf_op jit(solution)/shard_map/ppermute | solution.py:219
  34.5 11.8 %collective-permute-start.4 = (bf16[256,512]{1,0:T(8,128)(2,1)S(1)}, bf16[256,512]{1,0:T(8,128)(2,1)S(1)}, u32[]{:S(2)}, u32[]{:S(2)}) collective-permute-start(bf16[256,512]{1,0:T(8,128)(2,1)S(1)} %collective-permute-done.3.refs_5_), channel_id=1, source_target_pairs={{8,0},{10,2},{16,8},{18,10},{24,16},{26,18},{28,24},{30,26},{20,28... | collective-permute-start | bytes 786440 | tf_op jit(solution)/shard_map/ppermute | solution.py:220
  35.8 11.8 %collective-permute-start.7 = (bf16[256,512]{1,0:T(8,128)(2,1)S(1)}, bf16[256,512]{1,0:T(8,128)(2,1)S(1)}, u32[]{:S(2)}, u32[]{:S(2)}) collective-permute-start(bf16[256,512]{1,0:T(8,128)(2,1)S(1)} %collective-permute-done.6.refs_12_), channel_id=1, source_target_pairs={{0,8},{2,10},{8,16},{10,18},{16,24},{18,26},{24,28},{26,30},{28,20... | collective-permute-start | bytes 786440 | tf_op jit(solution)/shard_map/ppermute | solution.py:219
  45.0 21.5 %collective-permute-start.40 = (bf16[512,256]{1,0:T(8,128)(2,1)S(1)}, bf16[512,256]{1,0:T(8,128)(2,1)S(1)}, u32[]{:S(2)}, u32[]{:S(2)}) collective-permute-start(bf16[512,256]{1,0:T(8,128)(2,1)S(1)} %collective-permute-done.39.refs_1_), channel_id=1, source_target_pairs={{8,0},{10,2},{16,8},{18,10},{24,16},{26,18},{28,24},{30,26},{20,28... | collective-permute-start | bytes 786440 | tf_op jit(solution)/shard_map/ppermute | solution.py:220
  46.3 19.6 %collective-permute-start.5 = (bf16[256,512]{1,0:T(8,128)(2,1)S(1)}, bf16[256,512]{1,0:T(8,128)(2,1)S(1)}, u32[]{:S(2)}, u32[]{:S(2)}) collective-permute-start(bf16[256,512]{1,0:T(8,128)(2,1)S(1)} %collective-permute-done.4.refs_6_), channel_id=1, source_target_pairs={{8,0},{10,2},{16,8},{18,10},{24,16},{26,18},{28,24},{30,26},{20,28... | collective-permute-start | bytes 786440 | tf_op jit(solution)/shard_map/ppermute | solution.py:220
  47.6 18.2 %collective-permute-start.8 = (bf16[256,512]{1,0:T(8,128)(2,1)S(1)}, bf16[256,512]{1,0:T(8,128)(2,1)S(1)}, u32[]{:S(2)}, u32[]{:S(2)}) collective-permute-start(bf16[256,512]{1,0:T(8,128)(2,1)S(1)} %collective-permute-done.7.refs_11_), channel_id=1, source_target_pairs={{0,8},{2,10},{8,16},{10,18},{16,24},{18,26},{24,28},{26,30},{28,20... | collective-permute-start | bytes 786440 | tf_op jit(solution)/shard_map/ppermute | solution.py:219
  47.9 12.4 %collective-permute-start.22 = (bf16[128,256]{1,0:T(8,128)(2,1)S(1)}, bf16[128,256]{1,0:T(8,128)(2,1)S(1)}, u32[]{:S(2)}, u32[]{:S(2)}) collective-permute-start(bf16[128,256]{1,0:T(8,128)(2,1)S(1)} %collective-permute-done.21.refs_1_), channel_id=1, source_target_pairs={{8,0},{10,2},{16,8},{18,10},{24,16},{26,18},{28,24},{30,26},{20,28... | collective-permute-start | bytes 196616 | tf_op jit(solution)/shard_map/ppermute | solution.py:220
  53.8 13.7 %collective-permute-start.43 = (bf16[512,256]{1,0:T(8,128)(2,1)S(1)}, bf16[512,256]{1,0:T(8,128)(2,1)S(1)}, u32[]{:S(2)}, u32[]{:S(2)}) collective-permute-start(bf16[512,256]{1,0:T(8,128)(2,1)S(1)} %collective-permute-done.42.refs_8_), channel_id=1, source_target_pairs={{0,8},{2,10},{8,16},{10,18},{16,24},{18,26},{24,28},{26,30},{28,20... | collective-permute-start | bytes 786440 | tf_op jit(solution)/shard_map/ppermute | solution.py:219
  66.4 8.6 %collective-permute-start.10 = (bf16[128,512]{1,0:T(8,128)(2,1)S(1)}, bf16[128,512]{1,0:T(8,128)(2,1)S(1)}, u32[]{:S(2)}, u32[]{:S(2)}) collective-permute-start(bf16[128,512]{1,0:T(8,128)(2,1)S(1)} %slice.41), channel_id=1, source_target_pairs={{8,0},{10,2},{16,8},{18,10},{24,16},{26,18},{28,24},{30,26},{20,28... | collective-permute-start | bytes 393224 | tf_op jit(solution)/shard_map/ppermute | solution.py:228
  67.5 11.9 %collective-permute-start.29 = (bf16[128,256]{1,0:T(8,128)(2,1)S(1)}, bf16[128,256]{1,0:T(8,128)(2,1)S(1)}, u32[]{:S(2)}, u32[]{:S(2)}) collective-permute-start(bf16[128,256]{1,0:T(8,128)(2,1)S(1)} %keys.1.refs_0_), channel_id=1, source_target_pairs={{0,2},{2,0},{4,6},{6,4},{8,10},{10,8},{12,14},{14,12},{16,18},{18,... | collective-permute-start | bytes 196616 | tf_op jit(solution)/shard_map/ppermute | solution.py:307
  71.6 8.4 %collective-permute-start.30 = (bf16[128,256]{1,0:T(8,128)(2,1)S(1)}, bf16[128,256]{1,0:T(8,128)(2,1)S(1)}, u32[]{:S(2)}, u32[]{:S(2)}) collective-permute-start(bf16[128,256]{1,0:T(8,128)(2,1)S(1)} %collective-permute-done.21.refs_1_), channel_id=1, source_target_pairs={{0,2},{2,0},{4,6},{6,4},{8,10},{10,8},{12,14},{14,12},{16,18},{18,... | collective-permute-start | bytes 196616 | tf_op jit(solution)/shard_map/ppermute | solution.py:307
  71.7 10.6 %collective-permute-start.37 = (bf16[128,256]{1,0:T(8,128)(2,1)S(1)}, bf16[128,256]{1,0:T(8,128)(2,1)S(1)}, u32[]{:S(2)}, u32[]{:S(2)}) collective-permute-start(bf16[128,256]{1,0:T(8,128)(2,1)S(1)} %collective-permute-done.24.refs_8_), channel_id=1, source_target_pairs={{0,2},{2,0},{4,6},{6,4},{8,10},{10,8},{12,14},{14,12},{16,18},{18,... | collective-permute-start | bytes 196616 | tf_op jit(solution)/shard_map/ppermute | solution.py:307
  73.6 11.1 %collective-permute-start.31 = (bf16[128,256]{1,0:T(8,128)(2,1)S(1)}, bf16[128,256]{1,0:T(8,128)(2,1)S(1)}, u32[]{:S(2)}, u32[]{:S(2)}) collective-permute-start(bf16[128,256]{1,0:T(8,128)(2,1)S(1)} %collective-permute-done.22.refs_2_), channel_id=1, source_target_pairs={{0,2},{2,0},{4,6},{6,4},{8,10},{10,8},{12,14},{14,12},{16,18},{18,... | collective-permute-start | bytes 196616 | tf_op jit(solution)/shard_map/ppermute | solution.py:307
  75.0 10.3 %collective-permute-start.36 = (bf16[128,256]{1,0:T(8,128)(2,1)S(1)}, bf16[128,256]{1,0:T(8,128)(2,1)S(1)}, u32[]{:S(2)}, u32[]{:S(2)}) collective-permute-start(bf16[128,256]{1,0:T(8,128)(2,1)S(1)} %collective-permute-done.25.refs_7_), channel_id=1, source_target_pairs={{0,2},{2,0},{4,6},{6,4},{8,10},{10,8},{12,14},{14,12},{16,18},{18,... | collective-permute-start | bytes 196616 | tf_op jit(solution)/shard_map/ppermute | solution.py:307
  80.0 8.4 %collective-permute-start.41 = (bf16[512,256]{1,0:T(8,128)(2,1)S(1)}, bf16[512,256]{1,0:T(8,128)(2,1)S(1)}, u32[]{:S(2)}, u32[]{:S(2)}) collective-permute-start(bf16[512,256]{1,0:T(8,128)(2,1)S(1)} %collective-permute-done.40.refs_2_), channel_id=1, source_target_pairs={{8,0},{10,2},{16,8},{18,10},{24,16},{26,18},{28,24},{30,26},{20,28... | collective-permute-start | bytes 786440 | tf_op jit(solution)/shard_map/ppermute | solution.py:220
  80.6 8.6 %collective-permute-start.44 = (bf16[512,256]{1,0:T(8,128)(2,1)S(1)}, bf16[512,256]{1,0:T(8,128)(2,1)S(1)}, u32[]{:S(2)}, u32[]{:S(2)}) collective-permute-start(bf16[512,256]{1,0:T(8,128)(2,1)S(1)} %collective-permute-done.43.refs_7_), channel_id=1, source_target_pairs={{0,8},{2,10},{8,16},{10,18},{16,24},{18,26},{24,28},{26,30},{28,20... | collective-permute-start | bytes 786440 | tf_op jit(solution)/shard_map/ppermute | solution.py:219
  100.4 11.9 %collective-permute-start.49 = (bf16[8,64,256]{2,1,0:T(8,128)(2,1)S(1)}, bf16[8,64,256]{2,1,0:T(8,128)(2,1)S(1)}, u32[]{:S(2)}, u32[]{:S(2)}) collective-permute-start(bf16[8,64,256]{2,1,0:T(8,128)(2,1)S(1)} %get-tuple-element.24), channel_id=1, source_target_pairs={{0,3},{1,2},{2,1},{3,0},{4,7},{5,6},{6,5},{7,4},{8,11},{9,10},{10,... | collective-permute-start | bytes 786440 | tf_op jit(solution)/shard_map/ppermute | solution.py:345
  (64 other events, 350.6 us)

commit v2 on v1

--- a/solution.py
+++ b/solution.py
@@ -85,9 +85,9 @@
     ]
 
 
-def project_kernel(chips, groups, *refs):
+def project_kernel(chips, groups, outs, *refs):
     rows_refs, refs = refs[:groups], refs[groups:]
-    weight_refs, (mine_ref, theirs_ref) = refs[:-2], refs[-2:]
+    weight_refs, out_refs = refs[:-outs], refs[-outs:]
     weights = take_ring(weight_refs, chips)
     total = None
     for slot in range(chips):
@@ -100,9 +100,10 @@
             )
             total = part if total is None else total + part
             start += depth
-    half = mine_ref.shape[0]
-    mine_ref[...] = total[:half]
-    theirs_ref[...] = total[half:]
+    start = 0
+    for ref in out_refs:
+        ref[...] = total[start : start + ref.shape[0]]
+        start += ref.shape[0]
 
 
 def turn(values, cosine, sine):
@@ -110,8 +111,10 @@
 
 
 def keys_kernel(mine_ref, theirs_ref, cosine_ref, sine_ref, out_ref):
+    rows = out_ref.shape[0]
+    cosine, sine = cosine_ref[:rows, :], sine_ref[:rows, :]
     total = mine_ref[...] + theirs_ref[...]
-    out_ref[:, :HD] = turn(total[:, :HD], cosine_ref[...], sine_ref[...]).astype(jnp.bfloat16)
+    out_ref[:, :HD] = turn(total[:, :HD], cosine, sine).astype(jnp.bfloat16)
     out_ref[:, HD:] = total[:, HD:].astype(jnp.bfloat16)
 
 
@@ -127,11 +130,20 @@
     orig = orig_ref[...]
     allowed = (orig >= low_ref[...]) & (orig <= high_ref[...])
     scale = 1.0 / HD**0.5
+    rows = out_ref.shape[0]
+    half = rows // 2
+    lane = lax.broadcasted_iota(jnp.int32, (rows, HD), 1)
+    stats = jnp.zeros((rows, HD), jnp.float32)
     for head in range(QH_DEV):
         columns = slice(head * HD, (head + 1) * HD)
-        query = turn(
-            mine_ref[:, columns] + theirs_ref[:, columns], cosine_ref[...], sine_ref[...]
-        ).astype(jnp.bfloat16)
+        query = jnp.concatenate(
+            [
+                mine_ref[:half, columns] + theirs_ref[half:, columns],
+                mine_ref[half:, columns] + theirs_ref[:half, columns],
+            ],
+            axis=0,
+        )
+        query = turn(query, cosine_ref[...], sine_ref[...]).astype(jnp.bfloat16)
         scores = lax.dot_general(
             query, keys, (((1,), (1,)), ((), ())), preferred_element_type=jnp.float32
         )
@@ -139,15 +151,37 @@
         top = jnp.max(scores, axis=-1, keepdims=True)
         expo = jnp.where(allowed, jnp.exp(scores - top), 0.0)
         total = jnp.sum(expo, axis=-1, keepdims=True)
-        product = jnp.dot(expo.astype(jnp.bfloat16), values, preferred_element_type=jnp.float32)
-        out_ref[:, columns] = (product / total).astype(jnp.bfloat16)
+        out_ref[:, columns] = jnp.dot(
+            expo.astype(jnp.bfloat16), values, preferred_element_type=jnp.float32
+        )
+        stats = jnp.where(lane == 2 * head, total, stats)
+        stats = jnp.where(lane == 2 * head + 1, top, stats)
+    out_ref[:, HEAD_COLS:] = stats
 
 
 def output_kernel(chips, groups, mine_ref, theirs_ref, *refs):
     weight_refs, out_refs = refs[:-groups], refs[-groups:]
     weights = take_ring(weight_refs, chips)
-    mixed = jnp.concatenate([mine_ref[...], theirs_ref[...]], axis=0)
-    rows = mixed.shape[0] // groups
+    chip_rows = mine_ref.shape[0]
+    half = chip_rows // 2
+
+    def swapped(columns):
+        return jnp.concatenate([theirs_ref[half:, columns], theirs_ref[:half, columns]], axis=0)
+
+    pieces = []
+    for head in range(QH_DEV):
+        columns = slice(head * HD, (head + 1) * HD)
+        at = HEAD_COLS + 2 * head
+        total, top = mine_ref[:, at : at + 1], mine_ref[:, at + 1 : at + 2]
+        other_total, other_top = swapped(slice(at, at + 1)), swapped(slice(at + 1, at + 2))
+        peak = jnp.maximum(top, other_top)
+        factor, other_factor = jnp.exp(top - peak), jnp.exp(other_top - peak)
+        product = mine_ref[:, columns] * factor + swapped(columns) * other_factor
+        pieces.append(
+            (product / (total * factor + other_total * other_factor)).astype(jnp.bfloat16)
+        )
+    mixed = jnp.concatenate(pieces, axis=1)
+    rows = chip_rows // groups
     for slot in range(chips):
         start, total = 0, None
         for ref in weights[slot]:
@@ -212,22 +246,36 @@
     back = [(b, a) for a, b in ahead]
     sibling = [(c, c ^ 1) for c in range(n_context)]
 
-    def ring_gather(mine):
-        up, down = mine, mine
-        behind, before = [], []
-        for _ in range((chips - 1) // 2):
-            up = lax.ppermute(up, "context", ahead)
-            down = lax.ppermute(down, "context", back)
-            behind.append(up)
-            before.append(down)
-        middle = []
-        if chips % 2 == 0:
-            half = mine.shape[0] // 2
-            middle = [
-                lax.ppermute(up[:half], "context", ahead),
-                lax.ppermute(down[half:], "context", back),
-            ]
-        return [mine] + before + middle + behind[::-1]
+    def after(value, *earlier):
+        return lax.optimization_barrier((value, *earlier))[0]
+
+    class Ring:
+        def __init__(self, mine):
+            self.mine = mine
+            self.up, self.down = [mine], [mine]
+            self.middle = []
+
+        def step(self, *earlier):
+            up, down = self.up[-1], self.down[-1]
+            if earlier:
+                up, down = lax.optimization_barrier((up, down, *earlier))[:2]
+            if len(self.up) <= (chips - 1) // 2:
+                self.up.append(lax.ppermute(up, "context", ahead))
+                self.down.append(lax.ppermute(down, "context", back))
+            elif chips % 2 == 0 and not self.middle:
+                half = up.shape[0] // 2
+                self.middle = [
+                    lax.ppermute(up[:half], "context", ahead),
+                    lax.ppermute(down[half:], "context", back),
+                ]
+
+        def last(self):
+            return self.middle or [self.up[-1], self.down[-1]]
+
+        def finish(self):
+            while len(self.up) <= (chips - 1) // 2 or (chips % 2 == 0 and not self.middle):
+                self.step()
+            return self.down + self.middle + self.up[:0:-1]
 
     def member(e, d):
         return [
@@ -236,9 +284,11 @@
             for t in range(n_tensor)
         ]
 
-    keys_blocks = ring_gather(w_qkv[:, HEAD_COLS:])
-    query_blocks = ring_gather(w_qkv[:, :HEAD_COLS])
-    out_blocks = ring_gather(w_out)
+    keys_ring = Ring(w_qkv[:, HEAD_COLS:])
+    query_ring = Ring(w_qkv[:, :HEAD_COLS])
+    out_ring = Ring(w_out)
+    keys_ring.step()
+    query_ring.step()
 
     smem = pl.BlockSpec(memory_space=pltpu.SMEM)
     normed_shape = jax.ShapeDtypeStruct((chips, rows_here, block), jnp.bfloat16)
@@ -258,24 +308,25 @@
                 rows = lax.ppermute(rows, ("context", "tensor"), member(e, d))
             normed.append(rows)
 
-    def project(blocks, name):
+    def project(blocks, outs, name):
         columns = blocks[0].shape[1]
-        mine, theirs = pl.pallas_call(
-            functools.partial(project_kernel, chips, groups),
-            out_shape=[jax.ShapeDtypeStruct((tokens_here, columns), jnp.float32)] * 2,
+        return pl.pallas_call(
+            functools.partial(project_kernel, chips, groups, outs),
+            out_shape=[jax.ShapeDtypeStruct((2 * tokens_here // outs, columns), jnp.float32)]
+            * outs,
             in_specs=vmem_specs(groups + len(blocks)),
-            out_specs=vmem_specs(2),
+            out_specs=vmem_specs(outs),
             compiler_params=compute_params(),
             name=name,
         )(*normed, *blocks)
-        return mine, lax.ppermute(theirs, "context", sibling)
 
     doc_ends = jnp.cumsum(doc_lengths)
     inside = (
         (tensor + jnp.arange(n_tensor, dtype=jnp.int32)) % n_tensor * rows_here
     )[:, None] + jnp.arange(rows_here, dtype=jnp.int32)[None, :]
     inside = inside.reshape(-1)
-    query_orig, query_start = locate(context * tokens_here + inside, span_order, doc_ends)
+    both = jnp.concatenate([context * tokens_here + inside, (context ^ 1) * tokens_here + inside])
+    query_orig, query_start = locate(both, span_order, doc_ends)
     half = HD // 2
     freq = rope_theta ** (-(jnp.arange(half, dtype=jnp.float32) * 2.0 / HD))
     angle = (query_orig - query_start).astype(jnp.float32)[:, None] * freq[None, :]
@@ -290,11 +341,18 @@
         ),
         axis=1,
     ).astype(jnp.int32)
-    owner = jnp.concatenate([chip_of_slot * 2 + core, chip_of_slot * 2 + (1 - core)])
+    owner = chip_of_slot * 2 + core
     key_rows = (owner[:, None] * tokens_here + inside[None, :]).reshape(-1).astype(jnp.int32)
     key_orig, _ = locate(key_rows, span_order, doc_ends)
 
-    mine, theirs = project(keys_blocks, "project_keys")
+    for _ in range(2):
+        keys_ring.step(*keys_ring.last())
+        query_ring.step(*query_ring.last())
+    keys_ring.step()
+    out_ring.step(*keys_ring.up[1:], *keys_ring.down[1:])
+    query_ring.step()
+    mine, theirs = project(keys_ring.finish(), 2, "project_keys")
+    theirs = lax.ppermute(theirs, "context", sibling)
     kv = pl.pallas_call(
         keys_kernel,
         out_shape=jax.ShapeDtypeStruct((tokens_here, 2 * HD), jnp.bfloat16),
@@ -303,14 +361,19 @@
         compiler_params=compute_params(),
         name="keys",
     )(mine, theirs, cosine, sine)
-    kv_blocks = ring_gather(kv)
-    kv_blocks = kv_blocks + [lax.ppermute(b, "context", sibling) for b in kv_blocks]
-
-    mine, theirs = project(query_blocks, "project_queries")
-    count = n_context * tokens_here
+    kv_ring = Ring(kv)
+    kv_ring.step()
+    (mine,) = project(query_ring.finish(), 1, "project_queries")
+    theirs = lax.ppermute(mine, "context", sibling)
+    for _ in range(2):
+        kv_ring.step()
+        out_ring.step(*kv_ring.last())
+    kv_blocks = kv_ring.finish()
+
+    count = chips * tokens_here
     mixed = pl.pallas_call(
         attend_kernel,
-        out_shape=jax.ShapeDtypeStruct((tokens_here, HEAD_COLS), jnp.bfloat16),
+        out_shape=jax.ShapeDtypeStruct((2 * tokens_here, HEAD_COLS + HD), jnp.float32),
         in_specs=vmem_specs(7 + len(kv_blocks)),
         out_specs=vmem_specs(1)[0],
         scratch_shapes=[pltpu.VMEM((count, HD), jnp.bfloat16)] * 2,
@@ -327,6 +390,7 @@
         *kv_blocks,
     )
     mixed_theirs = lax.ppermute(mixed, "context", sibling)
+    out_blocks = out_ring.finish()
 
     out_block = w_out.shape[1]
     parts = pl.pallas_call(

time: 114 us -> 104 us (0.912)
  starting transfers between devices: 50.3 us -> 42.8 us
  local copies, waits for them, and re-layouts: 8.54 us -> 5.4 us
  waiting for transfers between devices: 42.7 us -> 44.1 us
    ppermute x43 -> x34, starting transfers between devices: 43.6 us -> 28 us  [the longest x12 13.7 us: step(): self.down.append(lax.ppermute(down, 'context', back))]
    ppermute x3, starting transfers between devices: 3.01 us -> 8.25 us  [per_device(): rows = lax.ppermute(rows, ('context', 'tensor'), member(e, d))]
    unnamed x76 -> x14, local copies, waits for them, and re-layouts: 6.7 us -> 2.65 us
    ppermute x1, starting transfers between devices: 0.69 us -> 2.9 us  [per_device(): mixed_theirs = lax.ppermute(mixed, 'context', sibling)]
    ppermute x43 -> x34, waiting for transfers between devices: 28.2 us -> 30.1 us  [the longest x12 16.9 us: step(): self.up.append(lax.ppermute(up, 'context', ahead))]
  transfers between devices with their start and end apart: 50 -> 41, of which waited for: 13 -> 15; matrix products, arithmetic and copies ran while one was open for 4% -> 5% of each run, Pallas kernels for 4% -> 5%
where the time goes in v2:
time: 104 us
  waiting for transfers between devices  44.1 us (42%)
  starting transfers between devices  42.8 us (41%)
  Pallas kernels  7.63 us (7%)
  local copies, waits for them, and re-layouts  5.4 us (5%)
  other arithmetic  3.47 us (3%)
    ppermute x12, waiting for transfers between devices, step(): self.up.append(lax.ppermute(up, 'context', ahead))  16.9 us
    ppermute x12, starting transfers between devices, step(): self.down.append(lax.ppermute(down, 'context', back))  13.7 us
    ppermute x3, waiting for transfers between devices, per_device(): part = lax.ppermute(part, ('context', 'tensor'), member(e, -d))  10 us
    ppermute x3, starting transfers between devices, per_device(): rows = lax.ppermute(rows, ('context', 'tensor'), member(e, d))  8.25 us
    ppermute x4, waiting for transfers between devices, step(): lax.ppermute(up[:half], 'context', ahead)  6.71 us
    ppermute x12, waiting for transfers between devices, step(): self.down.append(lax.ppermute(down, 'context', back))  6.14 us
    ppermute x4, starting transfers between devices, step(): lax.ppermute(down[half:], 'context', back)  5.02 us
    ppermute x12, starting transfers between devices, step(): self.up.append(lax.ppermute(up, 'context', ahead))  4.29 us
  transfers between devices with their start and end apart: 41, of which 15 were waited for; matrix products, arithmetic and copies ran while one was open for 5% of the time, Pallas kernels for 5%

profile of v2, /device:TPU:1, one launch (start us, length us, event | category | flops | bytes accessed | tf_op | source)
XLA Modules:
  0.0 103.7 jit_solution(8796793611446893519)
XLA Ops:
  1.0 2.1 %collective-permute-start.3 = (bf16[256,512]{1,0:T(8,128)(2,1)S(1)}, bf16[256,512]{1,0:T(8,128)(2,1)S(1)}, u32[]{:S(2)}, u32[]{:S(2)}) collective-permute-start(bf16[256,512]{1,0:T(8,128)(2,1)S(1)} %slice.30.refs_4_), channel_id=1, source_target_pairs={{8,0},{10,2},{16,8},{18,10},{24,16},{26,18},{28,24},{30,26},{20,28... | collective-permute-start | bytes 786440 | tf_op jit(solution)/shard_map/ppermute | solution.py:264
  4.2 1.4 %collective-permute-start.12 = (bf16[256,256]{1,0:T(8,128)(2,1)S(1)}, bf16[256,256]{1,0:T(8,128)(2,1)S(1)}, u32[]{:S(2)}, u32[]{:S(2)}) collective-permute-start(bf16[256,256]{1,0:T(8,128)(2,1)S(1)} %slice.33.refs_4_), channel_id=1, source_target_pairs={{8,0},{10,2},{16,8},{18,10},{24,16},{26,18},{28,24},{30,26},{20,28... | collective-permute-start | bytes 393224 | tf_op jit(solution)/shard_map/ppermute | solution.py:264
  9.2 1.4 %collective-permute-start = (bf16[8,64,256]{2,1,0:T(8,128)(2,1)S(1)}, bf16[8,64,256]{2,1,0:T(8,128)(2,1)S(1)}, u32[]{:S(2)}, u32[]{:S(2)}) collective-permute-start(bf16[8,64,256]{2,1,0:T(8,128)(2,1)S(1)} %get-tuple-element.27.refs_0_), channel_id=1, source_target_pairs={{0,1},{1,0},{2,3},{3,2},{4,5},{5,4},{6,7},{7,6},{8,9},{9,8},{10,11... | collective-permute-start | bytes 786440 | tf_op jit(solution)/shard_map/ppermute | solution.py:308
  15.3 1.6 %collective-permute-done.14.refs_6_ = bf16[256,256]{1,0:T(8,128)(2,1)S(1)} collective-permute-done((bf16[256,256]{1,0:T(8,128)(2,1)S(1)}, bf16[256,256]{1,0:T(8,128)(2,1)S(1)}, u32[]{:S(2)}, u32[]{:S(2)}) %collective-permute-start.14) | collective-permute-done | bytes 131104 | tf_op jit(solution)/shard_map/ppermute | solution.py:264
  16.9 2.7 %collective-permute-start.1 = (bf16[8,64,256]{2,1,0:T(8,128)(2,1)S(1)}, bf16[8,64,256]{2,1,0:T(8,128)(2,1)S(1)}, u32[]{:S(2)}, u32[]{:S(2)}) collective-permute-start(bf16[8,64,256]{2,1,0:T(8,128)(2,1)S(1)} %get-tuple-element.28), channel_id=1, source_target_pairs={{0,2},{1,3},{2,0},{3,1},{4,6},{5,7},{6,4},{7,5},{8,10},{9,11},{10,... | collective-permute-start | bytes 786440 | tf_op jit(solution)/shard_map/ppermute | solution.py:308
  21.0 1.3 %collective-permute-start.5 = (bf16[256,512]{1,0:T(8,128)(2,1)S(1)}, bf16[256,512]{1,0:T(8,128)(2,1)S(1)}, u32[]{:S(2)}, u32[]{:S(2)}) collective-permute-start(bf16[256,512]{1,0:T(8,128)(2,1)S(1)} %collective-permute-done.3.refs_5_), channel_id=1, source_target_pairs={{8,0},{10,2},{16,8},{18,10},{24,16},{26,18},{28,24},{30,26},{20,28... | collective-permute-start | bytes 786440 | tf_op jit(solution)/shard_map/ppermute | solution.py:264
  25.4 5.4 %collective-permute-done.17.refs_10_ = bf16[256,256]{1,0:T(8,128)(2,1)S(1)} collective-permute-done((bf16[256,256]{1,0:T(8,128)(2,1)S(1)}, bf16[256,256]{1,0:T(8,128)(2,1)S(1)}, u32[]{:S(2)}, u32[]{:S(2)}) %collective-permute-start.17) | collective-permute-done | bytes 131104 | tf_op jit(solution)/shard_map/ppermute | solution.py:263
  30.8 4.2 %collective-permute-start.2 = (bf16[8,64,256]{2,1,0:T(8,128)(2,1)S(1)}, bf16[8,64,256]{2,1,0:T(8,128)(2,1)S(1)}, u32[]{:S(2)}, u32[]{:S(2)}) collective-permute-start(bf16[8,64,256]{2,1,0:T(8,128)(2,1)S(1)} %get-tuple-element.28), channel_id=1, source_target_pairs={{0,3},{1,2},{2,1},{3,0},{4,7},{5,6},{6,5},{7,4},{8,11},{9,10},{10,... | collective-permute-start | bytes 786440 | tf_op jit(solution)/shard_map/ppermute | solution.py:308
  38.2 3.9 %collective-permute-done.2.refs_3_ = bf16[8,64,256]{2,1,0:T(8,128)(2,1)S(1)} collective-permute-done((bf16[8,64,256]{2,1,0:T(8,128)(2,1)S(1)}, bf16[8,64,256]{2,1,0:T(8,128)(2,1)S(1)}, u32[]{:S(2)}, u32[]{:S(2)}) %collective-permute-start.2) | collective-permute-done | bytes 262176 | tf_op jit(solution)/shard_map/ppermute | solution.py:308
  43.0 3.1 %collective-permute-done.8.refs_10_ = bf16[256,512]{1,0:T(8,128)(2,1)S(1)} collective-permute-done((bf16[256,512]{1,0:T(8,128)(2,1)S(1)}, bf16[256,512]{1,0:T(8,128)(2,1)S(1)}, u32[]{:S(2)}, u32[]{:S(2)}) %collective-permute-start.8) | collective-permute-done | bytes 262176 | tf_op jit(solution)/shard_map/ppermute | solution.py:263
  48.1 1.5 %collective-permute-start.24 = (bf16[128,256]{1,0:T(8,128)(2,1)S(1)}, bf16[128,256]{1,0:T(8,128)(2,1)S(1)}, u32[]{:S(2)}, u32[]{:S(2)}) collective-permute-start(bf16[128,256]{1,0:T(8,128)(2,1)S(1)} %keys.1.refs_0_), channel_id=1, source_target_pairs={{0,8},{2,10},{8,16},{10,18},{16,24},{18,26},{24,28},{26,30},{28,20... | collective-permute-start | bytes 196616 | tf_op jit(solution)/shard_map/ppermute | solution.py:263
  49.7 2.4 %collective-permute-done.21.refs_1_ = bf16[128,256]{1,0:T(8,128)(2,1)S(1)} collective-permute-done((bf16[128,256]{1,0:T(8,128)(2,1)S(1)}, bf16[128,256]{1,0:T(8,128)(2,1)S(1)}, u32[]{:S(2)}, u32[]{:S(2)}) %collective-permute-start.21) | collective-permute-done | bytes 65568 | tf_op jit(solution)/shard_map/ppermute | solution.py:264
  54.6 3.4 %collective-permute-start.11 = (f32[256,512]{1,0:T(8,128)S(1)}, f32[256,512]{1,0:T(8,128)S(1)}, u32[]{:S(2)}, u32[]{:S(2)}) collective-permute-start(f32[256,512]{1,0:T(8,128)S(1)} %project_queries.1.mine_ref), channel_id=1, source_target_pairs={{0,2},{2,0},{4,6},{6,4},{8,10},{10,8},{12,14},{14,12},{16,18},{18,... | collective-permute-start | bytes 1572872 | tf_op jit(solution)/shard_map/ppermute | solution.py:367
  65.0 4.1 %collective-permute-done.27.refs_4_ = bf16[64,256]{1,0:T(8,128)(2,1)S(1)} collective-permute-done((bf16[64,256]{1,0:T(8,128)(2,1)S(1)}, bf16[64,256]{1,0:T(8,128)(2,1)S(1)}, u32[]{:S(2)}, u32[]{:S(2)}) %collective-permute-start.27) | collective-permute-done | bytes 32800 | tf_op jit(solution)/shard_map/ppermute | solution.py:268
  69.1 2.6 %attend.1.mine_ref = f32[256,640]{1,0:T(8,128)S(1)} custom-call(f32[256,512]{1,0:T(8,128)S(1)} %project_queries.1.mine_ref, f32[256,512]{1,0:T(8,128)S(1)} %collective-permute-done.11.theirs_ref, f32[256,128]{1,0:T(8,128)S(1)} %get-tuple-element.58.cosine_ref, f32[256,128]{1,0:T(8,128)S(1)} %get-tuple-element.59.sine_ref, s32[256,1]{1,0:T(8,128)S(1)} %copy.32.low_ref, ...), custom_call_target="tpu_custom_call" | custom-call | tf_op jit(solution)/shard_map/attend/pallas_call | solution.py:374
  71.7 2.9 %collective-permute-start.29 = (f32[256,640]{1,0:T(8,128)S(1)}, f32[256,640]{1,0:T(8,128)S(1)}, u32[]{:S(2)}, u32[]{:S(2)}) collective-permute-start(f32[256,640]{1,0:T(8,128)S(1)} %attend.1.mine_ref), channel_id=1, source_target_pairs={{0,2},{2,0},{4,6},{6,4},{8,10},{10,8},{12,14},{14,12},{16,18},{18,... | collective-permute-start | bytes 1966088 | tf_op jit(solution)/shard_map/ppermute | solution.py:392
  76.1 6.4 %collective-permute-done.35.refs_6_ = bf16[512,256]{1,0:T(8,128)(2,1)S(1)} collective-permute-done((bf16[512,256]{1,0:T(8,128)(2,1)S(1)}, bf16[512,256]{1,0:T(8,128)(2,1)S(1)}, u32[]{:S(2)}, u32[]{:S(2)}) %collective-permute-start.35) | collective-permute-done | bytes 262176 | tf_op jit(solution)/shard_map/ppermute | solution.py:263
  84.1 2.6 %collective-permute-done.36.refs_4_ = bf16[256,256]{1,0:T(8,128)(2,1)S(1)} collective-permute-done((bf16[256,256]{1,0:T(8,128)(2,1)S(1)}, bf16[256,256]{1,0:T(8,128)(2,1)S(1)}, u32[]{:S(2)}, u32[]{:S(2)}) %collective-permute-start.36) | collective-permute-done | bytes 131104 | tf_op jit(solution)/shard_map/ppermute | solution.py:268
  87.1 1.4 %output.1 = (bf16[8,64,256]{2,1,0:T(8,128)(2,1)S(1)}, bf16[8,64,256]{2,1,0:T(8,128)(2,1)S(1)}, bf16[8,64,256]{2,1,0:T(8,128)(2,1)S(1)}, bf16[8,64,256]{2,1,0:T(8,128)(2,1)S(1)}) custom-call(f32[256,640]{1,0:T(8,128)S(1)} %attend.1.mine_ref, f32[256,640]{1,0:T(8,128)S(1)} %collective-permute-done.29.theirs_ref, bf16[512,256]{1,0:T(8,128)(2,1)S(1)} %copy-done.1, ...), custom_call_target="tpu_custom_call" | custom-call | tf_op jit(solution)/shard_map/output/pallas_call | solution.py:396
  88.5 2.0 %collective-permute-start.39 = (bf16[8,64,256]{2,1,0:T(8,128)(2,1)S(1)}, bf16[8,64,256]{2,1,0:T(8,128)(2,1)S(1)}, u32[]{:S(2)}, u32[]{:S(2)}) collective-permute-start(bf16[8,64,256]{2,1,0:T(8,128)(2,1)S(1)} %get-tuple-element.47), channel_id=1, source_target_pairs={{0,2},{1,3},{2,0},{3,1},{4,6},{5,7},{6,4},{7,5},{8,10},{9,11},{10,... | collective-permute-start | bytes 786440 | tf_op jit(solution)/shard_map/ppermute | solution.py:409
  90.6 1.6 %collective-permute-start.40 = (bf16[8,64,256]{2,1,0:T(8,128)(2,1)S(1)}, bf16[8,64,256]{2,1,0:T(8,128)(2,1)S(1)}, u32[]{:S(2)}, u32[]{:S(2)}) collective-permute-start(bf16[8,64,256]{2,1,0:T(8,128)(2,1)S(1)} %get-tuple-element.48), channel_id=1, source_target_pairs={{0,3},{1,2},{2,1},{3,0},{4,7},{5,6},{6,5},{7,4},{8,11},{9,10},{10,... | collective-permute-start | bytes 786440 | tf_op jit(solution)/shard_map/ppermute | solution.py:409
  92.1 2.2 %collective-permute-done.38.refs_1_ = bf16[8,64,256]{2,1,0:T(8,128)(2,1)S(1)} collective-permute-done((bf16[8,64,256]{2,1,0:T(8,128)(2,1)S(1)}, bf16[8,64,256]{2,1,0:T(8,128)(2,1)S(1)}, u32[]{:S(2)}, u32[]{:S(2)}) %collective-permute-start.38) | collective-permute-done | bytes 262176 | tf_op jit(solution)/shard_map/ppermute | solution.py:409
  94.3 7.8 %collective-permute-done.40.refs_3_ = bf16[8,64,256]{2,1,0:T(8,128)(2,1)S(1)} collective-permute-done((bf16[8,64,256]{2,1,0:T(8,128)(2,1)S(1)}, bf16[8,64,256]{2,1,0:T(8,128)(2,1)S(1)}, u32[]{:S(2)}, u32[]{:S(2)}) %collective-permute-start.40) | collective-permute-done | bytes 262176 | tf_op jit(solution)/shard_map/ppermute | solution.py:409
  102.2 1.5 %sum.1 = bf16[64,4096]{1,0:T(8,128)(2,1)} custom-call(s32[2]{0:T(128)S(1)} %pad_add_fusion.2.where_ref, bf16[8,64,256]{2,1,0:T(8,128)(2,1)S(1)} %get-tuple-element.45.refs_0_, bf16[8,64,256]{2,1,0:T(8,128)(2,1)S(1)} %collective-permute-done.38.refs_1_, bf16[8,64,256]{2,1,0:T(8,128)(2,1)S(1)} %collective-permute-done.39.refs_2_, ...), custom_call_target="tpu_custom_call" | custom-call | tf_op jit(solution)/shard_map/sum/pallas_call | solution.py:411
  (121 shorter events, 33.9 us)
Async XLA Ops:
  1.0 19.9 %collective-permute-start.3 = (bf16[256,512]{1,0:T(8,128)(2,1)S(1)}, bf16[256,512]{1,0:T(8,128)(2,1)S(1)}, u32[]{:S(2)}, u32[]{:S(2)}) collective-permute-start(bf16[256,512]{1,0:T(8,128)(2,1)S(1)} %slice.30.refs_4_), channel_id=1, source_target_pairs={{8,0},{10,2},{16,8},{18,10},{24,16},{26,18},{28,24},{30,26},{20,28... | collective-permute-start | bytes 786440 | tf_op jit(solution)/shard_map/ppermute | solution.py:264
  3.2 17.8 %collective-permute-start.4 = (bf16[256,512]{1,0:T(8,128)(2,1)S(1)}, bf16[256,512]{1,0:T(8,128)(2,1)S(1)}, u32[]{:S(2)}, u32[]{:S(2)}) collective-permute-start(bf16[256,512]{1,0:T(8,128)(2,1)S(1)} %slice.30.refs_4_), channel_id=1, source_target_pairs={{0,8},{2,10},{8,16},{10,18},{16,24},{18,26},{24,28},{26,30},{28,20... | collective-permute-start | bytes 786440 | tf_op jit(solution)/shard_map/ppermute | solution.py:263
  4.2 7.9 %collective-permute-start.12 = (bf16[256,256]{1,0:T(8,128)(2,1)S(1)}, bf16[256,256]{1,0:T(8,128)(2,1)S(1)}, u32[]{:S(2)}, u32[]{:S(2)}) collective-permute-start(bf16[256,256]{1,0:T(8,128)(2,1)S(1)} %slice.33.refs_4_), channel_id=1, source_target_pairs={{8,0},{10,2},{16,8},{18,10},{24,16},{26,18},{28,24},{30,26},{20,28... | collective-permute-start | bytes 393224 | tf_op jit(solution)/shard_map/ppermute | solution.py:264
  5.6 7.2 %collective-permute-start.13 = (bf16[256,256]{1,0:T(8,128)(2,1)S(1)}, bf16[256,256]{1,0:T(8,128)(2,1)S(1)}, u32[]{:S(2)}, u32[]{:S(2)}) collective-permute-start(bf16[256,256]{1,0:T(8,128)(2,1)S(1)} %slice.33.refs_4_), channel_id=1, source_target_pairs={{0,8},{2,10},{8,16},{10,18},{16,24},{18,26},{24,28},{26,30},{28,20... | collective-permute-start | bytes 393224 | tf_op jit(solution)/shard_map/ppermute | solution.py:263
  9.2 27.5 %collective-permute-start = (bf16[8,64,256]{2,1,0:T(8,128)(2,1)S(1)}, bf16[8,64,256]{2,1,0:T(8,128)(2,1)S(1)}, u32[]{:S(2)}, u32[]{:S(2)}) collective-permute-start(bf16[8,64,256]{2,1,0:T(8,128)(2,1)S(1)} %get-tuple-element.27.refs_0_), channel_id=1, source_target_pairs={{0,1},{1,0},{2,3},{3,2},{4,5},{5,4},{6,7},{7,6},{8,9},{9,8},{10,11... | collective-permute-start | bytes 786440 | tf_op jit(solution)/shard_map/ppermute | solution.py:308
  16.9 21.1 %collective-permute-start.1 = (bf16[8,64,256]{2,1,0:T(8,128)(2,1)S(1)}, bf16[8,64,256]{2,1,0:T(8,128)(2,1)S(1)}, u32[]{:S(2)}, u32[]{:S(2)}) collective-permute-start(bf16[8,64,256]{2,1,0:T(8,128)(2,1)S(1)} %get-tuple-element.28), channel_id=1, source_target_pairs={{0,2},{1,3},{2,0},{3,1},{4,6},{5,7},{6,4},{7,5},{8,10},{9,11},{10,... | collective-permute-start | bytes 786440 | tf_op jit(solution)/shard_map/ppermute | solution.py:308
  21.0 14.2 %collective-permute-start.5 = (bf16[256,512]{1,0:T(8,128)(2,1)S(1)}, bf16[256,512]{1,0:T(8,128)(2,1)S(1)}, u32[]{:S(2)}, u32[]{:S(2)}) collective-permute-start(bf16[256,512]{1,0:T(8,128)(2,1)S(1)} %collective-permute-done.3.refs_5_), channel_id=1, source_target_pairs={{8,0},{10,2},{16,8},{18,10},{24,16},{26,18},{28,24},{30,26},{20,28... | collective-permute-start | bytes 786440 | tf_op jit(solution)/shard_map/ppermute | solution.py:264
  22.3 13.1 %collective-permute-start.6 = (bf16[256,512]{1,0:T(8,128)(2,1)S(1)}, bf16[256,512]{1,0:T(8,128)(2,1)S(1)}, u32[]{:S(2)}, u32[]{:S(2)}) collective-permute-start(bf16[256,512]{1,0:T(8,128)(2,1)S(1)} %collective-permute-done.4.refs_12_), channel_id=1, source_target_pairs={{0,8},{2,10},{8,16},{10,18},{16,24},{18,26},{24,28},{26,30},{28,20... | collective-permute-start | bytes 786440 | tf_op jit(solution)/shard_map/ppermute | solution.py:263
  23.5 7.3 %collective-permute-start.17 = (bf16[256,256]{1,0:T(8,128)(2,1)S(1)}, bf16[256,256]{1,0:T(8,128)(2,1)S(1)}, u32[]{:S(2)}, u32[]{:S(2)}) collective-permute-start(bf16[256,256]{1,0:T(8,128)(2,1)S(1)} %collective-permute-done.15.refs_11_), channel_id=1, source_target_pairs={{0,8},{2,10},{8,16},{10,18},{16,24},{18,26},{24,28},{26,30},{28,20... | collective-permute-start | bytes 393224 | tf_op jit(solution)/shard_map/ppermute | solution.py:263
  30.8 11.3 %collective-permute-start.2 = (bf16[8,64,256]{2,1,0:T(8,128)(2,1)S(1)}, bf16[8,64,256]{2,1,0:T(8,128)(2,1)S(1)}, u32[]{:S(2)}, u32[]{:S(2)}) collective-permute-start(bf16[8,64,256]{2,1,0:T(8,128)(2,1)S(1)} %get-tuple-element.28), channel_id=1, source_target_pairs={{0,3},{1,2},{2,1},{3,0},{4,7},{5,6},{6,5},{7,4},{8,11},{9,10},{10,... | collective-permute-start | bytes 786440 | tf_op jit(solution)/shard_map/ppermute | solution.py:308
  35.2 6.9 %collective-permute-start.18 = (bf16[128,256]{1,0:T(8,128)(2,1)S(1)}, bf16[128,256]{1,0:T(8,128)(2,1)S(1)}, u32[]{:S(2)}, u32[]{:S(2)}) collective-permute-start(bf16[128,256]{1,0:T(8,128)(2,1)S(1)} %slice.42), channel_id=1, source_target_pairs={{0,8},{2,10},{8,16},{10,18},{16,24},{18,26},{24,28},{26,30},{28,20... | collective-permute-start | bytes 196616 | tf_op jit(solution)/shard_map/ppermute | solution.py:268
  36.7 9.7 %collective-permute-start.7 = (bf16[256,512]{1,0:T(8,128)(2,1)S(1)}, bf16[256,512]{1,0:T(8,128)(2,1)S(1)}, u32[]{:S(2)}, u32[]{:S(2)}) collective-permute-start(bf16[256,512]{1,0:T(8,128)(2,1)S(1)} %collective-permute-done.5.refs_6_), channel_id=1, source_target_pairs={{8,0},{10,2},{16,8},{18,10},{24,16},{26,18},{28,24},{30,26},{20,28... | collective-permute-start | bytes 786440 | tf_op jit(solution)/shard_map/ppermute | solution.py:264
  38.0 8.1 %collective-permute-start.8 = (bf16[256,512]{1,0:T(8,128)(2,1)S(1)}, bf16[256,512]{1,0:T(8,128)(2,1)S(1)}, u32[]{:S(2)}, u32[]{:S(2)}) collective-permute-start(bf16[256,512]{1,0:T(8,128)(2,1)S(1)} %collective-permute-done.6.refs_11_), channel_id=1, source_target_pairs={{0,8},{2,10},{8,16},{10,18},{16,24},{18,26},{24,28},{26,30},{28,20... | collective-permute-start | bytes 786440 | tf_op jit(solution)/shard_map/ppermute | solution.py:263
  46.1 7.5 %collective-permute-start.9 = (bf16[128,512]{1,0:T(8,128)(2,1)S(1)}, bf16[128,512]{1,0:T(8,128)(2,1)S(1)}, u32[]{:S(2)}, u32[]{:S(2)}) collective-permute-start(bf16[128,512]{1,0:T(8,128)(2,1)S(1)} %slice.40), channel_id=1, source_target_pairs={{0,8},{2,10},{8,16},{10,18},{16,24},{18,26},{24,28},{26,30},{28,20... | collective-permute-start | bytes 393224 | tf_op jit(solution)/shard_map/ppermute | solution.py:268
  46.4 7.4 %collective-permute-start.10 = (bf16[128,512]{1,0:T(8,128)(2,1)S(1)}, bf16[128,512]{1,0:T(8,128)(2,1)S(1)}, u32[]{:S(2)}, u32[]{:S(2)}) collective-permute-start(bf16[128,512]{1,0:T(8,128)(2,1)S(1)} %slice.41), channel_id=1, source_target_pairs={{8,0},{10,2},{16,8},{18,10},{24,16},{26,18},{28,24},{30,26},{20,28... | collective-permute-start | bytes 393224 | tf_op jit(solution)/shard_map/ppermute | solution.py:269
  49.6 11.0 %collective-permute-start.30 = (bf16[512,256]{1,0:T(8,128)(2,1)S(1)}, bf16[512,256]{1,0:T(8,128)(2,1)S(1)}, u32[]{:S(2)}, u32[]{:S(2)}) collective-permute-start(bf16[512,256]{1,0:T(8,128)(2,1)S(1)} %copy-done.1), channel_id=1, source_target_pairs={{8,0},{10,2},{16,8},{18,10},{24,16},{26,18},{28,24},{30,26},{20,28... | collective-permute-start | bytes 786440 | tf_op jit(solution)/shard_map/ppermute | solution.py:264
  52.1 8.5 %collective-permute-start.31 = (bf16[512,256]{1,0:T(8,128)(2,1)S(1)}, bf16[512,256]{1,0:T(8,128)(2,1)S(1)}, u32[]{:S(2)}, u32[]{:S(2)}) collective-permute-start(bf16[512,256]{1,0:T(8,128)(2,1)S(1)} %copy-done.1), channel_id=1, source_target_pairs={{0,8},{2,10},{8,16},{10,18},{16,24},{18,26},{24,28},{26,30},{28,20... | collective-permute-start | bytes 786440 | tf_op jit(solution)/shard_map/ppermute | solution.py:263
  54.6 14.6 %collective-permute-start.11 = (f32[256,512]{1,0:T(8,128)S(1)}, f32[256,512]{1,0:T(8,128)S(1)}, u32[]{:S(2)}, u32[]{:S(2)}) collective-permute-start(f32[256,512]{1,0:T(8,128)S(1)} %project_queries.1.mine_ref), channel_id=1, source_target_pairs={{0,2},{2,0},{4,6},{6,4},{8,10},{10,8},{12,14},{14,12},{16,18},{18,... | collective-permute-start | bytes 1572872 | tf_op jit(solution)/shard_map/ppermute | solution.py:367
  60.7 14.0 %collective-permute-start.32 = (bf16[512,256]{1,0:T(8,128)(2,1)S(1)}, bf16[512,256]{1,0:T(8,128)(2,1)S(1)}, u32[]{:S(2)}, u32[]{:S(2)}) collective-permute-start(bf16[512,256]{1,0:T(8,128)(2,1)S(1)} %collective-permute-done.30.refs_1_), channel_id=1, source_target_pairs={{8,0},{10,2},{16,8},{18,10},{24,16},{26,18},{28,24},{30,26},{20,28... | collective-permute-start | bytes 786440 | tf_op jit(solution)/shard_map/ppermute | solution.py:264
  61.8 12.8 %collective-permute-start.33 = (bf16[512,256]{1,0:T(8,128)(2,1)S(1)}, bf16[512,256]{1,0:T(8,128)(2,1)S(1)}, u32[]{:S(2)}, u32[]{:S(2)}) collective-permute-start(bf16[512,256]{1,0:T(8,128)(2,1)S(1)} %collective-permute-done.31.refs_8_), channel_id=1, source_target_pairs={{0,8},{2,10},{8,16},{10,18},{16,24},{18,26},{24,28},{26,30},{28,20... | collective-permute-start | bytes 786440 | tf_op jit(solution)/shard_map/ppermute | solution.py:263
  71.7 15.4 %collective-permute-start.29 = (f32[256,640]{1,0:T(8,128)S(1)}, f32[256,640]{1,0:T(8,128)S(1)}, u32[]{:S(2)}, u32[]{:S(2)}) collective-permute-start(f32[256,640]{1,0:T(8,128)S(1)} %attend.1.mine_ref), channel_id=1, source_target_pairs={{0,2},{2,0},{4,6},{6,4},{8,10},{10,8},{12,14},{14,12},{16,18},{18,... | collective-permute-start | bytes 1966088 | tf_op jit(solution)/shard_map/ppermute | solution.py:392
  74.6 7.9 %collective-permute-start.35 = (bf16[512,256]{1,0:T(8,128)(2,1)S(1)}, bf16[512,256]{1,0:T(8,128)(2,1)S(1)}, u32[]{:S(2)}, u32[]{:S(2)}) collective-permute-start(bf16[512,256]{1,0:T(8,128)(2,1)S(1)} %collective-permute-done.33.refs_7_), channel_id=1, source_target_pairs={{0,8},{2,10},{8,16},{10,18},{16,24},{18,26},{24,28},{26,30},{28,20... | collective-permute-start | bytes 786440 | tf_op jit(solution)/shard_map/ppermute | solution.py:263
  75.0 7.9 %collective-permute-start.34 = (bf16[512,256]{1,0:T(8,128)(2,1)S(1)}, bf16[512,256]{1,0:T(8,128)(2,1)S(1)}, u32[]{:S(2)}, u32[]{:S(2)}) collective-permute-start(bf16[512,256]{1,0:T(8,128)(2,1)S(1)} %collective-permute-done.32.refs_2_), channel_id=1, source_target_pairs={{8,0},{10,2},{16,8},{18,10},{24,16},{26,18},{28,24},{30,26},{20,28... | collective-permute-start | bytes 786440 | tf_op jit(solution)/shard_map/ppermute | solution.py:264
  90.6 11.6 %collective-permute-start.40 = (bf16[8,64,256]{2,1,0:T(8,128)(2,1)S(1)}, bf16[8,64,256]{2,1,0:T(8,128)(2,1)S(1)}, u32[]{:S(2)}, u32[]{:S(2)}) collective-permute-start(bf16[8,64,256]{2,1,0:T(8,128)(2,1)S(1)} %get-tuple-element.48), channel_id=1, source_target_pairs={{0,3},{1,2},{2,1},{3,0},{4,7},{5,6},{6,5},{7,4},{8,11},{9,10},{10,... | collective-permute-start | bytes 786440 | tf_op jit(solution)/shard_map/ppermute | solution.py:409
  (24 other events, 109.1 us)

commit v3 on v2

--- a/solution.py
+++ b/solution.py
@@ -118,7 +118,9 @@
     out_ref[:, HD:] = total[:, HD:].astype(jnp.bfloat16)
 
 
-def attend_kernel(mine_ref, theirs_ref, cosine_ref, sine_ref, low_ref, high_ref, orig_ref, *refs):
+def attend_kernel(
+    mine_ref, theirs_ref, cosine_ref, sine_ref, low_ref, high_ref, orig_ref, *refs
+):
     block_refs, (out_ref, keys_ref, values_ref) = refs[:-3], refs[-3:]
     start = 0
     for ref in block_refs:
@@ -159,9 +161,7 @@
     out_ref[:, HEAD_COLS:] = stats
 
 
-def output_kernel(chips, groups, mine_ref, theirs_ref, *refs):
-    weight_refs, out_refs = refs[:-groups], refs[-groups:]
-    weights = take_ring(weight_refs, chips)
+def output_kernel(chips, groups, mine_ref, theirs_ref, weight_ref, *out_refs):
     chip_rows = mine_ref.shape[0]
     half = chip_rows // 2
 
@@ -182,46 +182,34 @@
         )
     mixed = jnp.concatenate(pieces, axis=1)
     rows = chip_rows // groups
-    for slot in range(chips):
-        start, total = 0, None
-        for ref in weights[slot]:
-            depth = ref.shape[0]
-            part = jnp.dot(
-                mixed[:, start : start + depth], ref[...], preferred_element_type=jnp.float32
-            )
-            total = part if total is None else total + part
-            start += depth
+    for chip in range(chips):
+        total = jnp.dot(mixed, weight_ref[chip], preferred_element_type=jnp.float32)
         total = total.astype(jnp.bfloat16)
         for group in range(groups):
-            out_refs[group][slot] = total[group * rows : (group + 1) * rows]
-
-
-def sum_kernel(place, chips, groups, where_ref, *refs):
+            out_refs[group][chip] = total[group * rows : (group + 1) * rows]
+
+
+def sum_kernel(chips, groups, where_ref, *refs):
     part_refs, out_ref = refs[:groups], refs[groups]
-    at, core = where_ref[0], where_ref[1]
+    core = where_ref[1]
     block = part_refs[0].shape[2]
     half = groups // 2
 
-    def added(part, slot):
-        total = part_refs[part * half][slot].astype(jnp.float32)
+    def added(part, chip):
+        total = part_refs[part * half][chip].astype(jnp.float32)
         for ref in part_refs[part * half + 1 : (part + 1) * half]:
-            total += ref[slot].astype(jnp.float32)
+            total += ref[chip].astype(jnp.float32)
         return total.astype(jnp.bfloat16)
 
-    for chip in range(chips):
-        slot = lax.rem(place[chip] + chips - at, chips)
-        first = slice((2 * chip) * block, (2 * chip + 1) * block)
-        second = slice((2 * chip + 1) * block, (2 * chip + 2) * block)
-
-        @pl.when(core == 0)
+    for even in range(2):
+
+        @pl.when(core == even)
         def _():
-            out_ref[:, first] = added(0, slot)
-            out_ref[:, second] = added(1, slot)
-
-        @pl.when(core != 0)
-        def _():
-            out_ref[:, first] = added(1, slot)
-            out_ref[:, second] = added(0, slot)
+            for chip in range(chips):
+                first = slice((2 * chip) * block, (2 * chip + 1) * block)
+                second = slice((2 * chip + 1) * block, (2 * chip + 2) * block)
+                out_ref[:, first] = added(even, chip)
+                out_ref[:, second] = added(1 - even, chip)
 
 
 def per_device(n_context, n_tensor, hidden_rows, norm_gain, w_qkv, w_out, doc_lengths, span_order):
@@ -269,13 +257,19 @@
                     lax.ppermute(down[half:], "context", back),
                 ]
 
+        def done(self):
+            return len(self.up) > (chips - 1) // 2 and (chips % 2 == 1 or bool(self.middle))
+
         def last(self):
             return self.middle or [self.up[-1], self.down[-1]]
 
         def finish(self):
-            while len(self.up) <= (chips - 1) // 2 or (chips % 2 == 0 and not self.middle):
-                self.step()
             return self.down + self.middle + self.up[:0:-1]
+
+    same_core = [[2 * chip + k for chip in range(chips)] for k in range(2)]
+
+    def from_chips(mine):
+        return lax.all_gather(mine, "context", axis_index_groups=same_core)
 
     def member(e, d):
         return [
@@ -286,7 +280,7 @@
 
     keys_ring = Ring(w_qkv[:, HEAD_COLS:])
     query_ring = Ring(w_qkv[:, :HEAD_COLS])
-    out_ring = Ring(w_out)
+    out_blocks = from_chips(w_out)
     keys_ring.step()
     query_ring.step()
 
@@ -345,12 +339,12 @@
     key_rows = (owner[:, None] * tokens_here + inside[None, :]).reshape(-1).astype(jnp.int32)
     key_orig, _ = locate(key_rows, span_order, doc_ends)
 
-    for _ in range(2):
-        keys_ring.step(*keys_ring.last())
-        query_ring.step(*query_ring.last())
-    keys_ring.step()
-    out_ring.step(*keys_ring.up[1:], *keys_ring.down[1:])
-    query_ring.step()
+    queries_before = []
+    while not keys_ring.done():
+        keys_now, queries_now = keys_ring.last(), query_ring.last()
+        keys_ring.step(*queries_before)
+        query_ring.step(*keys_now)
+        queries_before = queries_now
     mine, theirs = project(keys_ring.finish(), 2, "project_keys")
     theirs = lax.ppermute(theirs, "context", sibling)
     kv = pl.pallas_call(
@@ -365,12 +359,11 @@
     kv_ring.step()
     (mine,) = project(query_ring.finish(), 1, "project_queries")
     theirs = lax.ppermute(mine, "context", sibling)
-    for _ in range(2):
-        kv_ring.step()
-        out_ring.step(*kv_ring.last())
+    while not kv_ring.done():
+        kv_ring.step(*kv_ring.last())
     kv_blocks = kv_ring.finish()
-
     count = chips * tokens_here
+
     mixed = pl.pallas_call(
         attend_kernel,
         out_shape=jax.ShapeDtypeStruct((2 * tokens_here, HEAD_COLS + HD), jnp.float32),
@@ -390,17 +383,16 @@
         *kv_blocks,
     )
     mixed_theirs = lax.ppermute(mixed, "context", sibling)
-    out_blocks = out_ring.finish()
 
     out_block = w_out.shape[1]
     parts = pl.pallas_call(
         functools.partial(output_kernel, chips, groups),
         out_shape=[jax.ShapeDtypeStruct((chips, rows_here, out_block), jnp.bfloat16)] * groups,
-        in_specs=vmem_specs(2 + len(out_blocks)),
+        in_specs=vmem_specs(3),
         out_specs=vmem_specs(groups),
         compiler_params=compute_params(),
         name="output",
-    )(mixed, mixed_theirs, *out_blocks)
+    )(mixed, mixed_theirs, out_blocks)
     arrived = []
     for e in range(2):
         for d in range(n_tensor):
@@ -409,7 +401,7 @@
                 part = lax.ppermute(part, ("context", "tensor"), member(e, -d))
             arrived.append(part)
     return pl.pallas_call(
-        functools.partial(sum_kernel, place, chips, groups),
+        functools.partial(sum_kernel, chips, groups),
         out_shape=jax.ShapeDtypeStruct((rows_here, n_context * out_block), jnp.bfloat16),
         in_specs=[smem] + vmem_specs(groups),
         out_specs=vmem_specs(1)[0],

time: 104 us -> 126 us (1.21)
  between operations: 0.29 us -> 13.7 us
  waiting for transfers between devices: 44.1 us -> 50.5 us
  other arithmetic: 3.47 us -> 4.95 us
    ppermute x12 -> x9, waiting for transfers between devices: 6.14 us -> 28.9 us  [step(): self.down.append(lax.ppermute(down, 'context', back))]
    ppermute x12 -> x9, waiting for transfers between devices: 16.9 us -> 5.42 us  [step(): self.up.append(lax.ppermute(up, 'context', ahead))]
    ppermute x12 -> x9, starting transfers between devices: 4.29 us -> 10.7 us  [step(): self.up.append(lax.ppermute(up, 'context', ahead))]
    ppermute x12 -> x9, starting transfers between devices: 13.7 us -> 7.73 us  [step(): self.down.append(lax.ppermute(down, 'context', back))]
    ppermute x4 -> x3, waiting for transfers between devices: 6.71 us -> 1.24 us  [step(): lax.ppermute(up[:half], 'context', ahead)]
    ppermute x3, waiting for transfers between devices: 3.9 us -> 0.01 us  [per_device(): rows = lax.ppermute(rows, ('context', 'tensor'), member(e, d))]
    ppermute x4 -> x3, starting transfers between devices: 5.02 us -> 2.07 us  [step(): lax.ppermute(down[half:], 'context', back)]
    ppermute x1, starting transfers between devices: 2.9 us -> 5.72 us  [per_device(): mixed_theirs = lax.ppermute(mixed, 'context', sibling)]
  transfers between devices with their start and end apart: 41 -> 34, of which waited for: 15 -> 14; matrix products, arithmetic and copies ran while one was open for 5% -> 6% of each run, Pallas kernels for 5% -> 4%
where the time goes in v3:
time: 126 us; the launch traced here: 125 us
  waiting for transfers between devices  50.5 us (40%)
  starting transfers between devices  42.6 us (34%)
  between operations  13.7 us (11%)
  Pallas kernels  7.56 us (6%)
  local copies, waits for them, and re-layouts  6.04 us (5%)
  other arithmetic  4.95 us (4%)
    ppermute x9, waiting for transfers between devices, step(): self.down.append(lax.ppermute(down, 'context', back))  28.9 us
    ppermute x3, waiting for transfers between devices, per_device(): part = lax.ppermute(part, ('context', 'tensor'), member(e, -d))  11.6 us
    ppermute x9, starting transfers between devices, step(): self.up.append(lax.ppermute(up, 'context', ahead))  10.7 us
    ppermute x9, starting transfers between devices, step(): self.down.append(lax.ppermute(down, 'context', back))  7.73 us
    ppermute x1, starting transfers between devices, per_device(): mixed_theirs = lax.ppermute(mixed, 'context', sibling)  5.72 us
    ppermute x3, starting transfers between devices, per_device(): rows = lax.ppermute(rows, ('context', 'tensor'), member(e, d))  5.68 us
    ppermute x9, waiting for transfers between devices, step(): self.up.append(lax.ppermute(up, 'context', ahead))  5.42 us
    ppermute x3, starting transfers between devices, step(): lax.ppermute(up[:half], 'context', ahead)  3.7 us
  transfers between devices with their start and end apart: 34, of which 14 were waited for; matrix products, arithmetic and copies ran while one was open for 6% of the time, Pallas kernels for 4%

profile of v3, /device:TPU:1, one launch (start us, length us, event | category | flops | bytes accessed | tf_op | source)
XLA Modules:
  0.0 125.3 jit_solution(14070598527316369949)
XLA Ops:
  7.5 2.1 %collective-permute-start.6 = (bf16[256,256]{1,0:T(8,128)(2,1)S(1)}, bf16[256,256]{1,0:T(8,128)(2,1)S(1)}, u32[]{:S(2)}, u32[]{:S(2)}) collective-permute-start(bf16[256,256]{1,0:T(8,128)(2,1)S(1)} %slice.25.refs_4_), channel_id=1, source_target_pairs={{8,0},{10,2},{16,8},{18,10},{24,16},{26,18},{28,24},{30,26},{20,28... | collective-permute-start | bytes 393224 | tf_op jit(solution)/shard_map/ppermute | solution.py:252
  21.7 2.2 %collective-permute-done.10.refs_6_ = bf16[256,256]{1,0:T(8,128)(2,1)S(1)} collective-permute-done((bf16[256,256]{1,0:T(8,128)(2,1)S(1)}, bf16[256,256]{1,0:T(8,128)(2,1)S(1)}, u32[]{:S(2)}, u32[]{:S(2)}) %collective-permute-start.10) | collective-permute-done | bytes 131104 | tf_op jit(solution)/shard_map/ppermute | solution.py:252
  23.9 2.9 %collective-permute-start.1 = (bf16[8,64,256]{2,1,0:T(8,128)(2,1)S(1)}, bf16[8,64,256]{2,1,0:T(8,128)(2,1)S(1)}, u32[]{:S(2)}, u32[]{:S(2)}) collective-permute-start(bf16[8,64,256]{2,1,0:T(8,128)(2,1)S(1)} %get-tuple-element.30), channel_id=1, source_target_pairs={{0,2},{1,3},{2,0},{3,1},{4,6},{5,7},{6,4},{7,5},{8,10},{9,11},{10,... | collective-permute-start | bytes 786440 | tf_op jit(solution)/shard_map/ppermute | solution.py:302
  29.7 3.8 %collective-permute-done.13.refs_10_ = bf16[256,256]{1,0:T(8,128)(2,1)S(1)} collective-permute-done((bf16[256,256]{1,0:T(8,128)(2,1)S(1)}, bf16[256,256]{1,0:T(8,128)(2,1)S(1)}, u32[]{:S(2)}, u32[]{:S(2)}) %collective-permute-start.13) | collective-permute-done | bytes 131104 | tf_op jit(solution)/shard_map/ppermute | solution.py:251
  33.5 2.2 %collective-permute-start.8 = (bf16[256,512]{1,0:T(8,128)(2,1)S(1)}, bf16[256,512]{1,0:T(8,128)(2,1)S(1)}, u32[]{:S(2)}, u32[]{:S(2)}) collective-permute-start(bf16[256,512]{1,0:T(8,128)(2,1)S(1)} %collective-permute-done.4.refs_12_), channel_id=1, source_target_pairs={{0,8},{2,10},{8,16},{10,18},{16,24},{18,26},{24,28},{26,30},{28,20... | collective-permute-start | bytes 786440 | tf_op jit(solution)/shard_map/ppermute | solution.py:251
  38.5 9.0 %collective-permute-done.7.refs_6_ = bf16[256,512]{1,0:T(8,128)(2,1)S(1)} collective-permute-done((bf16[256,512]{1,0:T(8,128)(2,1)S(1)}, bf16[256,512]{1,0:T(8,128)(2,1)S(1)}, u32[]{:S(2)}, u32[]{:S(2)}) %collective-permute-start.7) | collective-permute-done | bytes 262176 | tf_op jit(solution)/shard_map/ppermute | solution.py:252
  52.5 3.0 %collective-permute-start.20 = (f32[128,256]{1,0:T(8,128)S(1)}, f32[128,256]{1,0:T(8,128)S(1)}, u32[]{:S(2)}, u32[]{:S(2)}) collective-permute-start(f32[128,256]{1,0:T(8,128)S(1)} %get-tuple-element.42), channel_id=1, source_target_pairs={{0,2},{2,0},{4,6},{6,4},{8,10},{10,8},{12,14},{14,12},{16,18},{18,... | collective-permute-start | bytes 393224 | tf_op jit(solution)/shard_map/ppermute | solution.py:349
  55.5 6.9 %collective-permute-done.11.refs_7_ = bf16[256,512]{1,0:T(8,128)(2,1)S(1)} collective-permute-done((bf16[256,512]{1,0:T(8,128)(2,1)S(1)}, bf16[256,512]{1,0:T(8,128)(2,1)S(1)}, u32[]{:S(2)}, u32[]{:S(2)}) %collective-permute-start.11) | collective-permute-done | bytes 262176 | tf_op jit(solution)/shard_map/ppermute | solution.py:252
  62.5 2.7 %collective-permute-start.15 = (bf16[128,512]{1,0:T(8,128)(2,1)S(1)}, bf16[128,512]{1,0:T(8,128)(2,1)S(1)}, u32[]{:S(2)}, u32[]{:S(2)}) collective-permute-start(bf16[128,512]{1,0:T(8,128)(2,1)S(1)} %slice.26), channel_id=1, source_target_pairs={{0,8},{2,10},{8,16},{10,18},{16,24},{18,26},{24,28},{26,30},{28,20... | collective-permute-start | bytes 393224 | tf_op jit(solution)/shard_map/ppermute | solution.py:256
  65.6 3.6 %collective-permute-start.22 = (bf16[128,256]{1,0:T(8,128)(2,1)S(1)}, bf16[128,256]{1,0:T(8,128)(2,1)S(1)}, u32[]{:S(2)}, u32[]{:S(2)}) collective-permute-start(bf16[128,256]{1,0:T(8,128)(2,1)S(1)} %keys.1.refs_0_), channel_id=1, source_target_pairs={{0,8},{2,10},{8,16},{10,18},{16,24},{18,26},{24,28},{26,30},{28,20... | collective-permute-start | bytes 196616 | tf_op jit(solution)/shard_map/ppermute | solution.py:251
  69.2 9.2 %collective-permute-done.21.refs_1_ = bf16[128,256]{1,0:T(8,128)(2,1)S(1)} collective-permute-done((bf16[128,256]{1,0:T(8,128)(2,1)S(1)}, bf16[128,256]{1,0:T(8,128)(2,1)S(1)}, u32[]{:S(2)}, u32[]{:S(2)}) %collective-permute-start.21) | collective-permute-done | bytes 65568 | tf_op jit(solution)/shard_map/ppermute | solution.py:252
  78.5 1.5 %collective-permute-start.24 = (bf16[128,256]{1,0:T(8,128)(2,1)S(1)}, bf16[128,256]{1,0:T(8,128)(2,1)S(1)}, u32[]{:S(2)}, u32[]{:S(2)}) collective-permute-start(bf16[128,256]{1,0:T(8,128)(2,1)S(1)} %collective-permute-done.22.refs_8_), channel_id=1, source_target_pairs={{0,8},{2,10},{8,16},{10,18},{16,24},{18,26},{24,28},{26,30},{28,20... | collective-permute-start | bytes 196616 | tf_op jit(solution)/shard_map/ppermute | solution.py:251
  80.7 2.0 %collective-permute-start.17 = (f32[256,512]{1,0:T(8,128)S(1)}, f32[256,512]{1,0:T(8,128)S(1)}, u32[]{:S(2)}, u32[]{:S(2)}) collective-permute-start(f32[256,512]{1,0:T(8,128)S(1)} %project_queries.1.mine_ref), channel_id=1, source_target_pairs={{0,2},{2,0},{4,6},{6,4},{8,10},{10,8},{12,14},{14,12},{16,18},{18,... | collective-permute-start | bytes 1572872 | tf_op jit(solution)/shard_map/ppermute | solution.py:361
  84.4 1.5 %collective-permute-done.25.refs_3_ = bf16[128,256]{1,0:T(8,128)(2,1)S(1)} collective-permute-done((bf16[128,256]{1,0:T(8,128)(2,1)S(1)}, bf16[128,256]{1,0:T(8,128)(2,1)S(1)}, u32[]{:S(2)}, u32[]{:S(2)}) %collective-permute-start.25) | collective-permute-done | bytes 65568 | tf_op jit(solution)/shard_map/ppermute | solution.py:252
  85.9 1.6 %collective-permute-done.26.refs_6_ = bf16[128,256]{1,0:T(8,128)(2,1)S(1)} collective-permute-done((bf16[128,256]{1,0:T(8,128)(2,1)S(1)}, bf16[128,256]{1,0:T(8,128)(2,1)S(1)}, u32[]{:S(2)}, u32[]{:S(2)}) %collective-permute-start.26) | collective-permute-done | bytes 65568 | tf_op jit(solution)/shard_map/ppermute | solution.py:251
  87.5 1.5 %collective-permute-start.28 = (bf16[64,256]{1,0:T(8,128)(2,1)S(1)}, bf16[64,256]{1,0:T(8,128)(2,1)S(1)}, u32[]{:S(2)}, u32[]{:S(2)}) collective-permute-start(bf16[64,256]{1,0:T(8,128)(2,1)S(1)} %slice.31), channel_id=1, source_target_pairs={{8,0},{10,2},{16,8},{18,10},{24,16},{26,18},{28,24},{30,26},{20,28... | collective-permute-start | bytes 98312 | tf_op jit(solution)/shard_map/ppermute | solution.py:257
  90.3 2.6 %attend.1.mine_ref = f32[256,640]{1,0:T(8,128)S(1)} custom-call(f32[256,512]{1,0:T(8,128)S(1)} %project_queries.1.mine_ref, f32[256,512]{1,0:T(8,128)S(1)} %collective-permute-done.17.theirs_ref, f32[256,128]{1,0:T(8,128)S(1)} %get-tuple-element.62.cosine_ref, f32[256,128]{1,0:T(8,128)S(1)} %get-tuple-element.63.sine_ref, s32[256,1]{1,0:T(8,128)S(1)} %copy.32.low_ref, ...), custom_call_target="tpu_custom_call" | custom-call | tf_op jit(solution)/shard_map/attend/pallas_call | solution.py:367
  92.9 5.7 %collective-permute-start.29 = (f32[256,640]{1,0:T(8,128)S(1)}, f32[256,640]{1,0:T(8,128)S(1)}, u32[]{:S(2)}, u32[]{:S(2)}) collective-permute-start(f32[256,640]{1,0:T(8,128)S(1)} %attend.1.mine_ref), channel_id=1, source_target_pairs={{0,2},{2,0},{4,6},{6,4},{8,10},{10,8},{12,14},{14,12},{16,18},{18,... | collective-permute-start | bytes 1966088 | tf_op jit(solution)/shard_map/ppermute | solution.py:385
  98.6 1.7 %collective-permute-done.29.theirs_ref = f32[256,640]{1,0:T(8,128)S(1)} collective-permute-done((f32[256,640]{1,0:T(8,128)S(1)}, f32[256,640]{1,0:T(8,128)S(1)}, u32[]{:S(2)}, u32[]{:S(2)}) %collective-permute-start.29) | collective-permute-done | bytes 655392 | tf_op jit(solution)/shard_map/ppermute | solution.py:385
  100.3 1.6 %copy-done = bf16[4096,256]{1,0:T(8,128)(2,1)S(1)} copy-done((bf16[4096,256]{1,0:T(8,128)(2,1)S(1)}, bf16[4096,256]{1,0:T(8,128)(2,1)}, u32[]{:S(2)}) %copy-start) | copy-done | bytes 2097176
  103.8 1.6 %collective-permute-start.32 = (bf16[8,64,256]{2,1,0:T(8,128)(2,1)S(1)}, bf16[8,64,256]{2,1,0:T(8,128)(2,1)S(1)}, u32[]{:S(2)}, u32[]{:S(2)}) collective-permute-start(bf16[8,64,256]{2,1,0:T(8,128)(2,1)S(1)} %get-tuple-element.52), channel_id=1, source_target_pairs={{0,3},{1,2},{2,1},{3,0},{4,7},{5,6},{6,5},{7,4},{8,11},{9,10},{10,... | collective-permute-start | bytes 786440 | tf_op jit(solution)/shard_map/ppermute | solution.py:401
  105.3 5.5 %collective-permute-done.30.refs_1_ = bf16[8,64,256]{2,1,0:T(8,128)(2,1)S(1)} collective-permute-done((bf16[8,64,256]{2,1,0:T(8,128)(2,1)S(1)}, bf16[8,64,256]{2,1,0:T(8,128)(2,1)S(1)}, u32[]{:S(2)}, u32[]{:S(2)}) %collective-permute-start.30) | collective-permute-done | bytes 262176 | tf_op jit(solution)/shard_map/ppermute | solution.py:401
  110.8 6.1 %collective-permute-done.32.refs_3_ = bf16[8,64,256]{2,1,0:T(8,128)(2,1)S(1)} collective-permute-done((bf16[8,64,256]{2,1,0:T(8,128)(2,1)S(1)}, bf16[8,64,256]{2,1,0:T(8,128)(2,1)S(1)}, u32[]{:S(2)}, u32[]{:S(2)}) %collective-permute-start.32) | collective-permute-done | bytes 262176 | tf_op jit(solution)/shard_map/ppermute | solution.py:401
  117.0 1.5 %sum.1 = bf16[64,4096]{1,0:T(8,128)(2,1)} custom-call(s32[2]{0:T(128)S(1)} %pad_add_fusion.2.where_ref, bf16[8,64,256]{2,1,0:T(8,128)(2,1)S(1)} %get-tuple-element.49.refs_0_, bf16[8,64,256]{2,1,0:T(8,128)(2,1)S(1)} %collective-permute-done.30.refs_1_, bf16[8,64,256]{2,1,0:T(8,128)(2,1)S(1)} %collective-permute-done.31.refs_2_, ...), custom_call_target="tpu_custom_call" | custom-call | tf_op jit(solution)/shard_map/sum/pallas_call | solution.py:403
  (102 shorter events, 29.6 us)
Async XLA Ops:
  6.5 93.8 %all-gather.3.cloned.1.call-start = ((), (), s32[]{:S(2)}) async-start(), calls=%async_computation | async-start | bytes 2359296 | tf_op jit(solution)/shard_map/all_gather | solution.py:272
  7.5 12.2 %collective-permute-start.6 = (bf16[256,256]{1,0:T(8,128)(2,1)S(1)}, bf16[256,256]{1,0:T(8,128)(2,1)S(1)}, u32[]{:S(2)}, u32[]{:S(2)}) collective-permute-start(bf16[256,256]{1,0:T(8,128)(2,1)S(1)} %slice.25.refs_4_), channel_id=1, source_target_pairs={{8,0},{10,2},{16,8},{18,10},{24,16},{26,18},{28,24},{30,26},{20,28... | collective-permute-start | bytes 393224 | tf_op jit(solution)/shard_map/ppermute | solution.py:252
  9.6 11.4 %collective-permute-start.5 = (bf16[256,256]{1,0:T(8,128)(2,1)S(1)}, bf16[256,256]{1,0:T(8,128)(2,1)S(1)}, u32[]{:S(2)}, u32[]{:S(2)}) collective-permute-start(bf16[256,256]{1,0:T(8,128)(2,1)S(1)} %slice.25.refs_4_), channel_id=1, source_target_pairs={{0,8},{2,10},{8,16},{10,18},{16,24},{18,26},{24,28},{26,30},{28,20... | collective-permute-start | bytes 393224 | tf_op jit(solution)/shard_map/ppermute | solution.py:251
  10.7 16.1 %collective-permute-start.3 = (bf16[256,512]{1,0:T(8,128)(2,1)S(1)}, bf16[256,512]{1,0:T(8,128)(2,1)S(1)}, u32[]{:S(2)}, u32[]{:S(2)}) collective-permute-start(bf16[256,512]{1,0:T(8,128)(2,1)S(1)} %slice.24.refs_4_), channel_id=1, source_target_pairs={{8,0},{10,2},{16,8},{18,10},{24,16},{26,18},{28,24},{30,26},{20,28... | collective-permute-start | bytes 786440 | tf_op jit(solution)/shard_map/ppermute | solution.py:252
  12.1 14.8 %collective-permute-start.4 = (bf16[256,512]{1,0:T(8,128)(2,1)S(1)}, bf16[256,512]{1,0:T(8,128)(2,1)S(1)}, u32[]{:S(2)}, u32[]{:S(2)}) collective-permute-start(bf16[256,512]{1,0:T(8,128)(2,1)S(1)} %slice.24.refs_4_), channel_id=1, source_target_pairs={{0,8},{2,10},{8,16},{10,18},{16,24},{18,26},{24,28},{26,30},{28,20... | collective-permute-start | bytes 786440 | tf_op jit(solution)/shard_map/ppermute | solution.py:251
  16.9 32.1 %collective-permute-start = (bf16[8,64,256]{2,1,0:T(8,128)(2,1)S(1)}, bf16[8,64,256]{2,1,0:T(8,128)(2,1)S(1)}, u32[]{:S(2)}, u32[]{:S(2)}) collective-permute-start(bf16[8,64,256]{2,1,0:T(8,128)(2,1)S(1)} %get-tuple-element.29.refs_0_), channel_id=1, source_target_pairs={{0,1},{1,0},{2,3},{3,2},{4,5},{5,4},{6,7},{7,6},{8,9},{9,8},{10,11... | collective-permute-start | bytes 786440 | tf_op jit(solution)/shard_map/ppermute | solution.py:302
  23.9 25.1 %collective-permute-start.1 = (bf16[8,64,256]{2,1,0:T(8,128)(2,1)S(1)}, bf16[8,64,256]{2,1,0:T(8,128)(2,1)S(1)}, u32[]{:S(2)}, u32[]{:S(2)}) collective-permute-start(bf16[8,64,256]{2,1,0:T(8,128)(2,1)S(1)} %get-tuple-element.30), channel_id=1, source_target_pairs={{0,2},{1,3},{2,0},{3,1},{4,6},{5,7},{6,4},{7,5},{8,10},{9,11},{10,... | collective-permute-start | bytes 786440 | tf_op jit(solution)/shard_map/ppermute | solution.py:302
  26.9 6.7 %collective-permute-start.13 = (bf16[256,256]{1,0:T(8,128)(2,1)S(1)}, bf16[256,256]{1,0:T(8,128)(2,1)S(1)}, u32[]{:S(2)}, u32[]{:S(2)}) collective-permute-start(bf16[256,256]{1,0:T(8,128)(2,1)S(1)} %collective-permute-done.9.refs_11_), channel_id=1, source_target_pairs={{0,8},{2,10},{8,16},{10,18},{16,24},{18,26},{24,28},{26,30},{28,20... | collective-permute-start | bytes 393224 | tf_op jit(solution)/shard_map/ppermute | solution.py:251
  28.2 8.7 %collective-permute-start.14 = (bf16[256,256]{1,0:T(8,128)(2,1)S(1)}, bf16[256,256]{1,0:T(8,128)(2,1)S(1)}, u32[]{:S(2)}, u32[]{:S(2)}) collective-permute-start(bf16[256,256]{1,0:T(8,128)(2,1)S(1)} %collective-permute-done.10.refs_6_), channel_id=1, source_target_pairs={{8,0},{10,2},{16,8},{18,10},{24,16},{26,18},{28,24},{30,26},{20,28... | collective-permute-start | bytes 393224 | tf_op jit(solution)/shard_map/ppermute | solution.py:252
  28.4 19.0 %collective-permute-start.7 = (bf16[256,512]{1,0:T(8,128)(2,1)S(1)}, bf16[256,512]{1,0:T(8,128)(2,1)S(1)}, u32[]{:S(2)}, u32[]{:S(2)}) collective-permute-start(bf16[256,512]{1,0:T(8,128)(2,1)S(1)} %collective-permute-done.3.refs_5_), channel_id=1, source_target_pairs={{8,0},{10,2},{16,8},{18,10},{24,16},{26,18},{28,24},{30,26},{20,28... | collective-permute-start | bytes 786440 | tf_op jit(solution)/shard_map/ppermute | solution.py:252
  33.5 13.9 %collective-permute-start.8 = (bf16[256,512]{1,0:T(8,128)(2,1)S(1)}, bf16[256,512]{1,0:T(8,128)(2,1)S(1)}, u32[]{:S(2)}, u32[]{:S(2)}) collective-permute-start(bf16[256,512]{1,0:T(8,128)(2,1)S(1)} %collective-permute-done.4.refs_12_), channel_id=1, source_target_pairs={{0,8},{2,10},{8,16},{10,18},{16,24},{18,26},{24,28},{26,30},{28,20... | collective-permute-start | bytes 786440 | tf_op jit(solution)/shard_map/ppermute | solution.py:251
  36.9 13.5 %collective-permute-start.2 = (bf16[8,64,256]{2,1,0:T(8,128)(2,1)S(1)}, bf16[8,64,256]{2,1,0:T(8,128)(2,1)S(1)}, u32[]{:S(2)}, u32[]{:S(2)}) collective-permute-start(bf16[8,64,256]{2,1,0:T(8,128)(2,1)S(1)} %get-tuple-element.30), channel_id=1, source_target_pairs={{0,3},{1,2},{2,1},{3,0},{4,7},{5,6},{6,5},{7,4},{8,11},{9,10},{10,... | collective-permute-start | bytes 786440 | tf_op jit(solution)/shard_map/ppermute | solution.py:302
  49.0 13.5 %collective-permute-start.11 = (bf16[256,512]{1,0:T(8,128)(2,1)S(1)}, bf16[256,512]{1,0:T(8,128)(2,1)S(1)}, u32[]{:S(2)}, u32[]{:S(2)}) collective-permute-start(bf16[256,512]{1,0:T(8,128)(2,1)S(1)} %collective-permute-done.7.refs_6_), channel_id=1, source_target_pairs={{8,0},{10,2},{16,8},{18,10},{24,16},{26,18},{28,24},{30,26},{20,28... | collective-permute-start | bytes 786440 | tf_op jit(solution)/shard_map/ppermute | solution.py:252
  49.0 13.5 %collective-permute-start.12 = (bf16[256,512]{1,0:T(8,128)(2,1)S(1)}, bf16[256,512]{1,0:T(8,128)(2,1)S(1)}, u32[]{:S(2)}, u32[]{:S(2)}) collective-permute-start(bf16[256,512]{1,0:T(8,128)(2,1)S(1)} %collective-permute-done.8.refs_11_), channel_id=1, source_target_pairs={{0,8},{2,10},{8,16},{10,18},{16,24},{18,26},{24,28},{26,30},{28,20... | collective-permute-start | bytes 786440 | tf_op jit(solution)/shard_map/ppermute | solution.py:251
  52.5 12.9 %collective-permute-start.20 = (f32[128,256]{1,0:T(8,128)S(1)}, f32[128,256]{1,0:T(8,128)S(1)}, u32[]{:S(2)}, u32[]{:S(2)}) collective-permute-start(f32[128,256]{1,0:T(8,128)S(1)} %get-tuple-element.42), channel_id=1, source_target_pairs={{0,2},{2,0},{4,6},{6,4},{8,10},{10,8},{12,14},{14,12},{16,18},{18,... | collective-permute-start | bytes 393224 | tf_op jit(solution)/shard_map/ppermute | solution.py:349
  62.5 17.4 %collective-permute-start.15 = (bf16[128,512]{1,0:T(8,128)(2,1)S(1)}, bf16[128,512]{1,0:T(8,128)(2,1)S(1)}, u32[]{:S(2)}, u32[]{:S(2)}) collective-permute-start(bf16[128,512]{1,0:T(8,128)(2,1)S(1)} %slice.26), channel_id=1, source_target_pairs={{0,8},{2,10},{8,16},{10,18},{16,24},{18,26},{24,28},{26,30},{28,20... | collective-permute-start | bytes 393224 | tf_op jit(solution)/shard_map/ppermute | solution.py:256
  65.2 14.8 %collective-permute-start.16 = (bf16[128,512]{1,0:T(8,128)(2,1)S(1)}, bf16[128,512]{1,0:T(8,128)(2,1)S(1)}, u32[]{:S(2)}, u32[]{:S(2)}) collective-permute-start(bf16[128,512]{1,0:T(8,128)(2,1)S(1)} %slice.27), channel_id=1, source_target_pairs={{8,0},{10,2},{16,8},{18,10},{24,16},{26,18},{28,24},{30,26},{20,28... | collective-permute-start | bytes 393224 | tf_op jit(solution)/shard_map/ppermute | solution.py:257
  65.5 13.0 %collective-permute-start.21 = (bf16[128,256]{1,0:T(8,128)(2,1)S(1)}, bf16[128,256]{1,0:T(8,128)(2,1)S(1)}, u32[]{:S(2)}, u32[]{:S(2)}) collective-permute-start(bf16[128,256]{1,0:T(8,128)(2,1)S(1)} %keys.1.refs_0_), channel_id=1, source_target_pairs={{8,0},{10,2},{16,8},{18,10},{24,16},{26,18},{28,24},{30,26},{20,28... | collective-permute-start | bytes 196616 | tf_op jit(solution)/shard_map/ppermute | solution.py:252
  65.6 12.9 %collective-permute-start.22 = (bf16[128,256]{1,0:T(8,128)(2,1)S(1)}, bf16[128,256]{1,0:T(8,128)(2,1)S(1)}, u32[]{:S(2)}, u32[]{:S(2)}) collective-permute-start(bf16[128,256]{1,0:T(8,128)(2,1)S(1)} %keys.1.refs_0_), channel_id=1, source_target_pairs={{0,8},{2,10},{8,16},{10,18},{16,24},{18,26},{24,28},{26,30},{28,20... | collective-permute-start | bytes 196616 | tf_op jit(solution)/shard_map/ppermute | solution.py:251
  80.7 9.6 %collective-permute-start.17 = (f32[256,512]{1,0:T(8,128)S(1)}, f32[256,512]{1,0:T(8,128)S(1)}, u32[]{:S(2)}, u32[]{:S(2)}) collective-permute-start(f32[256,512]{1,0:T(8,128)S(1)} %project_queries.1.mine_ref), channel_id=1, source_target_pairs={{0,2},{2,0},{4,6},{6,4},{8,10},{10,8},{12,14},{14,12},{16,18},{18,... | collective-permute-start | bytes 1572872 | tf_op jit(solution)/shard_map/ppermute | solution.py:361
  92.9 7.4 %collective-permute-start.29 = (f32[256,640]{1,0:T(8,128)S(1)}, f32[256,640]{1,0:T(8,128)S(1)}, u32[]{:S(2)}, u32[]{:S(2)}) collective-permute-start(f32[256,640]{1,0:T(8,128)S(1)} %attend.1.mine_ref), channel_id=1, source_target_pairs={{0,2},{2,0},{4,6},{6,4},{8,10},{10,8},{12,14},{14,12},{16,18},{18,... | collective-permute-start | bytes 1966088 | tf_op jit(solution)/shard_map/ppermute | solution.py:385
  103.2 7.6 %collective-permute-start.30 = (bf16[8,64,256]{2,1,0:T(8,128)(2,1)S(1)}, bf16[8,64,256]{2,1,0:T(8,128)(2,1)S(1)}, u32[]{:S(2)}, u32[]{:S(2)}) collective-permute-start(bf16[8,64,256]{2,1,0:T(8,128)(2,1)S(1)} %get-tuple-element.50), channel_id=1, source_target_pairs={{0,1},{1,0},{2,3},{3,2},{4,5},{5,4},{6,7},{7,6},{8,9},{9,8},{10,11... | collective-permute-start | bytes 786440 | tf_op jit(solution)/shard_map/ppermute | solution.py:401
  103.3 7.5 %collective-permute-start.31 = (bf16[8,64,256]{2,1,0:T(8,128)(2,1)S(1)}, bf16[8,64,256]{2,1,0:T(8,128)(2,1)S(1)}, u32[]{:S(2)}, u32[]{:S(2)}) collective-permute-start(bf16[8,64,256]{2,1,0:T(8,128)(2,1)S(1)} %get-tuple-element.51), channel_id=1, source_target_pairs={{0,2},{1,3},{2,0},{3,1},{4,6},{5,7},{6,4},{7,5},{8,10},{9,11},{10,... | collective-permute-start | bytes 786440 | tf_op jit(solution)/shard_map/ppermute | solution.py:401
  103.8 13.2 %collective-permute-start.32 = (bf16[8,64,256]{2,1,0:T(8,128)(2,1)S(1)}, bf16[8,64,256]{2,1,0:T(8,128)(2,1)S(1)}, u32[]{:S(2)}, u32[]{:S(2)}) collective-permute-start(bf16[8,64,256]{2,1,0:T(8,128)(2,1)S(1)} %get-tuple-element.52), channel_id=1, source_target_pairs={{0,3},{1,2},{2,1},{3,0},{4,7},{5,6},{6,5},{7,4},{8,11},{9,10},{10,... | collective-permute-start | bytes 786440 | tf_op jit(solution)/shard_map/ppermute | solution.py:401
  (15 other events, 119.4 us)
Sparse Core Ops, SparseCore 0:
  18.4 60.8 all-gather.2

commit v4 on v2

--- a/solution.py
+++ b/solution.py
@@ -51,28 +51,32 @@
     return pltpu.CompilerParams(vmem_limit_bytes=VMEM_LIMIT)
 
 
-def norm_kernel(place, chips, where_ref, hidden_ref, gain_ref, own_ref, other_ref):
-    at, core = where_ref[0], where_ref[1]
+def place_of(place):
+    context = lax.axis_index("context")
+    at = jnp.int32(0)
+    for chip, spot in enumerate(place):
+        at = jnp.where(context // 2 == chip, jnp.int32(spot), at)
+    return at, context % 2
+
+
+def norm_kernel(place, chips, hidden_ref, gain_ref, own_ref, other_ref):
+    at, core = place_of(place)
     wide = hidden_ref[...].astype(jnp.float32)
     meansq = jnp.mean(wide * wide, axis=-1, keepdims=True)
     normed = (wide * lax.rsqrt(meansq + 1e-05) * gain_ref[...].astype(jnp.float32)).astype(
         jnp.bfloat16
     )
     block = own_ref.shape[2]
-    for chip in range(chips):
-        slot = lax.rem(place[chip] + chips - at, chips)
-        first = normed[:, (2 * chip) * block : (2 * chip + 1) * block]
-        second = normed[:, (2 * chip + 1) * block : (2 * chip + 2) * block]
-
-        @pl.when(core == 0)
+    for even in range(2):
+
+        @pl.when(core == even)
         def _():
-            own_ref[slot] = first
-            other_ref[slot] = second
-
-        @pl.when(core != 0)
-        def _():
-            own_ref[slot] = second
-            other_ref[slot] = first
+            for chip in range(chips):
+                slot = lax.rem(place[chip] + chips - at, chips)
+                for side in range(2):
+                    column = (2 * chip + side) * block
+                    ref = own_ref if side == even else other_ref
+                    ref[slot] = normed[:, column : column + block]
 
 
 def take_ring(refs, chips):
@@ -196,9 +200,9 @@
             out_refs[group][slot] = total[group * rows : (group + 1) * rows]
 
 
-def sum_kernel(place, chips, groups, where_ref, *refs):
+def sum_kernel(place, chips, groups, token_ref, *refs):
     part_refs, out_ref = refs[:groups], refs[groups]
-    at, core = where_ref[0], where_ref[1]
+    at, core = place_of(place)
     block = part_refs[0].shape[2]
     half = groups // 2
 
@@ -208,20 +212,15 @@
             total += ref[slot].astype(jnp.float32)
         return total.astype(jnp.bfloat16)
 
-    for chip in range(chips):
-        slot = lax.rem(place[chip] + chips - at, chips)
-        first = slice((2 * chip) * block, (2 * chip + 1) * block)
-        second = slice((2 * chip + 1) * block, (2 * chip + 2) * block)
-
-        @pl.when(core == 0)
+    for even in range(2):
+
+        @pl.when(core == even)
         def _():
-            out_ref[:, first] = added(0, slot)
-            out_ref[:, second] = added(1, slot)
-
-        @pl.when(core != 0)
-        def _():
-            out_ref[:, first] = added(1, slot)
-            out_ref[:, second] = added(0, slot)
+            for chip in range(chips):
+                slot = lax.rem(place[chip] + chips - at, chips)
+                for side in range(2):
+                    column = (2 * chip + side) * block
+                    out_ref[:, column : column + block] = added(side ^ even, slot)
 
 
 def per_device(n_context, n_tensor, hidden_rows, norm_gain, w_qkv, w_out, doc_lengths, span_order):
@@ -234,31 +233,26 @@
     block = width // n_context
     context = lax.axis_index("context")
     tensor = lax.axis_index("tensor")
-    core = context % 2
-    at = jnp.sum(
-        jnp.where(jnp.arange(chips) == context // 2, jnp.asarray(place, jnp.int32), 0)
-    ).astype(jnp.int32)
-    where = jnp.stack([at, core]).astype(jnp.int32)
-
     ahead = [
         (ring[i] * 2 + k, ring[(i + 1) % chips] * 2 + k) for i in range(chips) for k in range(2)
     ]
     back = [(b, a) for a, b in ahead]
     sibling = [(c, c ^ 1) for c in range(n_context)]
 
-    def after(value, *earlier):
-        return lax.optimization_barrier((value, *earlier))[0]
+    token = [doc_lengths]
+
+    def ordered(values):
+        held = lax.optimization_barrier((*values, token[0]))
+        token[0] = held[-1]
+        return list(held[:-1])
 
     class Ring:
         def __init__(self, mine):
-            self.mine = mine
             self.up, self.down = [mine], [mine]
             self.middle = []
 
-        def step(self, *earlier):
-            up, down = self.up[-1], self.down[-1]
-            if earlier:
-                up, down = lax.optimization_barrier((up, down, *earlier))[:2]
+        def step(self, earlier=()):
+            up, down, *earlier = ordered((self.up[-1], self.down[-1], *earlier))
             if len(self.up) <= (chips - 1) // 2:
                 self.up.append(lax.ppermute(up, "context", ahead))
                 self.down.append(lax.ppermute(down, "context", back))
@@ -268,12 +262,13 @@
                     lax.ppermute(up[:half], "context", ahead),
                     lax.ppermute(down[half:], "context", back),
                 ]
-
-        def last(self):
-            return self.middle or [self.up[-1], self.down[-1]]
+            return earlier
+
+        def done(self):
+            return len(self.up) > (chips - 1) // 2 and (chips % 2 == 1 or bool(self.middle))
 
         def finish(self):
-            while len(self.up) <= (chips - 1) // 2 or (chips % 2 == 0 and not self.middle):
+            while not self.done():
                 self.step()
             return self.down + self.middle + self.up[:0:-1]
 
@@ -285,21 +280,18 @@
         ]
 
     keys_ring = Ring(w_qkv[:, HEAD_COLS:])
-    query_ring = Ring(w_qkv[:, :HEAD_COLS])
-    out_ring = Ring(w_out)
     keys_ring.step()
-    query_ring.step()
-
-    smem = pl.BlockSpec(memory_space=pltpu.SMEM)
+
     normed_shape = jax.ShapeDtypeStruct((chips, rows_here, block), jnp.bfloat16)
     normed_own, normed_other = pl.pallas_call(
         functools.partial(norm_kernel, place, chips),
         out_shape=[normed_shape] * 2,
-        in_specs=[smem] + vmem_specs(2),
+        in_specs=vmem_specs(2),
         out_specs=vmem_specs(2),
         compiler_params=compute_params(),
         name="norm",
-    )(where, hidden_rows, norm_gain[None, :])
+    )(hidden_rows, norm_gain[None, :])
+    normed_own, normed_other = ordered((normed_own, normed_other))
     normed = []
     for e in range(2):
         for d in range(n_tensor):
@@ -307,6 +299,16 @@
             if e or d:
                 rows = lax.ppermute(rows, ("context", "tensor"), member(e, d))
             normed.append(rows)
+
+    keys_ring.step()
+    query_ring = Ring(ordered((w_qkv,))[0][:, :HEAD_COLS])
+    query_ring.step()
+    keys_ring.step()
+    normed = keys_ring.step(normed)
+    while not keys_ring.done():
+        keys_ring.step()
+    query_ring.step()
+    out_ring = Ring(w_out)
 
     def project(blocks, outs, name):
         columns = blocks[0].shape[1]
@@ -318,7 +320,7 @@
             out_specs=vmem_specs(outs),
             compiler_params=compute_params(),
             name=name,
-        )(*normed, *blocks)
+        )(*ordered((*normed, *blocks)))
 
     doc_ends = jnp.cumsum(doc_lengths)
     inside = (
@@ -333,6 +335,9 @@
     cosine, sine = jnp.cos(angle), jnp.sin(angle)
     cosine = jnp.concatenate([cosine, cosine], axis=1)
     sine = jnp.concatenate([-sine, sine], axis=1)
+    at = jnp.sum(
+        jnp.where(jnp.arange(chips) == context // 2, jnp.asarray(place, jnp.int32), 0)
+    ).astype(jnp.int32)
     chip_of_slot = jnp.sum(
         jnp.where(
             ((jnp.arange(chips) + at) % chips)[:, None] == jnp.arange(chips)[None, :],
@@ -341,18 +346,14 @@
         ),
         axis=1,
     ).astype(jnp.int32)
-    owner = chip_of_slot * 2 + core
+    owner = chip_of_slot * 2 + context % 2
     key_rows = (owner[:, None] * tokens_here + inside[None, :]).reshape(-1).astype(jnp.int32)
     key_orig, _ = locate(key_rows, span_order, doc_ends)
 
-    for _ in range(2):
-        keys_ring.step(*keys_ring.last())
-        query_ring.step(*query_ring.last())
-    keys_ring.step()
-    out_ring.step(*keys_ring.up[1:], *keys_ring.down[1:])
-    query_ring.step()
     mine, theirs = project(keys_ring.finish(), 2, "project_keys")
     theirs = lax.ppermute(theirs, "context", sibling)
+    out_ring.step()
+    mine, theirs = ordered((mine, theirs))
     kv = pl.pallas_call(
         keys_kernel,
         out_shape=jax.ShapeDtypeStruct((tokens_here, 2 * HD), jnp.bfloat16),
@@ -363,11 +364,17 @@
     )(mine, theirs, cosine, sine)
     kv_ring = Ring(kv)
     kv_ring.step()
+    query_ring.step()
+    kv_ring.step()
+    out_ring.step()
+    kv_ring.step()
+    while not query_ring.done():
+        query_ring.step()
+    while not kv_ring.done():
+        kv_ring.step()
+    out_ring.step()
     (mine,) = project(query_ring.finish(), 1, "project_queries")
     theirs = lax.ppermute(mine, "context", sibling)
-    for _ in range(2):
-        kv_ring.step()
-        out_ring.step(*kv_ring.last())
     kv_blocks = kv_ring.finish()
 
     count = chips * tokens_here
@@ -389,6 +396,7 @@
         key_orig[None, :],
         *kv_blocks,
     )
+    (mixed,) = ordered((mixed,))
     mixed_theirs = lax.ppermute(mixed, "context", sibling)
     out_blocks = out_ring.finish()
 
@@ -411,11 +419,11 @@
     return pl.pallas_call(
         functools.partial(sum_kernel, place, chips, groups),
         out_shape=jax.ShapeDtypeStruct((rows_here, n_context * out_block), jnp.bfloat16),
-        in_specs=[smem] + vmem_specs(groups),
+        in_specs=[pl.BlockSpec(memory_space=pl.ANY)] + vmem_specs(groups),
         out_specs=vmem_specs(1)[0],
         compiler_params=compute_params(),
         name="sum",
-    )(where, *arrived)
+    )(token[0], *arrived)
 
 
 def solution(mesh):

time: 104 us -> 119 us (1.14)
  waiting for transfers between devices: 44.1 us -> 51.5 us
  local copies, waits for them, and re-layouts: 5.4 us -> 11.1 us
  Pallas kernels: 7.63 us -> 9.37 us
    ppermute x12, starting transfers between devices: 13.7 us -> 2.05 us  [step(): self.down.append(lax.ppermute(down, 'context', back))]
    ppermute x12, starting transfers between devices: 4.29 us -> 15.7 us  [step(): self.up.append(lax.ppermute(up, 'context', ahead))]
    ppermute x12, waiting for transfers between devices: 6.14 us -> 14 us  [step(): self.down.append(lax.ppermute(down, 'context', back))]
    ppermute x4, waiting for transfers between devices: 0.34 us -> 6.23 us  [step(): lax.ppermute(down[half:], 'context', back)]
    ppermute x3, starting transfers between devices: 8.25 us -> 2.83 us  [per_device(): rows = lax.ppermute(rows, ('context', 'tensor'), member(e, d))]
    ppermute x1, starting transfers between devices: 0.42 us -> 5.24 us  [per_device(): theirs = lax.ppermute(theirs, 'context', sibling)]
    ppermute x4, starting transfers between devices: 5.02 us -> 0.8 us  [step(): lax.ppermute(down[half:], 'context', back)]
    ppermute x4, starting transfers between devices: 1.11 us -> 5.24 us  [step(): lax.ppermute(up[:half], 'context', ahead)]
  transfers between devices with their start and end apart: 41 -> 41, of which waited for: 15 -> 23; matrix products, arithmetic and copies ran while one was open for 5% -> 7% of each run, Pallas kernels for 5% -> 0%
where the time goes in v4:
time: 119 us
  waiting for transfers between devices  51.5 us (43%)
  starting transfers between devices  42.1 us (35%)
  local copies, waits for them, and re-layouts  11.1 us (9%)
  Pallas kernels  9.37 us (8%)
  other arithmetic  4.18 us (4%)
    ppermute x12, waiting for transfers between devices, step(): self.up.append(lax.ppermute(up, 'context', ahead))  16.7 us
    ppermute x12, starting transfers between devices, step(): self.up.append(lax.ppermute(up, 'context', ahead))  15.7 us
    ppermute x12, waiting for transfers between devices, step(): self.down.append(lax.ppermute(down, 'context', back))  14 us
    ppermute x3, waiting for transfers between devices, per_device(): part = lax.ppermute(part, ('context', 'tensor'), member(e, -d))  9.71 us
    ppermute x4, waiting for transfers between devices, step(): lax.ppermute(down[half:], 'context', back)  6.23 us
    unnamed x62, local copies, waits for them, and re-layouts  5.93 us
    ppermute x1, starting transfers between devices, per_device(): theirs = lax.ppermute(theirs, 'context', sibling)  5.24 us
    ppermute x4, starting transfers between devices, step(): lax.ppermute(up[:half], 'context', ahead)  5.24 us
  transfers between devices with their start and end apart: 41, of which 23 were waited for; matrix products, arithmetic and copies ran while one was open for 7% of the time, Pallas kernels for 0%

profile of v4, /device:TPU:1, one launch (start us, length us, event | category | flops | bytes accessed | tf_op | source)
XLA Modules:
  0.0 118.6 jit_solution(14290664474823243216)
XLA Ops:
  2.4 2.6 %collective-permute-start.8 = (bf16[8,64,256]{2,1,0:T(8,128)(2,1)S(1)}, bf16[8,64,256]{2,1,0:T(8,128)(2,1)S(1)}, u32[]{:S(2)}, u32[]{:S(2)}) collective-permute-start(bf16[8,64,256]{2,1,0:T(8,128)(2,1)S(1)} %get-tuple-element.118), channel_id=1, source_target_pairs={{0,3},{1,2},{2,1},{3,0},{4,7},{5,6},{6,5},{7,4},{8,11},{9,10},{10,... | collective-permute-start | bytes 786440 | tf_op jit(solution)/shard_map/ppermute | solution.py:300
  13.4 1.4 %collective-permute-done.2.refs_11_ = bf16[256,256]{1,0:T(8,128)(2,1)S(1)} collective-permute-done((bf16[256,256]{1,0:T(8,128)(2,1)S(1)}, bf16[256,256]{1,0:T(8,128)(2,1)S(1)}, u32[]{:S(2)}, u32[]{:S(2)}) %collective-permute-start.2) | collective-permute-done | bytes 131104 | tf_op jit(solution)/shard_map/ppermute | solution.py:257
  20.1 2.8 %collective-permute-done.4.refs_10_ = bf16[256,256]{1,0:T(8,128)(2,1)S(1)} collective-permute-done((bf16[256,256]{1,0:T(8,128)(2,1)S(1)}, bf16[256,256]{1,0:T(8,128)(2,1)S(1)}, u32[]{:S(2)}, u32[]{:S(2)}) %collective-permute-start.4) | collective-permute-done | bytes 131104 | tf_op jit(solution)/shard_map/ppermute | solution.py:257
  25.7 1.3 %collective-permute-start.18 = (bf16[256,512]{1,0:T(8,128)(2,1)S(1)}, bf16[256,512]{1,0:T(8,128)(2,1)S(1)}, u32[]{:S(2)}, u32[]{:S(2)}) collective-permute-start(bf16[256,512]{1,0:T(8,128)(2,1)S(1)} %collective-permute-done.11.refs_12_), channel_id=1, source_target_pairs={{0,8},{2,10},{8,16},{10,18},{16,24},{18,26},{24,28},{26,30},{28,20... | collective-permute-start | bytes 786440 | tf_op jit(solution)/shard_map/ppermute | solution.py:257
  28.1 5.2 %collective-permute-start.15 = (f32[128,256]{1,0:T(8,128)S(1)}, f32[128,256]{1,0:T(8,128)S(1)}, u32[]{:S(2)}, u32[]{:S(2)}) collective-permute-start(f32[128,256]{1,0:T(8,128)S(1)} %get-tuple-element.147), channel_id=1, source_target_pairs={{0,2},{2,0},{4,6},{6,4},{8,10},{10,8},{12,14},{14,12},{16,18},{18,... | collective-permute-start | bytes 393224 | tf_op jit(solution)/shard_map/ppermute | solution.py:354
  35.3 1.4 %collective-permute-start.16 = (bf16[128,256]{1,0:T(8,128)(2,1)S(1)}, bf16[128,256]{1,0:T(8,128)(2,1)S(1)}, u32[]{:S(2)}, u32[]{:S(2)}) collective-permute-start(bf16[128,256]{1,0:T(8,128)(2,1)S(1)} %keys.1.refs_0_), channel_id=1, source_target_pairs={{0,8},{2,10},{8,16},{10,18},{16,24},{18,26},{24,28},{26,30},{28,20... | collective-permute-start | bytes 196616 | tf_op jit(solution)/shard_map/ppermute | solution.py:257
  36.9 4.3 %collective-permute-done.19.refs_6_ = bf16[256,512]{1,0:T(8,128)(2,1)S(1)} collective-permute-done((bf16[256,512]{1,0:T(8,128)(2,1)S(1)}, bf16[256,512]{1,0:T(8,128)(2,1)S(1)}, u32[]{:S(2)}, u32[]{:S(2)}) %collective-permute-start.19) | collective-permute-done | bytes 262176 | tf_op jit(solution)/shard_map/ppermute | solution.py:258
  41.2 1.6 %collective-permute-done.16.refs_8_ = bf16[128,256]{1,0:T(8,128)(2,1)S(1)} collective-permute-done((bf16[128,256]{1,0:T(8,128)(2,1)S(1)}, bf16[128,256]{1,0:T(8,128)(2,1)S(1)}, u32[]{:S(2)}, u32[]{:S(2)}) %collective-permute-start.16) | collective-permute-done | bytes 65568 | tf_op jit(solution)/shard_map/ppermute | solution.py:257
  42.8 5.4 %collective-permute-done.17.refs_1_ = bf16[128,256]{1,0:T(8,128)(2,1)S(1)} collective-permute-done((bf16[128,256]{1,0:T(8,128)(2,1)S(1)}, bf16[128,256]{1,0:T(8,128)(2,1)S(1)}, u32[]{:S(2)}, u32[]{:S(2)}) %collective-permute-start.17) | collective-permute-done | bytes 65568 | tf_op jit(solution)/shard_map/ppermute | solution.py:258
  61.4 3.1 %collective-permute-done.24.refs_6_ = bf16[128,256]{1,0:T(8,128)(2,1)S(1)} collective-permute-done((bf16[128,256]{1,0:T(8,128)(2,1)S(1)}, bf16[128,256]{1,0:T(8,128)(2,1)S(1)}, u32[]{:S(2)}, u32[]{:S(2)}) %collective-permute-start.24) | collective-permute-done | bytes 65568 | tf_op jit(solution)/shard_map/ppermute | solution.py:257
  64.7 1.4 %copy.31 = s32[256,1]{1,0:T(8,128)} copy(s32[256,1]{0,1:T(1,128)} %bitcast.37) | data formatting | bytes 2048 | tf_op jit(solution)/shard_map/mul | solution.py:39
  67.3 2.0 %collective-permute-done.31.refs_9_ = bf16[128,512]{1,0:T(8,128)(2,1)} collective-permute-done((bf16[128,512]{1,0:T(8,128)(2,1)}, bf16[128,512]{1,0:T(8,128)(2,1)}, u32[]{:S(2)}, u32[]{:S(2)}) %collective-permute-start.31) | collective-permute-done | bytes 131104 | tf_op jit(solution)/shard_map/ppermute | solution.py:263
  70.2 1.7 %project_queries.1.mine_ref = f32[256,512]{1,0:T(8,128)S(1)} custom-call(bf16[8,64,256]{2,1,0:T(8,128)(2,1)S(1)} %get-tuple-element.176.refs_0_, bf16[8,64,256]{2,1,0:T(8,128)(2,1)S(1)} %collective-permute-done.6.refs_1_, bf16[8,64,256]{2,1,0:T(8,128)(2,1)S(1)} %collective-permute-done.7.refs_2_, bf16[8,64,256]{2,1,0:T(8,128)(2,1)S(1)} %collective-permute-done.8.refs_3_, ...), custom_call_target="tpu_custom_call" | custom-call | tf_op jit(solution)/shard_map/project_queries/pallas_call | solution.py:315
  71.9 4.2 %collective-permute-start.32 = (f32[256,512]{1,0:T(8,128)S(1)}, f32[256,512]{1,0:T(8,128)S(1)}, u32[]{:S(2)}, u32[]{:S(2)}) collective-permute-start(f32[256,512]{1,0:T(8,128)S(1)} %project_queries.1.mine_ref), channel_id=1, source_target_pairs={{0,2},{2,0},{4,6},{6,4},{8,10},{10,8},{12,14},{14,12},{16,18},{18,... | collective-permute-start | bytes 1572872 | tf_op jit(solution)/shard_map/ppermute | solution.py:377
  76.6 1.3 %collective-permute-start.33 = (bf16[64,256]{1,0:T(8,128)(2,1)S(1)}, bf16[64,256]{1,0:T(8,128)(2,1)S(1)}, u32[]{:S(2)}, u32[]{:S(2)}) collective-permute-start(bf16[64,256]{1,0:T(8,128)(2,1)S(1)} %slice.36), channel_id=1, source_target_pairs={{0,8},{2,10},{8,16},{10,18},{16,24},{18,26},{24,28},{26,30},{28,20... | collective-permute-start | bytes 98312 | tf_op jit(solution)/shard_map/ppermute | solution.py:262
  79.4 2.1 %collective-permute-done.34.refs_5_ = bf16[64,256]{1,0:T(8,128)(2,1)S(1)} collective-permute-done((bf16[64,256]{1,0:T(8,128)(2,1)S(1)}, bf16[64,256]{1,0:T(8,128)(2,1)S(1)}, u32[]{:S(2)}, u32[]{:S(2)}) %collective-permute-start.34) | collective-permute-done | bytes 32800 | tf_op jit(solution)/shard_map/ppermute | solution.py:263
  81.5 3.5 %attend.1.mine_ref = f32[256,640]{1,0:T(8,128)S(1)} custom-call(f32[256,512]{1,0:T(8,128)S(1)} %project_queries.1.mine_ref, f32[256,512]{1,0:T(8,128)S(1)} %collective-permute-done.32.theirs_ref, f32[256,128]{1,0:T(8,128)S(1)} %get-tuple-element.210.cosine_ref, f32[256,128]{1,0:T(8,128)S(1)} %get-tuple-element.211.sine_ref, s32[256,1]{1,0:T(8,128)S(1)} %copy.32.low_ref, ...), custom_call_target="tpu_custom_call" | custom-call | tf_op jit(solution)/shard_map/attend/pallas_call | solution.py:381
  85.0 2.0 %collective-permute-start.35 = (f32[256,640]{1,0:T(8,128)S(1)}, f32[256,640]{1,0:T(8,128)S(1)}, u32[]{:S(2)}, u32[]{:S(2)}) collective-permute-start(f32[256,640]{1,0:T(8,128)S(1)} %attend.1.mine_ref), channel_id=1, source_target_pairs={{0,2},{2,0},{4,6},{6,4},{8,10},{10,8},{12,14},{14,12},{16,18},{18,... | collective-permute-start | bytes 1966088 | tf_op jit(solution)/shard_map/ppermute | solution.py:400
  88.5 6.6 %collective-permute-done.28.refs_6_ = bf16[512,256]{1,0:T(8,128)(2,1)S(1)} collective-permute-done((bf16[512,256]{1,0:T(8,128)(2,1)}, bf16[512,256]{1,0:T(8,128)(2,1)S(1)}, u32[]{:S(2)}, u32[]{:S(2)}) %collective-permute-start.28) | collective-permute-done | bytes 262176 | tf_op jit(solution)/shard_map/ppermute | solution.py:257
  97.7 2.3 %collective-permute-done.36.refs_4_ = bf16[256,256]{1,0:T(8,128)(2,1)S(1)} collective-permute-done((bf16[256,256]{1,0:T(8,128)(2,1)S(1)}, bf16[256,256]{1,0:T(8,128)(2,1)S(1)}, u32[]{:S(2)}, u32[]{:S(2)}) %collective-permute-start.36) | collective-permute-done | bytes 131104 | tf_op jit(solution)/shard_map/ppermute | solution.py:262
  100.0 1.6 %collective-permute-done.37.refs_5_ = bf16[256,256]{1,0:T(8,128)(2,1)S(1)} collective-permute-done((bf16[256,256]{1,0:T(8,128)(2,1)S(1)}, bf16[256,256]{1,0:T(8,128)(2,1)S(1)}, u32[]{:S(2)}, u32[]{:S(2)}) %collective-permute-start.37) | collective-permute-done | bytes 131104 | tf_op jit(solution)/shard_map/ppermute | solution.py:263
  101.6 2.4 %output.1 = (bf16[8,64,256]{2,1,0:T(8,128)(2,1)S(1)}, bf16[8,64,256]{2,1,0:T(8,128)(2,1)S(1)}, bf16[8,64,256]{2,1,0:T(8,128)(2,1)S(1)}, bf16[8,64,256]{2,1,0:T(8,128)(2,1)S(1)}) custom-call(f32[256,640]{1,0:T(8,128)S(1)} %attend.1.mine_ref, f32[256,640]{1,0:T(8,128)S(1)} %collective-permute-done.35.theirs_ref, bf16[512,256]{1,0:T(8,128)(2,1)S(1)} %copy-done.4, ...), custom_call_target="tpu_custom_call" | custom-call | tf_op jit(solution)/shard_map/output/pallas_call | solution.py:404
  104.9 2.6 %collective-permute-start.39 = (bf16[8,64,256]{2,1,0:T(8,128)(2,1)S(1)}, bf16[8,64,256]{2,1,0:T(8,128)(2,1)S(1)}, u32[]{:S(2)}, u32[]{:S(2)}) collective-permute-start(bf16[8,64,256]{2,1,0:T(8,128)(2,1)S(1)} %get-tuple-element.199), channel_id=1, source_target_pairs={{0,2},{1,3},{2,0},{3,1},{4,6},{5,7},{6,4},{7,5},{8,10},{9,11},{10,... | collective-permute-start | bytes 786440 | tf_op jit(solution)/shard_map/ppermute | solution.py:417
  109.3 8.4 %collective-permute-done.40.refs_3_ = bf16[8,64,256]{2,1,0:T(8,128)(2,1)S(1)} collective-permute-done((bf16[8,64,256]{2,1,0:T(8,128)(2,1)S(1)}, bf16[8,64,256]{2,1,0:T(8,128)(2,1)S(1)}, u32[]{:S(2)}, u32[]{:S(2)}) %collective-permute-start.40) | collective-permute-done | bytes 262176 | tf_op jit(solution)/shard_map/ppermute | solution.py:417
  (168 shorter events, 46.8 us)
Async XLA Ops:
  2.3 16.2 %collective-permute-start.7 = (bf16[8,64,256]{2,1,0:T(8,128)(2,1)S(1)}, bf16[8,64,256]{2,1,0:T(8,128)(2,1)S(1)}, u32[]{:S(2)}, u32[]{:S(2)}) collective-permute-start(bf16[8,64,256]{2,1,0:T(8,128)(2,1)S(1)} %get-tuple-element.118), channel_id=1, source_target_pairs={{0,2},{1,3},{2,0},{3,1},{4,6},{5,7},{6,4},{7,5},{8,10},{9,11},{10,... | collective-permute-start | bytes 786440 | tf_op jit(solution)/shard_map/ppermute | solution.py:300
  2.4 17.6 %collective-permute-start.8 = (bf16[8,64,256]{2,1,0:T(8,128)(2,1)S(1)}, bf16[8,64,256]{2,1,0:T(8,128)(2,1)S(1)}, u32[]{:S(2)}, u32[]{:S(2)}) collective-permute-start(bf16[8,64,256]{2,1,0:T(8,128)(2,1)S(1)} %get-tuple-element.118), channel_id=1, source_target_pairs={{0,3},{1,2},{2,1},{3,0},{4,7},{5,6},{6,5},{7,4},{8,11},{9,10},{10,... | collective-permute-start | bytes 786440 | tf_op jit(solution)/shard_map/ppermute | solution.py:300
  6.5 10.8 %collective-permute-start.6 = (bf16[8,64,256]{2,1,0:T(8,128)(2,1)S(1)}, bf16[8,64,256]{2,1,0:T(8,128)(2,1)S(1)}, u32[]{:S(2)}, u32[]{:S(2)}) collective-permute-start(bf16[8,64,256]{2,1,0:T(8,128)(2,1)S(1)} %get-tuple-element.176.refs_0_), channel_id=1, source_target_pairs={{0,1},{1,0},{2,3},{3,2},{4,5},{5,4},{6,7},{7,6},{8,9},{9,8},{10,11... | collective-permute-start | bytes 786440 | tf_op jit(solution)/shard_map/ppermute | solution.py:300
  14.8 10.9 %collective-permute-start.11 = (bf16[256,512]{1,0:T(8,128)(2,1)S(1)}, bf16[256,512]{1,0:T(8,128)(2,1)S(1)}, u32[]{:S(2)}, u32[]{:S(2)}) collective-permute-start(bf16[256,512]{1,0:T(8,128)(2,1)S(1)} %slice.31.refs_4_), channel_id=1, source_target_pairs={{0,8},{2,10},{8,16},{10,18},{16,24},{18,26},{24,28},{26,30},{28,20... | collective-permute-start | bytes 786440 | tf_op jit(solution)/shard_map/ppermute | solution.py:257
  16.1 9.6 %collective-permute-start.12 = (bf16[256,512]{1,0:T(8,128)(2,1)S(1)}, bf16[256,512]{1,0:T(8,128)(2,1)S(1)}, u32[]{:S(2)}, u32[]{:S(2)}) collective-permute-start(bf16[256,512]{1,0:T(8,128)(2,1)S(1)} %slice.31.refs_4_), channel_id=1, source_target_pairs={{8,0},{10,2},{16,8},{18,10},{24,16},{26,18},{28,24},{30,26},{20,28... | collective-permute-start | bytes 786440 | tf_op jit(solution)/shard_map/ppermute | solution.py:258
  25.7 10.9 %collective-permute-start.18 = (bf16[256,512]{1,0:T(8,128)(2,1)S(1)}, bf16[256,512]{1,0:T(8,128)(2,1)S(1)}, u32[]{:S(2)}, u32[]{:S(2)}) collective-permute-start(bf16[256,512]{1,0:T(8,128)(2,1)S(1)} %collective-permute-done.11.refs_12_), channel_id=1, source_target_pairs={{0,8},{2,10},{8,16},{10,18},{16,24},{18,26},{24,28},{26,30},{28,20... | collective-permute-start | bytes 786440 | tf_op jit(solution)/shard_map/ppermute | solution.py:257
  28.1 7.1 %collective-permute-start.15 = (f32[128,256]{1,0:T(8,128)S(1)}, f32[128,256]{1,0:T(8,128)S(1)}, u32[]{:S(2)}, u32[]{:S(2)}) collective-permute-start(f32[128,256]{1,0:T(8,128)S(1)} %get-tuple-element.147), channel_id=1, source_target_pairs={{0,2},{2,0},{4,6},{6,4},{8,10},{10,8},{12,14},{14,12},{16,18},{18,... | collective-permute-start | bytes 393224 | tf_op jit(solution)/shard_map/ppermute | solution.py:354
  33.4 7.9 %collective-permute-start.19 = (bf16[256,512]{1,0:T(8,128)(2,1)S(1)}, bf16[256,512]{1,0:T(8,128)(2,1)S(1)}, u32[]{:S(2)}, u32[]{:S(2)}) collective-permute-start(bf16[256,512]{1,0:T(8,128)(2,1)S(1)} %collective-permute-done.12.refs_5_), channel_id=1, source_target_pairs={{8,0},{10,2},{16,8},{18,10},{24,16},{26,18},{28,24},{30,26},{20,28... | collective-permute-start | bytes 786440 | tf_op jit(solution)/shard_map/ppermute | solution.py:258
  33.5 18.8 %collective-permute-start.13 = (bf16[512,256]{1,0:T(8,128)(2,1)S(1)}, bf16[512,256]{1,0:T(8,128)(2,1)S(1)}, u32[]{:S(2)}, u32[]{:S(2)}) collective-permute-start(bf16[512,256]{1,0:T(8,128)(2,1)S(1)} %copy-done.3), channel_id=1, source_target_pairs={{0,8},{2,10},{8,16},{10,18},{16,24},{18,26},{24,28},{26,30},{28,20... | collective-permute-start | bytes 786440 | tf_op jit(solution)/shard_map/ppermute | solution.py:257
  35.0 17.5 %collective-permute-start.14 = (bf16[512,256]{1,0:T(8,128)(2,1)S(1)}, bf16[512,256]{1,0:T(8,128)(2,1)S(1)}, u32[]{:S(2)}, u32[]{:S(2)}) collective-permute-start(bf16[512,256]{1,0:T(8,128)(2,1)S(1)} %copy-done.3), channel_id=1, source_target_pairs={{8,0},{10,2},{16,8},{18,10},{24,16},{26,18},{28,24},{30,26},{20,28... | collective-permute-start | bytes 786440 | tf_op jit(solution)/shard_map/ppermute | solution.py:258
  35.3 7.5 %collective-permute-start.16 = (bf16[128,256]{1,0:T(8,128)(2,1)S(1)}, bf16[128,256]{1,0:T(8,128)(2,1)S(1)}, u32[]{:S(2)}, u32[]{:S(2)}) collective-permute-start(bf16[128,256]{1,0:T(8,128)(2,1)S(1)} %keys.1.refs_0_), channel_id=1, source_target_pairs={{0,8},{2,10},{8,16},{10,18},{16,24},{18,26},{24,28},{26,30},{28,20... | collective-permute-start | bytes 196616 | tf_op jit(solution)/shard_map/ppermute | solution.py:257
  36.7 11.6 %collective-permute-start.17 = (bf16[128,256]{1,0:T(8,128)(2,1)S(1)}, bf16[128,256]{1,0:T(8,128)(2,1)S(1)}, u32[]{:S(2)}, u32[]{:S(2)}) collective-permute-start(bf16[128,256]{1,0:T(8,128)(2,1)S(1)} %keys.1.refs_0_), channel_id=1, source_target_pairs={{8,0},{10,2},{16,8},{18,10},{24,16},{26,18},{28,24},{30,26},{20,28... | collective-permute-start | bytes 196616 | tf_op jit(solution)/shard_map/ppermute | solution.py:258
  50.9 6.4 %collective-permute-start.26 = (bf16[256,512]{1,0:T(8,128)(2,1)S(1)}, bf16[256,512]{1,0:T(8,128)(2,1)S(1)}, u32[]{:S(2)}, u32[]{:S(2)}) collective-permute-start(bf16[256,512]{1,0:T(8,128)(2,1)S(1)} %collective-permute-done.18.refs_11_), channel_id=1, source_target_pairs={{0,8},{2,10},{8,16},{10,18},{16,24},{18,26},{24,28},{26,30},{28,20... | collective-permute-start | bytes 786440 | tf_op jit(solution)/shard_map/ppermute | solution.py:257
  52.2 6.5 %collective-permute-start.27 = (bf16[256,512]{1,0:T(8,128)(2,1)S(1)}, bf16[256,512]{1,0:T(8,128)(2,1)S(1)}, u32[]{:S(2)}, u32[]{:S(2)}) collective-permute-start(bf16[256,512]{1,0:T(8,128)(2,1)S(1)} %collective-permute-done.19.refs_6_), channel_id=1, source_target_pairs={{8,0},{10,2},{16,8},{18,10},{24,16},{26,18},{28,24},{30,26},{20,28... | collective-permute-start | bytes 786440 | tf_op jit(solution)/shard_map/ppermute | solution.py:258
  52.5 13.6 %collective-permute-start.20 = (bf16[512,256]{1,0:T(8,128)(2,1)S(1)}, bf16[512,256]{1,0:T(8,128)(2,1)}, u32[]{:S(2)}, u32[]{:S(2)}) collective-permute-start(bf16[512,256]{1,0:T(8,128)(2,1)S(1)} %collective-permute-done.13.refs_8_), channel_id=1, source_target_pairs={{0,8},{2,10},{8,16},{10,18},{16,24},{18,26},{24,28},{26,30},{28,20... | collective-permute-start | bytes 786440 | tf_op jit(solution)/shard_map/ppermute | solution.py:257
  53.9 12.2 %collective-permute-start.21 = (bf16[512,256]{1,0:T(8,128)(2,1)S(1)}, bf16[512,256]{1,0:T(8,128)(2,1)}, u32[]{:S(2)}, u32[]{:S(2)}) collective-permute-start(bf16[512,256]{1,0:T(8,128)(2,1)S(1)} %collective-permute-done.14.refs_1_), channel_id=1, source_target_pairs={{8,0},{10,2},{16,8},{18,10},{24,16},{26,18},{28,24},{30,26},{20,28... | collective-permute-start | bytes 786440 | tf_op jit(solution)/shard_map/ppermute | solution.py:258
  54.8 9.7 %collective-permute-start.24 = (bf16[128,256]{1,0:T(8,128)(2,1)S(1)}, bf16[128,256]{1,0:T(8,128)(2,1)S(1)}, u32[]{:S(2)}, u32[]{:S(2)}) collective-permute-start(bf16[128,256]{1,0:T(8,128)(2,1)S(1)} %collective-permute-done.22.refs_7_), channel_id=1, source_target_pairs={{0,8},{2,10},{8,16},{10,18},{16,24},{18,26},{24,28},{26,30},{28,20... | collective-permute-start | bytes 196616 | tf_op jit(solution)/shard_map/ppermute | solution.py:257
  57.3 8.8 %collective-permute-start.25 = (bf16[128,256]{1,0:T(8,128)(2,1)}, bf16[128,256]{1,0:T(8,128)(2,1)}, u32[]{:S(2)}, u32[]{:S(2)}) collective-permute-start(bf16[128,256]{1,0:T(8,128)(2,1)} %collective-permute-done.23.refs_2_), channel_id=1, source_target_pairs={{8,0},{10,2},{16,8},{18,10},{24,16},{26,18},{28,24},{30,26},{20,28... | collective-permute-start | bytes 196616 | tf_op jit(solution)/shard_map/ppermute | solution.py:258
  59.4 7.9 %collective-permute-start.30 = (bf16[128,512]{1,0:T(8,128)(2,1)}, bf16[128,512]{1,0:T(8,128)(2,1)}, u32[]{:S(2)}, u32[]{:S(2)}) collective-permute-start(bf16[128,512]{1,0:T(8,128)(2,1)} %slice.34), channel_id=1, source_target_pairs={{0,8},{2,10},{8,16},{10,18},{16,24},{18,26},{24,28},{26,30},{28,20... | collective-permute-start | bytes 393224 | tf_op jit(solution)/shard_map/ppermute | solution.py:262
  71.9 9.6 %collective-permute-start.32 = (f32[256,512]{1,0:T(8,128)S(1)}, f32[256,512]{1,0:T(8,128)S(1)}, u32[]{:S(2)}, u32[]{:S(2)}) collective-permute-start(f32[256,512]{1,0:T(8,128)S(1)} %project_queries.1.mine_ref), channel_id=1, source_target_pairs={{0,2},{2,0},{4,6},{6,4},{8,10},{10,8},{12,14},{14,12},{16,18},{18,... | collective-permute-start | bytes 1572872 | tf_op jit(solution)/shard_map/ppermute | solution.py:377
  85.0 16.5 %collective-permute-start.35 = (f32[256,640]{1,0:T(8,128)S(1)}, f32[256,640]{1,0:T(8,128)S(1)}, u32[]{:S(2)}, u32[]{:S(2)}) collective-permute-start(f32[256,640]{1,0:T(8,128)S(1)} %attend.1.mine_ref), channel_id=1, source_target_pairs={{0,2},{2,0},{4,6},{6,4},{8,10},{10,8},{12,14},{14,12},{16,18},{18,... | collective-permute-start | bytes 1966088 | tf_op jit(solution)/shard_map/ppermute | solution.py:400
  87.0 8.1 %collective-permute-start.28 = (bf16[512,256]{1,0:T(8,128)(2,1)}, bf16[512,256]{1,0:T(8,128)(2,1)S(1)}, u32[]{:S(2)}, u32[]{:S(2)}) collective-permute-start(bf16[512,256]{1,0:T(8,128)(2,1)} %collective-permute-done.20.refs_7_), channel_id=1, source_target_pairs={{0,8},{2,10},{8,16},{10,18},{16,24},{18,26},{24,28},{26,30},{28,20... | collective-permute-start | bytes 786440 | tf_op jit(solution)/shard_map/ppermute | solution.py:257
  88.3 7.8 %collective-permute-start.29 = (bf16[512,256]{1,0:T(8,128)(2,1)}, bf16[512,256]{1,0:T(8,128)(2,1)S(1)}, u32[]{:S(2)}, u32[]{:S(2)}) collective-permute-start(bf16[512,256]{1,0:T(8,128)(2,1)} %collective-permute-done.21.refs_2_), channel_id=1, source_target_pairs={{8,0},{10,2},{16,8},{18,10},{24,16},{26,18},{28,24},{30,26},{20,28... | collective-permute-start | bytes 786440 | tf_op jit(solution)/shard_map/ppermute | solution.py:258
  107.5 10.2 %collective-permute-start.40 = (bf16[8,64,256]{2,1,0:T(8,128)(2,1)S(1)}, bf16[8,64,256]{2,1,0:T(8,128)(2,1)S(1)}, u32[]{:S(2)}, u32[]{:S(2)}) collective-permute-start(bf16[8,64,256]{2,1,0:T(8,128)(2,1)S(1)} %get-tuple-element.200), channel_id=1, source_target_pairs={{0,3},{1,2},{2,1},{3,0},{4,7},{5,6},{6,5},{7,4},{8,11},{9,10},{10,... | collective-permute-start | bytes 786440 | tf_op jit(solution)/shard_map/ppermute | solution.py:417
  (48 other events, 286.4 us)

commit v5 on v4

--- a/solution.py
+++ b/solution.py
@@ -11,7 +11,7 @@
 QH_DEV = 4
 SPAN = 64
 HEAD_COLS = QH_DEV * HD
-VMEM_LIMIT = 48 * 1024 * 1024
+VMEM_LIMIT = 24 * 1024 * 1024
 
 rope_theta = 500000.0
 
@@ -281,6 +281,8 @@
 
     keys_ring = Ring(w_qkv[:, HEAD_COLS:])
     keys_ring.step()
+    query_ring = Ring(w_qkv[:, :HEAD_COLS])
+    query_ring.step()
 
     normed_shape = jax.ShapeDtypeStruct((chips, rows_here, block), jnp.bfloat16)
     normed_own, normed_other = pl.pallas_call(
@@ -291,6 +293,7 @@
         compiler_params=compute_params(),
         name="norm",
     )(hidden_rows, norm_gain[None, :])
+    keys_ring.step()
     normed_own, normed_other = ordered((normed_own, normed_other))
     normed = []
     for e in range(2):
@@ -300,15 +303,12 @@
                 rows = lax.ppermute(rows, ("context", "tensor"), member(e, d))
             normed.append(rows)
 
-    keys_ring.step()
-    query_ring = Ring(ordered((w_qkv,))[0][:, :HEAD_COLS])
     query_ring.step()
     keys_ring.step()
-    normed = keys_ring.step(normed)
+    query_ring.step()
     while not keys_ring.done():
-        keys_ring.step()
-    query_ring.step()
-    out_ring = Ring(w_out)
+        normed = keys_ring.step(normed)
+        query_ring.step()
 
     def project(blocks, outs, name):
         columns = blocks[0].shape[1]
@@ -335,23 +335,18 @@
     cosine, sine = jnp.cos(angle), jnp.sin(angle)
     cosine = jnp.concatenate([cosine, cosine], axis=1)
     sine = jnp.concatenate([-sine, sine], axis=1)
-    at = jnp.sum(
-        jnp.where(jnp.arange(chips) == context // 2, jnp.asarray(place, jnp.int32), 0)
-    ).astype(jnp.int32)
-    chip_of_slot = jnp.sum(
-        jnp.where(
-            ((jnp.arange(chips) + at) % chips)[:, None] == jnp.arange(chips)[None, :],
-            jnp.asarray(ring, jnp.int32)[None, :],
-            0,
-        ),
-        axis=1,
-    ).astype(jnp.int32)
-    owner = chip_of_slot * 2 + context % 2
+    at, core = place_of(place)
+    spot = (jnp.arange(chips, dtype=jnp.int32) + at) % chips
+    chip_of_slot = jnp.zeros((chips,), jnp.int32)
+    for i, chip in enumerate(ring):
+        chip_of_slot = jnp.where(spot == i, jnp.int32(chip), chip_of_slot)
+    owner = chip_of_slot * 2 + core
     key_rows = (owner[:, None] * tokens_here + inside[None, :]).reshape(-1).astype(jnp.int32)
     key_orig, _ = locate(key_rows, span_order, doc_ends)
 
     mine, theirs = project(keys_ring.finish(), 2, "project_keys")
     theirs = lax.ppermute(theirs, "context", sibling)
+    out_ring = Ring(w_out)
     out_ring.step()
     mine, theirs = ordered((mine, theirs))
     kv = pl.pallas_call(
@@ -364,17 +359,11 @@
     )(mine, theirs, cosine, sine)
     kv_ring = Ring(kv)
     kv_ring.step()
-    query_ring.step()
-    kv_ring.step()
-    out_ring.step()
-    kv_ring.step()
-    while not query_ring.done():
-        query_ring.step()
-    while not kv_ring.done():
-        kv_ring.step()
-    out_ring.step()
     (mine,) = project(query_ring.finish(), 1, "project_queries")
     theirs = lax.ppermute(mine, "context", sibling)
+    while not kv_ring.done():
+        out_ring.step()
+        kv_ring.step()
     kv_blocks = kv_ring.finish()
 
     count = chips * tokens_here

time: 119 us -> 108 us (0.908)
  waiting for transfers between devices: 51.5 us -> 41.9 us
  starting transfers between devices: 42.1 us -> 46.8 us
  local copies, waits for them, and re-layouts: 11.1 us -> 8.03 us
  other arithmetic: 4.18 us -> 2.21 us
    ppermute x12, waiting for transfers between devices: 16.7 us -> 2.83 us  [step(): self.up.append(lax.ppermute(up, 'context', ahead))]
    ppermute x3, waiting for transfers between devices: 1.07 us -> 10.7 us  [per_device(): rows = lax.ppermute(rows, ('context', 'tensor'), member(e, d))]
    ppermute x12, waiting for transfers between devices: 14 us -> 5.97 us  [step(): self.down.append(lax.ppermute(down, 'context', back))]
    ppermute x3, starting transfers between devices: 2.83 us -> 6.5 us  [per_device(): rows = lax.ppermute(rows, ('context', 'tensor'), member(e, d))]
    ppermute x1, starting transfers between devices: 1.96 us -> 5.31 us  [per_device(): mixed_theirs = lax.ppermute(mixed, 'context', sibling)]
    ppermute x4, waiting for transfers between devices: 3.76 us -> 6.53 us  [step(): lax.ppermute(up[:half], 'context', ahead)]
    ppermute x1, starting transfers between devices: 5.24 us -> 3.05 us  [per_device(): theirs = lax.ppermute(theirs, 'context', sibling)]
    ppermute x4, waiting for transfers between devices: 6.23 us -> 4.22 us  [step(): lax.ppermute(down[half:], 'context', back)]
  transfers between devices with their start and end apart: 41 -> 41, of which waited for: 23 -> 18; matrix products, arithmetic and copies ran while one was open for 7% -> 4% of each run, Pallas kernels for 0% -> 2%
where the time goes in v5:
time: 108 us
  starting transfers between devices  46.8 us (43%)
  waiting for transfers between devices  41.9 us (39%)
  Pallas kernels  8.21 us (8%)
  local copies, waits for them, and re-layouts  8.03 us (7%)
  other arithmetic  2.21 us (2%)
    ppermute x12, starting transfers between devices, step(): self.up.append(lax.ppermute(up, 'context', ahead))  15.5 us
    ppermute x3, waiting for transfers between devices, per_device(): part = lax.ppermute(part, ('context', 'tensor'), member(e, -d))  10.9 us
    ppermute x3, waiting for transfers between devices, per_device(): rows = lax.ppermute(rows, ('context', 'tensor'), member(e, d))  10.7 us
    ppermute x4, waiting for transfers between devices, step(): lax.ppermute(up[:half], 'context', ahead)  6.53 us
    ppermute x3, starting transfers between devices, per_device(): rows = lax.ppermute(rows, ('context', 'tensor'), member(e, d))  6.5 us
    ppermute x12, waiting for transfers between devices, step(): self.down.append(lax.ppermute(down, 'context', back))  5.97 us
    ppermute x4, starting transfers between devices, step(): lax.ppermute(up[:half], 'context', ahead)  5.36 us
    ppermute x1, starting transfers between devices, per_device(): mixed_theirs = lax.ppermute(mixed, 'context', sibling)  5.31 us
  transfers between devices with their start and end apart: 41, of which 18 were waited for; matrix products, arithmetic and copies ran while one was open for 4% of the time, Pallas kernels for 2%

profile of v5, /device:TPU:1, one launch (start us, length us, event | category | flops | bytes accessed | tf_op | source)
XLA Modules:
  0.0 107.7 jit_solution(11922330620727311026)
XLA Ops:
  1.0 2.2 %collective-permute-start = (bf16[256,256]{1,0:T(8,128)(2,1)S(1)}, bf16[256,256]{1,0:T(8,128)(2,1)S(1)}, u32[]{:S(2)}, u32[]{:S(2)}) collective-permute-start(bf16[256,256]{1,0:T(8,128)(2,1)S(1)} %slice.30.refs_4_), channel_id=1, source_target_pairs={{0,8},{2,10},{8,16},{10,18},{16,24},{18,26},{24,28},{26,30},{28,20... | collective-permute-start | bytes 393224 | tf_op jit(solution)/shard_map/ppermute | solution.py:257
  4.1 1.5 %collective-permute-start.4 = (bf16[256,512]{1,0:T(8,128)(2,1)S(1)}, bf16[256,512]{1,0:T(8,128)(2,1)S(1)}, u32[]{:S(2)}, u32[]{:S(2)}) collective-permute-start(bf16[256,512]{1,0:T(8,128)(2,1)S(1)} %slice.31.refs_4_), channel_id=1, source_target_pairs={{0,8},{2,10},{8,16},{10,18},{16,24},{18,26},{24,28},{26,30},{28,20... | collective-permute-start | bytes 786440 | tf_op jit(solution)/shard_map/ppermute | solution.py:257
  9.8 1.8 %collective-permute-done.4.refs_12_ = bf16[256,512]{1,0:T(8,128)(2,1)S(1)} collective-permute-done((bf16[256,512]{1,0:T(8,128)(2,1)S(1)}, bf16[256,512]{1,0:T(8,128)(2,1)S(1)}, u32[]{:S(2)}, u32[]{:S(2)}) %collective-permute-start.4) | collective-permute-done | bytes 262176 | tf_op jit(solution)/shard_map/ppermute | solution.py:257
  17.8 3.9 %collective-permute-start.9 = (bf16[8,64,256]{2,1,0:T(8,128)(2,1)}, bf16[8,64,256]{2,1,0:T(8,128)(2,1)S(1)}, u32[]{:S(2)}, u32[]{:S(2)}) collective-permute-start(bf16[8,64,256]{2,1,0:T(8,128)(2,1)} %get-tuple-element.117), channel_id=1, source_target_pairs={{0,2},{1,3},{2,0},{3,1},{4,6},{5,7},{6,4},{7,5},{8,10},{9,11},{10,... | collective-permute-start | bytes 786440 | tf_op jit(solution)/shard_map/ppermute | solution.py:303
  21.8 2.5 %collective-permute-start.10 = (bf16[8,64,256]{2,1,0:T(8,128)(2,1)}, bf16[8,64,256]{2,1,0:T(8,128)(2,1)S(1)}, u32[]{:S(2)}, u32[]{:S(2)}) collective-permute-start(bf16[8,64,256]{2,1,0:T(8,128)(2,1)} %get-tuple-element.117), channel_id=1, source_target_pairs={{0,3},{1,2},{2,1},{3,0},{4,7},{5,6},{6,5},{7,4},{8,11},{9,10},{10,... | collective-permute-start | bytes 786440 | tf_op jit(solution)/shard_map/ppermute | solution.py:303
  24.5 1.5 %collective-permute-start.13 = (bf16[256,512]{1,0:T(8,128)(2,1)S(1)}, bf16[256,512]{1,0:T(8,128)(2,1)S(1)}, u32[]{:S(2)}, u32[]{:S(2)}) collective-permute-start(bf16[256,512]{1,0:T(8,128)(2,1)S(1)} %collective-permute-done.12.refs_6_), channel_id=1, source_target_pairs={{8,0},{10,2},{16,8},{18,10},{24,16},{26,18},{28,24},{30,26},{20,28... | collective-permute-start | bytes 786440 | tf_op jit(solution)/shard_map/ppermute | solution.py:258
  26.1 10.7 %collective-permute-done.8.refs_1_ = bf16[8,64,256]{2,1,0:T(8,128)(2,1)S(1)} collective-permute-done((bf16[8,64,256]{2,1,0:T(8,128)(2,1)S(1)}, bf16[8,64,256]{2,1,0:T(8,128)(2,1)S(1)}, u32[]{:S(2)}, u32[]{:S(2)}) %collective-permute-start.8) | collective-permute-done | bytes 262176 | tf_op jit(solution)/shard_map/ppermute | solution.py:303
  36.8 1.8 %collective-permute-start.17 = (bf16[128,256]{1,0:T(8,128)(2,1)S(1)}, bf16[128,256]{1,0:T(8,128)(2,1)S(1)}, u32[]{:S(2)}, u32[]{:S(2)}) collective-permute-start(bf16[128,256]{1,0:T(8,128)(2,1)S(1)} %slice.34), channel_id=1, source_target_pairs={{0,8},{2,10},{8,16},{10,18},{16,24},{18,26},{24,28},{26,30},{28,20... | collective-permute-start | bytes 196616 | tf_op jit(solution)/shard_map/ppermute | solution.py:262
  38.6 1.6 %collective-permute-done.17.refs_8_ = bf16[128,256]{1,0:T(8,128)(2,1)S(1)} collective-permute-done((bf16[128,256]{1,0:T(8,128)(2,1)S(1)}, bf16[128,256]{1,0:T(8,128)(2,1)S(1)}, u32[]{:S(2)}, u32[]{:S(2)}) %collective-permute-start.17) | collective-permute-done | bytes 65568 | tf_op jit(solution)/shard_map/ppermute | solution.py:262
  45.1 1.3 %collective-permute-start.15 = (bf16[128,512]{1,0:T(8,128)(2,1)S(1)}, bf16[128,512]{1,0:T(8,128)(2,1)S(1)}, u32[]{:S(2)}, u32[]{:S(2)}) collective-permute-start(bf16[128,512]{1,0:T(8,128)(2,1)S(1)} %slice.32), channel_id=1, source_target_pairs={{0,8},{2,10},{8,16},{10,18},{16,24},{18,26},{24,28},{26,30},{28,20... | collective-permute-start | bytes 393224 | tf_op jit(solution)/shard_map/ppermute | solution.py:262
  47.2 3.1 %collective-permute-start.19 = (f32[128,256]{1,0:T(8,128)S(1)}, f32[128,256]{1,0:T(8,128)S(1)}, u32[]{:S(2)}, u32[]{:S(2)}) collective-permute-start(f32[128,256]{1,0:T(8,128)S(1)} %get-tuple-element.148), channel_id=1, source_target_pairs={{0,2},{2,0},{4,6},{6,4},{8,10},{10,8},{12,14},{14,12},{16,18},{18,... | collective-permute-start | bytes 393224 | tf_op jit(solution)/shard_map/ppermute | solution.py:348
  52.4 1.3 %collective-permute-start.27 = (bf16[512,256]{1,0:T(8,128)(2,1)}, bf16[512,256]{1,0:T(8,128)(2,1)S(1)}, u32[]{:S(2)}, u32[]{:S(2)}) collective-permute-start(bf16[512,256]{1,0:T(8,128)(2,1)} %collective-permute-done.23.refs_8_), channel_id=1, source_target_pairs={{0,8},{2,10},{8,16},{10,18},{16,24},{18,26},{24,28},{26,30},{28,20... | collective-permute-start | bytes 786440 | tf_op jit(solution)/shard_map/ppermute | solution.py:257
  54.1 1.3 %collective-permute-start.22 = (bf16[128,256]{1,0:T(8,128)(2,1)S(1)}, bf16[128,256]{1,0:T(8,128)(2,1)S(1)}, u32[]{:S(2)}, u32[]{:S(2)}) collective-permute-start(bf16[128,256]{1,0:T(8,128)(2,1)S(1)} %keys.1.refs_0_), channel_id=1, source_target_pairs={{0,8},{2,10},{8,16},{10,18},{16,24},{18,26},{24,28},{26,30},{28,20... | collective-permute-start | bytes 196616 | tf_op jit(solution)/shard_map/ppermute | solution.py:257
  56.3 4.2 %collective-permute-start.20 = (f32[256,512]{1,0:T(8,128)S(1)}, f32[256,512]{1,0:T(8,128)S(1)}, u32[]{:S(2)}, u32[]{:S(2)}) collective-permute-start(f32[256,512]{1,0:T(8,128)S(1)} %project_queries.1.mine_ref), channel_id=1, source_target_pairs={{0,2},{2,0},{4,6},{6,4},{8,10},{10,8},{12,14},{14,12},{16,18},{18,... | collective-permute-start | bytes 1572872 | tf_op jit(solution)/shard_map/ppermute | solution.py:363
  63.2 1.3 %collective-permute-start.31 = (bf16[512,256]{1,0:T(8,128)(2,1)S(1)}, bf16[512,256]{1,0:T(8,128)(2,1)S(1)}, u32[]{:S(2)}, u32[]{:S(2)}) collective-permute-start(bf16[512,256]{1,0:T(8,128)(2,1)S(1)} %collective-permute-done.27.refs_7_), channel_id=1, source_target_pairs={{0,8},{2,10},{8,16},{10,18},{16,24},{18,26},{24,28},{26,30},{28,20... | collective-permute-start | bytes 786440 | tf_op jit(solution)/shard_map/ppermute | solution.py:257
  68.7 2.7 %collective-permute-done.32.refs_3_ = bf16[512,256]{1,0:T(8,128)(2,1)S(1)} collective-permute-done((bf16[512,256]{1,0:T(8,128)(2,1)S(1)}, bf16[512,256]{1,0:T(8,128)(2,1)S(1)}, u32[]{:S(2)}, u32[]{:S(2)}) %collective-permute-start.32) | collective-permute-done | bytes 262176 | tf_op jit(solution)/shard_map/ppermute | solution.py:258
  73.8 1.4 %collective-permute-done.33.refs_4_ = bf16[64,256]{1,0:T(8,128)(2,1)S(1)} collective-permute-done((bf16[64,256]{1,0:T(8,128)(2,1)S(1)}, bf16[64,256]{1,0:T(8,128)(2,1)S(1)}, u32[]{:S(2)}, u32[]{:S(2)}) %collective-permute-start.33) | collective-permute-done | bytes 32800 | tf_op jit(solution)/shard_map/ppermute | solution.py:262
  75.2 1.7 %collective-permute-done.34.refs_5_ = bf16[64,256]{1,0:T(8,128)(2,1)S(1)} collective-permute-done((bf16[64,256]{1,0:T(8,128)(2,1)S(1)}, bf16[64,256]{1,0:T(8,128)(2,1)S(1)}, u32[]{:S(2)}, u32[]{:S(2)}) %collective-permute-start.34) | collective-permute-done | bytes 32800 | tf_op jit(solution)/shard_map/ppermute | solution.py:263
  76.8 2.6 %attend.1.mine_ref = f32[256,640]{1,0:T(8,128)S(1)} custom-call(f32[256,512]{1,0:T(8,128)S(1)} %project_queries.1.mine_ref, f32[256,512]{1,0:T(8,128)S(1)} %collective-permute-done.20.theirs_ref, f32[256,128]{1,0:T(8,128)S(1)} %get-tuple-element.206.cosine_ref, f32[256,128]{1,0:T(8,128)S(1)} %get-tuple-element.207.sine_ref, s32[256,1]{1,0:T(8,128)S(1)} %copy.30.low_ref, ...), custom_call_target="tpu_custom_call" | custom-call | tf_op jit(solution)/shard_map/attend/pallas_call | solution.py:370
  79.5 5.3 %collective-permute-start.35 = (f32[256,640]{1,0:T(8,128)S(1)}, f32[256,640]{1,0:T(8,128)S(1)}, u32[]{:S(2)}, u32[]{:S(2)}) collective-permute-start(f32[256,640]{1,0:T(8,128)S(1)} %attend.1.mine_ref), channel_id=1, source_target_pairs={{0,2},{2,0},{4,6},{6,4},{8,10},{10,8},{12,14},{14,12},{16,18},{18,... | collective-permute-start | bytes 1966088 | tf_op jit(solution)/shard_map/ppermute | solution.py:389
  86.4 3.6 %collective-permute-done.36.refs_4_ = bf16[256,256]{1,0:T(8,128)(2,1)S(1)} collective-permute-done((bf16[256,256]{1,0:T(8,128)(2,1)S(1)}, bf16[256,256]{1,0:T(8,128)(2,1)S(1)}, u32[]{:S(2)}, u32[]{:S(2)}) %collective-permute-start.36) | collective-permute-done | bytes 131104 | tf_op jit(solution)/shard_map/ppermute | solution.py:262
  90.6 2.4 %output.1 = (bf16[8,64,256]{2,1,0:T(8,128)(2,1)S(1)}, bf16[8,64,256]{2,1,0:T(8,128)(2,1)S(1)}, bf16[8,64,256]{2,1,0:T(8,128)(2,1)S(1)}, bf16[8,64,256]{2,1,0:T(8,128)(2,1)S(1)}) custom-call(f32[256,640]{1,0:T(8,128)S(1)} %attend.1.mine_ref, f32[256,640]{1,0:T(8,128)S(1)} %collective-permute-done.35.theirs_ref, bf16[512,256]{1,0:T(8,128)(2,1)S(1)} %copy-done.5, ...), custom_call_target="tpu_custom_call" | custom-call | tf_op jit(solution)/shard_map/output/pallas_call | solution.py:393
  95.8 3.9 %collective-permute-done.38.refs_1_ = bf16[8,64,256]{2,1,0:T(8,128)(2,1)S(1)} collective-permute-done((bf16[8,64,256]{2,1,0:T(8,128)(2,1)S(1)}, bf16[8,64,256]{2,1,0:T(8,128)(2,1)S(1)}, u32[]{:S(2)}, u32[]{:S(2)}) %collective-permute-start.38) | collective-permute-done | bytes 262176 | tf_op jit(solution)/shard_map/ppermute | solution.py:406
  99.8 7.0 %collective-permute-done.40.refs_3_ = bf16[8,64,256]{2,1,0:T(8,128)(2,1)S(1)} collective-permute-done((bf16[8,64,256]{2,1,0:T(8,128)(2,1)S(1)}, bf16[8,64,256]{2,1,0:T(8,128)(2,1)S(1)}, u32[]{:S(2)}, u32[]{:S(2)}) %collective-permute-start.40) | collective-permute-done | bytes 262176 | tf_op jit(solution)/shard_map/ppermute | solution.py:406
  (165 shorter events, 36.8 us)
Async XLA Ops:
  4.1 7.4 %collective-permute-start.4 = (bf16[256,512]{1,0:T(8,128)(2,1)S(1)}, bf16[256,512]{1,0:T(8,128)(2,1)S(1)}, u32[]{:S(2)}, u32[]{:S(2)}) collective-permute-start(bf16[256,512]{1,0:T(8,128)(2,1)S(1)} %slice.31.refs_4_), channel_id=1, source_target_pairs={{0,8},{2,10},{8,16},{10,18},{16,24},{18,26},{24,28},{26,30},{28,20... | collective-permute-start | bytes 786440 | tf_op jit(solution)/shard_map/ppermute | solution.py:257
  5.6 6.9 %collective-permute-start.5 = (bf16[256,512]{1,0:T(8,128)(2,1)S(1)}, bf16[256,512]{1,0:T(8,128)(2,1)S(1)}, u32[]{:S(2)}, u32[]{:S(2)}) collective-permute-start(bf16[256,512]{1,0:T(8,128)(2,1)S(1)} %slice.31.refs_4_), channel_id=1, source_target_pairs={{8,0},{10,2},{16,8},{18,10},{24,16},{26,18},{28,24},{30,26},{20,28... | collective-permute-start | bytes 786440 | tf_op jit(solution)/shard_map/ppermute | solution.py:258
  7.3 7.3 %collective-permute-start.2 = (bf16[256,256]{1,0:T(8,128)(2,1)S(1)}, bf16[256,256]{1,0:T(8,128)(2,1)S(1)}, u32[]{:S(2)}, u32[]{:S(2)}) collective-permute-start(bf16[256,256]{1,0:T(8,128)(2,1)S(1)} %collective-permute-done.refs_12_), channel_id=1, source_target_pairs={{0,8},{2,10},{8,16},{10,18},{16,24},{18,26},{24,28},{26,30},{28,20... | collective-permute-start | bytes 393224 | tf_op jit(solution)/shard_map/ppermute | solution.py:257
  8.6 6.8 %collective-permute-start.3 = (bf16[256,256]{1,0:T(8,128)(2,1)S(1)}, bf16[256,256]{1,0:T(8,128)(2,1)S(1)}, u32[]{:S(2)}, u32[]{:S(2)}) collective-permute-start(bf16[256,256]{1,0:T(8,128)(2,1)S(1)} %collective-permute-done.1.refs_5_), channel_id=1, source_target_pairs={{8,0},{10,2},{16,8},{18,10},{24,16},{26,18},{28,24},{30,26},{20,28... | collective-permute-start | bytes 393224 | tf_op jit(solution)/shard_map/ppermute | solution.py:258
  12.6 9.2 %collective-permute-start.11 = (bf16[256,512]{1,0:T(8,128)(2,1)S(1)}, bf16[256,512]{1,0:T(8,128)(2,1)S(1)}, u32[]{:S(2)}, u32[]{:S(2)}) collective-permute-start(bf16[256,512]{1,0:T(8,128)(2,1)S(1)} %collective-permute-done.4.refs_12_), channel_id=1, source_target_pairs={{0,8},{2,10},{8,16},{10,18},{16,24},{18,26},{24,28},{26,30},{28,20... | collective-permute-start | bytes 786440 | tf_op jit(solution)/shard_map/ppermute | solution.py:257
  13.9 10.4 %collective-permute-start.12 = (bf16[256,512]{1,0:T(8,128)(2,1)S(1)}, bf16[256,512]{1,0:T(8,128)(2,1)S(1)}, u32[]{:S(2)}, u32[]{:S(2)}) collective-permute-start(bf16[256,512]{1,0:T(8,128)(2,1)S(1)} %collective-permute-done.5.refs_5_), channel_id=1, source_target_pairs={{8,0},{10,2},{16,8},{18,10},{24,16},{26,18},{28,24},{30,26},{20,28... | collective-permute-start | bytes 786440 | tf_op jit(solution)/shard_map/ppermute | solution.py:258
  15.4 9.0 %collective-permute-start.6 = (bf16[256,256]{1,0:T(8,128)(2,1)S(1)}, bf16[256,256]{1,0:T(8,128)(2,1)S(1)}, u32[]{:S(2)}, u32[]{:S(2)}) collective-permute-start(bf16[256,256]{1,0:T(8,128)(2,1)S(1)} %collective-permute-done.2.refs_11_), channel_id=1, source_target_pairs={{0,8},{2,10},{8,16},{10,18},{16,24},{18,26},{24,28},{26,30},{28,20... | collective-permute-start | bytes 393224 | tf_op jit(solution)/shard_map/ppermute | solution.py:257
  16.7 9.3 %collective-permute-start.7 = (bf16[256,256]{1,0:T(8,128)(2,1)S(1)}, bf16[256,256]{1,0:T(8,128)(2,1)S(1)}, u32[]{:S(2)}, u32[]{:S(2)}) collective-permute-start(bf16[256,256]{1,0:T(8,128)(2,1)S(1)} %collective-permute-done.3.refs_6_), channel_id=1, source_target_pairs={{8,0},{10,2},{16,8},{18,10},{24,16},{26,18},{28,24},{30,26},{20,28... | collective-permute-start | bytes 393224 | tf_op jit(solution)/shard_map/ppermute | solution.py:258
  17.8 18.9 %collective-permute-start.9 = (bf16[8,64,256]{2,1,0:T(8,128)(2,1)}, bf16[8,64,256]{2,1,0:T(8,128)(2,1)S(1)}, u32[]{:S(2)}, u32[]{:S(2)}) collective-permute-start(bf16[8,64,256]{2,1,0:T(8,128)(2,1)} %get-tuple-element.117), channel_id=1, source_target_pairs={{0,2},{1,3},{2,0},{3,1},{4,6},{5,7},{6,4},{7,5},{8,10},{9,11},{10,... | collective-permute-start | bytes 786440 | tf_op jit(solution)/shard_map/ppermute | solution.py:303
  21.8 15.0 %collective-permute-start.10 = (bf16[8,64,256]{2,1,0:T(8,128)(2,1)}, bf16[8,64,256]{2,1,0:T(8,128)(2,1)S(1)}, u32[]{:S(2)}, u32[]{:S(2)}) collective-permute-start(bf16[8,64,256]{2,1,0:T(8,128)(2,1)} %get-tuple-element.117), channel_id=1, source_target_pairs={{0,3},{1,2},{2,1},{3,0},{4,7},{5,6},{6,5},{7,4},{8,11},{9,10},{10,... | collective-permute-start | bytes 786440 | tf_op jit(solution)/shard_map/ppermute | solution.py:303
  24.3 12.4 %collective-permute-start.8 = (bf16[8,64,256]{2,1,0:T(8,128)(2,1)S(1)}, bf16[8,64,256]{2,1,0:T(8,128)(2,1)S(1)}, u32[]{:S(2)}, u32[]{:S(2)}) collective-permute-start(bf16[8,64,256]{2,1,0:T(8,128)(2,1)S(1)} %get-tuple-element.155.refs_0_), channel_id=1, source_target_pairs={{0,1},{1,0},{2,3},{3,2},{4,5},{5,4},{6,7},{7,6},{8,9},{9,8},{10,11... | collective-permute-start | bytes 786440 | tf_op jit(solution)/shard_map/ppermute | solution.py:303
  24.5 14.2 %collective-permute-start.13 = (bf16[256,512]{1,0:T(8,128)(2,1)S(1)}, bf16[256,512]{1,0:T(8,128)(2,1)S(1)}, u32[]{:S(2)}, u32[]{:S(2)}) collective-permute-start(bf16[256,512]{1,0:T(8,128)(2,1)S(1)} %collective-permute-done.12.refs_6_), channel_id=1, source_target_pairs={{8,0},{10,2},{16,8},{18,10},{24,16},{26,18},{28,24},{30,26},{20,28... | collective-permute-start | bytes 786440 | tf_op jit(solution)/shard_map/ppermute | solution.py:258
  26.0 12.6 %collective-permute-start.14 = (bf16[256,512]{1,0:T(8,128)(2,1)S(1)}, bf16[256,512]{1,0:T(8,128)(2,1)S(1)}, u32[]{:S(2)}, u32[]{:S(2)}) collective-permute-start(bf16[256,512]{1,0:T(8,128)(2,1)S(1)} %collective-permute-done.11.refs_11_), channel_id=1, source_target_pairs={{0,8},{2,10},{8,16},{10,18},{16,24},{18,26},{24,28},{26,30},{28,20... | collective-permute-start | bytes 786440 | tf_op jit(solution)/shard_map/ppermute | solution.py:257
  42.3 10.1 %collective-permute-start.23 = (bf16[512,256]{1,0:T(8,128)(2,1)}, bf16[512,256]{1,0:T(8,128)(2,1)}, u32[]{:S(2)}, u32[]{:S(2)}) collective-permute-start(bf16[512,256]{1,0:T(8,128)(2,1)} %refs_0_.1), channel_id=1, source_target_pairs={{0,8},{2,10},{8,16},{10,18},{16,24},{18,26},{24,28},{26,30},{28,20... | collective-permute-start | bytes 786440 | tf_op jit(solution)/shard_map/ppermute | solution.py:257
  43.6 8.8 %collective-permute-start.24 = (bf16[512,256]{1,0:T(8,128)(2,1)}, bf16[512,256]{1,0:T(8,128)(2,1)}, u32[]{:S(2)}, u32[]{:S(2)}) collective-permute-start(bf16[512,256]{1,0:T(8,128)(2,1)} %refs_0_.1), channel_id=1, source_target_pairs={{8,0},{10,2},{16,8},{18,10},{24,16},{26,18},{28,24},{30,26},{20,28... | collective-permute-start | bytes 786440 | tf_op jit(solution)/shard_map/ppermute | solution.py:258
  45.1 6.3 %collective-permute-start.15 = (bf16[128,512]{1,0:T(8,128)(2,1)S(1)}, bf16[128,512]{1,0:T(8,128)(2,1)S(1)}, u32[]{:S(2)}, u32[]{:S(2)}) collective-permute-start(bf16[128,512]{1,0:T(8,128)(2,1)S(1)} %slice.32), channel_id=1, source_target_pairs={{0,8},{2,10},{8,16},{10,18},{16,24},{18,26},{24,28},{26,30},{28,20... | collective-permute-start | bytes 393224 | tf_op jit(solution)/shard_map/ppermute | solution.py:262
  52.4 10.8 %collective-permute-start.27 = (bf16[512,256]{1,0:T(8,128)(2,1)}, bf16[512,256]{1,0:T(8,128)(2,1)S(1)}, u32[]{:S(2)}, u32[]{:S(2)}) collective-permute-start(bf16[512,256]{1,0:T(8,128)(2,1)} %collective-permute-done.23.refs_8_), channel_id=1, source_target_pairs={{0,8},{2,10},{8,16},{10,18},{16,24},{18,26},{24,28},{26,30},{28,20... | collective-permute-start | bytes 786440 | tf_op jit(solution)/shard_map/ppermute | solution.py:257
  53.7 9.5 %collective-permute-start.28 = (bf16[512,256]{1,0:T(8,128)(2,1)}, bf16[512,256]{1,0:T(8,128)(2,1)S(1)}, u32[]{:S(2)}, u32[]{:S(2)}) collective-permute-start(bf16[512,256]{1,0:T(8,128)(2,1)} %collective-permute-done.24.refs_1_), channel_id=1, source_target_pairs={{8,0},{10,2},{16,8},{18,10},{24,16},{26,18},{28,24},{30,26},{20,28... | collective-permute-start | bytes 786440 | tf_op jit(solution)/shard_map/ppermute | solution.py:258
  54.0 6.5 %collective-permute-start.21 = (bf16[128,256]{1,0:T(8,128)(2,1)S(1)}, bf16[128,256]{1,0:T(8,128)(2,1)S(1)}, u32[]{:S(2)}, u32[]{:S(2)}) collective-permute-start(bf16[128,256]{1,0:T(8,128)(2,1)S(1)} %keys.1.refs_0_), channel_id=1, source_target_pairs={{8,0},{10,2},{16,8},{18,10},{24,16},{26,18},{28,24},{30,26},{20,28... | collective-permute-start | bytes 196616 | tf_op jit(solution)/shard_map/ppermute | solution.py:258
  54.1 6.3 %collective-permute-start.22 = (bf16[128,256]{1,0:T(8,128)(2,1)S(1)}, bf16[128,256]{1,0:T(8,128)(2,1)S(1)}, u32[]{:S(2)}, u32[]{:S(2)}) collective-permute-start(bf16[128,256]{1,0:T(8,128)(2,1)S(1)} %keys.1.refs_0_), channel_id=1, source_target_pairs={{0,8},{2,10},{8,16},{10,18},{16,24},{18,26},{24,28},{26,30},{28,20... | collective-permute-start | bytes 196616 | tf_op jit(solution)/shard_map/ppermute | solution.py:257
  56.3 17.5 %collective-permute-start.20 = (f32[256,512]{1,0:T(8,128)S(1)}, f32[256,512]{1,0:T(8,128)S(1)}, u32[]{:S(2)}, u32[]{:S(2)}) collective-permute-start(f32[256,512]{1,0:T(8,128)S(1)} %project_queries.1.mine_ref), channel_id=1, source_target_pairs={{0,2},{2,0},{4,6},{6,4},{8,10},{10,8},{12,14},{14,12},{16,18},{18,... | collective-permute-start | bytes 1572872 | tf_op jit(solution)/shard_map/ppermute | solution.py:363
  79.5 11.2 %collective-permute-start.35 = (f32[256,640]{1,0:T(8,128)S(1)}, f32[256,640]{1,0:T(8,128)S(1)}, u32[]{:S(2)}, u32[]{:S(2)}) collective-permute-start(f32[256,640]{1,0:T(8,128)S(1)} %attend.1.mine_ref), channel_id=1, source_target_pairs={{0,2},{2,0},{4,6},{6,4},{8,10},{10,8},{12,14},{14,12},{16,18},{18,... | collective-permute-start | bytes 1966088 | tf_op jit(solution)/shard_map/ppermute | solution.py:389
  93.0 6.7 %collective-permute-start.38 = (bf16[8,64,256]{2,1,0:T(8,128)(2,1)S(1)}, bf16[8,64,256]{2,1,0:T(8,128)(2,1)S(1)}, u32[]{:S(2)}, u32[]{:S(2)}) collective-permute-start(bf16[8,64,256]{2,1,0:T(8,128)(2,1)S(1)} %get-tuple-element.194), channel_id=1, source_target_pairs={{0,1},{1,0},{2,3},{3,2},{4,5},{5,4},{6,7},{7,6},{8,9},{9,8},{10,11... | collective-permute-start | bytes 786440 | tf_op jit(solution)/shard_map/ppermute | solution.py:406
  95.4 11.4 %collective-permute-start.40 = (bf16[8,64,256]{2,1,0:T(8,128)(2,1)S(1)}, bf16[8,64,256]{2,1,0:T(8,128)(2,1)S(1)}, u32[]{:S(2)}, u32[]{:S(2)}) collective-permute-start(bf16[8,64,256]{2,1,0:T(8,128)(2,1)S(1)} %get-tuple-element.196), channel_id=1, source_target_pairs={{0,3},{1,2},{2,1},{3,0},{4,7},{5,6},{6,5},{7,4},{8,11},{9,10},{10,... | collective-permute-start | bytes 786440 | tf_op jit(solution)/shard_map/ppermute | solution.py:406
  (48 other events, 205.5 us)

commit v6 on v5

--- a/solution.py
+++ b/solution.py
@@ -281,8 +281,6 @@
 
     keys_ring = Ring(w_qkv[:, HEAD_COLS:])
     keys_ring.step()
-    query_ring = Ring(w_qkv[:, :HEAD_COLS])
-    query_ring.step()
 
     normed_shape = jax.ShapeDtypeStruct((chips, rows_here, block), jnp.bfloat16)
     normed_own, normed_other = pl.pallas_call(
@@ -293,7 +291,6 @@
         compiler_params=compute_params(),
         name="norm",
     )(hidden_rows, norm_gain[None, :])
-    keys_ring.step()
     normed_own, normed_other = ordered((normed_own, normed_other))
     normed = []
     for e in range(2):
@@ -303,12 +300,14 @@
                 rows = lax.ppermute(rows, ("context", "tensor"), member(e, d))
             normed.append(rows)
 
+    query_ring = Ring(w_qkv[:, :HEAD_COLS])
     query_ring.step()
     keys_ring.step()
     query_ring.step()
+    normed = keys_ring.step(normed)
+    query_ring.step()
     while not keys_ring.done():
-        normed = keys_ring.step(normed)
-        query_ring.step()
+        keys_ring.step()
 
     def project(blocks, outs, name):
         columns = blocks[0].shape[1]
@@ -346,6 +345,7 @@
 
     mine, theirs = project(keys_ring.finish(), 2, "project_keys")
     theirs = lax.ppermute(theirs, "context", sibling)
+    query_ring.step()
     out_ring = Ring(w_out)
     out_ring.step()
     mine, theirs = ordered((mine, theirs))
@@ -362,8 +362,8 @@
     (mine,) = project(query_ring.finish(), 1, "project_queries")
     theirs = lax.ppermute(mine, "context", sibling)
     while not kv_ring.done():
+        kv_ring.step()
         out_ring.step()
-        kv_ring.step()
     kv_blocks = kv_ring.finish()
 
     count = chips * tokens_here

time: 108 us -> 103 us (0.954)
  starting transfers between devices: 46.8 us -> 39.5 us
  waiting for transfers between devices: 41.9 us -> 45.3 us
  local copies, waits for them, and re-layouts: 8.03 us -> 6.47 us
    ppermute x4, waiting for transfers between devices: 6.53 us -> 13.5 us  [step(): lax.ppermute(up[:half], 'context', ahead)]
    ppermute x3, waiting for transfers between devices: 10.7 us -> 3.99 us  [per_device(): rows = lax.ppermute(rows, ('context', 'tensor'), member(e, d))]
    ppermute x12, starting transfers between devices: 3.12 us -> 7.47 us  [step(): self.down.append(lax.ppermute(down, 'context', back))]
    ppermute x1, starting transfers between devices: 5.31 us -> 2.26 us  [per_device(): mixed_theirs = lax.ppermute(mixed, 'context', sibling)]
    ppermute x3, starting transfers between devices: 6.5 us -> 3.52 us  [per_device(): rows = lax.ppermute(rows, ('context', 'tensor'), member(e, d))]
    ppermute x12, starting transfers between devices: 15.5 us -> 13.1 us  [step(): self.up.append(lax.ppermute(up, 'context', ahead))]
    ppermute x12, waiting for transfers between devices: 2.83 us -> 4.72 us  [step(): self.up.append(lax.ppermute(up, 'context', ahead))]
    ppermute x4, waiting for transfers between devices: 4.22 us -> 5.93 us  [step(): lax.ppermute(down[half:], 'context', back)]
  transfers between devices with their start and end apart: 41 -> 41, of which waited for: 18 -> 17; matrix products, arithmetic and copies ran while one was open for 4% -> 2% of each run, Pallas kernels for 2% -> 6%
where the time goes in v6:
time: 103 us; the launch traced here: 102 us
  waiting for transfers between devices  45.3 us (44%)
  starting transfers between devices  39.5 us (38%)
  Pallas kernels  9.11 us (9%)
  local copies, waits for them, and re-layouts  6.47 us (6%)
  other arithmetic  1.47 us (1%)
    ppermute x4, waiting for transfers between devices, step(): lax.ppermute(up[:half], 'context', ahead)  13.5 us
    ppermute x12, starting transfers between devices, step(): self.up.append(lax.ppermute(up, 'context', ahead))  13.1 us
    ppermute x3, waiting for transfers between devices, per_device(): part = lax.ppermute(part, ('context', 'tensor'), member(e, -d))  10.9 us
    ppermute x12, starting transfers between devices, step(): self.down.append(lax.ppermute(down, 'context', back))  7.47 us
    ppermute x12, waiting for transfers between devices, step(): self.down.append(lax.ppermute(down, 'context', back))  6.26 us
    ppermute x4, waiting for transfers between devices, step(): lax.ppermute(down[half:], 'context', back)  5.93 us
    ppermute x12, waiting for transfers between devices, step(): self.up.append(lax.ppermute(up, 'context', ahead))  4.72 us
    unnamed x48, local copies, waits for them, and re-layouts  4.71 us
  transfers between devices with their start and end apart: 41, of which 17 were waited for; matrix products, arithmetic and copies ran while one was open for 2% of the time, Pallas kernels for 6%

profile of v6, /device:TPU:1, one launch (start us, length us, event | category | flops | bytes accessed | tf_op | source)
XLA Modules:
  0.0 102.3 jit_solution(8256617029044603783)
XLA Ops:
  0.9 2.2 %collective-permute-start = (bf16[256,256]{1,0:T(8,128)(2,1)S(1)}, bf16[256,256]{1,0:T(8,128)(2,1)S(1)}, u32[]{:S(2)}, u32[]{:S(2)}) collective-permute-start(bf16[256,256]{1,0:T(8,128)(2,1)S(1)} %slice.30.refs_4_), channel_id=1, source_target_pairs={{0,8},{2,10},{8,16},{10,18},{16,24},{18,26},{24,28},{26,30},{28,20... | collective-permute-start | bytes 393224 | tf_op jit(solution)/shard_map/ppermute | solution.py:257
  5.5 1.8 %collective-permute-start.7 = (bf16[256,512]{1,0:T(8,128)(2,1)S(1)}, bf16[256,512]{1,0:T(8,128)(2,1)S(1)}, u32[]{:S(2)}, u32[]{:S(2)}) collective-permute-start(bf16[256,512]{1,0:T(8,128)(2,1)S(1)} %slice.31.refs_4_), channel_id=1, source_target_pairs={{0,8},{2,10},{8,16},{10,18},{16,24},{18,26},{24,28},{26,30},{28,20... | collective-permute-start | bytes 786440 | tf_op jit(solution)/shard_map/ppermute | solution.py:257
  9.7 2.5 %collective-permute-start.6 = (bf16[8,64,256]{2,1,0:T(8,128)(2,1)S(1)}, bf16[8,64,256]{2,1,0:T(8,128)(2,1)S(1)}, u32[]{:S(2)}, u32[]{:S(2)}) collective-permute-start(bf16[8,64,256]{2,1,0:T(8,128)(2,1)S(1)} %get-tuple-element.111), channel_id=1, source_target_pairs={{0,3},{1,2},{2,1},{3,0},{4,7},{5,6},{6,5},{7,4},{8,11},{9,10},{10,... | collective-permute-start | bytes 786440 | tf_op jit(solution)/shard_map/ppermute | solution.py:300
  14.8 2.6 %collective-permute-done.2.refs_11_ = bf16[256,256]{1,0:T(8,128)(2,1)S(1)} collective-permute-done((bf16[256,256]{1,0:T(8,128)(2,1)S(1)}, bf16[256,256]{1,0:T(8,128)(2,1)S(1)}, u32[]{:S(2)}, u32[]{:S(2)}) %collective-permute-start.2) | collective-permute-done | bytes 131104 | tf_op jit(solution)/shard_map/ppermute | solution.py:257
  20.1 4.0 %collective-permute-done.4.refs_1_ = bf16[8,64,256]{2,1,0:T(8,128)(2,1)S(1)} collective-permute-done((bf16[8,64,256]{2,1,0:T(8,128)(2,1)S(1)}, bf16[8,64,256]{2,1,0:T(8,128)(2,1)S(1)}, u32[]{:S(2)}, u32[]{:S(2)}) %collective-permute-start.4) | collective-permute-done | bytes 262176 | tf_op jit(solution)/shard_map/ppermute | solution.py:300
  24.1 2.0 %collective-permute-start.13 = (bf16[256,256]{1,0:T(8,128)(2,1)S(1)}, bf16[256,256]{1,0:T(8,128)(2,1)S(1)}, u32[]{:S(2)}, u32[]{:S(2)}) collective-permute-start(bf16[256,256]{1,0:T(8,128)(2,1)S(1)} %collective-permute-done.3.refs_6_), channel_id=1, source_target_pairs={{8,0},{10,2},{16,8},{18,10},{24,16},{26,18},{28,24},{30,26},{20,28... | collective-permute-start | bytes 393224 | tf_op jit(solution)/shard_map/ppermute | solution.py:258
  26.2 1.4 %collective-permute-start.11 = (bf16[256,512]{1,0:T(8,128)(2,1)S(1)}, bf16[256,512]{1,0:T(8,128)(2,1)S(1)}, u32[]{:S(2)}, u32[]{:S(2)}) collective-permute-start(bf16[256,512]{1,0:T(8,128)(2,1)S(1)} %collective-permute-done.9.refs_6_), channel_id=1, source_target_pairs={{8,0},{10,2},{16,8},{18,10},{24,16},{26,18},{28,24},{30,26},{20,28... | collective-permute-start | bytes 786440 | tf_op jit(solution)/shard_map/ppermute | solution.py:258
  27.8 1.9 %collective-permute-done.13.refs_7_ = bf16[256,256]{1,0:T(8,128)(2,1)S(1)} collective-permute-done((bf16[256,256]{1,0:T(8,128)(2,1)S(1)}, bf16[256,256]{1,0:T(8,128)(2,1)S(1)}, u32[]{:S(2)}, u32[]{:S(2)}) %collective-permute-start.13) | collective-permute-done | bytes 131104 | tf_op jit(solution)/shard_map/ppermute | solution.py:258
  30.4 1.4 %collective-permute-start.15 = (bf16[128,256]{1,0:T(8,128)(2,1)S(1)}, bf16[128,256]{1,0:T(8,128)(2,1)S(1)}, u32[]{:S(2)}, u32[]{:S(2)}) collective-permute-start(bf16[128,256]{1,0:T(8,128)(2,1)S(1)} %slice.32), channel_id=1, source_target_pairs={{0,8},{2,10},{8,16},{10,18},{16,24},{18,26},{24,28},{26,30},{28,20... | collective-permute-start | bytes 196616 | tf_op jit(solution)/shard_map/ppermute | solution.py:262
  32.4 5.0 %collective-permute-done.15.refs_8_ = bf16[128,256]{1,0:T(8,128)(2,1)S(1)} collective-permute-done((bf16[128,256]{1,0:T(8,128)(2,1)S(1)}, bf16[128,256]{1,0:T(8,128)(2,1)S(1)}, u32[]{:S(2)}, u32[]{:S(2)}) %collective-permute-start.15) | collective-permute-done | bytes 65568 | tf_op jit(solution)/shard_map/ppermute | solution.py:262
  38.6 1.6 %collective-permute-start.19 = (f32[128,256]{1,0:T(8,128)}, f32[128,256]{1,0:T(8,128)}, u32[]{:S(2)}, u32[]{:S(2)}) collective-permute-start(f32[128,256]{1,0:T(8,128)} %get-tuple-element.148), channel_id=1, source_target_pairs={{0,2},{2,0},{4,6},{6,4},{8,10},{10,8},{12,14},{14,12},{16,18},{18,... | collective-permute-start | bytes 393224 | tf_op jit(solution)/shard_map/ppermute | solution.py:347
  45.3 1.4 %collective-permute-start.21 = (bf16[128,256]{1,0:T(8,128)(2,1)S(1)}, bf16[128,256]{1,0:T(8,128)(2,1)S(1)}, u32[]{:S(2)}, u32[]{:S(2)}) collective-permute-start(bf16[128,256]{1,0:T(8,128)(2,1)S(1)} %keys.1.refs_0_), channel_id=1, source_target_pairs={{8,0},{10,2},{16,8},{18,10},{24,16},{26,18},{28,24},{30,26},{20,28... | collective-permute-start | bytes 196616 | tf_op jit(solution)/shard_map/ppermute | solution.py:258
  47.5 5.1 %collective-permute-done.18.refs_9_ = bf16[128,512]{1,0:T(8,128)(2,1)S(1)} collective-permute-done((bf16[128,512]{1,0:T(8,128)(2,1)S(1)}, bf16[128,512]{1,0:T(8,128)(2,1)S(1)}, u32[]{:S(2)}, u32[]{:S(2)}) %collective-permute-start.18) | collective-permute-done | bytes 131104 | tf_op jit(solution)/shard_map/ppermute | solution.py:263
  52.6 1.4 %collective-permute-done.21.refs_1_ = bf16[128,256]{1,0:T(8,128)(2,1)S(1)} collective-permute-done((bf16[128,256]{1,0:T(8,128)(2,1)S(1)}, bf16[128,256]{1,0:T(8,128)(2,1)S(1)}, u32[]{:S(2)}, u32[]{:S(2)}) %collective-permute-start.21) | collective-permute-done | bytes 65568 | tf_op jit(solution)/shard_map/ppermute | solution.py:258
  57.4 2.7 %collective-permute-start.20 = (f32[256,512]{1,0:T(8,128)S(1)}, f32[256,512]{1,0:T(8,128)S(1)}, u32[]{:S(2)}, u32[]{:S(2)}) collective-permute-start(f32[256,512]{1,0:T(8,128)S(1)} %project_queries.1.mine_ref), channel_id=1, source_target_pairs={{0,2},{2,0},{4,6},{6,4},{8,10},{10,8},{12,14},{14,12},{16,18},{18,... | collective-permute-start | bytes 1572872 | tf_op jit(solution)/shard_map/ppermute | solution.py:363
  61.6 2.8 %collective-permute-done.23.refs_2_ = bf16[128,256]{1,0:T(8,128)(2,1)S(1)} collective-permute-done((bf16[128,256]{1,0:T(8,128)(2,1)S(1)}, bf16[128,256]{1,0:T(8,128)(2,1)S(1)}, u32[]{:S(2)}, u32[]{:S(2)}) %collective-permute-start.23) | collective-permute-done | bytes 65568 | tf_op jit(solution)/shard_map/ppermute | solution.py:258
  69.4 5.0 %collective-permute-done.31.refs_4_ = bf16[64,256]{1,0:T(8,128)(2,1)S(1)} collective-permute-done((bf16[64,256]{1,0:T(8,128)(2,1)S(1)}, bf16[64,256]{1,0:T(8,128)(2,1)S(1)}, u32[]{:S(2)}, u32[]{:S(2)}) %collective-permute-start.31) | collective-permute-done | bytes 32800 | tf_op jit(solution)/shard_map/ppermute | solution.py:262
  74.4 2.6 %attend.1.mine_ref = f32[256,640]{1,0:T(8,128)S(1)} custom-call(f32[256,512]{1,0:T(8,128)S(1)} %project_queries.1.mine_ref, f32[256,512]{1,0:T(8,128)S(1)} %collective-permute-done.20.theirs_ref, f32[256,128]{1,0:T(8,128)S(1)} %get-tuple-element.206.cosine_ref, f32[256,128]{1,0:T(8,128)S(1)} %get-tuple-element.207.sine_ref, s32[256,1]{1,0:T(8,128)S(1)} %copy.30.low_ref, ...), custom_call_target="tpu_custom_call" | custom-call | tf_op jit(solution)/shard_map/attend/pallas_call | solution.py:370
  77.0 2.3 %collective-permute-start.35 = (f32[256,640]{1,0:T(8,128)S(1)}, f32[256,640]{1,0:T(8,128)S(1)}, u32[]{:S(2)}, u32[]{:S(2)}) collective-permute-start(f32[256,640]{1,0:T(8,128)S(1)} %attend.1.mine_ref), channel_id=1, source_target_pairs={{0,2},{2,0},{4,6},{6,4},{8,10},{10,8},{12,14},{14,12},{16,18},{18,... | collective-permute-start | bytes 1966088 | tf_op jit(solution)/shard_map/ppermute | solution.py:389
  80.9 3.6 %collective-permute-done.36.refs_4_ = bf16[256,256]{1,0:T(8,128)(2,1)S(1)} collective-permute-done((bf16[256,256]{1,0:T(8,128)(2,1)S(1)}, bf16[256,256]{1,0:T(8,128)(2,1)S(1)}, u32[]{:S(2)}, u32[]{:S(2)}) %collective-permute-start.36) | collective-permute-done | bytes 131104 | tf_op jit(solution)/shard_map/ppermute | solution.py:262
  85.3 2.4 %output.1 = (bf16[8,64,256]{2,1,0:T(8,128)(2,1)S(1)}, bf16[8,64,256]{2,1,0:T(8,128)(2,1)S(1)}, bf16[8,64,256]{2,1,0:T(8,128)(2,1)S(1)}, bf16[8,64,256]{2,1,0:T(8,128)(2,1)S(1)}) custom-call(f32[256,640]{1,0:T(8,128)S(1)} %attend.1.mine_ref, f32[256,640]{1,0:T(8,128)S(1)} %collective-permute-done.35.theirs_ref, bf16[512,256]{1,0:T(8,128)(2,1)S(1)} %copy-done.6, ...), custom_call_target="tpu_custom_call" | custom-call | tf_op jit(solution)/shard_map/output/pallas_call | solution.py:393
  88.7 1.4 %collective-permute-start.39 = (bf16[8,64,256]{2,1,0:T(8,128)(2,1)S(1)}, bf16[8,64,256]{2,1,0:T(8,128)(2,1)S(1)}, u32[]{:S(2)}, u32[]{:S(2)}) collective-permute-start(bf16[8,64,256]{2,1,0:T(8,128)(2,1)S(1)} %get-tuple-element.195), channel_id=1, source_target_pairs={{0,2},{1,3},{2,0},{3,1},{4,6},{5,7},{6,4},{7,5},{8,10},{9,11},{10,... | collective-permute-start | bytes 786440 | tf_op jit(solution)/shard_map/ppermute | solution.py:406
  90.5 3.9 %collective-permute-done.38.refs_1_ = bf16[8,64,256]{2,1,0:T(8,128)(2,1)S(1)} collective-permute-done((bf16[8,64,256]{2,1,0:T(8,128)(2,1)S(1)}, bf16[8,64,256]{2,1,0:T(8,128)(2,1)S(1)}, u32[]{:S(2)}, u32[]{:S(2)}) %collective-permute-start.38) | collective-permute-done | bytes 262176 | tf_op jit(solution)/shard_map/ppermute | solution.py:406
  94.5 7.0 %collective-permute-done.40.refs_3_ = bf16[8,64,256]{2,1,0:T(8,128)(2,1)S(1)} collective-permute-done((bf16[8,64,256]{2,1,0:T(8,128)(2,1)S(1)}, bf16[8,64,256]{2,1,0:T(8,128)(2,1)S(1)}, u32[]{:S(2)}, u32[]{:S(2)}) %collective-permute-start.40) | collective-permute-done | bytes 262176 | tf_op jit(solution)/shard_map/ppermute | solution.py:406
  (151 shorter events, 34.2 us)
Async XLA Ops:
  0.9 8.7 %collective-permute-start = (bf16[256,256]{1,0:T(8,128)(2,1)S(1)}, bf16[256,256]{1,0:T(8,128)(2,1)S(1)}, u32[]{:S(2)}, u32[]{:S(2)}) collective-permute-start(bf16[256,256]{1,0:T(8,128)(2,1)S(1)} %slice.30.refs_4_), channel_id=1, source_target_pairs={{0,8},{2,10},{8,16},{10,18},{16,24},{18,26},{24,28},{26,30},{28,20... | collective-permute-start | bytes 393224 | tf_op jit(solution)/shard_map/ppermute | solution.py:257
  3.1 9.1 %collective-permute-start.1 = (bf16[256,256]{1,0:T(8,128)(2,1)S(1)}, bf16[256,256]{1,0:T(8,128)(2,1)S(1)}, u32[]{:S(2)}, u32[]{:S(2)}) collective-permute-start(bf16[256,256]{1,0:T(8,128)(2,1)S(1)} %slice.30.refs_4_), channel_id=1, source_target_pairs={{8,0},{10,2},{16,8},{18,10},{24,16},{26,18},{28,24},{30,26},{20,28... | collective-permute-start | bytes 393224 | tf_op jit(solution)/shard_map/ppermute | solution.py:258
  4.5 19.6 %collective-permute-start.5 = (bf16[8,64,256]{2,1,0:T(8,128)(2,1)S(1)}, bf16[8,64,256]{2,1,0:T(8,128)(2,1)S(1)}, u32[]{:S(2)}, u32[]{:S(2)}) collective-permute-start(bf16[8,64,256]{2,1,0:T(8,128)(2,1)S(1)} %get-tuple-element.111), channel_id=1, source_target_pairs={{0,2},{1,3},{2,0},{3,1},{4,6},{5,7},{6,4},{7,5},{8,10},{9,11},{10,... | collective-permute-start | bytes 786440 | tf_op jit(solution)/shard_map/ppermute | solution.py:300
  5.5 7.8 %collective-permute-start.7 = (bf16[256,512]{1,0:T(8,128)(2,1)S(1)}, bf16[256,512]{1,0:T(8,128)(2,1)S(1)}, u32[]{:S(2)}, u32[]{:S(2)}) collective-permute-start(bf16[256,512]{1,0:T(8,128)(2,1)S(1)} %slice.31.refs_4_), channel_id=1, source_target_pairs={{0,8},{2,10},{8,16},{10,18},{16,24},{18,26},{24,28},{26,30},{28,20... | collective-permute-start | bytes 786440 | tf_op jit(solution)/shard_map/ppermute | solution.py:257
  7.3 7.2 %collective-permute-start.8 = (bf16[256,512]{1,0:T(8,128)(2,1)S(1)}, bf16[256,512]{1,0:T(8,128)(2,1)S(1)}, u32[]{:S(2)}, u32[]{:S(2)}) collective-permute-start(bf16[256,512]{1,0:T(8,128)(2,1)S(1)} %slice.31.refs_4_), channel_id=1, source_target_pairs={{8,0},{10,2},{16,8},{18,10},{24,16},{26,18},{28,24},{30,26},{20,28... | collective-permute-start | bytes 786440 | tf_op jit(solution)/shard_map/ppermute | solution.py:258
  9.7 14.4 %collective-permute-start.6 = (bf16[8,64,256]{2,1,0:T(8,128)(2,1)S(1)}, bf16[8,64,256]{2,1,0:T(8,128)(2,1)S(1)}, u32[]{:S(2)}, u32[]{:S(2)}) collective-permute-start(bf16[8,64,256]{2,1,0:T(8,128)(2,1)S(1)} %get-tuple-element.111), channel_id=1, source_target_pairs={{0,3},{1,2},{2,1},{3,0},{4,7},{5,6},{6,5},{7,4},{8,11},{9,10},{10,... | collective-permute-start | bytes 786440 | tf_op jit(solution)/shard_map/ppermute | solution.py:300
  12.2 11.9 %collective-permute-start.4 = (bf16[8,64,256]{2,1,0:T(8,128)(2,1)S(1)}, bf16[8,64,256]{2,1,0:T(8,128)(2,1)S(1)}, u32[]{:S(2)}, u32[]{:S(2)}) collective-permute-start(bf16[8,64,256]{2,1,0:T(8,128)(2,1)S(1)} %get-tuple-element.155.refs_0_), channel_id=1, source_target_pairs={{0,1},{1,0},{2,3},{3,2},{4,5},{5,4},{6,7},{7,6},{8,9},{9,8},{10,11... | collective-permute-start | bytes 786440 | tf_op jit(solution)/shard_map/ppermute | solution.py:300
  17.4 8.8 %collective-permute-start.9 = (bf16[256,512]{1,0:T(8,128)(2,1)S(1)}, bf16[256,512]{1,0:T(8,128)(2,1)S(1)}, u32[]{:S(2)}, u32[]{:S(2)}) collective-permute-start(bf16[256,512]{1,0:T(8,128)(2,1)S(1)} %collective-permute-done.8.refs_5_), channel_id=1, source_target_pairs={{8,0},{10,2},{16,8},{18,10},{24,16},{26,18},{28,24},{30,26},{20,28... | collective-permute-start | bytes 786440 | tf_op jit(solution)/shard_map/ppermute | solution.py:258
  18.7 7.5 %collective-permute-start.10 = (bf16[256,512]{1,0:T(8,128)(2,1)S(1)}, bf16[256,512]{1,0:T(8,128)(2,1)S(1)}, u32[]{:S(2)}, u32[]{:S(2)}) collective-permute-start(bf16[256,512]{1,0:T(8,128)(2,1)S(1)} %collective-permute-done.7.refs_12_), channel_id=1, source_target_pairs={{0,8},{2,10},{8,16},{10,18},{16,24},{18,26},{24,28},{26,30},{28,20... | collective-permute-start | bytes 786440 | tf_op jit(solution)/shard_map/ppermute | solution.py:257
  26.2 13.9 %collective-permute-start.11 = (bf16[256,512]{1,0:T(8,128)(2,1)S(1)}, bf16[256,512]{1,0:T(8,128)(2,1)S(1)}, u32[]{:S(2)}, u32[]{:S(2)}) collective-permute-start(bf16[256,512]{1,0:T(8,128)(2,1)S(1)} %collective-permute-done.9.refs_6_), channel_id=1, source_target_pairs={{8,0},{10,2},{16,8},{18,10},{24,16},{26,18},{28,24},{30,26},{20,28... | collective-permute-start | bytes 786440 | tf_op jit(solution)/shard_map/ppermute | solution.py:258
  27.6 12.5 %collective-permute-start.12 = (bf16[256,512]{1,0:T(8,128)(2,1)S(1)}, bf16[256,512]{1,0:T(8,128)(2,1)S(1)}, u32[]{:S(2)}, u32[]{:S(2)}) collective-permute-start(bf16[256,512]{1,0:T(8,128)(2,1)S(1)} %collective-permute-done.10.refs_11_), channel_id=1, source_target_pairs={{0,8},{2,10},{8,16},{10,18},{16,24},{18,26},{24,28},{26,30},{28,20... | collective-permute-start | bytes 786440 | tf_op jit(solution)/shard_map/ppermute | solution.py:257
  30.4 7.0 %collective-permute-start.15 = (bf16[128,256]{1,0:T(8,128)(2,1)S(1)}, bf16[128,256]{1,0:T(8,128)(2,1)S(1)}, u32[]{:S(2)}, u32[]{:S(2)}) collective-permute-start(bf16[128,256]{1,0:T(8,128)(2,1)S(1)} %slice.32), channel_id=1, source_target_pairs={{0,8},{2,10},{8,16},{10,18},{16,24},{18,26},{24,28},{26,30},{28,20... | collective-permute-start | bytes 196616 | tf_op jit(solution)/shard_map/ppermute | solution.py:262
  41.8 12.2 %collective-permute-start.25 = (bf16[512,256]{1,0:T(8,128)(2,1)S(1)}, bf16[512,256]{1,0:T(8,128)(2,1)S(1)}, u32[]{:S(2)}, u32[]{:S(2)}) collective-permute-start(bf16[512,256]{1,0:T(8,128)(2,1)S(1)} %copy-done.5), channel_id=1, source_target_pairs={{0,8},{2,10},{8,16},{10,18},{16,24},{18,26},{24,28},{26,30},{28,20... | collective-permute-start | bytes 786440 | tf_op jit(solution)/shard_map/ppermute | solution.py:257
  43.1 10.9 %collective-permute-start.26 = (bf16[512,256]{1,0:T(8,128)(2,1)S(1)}, bf16[512,256]{1,0:T(8,128)(2,1)S(1)}, u32[]{:S(2)}, u32[]{:S(2)}) collective-permute-start(bf16[512,256]{1,0:T(8,128)(2,1)S(1)} %copy-done.5), channel_id=1, source_target_pairs={{8,0},{10,2},{16,8},{18,10},{24,16},{26,18},{28,24},{30,26},{20,28... | collective-permute-start | bytes 786440 | tf_op jit(solution)/shard_map/ppermute | solution.py:258
  43.4 9.3 %collective-permute-start.18 = (bf16[128,512]{1,0:T(8,128)(2,1)S(1)}, bf16[128,512]{1,0:T(8,128)(2,1)S(1)}, u32[]{:S(2)}, u32[]{:S(2)}) collective-permute-start(bf16[128,512]{1,0:T(8,128)(2,1)S(1)} %slice.35), channel_id=1, source_target_pairs={{8,0},{10,2},{16,8},{18,10},{24,16},{26,18},{28,24},{30,26},{20,28... | collective-permute-start | bytes 393224 | tf_op jit(solution)/shard_map/ppermute | solution.py:263
  45.3 8.7 %collective-permute-start.21 = (bf16[128,256]{1,0:T(8,128)(2,1)S(1)}, bf16[128,256]{1,0:T(8,128)(2,1)S(1)}, u32[]{:S(2)}, u32[]{:S(2)}) collective-permute-start(bf16[128,256]{1,0:T(8,128)(2,1)S(1)} %keys.1.refs_0_), channel_id=1, source_target_pairs={{8,0},{10,2},{16,8},{18,10},{24,16},{26,18},{28,24},{30,26},{20,28... | collective-permute-start | bytes 196616 | tf_op jit(solution)/shard_map/ppermute | solution.py:258
  54.1 11.8 %collective-permute-start.29 = (bf16[512,256]{1,0:T(8,128)(2,1)S(1)}, bf16[512,256]{1,0:T(8,128)(2,1)}, u32[]{:S(2)}, u32[]{:S(2)}) collective-permute-start(bf16[512,256]{1,0:T(8,128)(2,1)S(1)} %collective-permute-done.25.refs_8_), channel_id=1, source_target_pairs={{0,8},{2,10},{8,16},{10,18},{16,24},{18,26},{24,28},{26,30},{28,20... | collective-permute-start | bytes 786440 | tf_op jit(solution)/shard_map/ppermute | solution.py:257
  55.3 10.5 %collective-permute-start.30 = (bf16[512,256]{1,0:T(8,128)(2,1)S(1)}, bf16[512,256]{1,0:T(8,128)(2,1)}, u32[]{:S(2)}, u32[]{:S(2)}) collective-permute-start(bf16[512,256]{1,0:T(8,128)(2,1)S(1)} %collective-permute-done.26.refs_1_), channel_id=1, source_target_pairs={{8,0},{10,2},{16,8},{18,10},{24,16},{26,18},{28,24},{30,26},{20,28... | collective-permute-start | bytes 786440 | tf_op jit(solution)/shard_map/ppermute | solution.py:258
  57.4 16.9 %collective-permute-start.20 = (f32[256,512]{1,0:T(8,128)S(1)}, f32[256,512]{1,0:T(8,128)S(1)}, u32[]{:S(2)}, u32[]{:S(2)}) collective-permute-start(f32[256,512]{1,0:T(8,128)S(1)} %project_queries.1.mine_ref), channel_id=1, source_target_pairs={{0,2},{2,0},{4,6},{6,4},{8,10},{10,8},{12,14},{14,12},{16,18},{18,... | collective-permute-start | bytes 1572872 | tf_op jit(solution)/shard_map/ppermute | solution.py:363
  65.8 11.2 %collective-permute-start.33 = (bf16[512,256]{1,0:T(8,128)(2,1)}, bf16[512,256]{1,0:T(8,128)(2,1)S(1)}, u32[]{:S(2)}, u32[]{:S(2)}) collective-permute-start(bf16[512,256]{1,0:T(8,128)(2,1)} %collective-permute-done.29.refs_7_), channel_id=1, source_target_pairs={{0,8},{2,10},{8,16},{10,18},{16,24},{18,26},{24,28},{26,30},{28,20... | collective-permute-start | bytes 786440 | tf_op jit(solution)/shard_map/ppermute | solution.py:257
  66.9 10.1 %collective-permute-start.34 = (bf16[512,256]{1,0:T(8,128)(2,1)}, bf16[512,256]{1,0:T(8,128)(2,1)S(1)}, u32[]{:S(2)}, u32[]{:S(2)}) collective-permute-start(bf16[512,256]{1,0:T(8,128)(2,1)} %collective-permute-done.30.refs_2_), channel_id=1, source_target_pairs={{8,0},{10,2},{16,8},{18,10},{24,16},{26,18},{28,24},{30,26},{20,28... | collective-permute-start | bytes 786440 | tf_op jit(solution)/shard_map/ppermute | solution.py:258
  77.0 8.3 %collective-permute-start.35 = (f32[256,640]{1,0:T(8,128)S(1)}, f32[256,640]{1,0:T(8,128)S(1)}, u32[]{:S(2)}, u32[]{:S(2)}) collective-permute-start(f32[256,640]{1,0:T(8,128)S(1)} %attend.1.mine_ref), channel_id=1, source_target_pairs={{0,2},{2,0},{4,6},{6,4},{8,10},{10,8},{12,14},{14,12},{16,18},{18,... | collective-permute-start | bytes 1966088 | tf_op jit(solution)/shard_map/ppermute | solution.py:389
  87.7 6.7 %collective-permute-start.38 = (bf16[8,64,256]{2,1,0:T(8,128)(2,1)S(1)}, bf16[8,64,256]{2,1,0:T(8,128)(2,1)S(1)}, u32[]{:S(2)}, u32[]{:S(2)}) collective-permute-start(bf16[8,64,256]{2,1,0:T(8,128)(2,1)S(1)} %get-tuple-element.194), channel_id=1, source_target_pairs={{0,1},{1,0},{2,3},{3,2},{4,5},{5,4},{6,7},{7,6},{8,9},{9,8},{10,11... | collective-permute-start | bytes 786440 | tf_op jit(solution)/shard_map/ppermute | solution.py:406
  90.1 11.3 %collective-permute-start.40 = (bf16[8,64,256]{2,1,0:T(8,128)(2,1)S(1)}, bf16[8,64,256]{2,1,0:T(8,128)(2,1)S(1)}, u32[]{:S(2)}, u32[]{:S(2)}) collective-permute-start(bf16[8,64,256]{2,1,0:T(8,128)(2,1)S(1)} %get-tuple-element.196), channel_id=1, source_target_pairs={{0,3},{1,2},{2,1},{3,0},{4,7},{5,6},{6,5},{7,4},{8,11},{9,10},{10,... | collective-permute-start | bytes 786440 | tf_op jit(solution)/shard_map/ppermute | solution.py:406
  (41 other events, 199.2 us)

commit v7 on v6

--- a/solution.py
+++ b/solution.py
@@ -114,23 +114,22 @@
     return values * cosine + pltpu.roll(values, HD // 2, 1) * sine
 
 
-def keys_kernel(mine_ref, theirs_ref, cosine_ref, sine_ref, out_ref):
-    rows = out_ref.shape[0]
+def keys_kernel(chips, mine_ref, theirs_ref, cosine_ref, sine_ref, out_ref):
+    rows = out_ref.shape[0] // chips
     cosine, sine = cosine_ref[:rows, :], sine_ref[:rows, :]
     total = mine_ref[...] + theirs_ref[...]
-    out_ref[:, :HD] = turn(total[:, :HD], cosine, sine).astype(jnp.bfloat16)
-    out_ref[:, HD:] = total[:, HD:].astype(jnp.bfloat16)
-
-
-def attend_kernel(mine_ref, theirs_ref, cosine_ref, sine_ref, low_ref, high_ref, orig_ref, *refs):
-    block_refs, (out_ref, keys_ref, values_ref) = refs[:-3], refs[-3:]
-    start = 0
-    for ref in block_refs:
-        keys_ref[start : start + ref.shape[0], :] = ref[:, :HD]
-        values_ref[start : start + ref.shape[0], :] = ref[:, HD:]
-        start += ref.shape[0]
-    keys = keys_ref[...]
-    values = values_ref[...]
+    keys = turn(total[:, :HD], cosine, sine).astype(jnp.bfloat16)
+    values = total[:, HD:].astype(jnp.bfloat16)
+    for chip in range(chips):
+        out_ref[chip * rows : (chip + 1) * rows, :HD] = keys
+        out_ref[chip * rows : (chip + 1) * rows, HD:] = values
+
+
+def attend_kernel(
+    mine_ref, theirs_ref, cosine_ref, sine_ref, low_ref, high_ref, orig_ref, kv_ref, out_ref
+):
+    keys = kv_ref[:, :HD]
+    values = kv_ref[:, HD:]
     orig = orig_ref[...]
     allowed = (orig >= low_ref[...]) & (orig <= high_ref[...])
     scale = 1.0 / HD**0.5
@@ -239,6 +238,7 @@
     back = [(b, a) for a, b in ahead]
     sibling = [(c, c ^ 1) for c in range(n_context)]
 
+    same_core = [[2 * chip + k for chip in range(chips)] for k in range(2)]
     token = [doc_lengths]
 
     def ordered(values):
@@ -334,12 +334,7 @@
     cosine, sine = jnp.cos(angle), jnp.sin(angle)
     cosine = jnp.concatenate([cosine, cosine], axis=1)
     sine = jnp.concatenate([-sine, sine], axis=1)
-    at, core = place_of(place)
-    spot = (jnp.arange(chips, dtype=jnp.int32) + at) % chips
-    chip_of_slot = jnp.zeros((chips,), jnp.int32)
-    for i, chip in enumerate(ring):
-        chip_of_slot = jnp.where(spot == i, jnp.int32(chip), chip_of_slot)
-    owner = chip_of_slot * 2 + core
+    owner = 2 * jnp.arange(chips, dtype=jnp.int32) + context % 2
     key_rows = (owner[:, None] * tokens_here + inside[None, :]).reshape(-1).astype(jnp.int32)
     key_orig, _ = locate(key_rows, span_order, doc_ends)
 
@@ -350,29 +345,26 @@
     out_ring.step()
     mine, theirs = ordered((mine, theirs))
     kv = pl.pallas_call(
-        keys_kernel,
-        out_shape=jax.ShapeDtypeStruct((tokens_here, 2 * HD), jnp.bfloat16),
+        functools.partial(keys_kernel, chips),
+        out_shape=jax.ShapeDtypeStruct((chips * tokens_here, 2 * HD), jnp.bfloat16),
         in_specs=vmem_specs(4),
         out_specs=vmem_specs(1)[0],
         compiler_params=compute_params(),
         name="keys",
     )(mine, theirs, cosine, sine)
-    kv_ring = Ring(kv)
-    kv_ring.step()
+    (kv,) = ordered((kv,))
+    kv = lax.all_to_all(
+        kv, "context", split_axis=0, concat_axis=0, axis_index_groups=same_core, tiled=True
+    )
     (mine,) = project(query_ring.finish(), 1, "project_queries")
     theirs = lax.ppermute(mine, "context", sibling)
-    while not kv_ring.done():
-        kv_ring.step()
-        out_ring.step()
-    kv_blocks = kv_ring.finish()
-
-    count = chips * tokens_here
+    out_ring.step()
+
     mixed = pl.pallas_call(
         attend_kernel,
         out_shape=jax.ShapeDtypeStruct((2 * tokens_here, HEAD_COLS + HD), jnp.float32),
-        in_specs=vmem_specs(7 + len(kv_blocks)),
+        in_specs=vmem_specs(8),
         out_specs=vmem_specs(1)[0],
-        scratch_shapes=[pltpu.VMEM((count, HD), jnp.bfloat16)] * 2,
         compiler_params=compute_params(),
         name="attend",
     )(
@@ -383,7 +375,7 @@
         query_start[:, None],
         query_orig[:, None],
         key_orig[None, :],
-        *kv_blocks,
+        kv,
     )
     (mixed,) = ordered((mixed,))
     mixed_theirs = lax.ppermute(mixed, "context", sibling)

time: 103 us -> 110 us (1.068)
  starting transfers between devices: 39.5 us -> 46 us
  other arithmetic: 1.47 us -> 2.77 us
    ppermute x12 -> x9, waiting for transfers between devices: 4.72 us -> 13.9 us  [step(): self.up.append(lax.ppermute(up, 'context', ahead))]
    ppermute x4 -> x3, waiting for transfers between devices: 13.5 us -> 8.11 us  [step(): lax.ppermute(up[:half], 'context', ahead)]
    ppermute x1, starting transfers between devices: 2.67 us -> 7.46 us  [per_device(): theirs = lax.ppermute(mine, 'context', sibling)]
    ppermute x12 -> x9, starting transfers between devices: 7.47 us -> 2.74 us  [step(): self.down.append(lax.ppermute(down, 'context', back))]
    ppermute x4 -> x3, waiting for transfers between devices: 5.93 us -> 1.74 us  [step(): lax.ppermute(down[half:], 'context', back)]
    all_to_all x0 -> x1, starting transfers between devices: none -> 3.67 us  [per_device(): lax.all_to_all(kv, 'context', split_axis=0, concat_axis=0, axis_index_gro...]
    ppermute x1, starting transfers between devices: 1.6 us -> 3.8 us  [per_device(): theirs = lax.ppermute(theirs, 'context', sibling)]
    ppermute x12 -> x9, starting transfers between devices: 13.1 us -> 15.2 us  [step(): self.up.append(lax.ppermute(up, 'context', ahead))]
  transfers between devices with their start and end apart: 41 -> 34, of which waited for: 17 -> 20; matrix products, arithmetic and copies ran while one was open for 2% -> 4% of each run, Pallas kernels for 6% -> 4%
where the time goes in v7:
time: 110 us; the launch traced here: 109 us
  starting transfers between devices  46 us (42%)
  waiting for transfers between devices  45.4 us (41%)
  Pallas kernels  8.33 us (8%)
  local copies, waits for them, and re-layouts  6.32 us (6%)
  other arithmetic  2.77 us (3%)
    ppermute x9, starting transfers between devices, step(): self.up.append(lax.ppermute(up, 'context', ahead))  15.2 us
    ppermute x9, waiting for transfers between devices, step(): self.up.append(lax.ppermute(up, 'context', ahead))  13.9 us
    ppermute x3, waiting for transfers between devices, per_device(): part = lax.ppermute(part, ('context', 'tensor'), member(e, -d))  9.66 us
    ppermute x9, waiting for transfers between devices, step(): self.down.append(lax.ppermute(down, 'context', back))  8.27 us
    ppermute x3, waiting for transfers between devices, step(): lax.ppermute(up[:half], 'context', ahead)  8.11 us
    ppermute x1, starting transfers between devices, per_device(): theirs = lax.ppermute(mine, 'context', sibling)  7.46 us
    ppermute x3, starting transfers between devices, per_device(): part = lax.ppermute(part, ('context', 'tensor'), member(e, -d))  4.9 us
    ppermute x1, starting transfers between devices, per_device(): theirs = lax.ppermute(theirs, 'context', sibling)  3.8 us
  transfers between devices with their start and end apart: 34, of which 20 were waited for; matrix products, arithmetic and copies ran while one was open for 4% of the time, Pallas kernels for 4%

profile of v7, /device:TPU:1, one launch (start us, length us, event | category | flops | bytes accessed | tf_op | source)
XLA Modules:
  0.0 109.2 jit_solution(1682737982732458491)
XLA Ops:
  1.0 2.2 %collective-permute-start.2 = (bf16[256,256]{1,0:T(8,128)(2,1)S(1)}, bf16[256,256]{1,0:T(8,128)(2,1)S(1)}, u32[]{:S(2)}, u32[]{:S(2)}) collective-permute-start(bf16[256,256]{1,0:T(8,128)(2,1)S(1)} %slice.25.refs_4_), channel_id=1, source_target_pairs={{0,8},{2,10},{8,16},{10,18},{16,24},{18,26},{24,28},{26,30},{28,20... | collective-permute-start | bytes 393224 | tf_op jit(solution)/shard_map/ppermute | solution.py:257
  4.5 1.5 %collective-permute-start = (bf16[256,512]{1,0:T(8,128)(2,1)S(1)}, bf16[256,512]{1,0:T(8,128)(2,1)S(1)}, u32[]{:S(2)}, u32[]{:S(2)}) collective-permute-start(bf16[256,512]{1,0:T(8,128)(2,1)S(1)} %slice.24.refs_4_), channel_id=1, source_target_pairs={{0,8},{2,10},{8,16},{10,18},{16,24},{18,26},{24,28},{26,30},{28,20... | collective-permute-start | bytes 786440 | tf_op jit(solution)/shard_map/ppermute | solution.py:257
  6.0 3.1 %collective-permute-start.10 = (bf16[8,64,256]{2,1,0:T(8,128)(2,1)S(1)}, bf16[8,64,256]{2,1,0:T(8,128)(2,1)S(1)}, u32[]{:S(2)}, u32[]{:S(2)}) collective-permute-start(bf16[8,64,256]{2,1,0:T(8,128)(2,1)S(1)} %get-tuple-element.106), channel_id=1, source_target_pairs={{0,3},{1,2},{2,1},{3,0},{4,7},{5,6},{6,5},{7,4},{8,11},{9,10},{10,... | collective-permute-start | bytes 786440 | tf_op jit(solution)/shard_map/ppermute | solution.py:300
  11.8 1.5 %collective-permute-start.6 = (bf16[256,256]{1,0:T(8,128)(2,1)S(1)}, bf16[256,256]{1,0:T(8,128)(2,1)S(1)}, u32[]{:S(2)}, u32[]{:S(2)}) collective-permute-start(bf16[256,256]{1,0:T(8,128)(2,1)S(1)} %collective-permute-done.2.refs_12_), channel_id=1, source_target_pairs={{0,8},{2,10},{8,16},{10,18},{16,24},{18,26},{24,28},{26,30},{28,20... | collective-permute-start | bytes 393224 | tf_op jit(solution)/shard_map/ppermute | solution.py:257
  13.3 2.3 %collective-permute-done.6.refs_11_ = bf16[256,256]{1,0:T(8,128)(2,1)S(1)} collective-permute-done((bf16[256,256]{1,0:T(8,128)(2,1)S(1)}, bf16[256,256]{1,0:T(8,128)(2,1)S(1)}, u32[]{:S(2)}, u32[]{:S(2)}) %collective-permute-start.6) | collective-permute-done | bytes 131104 | tf_op jit(solution)/shard_map/ppermute | solution.py:257
  15.6 1.8 %collective-permute-done.7.refs_6_ = bf16[256,256]{1,0:T(8,128)(2,1)S(1)} collective-permute-done((bf16[256,256]{1,0:T(8,128)(2,1)S(1)}, bf16[256,256]{1,0:T(8,128)(2,1)S(1)}, u32[]{:S(2)}, u32[]{:S(2)}) %collective-permute-start.7) | collective-permute-done | bytes 131104 | tf_op jit(solution)/shard_map/ppermute | solution.py:258
  17.4 3.5 %collective-permute-done.8.refs_1_ = bf16[8,64,256]{2,1,0:T(8,128)(2,1)S(1)} collective-permute-done((bf16[8,64,256]{2,1,0:T(8,128)(2,1)S(1)}, bf16[8,64,256]{2,1,0:T(8,128)(2,1)S(1)}, u32[]{:S(2)}, u32[]{:S(2)}) %collective-permute-start.8) | collective-permute-done | bytes 262176 | tf_op jit(solution)/shard_map/ppermute | solution.py:300
  21.0 2.1 %collective-permute-start.4 = (bf16[256,512]{1,0:T(8,128)(2,1)S(1)}, bf16[256,512]{1,0:T(8,128)(2,1)S(1)}, u32[]{:S(2)}, u32[]{:S(2)}) collective-permute-start(bf16[256,512]{1,0:T(8,128)(2,1)S(1)} %collective-permute-done.refs_12_), channel_id=1, source_target_pairs={{0,8},{2,10},{8,16},{10,18},{16,24},{18,26},{24,28},{26,30},{28,20... | collective-permute-start | bytes 786440 | tf_op jit(solution)/shard_map/ppermute | solution.py:257
  25.9 3.4 %collective-permute-done.4.refs_11_ = bf16[256,512]{1,0:T(8,128)(2,1)S(1)} collective-permute-done((bf16[256,512]{1,0:T(8,128)(2,1)S(1)}, bf16[256,512]{1,0:T(8,128)(2,1)S(1)}, u32[]{:S(2)}, u32[]{:S(2)}) %collective-permute-start.4) | collective-permute-done | bytes 262176 | tf_op jit(solution)/shard_map/ppermute | solution.py:257
  30.2 2.8 %collective-permute-done.13.refs_7_ = bf16[256,256]{1,0:T(8,128)(2,1)S(1)} collective-permute-done((bf16[256,256]{1,0:T(8,128)(2,1)S(1)}, bf16[256,256]{1,0:T(8,128)(2,1)S(1)}, u32[]{:S(2)}, u32[]{:S(2)}) %collective-permute-start.13) | collective-permute-done | bytes 131104 | tf_op jit(solution)/shard_map/ppermute | solution.py:258
  38.0 3.8 %collective-permute-start.21 = (f32[128,256]{1,0:T(8,128)S(1)}, f32[128,256]{1,0:T(8,128)S(1)}, u32[]{:S(2)}, u32[]{:S(2)}) collective-permute-start(f32[128,256]{1,0:T(8,128)S(1)} %get-tuple-element.141), channel_id=1, source_target_pairs={{0,2},{2,0},{4,6},{6,4},{8,10},{10,8},{12,14},{14,12},{16,18},{18,... | collective-permute-start | bytes 393224 | tf_op jit(solution)/shard_map/ppermute | solution.py:342
  43.7 3.7 %all-to-all-start = ((bf16[8,128,256]{2,1,0:T(8,128)(2,1)}), bf16[8,128,256]{2,1,0:T(8,128)(2,1)S(1)}, u32[]{:S(2)}, u32[]{:S(2)}) async-start(bf16[8,128,256]{2,1,0:T(8,128)(2,1)} %bitcast.8), calls=%async_computation | async-start | bytes 1048576 | tf_op jit(solution)/shard_map/all_to_all | solution.py:356
  47.4 1.5 %collective-permute-start.19 = (bf16[128,512]{1,0:T(8,128)(2,1)S(1)}, bf16[128,512]{1,0:T(8,128)(2,1)S(1)}, u32[]{:S(2)}, u32[]{:S(2)}) collective-permute-start(bf16[128,512]{1,0:T(8,128)(2,1)S(1)} %slice.28), channel_id=1, source_target_pairs={{0,8},{2,10},{8,16},{10,18},{16,24},{18,26},{24,28},{26,30},{28,20... | collective-permute-start | bytes 393224 | tf_op jit(solution)/shard_map/ppermute | solution.py:262
  50.5 5.7 %collective-permute-done.19.refs_8_ = bf16[128,512]{1,0:T(8,128)(2,1)S(1)} collective-permute-done((bf16[128,512]{1,0:T(8,128)(2,1)S(1)}, bf16[128,512]{1,0:T(8,128)(2,1)S(1)}, u32[]{:S(2)}, u32[]{:S(2)}) %collective-permute-start.19) | collective-permute-done | bytes 131104 | tf_op jit(solution)/shard_map/ppermute | solution.py:262
  58.0 7.5 %collective-permute-start.24 = (f32[256,512]{1,0:T(8,128)S(1)}, f32[256,512]{1,0:T(8,128)S(1)}, u32[]{:S(2)}, u32[]{:S(2)}) collective-permute-start(f32[256,512]{1,0:T(8,128)S(1)} %project_queries.1.mine_ref), channel_id=1, source_target_pairs={{0,2},{2,0},{4,6},{6,4},{8,10},{10,8},{12,14},{14,12},{16,18},{18,... | collective-permute-start | bytes 1572872 | tf_op jit(solution)/shard_map/ppermute | solution.py:360
  67.3 4.7 %collective-permute-start.22 = (bf16[512,256]{1,0:T(8,128)(2,1)}, bf16[512,256]{1,0:T(8,128)(2,1)S(1)}, u32[]{:S(2)}, u32[]{:S(2)}) collective-permute-start(bf16[512,256]{1,0:T(8,128)(2,1)} %collective-permute-done.17.refs_8_), channel_id=1, source_target_pairs={{0,8},{2,10},{8,16},{10,18},{16,24},{18,26},{24,28},{26,30},{28,20... | collective-permute-start | bytes 786440 | tf_op jit(solution)/shard_map/ppermute | solution.py:257
  72.2 2.5 %attend.1.mine_ref = f32[256,640]{1,0:T(8,128)S(1)} custom-call(f32[256,512]{1,0:T(8,128)S(1)} %project_queries.1.mine_ref, f32[256,512]{1,0:T(8,128)S(1)} %collective-permute-done.24.theirs_ref, f32[256,128]{1,0:T(8,128)S(1)} %get-tuple-element.186.cosine_ref, f32[256,128]{1,0:T(8,128)S(1)} %get-tuple-element.187.sine_ref, s32[256,1]{1,0:T(8,128)S(1)} %copy.30.low_ref, ...), custom_call_target="tpu_custom_call" | custom-call | tf_op jit(solution)/shard_map/attend/pallas_call | solution.py:363
  75.1 2.9 %collective-permute-done.22.refs_7_ = bf16[512,256]{1,0:T(8,128)(2,1)S(1)} collective-permute-done((bf16[512,256]{1,0:T(8,128)(2,1)}, bf16[512,256]{1,0:T(8,128)(2,1)S(1)}, u32[]{:S(2)}, u32[]{:S(2)}) %collective-permute-start.22) | collective-permute-done | bytes 262176 | tf_op jit(solution)/shard_map/ppermute | solution.py:257
  78.1 1.8 %collective-permute-done.23.refs_2_ = bf16[512,256]{1,0:T(8,128)(2,1)S(1)} collective-permute-done((bf16[512,256]{1,0:T(8,128)(2,1)}, bf16[512,256]{1,0:T(8,128)(2,1)S(1)}, u32[]{:S(2)}, u32[]{:S(2)}) %collective-permute-start.23) | collective-permute-done | bytes 262176 | tf_op jit(solution)/shard_map/ppermute | solution.py:258
  81.3 5.2 %collective-permute-done.25.refs_6_ = bf16[512,256]{1,0:T(8,128)(2,1)S(1)} collective-permute-done((bf16[512,256]{1,0:T(8,128)(2,1)S(1)}, bf16[512,256]{1,0:T(8,128)(2,1)S(1)}, u32[]{:S(2)}, u32[]{:S(2)}) %collective-permute-start.25) | collective-permute-done | bytes 262176 | tf_op jit(solution)/shard_map/ppermute | solution.py:257
  88.5 2.3 %collective-permute-done.28.refs_4_ = bf16[256,256]{1,0:T(8,128)(2,1)S(1)} collective-permute-done((bf16[256,256]{1,0:T(8,128)(2,1)S(1)}, bf16[256,256]{1,0:T(8,128)(2,1)S(1)}, u32[]{:S(2)}, u32[]{:S(2)}) %collective-permute-start.28) | collective-permute-done | bytes 131104 | tf_op jit(solution)/shard_map/ppermute | solution.py:262
  91.3 2.5 %output.1 = (bf16[8,64,256]{2,1,0:T(8,128)(2,1)S(1)}, bf16[8,64,256]{2,1,0:T(8,128)(2,1)S(1)}, bf16[8,64,256]{2,1,0:T(8,128)(2,1)S(1)}, bf16[8,64,256]{2,1,0:T(8,128)(2,1)S(1)}) custom-call(f32[256,640]{1,0:T(8,128)S(1)} %attend.1.mine_ref, f32[256,640]{1,0:T(8,128)S(1)} %collective-permute-done.27.theirs_ref, bf16[512,256]{1,0:T(8,128)(2,1)} %refs_0_.1, ...), custom_call_target="tpu_custom_call" | custom-call | tf_op jit(solution)/shard_map/output/pallas_call | solution.py:385
  94.4 3.6 %collective-permute-start.31 = (bf16[8,64,256]{2,1,0:T(8,128)(2,1)S(1)}, bf16[8,64,256]{2,1,0:T(8,128)(2,1)S(1)}, u32[]{:S(2)}, u32[]{:S(2)}) collective-permute-start(bf16[8,64,256]{2,1,0:T(8,128)(2,1)S(1)} %get-tuple-element.175), channel_id=1, source_target_pairs={{0,2},{1,3},{2,0},{3,1},{4,6},{5,7},{6,4},{7,5},{8,10},{9,11},{10,... | collective-permute-start | bytes 786440 | tf_op jit(solution)/shard_map/ppermute | solution.py:398
  99.2 9.2 %collective-permute-done.32.refs_3_ = bf16[8,64,256]{2,1,0:T(8,128)(2,1)S(1)} collective-permute-done((bf16[8,64,256]{2,1,0:T(8,128)(2,1)S(1)}, bf16[8,64,256]{2,1,0:T(8,128)(2,1)S(1)}, u32[]{:S(2)}, u32[]{:S(2)}) %collective-permute-start.32) | collective-permute-done | bytes 262176 | tf_op jit(solution)/shard_map/ppermute | solution.py:398
  (133 shorter events, 27.8 us)
Async XLA Ops:
  1.0 10.6 %collective-permute-start.2 = (bf16[256,256]{1,0:T(8,128)(2,1)S(1)}, bf16[256,256]{1,0:T(8,128)(2,1)S(1)}, u32[]{:S(2)}, u32[]{:S(2)}) collective-permute-start(bf16[256,256]{1,0:T(8,128)(2,1)S(1)} %slice.25.refs_4_), channel_id=1, source_target_pairs={{0,8},{2,10},{8,16},{10,18},{16,24},{18,26},{24,28},{26,30},{28,20... | collective-permute-start | bytes 393224 | tf_op jit(solution)/shard_map/ppermute | solution.py:257
  3.2 8.5 %collective-permute-start.3 = (bf16[256,256]{1,0:T(8,128)(2,1)S(1)}, bf16[256,256]{1,0:T(8,128)(2,1)S(1)}, u32[]{:S(2)}, u32[]{:S(2)}) collective-permute-start(bf16[256,256]{1,0:T(8,128)(2,1)S(1)} %slice.25.refs_4_), channel_id=1, source_target_pairs={{8,0},{10,2},{16,8},{18,10},{24,16},{26,18},{28,24},{30,26},{20,28... | collective-permute-start | bytes 393224 | tf_op jit(solution)/shard_map/ppermute | solution.py:258
  4.5 7.3 %collective-permute-start = (bf16[256,512]{1,0:T(8,128)(2,1)S(1)}, bf16[256,512]{1,0:T(8,128)(2,1)S(1)}, u32[]{:S(2)}, u32[]{:S(2)}) collective-permute-start(bf16[256,512]{1,0:T(8,128)(2,1)S(1)} %slice.24.refs_4_), channel_id=1, source_target_pairs={{0,8},{2,10},{8,16},{10,18},{16,24},{18,26},{24,28},{26,30},{28,20... | collective-permute-start | bytes 786440 | tf_op jit(solution)/shard_map/ppermute | solution.py:257
  6.0 7.3 %collective-permute-start.1 = (bf16[256,512]{1,0:T(8,128)(2,1)S(1)}, bf16[256,512]{1,0:T(8,128)(2,1)S(1)}, u32[]{:S(2)}, u32[]{:S(2)}) collective-permute-start(bf16[256,512]{1,0:T(8,128)(2,1)S(1)} %slice.24.refs_4_), channel_id=1, source_target_pairs={{8,0},{10,2},{16,8},{18,10},{24,16},{26,18},{28,24},{30,26},{20,28... | collective-permute-start | bytes 786440 | tf_op jit(solution)/shard_map/ppermute | solution.py:258
  6.0 11.4 %collective-permute-start.10 = (bf16[8,64,256]{2,1,0:T(8,128)(2,1)S(1)}, bf16[8,64,256]{2,1,0:T(8,128)(2,1)S(1)}, u32[]{:S(2)}, u32[]{:S(2)}) collective-permute-start(bf16[8,64,256]{2,1,0:T(8,128)(2,1)S(1)} %get-tuple-element.106), channel_id=1, source_target_pairs={{0,3},{1,2},{2,1},{3,0},{4,7},{5,6},{6,5},{7,4},{8,11},{9,10},{10,... | collective-permute-start | bytes 786440 | tf_op jit(solution)/shard_map/ppermute | solution.py:300
  11.6 9.4 %collective-permute-start.9 = (bf16[8,64,256]{2,1,0:T(8,128)(2,1)S(1)}, bf16[8,64,256]{2,1,0:T(8,128)(2,1)S(1)}, u32[]{:S(2)}, u32[]{:S(2)}) collective-permute-start(bf16[8,64,256]{2,1,0:T(8,128)(2,1)S(1)} %get-tuple-element.106), channel_id=1, source_target_pairs={{0,2},{1,3},{2,0},{3,1},{4,6},{5,7},{6,4},{7,5},{8,10},{9,11},{10,... | collective-permute-start | bytes 786440 | tf_op jit(solution)/shard_map/ppermute | solution.py:300
  11.7 9.3 %collective-permute-start.8 = (bf16[8,64,256]{2,1,0:T(8,128)(2,1)S(1)}, bf16[8,64,256]{2,1,0:T(8,128)(2,1)S(1)}, u32[]{:S(2)}, u32[]{:S(2)}) collective-permute-start(bf16[8,64,256]{2,1,0:T(8,128)(2,1)S(1)} %get-tuple-element.150.refs_0_), channel_id=1, source_target_pairs={{0,1},{1,0},{2,3},{3,2},{4,5},{5,4},{6,7},{7,6},{8,9},{9,8},{10,11... | collective-permute-start | bytes 786440 | tf_op jit(solution)/shard_map/ppermute | solution.py:300
  21.0 8.3 %collective-permute-start.4 = (bf16[256,512]{1,0:T(8,128)(2,1)S(1)}, bf16[256,512]{1,0:T(8,128)(2,1)S(1)}, u32[]{:S(2)}, u32[]{:S(2)}) collective-permute-start(bf16[256,512]{1,0:T(8,128)(2,1)S(1)} %collective-permute-done.refs_12_), channel_id=1, source_target_pairs={{0,8},{2,10},{8,16},{10,18},{16,24},{18,26},{24,28},{26,30},{28,20... | collective-permute-start | bytes 786440 | tf_op jit(solution)/shard_map/ppermute | solution.py:257
  23.1 7.1 %collective-permute-start.5 = (bf16[256,512]{1,0:T(8,128)(2,1)S(1)}, bf16[256,512]{1,0:T(8,128)(2,1)S(1)}, u32[]{:S(2)}, u32[]{:S(2)}) collective-permute-start(bf16[256,512]{1,0:T(8,128)(2,1)S(1)} %collective-permute-done.1.refs_5_), channel_id=1, source_target_pairs={{8,0},{10,2},{16,8},{18,10},{24,16},{26,18},{28,24},{30,26},{20,28... | collective-permute-start | bytes 786440 | tf_op jit(solution)/shard_map/ppermute | solution.py:258
  23.1 9.9 %collective-permute-start.13 = (bf16[256,256]{1,0:T(8,128)(2,1)S(1)}, bf16[256,256]{1,0:T(8,128)(2,1)S(1)}, u32[]{:S(2)}, u32[]{:S(2)}) collective-permute-start(bf16[256,256]{1,0:T(8,128)(2,1)S(1)} %collective-permute-done.7.refs_6_), channel_id=1, source_target_pairs={{8,0},{10,2},{16,8},{18,10},{24,16},{26,18},{28,24},{30,26},{20,28... | collective-permute-start | bytes 393224 | tf_op jit(solution)/shard_map/ppermute | solution.py:258
  24.5 8.5 %collective-permute-start.14 = (bf16[256,256]{1,0:T(8,128)(2,1)S(1)}, bf16[256,256]{1,0:T(8,128)(2,1)S(1)}, u32[]{:S(2)}, u32[]{:S(2)}) collective-permute-start(bf16[256,256]{1,0:T(8,128)(2,1)S(1)} %collective-permute-done.6.refs_11_), channel_id=1, source_target_pairs={{0,8},{2,10},{8,16},{10,18},{16,24},{18,26},{24,28},{26,30},{28,20... | collective-permute-start | bytes 393224 | tf_op jit(solution)/shard_map/ppermute | solution.py:257
  34.5 7.5 %collective-permute-start.11 = (bf16[256,512]{1,0:T(8,128)(2,1)S(1)}, bf16[256,512]{1,0:T(8,128)(2,1)S(1)}, u32[]{:S(2)}, u32[]{:S(2)}) collective-permute-start(bf16[256,512]{1,0:T(8,128)(2,1)S(1)} %collective-permute-done.4.refs_11_), channel_id=1, source_target_pairs={{0,8},{2,10},{8,16},{10,18},{16,24},{18,26},{24,28},{26,30},{28,20... | collective-permute-start | bytes 786440 | tf_op jit(solution)/shard_map/ppermute | solution.py:257
  35.8 6.7 %collective-permute-start.12 = (bf16[256,512]{1,0:T(8,128)(2,1)S(1)}, bf16[256,512]{1,0:T(8,128)(2,1)S(1)}, u32[]{:S(2)}, u32[]{:S(2)}) collective-permute-start(bf16[256,512]{1,0:T(8,128)(2,1)S(1)} %collective-permute-done.5.refs_6_), channel_id=1, source_target_pairs={{8,0},{10,2},{16,8},{18,10},{24,16},{26,18},{28,24},{30,26},{20,28... | collective-permute-start | bytes 786440 | tf_op jit(solution)/shard_map/ppermute | solution.py:258
  43.7 28.5 %all-to-all-start = ((bf16[8,128,256]{2,1,0:T(8,128)(2,1)}), bf16[8,128,256]{2,1,0:T(8,128)(2,1)S(1)}, u32[]{:S(2)}, u32[]{:S(2)}) async-start(bf16[8,128,256]{2,1,0:T(8,128)(2,1)} %bitcast.8), calls=%async_computation | async-start | bytes 1048576 | tf_op jit(solution)/shard_map/all_to_all | solution.py:356
  47.4 8.9 %collective-permute-start.19 = (bf16[128,512]{1,0:T(8,128)(2,1)S(1)}, bf16[128,512]{1,0:T(8,128)(2,1)S(1)}, u32[]{:S(2)}, u32[]{:S(2)}) collective-permute-start(bf16[128,512]{1,0:T(8,128)(2,1)S(1)} %slice.28), channel_id=1, source_target_pairs={{0,8},{2,10},{8,16},{10,18},{16,24},{18,26},{24,28},{26,30},{28,20... | collective-permute-start | bytes 393224 | tf_op jit(solution)/shard_map/ppermute | solution.py:262
  48.9 7.4 %collective-permute-start.20 = (bf16[128,512]{1,0:T(8,128)(2,1)S(1)}, bf16[128,512]{1,0:T(8,128)(2,1)S(1)}, u32[]{:S(2)}, u32[]{:S(2)}) collective-permute-start(bf16[128,512]{1,0:T(8,128)(2,1)S(1)} %slice.29), channel_id=1, source_target_pairs={{8,0},{10,2},{16,8},{18,10},{24,16},{26,18},{28,24},{30,26},{20,28... | collective-permute-start | bytes 393224 | tf_op jit(solution)/shard_map/ppermute | solution.py:263
  49.1 18.3 %collective-permute-start.17 = (bf16[512,256]{1,0:T(8,128)(2,1)}, bf16[512,256]{1,0:T(8,128)(2,1)}, u32[]{:S(2)}, u32[]{:S(2)}) collective-permute-start(bf16[512,256]{1,0:T(8,128)(2,1)} %refs_0_.1), channel_id=1, source_target_pairs={{0,8},{2,10},{8,16},{10,18},{16,24},{18,26},{24,28},{26,30},{28,20... | collective-permute-start | bytes 786440 | tf_op jit(solution)/shard_map/ppermute | solution.py:257
  50.5 16.8 %collective-permute-start.18 = (bf16[512,256]{1,0:T(8,128)(2,1)}, bf16[512,256]{1,0:T(8,128)(2,1)}, u32[]{:S(2)}, u32[]{:S(2)}) collective-permute-start(bf16[512,256]{1,0:T(8,128)(2,1)} %refs_0_.1), channel_id=1, source_target_pairs={{8,0},{10,2},{16,8},{18,10},{24,16},{26,18},{28,24},{30,26},{20,28... | collective-permute-start | bytes 786440 | tf_op jit(solution)/shard_map/ppermute | solution.py:258
  58.0 14.2 %collective-permute-start.24 = (f32[256,512]{1,0:T(8,128)S(1)}, f32[256,512]{1,0:T(8,128)S(1)}, u32[]{:S(2)}, u32[]{:S(2)}) collective-permute-start(f32[256,512]{1,0:T(8,128)S(1)} %project_queries.1.mine_ref), channel_id=1, source_target_pairs={{0,2},{2,0},{4,6},{6,4},{8,10},{10,8},{12,14},{14,12},{16,18},{18,... | collective-permute-start | bytes 1572872 | tf_op jit(solution)/shard_map/ppermute | solution.py:360
  67.3 10.7 %collective-permute-start.22 = (bf16[512,256]{1,0:T(8,128)(2,1)}, bf16[512,256]{1,0:T(8,128)(2,1)S(1)}, u32[]{:S(2)}, u32[]{:S(2)}) collective-permute-start(bf16[512,256]{1,0:T(8,128)(2,1)} %collective-permute-done.17.refs_8_), channel_id=1, source_target_pairs={{0,8},{2,10},{8,16},{10,18},{16,24},{18,26},{24,28},{26,30},{28,20... | collective-permute-start | bytes 786440 | tf_op jit(solution)/shard_map/ppermute | solution.py:257
  72.0 7.8 %collective-permute-start.23 = (bf16[512,256]{1,0:T(8,128)(2,1)}, bf16[512,256]{1,0:T(8,128)(2,1)S(1)}, u32[]{:S(2)}, u32[]{:S(2)}) collective-permute-start(bf16[512,256]{1,0:T(8,128)(2,1)} %collective-permute-done.18.refs_1_), channel_id=1, source_target_pairs={{8,0},{10,2},{16,8},{18,10},{24,16},{26,18},{28,24},{30,26},{20,28... | collective-permute-start | bytes 786440 | tf_op jit(solution)/shard_map/ppermute | solution.py:258
  74.8 16.5 %collective-permute-start.27 = (f32[256,640]{1,0:T(8,128)S(1)}, f32[256,640]{1,0:T(8,128)S(1)}, u32[]{:S(2)}, u32[]{:S(2)}) collective-permute-start(f32[256,640]{1,0:T(8,128)S(1)} %attend.1.mine_ref), channel_id=1, source_target_pairs={{0,2},{2,0},{4,6},{6,4},{8,10},{10,8},{12,14},{14,12},{16,18},{18,... | collective-permute-start | bytes 1966088 | tf_op jit(solution)/shard_map/ppermute | solution.py:381
  80.2 6.7 %collective-permute-start.26 = (bf16[512,256]{1,0:T(8,128)(2,1)S(1)}, bf16[512,256]{1,0:T(8,128)(2,1)S(1)}, u32[]{:S(2)}, u32[]{:S(2)}) collective-permute-start(bf16[512,256]{1,0:T(8,128)(2,1)S(1)} %collective-permute-done.23.refs_2_), channel_id=1, source_target_pairs={{8,0},{10,2},{16,8},{18,10},{24,16},{26,18},{28,24},{30,26},{20,28... | collective-permute-start | bytes 786440 | tf_op jit(solution)/shard_map/ppermute | solution.py:258
  98.0 10.3 %collective-permute-start.32 = (bf16[8,64,256]{2,1,0:T(8,128)(2,1)S(1)}, bf16[8,64,256]{2,1,0:T(8,128)(2,1)S(1)}, u32[]{:S(2)}, u32[]{:S(2)}) collective-permute-start(bf16[8,64,256]{2,1,0:T(8,128)(2,1)S(1)} %get-tuple-element.176), channel_id=1, source_target_pairs={{0,3},{1,2},{2,1},{3,0},{4,7},{5,6},{6,5},{7,4},{8,11},{9,10},{10,... | collective-permute-start | bytes 786440 | tf_op jit(solution)/shard_map/ppermute | solution.py:398
  (33 other events, 179.3 us)

commit v8 on v7

--- a/solution.py
+++ b/solution.py
@@ -89,9 +89,9 @@
     ]
 
 
-def project_kernel(chips, groups, outs, *refs):
+def project_kernel(chips, groups, *refs):
     rows_refs, refs = refs[:groups], refs[groups:]
-    weight_refs, out_refs = refs[:-outs], refs[-outs:]
+    weight_refs, (mine_ref, theirs_ref, queries_ref) = refs[:-3], refs[-3:]
     weights = take_ring(weight_refs, chips)
     total = None
     for slot in range(chips):
@@ -104,10 +104,10 @@
             )
             total = part if total is None else total + part
             start += depth
-    start = 0
-    for ref in out_refs:
-        ref[...] = total[start : start + ref.shape[0]]
-        start += ref.shape[0]
+    half = mine_ref.shape[0]
+    mine_ref[...] = total[:half, HEAD_COLS:]
+    theirs_ref[...] = total[half:, HEAD_COLS:]
+    queries_ref[...] = total[:, :HEAD_COLS]
 
 
 def turn(values, cosine, sine):
@@ -279,8 +279,8 @@
             for t in range(n_tensor)
         ]
 
-    keys_ring = Ring(w_qkv[:, HEAD_COLS:])
-    keys_ring.step()
+    qkv_ring = Ring(w_qkv)
+    qkv_ring.step()
 
     normed_shape = jax.ShapeDtypeStruct((chips, rows_here, block), jnp.bfloat16)
     normed_own, normed_other = pl.pallas_call(
@@ -300,26 +300,27 @@
                 rows = lax.ppermute(rows, ("context", "tensor"), member(e, d))
             normed.append(rows)
 
-    query_ring = Ring(w_qkv[:, :HEAD_COLS])
-    query_ring.step()
-    keys_ring.step()
-    query_ring.step()
-    normed = keys_ring.step(normed)
-    query_ring.step()
-    while not keys_ring.done():
-        keys_ring.step()
-
-    def project(blocks, outs, name):
-        columns = blocks[0].shape[1]
-        return pl.pallas_call(
-            functools.partial(project_kernel, chips, groups, outs),
-            out_shape=[jax.ShapeDtypeStruct((2 * tokens_here // outs, columns), jnp.float32)]
-            * outs,
-            in_specs=vmem_specs(groups + len(blocks)),
-            out_specs=vmem_specs(outs),
-            compiler_params=compute_params(),
-            name=name,
-        )(*ordered((*normed, *blocks)))
+    out_ring = Ring(w_out)
+    out_ring.step()
+    qkv_ring.step()
+    out_ring.step()
+    normed = qkv_ring.step(normed)
+    out_ring.step()
+    while not qkv_ring.done():
+        qkv_ring.step()
+    mine, theirs, queries = pl.pallas_call(
+        functools.partial(project_kernel, chips, groups),
+        out_shape=[
+            jax.ShapeDtypeStruct((tokens_here, 2 * HD), jnp.float32),
+            jax.ShapeDtypeStruct((tokens_here, 2 * HD), jnp.float32),
+            jax.ShapeDtypeStruct((2 * tokens_here, HEAD_COLS), jnp.float32),
+        ],
+        in_specs=vmem_specs(groups + len(qkv_ring.finish())),
+        out_specs=vmem_specs(3),
+        compiler_params=compute_params(),
+        name="project",
+    )(*ordered((*normed, *qkv_ring.finish())))
+    theirs = lax.ppermute(theirs, "context", sibling)
 
     doc_ends = jnp.cumsum(doc_lengths)
     inside = (
@@ -338,11 +339,6 @@
     key_rows = (owner[:, None] * tokens_here + inside[None, :]).reshape(-1).astype(jnp.int32)
     key_orig, _ = locate(key_rows, span_order, doc_ends)
 
-    mine, theirs = project(keys_ring.finish(), 2, "project_keys")
-    theirs = lax.ppermute(theirs, "context", sibling)
-    query_ring.step()
-    out_ring = Ring(w_out)
-    out_ring.step()
     mine, theirs = ordered((mine, theirs))
     kv = pl.pallas_call(
         functools.partial(keys_kernel, chips),
@@ -356,9 +352,9 @@
     kv = lax.all_to_all(
         kv, "context", split_axis=0, concat_axis=0, axis_index_groups=same_core, tiled=True
     )
-    (mine,) = project(query_ring.finish(), 1, "project_queries")
-    theirs = lax.ppermute(mine, "context", sibling)
-    out_ring.step()
+    queries_theirs = lax.ppermute(queries, "context", sibling)
+    while not out_ring.done():
+        out_ring.step()
 
     mixed = pl.pallas_call(
         attend_kernel,
@@ -368,8 +364,8 @@
         compiler_params=compute_params(),
         name="attend",
     )(
-        mine,
-        theirs,
+        queries,
+        queries_theirs,
         cosine,
         sine,
         query_start[:, None],

time: 110 us -> 112 us (1.018)
  waiting for transfers between devices: 45.4 us -> 61.2 us
  starting transfers between devices: 46 us -> 32.3 us
    ppermute x9 -> x6, waiting for transfers between devices: 13.9 us -> 25.5 us  [step(): self.up.append(lax.ppermute(up, 'context', ahead))]
    ppermute x3, waiting for transfers between devices: 3.55 us -> 11 us  [per_device(): rows = lax.ppermute(rows, ('context', 'tensor'), member(e, d))]
    ppermute x1, starting transfers between devices: 7.46 us -> 0.71 us  [per_device(): queries_theirs = lax.ppermute(queries, 'context', sibling)]
    ppermute x9 -> x6, starting transfers between devices: 15.2 us -> 10.5 us  [step(): self.up.append(lax.ppermute(up, 'context', ahead))]
    ppermute x9 -> x6, waiting for transfers between devices: 8.27 us -> 4.15 us  [step(): self.down.append(lax.ppermute(down, 'context', back))]
    ppermute x3 -> x2, waiting for transfers between devices: 8.11 us -> 5.28 us  [step(): lax.ppermute(up[:half], 'context', ahead)]
    ppermute x9 -> x6, starting transfers between devices: 2.74 us -> 0.3 us  [step(): self.down.append(lax.ppermute(down, 'context', back))]
    ppermute x3 -> x2, starting transfers between devices: 3.27 us -> 5.39 us  [step(): lax.ppermute(up[:half], 'context', ahead)]
  transfers between devices with their start and end apart: 34 -> 26, of which waited for: 20 -> 15; matrix products, arithmetic and copies ran while one was open for 4% -> 5% of each run, Pallas kernels for 4% -> 0%
where the time goes in v8:
time: 112 us
  waiting for transfers between devices  61.2 us (55%)
  starting transfers between devices  32.3 us (29%)
  Pallas kernels  8.11 us (7%)
  local copies, waits for them, and re-layouts  6.93 us (6%)
  other arithmetic  3.01 us (3%)
    ppermute x6, waiting for transfers between devices, step(): self.up.append(lax.ppermute(up, 'context', ahead))  25.5 us
    ppermute x3, waiting for transfers between devices, per_device(): rows = lax.ppermute(rows, ('context', 'tensor'), member(e, d))  11 us
    ppermute x3, waiting for transfers between devices, per_device(): part = lax.ppermute(part, ('context', 'tensor'), member(e, -d))  10.9 us
    ppermute x6, starting transfers between devices, step(): self.up.append(lax.ppermute(up, 'context', ahead))  10.5 us
    ppermute x2, starting transfers between devices, step(): lax.ppermute(up[:half], 'context', ahead)  5.39 us
    ppermute x2, waiting for transfers between devices, step(): lax.ppermute(up[:half], 'context', ahead)  5.28 us
    ppermute x3, starting transfers between devices, per_device(): rows = lax.ppermute(rows, ('context', 'tensor'), member(e, d))  5.21 us
    ppermute x6, waiting for transfers between devices, step(): self.down.append(lax.ppermute(down, 'context', back))  4.15 us
  transfers between devices with their start and end apart: 26, of which 15 were waited for; matrix products, arithmetic and copies ran while one was open for 5% of the time, Pallas kernels for 0%

profile of v8, /device:TPU:1, one launch (start us, length us, event | category | flops | bytes accessed | tf_op | source)
XLA Modules:
  0.0 111.8 jit_solution(13026235344114126616)
XLA Ops:
  0.0 2.1 %collective-permute-start = (bf16[256,768]{1,0:T(8,128)(2,1)}, bf16[256,768]{1,0:T(8,128)(2,1)S(1)}, u32[]{:S(2)}, u32[]{:S(2)}) collective-permute-start(bf16[256,768]{1,0:T(8,128)(2,1)} %refs_4_), channel_id=1, source_target_pairs={{0,8},{2,10},{8,16},{10,18},{16,24},{18,26},{24,28},{26,30},{28,20... | collective-permute-start | bytes 1179656 | tf_op jit(solution)/shard_map/ppermute | solution.py:257
  4.8 1.5 %collective-permute-start.7 = (bf16[512,256]{1,0:T(8,128)(2,1)S(1)}, bf16[512,256]{1,0:T(8,128)(2,1)S(1)}, u32[]{:S(2)}, u32[]{:S(2)}) collective-permute-start(bf16[512,256]{1,0:T(8,128)(2,1)S(1)} %copy-done.2), channel_id=1, source_target_pairs={{0,8},{2,10},{8,16},{10,18},{16,24},{18,26},{24,28},{26,30},{28,20... | collective-permute-start | bytes 786440 | tf_op jit(solution)/shard_map/ppermute | solution.py:257
  6.3 1.5 %collective-permute-start.5 = (bf16[8,64,256]{2,1,0:T(8,128)(2,1)S(1)}, bf16[8,64,256]{2,1,0:T(8,128)(2,1)S(1)}, u32[]{:S(2)}, u32[]{:S(2)}) collective-permute-start(bf16[8,64,256]{2,1,0:T(8,128)(2,1)S(1)} %get-tuple-element.76), channel_id=1, source_target_pairs={{0,2},{1,3},{2,0},{3,1},{4,6},{5,7},{6,4},{7,5},{8,10},{9,11},{10,... | collective-permute-start | bytes 786440 | tf_op jit(solution)/shard_map/ppermute | solution.py:300
  8.5 2.6 %collective-permute-done.refs_12_ = bf16[256,768]{1,0:T(8,128)(2,1)S(1)} collective-permute-done((bf16[256,768]{1,0:T(8,128)(2,1)}, bf16[256,768]{1,0:T(8,128)(2,1)S(1)}, u32[]{:S(2)}, u32[]{:S(2)}) %collective-permute-start) | collective-permute-done | bytes 393248 | tf_op jit(solution)/shard_map/ppermute | solution.py:257
  14.5 2.3 %collective-permute-done.7.refs_8_ = bf16[512,256]{1,0:T(8,128)(2,1)S(1)} collective-permute-done((bf16[512,256]{1,0:T(8,128)(2,1)S(1)}, bf16[512,256]{1,0:T(8,128)(2,1)S(1)}, u32[]{:S(2)}, u32[]{:S(2)}) %collective-permute-start.7) | collective-permute-done | bytes 262176 | tf_op jit(solution)/shard_map/ppermute | solution.py:257
  16.7 3.7 %collective-permute-start.6 = (bf16[8,64,256]{2,1,0:T(8,128)(2,1)S(1)}, bf16[8,64,256]{2,1,0:T(8,128)(2,1)S(1)}, u32[]{:S(2)}, u32[]{:S(2)}) collective-permute-start(bf16[8,64,256]{2,1,0:T(8,128)(2,1)S(1)} %get-tuple-element.76), channel_id=1, source_target_pairs={{0,3},{1,2},{2,1},{3,0},{4,7},{5,6},{6,5},{7,4},{8,11},{9,10},{10,... | collective-permute-start | bytes 786440 | tf_op jit(solution)/shard_map/ppermute | solution.py:300
  21.1 11.0 %collective-permute-done.4.refs_1_ = bf16[8,64,256]{2,1,0:T(8,128)(2,1)S(1)} collective-permute-done((bf16[8,64,256]{2,1,0:T(8,128)(2,1)S(1)}, bf16[8,64,256]{2,1,0:T(8,128)(2,1)S(1)}, u32[]{:S(2)}, u32[]{:S(2)}) %collective-permute-start.4) | collective-permute-done | bytes 262176 | tf_op jit(solution)/shard_map/ppermute | solution.py:300
  32.1 2.4 %collective-permute-start.10 = (bf16[256,768]{1,0:T(8,128)(2,1)S(1)}, bf16[256,768]{1,0:T(8,128)(2,1)S(1)}, u32[]{:S(2)}, u32[]{:S(2)}) collective-permute-start(bf16[256,768]{1,0:T(8,128)(2,1)S(1)} %collective-permute-done.2.refs_11_), channel_id=1, source_target_pairs={{0,8},{2,10},{8,16},{10,18},{16,24},{18,26},{24,28},{26,30},{28,20... | collective-permute-start | bytes 1179656 | tf_op jit(solution)/shard_map/ppermute | solution.py:257
  34.5 1.5 %collective-permute-start.11 = (bf16[512,256]{1,0:T(8,128)(2,1)S(1)}, bf16[512,256]{1,0:T(8,128)(2,1)}, u32[]{:S(2)}, u32[]{:S(2)}) collective-permute-start(bf16[512,256]{1,0:T(8,128)(2,1)S(1)} %collective-permute-done.7.refs_8_), channel_id=1, source_target_pairs={{0,8},{2,10},{8,16},{10,18},{16,24},{18,26},{24,28},{26,30},{28,20... | collective-permute-start | bytes 786440 | tf_op jit(solution)/shard_map/ppermute | solution.py:257
  36.0 13.2 %collective-permute-done.11.refs_7_ = bf16[512,256]{1,0:T(8,128)(2,1)} collective-permute-done((bf16[512,256]{1,0:T(8,128)(2,1)S(1)}, bf16[512,256]{1,0:T(8,128)(2,1)}, u32[]{:S(2)}, u32[]{:S(2)}) %collective-permute-start.11) | collective-permute-done | bytes 262176 | tf_op jit(solution)/shard_map/ppermute | solution.py:257
  52.3 2.4 %collective-permute-done.13.refs_8_ = bf16[128,768]{1,0:T(8,128)(2,1)S(1)} collective-permute-done((bf16[128,768]{1,0:T(8,128)(2,1)S(1)}, bf16[128,768]{1,0:T(8,128)(2,1)S(1)}, u32[]{:S(2)}, u32[]{:S(2)}) %collective-permute-start.13) | collective-permute-done | bytes 196640 | tf_op jit(solution)/shard_map/ppermute | solution.py:262
  54.8 1.7 %collective-permute-done.14.refs_9_ = bf16[128,768]{1,0:T(8,128)(2,1)S(1)} collective-permute-done((bf16[128,768]{1,0:T(8,128)(2,1)S(1)}, bf16[128,768]{1,0:T(8,128)(2,1)S(1)}, u32[]{:S(2)}, u32[]{:S(2)}) %collective-permute-start.14) | collective-permute-done | bytes 196640 | tf_op jit(solution)/shard_map/ppermute | solution.py:263
  57.5 2.8 %collective-permute-start.16 = (f32[128,256]{1,0:T(8,128)S(1)}, f32[128,256]{1,0:T(8,128)S(1)}, u32[]{:S(2)}, u32[]{:S(2)}) collective-permute-start(f32[128,256]{1,0:T(8,128)S(1)} %get-tuple-element.109), channel_id=1, source_target_pairs={{0,2},{2,0},{4,6},{6,4},{8,10},{10,8},{12,14},{14,12},{16,18},{18,... | collective-permute-start | bytes 393224 | tf_op jit(solution)/shard_map/ppermute | solution.py:323
  62.2 3.7 %all-to-all-start = ((bf16[8,128,256]{2,1,0:T(8,128)(2,1)}), bf16[8,128,256]{2,1,0:T(8,128)(2,1)S(1)}, u32[]{:S(2)}, u32[]{:S(2)}) async-start(bf16[8,128,256]{2,1,0:T(8,128)(2,1)} %bitcast.8), calls=%async_computation | async-start | bytes 1048576 | tf_op jit(solution)/shard_map/all_to_all | solution.py:352
  67.4 1.8 %collective-permute-start.17 = (bf16[512,256]{1,0:T(8,128)(2,1)}, bf16[512,256]{1,0:T(8,128)(2,1)S(1)}, u32[]{:S(2)}, u32[]{:S(2)}) collective-permute-start(bf16[512,256]{1,0:T(8,128)(2,1)} %collective-permute-done.11.refs_7_), channel_id=1, source_target_pairs={{0,8},{2,10},{8,16},{10,18},{16,24},{18,26},{24,28},{26,30},{28,20... | collective-permute-start | bytes 786440 | tf_op jit(solution)/shard_map/ppermute | solution.py:257
  72.9 7.4 %collective-permute-done.17.refs_6_ = bf16[512,256]{1,0:T(8,128)(2,1)S(1)} collective-permute-done((bf16[512,256]{1,0:T(8,128)(2,1)}, bf16[512,256]{1,0:T(8,128)(2,1)S(1)}, u32[]{:S(2)}, u32[]{:S(2)}) %collective-permute-start.17) | collective-permute-done | bytes 262176 | tf_op jit(solution)/shard_map/ppermute | solution.py:257
  80.3 2.4 %collective-permute-done.18.refs_3_ = bf16[512,256]{1,0:T(8,128)(2,1)S(1)} collective-permute-done((bf16[512,256]{1,0:T(8,128)(2,1)}, bf16[512,256]{1,0:T(8,128)(2,1)S(1)}, u32[]{:S(2)}, u32[]{:S(2)}) %collective-permute-start.18) | collective-permute-done | bytes 262176 | tf_op jit(solution)/shard_map/ppermute | solution.py:258
  82.7 2.5 %attend.1.mine_ref = f32[256,640]{1,0:T(8,128)S(1)} custom-call(f32[256,512]{1,0:T(8,128)S(1)} %get-tuple-element.107.mine_ref, f32[256,512]{1,0:T(8,128)S(1)} %collective-permute-done.15.theirs_ref, f32[256,128]{1,0:T(8,128)S(1)} %get-tuple-element.136.cosine_ref, f32[256,128]{1,0:T(8,128)S(1)} %get-tuple-element.137.sine_ref, s32[256,1]{1,0:T(8,128)S(1)} %copy.30.low_ref, ...), custom_call_target="tpu_custom_call" | custom-call | tf_op jit(solution)/shard_map/attend/pallas_call | solution.py:359
  85.9 4.0 %collective-permute-start.20 = (bf16[256,256]{1,0:T(8,128)(2,1)S(1)}, bf16[256,256]{1,0:T(8,128)(2,1)S(1)}, u32[]{:S(2)}, u32[]{:S(2)}) collective-permute-start(bf16[256,256]{1,0:T(8,128)(2,1)S(1)} %slice.14), channel_id=1, source_target_pairs={{0,8},{2,10},{8,16},{10,18},{16,24},{18,26},{24,28},{26,30},{28,20... | collective-permute-start | bytes 393224 | tf_op jit(solution)/shard_map/ppermute | solution.py:262
  90.0 2.8 %collective-permute-done.20.refs_4_ = bf16[256,256]{1,0:T(8,128)(2,1)S(1)} collective-permute-done((bf16[256,256]{1,0:T(8,128)(2,1)S(1)}, bf16[256,256]{1,0:T(8,128)(2,1)S(1)}, u32[]{:S(2)}, u32[]{:S(2)}) %collective-permute-start.20) | collective-permute-done | bytes 131104 | tf_op jit(solution)/shard_map/ppermute | solution.py:262
  92.8 1.9 %collective-permute-done.21.refs_5_ = bf16[256,256]{1,0:T(8,128)(2,1)S(1)} collective-permute-done((bf16[256,256]{1,0:T(8,128)(2,1)S(1)}, bf16[256,256]{1,0:T(8,128)(2,1)S(1)}, u32[]{:S(2)}, u32[]{:S(2)}) %collective-permute-start.21) | collective-permute-done | bytes 131104 | tf_op jit(solution)/shard_map/ppermute | solution.py:263
  94.8 2.4 %output.1 = (bf16[8,64,256]{2,1,0:T(8,128)(2,1)S(1)}, bf16[8,64,256]{2,1,0:T(8,128)(2,1)S(1)}, bf16[8,64,256]{2,1,0:T(8,128)(2,1)S(1)}, bf16[8,64,256]{2,1,0:T(8,128)(2,1)S(1)}) custom-call(f32[256,640]{1,0:T(8,128)S(1)} %attend.1.mine_ref, f32[256,640]{1,0:T(8,128)S(1)} %collective-permute-done.19.theirs_ref, bf16[512,256]{1,0:T(8,128)(2,1)S(1)} %copy-done.2, ...), custom_call_target="tpu_custom_call" | custom-call | tf_op jit(solution)/shard_map/output/pallas_call | solution.py:381
  100.0 3.9 %collective-permute-done.22.refs_1_ = bf16[8,64,256]{2,1,0:T(8,128)(2,1)S(1)} collective-permute-done((bf16[8,64,256]{2,1,0:T(8,128)(2,1)S(1)}, bf16[8,64,256]{2,1,0:T(8,128)(2,1)S(1)}, u32[]{:S(2)}, u32[]{:S(2)}) %collective-permute-start.22) | collective-permute-done | bytes 262176 | tf_op jit(solution)/shard_map/ppermute | solution.py:394
  103.9 7.0 %collective-permute-done.24.refs_3_ = bf16[8,64,256]{2,1,0:T(8,128)(2,1)S(1)} collective-permute-done((bf16[8,64,256]{2,1,0:T(8,128)(2,1)S(1)}, bf16[8,64,256]{2,1,0:T(8,128)(2,1)S(1)}, u32[]{:S(2)}, u32[]{:S(2)}) %collective-permute-start.24) | collective-permute-done | bytes 262176 | tf_op jit(solution)/shard_map/ppermute | solution.py:394
  (88 shorter events, 23.1 us)
Async XLA Ops:
  0.0 11.1 %collective-permute-start = (bf16[256,768]{1,0:T(8,128)(2,1)}, bf16[256,768]{1,0:T(8,128)(2,1)S(1)}, u32[]{:S(2)}, u32[]{:S(2)}) collective-permute-start(bf16[256,768]{1,0:T(8,128)(2,1)} %refs_4_), channel_id=1, source_target_pairs={{0,8},{2,10},{8,16},{10,18},{16,24},{18,26},{24,28},{26,30},{28,20... | collective-permute-start | bytes 1179656 | tf_op jit(solution)/shard_map/ppermute | solution.py:257
  2.1 9.9 %collective-permute-start.1 = (bf16[256,768]{1,0:T(8,128)(2,1)}, bf16[256,768]{1,0:T(8,128)(2,1)S(1)}, u32[]{:S(2)}, u32[]{:S(2)}) collective-permute-start(bf16[256,768]{1,0:T(8,128)(2,1)} %refs_4_), channel_id=1, source_target_pairs={{8,0},{10,2},{16,8},{18,10},{24,16},{26,18},{28,24},{30,26},{20,28... | collective-permute-start | bytes 1179656 | tf_op jit(solution)/shard_map/ppermute | solution.py:258
  4.8 11.9 %collective-permute-start.7 = (bf16[512,256]{1,0:T(8,128)(2,1)S(1)}, bf16[512,256]{1,0:T(8,128)(2,1)S(1)}, u32[]{:S(2)}, u32[]{:S(2)}) collective-permute-start(bf16[512,256]{1,0:T(8,128)(2,1)S(1)} %copy-done.2), channel_id=1, source_target_pairs={{0,8},{2,10},{8,16},{10,18},{16,24},{18,26},{24,28},{26,30},{28,20... | collective-permute-start | bytes 786440 | tf_op jit(solution)/shard_map/ppermute | solution.py:257
  6.3 14.1 %collective-permute-start.8 = (bf16[512,256]{1,0:T(8,128)(2,1)S(1)}, bf16[512,256]{1,0:T(8,128)(2,1)S(1)}, u32[]{:S(2)}, u32[]{:S(2)}) collective-permute-start(bf16[512,256]{1,0:T(8,128)(2,1)S(1)} %copy-done.2), channel_id=1, source_target_pairs={{8,0},{10,2},{16,8},{18,10},{24,16},{26,18},{28,24},{30,26},{20,28... | collective-permute-start | bytes 786440 | tf_op jit(solution)/shard_map/ppermute | solution.py:258
  6.3 25.8 %collective-permute-start.5 = (bf16[8,64,256]{2,1,0:T(8,128)(2,1)S(1)}, bf16[8,64,256]{2,1,0:T(8,128)(2,1)S(1)}, u32[]{:S(2)}, u32[]{:S(2)}) collective-permute-start(bf16[8,64,256]{2,1,0:T(8,128)(2,1)S(1)} %get-tuple-element.76), channel_id=1, source_target_pairs={{0,2},{1,3},{2,0},{3,1},{4,6},{5,7},{6,4},{7,5},{8,10},{9,11},{10,... | collective-permute-start | bytes 786440 | tf_op jit(solution)/shard_map/ppermute | solution.py:300
  12.0 20.1 %collective-permute-start.2 = (bf16[256,768]{1,0:T(8,128)(2,1)S(1)}, bf16[256,768]{1,0:T(8,128)(2,1)S(1)}, u32[]{:S(2)}, u32[]{:S(2)}) collective-permute-start(bf16[256,768]{1,0:T(8,128)(2,1)S(1)} %collective-permute-done.refs_12_), channel_id=1, source_target_pairs={{0,8},{2,10},{8,16},{10,18},{16,24},{18,26},{24,28},{26,30},{28,20... | collective-permute-start | bytes 1179656 | tf_op jit(solution)/shard_map/ppermute | solution.py:257
  13.3 18.8 %collective-permute-start.3 = (bf16[256,768]{1,0:T(8,128)(2,1)S(1)}, bf16[256,768]{1,0:T(8,128)(2,1)S(1)}, u32[]{:S(2)}, u32[]{:S(2)}) collective-permute-start(bf16[256,768]{1,0:T(8,128)(2,1)S(1)} %collective-permute-done.1.refs_5_), channel_id=1, source_target_pairs={{8,0},{10,2},{16,8},{18,10},{24,16},{26,18},{28,24},{30,26},{20,28... | collective-permute-start | bytes 1179656 | tf_op jit(solution)/shard_map/ppermute | solution.py:258
  16.7 15.4 %collective-permute-start.6 = (bf16[8,64,256]{2,1,0:T(8,128)(2,1)S(1)}, bf16[8,64,256]{2,1,0:T(8,128)(2,1)S(1)}, u32[]{:S(2)}, u32[]{:S(2)}) collective-permute-start(bf16[8,64,256]{2,1,0:T(8,128)(2,1)S(1)} %get-tuple-element.76), channel_id=1, source_target_pairs={{0,3},{1,2},{2,1},{3,0},{4,7},{5,6},{6,5},{7,4},{8,11},{9,10},{10,... | collective-permute-start | bytes 786440 | tf_op jit(solution)/shard_map/ppermute | solution.py:300
  20.4 11.7 %collective-permute-start.4 = (bf16[8,64,256]{2,1,0:T(8,128)(2,1)S(1)}, bf16[8,64,256]{2,1,0:T(8,128)(2,1)S(1)}, u32[]{:S(2)}, u32[]{:S(2)}) collective-permute-start(bf16[8,64,256]{2,1,0:T(8,128)(2,1)S(1)} %get-tuple-element.94.refs_0_), channel_id=1, source_target_pairs={{0,1},{1,0},{2,3},{3,2},{4,5},{5,4},{6,7},{7,6},{8,9},{9,8},{10,11... | collective-permute-start | bytes 786440 | tf_op jit(solution)/shard_map/ppermute | solution.py:300
  32.1 18.0 %collective-permute-start.10 = (bf16[256,768]{1,0:T(8,128)(2,1)S(1)}, bf16[256,768]{1,0:T(8,128)(2,1)S(1)}, u32[]{:S(2)}, u32[]{:S(2)}) collective-permute-start(bf16[256,768]{1,0:T(8,128)(2,1)S(1)} %collective-permute-done.2.refs_11_), channel_id=1, source_target_pairs={{0,8},{2,10},{8,16},{10,18},{16,24},{18,26},{24,28},{26,30},{28,20... | collective-permute-start | bytes 1179656 | tf_op jit(solution)/shard_map/ppermute | solution.py:257
  34.5 15.7 %collective-permute-start.9 = (bf16[256,768]{1,0:T(8,128)(2,1)S(1)}, bf16[256,768]{1,0:T(8,128)(2,1)S(1)}, u32[]{:S(2)}, u32[]{:S(2)}) collective-permute-start(bf16[256,768]{1,0:T(8,128)(2,1)S(1)} %collective-permute-done.3.refs_6_), channel_id=1, source_target_pairs={{8,0},{10,2},{16,8},{18,10},{24,16},{26,18},{28,24},{30,26},{20,28... | collective-permute-start | bytes 1179656 | tf_op jit(solution)/shard_map/ppermute | solution.py:258
  34.5 14.8 %collective-permute-start.11 = (bf16[512,256]{1,0:T(8,128)(2,1)S(1)}, bf16[512,256]{1,0:T(8,128)(2,1)}, u32[]{:S(2)}, u32[]{:S(2)}) collective-permute-start(bf16[512,256]{1,0:T(8,128)(2,1)S(1)} %collective-permute-done.7.refs_8_), channel_id=1, source_target_pairs={{0,8},{2,10},{8,16},{10,18},{16,24},{18,26},{24,28},{26,30},{28,20... | collective-permute-start | bytes 786440 | tf_op jit(solution)/shard_map/ppermute | solution.py:257
  36.0 14.2 %collective-permute-start.12 = (bf16[512,256]{1,0:T(8,128)(2,1)S(1)}, bf16[512,256]{1,0:T(8,128)(2,1)}, u32[]{:S(2)}, u32[]{:S(2)}) collective-permute-start(bf16[512,256]{1,0:T(8,128)(2,1)S(1)} %collective-permute-done.8.refs_1_), channel_id=1, source_target_pairs={{8,0},{10,2},{16,8},{18,10},{24,16},{26,18},{28,24},{30,26},{20,28... | collective-permute-start | bytes 786440 | tf_op jit(solution)/shard_map/ppermute | solution.py:258
  51.6 4.9 %collective-permute-start.14 = (bf16[128,768]{1,0:T(8,128)(2,1)S(1)}, bf16[128,768]{1,0:T(8,128)(2,1)S(1)}, u32[]{:S(2)}, u32[]{:S(2)}) collective-permute-start(bf16[128,768]{1,0:T(8,128)(2,1)S(1)} %slice.13), channel_id=1, source_target_pairs={{8,0},{10,2},{16,8},{18,10},{24,16},{26,18},{28,24},{30,26},{20,28... | collective-permute-start | bytes 589832 | tf_op jit(solution)/shard_map/ppermute | solution.py:263
  62.2 20.5 %all-to-all-start = ((bf16[8,128,256]{2,1,0:T(8,128)(2,1)}), bf16[8,128,256]{2,1,0:T(8,128)(2,1)S(1)}, u32[]{:S(2)}, u32[]{:S(2)}) async-start(bf16[8,128,256]{2,1,0:T(8,128)(2,1)} %bitcast.8), calls=%async_computation | async-start | bytes 1048576 | tf_op jit(solution)/shard_map/all_to_all | solution.py:352
  66.6 16.0 %collective-permute-start.15 = (f32[256,512]{1,0:T(8,128)S(1)}, f32[256,512]{1,0:T(8,128)S(1)}, u32[]{:S(2)}, u32[]{:S(2)}) collective-permute-start(f32[256,512]{1,0:T(8,128)S(1)} %get-tuple-element.107.mine_ref), channel_id=1, source_target_pairs={{0,2},{2,0},{4,6},{6,4},{8,10},{10,8},{12,14},{14,12},{16,18},{18,... | collective-permute-start | bytes 1572872 | tf_op jit(solution)/shard_map/ppermute | solution.py:355
  67.4 12.9 %collective-permute-start.17 = (bf16[512,256]{1,0:T(8,128)(2,1)}, bf16[512,256]{1,0:T(8,128)(2,1)S(1)}, u32[]{:S(2)}, u32[]{:S(2)}) collective-permute-start(bf16[512,256]{1,0:T(8,128)(2,1)} %collective-permute-done.11.refs_7_), channel_id=1, source_target_pairs={{0,8},{2,10},{8,16},{10,18},{16,24},{18,26},{24,28},{26,30},{28,20... | collective-permute-start | bytes 786440 | tf_op jit(solution)/shard_map/ppermute | solution.py:257
  69.2 13.5 %collective-permute-start.18 = (bf16[512,256]{1,0:T(8,128)(2,1)}, bf16[512,256]{1,0:T(8,128)(2,1)S(1)}, u32[]{:S(2)}, u32[]{:S(2)}) collective-permute-start(bf16[512,256]{1,0:T(8,128)(2,1)} %collective-permute-done.12.refs_2_), channel_id=1, source_target_pairs={{8,0},{10,2},{16,8},{18,10},{24,16},{26,18},{28,24},{30,26},{20,28... | collective-permute-start | bytes 786440 | tf_op jit(solution)/shard_map/ppermute | solution.py:258
  85.2 9.6 %collective-permute-start.19 = (f32[256,640]{1,0:T(8,128)S(1)}, f32[256,640]{1,0:T(8,128)S(1)}, u32[]{:S(2)}, u32[]{:S(2)}) collective-permute-start(f32[256,640]{1,0:T(8,128)S(1)} %attend.1.mine_ref), channel_id=1, source_target_pairs={{0,2},{2,0},{4,6},{6,4},{8,10},{10,8},{12,14},{14,12},{16,18},{18,... | collective-permute-start | bytes 1966088 | tf_op jit(solution)/shard_map/ppermute | solution.py:377
  85.9 7.0 %collective-permute-start.20 = (bf16[256,256]{1,0:T(8,128)(2,1)S(1)}, bf16[256,256]{1,0:T(8,128)(2,1)S(1)}, u32[]{:S(2)}, u32[]{:S(2)}) collective-permute-start(bf16[256,256]{1,0:T(8,128)(2,1)S(1)} %slice.14), channel_id=1, source_target_pairs={{0,8},{2,10},{8,16},{10,18},{16,24},{18,26},{24,28},{26,30},{28,20... | collective-permute-start | bytes 393224 | tf_op jit(solution)/shard_map/ppermute | solution.py:262
  89.9 4.8 %collective-permute-start.21 = (bf16[256,256]{1,0:T(8,128)(2,1)S(1)}, bf16[256,256]{1,0:T(8,128)(2,1)S(1)}, u32[]{:S(2)}, u32[]{:S(2)}) collective-permute-start(bf16[256,256]{1,0:T(8,128)(2,1)S(1)} %slice.15), channel_id=1, source_target_pairs={{8,0},{10,2},{16,8},{18,10},{24,16},{26,18},{28,24},{30,26},{20,28... | collective-permute-start | bytes 393224 | tf_op jit(solution)/shard_map/ppermute | solution.py:263
  97.1 6.7 %collective-permute-start.22 = (bf16[8,64,256]{2,1,0:T(8,128)(2,1)S(1)}, bf16[8,64,256]{2,1,0:T(8,128)(2,1)S(1)}, u32[]{:S(2)}, u32[]{:S(2)}) collective-permute-start(bf16[8,64,256]{2,1,0:T(8,128)(2,1)S(1)} %get-tuple-element.124), channel_id=1, source_target_pairs={{0,1},{1,0},{2,3},{3,2},{4,5},{5,4},{6,7},{7,6},{8,9},{9,8},{10,11... | collective-permute-start | bytes 786440 | tf_op jit(solution)/shard_map/ppermute | solution.py:394
  97.8 6.1 %collective-permute-start.23 = (bf16[8,64,256]{2,1,0:T(8,128)(2,1)S(1)}, bf16[8,64,256]{2,1,0:T(8,128)(2,1)S(1)}, u32[]{:S(2)}, u32[]{:S(2)}) collective-permute-start(bf16[8,64,256]{2,1,0:T(8,128)(2,1)S(1)} %get-tuple-element.125), channel_id=1, source_target_pairs={{0,2},{1,3},{2,0},{3,1},{4,6},{5,7},{6,4},{7,5},{8,10},{9,11},{10,... | collective-permute-start | bytes 786440 | tf_op jit(solution)/shard_map/ppermute | solution.py:394
  99.2 11.7 %collective-permute-start.24 = (bf16[8,64,256]{2,1,0:T(8,128)(2,1)S(1)}, bf16[8,64,256]{2,1,0:T(8,128)(2,1)S(1)}, u32[]{:S(2)}, u32[]{:S(2)}) collective-permute-start(bf16[8,64,256]{2,1,0:T(8,128)(2,1)S(1)} %get-tuple-element.126), channel_id=1, source_target_pairs={{0,3},{1,2},{2,1},{3,0},{4,7},{5,6},{6,5},{7,4},{8,11},{9,10},{10,... | collective-permute-start | bytes 786440 | tf_op jit(solution)/shard_map/ppermute | solution.py:394
  (13 other events, 54.9 us)

commit v9 on v7

--- a/solution.py
+++ b/solution.py
@@ -91,7 +91,7 @@
 
 def project_kernel(chips, groups, outs, *refs):
     rows_refs, refs = refs[:groups], refs[groups:]
-    weight_refs, out_refs = refs[:-outs], refs[-outs:]
+    weight_refs, out_refs = refs[: -len(outs)], refs[-len(outs) :]
     weights = take_ring(weight_refs, chips)
     total = None
     for slot in range(chips):
@@ -104,10 +104,8 @@
             )
             total = part if total is None else total + part
             start += depth
-    start = 0
-    for ref in out_refs:
-        ref[...] = total[start : start + ref.shape[0]]
-        start += ref.shape[0]
+    for ref, (rows, columns) in zip(out_refs, outs):
+        ref[...] = total[rows, columns]
 
 
 def turn(values, cosine, sine):
@@ -126,7 +124,17 @@
 
 
 def attend_kernel(
-    mine_ref, theirs_ref, cosine_ref, sine_ref, low_ref, high_ref, orig_ref, kv_ref, out_ref
+    first_ref,
+    first_theirs_ref,
+    last_ref,
+    last_theirs_ref,
+    cosine_ref,
+    sine_ref,
+    low_ref,
+    high_ref,
+    orig_ref,
+    kv_ref,
+    out_ref,
 ):
     keys = kv_ref[:, :HD]
     values = kv_ref[:, HD:]
@@ -138,7 +146,12 @@
     lane = lax.broadcasted_iota(jnp.int32, (rows, HD), 1)
     stats = jnp.zeros((rows, HD), jnp.float32)
     for head in range(QH_DEV):
-        columns = slice(head * HD, (head + 1) * HD)
+        if head < QH_DEV - 1:
+            mine_ref, theirs_ref = first_ref, first_theirs_ref
+            columns = slice(head * HD, (head + 1) * HD)
+        else:
+            mine_ref, theirs_ref = last_ref, last_theirs_ref
+            columns = slice(0, HD)
         query = jnp.concatenate(
             [
                 mine_ref[:half, columns] + theirs_ref[half:, columns],
@@ -154,7 +167,7 @@
         top = jnp.max(scores, axis=-1, keepdims=True)
         expo = jnp.where(allowed, jnp.exp(scores - top), 0.0)
         total = jnp.sum(expo, axis=-1, keepdims=True)
-        out_ref[:, columns] = jnp.dot(
+        out_ref[:, head * HD : (head + 1) * HD] = jnp.dot(
             expo.astype(jnp.bfloat16), values, preferred_element_type=jnp.float32
         )
         stats = jnp.where(lane == 2 * head, total, stats)
@@ -164,7 +177,10 @@
 
 def output_kernel(chips, groups, mine_ref, theirs_ref, *refs):
     weight_refs, out_refs = refs[:-groups], refs[-groups:]
-    weights = take_ring(weight_refs, chips)
+    count = len(weight_refs) // 2
+    upper = take_ring(weight_refs[:count], chips)
+    lower = take_ring(weight_refs[count:], chips)
+    weights = [a + b for a, b in zip(upper, lower)]
     chip_rows = mine_ref.shape[0]
     half = chip_rows // 2
 
@@ -279,8 +295,7 @@
             for t in range(n_tensor)
         ]
 
-    keys_ring = Ring(w_qkv[:, HEAD_COLS:])
-    keys_ring.step()
+    split = (QH_DEV - 1) * HD
 
     normed_shape = jax.ShapeDtypeStruct((chips, rows_here, block), jnp.bfloat16)
     normed_own, normed_other = pl.pallas_call(
@@ -291,7 +306,14 @@
         compiler_params=compute_params(),
         name="norm",
     )(hidden_rows, norm_gain[None, :])
-    normed_own, normed_other = ordered((normed_own, normed_other))
+    last_ring = Ring(w_qkv[:, split:])
+    first_ring = Ring(w_qkv[:, :split])
+    normed_own, normed_other, last_ring.up[0] = ordered(
+        (normed_own, normed_other, last_ring.up[0])
+    )
+    last_ring.down[0] = last_ring.up[0]
+    last_ring.step()
+    first_ring.step()
     normed = []
     for e in range(2):
         for d in range(n_tensor):
@@ -300,23 +322,29 @@
                 rows = lax.ppermute(rows, ("context", "tensor"), member(e, d))
             normed.append(rows)
 
-    query_ring = Ring(w_qkv[:, :HEAD_COLS])
-    query_ring.step()
-    keys_ring.step()
-    query_ring.step()
-    normed = keys_ring.step(normed)
-    query_ring.step()
-    while not keys_ring.done():
-        keys_ring.step()
+    last_ring.step()
+    first_ring.step()
+    normed = last_ring.step(normed)
+    first_ring.step()
+    while not last_ring.done():
+        last_ring.step()
+    while not first_ring.done():
+        first_ring.step()
+    half = w_out.shape[0] // 2
+    upper_ring, lower_ring = Ring(w_out[:half]), Ring(w_out[half:])
+    upper_ring.step()
+    lower_ring.step()
 
     def project(blocks, outs, name):
-        columns = blocks[0].shape[1]
+        shapes = [
+            jax.ShapeDtypeStruct((rows.stop - rows.start, columns.stop - columns.start), jnp.float32)
+            for rows, columns in outs
+        ]
         return pl.pallas_call(
             functools.partial(project_kernel, chips, groups, outs),
-            out_shape=[jax.ShapeDtypeStruct((2 * tokens_here // outs, columns), jnp.float32)]
-            * outs,
+            out_shape=shapes,
             in_specs=vmem_specs(groups + len(blocks)),
-            out_specs=vmem_specs(outs),
+            out_specs=vmem_specs(len(outs)),
             compiler_params=compute_params(),
             name=name,
         )(*ordered((*normed, *blocks)))
@@ -338,11 +366,16 @@
     key_rows = (owner[:, None] * tokens_here + inside[None, :]).reshape(-1).astype(jnp.int32)
     key_orig, _ = locate(key_rows, span_order, doc_ends)
 
-    mine, theirs = project(keys_ring.finish(), 2, "project_keys")
+    ours, siblings = slice(0, tokens_here), slice(tokens_here, 2 * tokens_here)
+    both_rows, kv_columns = slice(0, 2 * tokens_here), slice(HD, 3 * HD)
+    mine, theirs, last = project(
+        last_ring.finish(),
+        [(ours, kv_columns), (siblings, kv_columns), (both_rows, slice(0, HD))],
+        "project_keys",
+    )
     theirs = lax.ppermute(theirs, "context", sibling)
-    query_ring.step()
-    out_ring = Ring(w_out)
-    out_ring.step()
+    upper_ring.step()
+    lower_ring.step()
     mine, theirs = ordered((mine, theirs))
     kv = pl.pallas_call(
         functools.partial(keys_kernel, chips),
@@ -356,20 +389,26 @@
     kv = lax.all_to_all(
         kv, "context", split_axis=0, concat_axis=0, axis_index_groups=same_core, tiled=True
     )
-    (mine,) = project(query_ring.finish(), 1, "project_queries")
-    theirs = lax.ppermute(mine, "context", sibling)
-    out_ring.step()
+    (first,) = project(first_ring.finish(), [(both_rows, slice(0, split))], "project_queries")
+    first_theirs = lax.ppermute(first, "context", sibling)
+    last_theirs = lax.ppermute(last, "context", sibling)
+    while not lower_ring.done():
+        upper_ring.step()
+        lower_ring.step()
+    (kv,) = ordered((kv,))
 
     mixed = pl.pallas_call(
         attend_kernel,
         out_shape=jax.ShapeDtypeStruct((2 * tokens_here, HEAD_COLS + HD), jnp.float32),
-        in_specs=vmem_specs(8),
+        in_specs=vmem_specs(10),
         out_specs=vmem_specs(1)[0],
         compiler_params=compute_params(),
         name="attend",
     )(
-        mine,
-        theirs,
+        first,
+        first_theirs,
+        last,
+        last_theirs,
         cosine,
         sine,
         query_start[:, None],
@@ -379,7 +418,7 @@
     )
     (mixed,) = ordered((mixed,))
     mixed_theirs = lax.ppermute(mixed, "context", sibling)
-    out_blocks = out_ring.finish()
+    out_blocks = upper_ring.finish() + lower_ring.finish()
 
     out_block = w_out.shape[1]
     parts = pl.pallas_call(

time: 110 us -> 119 us (1.082)
  starting transfers between devices: 46 us -> 55 us
  local copies, waits for them, and re-layouts: 6.32 us -> 14.3 us
  waiting for transfers between devices: 45.4 us -> 37.6 us
    unnamed x46 -> x56, local copies, waits for them, and re-layouts: 3.57 us -> 10.7 us
    ppermute x9 -> x12, waiting for transfers between devices: 13.9 us -> 7.29 us  [step(): self.up.append(lax.ppermute(up, 'context', ahead))]
    ppermute x3, waiting for transfers between devices: 3.55 us -> 9.13 us  [per_device(): rows = lax.ppermute(rows, ('context', 'tensor'), member(e, d))]
    ppermute x3 -> x4, waiting for transfers between devices: 8.11 us -> 3.03 us  [step(): lax.ppermute(up[:half], 'context', ahead)]
    ppermute x9 -> x12, starting transfers between devices: 2.74 us -> 7.59 us  [step(): self.down.append(lax.ppermute(down, 'context', back))]
    ppermute x3 -> x4, starting transfers between devices: 1.39 us -> 4.37 us  [step(): lax.ppermute(down[half:], 'context', back)]
    ppermute x9 -> x12, waiting for transfers between devices: 8.27 us -> 5.31 us  [step(): self.down.append(lax.ppermute(down, 'context', back))]
    ppermute x1, starting transfers between devices: 0.37 us -> 2.16 us  [per_device(): mixed_theirs = lax.ppermute(mixed, 'context', sibling)]
  transfers between devices with their start and end apart: 34 -> 43, of which waited for: 20 -> 17; matrix products, arithmetic and copies ran while one was open for 4% -> 4% of each run, Pallas kernels for 4% -> 1%
where the time goes in v9:
time: 119 us
  starting transfers between devices  55 us (46%)
  waiting for transfers between devices  37.6 us (32%)
  local copies, waits for them, and re-layouts  14.3 us (12%)
  Pallas kernels  8.77 us (7%)
  other arithmetic  2.64 us (2%)
    ppermute x12, starting transfers between devices, step(): self.up.append(lax.ppermute(up, 'context', ahead))  14.6 us
    unnamed x56, local copies, waits for them, and re-layouts  10.7 us
    ppermute x3, waiting for transfers between devices, per_device(): part = lax.ppermute(part, ('context', 'tensor'), member(e, -d))  10.3 us
    ppermute x3, waiting for transfers between devices, per_device(): rows = lax.ppermute(rows, ('context', 'tensor'), member(e, d))  9.13 us
    ppermute x12, starting transfers between devices, step(): self.down.append(lax.ppermute(down, 'context', back))  7.59 us
    ppermute x1, starting transfers between devices, per_device(): first_theirs = lax.ppermute(first, 'context', sibling)  7.57 us
    ppermute x12, waiting for transfers between devices, step(): self.up.append(lax.ppermute(up, 'context', ahead))  7.29 us
    ppermute x12, waiting for transfers between devices, step(): self.down.append(lax.ppermute(down, 'context', back))  5.31 us
  transfers between devices with their start and end apart: 43, of which 17 were waited for; matrix products, arithmetic and copies ran while one was open for 4% of the time, Pallas kernels for 1%

profile of v9, /device:TPU:1, one launch (start us, length us, event | category | flops | bytes accessed | tf_op | source)
XLA Modules:
  0.0 118.7 jit_solution(2878825942116924490)
XLA Ops:
  2.2 2.2 %collective-permute-start = (bf16[256,384]{1,0:T(8,128)(2,1)S(1)}, bf16[256,384]{1,0:T(8,128)(2,1)S(1)}, u32[]{:S(2)}, u32[]{:S(2)}) collective-permute-start(bf16[256,384]{1,0:T(8,128)(2,1)S(1)} %get-tuple-element.147.refs_4_), channel_id=1, source_target_pairs={{0,8},{2,10},{8,16},{10,18},{16,24},{18,26},{24,28},{26,30},{28,20... | collective-permute-start | bytes 589832 | tf_op jit(solution)/shard_map/ppermute | solution.py:273
  5.3 1.7 %collective-permute-start.7 = (bf16[256,384]{1,0:T(8,128)(2,1)S(1)}, bf16[256,384]{1,0:T(8,128)(2,1)S(1)}, u32[]{:S(2)}, u32[]{:S(2)}) collective-permute-start(bf16[256,384]{1,0:T(8,128)(2,1)S(1)} %get-tuple-element.173.refs_4_), channel_id=1, source_target_pairs={{0,8},{2,10},{8,16},{10,18},{16,24},{18,26},{24,28},{26,30},{28,20... | collective-permute-start | bytes 589832 | tf_op jit(solution)/shard_map/ppermute | solution.py:273
  9.6 3.0 %collective-permute-start.6 = (bf16[8,64,256]{2,1,0:T(8,128)(2,1)S(1)}, bf16[8,64,256]{2,1,0:T(8,128)(2,1)S(1)}, u32[]{:S(2)}, u32[]{:S(2)}) collective-permute-start(bf16[8,64,256]{2,1,0:T(8,128)(2,1)S(1)} %get-tuple-element.118), channel_id=1, source_target_pairs={{0,3},{1,2},{2,1},{3,0},{4,7},{5,6},{6,5},{7,4},{8,11},{9,10},{10,... | collective-permute-start | bytes 786440 | tf_op jit(solution)/shard_map/ppermute | solution.py:322
  15.1 9.1 %collective-permute-done.4.refs_1_ = bf16[8,64,256]{2,1,0:T(8,128)(2,1)S(1)} collective-permute-done((bf16[8,64,256]{2,1,0:T(8,128)(2,1)S(1)}, bf16[8,64,256]{2,1,0:T(8,128)(2,1)S(1)}, u32[]{:S(2)}, u32[]{:S(2)}) %collective-permute-start.4) | collective-permute-done | bytes 262176 | tf_op jit(solution)/shard_map/ppermute | solution.py:322
  24.3 2.3 %collective-permute-start.9 = (bf16[256,384]{1,0:T(8,128)(2,1)S(1)}, bf16[256,384]{1,0:T(8,128)(2,1)S(1)}, u32[]{:S(2)}, u32[]{:S(2)}) collective-permute-start(bf16[256,384]{1,0:T(8,128)(2,1)S(1)} %collective-permute-done.8.refs_5_), channel_id=1, source_target_pairs={{8,0},{10,2},{16,8},{18,10},{24,16},{26,18},{28,24},{30,26},{20,28... | collective-permute-start | bytes 589832 | tf_op jit(solution)/shard_map/ppermute | solution.py:274
  29.2 2.3 %collective-permute-done.9.refs_6_ = bf16[256,384]{1,0:T(8,128)(2,1)S(1)} collective-permute-done((bf16[256,384]{1,0:T(8,128)(2,1)S(1)}, bf16[256,384]{1,0:T(8,128)(2,1)S(1)}, u32[]{:S(2)}, u32[]{:S(2)}) %collective-permute-start.9) | collective-permute-done | bytes 196640 | tf_op jit(solution)/shard_map/ppermute | solution.py:274
  33.7 2.7 %collective-permute-done.13.refs_10_ = bf16[256,384]{1,0:T(8,128)(2,1)S(1)} collective-permute-done((bf16[256,384]{1,0:T(8,128)(2,1)S(1)}, bf16[256,384]{1,0:T(8,128)(2,1)S(1)}, u32[]{:S(2)}, u32[]{:S(2)}) %collective-permute-start.13) | collective-permute-done | bytes 196640 | tf_op jit(solution)/shard_map/ppermute | solution.py:273
  43.9 4.7 %collective-permute-start.19 = (f32[128,256]{1,0:T(8,128)S(1)}, f32[128,256]{1,0:T(8,128)S(1)}, u32[]{:S(2)}, u32[]{:S(2)}) collective-permute-start(f32[128,256]{1,0:T(8,128)S(1)} %get-tuple-element.157), channel_id=1, source_target_pairs={{0,2},{2,0},{4,6},{6,4},{8,10},{10,8},{12,14},{14,12},{16,18},{18,... | collective-permute-start | bytes 393224 | tf_op jit(solution)/shard_map/ppermute | solution.py:376
  50.5 4.2 %all-to-all-start = ((bf16[8,128,256]{2,1,0:T(8,128)(2,1)}), bf16[8,128,256]{2,1,0:T(8,128)(2,1)S(1)}, u32[]{:S(2)}, u32[]{:S(2)}) async-start(bf16[8,128,256]{2,1,0:T(8,128)(2,1)} %bitcast.8), calls=%async_computation | async-start | bytes 1048576 | tf_op jit(solution)/shard_map/all_to_all | solution.py:389
  56.6 1.5 %collective-permute-start.15 = (bf16[128,384]{1,0:T(8,128)(2,1)S(1)}, bf16[128,384]{1,0:T(8,128)(2,1)S(1)}, u32[]{:S(2)}, u32[]{:S(2)}) collective-permute-start(bf16[128,384]{1,0:T(8,128)(2,1)S(1)} %slice.38), channel_id=1, source_target_pairs={{0,8},{2,10},{8,16},{10,18},{16,24},{18,26},{24,28},{26,30},{28,20... | collective-permute-start | bytes 294920 | tf_op jit(solution)/shard_map/ppermute | solution.py:278
  63.4 1.8 %collective-permute-done.16.refs_9_ = bf16[128,384]{1,0:T(8,128)(2,1)S(1)} collective-permute-done((bf16[128,384]{1,0:T(8,128)(2,1)S(1)}, bf16[128,384]{1,0:T(8,128)(2,1)S(1)}, u32[]{:S(2)}, u32[]{:S(2)}) %collective-permute-start.16) | collective-permute-done | bytes 98336 | tf_op jit(solution)/shard_map/ppermute | solution.py:279
  71.1 7.6 %collective-permute-start.24 = (f32[256,384]{1,0:T(8,128)S(1)}, f32[256,384]{1,0:T(8,128)S(1)}, u32[]{:S(2)}, u32[]{:S(2)}) collective-permute-start(f32[256,384]{1,0:T(8,128)S(1)} %project_queries.1.first_ref), channel_id=1, source_target_pairs={{0,2},{2,0},{4,6},{6,4},{8,10},{10,8},{12,14},{14,12},{16,18},{18,... | collective-permute-start | bytes 1179656 | tf_op jit(solution)/shard_map/ppermute | solution.py:393
  78.7 2.3 %collective-permute-start.32 = (bf16[256,256]{1,0:T(8,128)(2,1)}, bf16[256,256]{1,0:T(8,128)(2,1)S(1)}, u32[]{:S(2)}, u32[]{:S(2)}) collective-permute-start(bf16[256,256]{1,0:T(8,128)(2,1)} %collective-permute-done.28.refs_7_), channel_id=1, source_target_pairs={{0,8},{2,10},{8,16},{10,18},{16,24},{18,26},{24,28},{26,30},{28,20... | collective-permute-start | bytes 393224 | tf_op jit(solution)/shard_map/ppermute | solution.py:273
  82.7 1.6 %collective-permute-start.31 = (bf16[256,256]{1,0:T(8,128)(2,1)S(1)}, bf16[256,256]{1,0:T(8,128)(2,1)S(1)}, u32[]{:S(2)}, u32[]{:S(2)}) collective-permute-start(bf16[256,256]{1,0:T(8,128)(2,1)S(1)} %collective-permute-done.27.refs_11_), channel_id=1, source_target_pairs={{8,0},{10,2},{16,8},{18,10},{24,16},{26,18},{28,24},{30,26},{20,28... | collective-permute-start | bytes 393224 | tf_op jit(solution)/shard_map/ppermute | solution.py:274
  84.9 1.9 %collective-permute-done.32.refs_6_ = bf16[256,256]{1,0:T(8,128)(2,1)S(1)} collective-permute-done((bf16[256,256]{1,0:T(8,128)(2,1)}, bf16[256,256]{1,0:T(8,128)(2,1)S(1)}, u32[]{:S(2)}, u32[]{:S(2)}) %collective-permute-start.32) | collective-permute-done | bytes 131104 | tf_op jit(solution)/shard_map/ppermute | solution.py:273
  88.1 2.7 %collective-permute-done.33.refs_3_ = bf16[256,256]{1,0:T(8,128)(2,1)S(1)} collective-permute-done((bf16[256,256]{1,0:T(8,128)(2,1)}, bf16[256,256]{1,0:T(8,128)(2,1)S(1)}, u32[]{:S(2)}, u32[]{:S(2)}) %collective-permute-start.33) | collective-permute-done | bytes 131104 | tf_op jit(solution)/shard_map/ppermute | solution.py:274
  91.8 2.5 %attend.1.mine_ref = f32[256,640]{1,0:T(8,128)S(1)} custom-call(f32[256,384]{1,0:T(8,128)S(1)} %project_queries.1.first_ref, f32[256,384]{1,0:T(8,128)S(1)} %collective-permute-done.24.first_theirs_ref, f32[256,128]{1,0:T(8,128)S(1)} %copy-done.8, f32[256,128]{1,0:T(8,128)S(1)} %collective-permute-done.25.last_theirs_ref, ...), custom_call_target="tpu_custom_call" | custom-call | tf_op jit(solution)/shard_map/attend/pallas_call | solution.py:400
  94.3 2.2 %collective-permute-start.34 = (f32[256,640]{1,0:T(8,128)S(1)}, f32[256,640]{1,0:T(8,128)S(1)}, u32[]{:S(2)}, u32[]{:S(2)}) collective-permute-start(f32[256,640]{1,0:T(8,128)S(1)} %attend.1.mine_ref), channel_id=1, source_target_pairs={{0,2},{2,0},{4,6},{6,4},{8,10},{10,8},{12,14},{14,12},{16,18},{18,... | collective-permute-start | bytes 1966088 | tf_op jit(solution)/shard_map/ppermute | solution.py:420
  96.5 1.7 %collective-permute-start.36 = (bf16[128,256]{1,0:T(8,128)(2,1)S(1)}, bf16[128,256]{1,0:T(8,128)(2,1)S(1)}, u32[]{:S(2)}, u32[]{:S(2)}) collective-permute-start(bf16[128,256]{1,0:T(8,128)(2,1)S(1)} %slice.45), channel_id=1, source_target_pairs={{8,0},{10,2},{16,8},{18,10},{24,16},{26,18},{28,24},{30,26},{20,28... | collective-permute-start | bytes 196616 | tf_op jit(solution)/shard_map/ppermute | solution.py:279
  98.2 1.5 %collective-permute-start.38 = (bf16[128,256]{1,0:T(8,128)(2,1)S(1)}, bf16[128,256]{1,0:T(8,128)(2,1)S(1)}, u32[]{:S(2)}, u32[]{:S(2)}) collective-permute-start(bf16[128,256]{1,0:T(8,128)(2,1)S(1)} %slice.47), channel_id=1, source_target_pairs={{8,0},{10,2},{16,8},{18,10},{24,16},{26,18},{28,24},{30,26},{20,28... | collective-permute-start | bytes 196616 | tf_op jit(solution)/shard_map/ppermute | solution.py:279
  101.4 2.7 %output.1 = (bf16[8,64,256]{2,1,0:T(8,128)(2,1)S(1)}, bf16[8,64,256]{2,1,0:T(8,128)(2,1)S(1)}, bf16[8,64,256]{2,1,0:T(8,128)(2,1)S(1)}, bf16[8,64,256]{2,1,0:T(8,128)(2,1)S(1)}) custom-call(f32[256,640]{1,0:T(8,128)S(1)} %attend.1.mine_ref, f32[256,640]{1,0:T(8,128)S(1)} %collective-permute-done.34.theirs_ref, ...), custom_call_target="tpu_custom_call" | custom-call | tf_op jit(solution)/shard_map/output/pallas_call | solution.py:424
  104.2 2.0 %collective-permute-start.40 = (bf16[8,64,256]{2,1,0:T(8,128)(2,1)S(1)}, bf16[8,64,256]{2,1,0:T(8,128)(2,1)S(1)}, u32[]{:S(2)}, u32[]{:S(2)}) collective-permute-start(bf16[8,64,256]{2,1,0:T(8,128)(2,1)S(1)} %get-tuple-element.207), channel_id=1, source_target_pairs={{0,2},{1,3},{2,0},{3,1},{4,6},{5,7},{6,4},{7,5},{8,10},{9,11},{10,... | collective-permute-start | bytes 786440 | tf_op jit(solution)/shard_map/ppermute | solution.py:437
  107.5 2.7 %collective-permute-done.39.refs_1_ = bf16[8,64,256]{2,1,0:T(8,128)(2,1)S(1)} collective-permute-done((bf16[8,64,256]{2,1,0:T(8,128)(2,1)S(1)}, bf16[8,64,256]{2,1,0:T(8,128)(2,1)S(1)}, u32[]{:S(2)}, u32[]{:S(2)}) %collective-permute-start.39) | collective-permute-done | bytes 262176 | tf_op jit(solution)/shard_map/ppermute | solution.py:437
  110.2 7.6 %collective-permute-done.41.refs_3_ = bf16[8,64,256]{2,1,0:T(8,128)(2,1)S(1)} collective-permute-done((bf16[8,64,256]{2,1,0:T(8,128)(2,1)S(1)}, bf16[8,64,256]{2,1,0:T(8,128)(2,1)S(1)}, u32[]{:S(2)}, u32[]{:S(2)}) %collective-permute-start.41) | collective-permute-done | bytes 262176 | tf_op jit(solution)/shard_map/ppermute | solution.py:437
  (163 shorter events, 43.8 us)
Async XLA Ops:
  2.2 7.4 %collective-permute-start = (bf16[256,384]{1,0:T(8,128)(2,1)S(1)}, bf16[256,384]{1,0:T(8,128)(2,1)S(1)}, u32[]{:S(2)}, u32[]{:S(2)}) collective-permute-start(bf16[256,384]{1,0:T(8,128)(2,1)S(1)} %get-tuple-element.147.refs_4_), channel_id=1, source_target_pairs={{0,8},{2,10},{8,16},{10,18},{16,24},{18,26},{24,28},{26,30},{28,20... | collective-permute-start | bytes 589832 | tf_op jit(solution)/shard_map/ppermute | solution.py:273
  4.3 8.3 %collective-permute-start.1 = (bf16[256,384]{1,0:T(8,128)(2,1)S(1)}, bf16[256,384]{1,0:T(8,128)(2,1)S(1)}, u32[]{:S(2)}, u32[]{:S(2)}) collective-permute-start(bf16[256,384]{1,0:T(8,128)(2,1)S(1)} %get-tuple-element.147.refs_4_), channel_id=1, source_target_pairs={{8,0},{10,2},{16,8},{18,10},{24,16},{26,18},{28,24},{30,26},{20,28... | collective-permute-start | bytes 589832 | tf_op jit(solution)/shard_map/ppermute | solution.py:274
  4.3 22.2 %collective-permute-start.5 = (bf16[8,64,256]{2,1,0:T(8,128)(2,1)S(1)}, bf16[8,64,256]{2,1,0:T(8,128)(2,1)S(1)}, u32[]{:S(2)}, u32[]{:S(2)}) collective-permute-start(bf16[8,64,256]{2,1,0:T(8,128)(2,1)S(1)} %get-tuple-element.118), channel_id=1, source_target_pairs={{0,2},{1,3},{2,0},{3,1},{4,6},{5,7},{6,4},{7,5},{8,10},{9,11},{10,... | collective-permute-start | bytes 786440 | tf_op jit(solution)/shard_map/ppermute | solution.py:322
  5.3 7.8 %collective-permute-start.7 = (bf16[256,384]{1,0:T(8,128)(2,1)S(1)}, bf16[256,384]{1,0:T(8,128)(2,1)S(1)}, u32[]{:S(2)}, u32[]{:S(2)}) collective-permute-start(bf16[256,384]{1,0:T(8,128)(2,1)S(1)} %get-tuple-element.173.refs_4_), channel_id=1, source_target_pairs={{0,8},{2,10},{8,16},{10,18},{16,24},{18,26},{24,28},{26,30},{28,20... | collective-permute-start | bytes 589832 | tf_op jit(solution)/shard_map/ppermute | solution.py:273
  9.6 17.1 %collective-permute-start.6 = (bf16[8,64,256]{2,1,0:T(8,128)(2,1)S(1)}, bf16[8,64,256]{2,1,0:T(8,128)(2,1)S(1)}, u32[]{:S(2)}, u32[]{:S(2)}) collective-permute-start(bf16[8,64,256]{2,1,0:T(8,128)(2,1)S(1)} %get-tuple-element.118), channel_id=1, source_target_pairs={{0,3},{1,2},{2,1},{3,0},{4,7},{5,6},{6,5},{7,4},{8,11},{9,10},{10,... | collective-permute-start | bytes 786440 | tf_op jit(solution)/shard_map/ppermute | solution.py:322
  12.6 11.7 %collective-permute-start.4 = (bf16[8,64,256]{2,1,0:T(8,128)(2,1)S(1)}, bf16[8,64,256]{2,1,0:T(8,128)(2,1)S(1)}, u32[]{:S(2)}, u32[]{:S(2)}) collective-permute-start(bf16[8,64,256]{2,1,0:T(8,128)(2,1)S(1)} %get-tuple-element.169.refs_0_), channel_id=1, source_target_pairs={{0,1},{1,0},{2,3},{3,2},{4,5},{5,4},{6,7},{7,6},{8,9},{9,8},{10,11... | collective-permute-start | bytes 786440 | tf_op jit(solution)/shard_map/ppermute | solution.py:322
  13.1 13.5 %collective-permute-start.2 = (bf16[256,384]{1,0:T(8,128)(2,1)S(1)}, bf16[256,384]{1,0:T(8,128)(2,1)S(1)}, u32[]{:S(2)}, u32[]{:S(2)}) collective-permute-start(bf16[256,384]{1,0:T(8,128)(2,1)S(1)} %collective-permute-done.refs_12_), channel_id=1, source_target_pairs={{0,8},{2,10},{8,16},{10,18},{16,24},{18,26},{24,28},{26,30},{28,20... | collective-permute-start | bytes 589832 | tf_op jit(solution)/shard_map/ppermute | solution.py:273
  14.3 12.3 %collective-permute-start.3 = (bf16[256,384]{1,0:T(8,128)(2,1)S(1)}, bf16[256,384]{1,0:T(8,128)(2,1)S(1)}, u32[]{:S(2)}, u32[]{:S(2)}) collective-permute-start(bf16[256,384]{1,0:T(8,128)(2,1)S(1)} %collective-permute-done.1.refs_5_), channel_id=1, source_target_pairs={{8,0},{10,2},{16,8},{18,10},{24,16},{26,18},{28,24},{30,26},{20,28... | collective-permute-start | bytes 589832 | tf_op jit(solution)/shard_map/ppermute | solution.py:274
  26.7 9.8 %collective-permute-start.13 = (bf16[256,384]{1,0:T(8,128)(2,1)S(1)}, bf16[256,384]{1,0:T(8,128)(2,1)S(1)}, u32[]{:S(2)}, u32[]{:S(2)}) collective-permute-start(bf16[256,384]{1,0:T(8,128)(2,1)S(1)} %collective-permute-done.2.refs_11_), channel_id=1, source_target_pairs={{0,8},{2,10},{8,16},{10,18},{16,24},{18,26},{24,28},{26,30},{28,20... | collective-permute-start | bytes 589832 | tf_op jit(solution)/shard_map/ppermute | solution.py:273
  28.1 8.3 %collective-permute-start.14 = (bf16[256,384]{1,0:T(8,128)(2,1)S(1)}, bf16[256,384]{1,0:T(8,128)(2,1)S(1)}, u32[]{:S(2)}, u32[]{:S(2)}) collective-permute-start(bf16[256,384]{1,0:T(8,128)(2,1)S(1)} %collective-permute-done.3.refs_6_), channel_id=1, source_target_pairs={{8,0},{10,2},{16,8},{18,10},{24,16},{26,18},{28,24},{30,26},{20,28... | collective-permute-start | bytes 589832 | tf_op jit(solution)/shard_map/ppermute | solution.py:274
  39.8 9.1 %collective-permute-start.20 = (bf16[256,256]{1,0:T(8,128)(2,1)S(1)}, bf16[256,256]{1,0:T(8,128)(2,1)}, u32[]{:S(2)}, u32[]{:S(2)}) collective-permute-start(bf16[256,256]{1,0:T(8,128)(2,1)S(1)} %get-tuple-element.159.refs_9_), channel_id=1, source_target_pairs={{0,8},{2,10},{8,16},{10,18},{16,24},{18,26},{24,28},{26,30},{28,20... | collective-permute-start | bytes 393224 | tf_op jit(solution)/shard_map/ppermute | solution.py:273
  41.1 7.8 %collective-permute-start.21 = (bf16[256,256]{1,0:T(8,128)(2,1)S(1)}, bf16[256,256]{1,0:T(8,128)(2,1)}, u32[]{:S(2)}, u32[]{:S(2)}) collective-permute-start(bf16[256,256]{1,0:T(8,128)(2,1)S(1)} %get-tuple-element.159.refs_9_), channel_id=1, source_target_pairs={{8,0},{10,2},{16,8},{18,10},{24,16},{26,18},{28,24},{30,26},{20,28... | collective-permute-start | bytes 393224 | tf_op jit(solution)/shard_map/ppermute | solution.py:274
  41.3 7.6 %collective-permute-start.22 = (bf16[256,256]{1,0:T(8,128)(2,1)S(1)}, bf16[256,256]{1,0:T(8,128)(2,1)}, u32[]{:S(2)}, u32[]{:S(2)}) collective-permute-start(bf16[256,256]{1,0:T(8,128)(2,1)S(1)} %get-tuple-element.161.refs_0_), channel_id=1, source_target_pairs={{0,8},{2,10},{8,16},{10,18},{16,24},{18,26},{24,28},{26,30},{28,20... | collective-permute-start | bytes 393224 | tf_op jit(solution)/shard_map/ppermute | solution.py:273
  50.5 40.4 %all-to-all-start = ((bf16[8,128,256]{2,1,0:T(8,128)(2,1)}), bf16[8,128,256]{2,1,0:T(8,128)(2,1)S(1)}, u32[]{:S(2)}, u32[]{:S(2)}) async-start(bf16[8,128,256]{2,1,0:T(8,128)(2,1)} %bitcast.8), calls=%async_computation | async-start | bytes 1048576 | tf_op jit(solution)/shard_map/all_to_all | solution.py:389
  58.2 20.4 %collective-permute-start.28 = (bf16[256,256]{1,0:T(8,128)(2,1)}, bf16[256,256]{1,0:T(8,128)(2,1)}, u32[]{:S(2)}, u32[]{:S(2)}) collective-permute-start(bf16[256,256]{1,0:T(8,128)(2,1)} %collective-permute-done.22.refs_8_), channel_id=1, source_target_pairs={{0,8},{2,10},{8,16},{10,18},{16,24},{18,26},{24,28},{26,30},{28,20... | collective-permute-start | bytes 393224 | tf_op jit(solution)/shard_map/ppermute | solution.py:273
  59.7 19.0 %collective-permute-start.29 = (bf16[256,256]{1,0:T(8,128)(2,1)}, bf16[256,256]{1,0:T(8,128)(2,1)}, u32[]{:S(2)}, u32[]{:S(2)}) collective-permute-start(bf16[256,256]{1,0:T(8,128)(2,1)} %collective-permute-done.23.refs_1_), channel_id=1, source_target_pairs={{8,0},{10,2},{16,8},{18,10},{24,16},{26,18},{28,24},{30,26},{20,28... | collective-permute-start | bytes 393224 | tf_op jit(solution)/shard_map/ppermute | solution.py:274
  59.9 22.1 %collective-permute-start.26 = (bf16[256,256]{1,0:T(8,128)(2,1)}, bf16[256,256]{1,0:T(8,128)(2,1)S(1)}, u32[]{:S(2)}, u32[]{:S(2)}) collective-permute-start(bf16[256,256]{1,0:T(8,128)(2,1)} %collective-permute-done.20.refs_17_), channel_id=1, source_target_pairs={{0,8},{2,10},{8,16},{10,18},{16,24},{18,26},{24,28},{26,30},{28,20... | collective-permute-start | bytes 393224 | tf_op jit(solution)/shard_map/ppermute | solution.py:273
  63.4 18.6 %collective-permute-start.27 = (bf16[256,256]{1,0:T(8,128)(2,1)}, bf16[256,256]{1,0:T(8,128)(2,1)S(1)}, u32[]{:S(2)}, u32[]{:S(2)}) collective-permute-start(bf16[256,256]{1,0:T(8,128)(2,1)} %collective-permute-done.21.refs_10_), channel_id=1, source_target_pairs={{8,0},{10,2},{16,8},{18,10},{24,16},{26,18},{28,24},{30,26},{20,28... | collective-permute-start | bytes 393224 | tf_op jit(solution)/shard_map/ppermute | solution.py:274
  71.1 19.8 %collective-permute-start.24 = (f32[256,384]{1,0:T(8,128)S(1)}, f32[256,384]{1,0:T(8,128)S(1)}, u32[]{:S(2)}, u32[]{:S(2)}) collective-permute-start(f32[256,384]{1,0:T(8,128)S(1)} %project_queries.1.first_ref), channel_id=1, source_target_pairs={{0,2},{2,0},{4,6},{6,4},{8,10},{10,8},{12,14},{14,12},{16,18},{18,... | collective-permute-start | bytes 1179656 | tf_op jit(solution)/shard_map/ppermute | solution.py:393
  78.7 8.1 %collective-permute-start.32 = (bf16[256,256]{1,0:T(8,128)(2,1)}, bf16[256,256]{1,0:T(8,128)(2,1)S(1)}, u32[]{:S(2)}, u32[]{:S(2)}) collective-permute-start(bf16[256,256]{1,0:T(8,128)(2,1)} %collective-permute-done.28.refs_7_), channel_id=1, source_target_pairs={{0,8},{2,10},{8,16},{10,18},{16,24},{18,26},{24,28},{26,30},{28,20... | collective-permute-start | bytes 393224 | tf_op jit(solution)/shard_map/ppermute | solution.py:273
  81.7 9.2 %collective-permute-start.25 = (f32[256,128]{1,0:T(8,128)}, f32[256,128]{1,0:T(8,128)S(1)}, u32[]{:S(2)}, u32[]{:S(2)}) collective-permute-start(f32[256,128]{1,0:T(8,128)} %copy-done.7), channel_id=1, source_target_pairs={{0,2},{2,0},{4,6},{6,4},{8,10},{10,8},{12,14},{14,12},{16,18},{18,... | collective-permute-start | bytes 393224 | tf_op jit(solution)/shard_map/ppermute | solution.py:394
  82.0 8.8 %collective-permute-start.30 = (bf16[256,256]{1,0:T(8,128)(2,1)S(1)}, bf16[256,256]{1,0:T(8,128)(2,1)S(1)}, u32[]{:S(2)}, u32[]{:S(2)}) collective-permute-start(bf16[256,256]{1,0:T(8,128)(2,1)S(1)} %collective-permute-done.26.refs_16_), channel_id=1, source_target_pairs={{0,8},{2,10},{8,16},{10,18},{16,24},{18,26},{24,28},{26,30},{28,20... | collective-permute-start | bytes 393224 | tf_op jit(solution)/shard_map/ppermute | solution.py:273
  82.7 8.2 %collective-permute-start.31 = (bf16[256,256]{1,0:T(8,128)(2,1)S(1)}, bf16[256,256]{1,0:T(8,128)(2,1)S(1)}, u32[]{:S(2)}, u32[]{:S(2)}) collective-permute-start(bf16[256,256]{1,0:T(8,128)(2,1)S(1)} %collective-permute-done.27.refs_11_), channel_id=1, source_target_pairs={{8,0},{10,2},{16,8},{18,10},{24,16},{26,18},{28,24},{30,26},{20,28... | collective-permute-start | bytes 393224 | tf_op jit(solution)/shard_map/ppermute | solution.py:274
  106.2 11.6 %collective-permute-start.41 = (bf16[8,64,256]{2,1,0:T(8,128)(2,1)S(1)}, bf16[8,64,256]{2,1,0:T(8,128)(2,1)S(1)}, u32[]{:S(2)}, u32[]{:S(2)}) collective-permute-start(bf16[8,64,256]{2,1,0:T(8,128)(2,1)S(1)} %get-tuple-element.208), channel_id=1, source_target_pairs={{0,3},{1,2},{2,1},{3,0},{4,7},{5,6},{6,5},{7,4},{8,11},{9,10},{10,... | collective-permute-start | bytes 786440 | tf_op jit(solution)/shard_map/ppermute | solution.py:437
  (47 other events, 241.4 us)

commit v10 on v9

--- a/solution.py
+++ b/solution.py
@@ -63,8 +63,17 @@
     at, core = place_of(place)
     wide = hidden_ref[...].astype(jnp.float32)
     meansq = jnp.mean(wide * wide, axis=-1, keepdims=True)
-    normed = (wide * lax.rsqrt(meansq + 1e-05) * gain_ref[...].astype(jnp.float32)).astype(
-        jnp.bfloat16
+    scaled = wide * lax.rsqrt(meansq + 1e-05)
+    lanes = gain_ref.shape[1]
+    normed = jnp.concatenate(
+        [
+            (
+                scaled[:, i * lanes : (i + 1) * lanes]
+                * gain_ref[i : i + 1, :].astype(jnp.float32)
+            ).astype(jnp.bfloat16)
+            for i in range(gain_ref.shape[0])
+        ],
+        axis=1,
     )
     block = own_ref.shape[2]
     for even in range(2):
@@ -177,10 +186,7 @@
 
 def output_kernel(chips, groups, mine_ref, theirs_ref, *refs):
     weight_refs, out_refs = refs[:-groups], refs[-groups:]
-    count = len(weight_refs) // 2
-    upper = take_ring(weight_refs[:count], chips)
-    lower = take_ring(weight_refs[count:], chips)
-    weights = [a + b for a, b in zip(upper, lower)]
+    weights = take_ring(weight_refs, chips)
     chip_rows = mine_ref.shape[0]
     half = chip_rows // 2
 
@@ -305,7 +311,7 @@
         out_specs=vmem_specs(2),
         compiler_params=compute_params(),
         name="norm",
-    )(hidden_rows, norm_gain[None, :])
+    )(hidden_rows, norm_gain.reshape(-1, HD))
     last_ring = Ring(w_qkv[:, split:])
     first_ring = Ring(w_qkv[:, :split])
     normed_own, normed_other, last_ring.up[0] = ordered(
@@ -323,17 +329,12 @@
             normed.append(rows)
 
     last_ring.step()
-    first_ring.step()
-    normed = last_ring.step(normed)
-    first_ring.step()
+    normed = first_ring.step(normed)
     while not last_ring.done():
         last_ring.step()
-    while not first_ring.done():
         first_ring.step()
-    half = w_out.shape[0] // 2
-    upper_ring, lower_ring = Ring(w_out[:half]), Ring(w_out[half:])
-    upper_ring.step()
-    lower_ring.step()
+    out_ring = Ring(w_out)
+    out_ring.step()
 
     def project(blocks, outs, name):
         shapes = [
@@ -374,8 +375,8 @@
         "project_keys",
     )
     theirs = lax.ppermute(theirs, "context", sibling)
-    upper_ring.step()
-    lower_ring.step()
+    out_ring.step()
+    out_ring.step()
     mine, theirs = ordered((mine, theirs))
     kv = pl.pallas_call(
         functools.partial(keys_kernel, chips),
@@ -392,9 +393,7 @@
     (first,) = project(first_ring.finish(), [(both_rows, slice(0, split))], "project_queries")
     first_theirs = lax.ppermute(first, "context", sibling)
     last_theirs = lax.ppermute(last, "context", sibling)
-    while not lower_ring.done():
-        upper_ring.step()
-        lower_ring.step()
+    out_ring.step()
     (kv,) = ordered((kv,))
 
     mixed = pl.pallas_call(
@@ -418,7 +417,9 @@
     )
     (mixed,) = ordered((mixed,))
     mixed_theirs = lax.ppermute(mixed, "context", sibling)
-    out_blocks = upper_ring.finish() + lower_ring.finish()
+    while not out_ring.done():
+        out_ring.step()
+    out_blocks = out_ring.finish()
 
     out_block = w_out.shape[1]
     parts = pl.pallas_call(

time: 119 us -> 115 us (0.966)
  waiting for transfers between devices: 37.6 us -> 49.2 us
  local copies, waits for them, and re-layouts: 14.3 us -> 6.69 us
  starting transfers between devices: 55 us -> 48.2 us
    ppermute x4 -> x3, waiting for transfers between devices: 3.03 us -> 13.5 us  [step(): lax.ppermute(up[:half], 'context', ahead)]
    ppermute x3, waiting for transfers between devices: 9.13 us -> 0.01 us  [per_device(): rows = lax.ppermute(rows, ('context', 'tensor'), member(e, d))]
    ppermute x12 -> x9, waiting for transfers between devices: 7.29 us -> 15 us  [step(): self.up.append(lax.ppermute(up, 'context', ahead))]
    unnamed x56 -> x34, local copies, waits for them, and re-layouts: 10.7 us -> 4.75 us
    ppermute x1, starting transfers between devices: 4.75 us -> 9.69 us  [per_device(): theirs = lax.ppermute(theirs, 'context', sibling)]
    ppermute x1, starting transfers between devices: 7.57 us -> 3.2 us  [per_device(): first_theirs = lax.ppermute(first, 'context', sibling)]
    ppermute x12 -> x9, starting transfers between devices: 7.59 us -> 4.7 us  [step(): self.down.append(lax.ppermute(down, 'context', back))]
    ppermute x12 -> x9, waiting for transfers between devices: 5.31 us -> 7.76 us  [step(): self.down.append(lax.ppermute(down, 'context', back))]
  transfers between devices with their start and end apart: 43 -> 35, of which waited for: 17 -> 19; matrix products, arithmetic and copies ran while one was open for 4% -> 2% of each run, Pallas kernels for 1% -> 1%
where the time goes in v10:
time: 115 us; the launch traced here: 114 us
  waiting for transfers between devices  49.2 us (43%)
  starting transfers between devices  48.2 us (42%)
  Pallas kernels  8.47 us (7%)
  local copies, waits for them, and re-layouts  6.69 us (6%)
  other arithmetic  1.46 us (1%)
    ppermute x9, waiting for transfers between devices, step(): self.up.append(lax.ppermute(up, 'context', ahead))  15 us
    ppermute x3, waiting for transfers between devices, step(): lax.ppermute(up[:half], 'context', ahead)  13.5 us
    ppermute x9, starting transfers between devices, step(): self.up.append(lax.ppermute(up, 'context', ahead))  12.7 us
    ppermute x3, waiting for transfers between devices, per_device(): part = lax.ppermute(part, ('context', 'tensor'), member(e, -d))  11.1 us
    ppermute x1, starting transfers between devices, per_device(): theirs = lax.ppermute(theirs, 'context', sibling)  9.69 us
    ppermute x9, waiting for transfers between devices, step(): self.down.append(lax.ppermute(down, 'context', back))  7.76 us
    all_to_all x1, starting transfers between devices, per_device(): lax.all_to_all(kv, 'context', split_axis=0, concat_axis=0, axis_index_gro...  6.14 us
    unnamed x34, local copies, waits for them, and re-layouts  4.75 us
  transfers between devices with their start and end apart: 35, of which 19 were waited for; matrix products, arithmetic and copies ran while one was open for 2% of the time, Pallas kernels for 1%

profile of v10, /device:TPU:1, one launch (start us, length us, event | category | flops | bytes accessed | tf_op | source)
XLA Modules:
  0.0 114.3 jit_solution(9095087241120662108)
XLA Ops:
  1.6 2.6 %collective-permute-start.4 = (bf16[8,64,256]{2,1,0:T(8,128)(2,1)S(1)}, bf16[8,64,256]{2,1,0:T(8,128)(2,1)S(1)}, u32[]{:S(2)}, u32[]{:S(2)}) collective-permute-start(bf16[8,64,256]{2,1,0:T(8,128)(2,1)S(1)} %get-tuple-element.103), channel_id=1, source_target_pairs={{0,3},{1,2},{2,1},{3,0},{4,7},{5,6},{6,5},{7,4},{8,11},{9,10},{10,... | collective-permute-start | bytes 786440 | tf_op jit(solution)/shard_map/ppermute | solution.py:328
  4.3 1.5 %collective-permute-start.5 = (bf16[256,384]{1,0:T(8,128)(2,1)S(1)}, bf16[256,384]{1,0:T(8,128)(2,1)S(1)}, u32[]{:S(2)}, u32[]{:S(2)}) collective-permute-start(bf16[256,384]{1,0:T(8,128)(2,1)S(1)} %get-tuple-element.134.refs_4_), channel_id=1, source_target_pairs={{0,8},{2,10},{8,16},{10,18},{16,24},{18,26},{24,28},{26,30},{28,20... | collective-permute-start | bytes 589832 | tf_op jit(solution)/shard_map/ppermute | solution.py:279
  7.6 2.8 %collective-permute-done.5.refs_12_ = bf16[256,384]{1,0:T(8,128)(2,1)S(1)} collective-permute-done((bf16[256,384]{1,0:T(8,128)(2,1)S(1)}, bf16[256,384]{1,0:T(8,128)(2,1)S(1)}, u32[]{:S(2)}, u32[]{:S(2)}) %collective-permute-start.5) | collective-permute-done | bytes 196640 | tf_op jit(solution)/shard_map/ppermute | solution.py:279
  11.9 3.7 %collective-permute-done.refs_12_ = bf16[256,384]{1,0:T(8,128)(2,1)S(1)} collective-permute-done((bf16[256,384]{1,0:T(8,128)(2,1)S(1)}, bf16[256,384]{1,0:T(8,128)(2,1)S(1)}, u32[]{:S(2)}, u32[]{:S(2)}) %collective-permute-start) | collective-permute-done | bytes 196640 | tf_op jit(solution)/shard_map/ppermute | solution.py:279
  21.2 1.3 %collective-permute-start.13 = (bf16[256,384]{1,0:T(8,128)(2,1)S(1)}, bf16[256,384]{1,0:T(8,128)(2,1)S(1)}, u32[]{:S(2)}, u32[]{:S(2)}) collective-permute-start(bf16[256,384]{1,0:T(8,128)(2,1)S(1)} %collective-permute-done.9.refs_11_), channel_id=1, source_target_pairs={{0,8},{2,10},{8,16},{10,18},{16,24},{18,26},{24,28},{26,30},{28,20... | collective-permute-start | bytes 589832 | tf_op jit(solution)/shard_map/ppermute | solution.py:279
  22.6 1.5 %collective-permute-done.7.refs_6_ = bf16[256,384]{1,0:T(8,128)(2,1)S(1)} collective-permute-done((bf16[256,384]{1,0:T(8,128)(2,1)S(1)}, bf16[256,384]{1,0:T(8,128)(2,1)S(1)}, u32[]{:S(2)}, u32[]{:S(2)}) %collective-permute-start.7) | collective-permute-done | bytes 196640 | tf_op jit(solution)/shard_map/ppermute | solution.py:280
  28.0 1.4 %collective-permute-done.13.refs_10_ = bf16[256,384]{1,0:T(8,128)(2,1)S(1)} collective-permute-done((bf16[256,384]{1,0:T(8,128)(2,1)S(1)}, bf16[256,384]{1,0:T(8,128)(2,1)S(1)}, u32[]{:S(2)}, u32[]{:S(2)}) %collective-permute-start.13) | collective-permute-done | bytes 196640 | tf_op jit(solution)/shard_map/ppermute | solution.py:279
  29.5 3.2 %collective-permute-done.11.refs_7_ = bf16[256,384]{1,0:T(8,128)(2,1)S(1)} collective-permute-done((bf16[256,384]{1,0:T(8,128)(2,1)S(1)}, bf16[256,384]{1,0:T(8,128)(2,1)S(1)}, u32[]{:S(2)}, u32[]{:S(2)}) %collective-permute-start.11) | collective-permute-done | bytes 196640 | tf_op jit(solution)/shard_map/ppermute | solution.py:280
  37.1 3.9 %collective-permute-done.17.refs_8_ = bf16[128,384]{1,0:T(8,128)(2,1)S(1)} collective-permute-done((bf16[128,384]{1,0:T(8,128)(2,1)S(1)}, bf16[128,384]{1,0:T(8,128)(2,1)S(1)}, u32[]{:S(2)}, u32[]{:S(2)}) %collective-permute-start.17) | collective-permute-done | bytes 98336 | tf_op jit(solution)/shard_map/ppermute | solution.py:284
  44.1 9.7 %collective-permute-start.19 = (f32[128,256]{1,0:T(8,128)S(1)}, f32[128,256]{1,0:T(8,128)S(1)}, u32[]{:S(2)}, u32[]{:S(2)}) collective-permute-start(f32[128,256]{1,0:T(8,128)S(1)} %get-tuple-element.144), channel_id=1, source_target_pairs={{0,2},{2,0},{4,6},{6,4},{8,10},{10,8},{12,14},{14,12},{16,18},{18,... | collective-permute-start | bytes 393224 | tf_op jit(solution)/shard_map/ppermute | solution.py:377
  55.7 6.1 %all-to-all-start = ((bf16[8,128,256]{2,1,0:T(8,128)(2,1)}), bf16[8,128,256]{2,1,0:T(8,128)(2,1)S(1)}, u32[]{:S(2)}, u32[]{:S(2)}) async-start(bf16[8,128,256]{2,1,0:T(8,128)(2,1)} %bitcast.9), calls=%async_computation | async-start | bytes 1048576 | tf_op jit(solution)/shard_map/all_to_all | solution.py:390
  62.4 1.5 %collective-permute-start.15 = (bf16[128,384]{1,0:T(8,128)(2,1)S(1)}, bf16[128,384]{1,0:T(8,128)(2,1)S(1)}, u32[]{:S(2)}, u32[]{:S(2)}) collective-permute-start(bf16[128,384]{1,0:T(8,128)(2,1)S(1)} %slice.26), channel_id=1, source_target_pairs={{0,8},{2,10},{8,16},{10,18},{16,24},{18,26},{24,28},{26,30},{28,20... | collective-permute-start | bytes 294920 | tf_op jit(solution)/shard_map/ppermute | solution.py:284
  64.0 6.0 %collective-permute-done.15.refs_8_ = bf16[128,384]{1,0:T(8,128)(2,1)S(1)} collective-permute-done((bf16[128,384]{1,0:T(8,128)(2,1)S(1)}, bf16[128,384]{1,0:T(8,128)(2,1)S(1)}, u32[]{:S(2)}, u32[]{:S(2)}) %collective-permute-start.15) | collective-permute-done | bytes 98336 | tf_op jit(solution)/shard_map/ppermute | solution.py:284
  71.8 3.2 %collective-permute-start.24 = (f32[256,384]{1,0:T(8,128)S(1)}, f32[256,384]{1,0:T(8,128)S(1)}, u32[]{:S(2)}, u32[]{:S(2)}) collective-permute-start(f32[256,384]{1,0:T(8,128)S(1)} %project_queries.1.first_ref), channel_id=1, source_target_pairs={{0,2},{2,0},{4,6},{6,4},{8,10},{10,8},{12,14},{14,12},{16,18},{18,... | collective-permute-start | bytes 1179656 | tf_op jit(solution)/shard_map/ppermute | solution.py:394
  75.0 5.6 %collective-permute-start.26 = (bf16[512,256]{1,0:T(8,128)(2,1)}, bf16[512,256]{1,0:T(8,128)(2,1)S(1)}, u32[]{:S(2)}, u32[]{:S(2)}) collective-permute-start(bf16[512,256]{1,0:T(8,128)(2,1)} %collective-permute-done.22.refs_7_), channel_id=1, source_target_pairs={{0,8},{2,10},{8,16},{10,18},{16,24},{18,26},{24,28},{26,30},{28,20... | collective-permute-start | bytes 786440 | tf_op jit(solution)/shard_map/ppermute | solution.py:279
  81.2 5.3 %collective-permute-done.26.refs_6_ = bf16[512,256]{1,0:T(8,128)(2,1)S(1)} collective-permute-done((bf16[512,256]{1,0:T(8,128)(2,1)}, bf16[512,256]{1,0:T(8,128)(2,1)S(1)}, u32[]{:S(2)}, u32[]{:S(2)}) %collective-permute-start.26) | collective-permute-done | bytes 262176 | tf_op jit(solution)/shard_map/ppermute | solution.py:279
  86.5 1.8 %collective-permute-done.27.refs_3_ = bf16[512,256]{1,0:T(8,128)(2,1)S(1)} collective-permute-done((bf16[512,256]{1,0:T(8,128)(2,1)}, bf16[512,256]{1,0:T(8,128)(2,1)S(1)}, u32[]{:S(2)}, u32[]{:S(2)}) %collective-permute-start.27) | collective-permute-done | bytes 262176 | tf_op jit(solution)/shard_map/ppermute | solution.py:280
  88.3 2.5 %attend.1.mine_ref = f32[256,640]{1,0:T(8,128)S(1)} custom-call(f32[256,384]{1,0:T(8,128)S(1)} %project_queries.1.first_ref, f32[256,384]{1,0:T(8,128)S(1)} %collective-permute-done.24.first_theirs_ref, f32[256,128]{1,0:T(8,128)S(1)} %copy-done.13, f32[256,128]{1,0:T(8,128)S(1)} %collective-permute-done.25.last_theirs_ref, ...), custom_call_target="tpu_custom_call" | custom-call | tf_op jit(solution)/shard_map/attend/pallas_call | solution.py:399
  92.2 1.5 %collective-permute-start.30 = (bf16[256,256]{1,0:T(8,128)(2,1)S(1)}, bf16[256,256]{1,0:T(8,128)(2,1)S(1)}, u32[]{:S(2)}, u32[]{:S(2)}) collective-permute-start(bf16[256,256]{1,0:T(8,128)(2,1)S(1)} %slice.31), channel_id=1, source_target_pairs={{8,0},{10,2},{16,8},{18,10},{24,16},{26,18},{28,24},{30,26},{20,28... | collective-permute-start | bytes 393224 | tf_op jit(solution)/shard_map/ppermute | solution.py:285
  93.7 3.6 %collective-permute-done.29.refs_4_ = bf16[256,256]{1,0:T(8,128)(2,1)S(1)} collective-permute-done((bf16[256,256]{1,0:T(8,128)(2,1)S(1)}, bf16[256,256]{1,0:T(8,128)(2,1)S(1)}, u32[]{:S(2)}, u32[]{:S(2)}) %collective-permute-start.29) | collective-permute-done | bytes 131104 | tf_op jit(solution)/shard_map/ppermute | solution.py:284
  97.3 2.4 %output.1 = (bf16[8,64,256]{2,1,0:T(8,128)(2,1)S(1)}, bf16[8,64,256]{2,1,0:T(8,128)(2,1)S(1)}, bf16[8,64,256]{2,1,0:T(8,128)(2,1)S(1)}, bf16[8,64,256]{2,1,0:T(8,128)(2,1)S(1)}) custom-call(f32[256,640]{1,0:T(8,128)S(1)} %attend.1.mine_ref, f32[256,640]{1,0:T(8,128)S(1)} %collective-permute-done.28.theirs_ref, bf16[512,256]{1,0:T(8,128)(2,1)S(1)} %copy-done.1, ...), custom_call_target="tpu_custom_call" | custom-call | tf_op jit(solution)/shard_map/output/pallas_call | solution.py:425
  99.6 1.3 %collective-permute-start.31 = (bf16[8,64,256]{2,1,0:T(8,128)(2,1)S(1)}, bf16[8,64,256]{2,1,0:T(8,128)(2,1)S(1)}, u32[]{:S(2)}, u32[]{:S(2)}) collective-permute-start(bf16[8,64,256]{2,1,0:T(8,128)(2,1)S(1)} %get-tuple-element.182), channel_id=1, source_target_pairs={{0,1},{1,0},{2,3},{3,2},{4,5},{5,4},{6,7},{7,6},{8,9},{9,8},{10,11... | collective-permute-start | bytes 786440 | tf_op jit(solution)/shard_map/ppermute | solution.py:438
  102.2 4.4 %collective-permute-done.31.refs_1_ = bf16[8,64,256]{2,1,0:T(8,128)(2,1)S(1)} collective-permute-done((bf16[8,64,256]{2,1,0:T(8,128)(2,1)S(1)}, bf16[8,64,256]{2,1,0:T(8,128)(2,1)S(1)}, u32[]{:S(2)}, u32[]{:S(2)}) %collective-permute-start.31) | collective-permute-done | bytes 262176 | tf_op jit(solution)/shard_map/ppermute | solution.py:438
  106.7 6.7 %collective-permute-done.33.refs_3_ = bf16[8,64,256]{2,1,0:T(8,128)(2,1)S(1)} collective-permute-done((bf16[8,64,256]{2,1,0:T(8,128)(2,1)S(1)}, bf16[8,64,256]{2,1,0:T(8,128)(2,1)S(1)}, u32[]{:S(2)}, u32[]{:S(2)}) %collective-permute-start.33) | collective-permute-done | bytes 262176 | tf_op jit(solution)/shard_map/ppermute | solution.py:438
  (121 shorter events, 30.5 us)
Async XLA Ops:
  1.5 15.5 %collective-permute-start.3 = (bf16[8,64,256]{2,1,0:T(8,128)(2,1)S(1)}, bf16[8,64,256]{2,1,0:T(8,128)(2,1)S(1)}, u32[]{:S(2)}, u32[]{:S(2)}) collective-permute-start(bf16[8,64,256]{2,1,0:T(8,128)(2,1)S(1)} %get-tuple-element.103), channel_id=1, source_target_pairs={{0,2},{1,3},{2,0},{3,1},{4,6},{5,7},{6,4},{7,5},{8,10},{9,11},{10,... | collective-permute-start | bytes 786440 | tf_op jit(solution)/shard_map/ppermute | solution.py:328
  1.6 15.4 %collective-permute-start.4 = (bf16[8,64,256]{2,1,0:T(8,128)(2,1)S(1)}, bf16[8,64,256]{2,1,0:T(8,128)(2,1)S(1)}, u32[]{:S(2)}, u32[]{:S(2)}) collective-permute-start(bf16[8,64,256]{2,1,0:T(8,128)(2,1)S(1)} %get-tuple-element.103), channel_id=1, source_target_pairs={{0,3},{1,2},{2,1},{3,0},{4,7},{5,6},{6,5},{7,4},{8,11},{9,10},{10,... | collective-permute-start | bytes 786440 | tf_op jit(solution)/shard_map/ppermute | solution.py:328
  4.3 12.7 %collective-permute-start.2 = (bf16[8,64,256]{2,1,0:T(8,128)(2,1)S(1)}, bf16[8,64,256]{2,1,0:T(8,128)(2,1)S(1)}, u32[]{:S(2)}, u32[]{:S(2)}) collective-permute-start(bf16[8,64,256]{2,1,0:T(8,128)(2,1)S(1)} %get-tuple-element.156.refs_0_), channel_id=1, source_target_pairs={{0,1},{1,0},{2,3},{3,2},{4,5},{5,4},{6,7},{7,6},{8,9},{9,8},{10,11... | collective-permute-start | bytes 786440 | tf_op jit(solution)/shard_map/ppermute | solution.py:328
  17.0 7.2 %collective-permute-start.7 = (bf16[256,384]{1,0:T(8,128)(2,1)S(1)}, bf16[256,384]{1,0:T(8,128)(2,1)S(1)}, u32[]{:S(2)}, u32[]{:S(2)}) collective-permute-start(bf16[256,384]{1,0:T(8,128)(2,1)S(1)} %collective-permute-done.1.refs_5_), channel_id=1, source_target_pairs={{8,0},{10,2},{16,8},{18,10},{24,16},{26,18},{28,24},{30,26},{20,28... | collective-permute-start | bytes 589832 | tf_op jit(solution)/shard_map/ppermute | solution.py:280
  18.5 6.6 %collective-permute-start.8 = (bf16[256,384]{1,0:T(8,128)(2,1)S(1)}, bf16[256,384]{1,0:T(8,128)(2,1)S(1)}, u32[]{:S(2)}, u32[]{:S(2)}) collective-permute-start(bf16[256,384]{1,0:T(8,128)(2,1)S(1)} %collective-permute-done.refs_12_), channel_id=1, source_target_pairs={{0,8},{2,10},{8,16},{10,18},{16,24},{18,26},{24,28},{26,30},{28,20... | collective-permute-start | bytes 589832 | tf_op jit(solution)/shard_map/ppermute | solution.py:279
  21.2 8.2 %collective-permute-start.13 = (bf16[256,384]{1,0:T(8,128)(2,1)S(1)}, bf16[256,384]{1,0:T(8,128)(2,1)S(1)}, u32[]{:S(2)}, u32[]{:S(2)}) collective-permute-start(bf16[256,384]{1,0:T(8,128)(2,1)S(1)} %collective-permute-done.9.refs_11_), channel_id=1, source_target_pairs={{0,8},{2,10},{8,16},{10,18},{16,24},{18,26},{24,28},{26,30},{28,20... | collective-permute-start | bytes 589832 | tf_op jit(solution)/shard_map/ppermute | solution.py:279
  22.5 7.0 %collective-permute-start.14 = (bf16[256,384]{1,0:T(8,128)(2,1)S(1)}, bf16[256,384]{1,0:T(8,128)(2,1)S(1)}, u32[]{:S(2)}, u32[]{:S(2)}) collective-permute-start(bf16[256,384]{1,0:T(8,128)(2,1)S(1)} %collective-permute-done.10.refs_6_), channel_id=1, source_target_pairs={{8,0},{10,2},{16,8},{18,10},{24,16},{26,18},{28,24},{30,26},{20,28... | collective-permute-start | bytes 589832 | tf_op jit(solution)/shard_map/ppermute | solution.py:280
  25.1 7.5 %collective-permute-start.11 = (bf16[256,384]{1,0:T(8,128)(2,1)S(1)}, bf16[256,384]{1,0:T(8,128)(2,1)S(1)}, u32[]{:S(2)}, u32[]{:S(2)}) collective-permute-start(bf16[256,384]{1,0:T(8,128)(2,1)S(1)} %collective-permute-done.7.refs_6_), channel_id=1, source_target_pairs={{8,0},{10,2},{16,8},{18,10},{24,16},{26,18},{28,24},{30,26},{20,28... | collective-permute-start | bytes 589832 | tf_op jit(solution)/shard_map/ppermute | solution.py:280
  26.8 6.7 %collective-permute-start.12 = (bf16[256,384]{1,0:T(8,128)(2,1)S(1)}, bf16[256,384]{1,0:T(8,128)(2,1)S(1)}, u32[]{:S(2)}, u32[]{:S(2)}) collective-permute-start(bf16[256,384]{1,0:T(8,128)(2,1)S(1)} %collective-permute-done.8.refs_11_), channel_id=1, source_target_pairs={{0,8},{2,10},{8,16},{10,18},{16,24},{18,26},{24,28},{26,30},{28,20... | collective-permute-start | bytes 589832 | tf_op jit(solution)/shard_map/ppermute | solution.py:279
  33.5 7.6 %collective-permute-start.20 = (bf16[512,256]{1,0:T(8,128)(2,1)S(1)}, bf16[512,256]{1,0:T(8,128)(2,1)S(1)}, u32[]{:S(2)}, u32[]{:S(2)}) collective-permute-start(bf16[512,256]{1,0:T(8,128)(2,1)S(1)} %copy-done.1), channel_id=1, source_target_pairs={{0,8},{2,10},{8,16},{10,18},{16,24},{18,26},{24,28},{26,30},{28,20... | collective-permute-start | bytes 786440 | tf_op jit(solution)/shard_map/ppermute | solution.py:279
  34.5 6.6 %collective-permute-start.21 = (bf16[512,256]{1,0:T(8,128)(2,1)S(1)}, bf16[512,256]{1,0:T(8,128)(2,1)S(1)}, u32[]{:S(2)}, u32[]{:S(2)}) collective-permute-start(bf16[512,256]{1,0:T(8,128)(2,1)S(1)} %copy-done.1), channel_id=1, source_target_pairs={{8,0},{10,2},{16,8},{18,10},{24,16},{26,18},{28,24},{30,26},{20,28... | collective-permute-start | bytes 786440 | tf_op jit(solution)/shard_map/ppermute | solution.py:280
  41.1 12.9 %collective-permute-start.22 = (bf16[512,256]{1,0:T(8,128)(2,1)S(1)}, bf16[512,256]{1,0:T(8,128)(2,1)}, u32[]{:S(2)}, u32[]{:S(2)}) collective-permute-start(bf16[512,256]{1,0:T(8,128)(2,1)S(1)} %collective-permute-done.20.refs_8_), channel_id=1, source_target_pairs={{0,8},{2,10},{8,16},{10,18},{16,24},{18,26},{24,28},{26,30},{28,20... | collective-permute-start | bytes 786440 | tf_op jit(solution)/shard_map/ppermute | solution.py:279
  41.5 12.6 %collective-permute-start.23 = (bf16[512,256]{1,0:T(8,128)(2,1)S(1)}, bf16[512,256]{1,0:T(8,128)(2,1)}, u32[]{:S(2)}, u32[]{:S(2)}) collective-permute-start(bf16[512,256]{1,0:T(8,128)(2,1)S(1)} %collective-permute-done.21.refs_1_), channel_id=1, source_target_pairs={{8,0},{10,2},{16,8},{18,10},{24,16},{26,18},{28,24},{30,26},{20,28... | collective-permute-start | bytes 786440 | tf_op jit(solution)/shard_map/ppermute | solution.py:280
  44.1 10.7 %collective-permute-start.19 = (f32[128,256]{1,0:T(8,128)S(1)}, f32[128,256]{1,0:T(8,128)S(1)}, u32[]{:S(2)}, u32[]{:S(2)}) collective-permute-start(f32[128,256]{1,0:T(8,128)S(1)} %get-tuple-element.144), channel_id=1, source_target_pairs={{0,2},{2,0},{4,6},{6,4},{8,10},{10,8},{12,14},{14,12},{16,18},{18,... | collective-permute-start | bytes 393224 | tf_op jit(solution)/shard_map/ppermute | solution.py:377
  55.7 32.6 %all-to-all-start = ((bf16[8,128,256]{2,1,0:T(8,128)(2,1)}), bf16[8,128,256]{2,1,0:T(8,128)(2,1)S(1)}, u32[]{:S(2)}, u32[]{:S(2)}) async-start(bf16[8,128,256]{2,1,0:T(8,128)(2,1)} %bitcast.9), calls=%async_computation | async-start | bytes 1048576 | tf_op jit(solution)/shard_map/all_to_all | solution.py:390
  62.4 7.6 %collective-permute-start.15 = (bf16[128,384]{1,0:T(8,128)(2,1)S(1)}, bf16[128,384]{1,0:T(8,128)(2,1)S(1)}, u32[]{:S(2)}, u32[]{:S(2)}) collective-permute-start(bf16[128,384]{1,0:T(8,128)(2,1)S(1)} %slice.26), channel_id=1, source_target_pairs={{0,8},{2,10},{8,16},{10,18},{16,24},{18,26},{24,28},{26,30},{28,20... | collective-permute-start | bytes 294920 | tf_op jit(solution)/shard_map/ppermute | solution.py:284
  63.9 7.0 %collective-permute-start.16 = (bf16[128,384]{1,0:T(8,128)(2,1)S(1)}, bf16[128,384]{1,0:T(8,128)(2,1)S(1)}, u32[]{:S(2)}, u32[]{:S(2)}) collective-permute-start(bf16[128,384]{1,0:T(8,128)(2,1)S(1)} %slice.27), channel_id=1, source_target_pairs={{8,0},{10,2},{16,8},{18,10},{24,16},{26,18},{28,24},{30,26},{20,28... | collective-permute-start | bytes 294920 | tf_op jit(solution)/shard_map/ppermute | solution.py:285
  71.8 16.5 %collective-permute-start.24 = (f32[256,384]{1,0:T(8,128)S(1)}, f32[256,384]{1,0:T(8,128)S(1)}, u32[]{:S(2)}, u32[]{:S(2)}) collective-permute-start(f32[256,384]{1,0:T(8,128)S(1)} %project_queries.1.first_ref), channel_id=1, source_target_pairs={{0,2},{2,0},{4,6},{6,4},{8,10},{10,8},{12,14},{14,12},{16,18},{18,... | collective-permute-start | bytes 1179656 | tf_op jit(solution)/shard_map/ppermute | solution.py:394
  75.0 11.5 %collective-permute-start.26 = (bf16[512,256]{1,0:T(8,128)(2,1)}, bf16[512,256]{1,0:T(8,128)(2,1)S(1)}, u32[]{:S(2)}, u32[]{:S(2)}) collective-permute-start(bf16[512,256]{1,0:T(8,128)(2,1)} %collective-permute-done.22.refs_7_), channel_id=1, source_target_pairs={{0,8},{2,10},{8,16},{10,18},{16,24},{18,26},{24,28},{26,30},{28,20... | collective-permute-start | bytes 786440 | tf_op jit(solution)/shard_map/ppermute | solution.py:279
  80.5 7.8 %collective-permute-start.27 = (bf16[512,256]{1,0:T(8,128)(2,1)}, bf16[512,256]{1,0:T(8,128)(2,1)S(1)}, u32[]{:S(2)}, u32[]{:S(2)}) collective-permute-start(bf16[512,256]{1,0:T(8,128)(2,1)} %collective-permute-done.23.refs_2_), channel_id=1, source_target_pairs={{8,0},{10,2},{16,8},{18,10},{24,16},{26,18},{28,24},{30,26},{20,28... | collective-permute-start | bytes 786440 | tf_op jit(solution)/shard_map/ppermute | solution.py:280
  80.7 7.5 %collective-permute-start.25 = (f32[256,128]{1,0:T(8,128)S(1)}, f32[256,128]{1,0:T(8,128)S(1)}, u32[]{:S(2)}, u32[]{:S(2)}) collective-permute-start(f32[256,128]{1,0:T(8,128)S(1)} %copy-done.13), channel_id=1, source_target_pairs={{0,2},{2,0},{4,6},{6,4},{8,10},{10,8},{12,14},{14,12},{16,18},{18,... | collective-permute-start | bytes 393224 | tf_op jit(solution)/shard_map/ppermute | solution.py:395
  90.8 6.4 %collective-permute-start.28 = (f32[256,640]{1,0:T(8,128)S(1)}, f32[256,640]{1,0:T(8,128)S(1)}, u32[]{:S(2)}, u32[]{:S(2)}) collective-permute-start(f32[256,640]{1,0:T(8,128)S(1)} %attend.1.mine_ref), channel_id=1, source_target_pairs={{0,2},{2,0},{4,6},{6,4},{8,10},{10,8},{12,14},{14,12},{16,18},{18,... | collective-permute-start | bytes 1966088 | tf_op jit(solution)/shard_map/ppermute | solution.py:419
  99.6 7.0 %collective-permute-start.31 = (bf16[8,64,256]{2,1,0:T(8,128)(2,1)S(1)}, bf16[8,64,256]{2,1,0:T(8,128)(2,1)S(1)}, u32[]{:S(2)}, u32[]{:S(2)}) collective-permute-start(bf16[8,64,256]{2,1,0:T(8,128)(2,1)S(1)} %get-tuple-element.182), channel_id=1, source_target_pairs={{0,1},{1,0},{2,3},{3,2},{4,5},{5,4},{6,7},{7,6},{8,9},{9,8},{10,11... | collective-permute-start | bytes 786440 | tf_op jit(solution)/shard_map/ppermute | solution.py:438
  102.1 11.3 %collective-permute-start.33 = (bf16[8,64,256]{2,1,0:T(8,128)(2,1)S(1)}, bf16[8,64,256]{2,1,0:T(8,128)(2,1)S(1)}, u32[]{:S(2)}, u32[]{:S(2)}) collective-permute-start(bf16[8,64,256]{2,1,0:T(8,128)(2,1)S(1)} %get-tuple-element.184), channel_id=1, source_target_pairs={{0,3},{1,2},{2,1},{3,0},{4,7},{5,6},{6,5},{7,4},{8,11},{9,10},{10,... | collective-permute-start | bytes 786440 | tf_op jit(solution)/shard_map/ppermute | solution.py:438
  (28 other events, 148.9 us)

commit v11 on v10

--- a/solution.py
+++ b/solution.py
@@ -59,8 +59,7 @@
     return at, context % 2
 
 
-def norm_kernel(place, chips, hidden_ref, gain_ref, own_ref, other_ref):
-    at, core = place_of(place)
+def norm_kernel(hidden_ref, gain_ref, out_ref):
     wide = hidden_ref[...].astype(jnp.float32)
     meansq = jnp.mean(wide * wide, axis=-1, keepdims=True)
     scaled = wide * lax.rsqrt(meansq + 1e-05)
@@ -75,17 +74,9 @@
         ],
         axis=1,
     )
-    block = own_ref.shape[2]
-    for even in range(2):
-
-        @pl.when(core == even)
-        def _():
-            for chip in range(chips):
-                slot = lax.rem(place[chip] + chips - at, chips)
-                for side in range(2):
-                    column = (2 * chip + side) * block
-                    ref = own_ref if side == even else other_ref
-                    ref[slot] = normed[:, column : column + block]
+    block = out_ref.shape[2]
+    for owner in range(out_ref.shape[0]):
+        out_ref[owner] = normed[:, owner * block : (owner + 1) * block]
 
 
 def take_ring(refs, chips):
@@ -98,13 +89,20 @@
     ]
 
 
-def project_kernel(chips, groups, outs, *refs):
-    rows_refs, refs = refs[:groups], refs[groups:]
+def project_kernel(place, chips, n_tensor, outs, ring_ref, rows_ref, *refs):
     weight_refs, out_refs = refs[: -len(outs)], refs[-len(outs) :]
+    at, core = place_of(place)
+    tensor = lax.axis_index("tensor")
+    members = [
+        (core ^ e) * n_tensor + lax.rem(tensor + d, n_tensor)
+        for e in range(2)
+        for d in range(n_tensor)
+    ]
     weights = take_ring(weight_refs, chips)
     total = None
     for slot in range(chips):
-        rows = jnp.concatenate([ref[slot] for ref in rows_refs], axis=0)
+        owner = 2 * ring_ref[lax.rem(at + slot, chips)] + core
+        rows = jnp.concatenate([rows_ref[member, owner] for member in members], axis=0)
         start = 0
         for ref in weights[slot]:
             depth = ref.shape[0]
@@ -184,9 +182,8 @@
     out_ref[:, HEAD_COLS:] = stats
 
 
-def output_kernel(chips, groups, mine_ref, theirs_ref, *refs):
+def output_kernel(groups, pieces_of, mine_ref, theirs_ref, *refs):
     weight_refs, out_refs = refs[:-groups], refs[-groups:]
-    weights = take_ring(weight_refs, chips)
     chip_rows = mine_ref.shape[0]
     half = chip_rows // 2
 
@@ -207,9 +204,11 @@
         )
     mixed = jnp.concatenate(pieces, axis=1)
     rows = chip_rows // groups
-    for slot in range(chips):
+    weight_refs = iter(weight_refs)
+    for slot, pieces in enumerate(pieces_of):
         start, total = 0, None
-        for ref in weights[slot]:
+        for _ in range(pieces):
+            ref = next(weight_refs)
             depth = ref.shape[0]
             part = jnp.dot(
                 mixed[:, start : start + depth], ref[...], preferred_element_type=jnp.float32
@@ -221,16 +220,22 @@
             out_refs[group][slot] = total[group * rows : (group + 1) * rows]
 
 
-def sum_kernel(place, chips, groups, token_ref, *refs):
-    part_refs, out_ref = refs[:groups], refs[groups]
+def sum_kernel(place, chips, groups, near, token_ref, *refs):
+    near_refs, far_refs, out_ref = refs[:groups], refs[groups : 2 * groups], refs[2 * groups]
     at, core = place_of(place)
-    block = part_refs[0].shape[2]
+    block = near_refs[0].shape[2]
     half = groups // 2
 
     def added(part, slot):
-        total = part_refs[part * half][slot].astype(jnp.float32)
-        for ref in part_refs[part * half + 1 : (part + 1) * half]:
-            total += ref[slot].astype(jnp.float32)
+        turn_at = lax.rem(slot + near // 2, chips)
+        total = None
+        for group in range(part * half, (part + 1) * half):
+            rows = jnp.where(
+                turn_at < near,
+                near_refs[group][jnp.minimum(turn_at, near - 1)].astype(jnp.float32),
+                far_refs[group][jnp.maximum(turn_at - near, 0)].astype(jnp.float32),
+            )
+            total = rows if total is None else total + rows
         return total.astype(jnp.bfloat16)
 
     for even in range(2):
@@ -294,6 +299,12 @@
                 self.step()
             return self.down + self.middle + self.up[:0:-1]
 
+        def block(self, slot):
+            slot %= chips
+            if chips % 2 == 0 and slot == chips // 2:
+                return tuple(self.middle)
+            return (self.down[slot] if slot <= chips // 2 else self.up[chips - slot],)
+
     def member(e, d):
         return [
             (c * n_tensor + t, (c ^ e) * n_tensor + (t - d) % n_tensor)
@@ -303,38 +314,26 @@
 
     split = (QH_DEV - 1) * HD
 
-    normed_shape = jax.ShapeDtypeStruct((chips, rows_here, block), jnp.bfloat16)
-    normed_own, normed_other = pl.pallas_call(
-        functools.partial(norm_kernel, place, chips),
-        out_shape=[normed_shape] * 2,
+    normed = pl.pallas_call(
+        norm_kernel,
+        out_shape=jax.ShapeDtypeStruct((n_context, rows_here, block), jnp.bfloat16),
         in_specs=vmem_specs(2),
-        out_specs=vmem_specs(2),
+        out_specs=vmem_specs(1)[0],
         compiler_params=compute_params(),
         name="norm",
     )(hidden_rows, norm_gain.reshape(-1, HD))
+    sharers = [
+        [(2 * chip + k) * n_tensor + t for k in range(2) for t in range(n_tensor)]
+        for chip in range(chips)
+    ]
+    normed = lax.all_gather(normed, ("context", "tensor"), axis_index_groups=sharers)
     last_ring = Ring(w_qkv[:, split:])
     first_ring = Ring(w_qkv[:, :split])
-    normed_own, normed_other, last_ring.up[0] = ordered(
-        (normed_own, normed_other, last_ring.up[0])
-    )
-    last_ring.down[0] = last_ring.up[0]
     last_ring.step()
     first_ring.step()
-    normed = []
-    for e in range(2):
-        for d in range(n_tensor):
-            rows = normed_own if e == 0 else normed_other
-            if e or d:
-                rows = lax.ppermute(rows, ("context", "tensor"), member(e, d))
-            normed.append(rows)
-
-    last_ring.step()
-    normed = first_ring.step(normed)
     while not last_ring.done():
         last_ring.step()
         first_ring.step()
-    out_ring = Ring(w_out)
-    out_ring.step()
 
     def project(blocks, outs, name):
         shapes = [
@@ -342,13 +341,13 @@
             for rows, columns in outs
         ]
         return pl.pallas_call(
-            functools.partial(project_kernel, chips, groups, outs),
+            functools.partial(project_kernel, place, chips, n_tensor, outs),
             out_shape=shapes,
-            in_specs=vmem_specs(groups + len(blocks)),
+            in_specs=[pl.BlockSpec(memory_space=pltpu.SMEM)] + vmem_specs(1 + len(blocks)),
             out_specs=vmem_specs(len(outs)),
             compiler_params=compute_params(),
             name=name,
-        )(*ordered((*normed, *blocks)))
+        )(jnp.asarray(ring, jnp.int32), *ordered((normed, *blocks)))
 
     doc_ends = jnp.cumsum(doc_lengths)
     inside = (
@@ -375,7 +374,11 @@
         "project_keys",
     )
     theirs = lax.ppermute(theirs, "context", sibling)
+    out_ring = Ring(w_out)
     out_ring.step()
+    (first,) = project(first_ring.finish(), [(both_rows, slice(0, split))], "project_queries")
+    first_theirs = lax.ppermute(first, "context", sibling)
+    last_theirs = lax.ppermute(last, "context", sibling)
     out_ring.step()
     mine, theirs = ordered((mine, theirs))
     kv = pl.pallas_call(
@@ -390,10 +393,6 @@
     kv = lax.all_to_all(
         kv, "context", split_axis=0, concat_axis=0, axis_index_groups=same_core, tiled=True
     )
-    (first,) = project(first_ring.finish(), [(both_rows, slice(0, split))], "project_queries")
-    first_theirs = lax.ppermute(first, "context", sibling)
-    last_theirs = lax.ppermute(last, "context", sibling)
-    out_ring.step()
     (kv,) = ordered((kv,))
 
     mixed = pl.pallas_call(
@@ -415,32 +414,46 @@
         key_orig[None, :],
         kv,
     )
+    out_ring.step()
     (mixed,) = ordered((mixed,))
     mixed_theirs = lax.ppermute(mixed, "context", sibling)
+
+    out_block = w_out.shape[1]
+
+    def output(slots, name):
+        blocks = [out_ring.block(slot) for slot in slots]
+        flat = [piece for pieces in blocks for piece in pieces]
+        parts = pl.pallas_call(
+            functools.partial(output_kernel, groups, [len(pieces) for pieces in blocks]),
+            out_shape=[jax.ShapeDtypeStruct((len(slots), rows_here, out_block), jnp.bfloat16)]
+            * groups,
+            in_specs=vmem_specs(2 + len(flat)),
+            out_specs=vmem_specs(groups),
+            compiler_params=compute_params(),
+            name=name,
+        )(mixed, mixed_theirs, *flat)
+        parts = ordered(parts)
+        arrived = []
+        for e in range(2):
+            for d in range(n_tensor):
+                part = parts[e * n_tensor + d]
+                if e or d:
+                    part = lax.ppermute(part, ("context", "tensor"), member(e, -d))
+                arrived.append(part)
+        return arrived
+
+    reach = max(chips // 2 - 2, 0)
+    while len(out_ring.up) <= reach:
+        out_ring.step()
+    near = 2 * reach + 1
+    arrived = output(list(range(-reach, reach + 1)), "output_near")
     while not out_ring.done():
         out_ring.step()
-    out_blocks = out_ring.finish()
-
-    out_block = w_out.shape[1]
-    parts = pl.pallas_call(
-        functools.partial(output_kernel, chips, groups),
-        out_shape=[jax.ShapeDtypeStruct((chips, rows_here, out_block), jnp.bfloat16)] * groups,
-        in_specs=vmem_specs(2 + len(out_blocks)),
-        out_specs=vmem_specs(groups),
-        compiler_params=compute_params(),
-        name="output",
-    )(mixed, mixed_theirs, *out_blocks)
-    arrived = []
-    for e in range(2):
-        for d in range(n_tensor):
-            part = parts[e * n_tensor + d]
-            if e or d:
-                part = lax.ppermute(part, ("context", "tensor"), member(e, -d))
-            arrived.append(part)
+    arrived += output(list(range(reach + 1, chips - reach)), "output_far")
     return pl.pallas_call(
-        functools.partial(sum_kernel, place, chips, groups),
+        functools.partial(sum_kernel, place, chips, groups, near),
         out_shape=jax.ShapeDtypeStruct((rows_here, n_context * out_block), jnp.bfloat16),
-        in_specs=[pl.BlockSpec(memory_space=pl.ANY)] + vmem_specs(groups),
+        in_specs=[pl.BlockSpec(memory_space=pl.ANY)] + vmem_specs(2 * groups),
         out_specs=vmem_specs(1)[0],
         compiler_params=compute_params(),
         name="sum",

time: 115 us -> 125 us (1.087)
  between operations: 0.31 us -> 13.8 us
  waiting for transfers between devices: 49.2 us -> 40.2 us
  local copies, waits for them, and re-layouts: 6.69 us -> 14.4 us
  starting transfers between devices: 48.2 us -> 42 us
  Pallas kernels: 8.47 us -> 11.3 us
  other arithmetic: 1.46 us -> 2.89 us
    ppermute x9, waiting for transfers between devices: 15 us -> 25.1 us  [step(): self.up.append(lax.ppermute(up, 'context', ahead))]
    unnamed x34 -> x58, local copies, waits for them, and re-layouts: 4.75 us -> 12.6 us
    ppermute x3, waiting for transfers between devices: 13.5 us -> 5.74 us  [step(): lax.ppermute(up[:half], 'context', ahead)]
    ppermute x6, waiting for transfers between devices: 11.1 us -> 4.39 us  [output(): part = lax.ppermute(part, ('context', 'tensor'), member(e, -d))]
    ppermute x9, starting transfers between devices: 12.7 us -> 6.66 us  [step(): self.up.append(lax.ppermute(up, 'context', ahead))]
    ppermute x9, waiting for transfers between devices: 7.76 us -> 3.58 us  [step(): self.down.append(lax.ppermute(down, 'context', back))]
    ppermute x9, starting transfers between devices: 4.7 us -> 7.7 us  [step(): self.down.append(lax.ppermute(down, 'context', back))]
    pallas_call x5 -> x6, Pallas kernels: 5.05 us -> 7.9 us  [the longest x2 3.19 us: output(): pl.pallas_call(functools.partial(output_kernel, groups, [len(pieces) for...]
  transfers between devices with their start and end apart: 35 -> 36, of which waited for: 19 -> 12; matrix products, arithmetic and copies ran while one was open for 2% -> 4% of each run, Pallas kernels for 1% -> 5%
where the time goes in v11:
time: 125 us
  starting transfers between devices  42 us (34%)
  waiting for transfers between devices  40.2 us (32%)
  local copies, waits for them, and re-layouts  14.4 us (12%)
  between operations  13.8 us (11%)
  Pallas kernels  11.3 us (9%)
  other arithmetic  2.89 us (2%)
    ppermute x9, waiting for transfers between devices, step(): self.up.append(lax.ppermute(up, 'context', ahead))  25.1 us
    unnamed x58, local copies, waits for them, and re-layouts  12.6 us
    ppermute x6, starting transfers between devices, output(): part = lax.ppermute(part, ('context', 'tensor'), member(e, -d))  8 us
    ppermute x9, starting transfers between devices, step(): self.down.append(lax.ppermute(down, 'context', back))  7.7 us
    ppermute x1, starting transfers between devices, per_device(): theirs = lax.ppermute(theirs, 'context', sibling)  6.95 us
    ppermute x9, starting transfers between devices, step(): self.up.append(lax.ppermute(up, 'context', ahead))  6.66 us
    ppermute x3, waiting for transfers between devices, step(): lax.ppermute(up[:half], 'context', ahead)  5.74 us
    all_to_all x1, starting transfers between devices, per_device(): lax.all_to_all(kv, 'context', split_axis=0, concat_axis=0, axis_index_gro...  4.58 us
  transfers between devices with their start and end apart: 36, of which 12 were waited for; matrix products, arithmetic and copies ran while one was open for 4% of the time, Pallas kernels for 5%

profile of v11, /device:TPU:1, one launch (start us, length us, event | category | flops | bytes accessed | tf_op | source)
XLA Modules:
  0.0 124.6 jit_solution(10562076065804825595)
XLA Ops:
  10.5 2.1 %collective-permute-start = (bf16[256,384]{1,0:T(8,128)(2,1)S(1)}, bf16[256,384]{1,0:T(8,128)(2,1)S(1)}, u32[]{:S(2)}, u32[]{:S(2)}) collective-permute-start(bf16[256,384]{1,0:T(8,128)(2,1)S(1)} %get-tuple-element.120.refs_0_), channel_id=1, source_target_pairs={{8,0},{10,2},{16,8},{18,10},{24,16},{26,18},{28,24},{30,26},{20,28... | collective-permute-start | bytes 589832 | tf_op jit(solution)/shard_map/ppermute | solution.py:285
  12.7 1.4 %collective-permute-start.2 = (bf16[256,384]{1,0:T(8,128)(2,1)S(1)}, bf16[256,384]{1,0:T(8,128)(2,1)S(1)}, u32[]{:S(2)}, u32[]{:S(2)}) collective-permute-start(bf16[256,384]{1,0:T(8,128)(2,1)S(1)} %get-tuple-element.130.refs_0_), channel_id=1, source_target_pairs={{0,8},{2,10},{8,16},{10,18},{16,24},{18,26},{24,28},{26,30},{28,20... | collective-permute-start | bytes 589832 | tf_op jit(solution)/shard_map/ppermute | solution.py:284
  14.9 7.5 %collective-permute-done.2.refs_8_ = bf16[256,384]{1,0:T(8,128)(2,1)S(1)} collective-permute-done((bf16[256,384]{1,0:T(8,128)(2,1)S(1)}, bf16[256,384]{1,0:T(8,128)(2,1)S(1)}, u32[]{:S(2)}, u32[]{:S(2)}) %collective-permute-start.2) | collective-permute-done | bytes 196640 | tf_op jit(solution)/shard_map/ppermute | solution.py:284
  22.4 1.3 %collective-permute-start.4 = (bf16[256,384]{1,0:T(8,128)(2,1)S(1)}, bf16[256,384]{1,0:T(8,128)(2,1)S(1)}, u32[]{:S(2)}, u32[]{:S(2)}) collective-permute-start(bf16[256,384]{1,0:T(8,128)(2,1)S(1)} %collective-permute-done.refs_1_), channel_id=1, source_target_pairs={{8,0},{10,2},{16,8},{18,10},{24,16},{26,18},{28,24},{30,26},{20,28... | collective-permute-start | bytes 589832 | tf_op jit(solution)/shard_map/ppermute | solution.py:285
  25.4 7.0 %collective-permute-done.6.refs_7_ = bf16[256,384]{1,0:T(8,128)(2,1)S(1)} collective-permute-done((bf16[256,384]{1,0:T(8,128)(2,1)S(1)}, bf16[256,384]{1,0:T(8,128)(2,1)S(1)}, u32[]{:S(2)}, u32[]{:S(2)}) %collective-permute-start.6) | collective-permute-done | bytes 196640 | tf_op jit(solution)/shard_map/ppermute | solution.py:284
  32.4 1.3 %collective-permute-start.8 = (bf16[256,384]{1,0:T(8,128)(2,1)S(1)}, bf16[256,384]{1,0:T(8,128)(2,1)S(1)}, u32[]{:S(2)}, u32[]{:S(2)}) collective-permute-start(bf16[256,384]{1,0:T(8,128)(2,1)S(1)} %collective-permute-done.4.refs_2_), channel_id=1, source_target_pairs={{8,0},{10,2},{16,8},{18,10},{24,16},{26,18},{28,24},{30,26},{20,28... | collective-permute-start | bytes 589832 | tf_op jit(solution)/shard_map/ppermute | solution.py:285
  35.4 1.3 %fusion.2 = (f32[256,64]{1,0:T(8,128)}, f32[256,64]{1,0:T(8,128)}, f32[256,64]{1,0:T(8,128)}) fusion(f32[64]{0:T(128)S(1)} %negate_power_fusion, f32[256]{0:T(256)S(1)} %subtract_convert_fusion), kind=kLoop, calls=%fused_computation.11 | loop fusion | flops 32768 | bytes 197888 | tf_op jit(solution)/shard_map/neg | solution.py:364
  36.7 4.5 %collective-permute-done.10.refs_6_ = bf16[256,384]{1,0:T(8,128)(2,1)S(1)} collective-permute-done((bf16[256,384]{1,0:T(8,128)(2,1)S(1)}, bf16[256,384]{1,0:T(8,128)(2,1)S(1)}, u32[]{:S(2)}, u32[]{:S(2)}) %collective-permute-start.10) | collective-permute-done | bytes 196640 | tf_op jit(solution)/shard_map/ppermute | solution.py:284
  42.9 2.9 %collective-permute-done.14.refs_4_ = bf16[128,384]{1,0:T(8,128)(2,1)S(1)} collective-permute-done((bf16[128,384]{1,0:T(8,128)(2,1)S(1)}, bf16[128,384]{1,0:T(8,128)(2,1)S(1)}, u32[]{:S(2)}, u32[]{:S(2)}) %collective-permute-start.14) | collective-permute-done | bytes 98336 | tf_op jit(solution)/shard_map/ppermute | solution.py:289
  47.3 1.6 %copy-done = bf16[64,64,256]{2,1,0:T(8,128)(2,1)S(1)} copy-done((bf16[64,64,256]{2,1,0:T(8,128)(2,1)S(1)}, bf16[64,64,256]{2,1,0:T(8,128)(2,1)}, u32[]{:S(2)}) %copy-start) | copy-done | bytes 2097176
  50.3 6.9 %collective-permute-start.18 = (f32[128,256]{1,0:T(8,128)S(1)}, f32[128,256]{1,0:T(8,128)S(1)}, u32[]{:S(2)}, u32[]{:S(2)}) collective-permute-start(f32[128,256]{1,0:T(8,128)S(1)} %get-tuple-element.141), channel_id=1, source_target_pairs={{0,2},{2,0},{4,6},{6,4},{8,10},{10,8},{12,14},{14,12},{16,18},{18,... | collective-permute-start | bytes 393224 | tf_op jit(solution)/shard_map/ppermute | solution.py:376
  57.5 1.7 %collective-permute-start.13 = (bf16[128,384]{1,0:T(8,128)(2,1)S(1)}, bf16[128,384]{1,0:T(8,128)(2,1)S(1)}, u32[]{:S(2)}, u32[]{:S(2)}) collective-permute-start(bf16[128,384]{1,0:T(8,128)(2,1)S(1)} %slice.27), channel_id=1, source_target_pairs={{8,0},{10,2},{16,8},{18,10},{24,16},{26,18},{28,24},{30,26},{20,28... | collective-permute-start | bytes 294920 | tf_op jit(solution)/shard_map/ppermute | solution.py:290
  59.3 2.8 %collective-permute-done.12.refs_4_ = bf16[128,384]{1,0:T(8,128)(2,1)S(1)} collective-permute-done((bf16[128,384]{1,0:T(8,128)(2,1)S(1)}, bf16[128,384]{1,0:T(8,128)(2,1)S(1)}, u32[]{:S(2)}, u32[]{:S(2)}) %collective-permute-start.12) | collective-permute-done | bytes 98336 | tf_op jit(solution)/shard_map/ppermute | solution.py:289
  63.0 4.6 %all-to-all-start = ((bf16[8,128,256]{2,1,0:T(8,128)(2,1)}), bf16[8,128,256]{2,1,0:T(8,128)(2,1)S(1)}, u32[]{:S(2)}, u32[]{:S(2)}) async-start(bf16[8,128,256]{2,1,0:T(8,128)(2,1)} %bitcast.10), calls=%async_computation | async-start | bytes 1048576 | tf_op jit(solution)/shard_map/all_to_all | solution.py:393
  77.5 1.5 %collective-permute-start.16 = (f32[256,384]{1,0:T(8,128)S(1)}, f32[256,384]{1,0:T(8,128)S(1)}, u32[]{:S(2)}, u32[]{:S(2)}) collective-permute-start(f32[256,384]{1,0:T(8,128)S(1)} %project_queries.1.first_ref), channel_id=1, source_target_pairs={{0,2},{2,0},{4,6},{6,4},{8,10},{10,8},{12,14},{14,12},{16,18},{18,... | collective-permute-start | bytes 1179656 | tf_op jit(solution)/shard_map/ppermute | solution.py:380
  79.0 1.7 %collective-permute-start.21 = (bf16[512,256]{1,0:T(8,128)(2,1)}, bf16[512,256]{1,0:T(8,128)(2,1)S(1)}, u32[]{:S(2)}, u32[]{:S(2)}) collective-permute-start(bf16[512,256]{1,0:T(8,128)(2,1)} %collective-permute-done.19.refs_1_), channel_id=1, source_target_pairs={{0,8},{2,10},{8,16},{10,18},{16,24},{18,26},{24,28},{26,30},{28,20... | collective-permute-start | bytes 786440 | tf_op jit(solution)/shard_map/ppermute | solution.py:284
  81.5 6.1 %collective-permute-done.21.refs_0_ = bf16[512,256]{1,0:T(8,128)(2,1)S(1)} collective-permute-done((bf16[512,256]{1,0:T(8,128)(2,1)}, bf16[512,256]{1,0:T(8,128)(2,1)S(1)}, u32[]{:S(2)}, u32[]{:S(2)}) %collective-permute-start.21) | collective-permute-done | bytes 262176 | tf_op jit(solution)/shard_map/ppermute | solution.py:284
  90.3 2.5 %attend.1.mine_ref = f32[256,640]{1,0:T(8,128)S(1)} custom-call(f32[256,384]{1,0:T(8,128)S(1)} %project_queries.1.first_ref, f32[256,384]{1,0:T(8,128)S(1)} %collective-permute-done.16.first_theirs_ref, f32[256,128]{1,0:T(8,128)S(1)} %copy-done.17, f32[256,128]{1,0:T(8,128)S(1)} %collective-permute-done.17.last_theirs_ref, ...), custom_call_target="tpu_custom_call" | custom-call | tf_op jit(solution)/shard_map/attend/pallas_call | solution.py:398
  95.8 2.2 %output_near.1 = (bf16[5,64,256]{2,1,0:T(8,128)(2,1)S(1)}, bf16[5,64,256]{2,1,0:T(8,128)(2,1)S(1)}, bf16[5,64,256]{2,1,0:T(8,128)(2,1)S(1)}, bf16[5,64,256]{2,1,0:T(8,128)(2,1)S(1)}) custom-call(f32[256,640]{1,0:T(8,128)S(1)} %attend.1.mine_ref, f32[256,640]{1,0:T(8,128)S(1)} %collective-permute-done.23.theirs_ref, ...), custom_call_target="tpu_custom_call" | custom-call | tf_op jit(solution)/shard_map/output_near/pallas_call | solution.py:426
  99.3 2.6 %collective-permute-done.24.refs_0_ = bf16[512,256]{1,0:T(8,128)(2,1)S(1)} collective-permute-done((bf16[512,256]{1,0:T(8,128)(2,1)S(1)}, bf16[512,256]{1,0:T(8,128)(2,1)S(1)}, u32[]{:S(2)}, u32[]{:S(2)}) %collective-permute-start.24) | collective-permute-done | bytes 262176 | tf_op jit(solution)/shard_map/ppermute | solution.py:285
  103.5 1.6 %collective-permute-start.29 = (bf16[5,64,256]{2,1,0:T(8,128)(2,1)S(1)}, bf16[5,64,256]{2,1,0:T(8,128)(2,1)S(1)}, u32[]{:S(2)}, u32[]{:S(2)}) collective-permute-start(bf16[5,64,256]{2,1,0:T(8,128)(2,1)S(1)} %get-tuple-element.175), channel_id=1, source_target_pairs={{0,2},{1,3},{2,0},{3,1},{4,6},{5,7},{6,4},{7,5},{8,10},{9,11},{10,... | collective-permute-start | bytes 491528 | tf_op jit(solution)/shard_map/ppermute | solution.py:441
  108.3 1.3 %collective-permute-start.31 = (bf16[3,64,256]{2,1,0:T(8,128)(2,1)S(1)}, bf16[3,64,256]{2,1,0:T(8,128)(2,1)S(1)}, u32[]{:S(2)}, u32[]{:S(2)}) collective-permute-start(bf16[3,64,256]{2,1,0:T(8,128)(2,1)S(1)} %get-tuple-element.178), channel_id=1, source_target_pairs={{0,1},{1,0},{2,3},{3,2},{4,5},{5,4},{6,7},{7,6},{8,9},{9,8},{10,11... | collective-permute-start | bytes 294920 | tf_op jit(solution)/shard_map/ppermute | solution.py:441
  109.6 2.5 %collective-permute-start.32 = (bf16[3,64,256]{2,1,0:T(8,128)(2,1)S(1)}, bf16[3,64,256]{2,1,0:T(8,128)(2,1)S(1)}, u32[]{:S(2)}, u32[]{:S(2)}) collective-permute-start(bf16[3,64,256]{2,1,0:T(8,128)(2,1)S(1)} %get-tuple-element.179), channel_id=1, source_target_pairs={{0,2},{1,3},{2,0},{3,1},{4,6},{5,7},{6,4},{7,5},{8,10},{9,11},{10,... | collective-permute-start | bytes 294920 | tf_op jit(solution)/shard_map/ppermute | solution.py:441
  113.1 3.6 %collective-permute-done.33.refs_7_ = bf16[3,64,256]{2,1,0:T(8,128)(2,1)S(1)} collective-permute-done((bf16[3,64,256]{2,1,0:T(8,128)(2,1)S(1)}, bf16[3,64,256]{2,1,0:T(8,128)(2,1)S(1)}, u32[]{:S(2)}, u32[]{:S(2)}) %collective-permute-start.33) | collective-permute-done | bytes 98336 | tf_op jit(solution)/shard_map/ppermute | solution.py:441
  (149 shorter events, 38.1 us)
Async XLA Ops:
  6.5 39.2 %all-gather.3.cloned.1.call-start = ((), (), s32[]{:S(2)}) async-start(), calls=%async_computation.1 | async-start | bytes 2621440 | tf_op jit(solution)/shard_map/all_gather | solution.py:329
  10.5 11.9 %collective-permute-start = (bf16[256,384]{1,0:T(8,128)(2,1)S(1)}, bf16[256,384]{1,0:T(8,128)(2,1)S(1)}, u32[]{:S(2)}, u32[]{:S(2)}) collective-permute-start(bf16[256,384]{1,0:T(8,128)(2,1)S(1)} %get-tuple-element.120.refs_0_), channel_id=1, source_target_pairs={{8,0},{10,2},{16,8},{18,10},{24,16},{26,18},{28,24},{30,26},{20,28... | collective-permute-start | bytes 589832 | tf_op jit(solution)/shard_map/ppermute | solution.py:285
  12.6 9.8 %collective-permute-start.1 = (bf16[256,384]{1,0:T(8,128)(2,1)S(1)}, bf16[256,384]{1,0:T(8,128)(2,1)S(1)}, u32[]{:S(2)}, u32[]{:S(2)}) collective-permute-start(bf16[256,384]{1,0:T(8,128)(2,1)S(1)} %get-tuple-element.120.refs_0_), channel_id=1, source_target_pairs={{0,8},{2,10},{8,16},{10,18},{16,24},{18,26},{24,28},{26,30},{28,20... | collective-permute-start | bytes 589832 | tf_op jit(solution)/shard_map/ppermute | solution.py:284
  12.7 9.6 %collective-permute-start.2 = (bf16[256,384]{1,0:T(8,128)(2,1)S(1)}, bf16[256,384]{1,0:T(8,128)(2,1)S(1)}, u32[]{:S(2)}, u32[]{:S(2)}) collective-permute-start(bf16[256,384]{1,0:T(8,128)(2,1)S(1)} %get-tuple-element.130.refs_0_), channel_id=1, source_target_pairs={{0,8},{2,10},{8,16},{10,18},{16,24},{18,26},{24,28},{26,30},{28,20... | collective-permute-start | bytes 589832 | tf_op jit(solution)/shard_map/ppermute | solution.py:284
  14.1 8.2 %collective-permute-start.3 = (bf16[256,384]{1,0:T(8,128)(2,1)S(1)}, bf16[256,384]{1,0:T(8,128)(2,1)S(1)}, u32[]{:S(2)}, u32[]{:S(2)}) collective-permute-start(bf16[256,384]{1,0:T(8,128)(2,1)S(1)} %get-tuple-element.130.refs_0_), channel_id=1, source_target_pairs={{8,0},{10,2},{16,8},{18,10},{24,16},{26,18},{28,24},{30,26},{20,28... | collective-permute-start | bytes 589832 | tf_op jit(solution)/shard_map/ppermute | solution.py:285
  22.4 10.0 %collective-permute-start.4 = (bf16[256,384]{1,0:T(8,128)(2,1)S(1)}, bf16[256,384]{1,0:T(8,128)(2,1)S(1)}, u32[]{:S(2)}, u32[]{:S(2)}) collective-permute-start(bf16[256,384]{1,0:T(8,128)(2,1)S(1)} %collective-permute-done.refs_1_), channel_id=1, source_target_pairs={{8,0},{10,2},{16,8},{18,10},{24,16},{26,18},{28,24},{30,26},{20,28... | collective-permute-start | bytes 589832 | tf_op jit(solution)/shard_map/ppermute | solution.py:285
  23.8 8.7 %collective-permute-start.5 = (bf16[256,384]{1,0:T(8,128)(2,1)S(1)}, bf16[256,384]{1,0:T(8,128)(2,1)S(1)}, u32[]{:S(2)}, u32[]{:S(2)}) collective-permute-start(bf16[256,384]{1,0:T(8,128)(2,1)S(1)} %collective-permute-done.1.refs_8_), channel_id=1, source_target_pairs={{0,8},{2,10},{8,16},{10,18},{16,24},{18,26},{24,28},{26,30},{28,20... | collective-permute-start | bytes 589832 | tf_op jit(solution)/shard_map/ppermute | solution.py:284
  23.9 8.5 %collective-permute-start.6 = (bf16[256,384]{1,0:T(8,128)(2,1)S(1)}, bf16[256,384]{1,0:T(8,128)(2,1)S(1)}, u32[]{:S(2)}, u32[]{:S(2)}) collective-permute-start(bf16[256,384]{1,0:T(8,128)(2,1)S(1)} %collective-permute-done.2.refs_8_), channel_id=1, source_target_pairs={{0,8},{2,10},{8,16},{10,18},{16,24},{18,26},{24,28},{26,30},{28,20... | collective-permute-start | bytes 589832 | tf_op jit(solution)/shard_map/ppermute | solution.py:284
  24.3 8.1 %collective-permute-start.7 = (bf16[256,384]{1,0:T(8,128)(2,1)S(1)}, bf16[256,384]{1,0:T(8,128)(2,1)S(1)}, u32[]{:S(2)}, u32[]{:S(2)}) collective-permute-start(bf16[256,384]{1,0:T(8,128)(2,1)S(1)} %collective-permute-done.3.refs_1_), channel_id=1, source_target_pairs={{8,0},{10,2},{16,8},{18,10},{24,16},{26,18},{28,24},{30,26},{20,28... | collective-permute-start | bytes 589832 | tf_op jit(solution)/shard_map/ppermute | solution.py:285
  32.4 10.4 %collective-permute-start.8 = (bf16[256,384]{1,0:T(8,128)(2,1)S(1)}, bf16[256,384]{1,0:T(8,128)(2,1)S(1)}, u32[]{:S(2)}, u32[]{:S(2)}) collective-permute-start(bf16[256,384]{1,0:T(8,128)(2,1)S(1)} %collective-permute-done.4.refs_2_), channel_id=1, source_target_pairs={{8,0},{10,2},{16,8},{18,10},{24,16},{26,18},{28,24},{30,26},{20,28... | collective-permute-start | bytes 589832 | tf_op jit(solution)/shard_map/ppermute | solution.py:285
  33.8 9.1 %collective-permute-start.9 = (bf16[256,384]{1,0:T(8,128)(2,1)S(1)}, bf16[256,384]{1,0:T(8,128)(2,1)S(1)}, u32[]{:S(2)}, u32[]{:S(2)}) collective-permute-start(bf16[256,384]{1,0:T(8,128)(2,1)S(1)} %collective-permute-done.5.refs_7_), channel_id=1, source_target_pairs={{0,8},{2,10},{8,16},{10,18},{16,24},{18,26},{24,28},{26,30},{28,20... | collective-permute-start | bytes 589832 | tf_op jit(solution)/shard_map/ppermute | solution.py:284
  34.0 7.3 %collective-permute-start.10 = (bf16[256,384]{1,0:T(8,128)(2,1)S(1)}, bf16[256,384]{1,0:T(8,128)(2,1)S(1)}, u32[]{:S(2)}, u32[]{:S(2)}) collective-permute-start(bf16[256,384]{1,0:T(8,128)(2,1)S(1)} %collective-permute-done.6.refs_7_), channel_id=1, source_target_pairs={{0,8},{2,10},{8,16},{10,18},{16,24},{18,26},{24,28},{26,30},{28,20... | collective-permute-start | bytes 589832 | tf_op jit(solution)/shard_map/ppermute | solution.py:284
  45.8 16.3 %collective-permute-start.19 = (bf16[512,256]{1,0:T(8,128)(2,1)}, bf16[512,256]{1,0:T(8,128)(2,1)}, u32[]{:S(2)}, u32[]{:S(2)}) collective-permute-start(bf16[512,256]{1,0:T(8,128)(2,1)} %refs_2_.1), channel_id=1, source_target_pairs={{0,8},{2,10},{8,16},{10,18},{16,24},{18,26},{24,28},{26,30},{28,20... | collective-permute-start | bytes 786440 | tf_op jit(solution)/shard_map/ppermute | solution.py:284
  47.0 15.1 %collective-permute-start.20 = (bf16[512,256]{1,0:T(8,128)(2,1)}, bf16[512,256]{1,0:T(8,128)(2,1)}, u32[]{:S(2)}, u32[]{:S(2)}) collective-permute-start(bf16[512,256]{1,0:T(8,128)(2,1)} %refs_2_.1), channel_id=1, source_target_pairs={{8,0},{10,2},{16,8},{18,10},{24,16},{26,18},{28,24},{30,26},{20,28... | collective-permute-start | bytes 786440 | tf_op jit(solution)/shard_map/ppermute | solution.py:285
  50.3 11.9 %collective-permute-start.18 = (f32[128,256]{1,0:T(8,128)S(1)}, f32[128,256]{1,0:T(8,128)S(1)}, u32[]{:S(2)}, u32[]{:S(2)}) collective-permute-start(f32[128,256]{1,0:T(8,128)S(1)} %get-tuple-element.141), channel_id=1, source_target_pairs={{0,2},{2,0},{4,6},{6,4},{8,10},{10,8},{12,14},{14,12},{16,18},{18,... | collective-permute-start | bytes 393224 | tf_op jit(solution)/shard_map/ppermute | solution.py:376
  63.0 18.4 %all-to-all-start = ((bf16[8,128,256]{2,1,0:T(8,128)(2,1)}), bf16[8,128,256]{2,1,0:T(8,128)(2,1)S(1)}, u32[]{:S(2)}, u32[]{:S(2)}) async-start(bf16[8,128,256]{2,1,0:T(8,128)(2,1)} %bitcast.10), calls=%async_computation | async-start | bytes 1048576 | tf_op jit(solution)/shard_map/all_to_all | solution.py:393
  77.5 11.0 %collective-permute-start.16 = (f32[256,384]{1,0:T(8,128)S(1)}, f32[256,384]{1,0:T(8,128)S(1)}, u32[]{:S(2)}, u32[]{:S(2)}) collective-permute-start(f32[256,384]{1,0:T(8,128)S(1)} %project_queries.1.first_ref), channel_id=1, source_target_pairs={{0,2},{2,0},{4,6},{6,4},{8,10},{10,8},{12,14},{14,12},{16,18},{18,... | collective-permute-start | bytes 1179656 | tf_op jit(solution)/shard_map/ppermute | solution.py:380
  79.0 8.6 %collective-permute-start.21 = (bf16[512,256]{1,0:T(8,128)(2,1)}, bf16[512,256]{1,0:T(8,128)(2,1)S(1)}, u32[]{:S(2)}, u32[]{:S(2)}) collective-permute-start(bf16[512,256]{1,0:T(8,128)(2,1)} %collective-permute-done.19.refs_1_), channel_id=1, source_target_pairs={{0,8},{2,10},{8,16},{10,18},{16,24},{18,26},{24,28},{26,30},{28,20... | collective-permute-start | bytes 786440 | tf_op jit(solution)/shard_map/ppermute | solution.py:284
  80.7 7.8 %collective-permute-start.22 = (bf16[512,256]{1,0:T(8,128)(2,1)}, bf16[512,256]{1,0:T(8,128)(2,1)S(1)}, u32[]{:S(2)}, u32[]{:S(2)}) collective-permute-start(bf16[512,256]{1,0:T(8,128)(2,1)} %collective-permute-done.20.refs_3_), channel_id=1, source_target_pairs={{8,0},{10,2},{16,8},{18,10},{24,16},{26,18},{28,24},{30,26},{20,28... | collective-permute-start | bytes 786440 | tf_op jit(solution)/shard_map/ppermute | solution.py:285
  80.9 7.5 %collective-permute-start.17 = (f32[256,128]{1,0:T(8,128)}, f32[256,128]{1,0:T(8,128)S(1)}, u32[]{:S(2)}, u32[]{:S(2)}) collective-permute-start(f32[256,128]{1,0:T(8,128)} %copy-done.16), channel_id=1, source_target_pairs={{0,2},{2,0},{4,6},{6,4},{8,10},{10,8},{12,14},{14,12},{16,18},{18,... | collective-permute-start | bytes 393224 | tf_op jit(solution)/shard_map/ppermute | solution.py:381
  94.1 7.9 %collective-permute-start.24 = (bf16[512,256]{1,0:T(8,128)(2,1)S(1)}, bf16[512,256]{1,0:T(8,128)(2,1)S(1)}, u32[]{:S(2)}, u32[]{:S(2)}) collective-permute-start(bf16[512,256]{1,0:T(8,128)(2,1)S(1)} %collective-permute-done.22.refs_4_), channel_id=1, source_target_pairs={{8,0},{10,2},{16,8},{18,10},{24,16},{26,18},{28,24},{30,26},{20,28... | collective-permute-start | bytes 786440 | tf_op jit(solution)/shard_map/ppermute | solution.py:285
  94.3 7.7 %collective-permute-start.25 = (bf16[512,256]{1,0:T(8,128)(2,1)S(1)}, bf16[512,256]{1,0:T(8,128)(2,1)S(1)}, u32[]{:S(2)}, u32[]{:S(2)}) collective-permute-start(bf16[512,256]{1,0:T(8,128)(2,1)S(1)} %collective-permute-done.21.refs_0_), channel_id=1, source_target_pairs={{0,8},{2,10},{8,16},{10,18},{16,24},{18,26},{24,28},{26,30},{28,20... | collective-permute-start | bytes 786440 | tf_op jit(solution)/shard_map/ppermute | solution.py:284
  98.0 14.2 %collective-permute-start.28 = (bf16[5,64,256]{2,1,0:T(8,128)(2,1)S(1)}, bf16[5,64,256]{2,1,0:T(8,128)(2,1)S(1)}, u32[]{:S(2)}, u32[]{:S(2)}) collective-permute-start(bf16[5,64,256]{2,1,0:T(8,128)(2,1)S(1)} %get-tuple-element.174), channel_id=1, source_target_pairs={{0,1},{1,0},{2,3},{3,2},{4,5},{5,4},{6,7},{7,6},{8,9},{9,8},{10,11... | collective-permute-start | bytes 491528 | tf_op jit(solution)/shard_map/ppermute | solution.py:441
  103.5 8.8 %collective-permute-start.29 = (bf16[5,64,256]{2,1,0:T(8,128)(2,1)S(1)}, bf16[5,64,256]{2,1,0:T(8,128)(2,1)S(1)}, u32[]{:S(2)}, u32[]{:S(2)}) collective-permute-start(bf16[5,64,256]{2,1,0:T(8,128)(2,1)S(1)} %get-tuple-element.175), channel_id=1, source_target_pairs={{0,2},{1,3},{2,0},{3,1},{4,6},{5,7},{6,4},{7,5},{8,10},{9,11},{10,... | collective-permute-start | bytes 491528 | tf_op jit(solution)/shard_map/ppermute | solution.py:441
  (41 other events, 297.7 us)
Sparse Core Ops, SparseCore 0:
  9.5 25.0 all-gather.2

commit v12 on v11

--- a/solution.py
+++ b/solution.py
@@ -59,7 +59,8 @@
     return at, context % 2
 
 
-def norm_kernel(hidden_ref, gain_ref, out_ref):
+def norm_kernel(place, chips, hidden_ref, gain_ref, out_ref):
+    at, core = place_of(place)
     wide = hidden_ref[...].astype(jnp.float32)
     meansq = jnp.mean(wide * wide, axis=-1, keepdims=True)
     scaled = wide * lax.rsqrt(meansq + 1e-05)
@@ -74,9 +75,16 @@
         ],
         axis=1,
     )
-    block = out_ref.shape[2]
-    for owner in range(out_ref.shape[0]):
-        out_ref[owner] = normed[:, owner * block : (owner + 1) * block]
+    block = out_ref.shape[3]
+    for even in range(2):
+
+        @pl.when(core == even)
+        def _():
+            for chip in range(chips):
+                slot = lax.rem(place[chip] + chips - at, chips)
+                for side in range(2):
+                    column = (2 * chip + side) * block
+                    out_ref[side ^ even, slot] = normed[:, column : column + block]
 
 
 def take_ring(refs, chips):
@@ -89,20 +97,16 @@
     ]
 
 
-def project_kernel(place, chips, n_tensor, outs, ring_ref, rows_ref, *refs):
-    weight_refs, out_refs = refs[: -len(outs)], refs[-len(outs) :]
-    at, core = place_of(place)
-    tensor = lax.axis_index("tensor")
-    members = [
-        (core ^ e) * n_tensor + lax.rem(tensor + d, n_tensor)
-        for e in range(2)
-        for d in range(n_tensor)
-    ]
+def project_kernel(chips, groups, *refs):
+    rows_refs, refs = refs[:groups], refs[groups:]
+    weight_refs, (mine_ref, theirs_ref, queries_ref) = refs[:-3], refs[-3:]
+    half = groups // 2
     weights = take_ring(weight_refs, chips)
     total = None
     for slot in range(chips):
-        owner = 2 * ring_ref[lax.rem(at + slot, chips)] + core
-        rows = jnp.concatenate([rows_ref[member, owner] for member in members], axis=0)
+        rows = jnp.concatenate(
+            [ref[group // half, slot] for group, ref in enumerate(rows_refs)], axis=0
+        )
         start = 0
         for ref in weights[slot]:
             depth = ref.shape[0]
@@ -111,8 +115,10 @@
             )
             total = part if total is None else total + part
             start += depth
-    for ref, (rows, columns) in zip(out_refs, outs):
-        ref[...] = total[rows, columns]
+    count = mine_ref.shape[0]
+    mine_ref[...] = total[:count, HEAD_COLS:]
+    theirs_ref[...] = total[count:, HEAD_COLS:]
+    queries_ref[...] = total[:, :HEAD_COLS]
 
 
 def turn(values, cosine, sine):
@@ -131,10 +137,8 @@
 
 
 def attend_kernel(
-    first_ref,
-    first_theirs_ref,
-    last_ref,
-    last_theirs_ref,
+    mine_ref,
+    theirs_ref,
     cosine_ref,
     sine_ref,
     low_ref,
@@ -153,12 +157,7 @@
     lane = lax.broadcasted_iota(jnp.int32, (rows, HD), 1)
     stats = jnp.zeros((rows, HD), jnp.float32)
     for head in range(QH_DEV):
-        if head < QH_DEV - 1:
-            mine_ref, theirs_ref = first_ref, first_theirs_ref
-            columns = slice(head * HD, (head + 1) * HD)
-        else:
-            mine_ref, theirs_ref = last_ref, last_theirs_ref
-            columns = slice(0, HD)
+        columns = slice(head * HD, (head + 1) * HD)
         query = jnp.concatenate(
             [
                 mine_ref[:half, columns] + theirs_ref[half:, columns],
@@ -174,7 +173,7 @@
         top = jnp.max(scores, axis=-1, keepdims=True)
         expo = jnp.where(allowed, jnp.exp(scores - top), 0.0)
         total = jnp.sum(expo, axis=-1, keepdims=True)
-        out_ref[:, head * HD : (head + 1) * HD] = jnp.dot(
+        out_ref[:, columns] = jnp.dot(
             expo.astype(jnp.bfloat16), values, preferred_element_type=jnp.float32
         )
         stats = jnp.where(lane == 2 * head, total, stats)
@@ -312,42 +311,29 @@
             for t in range(n_tensor)
         ]
 
-    split = (QH_DEV - 1) * HD
-
+    qkv_ring = Ring(w_qkv)
+    qkv_ring.step()
     normed = pl.pallas_call(
-        norm_kernel,
-        out_shape=jax.ShapeDtypeStruct((n_context, rows_here, block), jnp.bfloat16),
+        functools.partial(norm_kernel, place, chips),
+        out_shape=jax.ShapeDtypeStruct((2, chips, rows_here, block), jnp.bfloat16),
         in_specs=vmem_specs(2),
         out_specs=vmem_specs(1)[0],
         compiler_params=compute_params(),
         name="norm",
     )(hidden_rows, norm_gain.reshape(-1, HD))
-    sharers = [
-        [(2 * chip + k) * n_tensor + t for k in range(2) for t in range(n_tensor)]
-        for chip in range(chips)
+    normed = [normed] + [
+        lax.ppermute(
+            normed, "tensor", [(t, (t - d) % n_tensor) for t in range(n_tensor)]
+        )
+        for d in range(1, n_tensor)
     ]
-    normed = lax.all_gather(normed, ("context", "tensor"), axis_index_groups=sharers)
-    last_ring = Ring(w_qkv[:, split:])
-    first_ring = Ring(w_qkv[:, :split])
-    last_ring.step()
-    first_ring.step()
-    while not last_ring.done():
-        last_ring.step()
-        first_ring.step()
-
-    def project(blocks, outs, name):
-        shapes = [
-            jax.ShapeDtypeStruct((rows.stop - rows.start, columns.stop - columns.start), jnp.float32)
-            for rows, columns in outs
-        ]
-        return pl.pallas_call(
-            functools.partial(project_kernel, place, chips, n_tensor, outs),
-            out_shape=shapes,
-            in_specs=[pl.BlockSpec(memory_space=pltpu.SMEM)] + vmem_specs(1 + len(blocks)),
-            out_specs=vmem_specs(len(outs)),
-            compiler_params=compute_params(),
-            name=name,
-        )(jnp.asarray(ring, jnp.int32), *ordered((normed, *blocks)))
+    normed += [lax.ppermute(rows, "context", sibling) for rows in normed]
+
+    qkv_ring.step()
+    qkv_ring.step()
+    normed = qkv_ring.step(normed)
+    while not qkv_ring.done():
+        qkv_ring.step()
 
     doc_ends = jnp.cumsum(doc_lengths)
     inside = (
@@ -366,19 +352,23 @@
     key_rows = (owner[:, None] * tokens_here + inside[None, :]).reshape(-1).astype(jnp.int32)
     key_orig, _ = locate(key_rows, span_order, doc_ends)
 
-    ours, siblings = slice(0, tokens_here), slice(tokens_here, 2 * tokens_here)
-    both_rows, kv_columns = slice(0, 2 * tokens_here), slice(HD, 3 * HD)
-    mine, theirs, last = project(
-        last_ring.finish(),
-        [(ours, kv_columns), (siblings, kv_columns), (both_rows, slice(0, HD))],
-        "project_keys",
-    )
-    theirs = lax.ppermute(theirs, "context", sibling)
     out_ring = Ring(w_out)
     out_ring.step()
-    (first,) = project(first_ring.finish(), [(both_rows, slice(0, split))], "project_queries")
-    first_theirs = lax.ppermute(first, "context", sibling)
-    last_theirs = lax.ppermute(last, "context", sibling)
+    blocks = qkv_ring.finish()
+    mine, theirs, queries = pl.pallas_call(
+        functools.partial(project_kernel, chips, groups),
+        out_shape=[
+            jax.ShapeDtypeStruct((tokens_here, 2 * HD), jnp.float32),
+            jax.ShapeDtypeStruct((tokens_here, 2 * HD), jnp.float32),
+            jax.ShapeDtypeStruct((2 * tokens_here, HEAD_COLS), jnp.float32),
+        ],
+        in_specs=vmem_specs(groups + len(blocks)),
+        out_specs=vmem_specs(3),
+        compiler_params=compute_params(),
+        name="project",
+    )(*ordered((*normed, *blocks)))
+    theirs = lax.ppermute(theirs, "context", sibling)
+    queries_theirs = lax.ppermute(queries, "context", sibling)
     out_ring.step()
     mine, theirs = ordered((mine, theirs))
     kv = pl.pallas_call(
@@ -398,15 +388,13 @@
     mixed = pl.pallas_call(
         attend_kernel,
         out_shape=jax.ShapeDtypeStruct((2 * tokens_here, HEAD_COLS + HD), jnp.float32),
-        in_specs=vmem_specs(10),
+        in_specs=vmem_specs(8),
         out_specs=vmem_specs(1)[0],
         compiler_params=compute_params(),
         name="attend",
     )(
-        first,
-        first_theirs,
-        last,
-        last_theirs,
+        queries,
+        queries_theirs,
         cosine,
         sine,
         query_start[:, None],

time: 125 us -> 103 us (0.82)
  between operations: 13.8 us -> 0.24 us
  waiting for transfers between devices: 40.2 us -> 51.1 us
  local copies, waits for them, and re-layouts: 14.4 us -> 4.72 us
  starting transfers between devices: 42 us -> 35.3 us
  other arithmetic: 2.89 us -> 1.47 us
    all_to_all x1, waiting for transfers between devices: 0.01 us -> 10.9 us  [per_device(): lax.all_to_all(kv, 'context', split_axis=0, concat_axis=0, axis_index_gro...]
    unnamed x58 -> x20, local copies, waits for them, and re-layouts: 12.6 us -> 3.92 us
    ppermute x9 -> x6, waiting for transfers between devices: 3.58 us -> 10.2 us  [step(): self.down.append(lax.ppermute(down, 'context', back))]
    ppermute x9 -> x6, starting transfers between devices: 7.7 us -> 1.99 us  [step(): self.down.append(lax.ppermute(down, 'context', back))]
    ppermute x9 -> x6, waiting for transfers between devices: 25.1 us -> 21.3 us  [step(): self.up.append(lax.ppermute(up, 'context', ahead))]
    ppermute x3 -> x2, waiting for transfers between devices: 5.74 us -> 2.15 us  [step(): lax.ppermute(up[:half], 'context', ahead)]
    ppermute x2 -> x4, starting transfers between devices: 1.98 us -> 5.22 us  [the longest x2 2.68 us: per_device(): normed += [lax.ppermute(rows, 'context', sibling) for rows in normed]]
    ppermute x9 -> x6, starting transfers between devices: 6.66 us -> 9.69 us  [step(): self.up.append(lax.ppermute(up, 'context', ahead))]
  transfers between devices with their start and end apart: 36 -> 29, of which waited for: 12 -> 19; matrix products, arithmetic and copies ran while one was open for 4% -> 2% of each run, Pallas kernels for 5% -> 5%
where the time goes in v12:
time: 103 us
  waiting for transfers between devices  51.1 us (50%)
  starting transfers between devices  35.3 us (34%)
  Pallas kernels  10.2 us (10%)
  local copies, waits for them, and re-layouts  4.72 us (5%)
  other arithmetic  1.47 us (1%)
    ppermute x6, waiting for transfers between devices, step(): self.up.append(lax.ppermute(up, 'context', ahead))  21.3 us
    all_to_all x1, waiting for transfers between devices, per_device(): lax.all_to_all(kv, 'context', split_axis=0, concat_axis=0, axis_index_gro...  10.9 us
    ppermute x6, waiting for transfers between devices, step(): self.down.append(lax.ppermute(down, 'context', back))  10.2 us
    ppermute x6, starting transfers between devices, step(): self.up.append(lax.ppermute(up, 'context', ahead))  9.69 us
    ppermute x1, starting transfers between devices, per_device(): theirs = lax.ppermute(theirs, 'context', sibling)  5.83 us
    ppermute x6, starting transfers between devices, output(): part = lax.ppermute(part, ('context', 'tensor'), member(e, -d))  5.17 us
    ppermute x6, waiting for transfers between devices, output(): part = lax.ppermute(part, ('context', 'tensor'), member(e, -d))  4.22 us
    unnamed x20, local copies, waits for them, and re-layouts  3.92 us
  transfers between devices with their start and end apart: 29, of which 19 were waited for; matrix products, arithmetic and copies ran while one was open for 2% of the time, Pallas kernels for 5%

profile of v12, /device:TPU:1, one launch (start us, length us, event | category | flops | bytes accessed | tf_op | source)
XLA Modules:
  0.0 103.0 jit_solution(10956484438628855892)
XLA Ops:
  2.0 2.1 %collective-permute-start.6 = (bf16[2,8,64,256]{3,2,1,0:T(8,128)(2,1)S(1)}, bf16[2,8,64,256]{3,2,1,0:T(8,128)(2,1)S(1)}, u32[]{:S(2)}, u32[]{:S(2)}) collective-permute-start(bf16[2,8,64,256]{3,2,1,0:T(8,128)(2,1)S(1)} %norm.1.refs_0_), channel_id=1, source_target_pairs={{0,1},{1,0},{2,3},{3,2},{4,5},{5,4},{6,7},{7,6},{8,9},{9,8},{10,11... | collective-permute-start | bytes 1572872 | tf_op jit(solution)/shard_map/ppermute | solution.py:325
  5.1 1.3 %collective-permute-start = (bf16[256,768]{1,0:T(8,128)(2,1)S(1)}, bf16[256,768]{1,0:T(8,128)(2,1)S(1)}, u32[]{:S(2)}, u32[]{:S(2)}) collective-permute-start(bf16[256,768]{1,0:T(8,128)(2,1)S(1)} %copy-done.1), channel_id=1, source_target_pairs={{0,8},{2,10},{8,16},{10,18},{16,24},{18,26},{24,28},{26,30},{28,20... | collective-permute-start | bytes 1179656 | tf_op jit(solution)/shard_map/ppermute | solution.py:283
  6.8 9.1 %collective-permute-done.refs_12_ = bf16[256,768]{1,0:T(8,128)(2,1)S(1)} collective-permute-done((bf16[256,768]{1,0:T(8,128)(2,1)S(1)}, bf16[256,768]{1,0:T(8,128)(2,1)S(1)}, u32[]{:S(2)}, u32[]{:S(2)}) %collective-permute-start) | collective-permute-done | bytes 393248 | tf_op jit(solution)/shard_map/ppermute | solution.py:283
  16.8 1.3 %collective-permute-start.2 = (bf16[256,768]{1,0:T(8,128)(2,1)S(1)}, bf16[256,768]{1,0:T(8,128)(2,1)}, u32[]{:S(2)}, u32[]{:S(2)}) collective-permute-start(bf16[256,768]{1,0:T(8,128)(2,1)S(1)} %collective-permute-done.refs_12_), channel_id=1, source_target_pairs={{0,8},{2,10},{8,16},{10,18},{16,24},{18,26},{24,28},{26,30},{28,20... | collective-permute-start | bytes 1179656 | tf_op jit(solution)/shard_map/ppermute | solution.py:283
  19.9 1.7 %collective-permute-start.8 = (bf16[2,8,64,256]{3,2,1,0:T(8,128)(2,1)S(1)}, bf16[2,8,64,256]{3,2,1,0:T(8,128)(2,1)S(1)}, u32[]{:S(2)}, u32[]{:S(2)}) collective-permute-start(bf16[2,8,64,256]{3,2,1,0:T(8,128)(2,1)S(1)} %collective-permute-done.6.refs_1_), channel_id=1, source_target_pairs={{0,2},{2,0},{4,6},{6,4},{8,10},{10,8},{12,14},{14,12},{16,18},{18,... | collective-permute-start | bytes 1572872 | tf_op jit(solution)/shard_map/ppermute | solution.py:330
  21.7 4.8 %collective-permute-done.2.refs_11_ = bf16[256,768]{1,0:T(8,128)(2,1)} collective-permute-done((bf16[256,768]{1,0:T(8,128)(2,1)S(1)}, bf16[256,768]{1,0:T(8,128)(2,1)}, u32[]{:S(2)}, u32[]{:S(2)}) %collective-permute-start.2) | collective-permute-done | bytes 393248 | tf_op jit(solution)/shard_map/ppermute | solution.py:283
  26.4 1.8 %collective-permute-done.3.refs_6_ = bf16[256,768]{1,0:T(8,128)(2,1)} collective-permute-done((bf16[256,768]{1,0:T(8,128)(2,1)S(1)}, bf16[256,768]{1,0:T(8,128)(2,1)}, u32[]{:S(2)}, u32[]{:S(2)}) %collective-permute-start.3) | collective-permute-done | bytes 393248 | tf_op jit(solution)/shard_map/ppermute | solution.py:284
  28.2 1.3 %collective-permute-start.4 = (bf16[256,768]{1,0:T(8,128)(2,1)}, bf16[256,768]{1,0:T(8,128)(2,1)S(1)}, u32[]{:S(2)}, u32[]{:S(2)}) collective-permute-start(bf16[256,768]{1,0:T(8,128)(2,1)} %collective-permute-done.2.refs_11_), channel_id=1, source_target_pairs={{0,8},{2,10},{8,16},{10,18},{16,24},{18,26},{24,28},{26,30},{28,20... | collective-permute-start | bytes 1179656 | tf_op jit(solution)/shard_map/ppermute | solution.py:283
  30.7 6.0 %collective-permute-done.4.refs_10_ = bf16[256,768]{1,0:T(8,128)(2,1)S(1)} collective-permute-done((bf16[256,768]{1,0:T(8,128)(2,1)}, bf16[256,768]{1,0:T(8,128)(2,1)S(1)}, u32[]{:S(2)}, u32[]{:S(2)}) %collective-permute-start.4) | collective-permute-done | bytes 393248 | tf_op jit(solution)/shard_map/ppermute | solution.py:283
  42.4 1.3 %collective-permute-done.10.refs_9_ = bf16[128,768]{1,0:T(8,128)(2,1)S(1)} collective-permute-done((bf16[128,768]{1,0:T(8,128)(2,1)S(1)}, bf16[128,768]{1,0:T(8,128)(2,1)S(1)}, u32[]{:S(2)}, u32[]{:S(2)}) %collective-permute-start.10) | collective-permute-done | bytes 196640 | tf_op jit(solution)/shard_map/ppermute | solution.py:289
  43.7 2.2 %project.1 = (f32[128,256]{1,0:T(8,128)S(1)}, f32[128,256]{1,0:T(8,128)S(1)}, f32[256,512]{1,0:T(8,128)S(1)}) custom-call(bf16[2,8,64,256]{3,2,1,0:T(8,128)(2,1)S(1)} %norm.1.refs_0_, bf16[2,8,64,256]{3,2,1,0:T(8,128)(2,1)S(1)} %collective-permute-done.6.refs_1_, bf16[2,8,64,256]{3,2,1,0:T(8,128)(2,1)S(1)} %collective-permute-done.7.refs_2_, ...), custom_call_target="tpu_custom_call" | custom-call | tf_op jit(solution)/shard_map/project/pallas_call | solution.py:358
  45.9 5.8 %collective-permute-start.12 = (f32[128,256]{1,0:T(8,128)S(1)}, f32[128,256]{1,0:T(8,128)S(1)}, u32[]{:S(2)}, u32[]{:S(2)}) collective-permute-start(f32[128,256]{1,0:T(8,128)S(1)} %get-tuple-element.109), channel_id=1, source_target_pairs={{0,2},{2,0},{4,6},{6,4},{8,10},{10,8},{12,14},{14,12},{16,18},{18,... | collective-permute-start | bytes 393224 | tf_op jit(solution)/shard_map/ppermute | solution.py:370
  53.6 3.5 %all-to-all-start = ((bf16[8,128,256]{2,1,0:T(8,128)(2,1)}), bf16[8,128,256]{2,1,0:T(8,128)(2,1)S(1)}, u32[]{:S(2)}, u32[]{:S(2)}) async-start(bf16[8,128,256]{2,1,0:T(8,128)(2,1)} %bitcast.9), calls=%async_computation | async-start | bytes 1048576 | tf_op jit(solution)/shard_map/all_to_all | solution.py:383
  57.7 1.7 %collective-permute-start.15 = (bf16[512,256]{1,0:T(8,128)(2,1)}, bf16[512,256]{1,0:T(8,128)(2,1)S(1)}, u32[]{:S(2)}, u32[]{:S(2)}) collective-permute-start(bf16[512,256]{1,0:T(8,128)(2,1)} %collective-permute-done.13.refs_1_), channel_id=1, source_target_pairs={{0,8},{2,10},{8,16},{10,18},{16,24},{18,26},{24,28},{26,30},{28,20... | collective-permute-start | bytes 786440 | tf_op jit(solution)/shard_map/ppermute | solution.py:283
  60.2 10.9 %all-to-all-done = bf16[8,128,256]{2,1,0:T(8,128)(2,1)S(1)} async-done(((bf16[8,128,256]{2,1,0:T(8,128)(2,1)}), bf16[8,128,256]{2,1,0:T(8,128)(2,1)S(1)}, u32[]{:S(2)}, u32[]{:S(2)}) %all-to-all-start) | async-done | bytes 524320 | tf_op jit(solution)/shard_map/all_to_all | solution.py:383
  71.5 2.2 %collective-permute-done.16.refs_4_ = bf16[512,256]{1,0:T(8,128)(2,1)S(1)} collective-permute-done((bf16[512,256]{1,0:T(8,128)(2,1)}, bf16[512,256]{1,0:T(8,128)(2,1)S(1)}, u32[]{:S(2)}, u32[]{:S(2)}) %collective-permute-start.16) | collective-permute-done | bytes 262176 | tf_op jit(solution)/shard_map/ppermute | solution.py:284
  73.7 2.5 %attend.1.mine_ref = f32[256,640]{1,0:T(8,128)S(1)} custom-call(f32[256,512]{1,0:T(8,128)S(1)} %get-tuple-element.107.mine_ref, f32[256,512]{1,0:T(8,128)S(1)} %collective-permute-done.11.theirs_ref, f32[256,128]{1,0:T(8,128)S(1)} %get-tuple-element.158.cosine_ref, f32[256,128]{1,0:T(8,128)S(1)} %get-tuple-element.159.sine_ref, s32[256,1]{1,0:T(8,128)S(1)} %copy.30.low_ref, ...), custom_call_target="tpu_custom_call" | custom-call | tf_op jit(solution)/shard_map/attend/pallas_call | solution.py:388
  78.2 2.8 %collective-permute-start.19 = (bf16[512,256]{1,0:T(8,128)(2,1)S(1)}, bf16[512,256]{1,0:T(8,128)(2,1)S(1)}, u32[]{:S(2)}, u32[]{:S(2)}) collective-permute-start(bf16[512,256]{1,0:T(8,128)(2,1)S(1)} %collective-permute-done.15.refs_0_), channel_id=1, source_target_pairs={{0,8},{2,10},{8,16},{10,18},{16,24},{18,26},{24,28},{26,30},{28,20... | collective-permute-start | bytes 786440 | tf_op jit(solution)/shard_map/ppermute | solution.py:283
  81.0 2.2 %output_near.1 = (bf16[5,64,256]{2,1,0:T(8,128)(2,1)S(1)}, bf16[5,64,256]{2,1,0:T(8,128)(2,1)S(1)}, bf16[5,64,256]{2,1,0:T(8,128)(2,1)S(1)}, bf16[5,64,256]{2,1,0:T(8,128)(2,1)S(1)}) custom-call(f32[256,640]{1,0:T(8,128)S(1)} %attend.1.mine_ref, f32[256,640]{1,0:T(8,128)S(1)} %collective-permute-done.17.theirs_ref, ...), custom_call_target="tpu_custom_call" | custom-call | tf_op jit(solution)/shard_map/output_near/pallas_call | solution.py:414
  83.3 4.3 %collective-permute-done.18.refs_0_ = bf16[512,256]{1,0:T(8,128)(2,1)S(1)} collective-permute-done((bf16[512,256]{1,0:T(8,128)(2,1)S(1)}, bf16[512,256]{1,0:T(8,128)(2,1)S(1)}, u32[]{:S(2)}, u32[]{:S(2)}) %collective-permute-start.18) | collective-permute-done | bytes 262176 | tf_op jit(solution)/shard_map/ppermute | solution.py:284
  90.2 1.4 %collective-permute-start.23 = (bf16[5,64,256]{2,1,0:T(8,128)(2,1)S(1)}, bf16[5,64,256]{2,1,0:T(8,128)(2,1)S(1)}, u32[]{:S(2)}, u32[]{:S(2)}) collective-permute-start(bf16[5,64,256]{2,1,0:T(8,128)(2,1)S(1)} %get-tuple-element.143), channel_id=1, source_target_pairs={{0,2},{1,3},{2,0},{3,1},{4,6},{5,7},{6,4},{7,5},{8,10},{9,11},{10,... | collective-permute-start | bytes 491528 | tf_op jit(solution)/shard_map/ppermute | solution.py:429
  94.2 2.3 %collective-permute-start.26 = (bf16[3,64,256]{2,1,0:T(8,128)(2,1)S(1)}, bf16[3,64,256]{2,1,0:T(8,128)(2,1)S(1)}, u32[]{:S(2)}, u32[]{:S(2)}) collective-permute-start(bf16[3,64,256]{2,1,0:T(8,128)(2,1)S(1)} %get-tuple-element.147), channel_id=1, source_target_pairs={{0,2},{1,3},{2,0},{3,1},{4,6},{5,7},{6,4},{7,5},{8,10},{9,11},{10,... | collective-permute-start | bytes 294920 | tf_op jit(solution)/shard_map/ppermute | solution.py:429
  96.4 1.3 %collective-permute-start.27 = (bf16[3,64,256]{2,1,0:T(8,128)(2,1)S(1)}, bf16[3,64,256]{2,1,0:T(8,128)(2,1)S(1)}, u32[]{:S(2)}, u32[]{:S(2)}) collective-permute-start(bf16[3,64,256]{2,1,0:T(8,128)(2,1)S(1)} %get-tuple-element.148), channel_id=1, source_target_pairs={{0,3},{1,2},{2,1},{3,0},{4,7},{5,6},{6,5},{7,4},{8,11},{9,10},{10,... | collective-permute-start | bytes 294920 | tf_op jit(solution)/shard_map/ppermute | solution.py:429
  98.5 3.5 %collective-permute-done.27.refs_7_ = bf16[3,64,256]{2,1,0:T(8,128)(2,1)S(1)} collective-permute-done((bf16[3,64,256]{2,1,0:T(8,128)(2,1)S(1)}, bf16[3,64,256]{2,1,0:T(8,128)(2,1)S(1)}, u32[]{:S(2)}, u32[]{:S(2)}) %collective-permute-start.27) | collective-permute-done | bytes 98336 | tf_op jit(solution)/shard_map/ppermute | solution.py:429
  (92 shorter events, 25.4 us)
Async XLA Ops:
  2.0 17.9 %collective-permute-start.6 = (bf16[2,8,64,256]{3,2,1,0:T(8,128)(2,1)S(1)}, bf16[2,8,64,256]{3,2,1,0:T(8,128)(2,1)S(1)}, u32[]{:S(2)}, u32[]{:S(2)}) collective-permute-start(bf16[2,8,64,256]{3,2,1,0:T(8,128)(2,1)S(1)} %norm.1.refs_0_), channel_id=1, source_target_pairs={{0,1},{1,0},{2,3},{3,2},{4,5},{5,4},{6,7},{7,6},{8,9},{9,8},{10,11... | collective-permute-start | bytes 1572872 | tf_op jit(solution)/shard_map/ppermute | solution.py:325
  4.1 26.5 %collective-permute-start.7 = (bf16[2,8,64,256]{3,2,1,0:T(8,128)(2,1)S(1)}, bf16[2,8,64,256]{3,2,1,0:T(8,128)(2,1)S(1)}, u32[]{:S(2)}, u32[]{:S(2)}) collective-permute-start(bf16[2,8,64,256]{3,2,1,0:T(8,128)(2,1)S(1)} %norm.1.refs_0_), channel_id=1, source_target_pairs={{0,2},{2,0},{4,6},{6,4},{8,10},{10,8},{12,14},{14,12},{16,18},{18,... | collective-permute-start | bytes 1572872 | tf_op jit(solution)/shard_map/ppermute | solution.py:330
  5.1 10.7 %collective-permute-start = (bf16[256,768]{1,0:T(8,128)(2,1)S(1)}, bf16[256,768]{1,0:T(8,128)(2,1)S(1)}, u32[]{:S(2)}, u32[]{:S(2)}) collective-permute-start(bf16[256,768]{1,0:T(8,128)(2,1)S(1)} %copy-done.1), channel_id=1, source_target_pairs={{0,8},{2,10},{8,16},{10,18},{16,24},{18,26},{24,28},{26,30},{28,20... | collective-permute-start | bytes 1179656 | tf_op jit(solution)/shard_map/ppermute | solution.py:283
  6.4 10.4 %collective-permute-start.1 = (bf16[256,768]{1,0:T(8,128)(2,1)S(1)}, bf16[256,768]{1,0:T(8,128)(2,1)S(1)}, u32[]{:S(2)}, u32[]{:S(2)}) collective-permute-start(bf16[256,768]{1,0:T(8,128)(2,1)S(1)} %copy-done.1), channel_id=1, source_target_pairs={{8,0},{10,2},{16,8},{18,10},{24,16},{26,18},{28,24},{30,26},{20,28... | collective-permute-start | bytes 1179656 | tf_op jit(solution)/shard_map/ppermute | solution.py:284
  16.8 9.6 %collective-permute-start.2 = (bf16[256,768]{1,0:T(8,128)(2,1)S(1)}, bf16[256,768]{1,0:T(8,128)(2,1)}, u32[]{:S(2)}, u32[]{:S(2)}) collective-permute-start(bf16[256,768]{1,0:T(8,128)(2,1)S(1)} %collective-permute-done.refs_12_), channel_id=1, source_target_pairs={{0,8},{2,10},{8,16},{10,18},{16,24},{18,26},{24,28},{26,30},{28,20... | collective-permute-start | bytes 1179656 | tf_op jit(solution)/shard_map/ppermute | solution.py:283
  18.9 9.3 %collective-permute-start.3 = (bf16[256,768]{1,0:T(8,128)(2,1)S(1)}, bf16[256,768]{1,0:T(8,128)(2,1)}, u32[]{:S(2)}, u32[]{:S(2)}) collective-permute-start(bf16[256,768]{1,0:T(8,128)(2,1)S(1)} %collective-permute-done.1.refs_5_), channel_id=1, source_target_pairs={{8,0},{10,2},{16,8},{18,10},{24,16},{26,18},{28,24},{30,26},{20,28... | collective-permute-start | bytes 1179656 | tf_op jit(solution)/shard_map/ppermute | solution.py:284
  19.9 10.8 %collective-permute-start.8 = (bf16[2,8,64,256]{3,2,1,0:T(8,128)(2,1)S(1)}, bf16[2,8,64,256]{3,2,1,0:T(8,128)(2,1)S(1)}, u32[]{:S(2)}, u32[]{:S(2)}) collective-permute-start(bf16[2,8,64,256]{3,2,1,0:T(8,128)(2,1)S(1)} %collective-permute-done.6.refs_1_), channel_id=1, source_target_pairs={{0,2},{2,0},{4,6},{6,4},{8,10},{10,8},{12,14},{14,12},{16,18},{18,... | collective-permute-start | bytes 1572872 | tf_op jit(solution)/shard_map/ppermute | solution.py:330
  28.2 8.5 %collective-permute-start.4 = (bf16[256,768]{1,0:T(8,128)(2,1)}, bf16[256,768]{1,0:T(8,128)(2,1)S(1)}, u32[]{:S(2)}, u32[]{:S(2)}) collective-permute-start(bf16[256,768]{1,0:T(8,128)(2,1)} %collective-permute-done.2.refs_11_), channel_id=1, source_target_pairs={{0,8},{2,10},{8,16},{10,18},{16,24},{18,26},{24,28},{26,30},{28,20... | collective-permute-start | bytes 1179656 | tf_op jit(solution)/shard_map/ppermute | solution.py:283
  29.5 8.2 %collective-permute-start.5 = (bf16[256,768]{1,0:T(8,128)(2,1)}, bf16[256,768]{1,0:T(8,128)(2,1)S(1)}, u32[]{:S(2)}, u32[]{:S(2)}) collective-permute-start(bf16[256,768]{1,0:T(8,128)(2,1)} %collective-permute-done.3.refs_6_), channel_id=1, source_target_pairs={{8,0},{10,2},{16,8},{18,10},{24,16},{26,18},{28,24},{30,26},{20,28... | collective-permute-start | bytes 1179656 | tf_op jit(solution)/shard_map/ppermute | solution.py:284
  37.8 4.6 %collective-permute-start.9 = (bf16[128,768]{1,0:T(8,128)(2,1)S(1)}, bf16[128,768]{1,0:T(8,128)(2,1)S(1)}, u32[]{:S(2)}, u32[]{:S(2)}) collective-permute-start(bf16[128,768]{1,0:T(8,128)(2,1)S(1)} %slice.12), channel_id=1, source_target_pairs={{0,8},{2,10},{8,16},{10,18},{16,24},{18,26},{24,28},{26,30},{28,20... | collective-permute-start | bytes 589832 | tf_op jit(solution)/shard_map/ppermute | solution.py:288
  39.9 12.0 %collective-permute-start.13 = (bf16[512,256]{1,0:T(8,128)(2,1)}, bf16[512,256]{1,0:T(8,128)(2,1)}, u32[]{:S(2)}, u32[]{:S(2)}) collective-permute-start(bf16[512,256]{1,0:T(8,128)(2,1)} %refs_2_.1), channel_id=1, source_target_pairs={{0,8},{2,10},{8,16},{10,18},{16,24},{18,26},{24,28},{26,30},{28,20... | collective-permute-start | bytes 786440 | tf_op jit(solution)/shard_map/ppermute | solution.py:283
  41.2 10.8 %collective-permute-start.14 = (bf16[512,256]{1,0:T(8,128)(2,1)}, bf16[512,256]{1,0:T(8,128)(2,1)}, u32[]{:S(2)}, u32[]{:S(2)}) collective-permute-start(bf16[512,256]{1,0:T(8,128)(2,1)} %refs_2_.1), channel_id=1, source_target_pairs={{8,0},{10,2},{16,8},{18,10},{24,16},{26,18},{28,24},{30,26},{20,28... | collective-permute-start | bytes 786440 | tf_op jit(solution)/shard_map/ppermute | solution.py:284
  45.9 6.8 %collective-permute-start.12 = (f32[128,256]{1,0:T(8,128)S(1)}, f32[128,256]{1,0:T(8,128)S(1)}, u32[]{:S(2)}, u32[]{:S(2)}) collective-permute-start(f32[128,256]{1,0:T(8,128)S(1)} %get-tuple-element.109), channel_id=1, source_target_pairs={{0,2},{2,0},{4,6},{6,4},{8,10},{10,8},{12,14},{14,12},{16,18},{18,... | collective-permute-start | bytes 393224 | tf_op jit(solution)/shard_map/ppermute | solution.py:370
  53.6 17.5 %all-to-all-start = ((bf16[8,128,256]{2,1,0:T(8,128)(2,1)}), bf16[8,128,256]{2,1,0:T(8,128)(2,1)S(1)}, u32[]{:S(2)}, u32[]{:S(2)}) async-start(bf16[8,128,256]{2,1,0:T(8,128)(2,1)} %bitcast.9), calls=%async_computation | async-start | bytes 1048576 | tf_op jit(solution)/shard_map/all_to_all | solution.py:383
  57.3 16.4 %collective-permute-start.11 = (f32[256,512]{1,0:T(8,128)S(1)}, f32[256,512]{1,0:T(8,128)S(1)}, u32[]{:S(2)}, u32[]{:S(2)}) collective-permute-start(f32[256,512]{1,0:T(8,128)S(1)} %get-tuple-element.107.mine_ref), channel_id=1, source_target_pairs={{0,2},{2,0},{4,6},{6,4},{8,10},{10,8},{12,14},{14,12},{16,18},{18,... | collective-permute-start | bytes 1572872 | tf_op jit(solution)/shard_map/ppermute | solution.py:371
  57.7 13.8 %collective-permute-start.15 = (bf16[512,256]{1,0:T(8,128)(2,1)}, bf16[512,256]{1,0:T(8,128)(2,1)S(1)}, u32[]{:S(2)}, u32[]{:S(2)}) collective-permute-start(bf16[512,256]{1,0:T(8,128)(2,1)} %collective-permute-done.13.refs_1_), channel_id=1, source_target_pairs={{0,8},{2,10},{8,16},{10,18},{16,24},{18,26},{24,28},{26,30},{28,20... | collective-permute-start | bytes 786440 | tf_op jit(solution)/shard_map/ppermute | solution.py:283
  59.4 14.2 %collective-permute-start.16 = (bf16[512,256]{1,0:T(8,128)(2,1)}, bf16[512,256]{1,0:T(8,128)(2,1)S(1)}, u32[]{:S(2)}, u32[]{:S(2)}) collective-permute-start(bf16[512,256]{1,0:T(8,128)(2,1)} %collective-permute-done.14.refs_3_), channel_id=1, source_target_pairs={{8,0},{10,2},{16,8},{18,10},{24,16},{26,18},{28,24},{30,26},{20,28... | collective-permute-start | bytes 786440 | tf_op jit(solution)/shard_map/ppermute | solution.py:284
  76.2 4.8 %collective-permute-start.17 = (f32[256,640]{1,0:T(8,128)S(1)}, f32[256,640]{1,0:T(8,128)S(1)}, u32[]{:S(2)}, u32[]{:S(2)}) collective-permute-start(f32[256,640]{1,0:T(8,128)S(1)} %attend.1.mine_ref), channel_id=1, source_target_pairs={{0,2},{2,0},{4,6},{6,4},{8,10},{10,8},{12,14},{14,12},{16,18},{18,... | collective-permute-start | bytes 1966088 | tf_op jit(solution)/shard_map/ppermute | solution.py:407
  77.0 10.6 %collective-permute-start.18 = (bf16[512,256]{1,0:T(8,128)(2,1)S(1)}, bf16[512,256]{1,0:T(8,128)(2,1)S(1)}, u32[]{:S(2)}, u32[]{:S(2)}) collective-permute-start(bf16[512,256]{1,0:T(8,128)(2,1)S(1)} %collective-permute-done.16.refs_4_), channel_id=1, source_target_pairs={{8,0},{10,2},{16,8},{18,10},{24,16},{26,18},{28,24},{30,26},{20,28... | collective-permute-start | bytes 786440 | tf_op jit(solution)/shard_map/ppermute | solution.py:284
  78.2 10.4 %collective-permute-start.19 = (bf16[512,256]{1,0:T(8,128)(2,1)S(1)}, bf16[512,256]{1,0:T(8,128)(2,1)S(1)}, u32[]{:S(2)}, u32[]{:S(2)}) collective-permute-start(bf16[512,256]{1,0:T(8,128)(2,1)S(1)} %collective-permute-done.15.refs_0_), channel_id=1, source_target_pairs={{0,8},{2,10},{8,16},{10,18},{16,24},{18,26},{24,28},{26,30},{28,20... | collective-permute-start | bytes 786440 | tf_op jit(solution)/shard_map/ppermute | solution.py:283
  83.2 13.2 %collective-permute-start.22 = (bf16[5,64,256]{2,1,0:T(8,128)(2,1)S(1)}, bf16[5,64,256]{2,1,0:T(8,128)(2,1)S(1)}, u32[]{:S(2)}, u32[]{:S(2)}) collective-permute-start(bf16[5,64,256]{2,1,0:T(8,128)(2,1)S(1)} %get-tuple-element.142), channel_id=1, source_target_pairs={{0,1},{1,0},{2,3},{3,2},{4,5},{5,4},{6,7},{7,6},{8,9},{9,8},{10,11... | collective-permute-start | bytes 491528 | tf_op jit(solution)/shard_map/ppermute | solution.py:429
  90.2 7.6 %collective-permute-start.23 = (bf16[5,64,256]{2,1,0:T(8,128)(2,1)S(1)}, bf16[5,64,256]{2,1,0:T(8,128)(2,1)S(1)}, u32[]{:S(2)}, u32[]{:S(2)}) collective-permute-start(bf16[5,64,256]{2,1,0:T(8,128)(2,1)S(1)} %get-tuple-element.143), channel_id=1, source_target_pairs={{0,2},{1,3},{2,0},{3,1},{4,6},{5,7},{6,4},{7,5},{8,10},{9,11},{10,... | collective-permute-start | bytes 491528 | tf_op jit(solution)/shard_map/ppermute | solution.py:429
  91.6 6.5 %collective-permute-start.24 = (bf16[5,64,256]{2,1,0:T(8,128)(2,1)S(1)}, bf16[5,64,256]{2,1,0:T(8,128)(2,1)S(1)}, u32[]{:S(2)}, u32[]{:S(2)}) collective-permute-start(bf16[5,64,256]{2,1,0:T(8,128)(2,1)S(1)} %get-tuple-element.144), channel_id=1, source_target_pairs={{0,3},{1,2},{2,1},{3,0},{4,7},{5,6},{6,5},{7,4},{8,11},{9,10},{10,... | collective-permute-start | bytes 491528 | tf_op jit(solution)/shard_map/ppermute | solution.py:429
  96.4 5.6 %collective-permute-start.27 = (bf16[3,64,256]{2,1,0:T(8,128)(2,1)S(1)}, bf16[3,64,256]{2,1,0:T(8,128)(2,1)S(1)}, u32[]{:S(2)}, u32[]{:S(2)}) collective-permute-start(bf16[3,64,256]{2,1,0:T(8,128)(2,1)S(1)} %get-tuple-element.148), channel_id=1, source_target_pairs={{0,3},{1,2},{2,1},{3,0},{4,7},{5,6},{6,5},{7,4},{8,11},{9,10},{10,... | collective-permute-start | bytes 294920 | tf_op jit(solution)/shard_map/ppermute | solution.py:429
  (15 other events, 59.7 us)

commit v13 on v12

--- a/solution.py
+++ b/solution.py
@@ -181,8 +181,9 @@
     out_ref[:, HEAD_COLS:] = stats
 
 
-def output_kernel(groups, pieces_of, mine_ref, theirs_ref, *refs):
+def output_kernel(chips, groups, mine_ref, theirs_ref, *refs):
     weight_refs, out_refs = refs[:-groups], refs[-groups:]
+    weights = take_ring(weight_refs, chips)
     chip_rows = mine_ref.shape[0]
     half = chip_rows // 2
 
@@ -203,11 +204,9 @@
         )
     mixed = jnp.concatenate(pieces, axis=1)
     rows = chip_rows // groups
-    weight_refs = iter(weight_refs)
-    for slot, pieces in enumerate(pieces_of):
+    for slot in range(chips):
         start, total = 0, None
-        for _ in range(pieces):
-            ref = next(weight_refs)
+        for ref in weights[slot]:
             depth = ref.shape[0]
             part = jnp.dot(
                 mixed[:, start : start + depth], ref[...], preferred_element_type=jnp.float32
@@ -219,22 +218,16 @@
             out_refs[group][slot] = total[group * rows : (group + 1) * rows]
 
 
-def sum_kernel(place, chips, groups, near, token_ref, *refs):
-    near_refs, far_refs, out_ref = refs[:groups], refs[groups : 2 * groups], refs[2 * groups]
+def sum_kernel(place, chips, groups, token_ref, *refs):
+    part_refs, out_ref = refs[:groups], refs[groups]
     at, core = place_of(place)
-    block = near_refs[0].shape[2]
+    block = part_refs[0].shape[2]
     half = groups // 2
 
     def added(part, slot):
-        turn_at = lax.rem(slot + near // 2, chips)
-        total = None
-        for group in range(part * half, (part + 1) * half):
-            rows = jnp.where(
-                turn_at < near,
-                near_refs[group][jnp.minimum(turn_at, near - 1)].astype(jnp.float32),
-                far_refs[group][jnp.maximum(turn_at - near, 0)].astype(jnp.float32),
-            )
-            total = rows if total is None else total + rows
+        total = part_refs[part * half][slot].astype(jnp.float32)
+        for ref in part_refs[part * half + 1 : (part + 1) * half]:
+            total += ref[slot].astype(jnp.float32)
         return total.astype(jnp.bfloat16)
 
     for even in range(2):
@@ -298,12 +291,6 @@
                 self.step()
             return self.down + self.middle + self.up[:0:-1]
 
-        def block(self, slot):
-            slot %= chips
-            if chips % 2 == 0 and slot == chips // 2:
-                return tuple(self.middle)
-            return (self.down[slot] if slot <= chips // 2 else self.up[chips - slot],)
-
     def member(e, d):
         return [
             (c * n_tensor + t, (c ^ e) * n_tensor + (t - d) % n_tensor)
@@ -329,11 +316,13 @@
     ]
     normed += [lax.ppermute(rows, "context", sibling) for rows in normed]
 
-    qkv_ring.step()
-    qkv_ring.step()
-    normed = qkv_ring.step(normed)
-    while not qkv_ring.done():
+    while len(qkv_ring.up) <= (chips - 1) // 2:
         qkv_ring.step()
+    out_ring = Ring(w_out)
+    out_ring.step()
+    *normed, out_ring.up[-1], out_ring.down[-1] = qkv_ring.step(
+        (*normed, out_ring.up[-1], out_ring.down[-1])
+    )
 
     doc_ends = jnp.cumsum(doc_lengths)
     inside = (
@@ -352,7 +341,6 @@
     key_rows = (owner[:, None] * tokens_here + inside[None, :]).reshape(-1).astype(jnp.int32)
     key_orig, _ = locate(key_rows, span_order, doc_ends)
 
-    out_ring = Ring(w_out)
     out_ring.step()
     blocks = qkv_ring.finish()
     mine, theirs, queries = pl.pallas_call(
@@ -408,40 +396,28 @@
 
     out_block = w_out.shape[1]
 
-    def output(slots, name):
-        blocks = [out_ring.block(slot) for slot in slots]
-        flat = [piece for pieces in blocks for piece in pieces]
-        parts = pl.pallas_call(
-            functools.partial(output_kernel, groups, [len(pieces) for pieces in blocks]),
-            out_shape=[jax.ShapeDtypeStruct((len(slots), rows_here, out_block), jnp.bfloat16)]
-            * groups,
-            in_specs=vmem_specs(2 + len(flat)),
-            out_specs=vmem_specs(groups),
-            compiler_params=compute_params(),
-            name=name,
-        )(mixed, mixed_theirs, *flat)
-        parts = ordered(parts)
-        arrived = []
-        for e in range(2):
-            for d in range(n_tensor):
-                part = parts[e * n_tensor + d]
-                if e or d:
-                    part = lax.ppermute(part, ("context", "tensor"), member(e, -d))
-                arrived.append(part)
-        return arrived
-
-    reach = max(chips // 2 - 2, 0)
-    while len(out_ring.up) <= reach:
-        out_ring.step()
-    near = 2 * reach + 1
-    arrived = output(list(range(-reach, reach + 1)), "output_near")
     while not out_ring.done():
         out_ring.step()
-    arrived += output(list(range(reach + 1, chips - reach)), "output_far")
+    blocks = out_ring.finish()
+    parts = pl.pallas_call(
+        functools.partial(output_kernel, chips, groups),
+        out_shape=[jax.ShapeDtypeStruct((chips, rows_here, out_block), jnp.bfloat16)] * groups,
+        in_specs=vmem_specs(2 + len(blocks)),
+        out_specs=vmem_specs(groups),
+        compiler_params=compute_params(),
+        name="output",
+    )(mixed, mixed_theirs, *blocks)
+    arrived = []
+    for e in range(2):
+        for d in range(n_tensor):
+            part = parts[e * n_tensor + d]
+            if e or d:
+                part = lax.ppermute(part, ("context", "tensor"), member(e, -d))
+            arrived.append(part)
     return pl.pallas_call(
-        functools.partial(sum_kernel, place, chips, groups, near),
+        functools.partial(sum_kernel, place, chips, groups),
         out_shape=jax.ShapeDtypeStruct((rows_here, n_context * out_block), jnp.bfloat16),
-        in_specs=[pl.BlockSpec(memory_space=pl.ANY)] + vmem_specs(2 * groups),
+        in_specs=[pl.BlockSpec(memory_space=pl.ANY)] + vmem_specs(groups),
         out_specs=vmem_specs(1)[0],
         compiler_params=compute_params(),
         name="sum",

time: 103 us -> 107 us (1.039)
  waiting for transfers between devices: 51.1 us -> 55.5 us
  starting transfers between devices: 35.3 us -> 32.9 us
  local copies, waits for them, and re-layouts: 4.72 us -> 7.06 us
  Pallas kernels: 10.2 us -> 8.18 us
  other arithmetic: 1.47 us -> 2.95 us
    ppermute x6 -> x3, waiting for transfers between devices: 4.22 us -> 10.9 us  [per_device(): part = lax.ppermute(part, ('context', 'tensor'), member(e, -d))]
    ppermute x6, waiting for transfers between devices: 10.2 us -> 5.9 us  [step(): self.down.append(lax.ppermute(down, 'context', back))]
    all_to_all x1, waiting for transfers between devices: 10.9 us -> 6.8 us  [per_device(): lax.all_to_all(kv, 'context', split_axis=0, concat_axis=0, axis_index_gro...]
    ppermute x2, starting transfers between devices: 1.62 us -> 5.35 us  [step(): lax.ppermute(up[:half], 'context', ahead)]
    ppermute x6, waiting for transfers between devices: 21.3 us -> 24.8 us  [step(): self.up.append(lax.ppermute(up, 'context', ahead))]
    ppermute x6 -> x3, starting transfers between devices: 5.17 us -> 2.81 us  [per_device(): part = lax.ppermute(part, ('context', 'tensor'), member(e, -d))]
    pallas_call x3 -> x2, Pallas kernels: 4.25 us -> 2.29 us  [the longest x1 1.37 us: per_device(): pl.pallas_call(functools.partial(output_kernel, chips, groups), out_shape...]
    ppermute x2, waiting for transfers between devices: 1.59 us -> 3.26 us  [step(): lax.ppermute(down[half:], 'context', back)]
  transfers between devices with their start and end apart: 29 -> 26, of which waited for: 19 -> 15; matrix products, arithmetic and copies ran while one was open for 2% -> 5% of each run, Pallas kernels for 5% -> 2%
where the time goes in v13:
time: 107 us
  waiting for transfers between devices  55.5 us (52%)
  starting transfers between devices  32.9 us (31%)
  Pallas kernels  8.18 us (8%)
  local copies, waits for them, and re-layouts  7.06 us (7%)
  other arithmetic  2.95 us (3%)
    ppermute x6, waiting for transfers between devices, step(): self.up.append(lax.ppermute(up, 'context', ahead))  24.8 us
    ppermute x3, waiting for transfers between devices, per_device(): part = lax.ppermute(part, ('context', 'tensor'), member(e, -d))  10.9 us
    ppermute x6, starting transfers between devices, step(): self.up.append(lax.ppermute(up, 'context', ahead))  8.22 us
    all_to_all x1, waiting for transfers between devices, per_device(): lax.all_to_all(kv, 'context', split_axis=0, concat_axis=0, axis_index_gro...  6.8 us
    ppermute x6, waiting for transfers between devices, step(): self.down.append(lax.ppermute(down, 'context', back))  5.9 us
    ppermute x1, starting transfers between devices, per_device(): theirs = lax.ppermute(theirs, 'context', sibling)  5.67 us
    ppermute x2, starting transfers between devices, step(): lax.ppermute(up[:half], 'context', ahead)  5.35 us
    unnamed x44, local copies, waits for them, and re-layouts  4.93 us
  transfers between devices with their start and end apart: 26, of which 15 were waited for; matrix products, arithmetic and copies ran while one was open for 5% of the time, Pallas kernels for 2%

profile of v13, /device:TPU:1, one launch (start us, length us, event | category | flops | bytes accessed | tf_op | source)
XLA Modules:
  0.0 106.8 jit_solution(18093873832119079876)
XLA Ops:
  2.0 2.1 %collective-permute-start.6 = (bf16[2,8,64,256]{3,2,1,0:T(8,128)(2,1)S(1)}, bf16[2,8,64,256]{3,2,1,0:T(8,128)(2,1)S(1)}, u32[]{:S(2)}, u32[]{:S(2)}) collective-permute-start(bf16[2,8,64,256]{3,2,1,0:T(8,128)(2,1)S(1)} %norm.1.refs_0_), channel_id=1, source_target_pairs={{0,1},{1,0},{2,3},{3,2},{4,5},{5,4},{6,7},{7,6},{8,9},{9,8},{10,11... | collective-permute-start | bytes 1572872 | tf_op jit(solution)/shard_map/ppermute | solution.py:312
  5.1 1.3 %collective-permute-start = (bf16[256,768]{1,0:T(8,128)(2,1)S(1)}, bf16[256,768]{1,0:T(8,128)(2,1)S(1)}, u32[]{:S(2)}, u32[]{:S(2)}) collective-permute-start(bf16[256,768]{1,0:T(8,128)(2,1)S(1)} %copy-done.1), channel_id=1, source_target_pairs={{0,8},{2,10},{8,16},{10,18},{16,24},{18,26},{24,28},{26,30},{28,20... | collective-permute-start | bytes 1179656 | tf_op jit(solution)/shard_map/ppermute | solution.py:276
  7.3 8.6 %collective-permute-done.refs_12_ = bf16[256,768]{1,0:T(8,128)(2,1)S(1)} collective-permute-done((bf16[256,768]{1,0:T(8,128)(2,1)S(1)}, bf16[256,768]{1,0:T(8,128)(2,1)S(1)}, u32[]{:S(2)}, u32[]{:S(2)}) %collective-permute-start) | collective-permute-done | bytes 393248 | tf_op jit(solution)/shard_map/ppermute | solution.py:276
  19.8 1.7 %collective-permute-start.8 = (bf16[2,8,64,256]{3,2,1,0:T(8,128)(2,1)S(1)}, bf16[2,8,64,256]{3,2,1,0:T(8,128)(2,1)S(1)}, u32[]{:S(2)}, u32[]{:S(2)}) collective-permute-start(bf16[2,8,64,256]{3,2,1,0:T(8,128)(2,1)S(1)} %collective-permute-done.6.refs_1_), channel_id=1, source_target_pairs={{0,2},{2,0},{4,6},{6,4},{8,10},{10,8},{12,14},{14,12},{16,18},{18,... | collective-permute-start | bytes 1572872 | tf_op jit(solution)/shard_map/ppermute | solution.py:317
  21.6 4.9 %collective-permute-done.2.refs_11_ = bf16[256,768]{1,0:T(8,128)(2,1)S(1)} collective-permute-done((bf16[256,768]{1,0:T(8,128)(2,1)S(1)}, bf16[256,768]{1,0:T(8,128)(2,1)S(1)}, u32[]{:S(2)}, u32[]{:S(2)}) %collective-permute-start.2) | collective-permute-done | bytes 393248 | tf_op jit(solution)/shard_map/ppermute | solution.py:276
  27.5 1.3 %collective-permute-start.4 = (bf16[256,768]{1,0:T(8,128)(2,1)S(1)}, bf16[256,768]{1,0:T(8,128)(2,1)S(1)}, u32[]{:S(2)}, u32[]{:S(2)}) collective-permute-start(bf16[256,768]{1,0:T(8,128)(2,1)S(1)} %collective-permute-done.2.refs_11_), channel_id=1, source_target_pairs={{0,8},{2,10},{8,16},{10,18},{16,24},{18,26},{24,28},{26,30},{28,20... | collective-permute-start | bytes 1179656 | tf_op jit(solution)/shard_map/ppermute | solution.py:276
  28.9 1.3 %collective-permute-start.9 = (bf16[512,256]{1,0:T(8,128)(2,1)S(1)}, bf16[512,256]{1,0:T(8,128)(2,1)S(1)}, u32[]{:S(2)}, u32[]{:S(2)}) collective-permute-start(bf16[512,256]{1,0:T(8,128)(2,1)S(1)} %copy-done.4), channel_id=1, source_target_pairs={{0,8},{2,10},{8,16},{10,18},{16,24},{18,26},{24,28},{26,30},{28,20... | collective-permute-start | bytes 786440 | tf_op jit(solution)/shard_map/ppermute | solution.py:276
  30.5 10.9 %collective-permute-done.9.refs_8_ = bf16[512,256]{1,0:T(8,128)(2,1)S(1)} collective-permute-done((bf16[512,256]{1,0:T(8,128)(2,1)S(1)}, bf16[512,256]{1,0:T(8,128)(2,1)S(1)}, u32[]{:S(2)}, u32[]{:S(2)}) %collective-permute-start.9) | collective-permute-done | bytes 262176 | tf_op jit(solution)/shard_map/ppermute | solution.py:276
  47.2 1.3 %collective-permute-done.12.refs_9_ = bf16[128,768]{1,0:T(8,128)(2,1)S(1)} collective-permute-done((bf16[128,768]{1,0:T(8,128)(2,1)S(1)}, bf16[128,768]{1,0:T(8,128)(2,1)S(1)}, u32[]{:S(2)}, u32[]{:S(2)}) %collective-permute-start.12) | collective-permute-done | bytes 196640 | tf_op jit(solution)/shard_map/ppermute | solution.py:282
  48.5 2.1 %project.1 = (f32[128,256]{1,0:T(8,128)S(1)}, f32[128,256]{1,0:T(8,128)S(1)}, f32[256,512]{1,0:T(8,128)S(1)}) custom-call(bf16[2,8,64,256]{3,2,1,0:T(8,128)(2,1)S(1)} %norm.1.refs_0_, bf16[2,8,64,256]{3,2,1,0:T(8,128)(2,1)S(1)} %collective-permute-done.6.refs_1_, bf16[2,8,64,256]{3,2,1,0:T(8,128)(2,1)S(1)} %collective-permute-done.7.refs_2_, ...), custom_call_target="tpu_custom_call" | custom-call | tf_op jit(solution)/shard_map/project/pallas_call | solution.py:346
  50.6 5.7 %collective-permute-start.14 = (f32[128,256]{1,0:T(8,128)S(1)}, f32[128,256]{1,0:T(8,128)S(1)}, u32[]{:S(2)}, u32[]{:S(2)}) collective-permute-start(f32[128,256]{1,0:T(8,128)S(1)} %get-tuple-element.102), channel_id=1, source_target_pairs={{0,2},{2,0},{4,6},{6,4},{8,10},{10,8},{12,14},{14,12},{16,18},{18,... | collective-permute-start | bytes 393224 | tf_op jit(solution)/shard_map/ppermute | solution.py:358
  58.2 3.6 %all-to-all-start = ((bf16[8,128,256]{2,1,0:T(8,128)(2,1)}), bf16[8,128,256]{2,1,0:T(8,128)(2,1)S(1)}, u32[]{:S(2)}, u32[]{:S(2)}) async-start(bf16[8,128,256]{2,1,0:T(8,128)(2,1)} %bitcast.9), calls=%async_computation | async-start | bytes 1048576 | tf_op jit(solution)/shard_map/all_to_all | solution.py:371
  63.3 1.7 %collective-permute-start.17 = (bf16[512,256]{1,0:T(8,128)(2,1)S(1)}, bf16[512,256]{1,0:T(8,128)(2,1)S(1)}, u32[]{:S(2)}, u32[]{:S(2)}) collective-permute-start(bf16[512,256]{1,0:T(8,128)(2,1)S(1)} %copy-done.10), channel_id=1, source_target_pairs={{0,8},{2,10},{8,16},{10,18},{16,24},{18,26},{24,28},{26,30},{28,20... | collective-permute-start | bytes 786440 | tf_op jit(solution)/shard_map/ppermute | solution.py:276
  68.6 6.8 %all-to-all-done = bf16[8,128,256]{2,1,0:T(8,128)(2,1)S(1)} async-done(((bf16[8,128,256]{2,1,0:T(8,128)(2,1)}), bf16[8,128,256]{2,1,0:T(8,128)(2,1)S(1)}, u32[]{:S(2)}, u32[]{:S(2)}) %all-to-all-start) | async-done | bytes 524320 | tf_op jit(solution)/shard_map/all_to_all | solution.py:371
  76.0 2.7 %collective-permute-done.18.refs_3_ = bf16[512,256]{1,0:T(8,128)(2,1)S(1)} collective-permute-done((bf16[512,256]{1,0:T(8,128)(2,1)S(1)}, bf16[512,256]{1,0:T(8,128)(2,1)S(1)}, u32[]{:S(2)}, u32[]{:S(2)}) %collective-permute-start.18) | collective-permute-done | bytes 262176 | tf_op jit(solution)/shard_map/ppermute | solution.py:277
  78.7 2.6 %attend.1.mine_ref = f32[256,640]{1,0:T(8,128)S(1)} custom-call(f32[256,512]{1,0:T(8,128)S(1)} %get-tuple-element.100.mine_ref, f32[256,512]{1,0:T(8,128)S(1)} %collective-permute-done.13.theirs_ref, f32[256,128]{1,0:T(8,128)S(1)} %get-tuple-element.134.cosine_ref, f32[256,128]{1,0:T(8,128)S(1)} %get-tuple-element.135.sine_ref, s32[256,1]{1,0:T(8,128)S(1)} %copy.30.low_ref, ...), custom_call_target="tpu_custom_call" | custom-call | tf_op jit(solution)/shard_map/attend/pallas_call | solution.py:376
  81.9 4.1 %collective-permute-start.20 = (bf16[256,256]{1,0:T(8,128)(2,1)S(1)}, bf16[256,256]{1,0:T(8,128)(2,1)S(1)}, u32[]{:S(2)}, u32[]{:S(2)}) collective-permute-start(bf16[256,256]{1,0:T(8,128)(2,1)S(1)} %slice.14), channel_id=1, source_target_pairs={{0,8},{2,10},{8,16},{10,18},{16,24},{18,26},{24,28},{26,30},{28,20... | collective-permute-start | bytes 393224 | tf_op jit(solution)/shard_map/ppermute | solution.py:281
  86.0 2.8 %collective-permute-done.20.refs_4_ = bf16[256,256]{1,0:T(8,128)(2,1)S(1)} collective-permute-done((bf16[256,256]{1,0:T(8,128)(2,1)S(1)}, bf16[256,256]{1,0:T(8,128)(2,1)S(1)}, u32[]{:S(2)}, u32[]{:S(2)}) %collective-permute-start.20) | collective-permute-done | bytes 131104 | tf_op jit(solution)/shard_map/ppermute | solution.py:281
  88.8 1.9 %collective-permute-done.21.refs_5_ = bf16[256,256]{1,0:T(8,128)(2,1)S(1)} collective-permute-done((bf16[256,256]{1,0:T(8,128)(2,1)S(1)}, bf16[256,256]{1,0:T(8,128)(2,1)S(1)}, u32[]{:S(2)}, u32[]{:S(2)}) %collective-permute-start.21) | collective-permute-done | bytes 131104 | tf_op jit(solution)/shard_map/ppermute | solution.py:282
  90.8 1.4 %output.1 = (bf16[8,64,256]{2,1,0:T(8,128)(2,1)S(1)}, bf16[8,64,256]{2,1,0:T(8,128)(2,1)S(1)}, bf16[8,64,256]{2,1,0:T(8,128)(2,1)S(1)}, bf16[8,64,256]{2,1,0:T(8,128)(2,1)S(1)}) custom-call(f32[256,640]{1,0:T(8,128)S(1)} %attend.1.mine_ref, f32[256,640]{1,0:T(8,128)S(1)} %collective-permute-done.19.theirs_ref, bf16[512,256]{1,0:T(8,128)(2,1)S(1)} %copy-done.4, ...), custom_call_target="tpu_custom_call" | custom-call | tf_op jit(solution)/shard_map/output/pallas_call | solution.py:402
  92.2 1.4 %collective-permute-start.23 = (bf16[8,64,256]{2,1,0:T(8,128)(2,1)S(1)}, bf16[8,64,256]{2,1,0:T(8,128)(2,1)S(1)}, u32[]{:S(2)}, u32[]{:S(2)}) collective-permute-start(bf16[8,64,256]{2,1,0:T(8,128)(2,1)S(1)} %get-tuple-element.123), channel_id=1, source_target_pairs={{0,2},{1,3},{2,0},{3,1},{4,6},{5,7},{6,4},{7,5},{8,10},{9,11},{10,... | collective-permute-start | bytes 786440 | tf_op jit(solution)/shard_map/ppermute | solution.py:415
  93.6 1.4 %collective-permute-start.24 = (bf16[8,64,256]{2,1,0:T(8,128)(2,1)S(1)}, bf16[8,64,256]{2,1,0:T(8,128)(2,1)S(1)}, u32[]{:S(2)}, u32[]{:S(2)}) collective-permute-start(bf16[8,64,256]{2,1,0:T(8,128)(2,1)S(1)} %get-tuple-element.124), channel_id=1, source_target_pairs={{0,3},{1,2},{2,1},{3,0},{4,7},{5,6},{6,5},{7,4},{8,11},{9,10},{10,... | collective-permute-start | bytes 786440 | tf_op jit(solution)/shard_map/ppermute | solution.py:415
  95.0 3.9 %collective-permute-done.22.refs_1_ = bf16[8,64,256]{2,1,0:T(8,128)(2,1)S(1)} collective-permute-done((bf16[8,64,256]{2,1,0:T(8,128)(2,1)S(1)}, bf16[8,64,256]{2,1,0:T(8,128)(2,1)S(1)}, u32[]{:S(2)}, u32[]{:S(2)}) %collective-permute-start.22) | collective-permute-done | bytes 262176 | tf_op jit(solution)/shard_map/ppermute | solution.py:415
  98.9 7.0 %collective-permute-done.24.refs_3_ = bf16[8,64,256]{2,1,0:T(8,128)(2,1)S(1)} collective-permute-done((bf16[8,64,256]{2,1,0:T(8,128)(2,1)S(1)}, bf16[8,64,256]{2,1,0:T(8,128)(2,1)S(1)}, u32[]{:S(2)}, u32[]{:S(2)}) %collective-permute-start.24) | collective-permute-done | bytes 262176 | tf_op jit(solution)/shard_map/ppermute | solution.py:415
  (109 shorter events, 24.2 us)
Async XLA Ops:
  2.0 17.8 %collective-permute-start.6 = (bf16[2,8,64,256]{3,2,1,0:T(8,128)(2,1)S(1)}, bf16[2,8,64,256]{3,2,1,0:T(8,128)(2,1)S(1)}, u32[]{:S(2)}, u32[]{:S(2)}) collective-permute-start(bf16[2,8,64,256]{3,2,1,0:T(8,128)(2,1)S(1)} %norm.1.refs_0_), channel_id=1, source_target_pairs={{0,1},{1,0},{2,3},{3,2},{4,5},{5,4},{6,7},{7,6},{8,9},{9,8},{10,11... | collective-permute-start | bytes 1572872 | tf_op jit(solution)/shard_map/ppermute | solution.py:312
  4.1 26.1 %collective-permute-start.7 = (bf16[2,8,64,256]{3,2,1,0:T(8,128)(2,1)S(1)}, bf16[2,8,64,256]{3,2,1,0:T(8,128)(2,1)S(1)}, u32[]{:S(2)}, u32[]{:S(2)}) collective-permute-start(bf16[2,8,64,256]{3,2,1,0:T(8,128)(2,1)S(1)} %norm.1.refs_0_), channel_id=1, source_target_pairs={{0,2},{2,0},{4,6},{6,4},{8,10},{10,8},{12,14},{14,12},{16,18},{18,... | collective-permute-start | bytes 1572872 | tf_op jit(solution)/shard_map/ppermute | solution.py:317
  5.1 10.7 %collective-permute-start = (bf16[256,768]{1,0:T(8,128)(2,1)S(1)}, bf16[256,768]{1,0:T(8,128)(2,1)S(1)}, u32[]{:S(2)}, u32[]{:S(2)}) collective-permute-start(bf16[256,768]{1,0:T(8,128)(2,1)S(1)} %copy-done.1), channel_id=1, source_target_pairs={{0,8},{2,10},{8,16},{10,18},{16,24},{18,26},{24,28},{26,30},{28,20... | collective-permute-start | bytes 1179656 | tf_op jit(solution)/shard_map/ppermute | solution.py:276
  6.4 10.4 %collective-permute-start.1 = (bf16[256,768]{1,0:T(8,128)(2,1)S(1)}, bf16[256,768]{1,0:T(8,128)(2,1)S(1)}, u32[]{:S(2)}, u32[]{:S(2)}) collective-permute-start(bf16[256,768]{1,0:T(8,128)(2,1)S(1)} %copy-done.1), channel_id=1, source_target_pairs={{8,0},{10,2},{16,8},{18,10},{24,16},{26,18},{28,24},{30,26},{20,28... | collective-permute-start | bytes 1179656 | tf_op jit(solution)/shard_map/ppermute | solution.py:277
  16.8 9.6 %collective-permute-start.2 = (bf16[256,768]{1,0:T(8,128)(2,1)S(1)}, bf16[256,768]{1,0:T(8,128)(2,1)S(1)}, u32[]{:S(2)}, u32[]{:S(2)}) collective-permute-start(bf16[256,768]{1,0:T(8,128)(2,1)S(1)} %collective-permute-done.refs_12_), channel_id=1, source_target_pairs={{0,8},{2,10},{8,16},{10,18},{16,24},{18,26},{24,28},{26,30},{28,20... | collective-permute-start | bytes 1179656 | tf_op jit(solution)/shard_map/ppermute | solution.py:276
  18.1 9.3 %collective-permute-start.3 = (bf16[256,768]{1,0:T(8,128)(2,1)S(1)}, bf16[256,768]{1,0:T(8,128)(2,1)}, u32[]{:S(2)}, u32[]{:S(2)}) collective-permute-start(bf16[256,768]{1,0:T(8,128)(2,1)S(1)} %collective-permute-done.1.refs_5_), channel_id=1, source_target_pairs={{8,0},{10,2},{16,8},{18,10},{24,16},{26,18},{28,24},{30,26},{20,28... | collective-permute-start | bytes 1179656 | tf_op jit(solution)/shard_map/ppermute | solution.py:277
  19.8 10.6 %collective-permute-start.8 = (bf16[2,8,64,256]{3,2,1,0:T(8,128)(2,1)S(1)}, bf16[2,8,64,256]{3,2,1,0:T(8,128)(2,1)S(1)}, u32[]{:S(2)}, u32[]{:S(2)}) collective-permute-start(bf16[2,8,64,256]{3,2,1,0:T(8,128)(2,1)S(1)} %collective-permute-done.6.refs_1_), channel_id=1, source_target_pairs={{0,2},{2,0},{4,6},{6,4},{8,10},{10,8},{12,14},{14,12},{16,18},{18,... | collective-permute-start | bytes 1572872 | tf_op jit(solution)/shard_map/ppermute | solution.py:317
  27.5 15.2 %collective-permute-start.4 = (bf16[256,768]{1,0:T(8,128)(2,1)S(1)}, bf16[256,768]{1,0:T(8,128)(2,1)S(1)}, u32[]{:S(2)}, u32[]{:S(2)}) collective-permute-start(bf16[256,768]{1,0:T(8,128)(2,1)S(1)} %collective-permute-done.2.refs_11_), channel_id=1, source_target_pairs={{0,8},{2,10},{8,16},{10,18},{16,24},{18,26},{24,28},{26,30},{28,20... | collective-permute-start | bytes 1179656 | tf_op jit(solution)/shard_map/ppermute | solution.py:276
  28.7 13.9 %collective-permute-start.5 = (bf16[256,768]{1,0:T(8,128)(2,1)}, bf16[256,768]{1,0:T(8,128)(2,1)S(1)}, u32[]{:S(2)}, u32[]{:S(2)}) collective-permute-start(bf16[256,768]{1,0:T(8,128)(2,1)} %collective-permute-done.3.refs_6_), channel_id=1, source_target_pairs={{8,0},{10,2},{16,8},{18,10},{24,16},{26,18},{28,24},{30,26},{20,28... | collective-permute-start | bytes 1179656 | tf_op jit(solution)/shard_map/ppermute | solution.py:277
  28.9 12.4 %collective-permute-start.9 = (bf16[512,256]{1,0:T(8,128)(2,1)S(1)}, bf16[512,256]{1,0:T(8,128)(2,1)S(1)}, u32[]{:S(2)}, u32[]{:S(2)}) collective-permute-start(bf16[512,256]{1,0:T(8,128)(2,1)S(1)} %copy-done.4), channel_id=1, source_target_pairs={{0,8},{2,10},{8,16},{10,18},{16,24},{18,26},{24,28},{26,30},{28,20... | collective-permute-start | bytes 786440 | tf_op jit(solution)/shard_map/ppermute | solution.py:276
  30.3 12.3 %collective-permute-start.10 = (bf16[512,256]{1,0:T(8,128)(2,1)S(1)}, bf16[512,256]{1,0:T(8,128)(2,1)S(1)}, u32[]{:S(2)}, u32[]{:S(2)}) collective-permute-start(bf16[512,256]{1,0:T(8,128)(2,1)S(1)} %copy-done.4), channel_id=1, source_target_pairs={{8,0},{10,2},{16,8},{18,10},{24,16},{26,18},{28,24},{30,26},{20,28... | collective-permute-start | bytes 786440 | tf_op jit(solution)/shard_map/ppermute | solution.py:277
  44.8 11.7 %collective-permute-start.15 = (bf16[512,256]{1,0:T(8,128)(2,1)S(1)}, bf16[512,256]{1,0:T(8,128)(2,1)S(1)}, u32[]{:S(2)}, u32[]{:S(2)}) collective-permute-start(bf16[512,256]{1,0:T(8,128)(2,1)S(1)} %collective-permute-done.9.refs_8_), channel_id=1, source_target_pairs={{0,8},{2,10},{8,16},{10,18},{16,24},{18,26},{24,28},{26,30},{28,20... | collective-permute-start | bytes 786440 | tf_op jit(solution)/shard_map/ppermute | solution.py:276
  46.1 10.5 %collective-permute-start.16 = (bf16[512,256]{1,0:T(8,128)(2,1)S(1)}, bf16[512,256]{1,0:T(8,128)(2,1)S(1)}, u32[]{:S(2)}, u32[]{:S(2)}) collective-permute-start(bf16[512,256]{1,0:T(8,128)(2,1)S(1)} %collective-permute-done.10.refs_1_), channel_id=1, source_target_pairs={{8,0},{10,2},{16,8},{18,10},{24,16},{26,18},{28,24},{30,26},{20,28... | collective-permute-start | bytes 786440 | tf_op jit(solution)/shard_map/ppermute | solution.py:277
  50.6 6.7 %collective-permute-start.14 = (f32[128,256]{1,0:T(8,128)S(1)}, f32[128,256]{1,0:T(8,128)S(1)}, u32[]{:S(2)}, u32[]{:S(2)}) collective-permute-start(f32[128,256]{1,0:T(8,128)S(1)} %get-tuple-element.102), channel_id=1, source_target_pairs={{0,2},{2,0},{4,6},{6,4},{8,10},{10,8},{12,14},{14,12},{16,18},{18,... | collective-permute-start | bytes 393224 | tf_op jit(solution)/shard_map/ppermute | solution.py:358
  58.2 17.2 %all-to-all-start = ((bf16[8,128,256]{2,1,0:T(8,128)(2,1)}), bf16[8,128,256]{2,1,0:T(8,128)(2,1)S(1)}, u32[]{:S(2)}, u32[]{:S(2)}) async-start(bf16[8,128,256]{2,1,0:T(8,128)(2,1)} %bitcast.9), calls=%async_computation | async-start | bytes 1048576 | tf_op jit(solution)/shard_map/all_to_all | solution.py:371
  62.6 16.0 %collective-permute-start.13 = (f32[256,512]{1,0:T(8,128)S(1)}, f32[256,512]{1,0:T(8,128)S(1)}, u32[]{:S(2)}, u32[]{:S(2)}) collective-permute-start(f32[256,512]{1,0:T(8,128)S(1)} %get-tuple-element.100.mine_ref), channel_id=1, source_target_pairs={{0,2},{2,0},{4,6},{6,4},{8,10},{10,8},{12,14},{14,12},{16,18},{18,... | collective-permute-start | bytes 1572872 | tf_op jit(solution)/shard_map/ppermute | solution.py:359
  63.3 12.7 %collective-permute-start.17 = (bf16[512,256]{1,0:T(8,128)(2,1)S(1)}, bf16[512,256]{1,0:T(8,128)(2,1)S(1)}, u32[]{:S(2)}, u32[]{:S(2)}) collective-permute-start(bf16[512,256]{1,0:T(8,128)(2,1)S(1)} %copy-done.10), channel_id=1, source_target_pairs={{0,8},{2,10},{8,16},{10,18},{16,24},{18,26},{24,28},{26,30},{28,20... | collective-permute-start | bytes 786440 | tf_op jit(solution)/shard_map/ppermute | solution.py:276
  65.0 13.7 %collective-permute-start.18 = (bf16[512,256]{1,0:T(8,128)(2,1)S(1)}, bf16[512,256]{1,0:T(8,128)(2,1)S(1)}, u32[]{:S(2)}, u32[]{:S(2)}) collective-permute-start(bf16[512,256]{1,0:T(8,128)(2,1)S(1)} %copy-done.12), channel_id=1, source_target_pairs={{8,0},{10,2},{16,8},{18,10},{24,16},{26,18},{28,24},{30,26},{20,28... | collective-permute-start | bytes 786440 | tf_op jit(solution)/shard_map/ppermute | solution.py:277
  81.3 9.5 %collective-permute-start.19 = (f32[256,640]{1,0:T(8,128)S(1)}, f32[256,640]{1,0:T(8,128)S(1)}, u32[]{:S(2)}, u32[]{:S(2)}) collective-permute-start(f32[256,640]{1,0:T(8,128)S(1)} %attend.1.mine_ref), channel_id=1, source_target_pairs={{0,2},{2,0},{4,6},{6,4},{8,10},{10,8},{12,14},{14,12},{16,18},{18,... | collective-permute-start | bytes 1966088 | tf_op jit(solution)/shard_map/ppermute | solution.py:395
  81.9 7.0 %collective-permute-start.20 = (bf16[256,256]{1,0:T(8,128)(2,1)S(1)}, bf16[256,256]{1,0:T(8,128)(2,1)S(1)}, u32[]{:S(2)}, u32[]{:S(2)}) collective-permute-start(bf16[256,256]{1,0:T(8,128)(2,1)S(1)} %slice.14), channel_id=1, source_target_pairs={{0,8},{2,10},{8,16},{10,18},{16,24},{18,26},{24,28},{26,30},{28,20... | collective-permute-start | bytes 393224 | tf_op jit(solution)/shard_map/ppermute | solution.py:281
  85.9 4.8 %collective-permute-start.21 = (bf16[256,256]{1,0:T(8,128)(2,1)S(1)}, bf16[256,256]{1,0:T(8,128)(2,1)S(1)}, u32[]{:S(2)}, u32[]{:S(2)}) collective-permute-start(bf16[256,256]{1,0:T(8,128)(2,1)S(1)} %slice.15), channel_id=1, source_target_pairs={{8,0},{10,2},{16,8},{18,10},{24,16},{26,18},{28,24},{30,26},{20,28... | collective-permute-start | bytes 393224 | tf_op jit(solution)/shard_map/ppermute | solution.py:282
  92.2 6.7 %collective-permute-start.22 = (bf16[8,64,256]{2,1,0:T(8,128)(2,1)S(1)}, bf16[8,64,256]{2,1,0:T(8,128)(2,1)S(1)}, u32[]{:S(2)}, u32[]{:S(2)}) collective-permute-start(bf16[8,64,256]{2,1,0:T(8,128)(2,1)S(1)} %get-tuple-element.122), channel_id=1, source_target_pairs={{0,1},{1,0},{2,3},{3,2},{4,5},{5,4},{6,7},{7,6},{8,9},{9,8},{10,11... | collective-permute-start | bytes 786440 | tf_op jit(solution)/shard_map/ppermute | solution.py:415
  92.2 6.7 %collective-permute-start.23 = (bf16[8,64,256]{2,1,0:T(8,128)(2,1)S(1)}, bf16[8,64,256]{2,1,0:T(8,128)(2,1)S(1)}, u32[]{:S(2)}, u32[]{:S(2)}) collective-permute-start(bf16[8,64,256]{2,1,0:T(8,128)(2,1)S(1)} %get-tuple-element.123), channel_id=1, source_target_pairs={{0,2},{1,3},{2,0},{3,1},{4,6},{5,7},{6,4},{7,5},{8,10},{9,11},{10,... | collective-permute-start | bytes 786440 | tf_op jit(solution)/shard_map/ppermute | solution.py:415
  93.6 12.2 %collective-permute-start.24 = (bf16[8,64,256]{2,1,0:T(8,128)(2,1)S(1)}, bf16[8,64,256]{2,1,0:T(8,128)(2,1)S(1)}, u32[]{:S(2)}, u32[]{:S(2)}) collective-permute-start(bf16[8,64,256]{2,1,0:T(8,128)(2,1)S(1)} %get-tuple-element.124), channel_id=1, source_target_pairs={{0,3},{1,2},{2,1},{3,0},{4,7},{5,6},{6,5},{7,4},{8,11},{9,10},{10,... | collective-permute-start | bytes 786440 | tf_op jit(solution)/shard_map/ppermute | solution.py:415
  (24 other events, 152.0 us)

commit v14 on v12

--- a/solution.py
+++ b/solution.py
@@ -2,6 +2,7 @@
 
 import jax
 import jax.numpy as jnp
+import numpy as np
 from jax import lax
 from jax.experimental import pallas as pl
 from jax.experimental.pallas import tpu as pltpu
@@ -32,17 +33,6 @@
     return [z * wide + y for z, y in ring]
 
 
-def locate(layout_rows, span_order, doc_ends):
-    span_index = layout_rows // SPAN
-    matches = span_index[:, None] == jnp.arange(span_order.shape[0], dtype=jnp.int32)[None, :]
-    source_span = jnp.sum(jnp.where(matches, span_order[None, :], 0), axis=1)
-    initial = source_span * SPAN + layout_rows % SPAN
-    doc_start = jnp.max(
-        jnp.where(doc_ends[None, :] <= initial[:, None], doc_ends[None, :], 0), axis=1
-    )
-    return (initial, doc_start)
-
-
 def vmem_specs(count):
     return [pl.BlockSpec(memory_space=pltpu.VMEM)] * count
 
@@ -57,6 +47,47 @@
     for chip, spot in enumerate(place):
         at = jnp.where(context // 2 == chip, jnp.int32(spot), at)
     return at, context % 2
+
+
+def where_kernel(
+    n_tensor, rows_here, spans_ref, lengths_ref, freq_ref, cos_ref, sin_ref, low_ref, high_ref, orig_ref
+):
+    context, tensor = lax.axis_index("context"), lax.axis_index("tensor")
+    rows = rows_here * n_tensor
+    spans = rows // SPAN
+
+    def shift(values, size):
+        return lax.shift_right_logical(values, jnp.int32(size.bit_length() - 1))
+
+    def inside_of(row):
+        row = row & (rows - 1)
+        turned = (tensor + shift(row, rows_here)) & (n_tensor - 1)
+        return turned * rows_here + (row & (rows_here - 1))
+
+    def initial(owner, inside):
+        source = jnp.zeros_like(inside)
+        for k in range(spans):
+            source = jnp.where(shift(inside, SPAN) == k, spans_ref[owner * spans + k], source)
+        return source * SPAN + (inside & (SPAN - 1))
+
+    row = lax.broadcasted_iota(jnp.int32, cos_ref.shape, 0)
+    inside = inside_of(row)
+    orig = jnp.where(row < rows, initial(context, inside), initial(context ^ 1, inside))
+    start, end = jnp.zeros_like(orig), jnp.int32(0)
+    for i in range(lengths_ref.shape[0]):
+        end = end + lengths_ref[i]
+        start = jnp.where(orig >= end, end, start)
+    low_ref[...] = start[:, :1]
+    high_ref[...] = orig[:, :1]
+    angle = (orig - start).astype(jnp.float32) * freq_ref[...]
+    lane = lax.broadcasted_iota(jnp.int32, cos_ref.shape, 1)
+    cos_ref[...] = jnp.cos(angle)
+    sine = jnp.sin(angle)
+    sin_ref[...] = jnp.where(lane < HD // 2, -sine, sine)
+    inside = inside_of(lax.broadcasted_iota(jnp.int32, (1, rows), 1))
+    for chip in range(orig_ref.shape[1] // rows):
+        owner = 2 * chip + context % 2
+        orig_ref[:, chip * rows : (chip + 1) * rows] = initial(owner, inside)
 
 
 def norm_kernel(place, chips, hidden_ref, gain_ref, out_ref):
@@ -311,6 +342,26 @@
             for t in range(n_tensor)
         ]
 
+    smem, vmem = pl.BlockSpec(memory_space=pltpu.SMEM), pl.BlockSpec(memory_space=pltpu.VMEM)
+    freq = rope_theta ** (-(np.arange(HD // 2, dtype=np.float64) * 2.0 / HD))
+    freq = np.concatenate([freq, freq]).astype(np.float32)[None, :]
+    table = jax.ShapeDtypeStruct((2 * tokens_here, HD), jnp.float32)
+    bound = jax.ShapeDtypeStruct((2 * tokens_here, 1), jnp.int32)
+    cosine, sine, query_start, query_orig, key_orig = pl.pallas_call(
+        functools.partial(where_kernel, n_tensor, rows_here),
+        out_shape=[
+            table,
+            table,
+            bound,
+            bound,
+            jax.ShapeDtypeStruct((1, chips * tokens_here), jnp.int32),
+        ],
+        in_specs=[smem, smem, vmem],
+        out_specs=vmem_specs(5),
+        compiler_params=compute_params(),
+        name="where",
+    )(span_order, doc_lengths, jnp.asarray(freq))
+
     qkv_ring = Ring(w_qkv)
     qkv_ring.step()
     normed = pl.pallas_call(
@@ -334,23 +385,6 @@
     normed = qkv_ring.step(normed)
     while not qkv_ring.done():
         qkv_ring.step()
-
-    doc_ends = jnp.cumsum(doc_lengths)
-    inside = (
-        (tensor + jnp.arange(n_tensor, dtype=jnp.int32)) % n_tensor * rows_here
-    )[:, None] + jnp.arange(rows_here, dtype=jnp.int32)[None, :]
-    inside = inside.reshape(-1)
-    both = jnp.concatenate([context * tokens_here + inside, (context ^ 1) * tokens_here + inside])
-    query_orig, query_start = locate(both, span_order, doc_ends)
-    half = HD // 2
-    freq = rope_theta ** (-(jnp.arange(half, dtype=jnp.float32) * 2.0 / HD))
-    angle = (query_orig - query_start).astype(jnp.float32)[:, None] * freq[None, :]
-    cosine, sine = jnp.cos(angle), jnp.sin(angle)
-    cosine = jnp.concatenate([cosine, cosine], axis=1)
-    sine = jnp.concatenate([-sine, sine], axis=1)
-    owner = 2 * jnp.arange(chips, dtype=jnp.int32) + context % 2
-    key_rows = (owner[:, None] * tokens_here + inside[None, :]).reshape(-1).astype(jnp.int32)
-    key_orig, _ = locate(key_rows, span_order, doc_ends)
 
     out_ring = Ring(w_out)
     out_ring.step()
@@ -383,6 +417,7 @@
     kv = lax.all_to_all(
         kv, "context", split_axis=0, concat_axis=0, axis_index_groups=same_core, tiled=True
     )
+    out_ring.step()
     (kv,) = ordered((kv,))
 
     mixed = pl.pallas_call(
@@ -397,12 +432,11 @@
         queries_theirs,
         cosine,
         sine,
-        query_start[:, None],
-        query_orig[:, None],
-        key_orig[None, :],
+        query_start,
+        query_orig,
+        key_orig,
         kv,
     )
-    out_ring.step()
     (mixed,) = ordered((mixed,))
     mixed_theirs = lax.ppermute(mixed, "context", sibling)
 

time: 103 us -> 95.7 us (0.929)
  waiting for transfers between devices: 51.1 us -> 44.3 us
  starting transfers between devices: 35.3 us -> 39.8 us
  local copies, waits for them, and re-layouts: 4.72 us -> 1.82 us
  other arithmetic: 1.47 us -> 0 us
    all_to_all x1, waiting for transfers between devices: 10.9 us -> 0.01 us  [per_device(): lax.all_to_all(kv, 'context', split_axis=0, concat_axis=0, axis_index_gro...]
    ppermute x6, waiting for transfers between devices: 21.3 us -> 26.5 us  [step(): self.up.append(lax.ppermute(up, 'context', ahead))]
    ppermute x6, starting transfers between devices: 5.17 us -> 7.47 us  [output(): part = lax.ppermute(part, ('context', 'tensor'), member(e, -d))]
    unnamed x20 -> x14, local copies, waits for them, and re-layouts: 3.92 us -> 1.77 us
    ppermute x2, starting transfers between devices: 2.68 us -> 4.3 us  [per_device(): normed += [lax.ppermute(rows, 'context', sibling) for rows in normed]]
    pallas_call x0 -> x1, Pallas kernels: none -> 1.24 us  [per_device(): pl.pallas_call(functools.partial(where_kernel, n_tensor, rows_here), out_...]
    pallas_call x1, Pallas kernels: 2.2 us -> 1.09 us  [per_device(): pl.pallas_call(functools.partial(project_kernel, chips, groups), out_shap...]
    pallas_call x2, Pallas kernels: 3.19 us -> 2.09 us  [output(): pl.pallas_call(functools.partial(output_kernel, groups, [len(pieces) for...]
  transfers between devices with their start and end apart: 29 -> 29, of which waited for: 19 -> 19; matrix products, arithmetic and copies ran while one was open for 2% -> 0% of each run, Pallas kernels for 5% -> 5%
where the time goes in v14:
time: 95.7 us; the launch traced here: 95.3 us
  waiting for transfers between devices  44.3 us (46%)
  starting transfers between devices  39.8 us (42%)
  Pallas kernels  9.19 us (10%)
  local copies, waits for them, and re-layouts  1.82 us (2%)
    ppermute x6, waiting for transfers between devices, step(): self.up.append(lax.ppermute(up, 'context', ahead))  26.5 us
    ppermute x6, starting transfers between devices, step(): self.up.append(lax.ppermute(up, 'context', ahead))  10.3 us
    ppermute x6, waiting for transfers between devices, step(): self.down.append(lax.ppermute(down, 'context', back))  9.32 us
    ppermute x6, starting transfers between devices, output(): part = lax.ppermute(part, ('context', 'tensor'), member(e, -d))  7.47 us
    ppermute x1, starting transfers between devices, per_device(): theirs = lax.ppermute(theirs, 'context', sibling)  6.09 us
    ppermute x6, waiting for transfers between devices, output(): part = lax.ppermute(part, ('context', 'tensor'), member(e, -d))  4.39 us
    ppermute x2, starting transfers between devices, per_device(): normed += [lax.ppermute(rows, 'context', sibling) for rows in normed]  4.3 us
    all_to_all x1, starting transfers between devices, per_device(): lax.all_to_all(kv, 'context', split_axis=0, concat_axis=0, axis_index_gro...  3.49 us
  transfers between devices with their start and end apart: 29, of which 19 were waited for; matrix products, arithmetic and copies ran while one was open for 0% of the time, Pallas kernels for 5%

profile of v14, /device:TPU:1, one launch (start us, length us, event | category | flops | bytes accessed | tf_op | source)
XLA Modules:
  0.0 95.3 jit_solution(11382581452990774920)
XLA Ops:
  0.0 2.1 %collective-permute-start = (bf16[256,768]{1,0:T(8,128)(2,1)}, bf16[256,768]{1,0:T(8,128)(2,1)S(1)}, u32[]{:S(2)}, u32[]{:S(2)}) collective-permute-start(bf16[256,768]{1,0:T(8,128)(2,1)} %refs_4_), channel_id=1, source_target_pairs={{0,8},{2,10},{8,16},{10,18},{16,24},{18,26},{24,28},{26,30},{28,20... | collective-permute-start | bytes 1179656 | tf_op jit(solution)/shard_map/ppermute | solution.py:314
  4.2 1.4 %collective-permute-start.6 = (bf16[2,8,64,256]{3,2,1,0:T(8,128)(2,1)S(1)}, bf16[2,8,64,256]{3,2,1,0:T(8,128)(2,1)S(1)}, u32[]{:S(2)}, u32[]{:S(2)}) collective-permute-start(bf16[2,8,64,256]{3,2,1,0:T(8,128)(2,1)S(1)} %norm.1.refs_0_), channel_id=1, source_target_pairs={{0,1},{1,0},{2,3},{3,2},{4,5},{5,4},{6,7},{7,6},{8,9},{9,8},{10,11... | collective-permute-start | bytes 1572872 | tf_op jit(solution)/shard_map/ppermute | solution.py:376
  5.6 5.5 %collective-permute-done.refs_12_ = bf16[256,768]{1,0:T(8,128)(2,1)S(1)} collective-permute-done((bf16[256,768]{1,0:T(8,128)(2,1)}, bf16[256,768]{1,0:T(8,128)(2,1)S(1)}, u32[]{:S(2)}, u32[]{:S(2)}) %collective-permute-start) | collective-permute-done | bytes 393248 | tf_op jit(solution)/shard_map/ppermute | solution.py:314
  12.0 1.3 %collective-permute-start.2 = (bf16[256,768]{1,0:T(8,128)(2,1)S(1)}, bf16[256,768]{1,0:T(8,128)(2,1)S(1)}, u32[]{:S(2)}, u32[]{:S(2)}) collective-permute-start(bf16[256,768]{1,0:T(8,128)(2,1)S(1)} %collective-permute-done.refs_12_), channel_id=1, source_target_pairs={{0,8},{2,10},{8,16},{10,18},{16,24},{18,26},{24,28},{26,30},{28,20... | collective-permute-start | bytes 1179656 | tf_op jit(solution)/shard_map/ppermute | solution.py:314
  13.5 2.4 %collective-permute-start.7 = (bf16[2,8,64,256]{3,2,1,0:T(8,128)(2,1)S(1)}, bf16[2,8,64,256]{3,2,1,0:T(8,128)(2,1)S(1)}, u32[]{:S(2)}, u32[]{:S(2)}) collective-permute-start(bf16[2,8,64,256]{3,2,1,0:T(8,128)(2,1)S(1)} %norm.1.refs_0_), channel_id=1, source_target_pairs={{0,2},{2,0},{4,6},{6,4},{8,10},{10,8},{12,14},{14,12},{16,18},{18,... | collective-permute-start | bytes 1572872 | tf_op jit(solution)/shard_map/ppermute | solution.py:381
  16.7 1.9 %collective-permute-start.8 = (bf16[2,8,64,256]{3,2,1,0:T(8,128)(2,1)S(1)}, bf16[2,8,64,256]{3,2,1,0:T(8,128)(2,1)S(1)}, u32[]{:S(2)}, u32[]{:S(2)}) collective-permute-start(bf16[2,8,64,256]{3,2,1,0:T(8,128)(2,1)S(1)} %collective-permute-done.6.refs_1_), channel_id=1, source_target_pairs={{0,2},{2,0},{4,6},{6,4},{8,10},{10,8},{12,14},{14,12},{16,18},{18,... | collective-permute-start | bytes 1572872 | tf_op jit(solution)/shard_map/ppermute | solution.py:381
  18.6 2.2 %collective-permute-done.2.refs_11_ = bf16[256,768]{1,0:T(8,128)(2,1)S(1)} collective-permute-done((bf16[256,768]{1,0:T(8,128)(2,1)S(1)}, bf16[256,768]{1,0:T(8,128)(2,1)S(1)}, u32[]{:S(2)}, u32[]{:S(2)}) %collective-permute-start.2) | collective-permute-done | bytes 393248 | tf_op jit(solution)/shard_map/ppermute | solution.py:314
  21.8 1.3 %collective-permute-start.4 = (bf16[256,768]{1,0:T(8,128)(2,1)S(1)}, bf16[256,768]{1,0:T(8,128)(2,1)S(1)}, u32[]{:S(2)}, u32[]{:S(2)}) collective-permute-start(bf16[256,768]{1,0:T(8,128)(2,1)S(1)} %collective-permute-done.2.refs_11_), channel_id=1, source_target_pairs={{0,8},{2,10},{8,16},{10,18},{16,24},{18,26},{24,28},{26,30},{28,20... | collective-permute-start | bytes 1179656 | tf_op jit(solution)/shard_map/ppermute | solution.py:314
  23.2 6.1 %collective-permute-done.4.refs_10_ = bf16[256,768]{1,0:T(8,128)(2,1)S(1)} collective-permute-done((bf16[256,768]{1,0:T(8,128)(2,1)S(1)}, bf16[256,768]{1,0:T(8,128)(2,1)S(1)}, u32[]{:S(2)}, u32[]{:S(2)}) %collective-permute-start.4) | collective-permute-done | bytes 393248 | tf_op jit(solution)/shard_map/ppermute | solution.py:314
  30.4 1.3 %collective-permute-start.9 = (bf16[128,768]{1,0:T(8,128)(2,1)S(1)}, bf16[128,768]{1,0:T(8,128)(2,1)S(1)}, u32[]{:S(2)}, u32[]{:S(2)}) collective-permute-start(bf16[128,768]{1,0:T(8,128)(2,1)S(1)} %slice.12), channel_id=1, source_target_pairs={{0,8},{2,10},{8,16},{10,18},{16,24},{18,26},{24,28},{26,30},{28,20... | collective-permute-start | bytes 589832 | tf_op jit(solution)/shard_map/ppermute | solution.py:319
  33.4 1.5 %collective-permute-done.9.refs_8_ = bf16[128,768]{1,0:T(8,128)(2,1)S(1)} collective-permute-done((bf16[128,768]{1,0:T(8,128)(2,1)S(1)}, bf16[128,768]{1,0:T(8,128)(2,1)S(1)}, u32[]{:S(2)}, u32[]{:S(2)}) %collective-permute-start.9) | collective-permute-done | bytes 196640 | tf_op jit(solution)/shard_map/ppermute | solution.py:319
  34.9 1.3 %collective-permute-done.10.refs_9_ = bf16[128,768]{1,0:T(8,128)(2,1)S(1)} collective-permute-done((bf16[128,768]{1,0:T(8,128)(2,1)S(1)}, bf16[128,768]{1,0:T(8,128)(2,1)S(1)}, u32[]{:S(2)}, u32[]{:S(2)}) %collective-permute-start.10) | collective-permute-done | bytes 196640 | tf_op jit(solution)/shard_map/ppermute | solution.py:320
  37.4 6.1 %collective-permute-start.12 = (f32[128,256]{1,0:T(8,128)S(1)}, f32[128,256]{1,0:T(8,128)S(1)}, u32[]{:S(2)}, u32[]{:S(2)}) collective-permute-start(f32[128,256]{1,0:T(8,128)S(1)} %get-tuple-element.119), channel_id=1, source_target_pairs={{0,2},{2,0},{4,6},{6,4},{8,10},{10,8},{12,14},{14,12},{16,18},{18,... | collective-permute-start | bytes 393224 | tf_op jit(solution)/shard_map/ppermute | solution.py:404
  45.7 3.5 %all-to-all-start = ((bf16[8,128,256]{2,1,0:T(8,128)(2,1)}), bf16[8,128,256]{2,1,0:T(8,128)(2,1)S(1)}, u32[]{:S(2)}, u32[]{:S(2)}) async-start(bf16[8,128,256]{2,1,0:T(8,128)(2,1)} %bitcast.1), calls=%async_computation | async-start | bytes 1048576 | tf_op jit(solution)/shard_map/all_to_all | solution.py:417
  49.8 1.6 %collective-permute-start.15 = (bf16[512,256]{1,0:T(8,128)(2,1)S(1)}, bf16[512,256]{1,0:T(8,128)(2,1)S(1)}, u32[]{:S(2)}, u32[]{:S(2)}) collective-permute-start(bf16[512,256]{1,0:T(8,128)(2,1)S(1)} %collective-permute-done.13.refs_1_), channel_id=1, source_target_pairs={{0,8},{2,10},{8,16},{10,18},{16,24},{18,26},{24,28},{26,30},{28,20... | collective-permute-start | bytes 786440 | tf_op jit(solution)/shard_map/ppermute | solution.py:314
  51.4 11.8 %collective-permute-done.15.refs_0_ = bf16[512,256]{1,0:T(8,128)(2,1)S(1)} collective-permute-done((bf16[512,256]{1,0:T(8,128)(2,1)S(1)}, bf16[512,256]{1,0:T(8,128)(2,1)S(1)}, u32[]{:S(2)}, u32[]{:S(2)}) %collective-permute-start.15) | collective-permute-done | bytes 262176 | tf_op jit(solution)/shard_map/ppermute | solution.py:314
  63.1 2.2 %collective-permute-done.16.refs_4_ = bf16[512,256]{1,0:T(8,128)(2,1)S(1)} collective-permute-done((bf16[512,256]{1,0:T(8,128)(2,1)S(1)}, bf16[512,256]{1,0:T(8,128)(2,1)S(1)}, u32[]{:S(2)}, u32[]{:S(2)}) %collective-permute-start.16) | collective-permute-done | bytes 262176 | tf_op jit(solution)/shard_map/ppermute | solution.py:315
  65.3 2.5 %attend.1.mine_ref = f32[256,640]{1,0:T(8,128)S(1)} custom-call(f32[256,512]{1,0:T(8,128)S(1)} %get-tuple-element.112.mine_ref, f32[256,512]{1,0:T(8,128)S(1)} %collective-permute-done.11.theirs_ref, f32[256,128]{1,0:T(8,128)S(1)} %get-tuple-element.113.cosine_ref, f32[256,128]{1,0:T(8,128)S(1)} %get-tuple-element.114.sine_ref, ...), custom_call_target="tpu_custom_call" | custom-call | tf_op jit(solution)/shard_map/attend/pallas_call | solution.py:423
  70.3 2.8 %collective-permute-start.19 = (bf16[512,256]{1,0:T(8,128)(2,1)S(1)}, bf16[512,256]{1,0:T(8,128)(2,1)S(1)}, u32[]{:S(2)}, u32[]{:S(2)}) collective-permute-start(bf16[512,256]{1,0:T(8,128)(2,1)S(1)} %collective-permute-done.15.refs_0_), channel_id=1, source_target_pairs={{0,8},{2,10},{8,16},{10,18},{16,24},{18,26},{24,28},{26,30},{28,20... | collective-permute-start | bytes 786440 | tf_op jit(solution)/shard_map/ppermute | solution.py:314
  75.4 4.2 %collective-permute-done.18.refs_0_ = bf16[512,256]{1,0:T(8,128)(2,1)S(1)} collective-permute-done((bf16[512,256]{1,0:T(8,128)(2,1)S(1)}, bf16[512,256]{1,0:T(8,128)(2,1)S(1)}, u32[]{:S(2)}, u32[]{:S(2)}) %collective-permute-start.18) | collective-permute-done | bytes 262176 | tf_op jit(solution)/shard_map/ppermute | solution.py:315
  82.2 1.4 %collective-permute-start.23 = (bf16[5,64,256]{2,1,0:T(8,128)(2,1)S(1)}, bf16[5,64,256]{2,1,0:T(8,128)(2,1)S(1)}, u32[]{:S(2)}, u32[]{:S(2)}) collective-permute-start(bf16[5,64,256]{2,1,0:T(8,128)(2,1)S(1)} %get-tuple-element.153), channel_id=1, source_target_pairs={{0,2},{1,3},{2,0},{3,1},{4,6},{5,7},{6,4},{7,5},{8,10},{9,11},{10,... | collective-permute-start | bytes 491528 | tf_op jit(solution)/shard_map/ppermute | solution.py:463
  86.1 1.3 %collective-permute-start.25 = (bf16[3,64,256]{2,1,0:T(8,128)(2,1)S(1)}, bf16[3,64,256]{2,1,0:T(8,128)(2,1)S(1)}, u32[]{:S(2)}, u32[]{:S(2)}) collective-permute-start(bf16[3,64,256]{2,1,0:T(8,128)(2,1)S(1)} %get-tuple-element.156), channel_id=1, source_target_pairs={{0,1},{1,0},{2,3},{3,2},{4,5},{5,4},{6,7},{7,6},{8,9},{9,8},{10,11... | collective-permute-start | bytes 294920 | tf_op jit(solution)/shard_map/ppermute | solution.py:463
  87.4 2.3 %collective-permute-start.26 = (bf16[3,64,256]{2,1,0:T(8,128)(2,1)S(1)}, bf16[3,64,256]{2,1,0:T(8,128)(2,1)S(1)}, u32[]{:S(2)}, u32[]{:S(2)}) collective-permute-start(bf16[3,64,256]{2,1,0:T(8,128)(2,1)S(1)} %get-tuple-element.157), channel_id=1, source_target_pairs={{0,2},{1,3},{2,0},{3,1},{4,6},{5,7},{6,4},{7,5},{8,10},{9,11},{10,... | collective-permute-start | bytes 294920 | tf_op jit(solution)/shard_map/ppermute | solution.py:463
  90.6 3.6 %collective-permute-done.27.refs_7_ = bf16[3,64,256]{2,1,0:T(8,128)(2,1)S(1)} collective-permute-done((bf16[3,64,256]{2,1,0:T(8,128)(2,1)S(1)}, bf16[3,64,256]{2,1,0:T(8,128)(2,1)S(1)}, u32[]{:S(2)}, u32[]{:S(2)}) %collective-permute-start.27) | collective-permute-done | bytes 98336 | tf_op jit(solution)/shard_map/ppermute | solution.py:463
  (60 shorter events, 23.6 us)
Async XLA Ops:
  0.0 11.1 %collective-permute-start = (bf16[256,768]{1,0:T(8,128)(2,1)}, bf16[256,768]{1,0:T(8,128)(2,1)S(1)}, u32[]{:S(2)}, u32[]{:S(2)}) collective-permute-start(bf16[256,768]{1,0:T(8,128)(2,1)} %refs_4_), channel_id=1, source_target_pairs={{0,8},{2,10},{8,16},{10,18},{16,24},{18,26},{24,28},{26,30},{28,20... | collective-permute-start | bytes 1179656 | tf_op jit(solution)/shard_map/ppermute | solution.py:314
  2.1 9.9 %collective-permute-start.1 = (bf16[256,768]{1,0:T(8,128)(2,1)}, bf16[256,768]{1,0:T(8,128)(2,1)S(1)}, u32[]{:S(2)}, u32[]{:S(2)}) collective-permute-start(bf16[256,768]{1,0:T(8,128)(2,1)} %refs_4_), channel_id=1, source_target_pairs={{8,0},{10,2},{16,8},{18,10},{24,16},{26,18},{28,24},{30,26},{20,28... | collective-permute-start | bytes 1179656 | tf_op jit(solution)/shard_map/ppermute | solution.py:315
  4.2 12.5 %collective-permute-start.6 = (bf16[2,8,64,256]{3,2,1,0:T(8,128)(2,1)S(1)}, bf16[2,8,64,256]{3,2,1,0:T(8,128)(2,1)S(1)}, u32[]{:S(2)}, u32[]{:S(2)}) collective-permute-start(bf16[2,8,64,256]{3,2,1,0:T(8,128)(2,1)S(1)} %norm.1.refs_0_), channel_id=1, source_target_pairs={{0,1},{1,0},{2,3},{3,2},{4,5},{5,4},{6,7},{7,6},{8,9},{9,8},{10,11... | collective-permute-start | bytes 1572872 | tf_op jit(solution)/shard_map/ppermute | solution.py:376
  12.0 8.7 %collective-permute-start.2 = (bf16[256,768]{1,0:T(8,128)(2,1)S(1)}, bf16[256,768]{1,0:T(8,128)(2,1)S(1)}, u32[]{:S(2)}, u32[]{:S(2)}) collective-permute-start(bf16[256,768]{1,0:T(8,128)(2,1)S(1)} %collective-permute-done.refs_12_), channel_id=1, source_target_pairs={{0,8},{2,10},{8,16},{10,18},{16,24},{18,26},{24,28},{26,30},{28,20... | collective-permute-start | bytes 1179656 | tf_op jit(solution)/shard_map/ppermute | solution.py:314
  13.3 8.5 %collective-permute-start.3 = (bf16[256,768]{1,0:T(8,128)(2,1)S(1)}, bf16[256,768]{1,0:T(8,128)(2,1)S(1)}, u32[]{:S(2)}, u32[]{:S(2)}) collective-permute-start(bf16[256,768]{1,0:T(8,128)(2,1)S(1)} %collective-permute-done.1.refs_5_), channel_id=1, source_target_pairs={{8,0},{10,2},{16,8},{18,10},{24,16},{26,18},{28,24},{30,26},{20,28... | collective-permute-start | bytes 1179656 | tf_op jit(solution)/shard_map/ppermute | solution.py:315
  13.5 9.8 %collective-permute-start.7 = (bf16[2,8,64,256]{3,2,1,0:T(8,128)(2,1)S(1)}, bf16[2,8,64,256]{3,2,1,0:T(8,128)(2,1)S(1)}, u32[]{:S(2)}, u32[]{:S(2)}) collective-permute-start(bf16[2,8,64,256]{3,2,1,0:T(8,128)(2,1)S(1)} %norm.1.refs_0_), channel_id=1, source_target_pairs={{0,2},{2,0},{4,6},{6,4},{8,10},{10,8},{12,14},{14,12},{16,18},{18,... | collective-permute-start | bytes 1572872 | tf_op jit(solution)/shard_map/ppermute | solution.py:381
  16.7 6.5 %collective-permute-start.8 = (bf16[2,8,64,256]{3,2,1,0:T(8,128)(2,1)S(1)}, bf16[2,8,64,256]{3,2,1,0:T(8,128)(2,1)S(1)}, u32[]{:S(2)}, u32[]{:S(2)}) collective-permute-start(bf16[2,8,64,256]{3,2,1,0:T(8,128)(2,1)S(1)} %collective-permute-done.6.refs_1_), channel_id=1, source_target_pairs={{0,2},{2,0},{4,6},{6,4},{8,10},{10,8},{12,14},{14,12},{16,18},{18,... | collective-permute-start | bytes 1572872 | tf_op jit(solution)/shard_map/ppermute | solution.py:381
  21.8 7.5 %collective-permute-start.4 = (bf16[256,768]{1,0:T(8,128)(2,1)S(1)}, bf16[256,768]{1,0:T(8,128)(2,1)S(1)}, u32[]{:S(2)}, u32[]{:S(2)}) collective-permute-start(bf16[256,768]{1,0:T(8,128)(2,1)S(1)} %collective-permute-done.2.refs_11_), channel_id=1, source_target_pairs={{0,8},{2,10},{8,16},{10,18},{16,24},{18,26},{24,28},{26,30},{28,20... | collective-permute-start | bytes 1179656 | tf_op jit(solution)/shard_map/ppermute | solution.py:314
  23.1 7.3 %collective-permute-start.5 = (bf16[256,768]{1,0:T(8,128)(2,1)S(1)}, bf16[256,768]{1,0:T(8,128)(2,1)S(1)}, u32[]{:S(2)}, u32[]{:S(2)}) collective-permute-start(bf16[256,768]{1,0:T(8,128)(2,1)S(1)} %collective-permute-done.3.refs_6_), channel_id=1, source_target_pairs={{8,0},{10,2},{16,8},{18,10},{24,16},{26,18},{28,24},{30,26},{20,28... | collective-permute-start | bytes 1179656 | tf_op jit(solution)/shard_map/ppermute | solution.py:315
  30.4 4.6 %collective-permute-start.9 = (bf16[128,768]{1,0:T(8,128)(2,1)S(1)}, bf16[128,768]{1,0:T(8,128)(2,1)S(1)}, u32[]{:S(2)}, u32[]{:S(2)}) collective-permute-start(bf16[128,768]{1,0:T(8,128)(2,1)S(1)} %slice.12), channel_id=1, source_target_pairs={{0,8},{2,10},{8,16},{10,18},{16,24},{18,26},{24,28},{26,30},{28,20... | collective-permute-start | bytes 589832 | tf_op jit(solution)/shard_map/ppermute | solution.py:319
  31.7 4.6 %collective-permute-start.10 = (bf16[128,768]{1,0:T(8,128)(2,1)S(1)}, bf16[128,768]{1,0:T(8,128)(2,1)S(1)}, u32[]{:S(2)}, u32[]{:S(2)}) collective-permute-start(bf16[128,768]{1,0:T(8,128)(2,1)S(1)} %slice.13), channel_id=1, source_target_pairs={{8,0},{10,2},{16,8},{18,10},{24,16},{26,18},{28,24},{30,26},{20,28... | collective-permute-start | bytes 589832 | tf_op jit(solution)/shard_map/ppermute | solution.py:320
  31.9 12.8 %collective-permute-start.13 = (bf16[512,256]{1,0:T(8,128)(2,1)S(1)}, bf16[512,256]{1,0:T(8,128)(2,1)S(1)}, u32[]{:S(2)}, u32[]{:S(2)}) collective-permute-start(bf16[512,256]{1,0:T(8,128)(2,1)S(1)} %copy-done.2), channel_id=1, source_target_pairs={{0,8},{2,10},{8,16},{10,18},{16,24},{18,26},{24,28},{26,30},{28,20... | collective-permute-start | bytes 786440 | tf_op jit(solution)/shard_map/ppermute | solution.py:314
  33.2 11.5 %collective-permute-start.14 = (bf16[512,256]{1,0:T(8,128)(2,1)S(1)}, bf16[512,256]{1,0:T(8,128)(2,1)S(1)}, u32[]{:S(2)}, u32[]{:S(2)}) collective-permute-start(bf16[512,256]{1,0:T(8,128)(2,1)S(1)} %copy-done.2), channel_id=1, source_target_pairs={{8,0},{10,2},{16,8},{18,10},{24,16},{26,18},{28,24},{30,26},{20,28... | collective-permute-start | bytes 786440 | tf_op jit(solution)/shard_map/ppermute | solution.py:315
  37.4 7.4 %collective-permute-start.12 = (f32[128,256]{1,0:T(8,128)S(1)}, f32[128,256]{1,0:T(8,128)S(1)}, u32[]{:S(2)}, u32[]{:S(2)}) collective-permute-start(f32[128,256]{1,0:T(8,128)S(1)} %get-tuple-element.119), channel_id=1, source_target_pairs={{0,2},{2,0},{4,6},{6,4},{8,10},{10,8},{12,14},{14,12},{16,18},{18,... | collective-permute-start | bytes 393224 | tf_op jit(solution)/shard_map/ppermute | solution.py:404
  45.7 19.7 %all-to-all-start = ((bf16[8,128,256]{2,1,0:T(8,128)(2,1)}), bf16[8,128,256]{2,1,0:T(8,128)(2,1)S(1)}, u32[]{:S(2)}, u32[]{:S(2)}) async-start(bf16[8,128,256]{2,1,0:T(8,128)(2,1)} %bitcast.1), calls=%async_computation | async-start | bytes 1048576 | tf_op jit(solution)/shard_map/all_to_all | solution.py:417
  49.2 16.2 %collective-permute-start.11 = (f32[256,512]{1,0:T(8,128)S(1)}, f32[256,512]{1,0:T(8,128)S(1)}, u32[]{:S(2)}, u32[]{:S(2)}) collective-permute-start(f32[256,512]{1,0:T(8,128)S(1)} %get-tuple-element.112.mine_ref), channel_id=1, source_target_pairs={{0,2},{2,0},{4,6},{6,4},{8,10},{10,8},{12,14},{14,12},{16,18},{18,... | collective-permute-start | bytes 1572872 | tf_op jit(solution)/shard_map/ppermute | solution.py:405
  49.8 13.3 %collective-permute-start.15 = (bf16[512,256]{1,0:T(8,128)(2,1)S(1)}, bf16[512,256]{1,0:T(8,128)(2,1)S(1)}, u32[]{:S(2)}, u32[]{:S(2)}) collective-permute-start(bf16[512,256]{1,0:T(8,128)(2,1)S(1)} %collective-permute-done.13.refs_1_), channel_id=1, source_target_pairs={{0,8},{2,10},{8,16},{10,18},{16,24},{18,26},{24,28},{26,30},{28,20... | collective-permute-start | bytes 786440 | tf_op jit(solution)/shard_map/ppermute | solution.py:314
  51.4 14.0 %collective-permute-start.16 = (bf16[512,256]{1,0:T(8,128)(2,1)S(1)}, bf16[512,256]{1,0:T(8,128)(2,1)S(1)}, u32[]{:S(2)}, u32[]{:S(2)}) collective-permute-start(bf16[512,256]{1,0:T(8,128)(2,1)S(1)} %collective-permute-done.14.refs_3_), channel_id=1, source_target_pairs={{8,0},{10,2},{16,8},{18,10},{24,16},{26,18},{28,24},{30,26},{20,28... | collective-permute-start | bytes 786440 | tf_op jit(solution)/shard_map/ppermute | solution.py:315
  67.9 5.2 %collective-permute-start.17 = (f32[256,640]{1,0:T(8,128)S(1)}, f32[256,640]{1,0:T(8,128)S(1)}, u32[]{:S(2)}, u32[]{:S(2)}) collective-permute-start(f32[256,640]{1,0:T(8,128)S(1)} %attend.1.mine_ref), channel_id=1, source_target_pairs={{0,2},{2,0},{4,6},{6,4},{8,10},{10,8},{12,14},{14,12},{16,18},{18,... | collective-permute-start | bytes 1966088 | tf_op jit(solution)/shard_map/ppermute | solution.py:441
  69.0 10.6 %collective-permute-start.18 = (bf16[512,256]{1,0:T(8,128)(2,1)S(1)}, bf16[512,256]{1,0:T(8,128)(2,1)S(1)}, u32[]{:S(2)}, u32[]{:S(2)}) collective-permute-start(bf16[512,256]{1,0:T(8,128)(2,1)S(1)} %collective-permute-done.16.refs_4_), channel_id=1, source_target_pairs={{8,0},{10,2},{16,8},{18,10},{24,16},{26,18},{28,24},{30,26},{20,28... | collective-permute-start | bytes 786440 | tf_op jit(solution)/shard_map/ppermute | solution.py:315
  70.3 10.4 %collective-permute-start.19 = (bf16[512,256]{1,0:T(8,128)(2,1)S(1)}, bf16[512,256]{1,0:T(8,128)(2,1)S(1)}, u32[]{:S(2)}, u32[]{:S(2)}) collective-permute-start(bf16[512,256]{1,0:T(8,128)(2,1)S(1)} %collective-permute-done.15.refs_0_), channel_id=1, source_target_pairs={{0,8},{2,10},{8,16},{10,18},{16,24},{18,26},{24,28},{26,30},{28,20... | collective-permute-start | bytes 786440 | tf_op jit(solution)/shard_map/ppermute | solution.py:314
  74.2 15.5 %collective-permute-start.22 = (bf16[5,64,256]{2,1,0:T(8,128)(2,1)S(1)}, bf16[5,64,256]{2,1,0:T(8,128)(2,1)S(1)}, u32[]{:S(2)}, u32[]{:S(2)}) collective-permute-start(bf16[5,64,256]{2,1,0:T(8,128)(2,1)S(1)} %get-tuple-element.152), channel_id=1, source_target_pairs={{0,1},{1,0},{2,3},{3,2},{4,5},{5,4},{6,7},{7,6},{8,9},{9,8},{10,11... | collective-permute-start | bytes 491528 | tf_op jit(solution)/shard_map/ppermute | solution.py:463
  82.2 7.6 %collective-permute-start.23 = (bf16[5,64,256]{2,1,0:T(8,128)(2,1)S(1)}, bf16[5,64,256]{2,1,0:T(8,128)(2,1)S(1)}, u32[]{:S(2)}, u32[]{:S(2)}) collective-permute-start(bf16[5,64,256]{2,1,0:T(8,128)(2,1)S(1)} %get-tuple-element.153), channel_id=1, source_target_pairs={{0,2},{1,3},{2,0},{3,1},{4,6},{5,7},{6,4},{7,5},{8,10},{9,11},{10,... | collective-permute-start | bytes 491528 | tf_op jit(solution)/shard_map/ppermute | solution.py:463
  83.6 6.5 %collective-permute-start.24 = (bf16[5,64,256]{2,1,0:T(8,128)(2,1)S(1)}, bf16[5,64,256]{2,1,0:T(8,128)(2,1)S(1)}, u32[]{:S(2)}, u32[]{:S(2)}) collective-permute-start(bf16[5,64,256]{2,1,0:T(8,128)(2,1)S(1)} %get-tuple-element.154), channel_id=1, source_target_pairs={{0,3},{1,2},{2,1},{3,0},{4,7},{5,6},{6,5},{7,4},{8,11},{9,10},{10,... | collective-permute-start | bytes 491528 | tf_op jit(solution)/shard_map/ppermute | solution.py:463
  (12 other events, 74.3 us)

commit v15 on v14

--- a/solution.py
+++ b/solution.py
@@ -50,7 +50,18 @@
 
 
 def where_kernel(
-    n_tensor, rows_here, spans_ref, lengths_ref, freq_ref, cos_ref, sin_ref, low_ref, high_ref, orig_ref
+    ring,
+    place,
+    n_tensor,
+    rows_here,
+    spans_ref,
+    lengths_ref,
+    freq_ref,
+    cos_ref,
+    sin_ref,
+    low_ref,
+    high_ref,
+    orig_ref,
 ):
     context, tensor = lax.axis_index("context"), lax.axis_index("tensor")
     rows = rows_here * n_tensor
@@ -85,9 +96,14 @@
     sine = jnp.sin(angle)
     sin_ref[...] = jnp.where(lane < HD // 2, -sine, sine)
     inside = inside_of(lax.broadcasted_iota(jnp.int32, (1, rows), 1))
-    for chip in range(orig_ref.shape[1] // rows):
-        owner = 2 * chip + context % 2
-        orig_ref[:, chip * rows : (chip + 1) * rows] = initial(owner, inside)
+    at, core = place_of(place)
+    for slot in range(len(ring)):
+        spot = lax.rem(at + slot, len(ring))
+        chip = jnp.int32(0)
+        for i, at_spot in enumerate(ring):
+            chip = jnp.where(spot == i, jnp.int32(at_spot), chip)
+        owner = 2 * chip + core
+        orig_ref[:, slot * rows : (slot + 1) * rows] = initial(owner, inside)
 
 
 def norm_kernel(place, chips, hidden_ref, gain_ref, out_ref):
@@ -156,15 +172,13 @@
     return values * cosine + pltpu.roll(values, HD // 2, 1) * sine
 
 
-def keys_kernel(chips, mine_ref, theirs_ref, cosine_ref, sine_ref, out_ref):
-    rows = out_ref.shape[0] // chips
-    cosine, sine = cosine_ref[:rows, :], sine_ref[:rows, :]
+def keys_kernel(mine_ref, theirs_ref, cosine_ref, sine_ref, out_ref):
+    rows = out_ref.shape[0]
     total = mine_ref[...] + theirs_ref[...]
-    keys = turn(total[:, :HD], cosine, sine).astype(jnp.bfloat16)
-    values = total[:, HD:].astype(jnp.bfloat16)
-    for chip in range(chips):
-        out_ref[chip * rows : (chip + 1) * rows, :HD] = keys
-        out_ref[chip * rows : (chip + 1) * rows, HD:] = values
+    out_ref[:, :HD] = turn(total[:, :HD], cosine_ref[:rows, :], sine_ref[:rows, :]).astype(
+        jnp.bfloat16
+    )
+    out_ref[:, HD:] = total[:, HD:].astype(jnp.bfloat16)
 
 
 def attend_kernel(
@@ -175,11 +189,16 @@
     low_ref,
     high_ref,
     orig_ref,
-    kv_ref,
-    out_ref,
+    *refs,
 ):
-    keys = kv_ref[:, :HD]
-    values = kv_ref[:, HD:]
+    block_refs, (out_ref, keys_ref, values_ref) = refs[:-3], refs[-3:]
+    start = 0
+    for ref in block_refs:
+        keys_ref[start : start + ref.shape[0], :] = ref[:, :HD]
+        values_ref[start : start + ref.shape[0], :] = ref[:, HD:]
+        start += ref.shape[0]
+    keys = keys_ref[...]
+    values = values_ref[...]
     orig = orig_ref[...]
     allowed = (orig >= low_ref[...]) & (orig <= high_ref[...])
     scale = 1.0 / HD**0.5
@@ -295,7 +314,6 @@
     back = [(b, a) for a, b in ahead]
     sibling = [(c, c ^ 1) for c in range(n_context)]
 
-    same_core = [[2 * chip + k for chip in range(chips)] for k in range(2)]
     token = [doc_lengths]
 
     def ordered(values):
@@ -348,7 +366,7 @@
     table = jax.ShapeDtypeStruct((2 * tokens_here, HD), jnp.float32)
     bound = jax.ShapeDtypeStruct((2 * tokens_here, 1), jnp.int32)
     cosine, sine, query_start, query_orig, key_orig = pl.pallas_call(
-        functools.partial(where_kernel, n_tensor, rows_here),
+        functools.partial(where_kernel, ring, place, n_tensor, rows_here),
         out_shape=[
             table,
             table,
@@ -381,6 +399,9 @@
     normed += [lax.ppermute(rows, "context", sibling) for rows in normed]
 
     qkv_ring.step()
+    cosine, sine, query_start, query_orig, key_orig = ordered(
+        (cosine, sine, query_start, query_orig, key_orig)
+    )
     qkv_ring.step()
     normed = qkv_ring.step(normed)
     while not qkv_ring.done():
@@ -403,28 +424,32 @@
     )(*ordered((*normed, *blocks)))
     theirs = lax.ppermute(theirs, "context", sibling)
     queries_theirs = lax.ppermute(queries, "context", sibling)
+    mine, theirs = ordered((mine, theirs))
     out_ring.step()
-    mine, theirs = ordered((mine, theirs))
     kv = pl.pallas_call(
-        functools.partial(keys_kernel, chips),
-        out_shape=jax.ShapeDtypeStruct((chips * tokens_here, 2 * HD), jnp.bfloat16),
+        keys_kernel,
+        out_shape=jax.ShapeDtypeStruct((tokens_here, 2 * HD), jnp.bfloat16),
         in_specs=vmem_specs(4),
         out_specs=vmem_specs(1)[0],
         compiler_params=compute_params(),
         name="keys",
     )(mine, theirs, cosine, sine)
-    (kv,) = ordered((kv,))
-    kv = lax.all_to_all(
-        kv, "context", split_axis=0, concat_axis=0, axis_index_groups=same_core, tiled=True
-    )
+    kv_ring = Ring(kv)
+    kv_ring.step()
+    kv_ring.step()
     out_ring.step()
-    (kv,) = ordered((kv,))
+    while not kv_ring.done():
+        kv_ring.step()
+    while not out_ring.done():
+        out_ring.step()
+    kv_blocks = ordered(kv_ring.finish())
 
     mixed = pl.pallas_call(
         attend_kernel,
         out_shape=jax.ShapeDtypeStruct((2 * tokens_here, HEAD_COLS + HD), jnp.float32),
-        in_specs=vmem_specs(8),
+        in_specs=vmem_specs(7 + len(kv_blocks)),
         out_specs=vmem_specs(1)[0],
+        scratch_shapes=[pltpu.VMEM((chips * tokens_here, HD), jnp.bfloat16)] * 2,
         compiler_params=compute_params(),
         name="attend",
     )(
@@ -435,7 +460,7 @@
         query_start,
         query_orig,
         key_orig,
-        kv,
+        *kv_blocks,
     )
     (mixed,) = ordered((mixed,))
     mixed_theirs = lax.ppermute(mixed, "context", sibling)
@@ -464,14 +489,11 @@
                 arrived.append(part)
         return arrived
 
-    reach = max(chips // 2 - 2, 0)
-    while len(out_ring.up) <= reach:
-        out_ring.step()
+    reach = (chips - 1) // 2
     near = 2 * reach + 1
     arrived = output(list(range(-reach, reach + 1)), "output_near")
-    while not out_ring.done():
-        out_ring.step()
-    arrived += output(list(range(reach + 1, chips - reach)), "output_far")
+    if near < chips:
+        arrived += output(list(range(reach + 1, chips - reach)), "output_far")
     return pl.pallas_call(
         functools.partial(sum_kernel, place, chips, groups, near),
         out_shape=jax.ShapeDtypeStruct((rows_here, n_context * out_block), jnp.bfloat16),

time: 95.7 us -> 98.3 us (1.027)
  starting transfers between devices: 39.8 us -> 45.5 us
  waiting for transfers between devices: 44.3 us -> 41.9 us
    ppermute x6 -> x9, waiting for transfers between devices: 26.5 us -> 12.7 us  [step(): self.up.append(lax.ppermute(up, 'context', ahead))]
    ppermute x2 -> x3, waiting for transfers between devices: 1.59 us -> 7.48 us  [step(): lax.ppermute(down[half:], 'context', back)]
    ppermute x6 -> x9, waiting for transfers between devices: 9.32 us -> 14.2 us  [step(): self.down.append(lax.ppermute(down, 'context', back))]
    ppermute x1, starting transfers between devices: 1.14 us -> 5.47 us  [per_device(): mixed_theirs = lax.ppermute(mixed, 'context', sibling)]
    all_to_all x1 -> x0, starting transfers between devices: 3.49 us -> none  [per_device(): lax.all_to_all(kv, 'context', split_axis=0, concat_axis=0, axis_index_gro...]
    ppermute x2 -> x3, starting transfers between devices: 1.61 us -> 4.27 us  [step(): lax.ppermute(up[:half], 'context', ahead)]
    ppermute x6 -> x9, starting transfers between devices: 10.3 us -> 12.5 us  [step(): self.up.append(lax.ppermute(up, 'context', ahead))]
    ppermute x1, waiting for transfers between devices: 0.01 us -> 1.72 us  [per_device(): mixed_theirs = lax.ppermute(mixed, 'context', sibling)]
  transfers between devices with their start and end apart: 29 -> 36, of which waited for: 19 -> 18; matrix products, arithmetic and copies ran while one was open for 0% -> 0% of each run, Pallas kernels for 5% -> 4%
where the time goes in v15:
time: 98.3 us; the launch traced here: 97.8 us
  starting transfers between devices  45.5 us (46%)
  waiting for transfers between devices  41.9 us (43%)
  Pallas kernels  8.49 us (9%)
  local copies, waits for them, and re-layouts  1.82 us (2%)
    ppermute x9, waiting for transfers between devices, step(): self.down.append(lax.ppermute(down, 'context', back))  14.2 us
    ppermute x9, waiting for transfers between devices, step(): self.up.append(lax.ppermute(up, 'context', ahead))  12.7 us
    ppermute x9, starting transfers between devices, step(): self.up.append(lax.ppermute(up, 'context', ahead))  12.5 us
    ppermute x6, starting transfers between devices, output(): part = lax.ppermute(part, ('context', 'tensor'), member(e, -d))  7.61 us
    ppermute x3, waiting for transfers between devices, step(): lax.ppermute(down[half:], 'context', back)  7.48 us
    ppermute x1, starting transfers between devices, per_device(): theirs = lax.ppermute(theirs, 'context', sibling)  5.86 us
    ppermute x1, starting transfers between devices, per_device(): mixed_theirs = lax.ppermute(mixed, 'context', sibling)  5.47 us
    ppermute x2, starting transfers between devices, per_device(): normed += [lax.ppermute(rows, 'context', sibling) for rows in normed]  4.3 us
  transfers between devices with their start and end apart: 36, of which 18 were waited for; matrix products, arithmetic and copies ran while one was open for 0% of the time, Pallas kernels for 4%

profile of v15, /device:TPU:1, one launch (start us, length us, event | category | flops | bytes accessed | tf_op | source)
XLA Modules:
  0.0 97.8 jit_solution(9597726216390012749)
XLA Ops:
  0.0 2.1 %collective-permute-start = (bf16[256,768]{1,0:T(8,128)(2,1)}, bf16[256,768]{1,0:T(8,128)(2,1)S(1)}, u32[]{:S(2)}, u32[]{:S(2)}) collective-permute-start(bf16[256,768]{1,0:T(8,128)(2,1)} %refs_4_), channel_id=1, source_target_pairs={{0,8},{2,10},{8,16},{10,18},{16,24},{18,26},{24,28},{26,30},{28,20... | collective-permute-start | bytes 1179656 | tf_op jit(solution)/shard_map/ppermute | solution.py:332
  4.2 1.4 %collective-permute-start.6 = (bf16[2,8,64,256]{3,2,1,0:T(8,128)(2,1)S(1)}, bf16[2,8,64,256]{3,2,1,0:T(8,128)(2,1)S(1)}, u32[]{:S(2)}, u32[]{:S(2)}) collective-permute-start(bf16[2,8,64,256]{3,2,1,0:T(8,128)(2,1)S(1)} %norm.1.refs_0_), channel_id=1, source_target_pairs={{0,1},{1,0},{2,3},{3,2},{4,5},{5,4},{6,7},{7,6},{8,9},{9,8},{10,11... | collective-permute-start | bytes 1572872 | tf_op jit(solution)/shard_map/ppermute | solution.py:394
  5.6 5.5 %collective-permute-done.refs_12_ = bf16[256,768]{1,0:T(8,128)(2,1)S(1)} collective-permute-done((bf16[256,768]{1,0:T(8,128)(2,1)}, bf16[256,768]{1,0:T(8,128)(2,1)S(1)}, u32[]{:S(2)}, u32[]{:S(2)}) %collective-permute-start) | collective-permute-done | bytes 393248 | tf_op jit(solution)/shard_map/ppermute | solution.py:332
  13.5 2.4 %collective-permute-start.7 = (bf16[2,8,64,256]{3,2,1,0:T(8,128)(2,1)S(1)}, bf16[2,8,64,256]{3,2,1,0:T(8,128)(2,1)S(1)}, u32[]{:S(2)}, u32[]{:S(2)}) collective-permute-start(bf16[2,8,64,256]{3,2,1,0:T(8,128)(2,1)S(1)} %norm.1.refs_0_), channel_id=1, source_target_pairs={{0,2},{2,0},{4,6},{6,4},{8,10},{10,8},{12,14},{14,12},{16,18},{18,... | collective-permute-start | bytes 1572872 | tf_op jit(solution)/shard_map/ppermute | solution.py:399
  16.7 1.9 %collective-permute-start.8 = (bf16[2,8,64,256]{3,2,1,0:T(8,128)(2,1)S(1)}, bf16[2,8,64,256]{3,2,1,0:T(8,128)(2,1)S(1)}, u32[]{:S(2)}, u32[]{:S(2)}) collective-permute-start(bf16[2,8,64,256]{3,2,1,0:T(8,128)(2,1)S(1)} %collective-permute-done.6.refs_1_), channel_id=1, source_target_pairs={{0,2},{2,0},{4,6},{6,4},{8,10},{10,8},{12,14},{14,12},{16,18},{18,... | collective-permute-start | bytes 1572872 | tf_op jit(solution)/shard_map/ppermute | solution.py:399
  23.2 6.1 %collective-permute-done.4.refs_10_ = bf16[256,768]{1,0:T(8,128)(2,1)S(1)} collective-permute-done((bf16[256,768]{1,0:T(8,128)(2,1)S(1)}, bf16[256,768]{1,0:T(8,128)(2,1)S(1)}, u32[]{:S(2)}, u32[]{:S(2)}) %collective-permute-start.4) | collective-permute-done | bytes 393248 | tf_op jit(solution)/shard_map/ppermute | solution.py:332
  33.4 2.6 %collective-permute-done.10.refs_9_ = bf16[128,768]{1,0:T(8,128)(2,1)S(1)} collective-permute-done((bf16[128,768]{1,0:T(8,128)(2,1)S(1)}, bf16[128,768]{1,0:T(8,128)(2,1)S(1)}, u32[]{:S(2)}, u32[]{:S(2)}) %collective-permute-start.10) | collective-permute-done | bytes 196640 | tf_op jit(solution)/shard_map/ppermute | solution.py:338
  37.1 5.9 %collective-permute-start.12 = (f32[128,256]{1,0:T(8,128)S(1)}, f32[128,256]{1,0:T(8,128)S(1)}, u32[]{:S(2)}, u32[]{:S(2)}) collective-permute-start(f32[128,256]{1,0:T(8,128)S(1)} %get-tuple-element.149), channel_id=1, source_target_pairs={{0,2},{2,0},{4,6},{6,4},{8,10},{10,8},{12,14},{14,12},{16,18},{18,... | collective-permute-start | bytes 393224 | tf_op jit(solution)/shard_map/ppermute | solution.py:425
  45.4 2.2 %collective-permute-start.11 = (f32[256,512]{1,0:T(8,128)S(1)}, f32[256,512]{1,0:T(8,128)S(1)}, u32[]{:S(2)}, u32[]{:S(2)}) collective-permute-start(f32[256,512]{1,0:T(8,128)S(1)} %get-tuple-element.142.mine_ref), channel_id=1, source_target_pairs={{0,2},{2,0},{4,6},{6,4},{8,10},{10,8},{12,14},{14,12},{16,18},{18,... | collective-permute-start | bytes 1572872 | tf_op jit(solution)/shard_map/ppermute | solution.py:426
  49.3 4.3 %collective-permute-done.15.refs_1_ = bf16[128,256]{1,0:T(8,128)(2,1)S(1)} collective-permute-done((bf16[128,256]{1,0:T(8,128)(2,1)S(1)}, bf16[128,256]{1,0:T(8,128)(2,1)S(1)}, u32[]{:S(2)}, u32[]{:S(2)}) %collective-permute-start.15) | collective-permute-done | bytes 65568 | tf_op jit(solution)/shard_map/ppermute | solution.py:333
  55.1 1.4 %collective-permute-start.18 = (bf16[128,256]{1,0:T(8,128)(2,1)S(1)}, bf16[128,256]{1,0:T(8,128)(2,1)S(1)}, u32[]{:S(2)}, u32[]{:S(2)}) collective-permute-start(bf16[128,256]{1,0:T(8,128)(2,1)S(1)} %collective-permute-done.16.refs_8_), channel_id=1, source_target_pairs={{0,8},{2,10},{8,16},{10,18},{16,24},{18,26},{24,28},{26,30},{28,20... | collective-permute-start | bytes 196616 | tf_op jit(solution)/shard_map/ppermute | solution.py:332
  56.5 5.4 %collective-permute-done.17.refs_2_ = bf16[128,256]{1,0:T(8,128)(2,1)S(1)} collective-permute-done((bf16[128,256]{1,0:T(8,128)(2,1)S(1)}, bf16[128,256]{1,0:T(8,128)(2,1)S(1)}, u32[]{:S(2)}, u32[]{:S(2)}) %collective-permute-start.17) | collective-permute-done | bytes 65568 | tf_op jit(solution)/shard_map/ppermute | solution.py:333
  63.4 1.6 %collective-permute-done.21.refs_3_ = bf16[128,256]{1,0:T(8,128)(2,1)S(1)} collective-permute-done((bf16[128,256]{1,0:T(8,128)(2,1)S(1)}, bf16[128,256]{1,0:T(8,128)(2,1)S(1)}, u32[]{:S(2)}, u32[]{:S(2)}) %collective-permute-start.21) | collective-permute-done | bytes 65568 | tf_op jit(solution)/shard_map/ppermute | solution.py:333
  65.3 1.5 %collective-permute-start.23 = (bf16[64,256]{1,0:T(8,128)(2,1)S(1)}, bf16[64,256]{1,0:T(8,128)(2,1)S(1)}, u32[]{:S(2)}, u32[]{:S(2)}) collective-permute-start(bf16[64,256]{1,0:T(8,128)(2,1)S(1)} %slice.20), channel_id=1, source_target_pairs={{0,8},{2,10},{8,16},{10,18},{16,24},{18,26},{24,28},{26,30},{28,20... | collective-permute-start | bytes 98312 | tf_op jit(solution)/shard_map/ppermute | solution.py:337
  66.8 1.8 %collective-permute-done.24.refs_5_ = bf16[64,256]{1,0:T(8,128)(2,1)S(1)} collective-permute-done((bf16[64,256]{1,0:T(8,128)(2,1)S(1)}, bf16[64,256]{1,0:T(8,128)(2,1)S(1)}, u32[]{:S(2)}, u32[]{:S(2)}) %collective-permute-start.24) | collective-permute-done | bytes 32800 | tf_op jit(solution)/shard_map/ppermute | solution.py:338
  68.6 2.6 %attend.1.mine_ref = f32[256,640]{1,0:T(8,128)S(1)} custom-call(f32[256,512]{1,0:T(8,128)S(1)} %get-tuple-element.142.mine_ref, f32[256,512]{1,0:T(8,128)S(1)} %collective-permute-done.11.theirs_ref, f32[256,128]{1,0:T(8,128)S(1)} %get-tuple-element.143.cosine_ref, f32[256,128]{1,0:T(8,128)S(1)} %get-tuple-element.144.sine_ref, ...), custom_call_target="tpu_custom_call" | custom-call | tf_op jit(solution)/shard_map/attend/pallas_call | solution.py:447
  71.2 5.5 %collective-permute-start.27 = (f32[256,640]{1,0:T(8,128)S(1)}, f32[256,640]{1,0:T(8,128)S(1)}, u32[]{:S(2)}, u32[]{:S(2)}) collective-permute-start(f32[256,640]{1,0:T(8,128)S(1)} %attend.1.mine_ref), channel_id=1, source_target_pairs={{0,2},{2,0},{4,6},{6,4},{8,10},{10,8},{12,14},{14,12},{16,18},{18,... | collective-permute-start | bytes 1966088 | tf_op jit(solution)/shard_map/ppermute | solution.py:466
  76.7 1.7 %collective-permute-done.27.theirs_ref = f32[256,640]{1,0:T(8,128)S(1)} collective-permute-done((f32[256,640]{1,0:T(8,128)S(1)}, f32[256,640]{1,0:T(8,128)S(1)}, u32[]{:S(2)}, u32[]{:S(2)}) %collective-permute-start.27) | collective-permute-done | bytes 655392 | tf_op jit(solution)/shard_map/ppermute | solution.py:466
  81.9 1.5 %collective-permute-start.28 = (bf16[256,256]{1,0:T(8,128)(2,1)S(1)}, bf16[256,256]{1,0:T(8,128)(2,1)S(1)}, u32[]{:S(2)}, u32[]{:S(2)}) collective-permute-start(bf16[256,256]{1,0:T(8,128)(2,1)S(1)} %slice.22), channel_id=1, source_target_pairs={{0,8},{2,10},{8,16},{10,18},{16,24},{18,26},{24,28},{26,30},{28,20... | collective-permute-start | bytes 393224 | tf_op jit(solution)/shard_map/ppermute | solution.py:337
  83.4 3.0 %collective-permute-done.29.refs_1_ = bf16[256,256]{1,0:T(8,128)(2,1)S(1)} collective-permute-done((bf16[256,256]{1,0:T(8,128)(2,1)S(1)}, bf16[256,256]{1,0:T(8,128)(2,1)S(1)}, u32[]{:S(2)}, u32[]{:S(2)}) %collective-permute-start.29) | collective-permute-done | bytes 131104 | tf_op jit(solution)/shard_map/ppermute | solution.py:338
  88.5 1.6 %collective-permute-start.34 = (bf16[1,64,256]{2,1,0:T(8,128)(2,1)S(1)}, bf16[1,64,256]{2,1,0:T(8,128)(2,1)S(1)}, u32[]{:S(2)}, u32[]{:S(2)}) collective-permute-start(bf16[1,64,256]{2,1,0:T(8,128)(2,1)S(1)} %get-tuple-element.205), channel_id=1, source_target_pairs={{0,2},{1,3},{2,0},{3,1},{4,6},{5,7},{6,4},{7,5},{8,10},{9,11},{10,... | collective-permute-start | bytes 98312 | tf_op jit(solution)/shard_map/ppermute | solution.py:488
  90.1 1.7 %collective-permute-done.33.refs_5_ = bf16[1,64,256]{2,1,0:T(8,128)(2,1)S(1)} collective-permute-done((bf16[1,64,256]{2,1,0:T(8,128)(2,1)S(1)}, bf16[1,64,256]{2,1,0:T(8,128)(2,1)S(1)}, u32[]{:S(2)}, u32[]{:S(2)}) %collective-permute-start.33) | collective-permute-done | bytes 32800 | tf_op jit(solution)/shard_map/ppermute | solution.py:488
  91.9 2.6 %collective-permute-start.35 = (bf16[1,64,256]{2,1,0:T(8,128)(2,1)S(1)}, bf16[1,64,256]{2,1,0:T(8,128)(2,1)S(1)}, u32[]{:S(2)}, u32[]{:S(2)}) collective-permute-start(bf16[1,64,256]{2,1,0:T(8,128)(2,1)S(1)} %get-tuple-element.206), channel_id=1, source_target_pairs={{0,3},{1,2},{2,1},{3,0},{4,7},{5,6},{6,5},{7,4},{8,11},{9,10},{10,... | collective-permute-start | bytes 98312 | tf_op jit(solution)/shard_map/ppermute | solution.py:488
  94.5 2.2 %collective-permute-done.35.refs_7_ = bf16[1,64,256]{2,1,0:T(8,128)(2,1)S(1)} collective-permute-done((bf16[1,64,256]{2,1,0:T(8,128)(2,1)S(1)}, bf16[1,64,256]{2,1,0:T(8,128)(2,1)S(1)}, u32[]{:S(2)}, u32[]{:S(2)}) %collective-permute-start.35) | collective-permute-done | bytes 32800 | tf_op jit(solution)/shard_map/ppermute | solution.py:488
  (76 shorter events, 29.0 us)
Async XLA Ops:
  0.0 11.1 %collective-permute-start = (bf16[256,768]{1,0:T(8,128)(2,1)}, bf16[256,768]{1,0:T(8,128)(2,1)S(1)}, u32[]{:S(2)}, u32[]{:S(2)}) collective-permute-start(bf16[256,768]{1,0:T(8,128)(2,1)} %refs_4_), channel_id=1, source_target_pairs={{0,8},{2,10},{8,16},{10,18},{16,24},{18,26},{24,28},{26,30},{28,20... | collective-permute-start | bytes 1179656 | tf_op jit(solution)/shard_map/ppermute | solution.py:332
  2.1 9.9 %collective-permute-start.1 = (bf16[256,768]{1,0:T(8,128)(2,1)}, bf16[256,768]{1,0:T(8,128)(2,1)S(1)}, u32[]{:S(2)}, u32[]{:S(2)}) collective-permute-start(bf16[256,768]{1,0:T(8,128)(2,1)} %refs_4_), channel_id=1, source_target_pairs={{8,0},{10,2},{16,8},{18,10},{24,16},{26,18},{28,24},{30,26},{20,28... | collective-permute-start | bytes 1179656 | tf_op jit(solution)/shard_map/ppermute | solution.py:333
  4.2 12.5 %collective-permute-start.6 = (bf16[2,8,64,256]{3,2,1,0:T(8,128)(2,1)S(1)}, bf16[2,8,64,256]{3,2,1,0:T(8,128)(2,1)S(1)}, u32[]{:S(2)}, u32[]{:S(2)}) collective-permute-start(bf16[2,8,64,256]{3,2,1,0:T(8,128)(2,1)S(1)} %norm.1.refs_0_), channel_id=1, source_target_pairs={{0,1},{1,0},{2,3},{3,2},{4,5},{5,4},{6,7},{7,6},{8,9},{9,8},{10,11... | collective-permute-start | bytes 1572872 | tf_op jit(solution)/shard_map/ppermute | solution.py:394
  12.0 8.7 %collective-permute-start.2 = (bf16[256,768]{1,0:T(8,128)(2,1)S(1)}, bf16[256,768]{1,0:T(8,128)(2,1)S(1)}, u32[]{:S(2)}, u32[]{:S(2)}) collective-permute-start(bf16[256,768]{1,0:T(8,128)(2,1)S(1)} %collective-permute-done.refs_12_), channel_id=1, source_target_pairs={{0,8},{2,10},{8,16},{10,18},{16,24},{18,26},{24,28},{26,30},{28,20... | collective-permute-start | bytes 1179656 | tf_op jit(solution)/shard_map/ppermute | solution.py:332
  13.3 8.5 %collective-permute-start.3 = (bf16[256,768]{1,0:T(8,128)(2,1)S(1)}, bf16[256,768]{1,0:T(8,128)(2,1)S(1)}, u32[]{:S(2)}, u32[]{:S(2)}) collective-permute-start(bf16[256,768]{1,0:T(8,128)(2,1)S(1)} %collective-permute-done.1.refs_5_), channel_id=1, source_target_pairs={{8,0},{10,2},{16,8},{18,10},{24,16},{26,18},{28,24},{30,26},{20,28... | collective-permute-start | bytes 1179656 | tf_op jit(solution)/shard_map/ppermute | solution.py:333
  13.5 9.8 %collective-permute-start.7 = (bf16[2,8,64,256]{3,2,1,0:T(8,128)(2,1)S(1)}, bf16[2,8,64,256]{3,2,1,0:T(8,128)(2,1)S(1)}, u32[]{:S(2)}, u32[]{:S(2)}) collective-permute-start(bf16[2,8,64,256]{3,2,1,0:T(8,128)(2,1)S(1)} %norm.1.refs_0_), channel_id=1, source_target_pairs={{0,2},{2,0},{4,6},{6,4},{8,10},{10,8},{12,14},{14,12},{16,18},{18,... | collective-permute-start | bytes 1572872 | tf_op jit(solution)/shard_map/ppermute | solution.py:399
  16.7 6.5 %collective-permute-start.8 = (bf16[2,8,64,256]{3,2,1,0:T(8,128)(2,1)S(1)}, bf16[2,8,64,256]{3,2,1,0:T(8,128)(2,1)S(1)}, u32[]{:S(2)}, u32[]{:S(2)}) collective-permute-start(bf16[2,8,64,256]{3,2,1,0:T(8,128)(2,1)S(1)} %collective-permute-done.6.refs_1_), channel_id=1, source_target_pairs={{0,2},{2,0},{4,6},{6,4},{8,10},{10,8},{12,14},{14,12},{16,18},{18,... | collective-permute-start | bytes 1572872 | tf_op jit(solution)/shard_map/ppermute | solution.py:399
  21.8 7.5 %collective-permute-start.4 = (bf16[256,768]{1,0:T(8,128)(2,1)S(1)}, bf16[256,768]{1,0:T(8,128)(2,1)S(1)}, u32[]{:S(2)}, u32[]{:S(2)}) collective-permute-start(bf16[256,768]{1,0:T(8,128)(2,1)S(1)} %collective-permute-done.2.refs_11_), channel_id=1, source_target_pairs={{0,8},{2,10},{8,16},{10,18},{16,24},{18,26},{24,28},{26,30},{28,20... | collective-permute-start | bytes 1179656 | tf_op jit(solution)/shard_map/ppermute | solution.py:332
  23.1 7.3 %collective-permute-start.5 = (bf16[256,768]{1,0:T(8,128)(2,1)S(1)}, bf16[256,768]{1,0:T(8,128)(2,1)S(1)}, u32[]{:S(2)}, u32[]{:S(2)}) collective-permute-start(bf16[256,768]{1,0:T(8,128)(2,1)S(1)} %collective-permute-done.3.refs_6_), channel_id=1, source_target_pairs={{8,0},{10,2},{16,8},{18,10},{24,16},{26,18},{28,24},{30,26},{20,28... | collective-permute-start | bytes 1179656 | tf_op jit(solution)/shard_map/ppermute | solution.py:333
  31.9 12.1 %collective-permute-start.13 = (bf16[512,256]{1,0:T(8,128)(2,1)S(1)}, bf16[512,256]{1,0:T(8,128)(2,1)S(1)}, u32[]{:S(2)}, u32[]{:S(2)}) collective-permute-start(bf16[512,256]{1,0:T(8,128)(2,1)S(1)} %copy-done.2), channel_id=1, source_target_pairs={{0,8},{2,10},{8,16},{10,18},{16,24},{18,26},{24,28},{26,30},{28,20... | collective-permute-start | bytes 786440 | tf_op jit(solution)/shard_map/ppermute | solution.py:332
  33.1 10.8 %collective-permute-start.14 = (bf16[512,256]{1,0:T(8,128)(2,1)S(1)}, bf16[512,256]{1,0:T(8,128)(2,1)S(1)}, u32[]{:S(2)}, u32[]{:S(2)}) collective-permute-start(bf16[512,256]{1,0:T(8,128)(2,1)S(1)} %copy-done.2), channel_id=1, source_target_pairs={{8,0},{10,2},{16,8},{18,10},{24,16},{26,18},{28,24},{30,26},{20,28... | collective-permute-start | bytes 786440 | tf_op jit(solution)/shard_map/ppermute | solution.py:333
  37.1 6.8 %collective-permute-start.12 = (f32[128,256]{1,0:T(8,128)S(1)}, f32[128,256]{1,0:T(8,128)S(1)}, u32[]{:S(2)}, u32[]{:S(2)}) collective-permute-start(f32[128,256]{1,0:T(8,128)S(1)} %get-tuple-element.149), channel_id=1, source_target_pairs={{0,2},{2,0},{4,6},{6,4},{8,10},{10,8},{12,14},{14,12},{16,18},{18,... | collective-permute-start | bytes 393224 | tf_op jit(solution)/shard_map/ppermute | solution.py:425
  44.0 9.6 %collective-permute-start.19 = (bf16[512,256]{1,0:T(8,128)(2,1)S(1)}, bf16[512,256]{1,0:T(8,128)(2,1)S(1)}, u32[]{:S(2)}, u32[]{:S(2)}) collective-permute-start(bf16[512,256]{1,0:T(8,128)(2,1)S(1)} %collective-permute-done.13.refs_2_), channel_id=1, source_target_pairs={{0,8},{2,10},{8,16},{10,18},{16,24},{18,26},{24,28},{26,30},{28,20... | collective-permute-start | bytes 786440 | tf_op jit(solution)/shard_map/ppermute | solution.py:332
  45.3 8.3 %collective-permute-start.20 = (bf16[512,256]{1,0:T(8,128)(2,1)S(1)}, bf16[512,256]{1,0:T(8,128)(2,1)S(1)}, u32[]{:S(2)}, u32[]{:S(2)}) collective-permute-start(bf16[512,256]{1,0:T(8,128)(2,1)S(1)} %collective-permute-done.14.refs_4_), channel_id=1, source_target_pairs={{8,0},{10,2},{16,8},{18,10},{24,16},{26,18},{28,24},{30,26},{20,28... | collective-permute-start | bytes 786440 | tf_op jit(solution)/shard_map/ppermute | solution.py:333
  45.4 23.1 %collective-permute-start.11 = (f32[256,512]{1,0:T(8,128)S(1)}, f32[256,512]{1,0:T(8,128)S(1)}, u32[]{:S(2)}, u32[]{:S(2)}) collective-permute-start(f32[256,512]{1,0:T(8,128)S(1)} %get-tuple-element.142.mine_ref), channel_id=1, source_target_pairs={{0,2},{2,0},{4,6},{6,4},{8,10},{10,8},{12,14},{14,12},{16,18},{18,... | collective-permute-start | bytes 1572872 | tf_op jit(solution)/shard_map/ppermute | solution.py:426
  53.5 13.2 %collective-permute-start.25 = (bf16[512,256]{1,0:T(8,128)(2,1)S(1)}, bf16[512,256]{1,0:T(8,128)(2,1)S(1)}, u32[]{:S(2)}, u32[]{:S(2)}) collective-permute-start(bf16[512,256]{1,0:T(8,128)(2,1)S(1)} %collective-permute-done.19.refs_1_), channel_id=1, source_target_pairs={{0,8},{2,10},{8,16},{10,18},{16,24},{18,26},{24,28},{26,30},{28,20... | collective-permute-start | bytes 786440 | tf_op jit(solution)/shard_map/ppermute | solution.py:332
  54.8 11.9 %collective-permute-start.26 = (bf16[512,256]{1,0:T(8,128)(2,1)S(1)}, bf16[512,256]{1,0:T(8,128)(2,1)S(1)}, u32[]{:S(2)}, u32[]{:S(2)}) collective-permute-start(bf16[512,256]{1,0:T(8,128)(2,1)S(1)} %collective-permute-done.20.refs_5_), channel_id=1, source_target_pairs={{8,0},{10,2},{16,8},{18,10},{24,16},{26,18},{28,24},{30,26},{20,28... | collective-permute-start | bytes 786440 | tf_op jit(solution)/shard_map/ppermute | solution.py:333
  55.1 6.9 %collective-permute-start.17 = (bf16[128,256]{1,0:T(8,128)(2,1)S(1)}, bf16[128,256]{1,0:T(8,128)(2,1)S(1)}, u32[]{:S(2)}, u32[]{:S(2)}) collective-permute-start(bf16[128,256]{1,0:T(8,128)(2,1)S(1)} %collective-permute-done.15.refs_1_), channel_id=1, source_target_pairs={{8,0},{10,2},{16,8},{18,10},{24,16},{26,18},{28,24},{30,26},{20,28... | collective-permute-start | bytes 196616 | tf_op jit(solution)/shard_map/ppermute | solution.py:333
  55.1 6.8 %collective-permute-start.18 = (bf16[128,256]{1,0:T(8,128)(2,1)S(1)}, bf16[128,256]{1,0:T(8,128)(2,1)S(1)}, u32[]{:S(2)}, u32[]{:S(2)}) collective-permute-start(bf16[128,256]{1,0:T(8,128)(2,1)S(1)} %collective-permute-done.16.refs_8_), channel_id=1, source_target_pairs={{0,8},{2,10},{8,16},{10,18},{16,24},{18,26},{24,28},{26,30},{28,20... | collective-permute-start | bytes 196616 | tf_op jit(solution)/shard_map/ppermute | solution.py:332
  71.2 7.2 %collective-permute-start.27 = (f32[256,640]{1,0:T(8,128)S(1)}, f32[256,640]{1,0:T(8,128)S(1)}, u32[]{:S(2)}, u32[]{:S(2)}) collective-permute-start(f32[256,640]{1,0:T(8,128)S(1)} %attend.1.mine_ref), channel_id=1, source_target_pairs={{0,2},{2,0},{4,6},{6,4},{8,10},{10,8},{12,14},{14,12},{16,18},{18,... | collective-permute-start | bytes 1966088 | tf_op jit(solution)/shard_map/ppermute | solution.py:466
  79.7 17.0 %collective-permute-start.30 = (bf16[7,64,256]{2,1,0:T(8,128)(2,1)S(1)}, bf16[7,64,256]{2,1,0:T(8,128)(2,1)S(1)}, u32[]{:S(2)}, u32[]{:S(2)}) collective-permute-start(bf16[7,64,256]{2,1,0:T(8,128)(2,1)S(1)} %get-tuple-element.200), channel_id=1, source_target_pairs={{0,1},{1,0},{2,3},{3,2},{4,5},{5,4},{6,7},{7,6},{8,9},{9,8},{10,11... | collective-permute-start | bytes 688136 | tf_op jit(solution)/shard_map/ppermute | solution.py:488
  81.0 15.7 %collective-permute-start.31 = (bf16[7,64,256]{2,1,0:T(8,128)(2,1)S(1)}, bf16[7,64,256]{2,1,0:T(8,128)(2,1)S(1)}, u32[]{:S(2)}, u32[]{:S(2)}) collective-permute-start(bf16[7,64,256]{2,1,0:T(8,128)(2,1)S(1)} %get-tuple-element.201), channel_id=1, source_target_pairs={{0,2},{1,3},{2,0},{3,1},{4,6},{5,7},{6,4},{7,5},{8,10},{9,11},{10,... | collective-permute-start | bytes 688136 | tf_op jit(solution)/shard_map/ppermute | solution.py:488
  81.6 15.0 %collective-permute-start.32 = (bf16[7,64,256]{2,1,0:T(8,128)(2,1)S(1)}, bf16[7,64,256]{2,1,0:T(8,128)(2,1)S(1)}, u32[]{:S(2)}, u32[]{:S(2)}) collective-permute-start(bf16[7,64,256]{2,1,0:T(8,128)(2,1)S(1)} %get-tuple-element.202), channel_id=1, source_target_pairs={{0,3},{1,2},{2,1},{3,0},{4,7},{5,6},{6,5},{7,4},{8,11},{9,10},{10,... | collective-permute-start | bytes 688136 | tf_op jit(solution)/shard_map/ppermute | solution.py:488
  88.5 6.0 %collective-permute-start.34 = (bf16[1,64,256]{2,1,0:T(8,128)(2,1)S(1)}, bf16[1,64,256]{2,1,0:T(8,128)(2,1)S(1)}, u32[]{:S(2)}, u32[]{:S(2)}) collective-permute-start(bf16[1,64,256]{2,1,0:T(8,128)(2,1)S(1)} %get-tuple-element.205), channel_id=1, source_target_pairs={{0,2},{1,3},{2,0},{3,1},{4,6},{5,7},{6,4},{7,5},{8,10},{9,11},{10,... | collective-permute-start | bytes 98312 | tf_op jit(solution)/shard_map/ppermute | solution.py:488
  (19 other events, 117.4 us)

commit v16 on v14

--- a/solution.py
+++ b/solution.py
@@ -381,6 +381,9 @@
     normed += [lax.ppermute(rows, "context", sibling) for rows in normed]
 
     qkv_ring.step()
+    cosine, sine, query_start, query_orig, key_orig = ordered(
+        (cosine, sine, query_start, query_orig, key_orig)
+    )
     qkv_ring.step()
     normed = qkv_ring.step(normed)
     while not qkv_ring.done():
@@ -437,6 +440,8 @@
         key_orig,
         kv,
     )
+    while not out_ring.done():
+        out_ring.step()
     (mixed,) = ordered((mixed,))
     mixed_theirs = lax.ppermute(mixed, "context", sibling)
 
@@ -464,13 +469,9 @@
                 arrived.append(part)
         return arrived
 
-    reach = max(chips // 2 - 2, 0)
-    while len(out_ring.up) <= reach:
-        out_ring.step()
+    reach = (chips - 1) // 2
     near = 2 * reach + 1
     arrived = output(list(range(-reach, reach + 1)), "output_near")
-    while not out_ring.done():
-        out_ring.step()
     arrived += output(list(range(reach + 1, chips - reach)), "output_far")
     return pl.pallas_call(
         functools.partial(sum_kernel, place, chips, groups, near),

time: 95.7 us -> 103 us (1.076)
  starting transfers between devices: 39.8 us -> 45.2 us
    ppermute x2, waiting for transfers between devices: 1.59 us -> 5.72 us  [step(): lax.ppermute(down[half:], 'context', back)]
    ppermute x6, waiting for transfers between devices: 9.32 us -> 5.82 us  [step(): self.down.append(lax.ppermute(down, 'context', back))]
    ppermute x6, starting transfers between devices: 10.3 us -> 12.9 us  [step(): self.up.append(lax.ppermute(up, 'context', ahead))]
    ppermute x1, starting transfers between devices: 1.14 us -> 3.66 us  [per_device(): mixed_theirs = lax.ppermute(mixed, 'context', sibling)]
    ppermute x1, waiting for transfers between devices: 0.01 us -> 1.72 us  [per_device(): mixed_theirs = lax.ppermute(mixed, 'context', sibling)]
    ppermute x2, waiting for transfers between devices: 1.64 us -> 0.01 us  [step(): lax.ppermute(up[:half], 'context', ahead)]
    ppermute x1, starting transfers between devices: 0.64 us -> 2.17 us  [per_device(): queries_theirs = lax.ppermute(queries, 'context', sibling)]
    ppermute x6, waiting for transfers between devices: 26.5 us -> 25.2 us  [step(): self.up.append(lax.ppermute(up, 'context', ahead))]
  transfers between devices with their start and end apart: 29 -> 29, of which waited for: 19 -> 17; matrix products, arithmetic and copies ran while one was open for 0% -> 0% of each run, Pallas kernels for 5% -> 3%
where the time goes in v16:
time: 103 us; the launch traced here: 102 us
  starting transfers between devices  45.2 us (44%)
  waiting for transfers between devices  44.1 us (43%)
  Pallas kernels  10.1 us (10%)
  local copies, waits for them, and re-layouts  2.72 us (3%)
    ppermute x6, waiting for transfers between devices, step(): self.up.append(lax.ppermute(up, 'context', ahead))  25.2 us
    ppermute x6, starting transfers between devices, step(): self.up.append(lax.ppermute(up, 'context', ahead))  12.9 us
    ppermute x6, starting transfers between devices, output(): part = lax.ppermute(part, ('context', 'tensor'), member(e, -d))  7.63 us
    ppermute x1, starting transfers between devices, per_device(): theirs = lax.ppermute(theirs, 'context', sibling)  5.86 us
    ppermute x6, waiting for transfers between devices, step(): self.down.append(lax.ppermute(down, 'context', back))  5.82 us
    ppermute x2, waiting for transfers between devices, step(): lax.ppermute(down[half:], 'context', back)  5.72 us
    ppermute x2, starting transfers between devices, per_device(): normed += [lax.ppermute(rows, 'context', sibling) for rows in normed]  4.3 us
    ppermute x6, waiting for transfers between devices, output(): part = lax.ppermute(part, ('context', 'tensor'), member(e, -d))  3.91 us
  transfers between devices with their start and end apart: 29, of which 17 were waited for; matrix products, arithmetic and copies ran while one was open for 0% of the time, Pallas kernels for 3%

profile of v16, /device:TPU:1, one launch (start us, length us, event | category | flops | bytes accessed | tf_op | source)
XLA Modules:
  0.0 102.3 jit_solution(17171744407323076626)
XLA Ops:
  0.0 2.1 %collective-permute-start = (bf16[256,768]{1,0:T(8,128)(2,1)}, bf16[256,768]{1,0:T(8,128)(2,1)S(1)}, u32[]{:S(2)}, u32[]{:S(2)}) collective-permute-start(bf16[256,768]{1,0:T(8,128)(2,1)} %refs_4_), channel_id=1, source_target_pairs={{0,8},{2,10},{8,16},{10,18},{16,24},{18,26},{24,28},{26,30},{28,20... | collective-permute-start | bytes 1179656 | tf_op jit(solution)/shard_map/ppermute | solution.py:314
  5.6 5.5 %collective-permute-done.refs_12_ = bf16[256,768]{1,0:T(8,128)(2,1)S(1)} collective-permute-done((bf16[256,768]{1,0:T(8,128)(2,1)}, bf16[256,768]{1,0:T(8,128)(2,1)S(1)}, u32[]{:S(2)}, u32[]{:S(2)}) %collective-permute-start) | collective-permute-done | bytes 393248 | tf_op jit(solution)/shard_map/ppermute | solution.py:314
  13.5 2.4 %collective-permute-start.7 = (bf16[2,8,64,256]{3,2,1,0:T(8,128)(2,1)S(1)}, bf16[2,8,64,256]{3,2,1,0:T(8,128)(2,1)S(1)}, u32[]{:S(2)}, u32[]{:S(2)}) collective-permute-start(bf16[2,8,64,256]{3,2,1,0:T(8,128)(2,1)S(1)} %norm.1.refs_0_), channel_id=1, source_target_pairs={{0,2},{2,0},{4,6},{6,4},{8,10},{10,8},{12,14},{14,12},{16,18},{18,... | collective-permute-start | bytes 1572872 | tf_op jit(solution)/shard_map/ppermute | solution.py:381
  16.7 1.9 %collective-permute-start.8 = (bf16[2,8,64,256]{3,2,1,0:T(8,128)(2,1)S(1)}, bf16[2,8,64,256]{3,2,1,0:T(8,128)(2,1)S(1)}, u32[]{:S(2)}, u32[]{:S(2)}) collective-permute-start(bf16[2,8,64,256]{3,2,1,0:T(8,128)(2,1)S(1)} %collective-permute-done.6.refs_1_), channel_id=1, source_target_pairs={{0,2},{2,0},{4,6},{6,4},{8,10},{10,8},{12,14},{14,12},{16,18},{18,... | collective-permute-start | bytes 1572872 | tf_op jit(solution)/shard_map/ppermute | solution.py:381
  23.2 6.1 %collective-permute-done.4.refs_10_ = bf16[256,768]{1,0:T(8,128)(2,1)S(1)} collective-permute-done((bf16[256,768]{1,0:T(8,128)(2,1)S(1)}, bf16[256,768]{1,0:T(8,128)(2,1)S(1)}, u32[]{:S(2)}, u32[]{:S(2)}) %collective-permute-start.4) | collective-permute-done | bytes 393248 | tf_op jit(solution)/shard_map/ppermute | solution.py:314
  33.4 2.6 %collective-permute-done.10.refs_9_ = bf16[128,768]{1,0:T(8,128)(2,1)S(1)} collective-permute-done((bf16[128,768]{1,0:T(8,128)(2,1)S(1)}, bf16[128,768]{1,0:T(8,128)(2,1)S(1)}, u32[]{:S(2)}, u32[]{:S(2)}) %collective-permute-start.10) | collective-permute-done | bytes 196640 | tf_op jit(solution)/shard_map/ppermute | solution.py:320
  37.1 5.9 %collective-permute-start.12 = (f32[128,256]{1,0:T(8,128)S(1)}, f32[128,256]{1,0:T(8,128)S(1)}, u32[]{:S(2)}, u32[]{:S(2)}) collective-permute-start(f32[128,256]{1,0:T(8,128)S(1)} %get-tuple-element.131), channel_id=1, source_target_pairs={{0,2},{2,0},{4,6},{6,4},{8,10},{10,8},{12,14},{14,12},{16,18},{18,... | collective-permute-start | bytes 393224 | tf_op jit(solution)/shard_map/ppermute | solution.py:407
  44.9 3.6 %all-to-all-start = ((bf16[8,128,256]{2,1,0:T(8,128)(2,1)}), bf16[8,128,256]{2,1,0:T(8,128)(2,1)S(1)}, u32[]{:S(2)}, u32[]{:S(2)}) async-start(bf16[8,128,256]{2,1,0:T(8,128)(2,1)} %bitcast.1), calls=%async_computation | async-start | bytes 1048576 | tf_op jit(solution)/shard_map/all_to_all | solution.py:420
  48.4 1.5 %collective-permute-start.15 = (bf16[512,256]{1,0:T(8,128)(2,1)S(1)}, bf16[512,256]{1,0:T(8,128)(2,1)S(1)}, u32[]{:S(2)}, u32[]{:S(2)}) collective-permute-start(bf16[512,256]{1,0:T(8,128)(2,1)S(1)} %collective-permute-done.13.refs_2_), channel_id=1, source_target_pairs={{0,8},{2,10},{8,16},{10,18},{16,24},{18,26},{24,28},{26,30},{28,20... | collective-permute-start | bytes 786440 | tf_op jit(solution)/shard_map/ppermute | solution.py:314
  49.9 2.2 %collective-permute-start.11 = (f32[256,512]{1,0:T(8,128)S(1)}, f32[256,512]{1,0:T(8,128)S(1)}, u32[]{:S(2)}, u32[]{:S(2)}) collective-permute-start(f32[256,512]{1,0:T(8,128)S(1)} %get-tuple-element.124.mine_ref), channel_id=1, source_target_pairs={{0,2},{2,0},{4,6},{6,4},{8,10},{10,8},{12,14},{14,12},{16,18},{18,... | collective-permute-start | bytes 1572872 | tf_op jit(solution)/shard_map/ppermute | solution.py:408
  52.1 9.4 %collective-permute-done.15.refs_1_ = bf16[512,256]{1,0:T(8,128)(2,1)S(1)} collective-permute-done((bf16[512,256]{1,0:T(8,128)(2,1)S(1)}, bf16[512,256]{1,0:T(8,128)(2,1)S(1)}, u32[]{:S(2)}, u32[]{:S(2)}) %collective-permute-start.15) | collective-permute-done | bytes 262176 | tf_op jit(solution)/shard_map/ppermute | solution.py:314
  62.3 5.5 %collective-permute-start.17 = (bf16[512,256]{1,0:T(8,128)(2,1)S(1)}, bf16[512,256]{1,0:T(8,128)(2,1)S(1)}, u32[]{:S(2)}, u32[]{:S(2)}) collective-permute-start(bf16[512,256]{1,0:T(8,128)(2,1)S(1)} %collective-permute-done.15.refs_1_), channel_id=1, source_target_pairs={{0,8},{2,10},{8,16},{10,18},{16,24},{18,26},{24,28},{26,30},{28,20... | collective-permute-start | bytes 786440 | tf_op jit(solution)/shard_map/ppermute | solution.py:314
  67.8 3.3 %collective-permute-done.17.refs_0_ = bf16[512,256]{1,0:T(8,128)(2,1)S(1)} collective-permute-done((bf16[512,256]{1,0:T(8,128)(2,1)S(1)}, bf16[512,256]{1,0:T(8,128)(2,1)S(1)}, u32[]{:S(2)}, u32[]{:S(2)}) %collective-permute-start.17) | collective-permute-done | bytes 262176 | tf_op jit(solution)/shard_map/ppermute | solution.py:314
  71.1 2.1 %collective-permute-done.18.refs_6_ = bf16[512,256]{1,0:T(8,128)(2,1)S(1)} collective-permute-done((bf16[512,256]{1,0:T(8,128)(2,1)}, bf16[512,256]{1,0:T(8,128)(2,1)S(1)}, u32[]{:S(2)}, u32[]{:S(2)}) %collective-permute-start.18) | collective-permute-done | bytes 262176 | tf_op jit(solution)/shard_map/ppermute | solution.py:315
  74.1 2.5 %attend.1.mine_ref = f32[256,640]{1,0:T(8,128)S(1)} custom-call(f32[256,512]{1,0:T(8,128)S(1)} %get-tuple-element.124.mine_ref, f32[256,512]{1,0:T(8,128)S(1)} %collective-permute-done.11.theirs_ref, f32[256,128]{1,0:T(8,128)S(1)} %get-tuple-element.125.cosine_ref, f32[256,128]{1,0:T(8,128)S(1)} %get-tuple-element.126.sine_ref, ...), custom_call_target="tpu_custom_call" | custom-call | tf_op jit(solution)/shard_map/attend/pallas_call | solution.py:426
  76.6 3.7 %collective-permute-start.19 = (f32[256,640]{1,0:T(8,128)S(1)}, f32[256,640]{1,0:T(8,128)S(1)}, u32[]{:S(2)}, u32[]{:S(2)}) collective-permute-start(f32[256,640]{1,0:T(8,128)S(1)} %attend.1.mine_ref), channel_id=1, source_target_pairs={{0,2},{2,0},{4,6},{6,4},{8,10},{10,8},{12,14},{14,12},{16,18},{18,... | collective-permute-start | bytes 1966088 | tf_op jit(solution)/shard_map/ppermute | solution.py:446
  80.3 1.7 %collective-permute-done.19.theirs_ref = f32[256,640]{1,0:T(8,128)S(1)} collective-permute-done((f32[256,640]{1,0:T(8,128)S(1)}, f32[256,640]{1,0:T(8,128)S(1)}, u32[]{:S(2)}, u32[]{:S(2)}) %collective-permute-start.19) | collective-permute-done | bytes 655392 | tf_op jit(solution)/shard_map/ppermute | solution.py:446
  82.0 2.2 %output_near.1 = (bf16[7,64,256]{2,1,0:T(8,128)(2,1)S(1)}, bf16[7,64,256]{2,1,0:T(8,128)(2,1)S(1)}, bf16[7,64,256]{2,1,0:T(8,128)(2,1)S(1)}, bf16[7,64,256]{2,1,0:T(8,128)(2,1)S(1)}) custom-call(f32[256,640]{1,0:T(8,128)S(1)} %attend.1.mine_ref, f32[256,640]{1,0:T(8,128)S(1)} %collective-permute-done.19.theirs_ref, ...), custom_call_target="tpu_custom_call" | custom-call | tf_op jit(solution)/shard_map/output_near/pallas_call | solution.py:453
  86.4 1.5 %collective-permute-start.20 = (bf16[256,256]{1,0:T(8,128)(2,1)S(1)}, bf16[256,256]{1,0:T(8,128)(2,1)S(1)}, u32[]{:S(2)}, u32[]{:S(2)}) collective-permute-start(bf16[256,256]{1,0:T(8,128)(2,1)S(1)} %slice.14), channel_id=1, source_target_pairs={{0,8},{2,10},{8,16},{10,18},{16,24},{18,26},{24,28},{26,30},{28,20... | collective-permute-start | bytes 393224 | tf_op jit(solution)/shard_map/ppermute | solution.py:319
  87.9 3.1 %collective-permute-done.21.refs_1_ = bf16[256,256]{1,0:T(8,128)(2,1)S(1)} collective-permute-done((bf16[256,256]{1,0:T(8,128)(2,1)S(1)}, bf16[256,256]{1,0:T(8,128)(2,1)S(1)}, u32[]{:S(2)}, u32[]{:S(2)}) %collective-permute-start.21) | collective-permute-done | bytes 131104 | tf_op jit(solution)/shard_map/ppermute | solution.py:320
  93.0 1.7 %collective-permute-start.26 = (bf16[1,64,256]{2,1,0:T(8,128)(2,1)S(1)}, bf16[1,64,256]{2,1,0:T(8,128)(2,1)S(1)}, u32[]{:S(2)}, u32[]{:S(2)}) collective-permute-start(bf16[1,64,256]{2,1,0:T(8,128)(2,1)S(1)} %get-tuple-element.169), channel_id=1, source_target_pairs={{0,2},{1,3},{2,0},{3,1},{4,6},{5,7},{6,4},{7,5},{8,10},{9,11},{10,... | collective-permute-start | bytes 98312 | tf_op jit(solution)/shard_map/ppermute | solution.py:468
  94.7 1.7 %collective-permute-done.25.refs_5_ = bf16[1,64,256]{2,1,0:T(8,128)(2,1)S(1)} collective-permute-done((bf16[1,64,256]{2,1,0:T(8,128)(2,1)S(1)}, bf16[1,64,256]{2,1,0:T(8,128)(2,1)S(1)}, u32[]{:S(2)}, u32[]{:S(2)}) %collective-permute-start.25) | collective-permute-done | bytes 32800 | tf_op jit(solution)/shard_map/ppermute | solution.py:468
  96.5 2.6 %collective-permute-start.27 = (bf16[1,64,256]{2,1,0:T(8,128)(2,1)S(1)}, bf16[1,64,256]{2,1,0:T(8,128)(2,1)S(1)}, u32[]{:S(2)}, u32[]{:S(2)}) collective-permute-start(bf16[1,64,256]{2,1,0:T(8,128)(2,1)S(1)} %get-tuple-element.170), channel_id=1, source_target_pairs={{0,3},{1,2},{2,1},{3,0},{4,7},{5,6},{6,5},{7,4},{8,11},{9,10},{10,... | collective-permute-start | bytes 98312 | tf_op jit(solution)/shard_map/ppermute | solution.py:468
  99.1 2.2 %collective-permute-done.27.refs_7_ = bf16[1,64,256]{2,1,0:T(8,128)(2,1)S(1)} collective-permute-done((bf16[1,64,256]{2,1,0:T(8,128)(2,1)S(1)}, bf16[1,64,256]{2,1,0:T(8,128)(2,1)S(1)}, u32[]{:S(2)}, u32[]{:S(2)}) %collective-permute-start.27) | collective-permute-done | bytes 32800 | tf_op jit(solution)/shard_map/ppermute | solution.py:468
  (64 shorter events, 25.3 us)
Async XLA Ops:
  0.0 11.1 %collective-permute-start = (bf16[256,768]{1,0:T(8,128)(2,1)}, bf16[256,768]{1,0:T(8,128)(2,1)S(1)}, u32[]{:S(2)}, u32[]{:S(2)}) collective-permute-start(bf16[256,768]{1,0:T(8,128)(2,1)} %refs_4_), channel_id=1, source_target_pairs={{0,8},{2,10},{8,16},{10,18},{16,24},{18,26},{24,28},{26,30},{28,20... | collective-permute-start | bytes 1179656 | tf_op jit(solution)/shard_map/ppermute | solution.py:314
  2.1 9.9 %collective-permute-start.1 = (bf16[256,768]{1,0:T(8,128)(2,1)}, bf16[256,768]{1,0:T(8,128)(2,1)S(1)}, u32[]{:S(2)}, u32[]{:S(2)}) collective-permute-start(bf16[256,768]{1,0:T(8,128)(2,1)} %refs_4_), channel_id=1, source_target_pairs={{8,0},{10,2},{16,8},{18,10},{24,16},{26,18},{28,24},{30,26},{20,28... | collective-permute-start | bytes 1179656 | tf_op jit(solution)/shard_map/ppermute | solution.py:315
  4.2 12.5 %collective-permute-start.6 = (bf16[2,8,64,256]{3,2,1,0:T(8,128)(2,1)S(1)}, bf16[2,8,64,256]{3,2,1,0:T(8,128)(2,1)S(1)}, u32[]{:S(2)}, u32[]{:S(2)}) collective-permute-start(bf16[2,8,64,256]{3,2,1,0:T(8,128)(2,1)S(1)} %norm.1.refs_0_), channel_id=1, source_target_pairs={{0,1},{1,0},{2,3},{3,2},{4,5},{5,4},{6,7},{7,6},{8,9},{9,8},{10,11... | collective-permute-start | bytes 1572872 | tf_op jit(solution)/shard_map/ppermute | solution.py:376
  12.0 8.7 %collective-permute-start.2 = (bf16[256,768]{1,0:T(8,128)(2,1)S(1)}, bf16[256,768]{1,0:T(8,128)(2,1)S(1)}, u32[]{:S(2)}, u32[]{:S(2)}) collective-permute-start(bf16[256,768]{1,0:T(8,128)(2,1)S(1)} %collective-permute-done.refs_12_), channel_id=1, source_target_pairs={{0,8},{2,10},{8,16},{10,18},{16,24},{18,26},{24,28},{26,30},{28,20... | collective-permute-start | bytes 1179656 | tf_op jit(solution)/shard_map/ppermute | solution.py:314
  13.3 8.5 %collective-permute-start.3 = (bf16[256,768]{1,0:T(8,128)(2,1)S(1)}, bf16[256,768]{1,0:T(8,128)(2,1)S(1)}, u32[]{:S(2)}, u32[]{:S(2)}) collective-permute-start(bf16[256,768]{1,0:T(8,128)(2,1)S(1)} %collective-permute-done.1.refs_5_), channel_id=1, source_target_pairs={{8,0},{10,2},{16,8},{18,10},{24,16},{26,18},{28,24},{30,26},{20,28... | collective-permute-start | bytes 1179656 | tf_op jit(solution)/shard_map/ppermute | solution.py:315
  13.5 9.8 %collective-permute-start.7 = (bf16[2,8,64,256]{3,2,1,0:T(8,128)(2,1)S(1)}, bf16[2,8,64,256]{3,2,1,0:T(8,128)(2,1)S(1)}, u32[]{:S(2)}, u32[]{:S(2)}) collective-permute-start(bf16[2,8,64,256]{3,2,1,0:T(8,128)(2,1)S(1)} %norm.1.refs_0_), channel_id=1, source_target_pairs={{0,2},{2,0},{4,6},{6,4},{8,10},{10,8},{12,14},{14,12},{16,18},{18,... | collective-permute-start | bytes 1572872 | tf_op jit(solution)/shard_map/ppermute | solution.py:381
  16.7 6.5 %collective-permute-start.8 = (bf16[2,8,64,256]{3,2,1,0:T(8,128)(2,1)S(1)}, bf16[2,8,64,256]{3,2,1,0:T(8,128)(2,1)S(1)}, u32[]{:S(2)}, u32[]{:S(2)}) collective-permute-start(bf16[2,8,64,256]{3,2,1,0:T(8,128)(2,1)S(1)} %collective-permute-done.6.refs_1_), channel_id=1, source_target_pairs={{0,2},{2,0},{4,6},{6,4},{8,10},{10,8},{12,14},{14,12},{16,18},{18,... | collective-permute-start | bytes 1572872 | tf_op jit(solution)/shard_map/ppermute | solution.py:381
  21.8 7.5 %collective-permute-start.4 = (bf16[256,768]{1,0:T(8,128)(2,1)S(1)}, bf16[256,768]{1,0:T(8,128)(2,1)S(1)}, u32[]{:S(2)}, u32[]{:S(2)}) collective-permute-start(bf16[256,768]{1,0:T(8,128)(2,1)S(1)} %collective-permute-done.2.refs_11_), channel_id=1, source_target_pairs={{0,8},{2,10},{8,16},{10,18},{16,24},{18,26},{24,28},{26,30},{28,20... | collective-permute-start | bytes 1179656 | tf_op jit(solution)/shard_map/ppermute | solution.py:314
  23.1 7.3 %collective-permute-start.5 = (bf16[256,768]{1,0:T(8,128)(2,1)S(1)}, bf16[256,768]{1,0:T(8,128)(2,1)S(1)}, u32[]{:S(2)}, u32[]{:S(2)}) collective-permute-start(bf16[256,768]{1,0:T(8,128)(2,1)S(1)} %collective-permute-done.3.refs_6_), channel_id=1, source_target_pairs={{8,0},{10,2},{16,8},{18,10},{24,16},{26,18},{28,24},{30,26},{20,28... | collective-permute-start | bytes 1179656 | tf_op jit(solution)/shard_map/ppermute | solution.py:315
  30.4 5.6 %collective-permute-start.10 = (bf16[128,768]{1,0:T(8,128)(2,1)S(1)}, bf16[128,768]{1,0:T(8,128)(2,1)S(1)}, u32[]{:S(2)}, u32[]{:S(2)}) collective-permute-start(bf16[128,768]{1,0:T(8,128)(2,1)S(1)} %slice.13), channel_id=1, source_target_pairs={{8,0},{10,2},{16,8},{18,10},{24,16},{26,18},{28,24},{30,26},{20,28... | collective-permute-start | bytes 589832 | tf_op jit(solution)/shard_map/ppermute | solution.py:320
  30.6 5.4 %collective-permute-start.9 = (bf16[128,768]{1,0:T(8,128)(2,1)S(1)}, bf16[128,768]{1,0:T(8,128)(2,1)S(1)}, u32[]{:S(2)}, u32[]{:S(2)}) collective-permute-start(bf16[128,768]{1,0:T(8,128)(2,1)S(1)} %slice.12), channel_id=1, source_target_pairs={{0,8},{2,10},{8,16},{10,18},{16,24},{18,26},{24,28},{26,30},{28,20... | collective-permute-start | bytes 589832 | tf_op jit(solution)/shard_map/ppermute | solution.py:319
  31.9 11.1 %collective-permute-start.13 = (bf16[512,256]{1,0:T(8,128)(2,1)S(1)}, bf16[512,256]{1,0:T(8,128)(2,1)S(1)}, u32[]{:S(2)}, u32[]{:S(2)}) collective-permute-start(bf16[512,256]{1,0:T(8,128)(2,1)S(1)} %copy-done.2), channel_id=1, source_target_pairs={{0,8},{2,10},{8,16},{10,18},{16,24},{18,26},{24,28},{26,30},{28,20... | collective-permute-start | bytes 786440 | tf_op jit(solution)/shard_map/ppermute | solution.py:314
  33.1 9.8 %collective-permute-start.14 = (bf16[512,256]{1,0:T(8,128)(2,1)S(1)}, bf16[512,256]{1,0:T(8,128)(2,1)S(1)}, u32[]{:S(2)}, u32[]{:S(2)}) collective-permute-start(bf16[512,256]{1,0:T(8,128)(2,1)S(1)} %copy-done.2), channel_id=1, source_target_pairs={{8,0},{10,2},{16,8},{18,10},{24,16},{26,18},{28,24},{30,26},{20,28... | collective-permute-start | bytes 786440 | tf_op jit(solution)/shard_map/ppermute | solution.py:315
  37.1 6.8 %collective-permute-start.12 = (f32[128,256]{1,0:T(8,128)S(1)}, f32[128,256]{1,0:T(8,128)S(1)}, u32[]{:S(2)}, u32[]{:S(2)}) collective-permute-start(f32[128,256]{1,0:T(8,128)S(1)} %get-tuple-element.131), channel_id=1, source_target_pairs={{0,2},{2,0},{4,6},{6,4},{8,10},{10,8},{12,14},{14,12},{16,18},{18,... | collective-permute-start | bytes 393224 | tf_op jit(solution)/shard_map/ppermute | solution.py:407
  44.9 22.9 %all-to-all-start = ((bf16[8,128,256]{2,1,0:T(8,128)(2,1)}), bf16[8,128,256]{2,1,0:T(8,128)(2,1)S(1)}, u32[]{:S(2)}, u32[]{:S(2)}) async-start(bf16[8,128,256]{2,1,0:T(8,128)(2,1)} %bitcast.1), calls=%async_computation | async-start | bytes 1048576 | tf_op jit(solution)/shard_map/all_to_all | solution.py:420
  48.4 13.1 %collective-permute-start.15 = (bf16[512,256]{1,0:T(8,128)(2,1)S(1)}, bf16[512,256]{1,0:T(8,128)(2,1)S(1)}, u32[]{:S(2)}, u32[]{:S(2)}) collective-permute-start(bf16[512,256]{1,0:T(8,128)(2,1)S(1)} %collective-permute-done.13.refs_2_), channel_id=1, source_target_pairs={{0,8},{2,10},{8,16},{10,18},{16,24},{18,26},{24,28},{26,30},{28,20... | collective-permute-start | bytes 786440 | tf_op jit(solution)/shard_map/ppermute | solution.py:314
  49.9 12.4 %collective-permute-start.16 = (bf16[512,256]{1,0:T(8,128)(2,1)S(1)}, bf16[512,256]{1,0:T(8,128)(2,1)}, u32[]{:S(2)}, u32[]{:S(2)}) collective-permute-start(bf16[512,256]{1,0:T(8,128)(2,1)S(1)} %collective-permute-done.14.refs_4_), channel_id=1, source_target_pairs={{8,0},{10,2},{16,8},{18,10},{24,16},{26,18},{28,24},{30,26},{20,28... | collective-permute-start | bytes 786440 | tf_op jit(solution)/shard_map/ppermute | solution.py:315
  49.9 23.3 %collective-permute-start.11 = (f32[256,512]{1,0:T(8,128)S(1)}, f32[256,512]{1,0:T(8,128)S(1)}, u32[]{:S(2)}, u32[]{:S(2)}) collective-permute-start(f32[256,512]{1,0:T(8,128)S(1)} %get-tuple-element.124.mine_ref), channel_id=1, source_target_pairs={{0,2},{2,0},{4,6},{6,4},{8,10},{10,8},{12,14},{14,12},{16,18},{18,... | collective-permute-start | bytes 1572872 | tf_op jit(solution)/shard_map/ppermute | solution.py:408
  62.3 8.8 %collective-permute-start.17 = (bf16[512,256]{1,0:T(8,128)(2,1)S(1)}, bf16[512,256]{1,0:T(8,128)(2,1)S(1)}, u32[]{:S(2)}, u32[]{:S(2)}) collective-permute-start(bf16[512,256]{1,0:T(8,128)(2,1)S(1)} %collective-permute-done.15.refs_1_), channel_id=1, source_target_pairs={{0,8},{2,10},{8,16},{10,18},{16,24},{18,26},{24,28},{26,30},{28,20... | collective-permute-start | bytes 786440 | tf_op jit(solution)/shard_map/ppermute | solution.py:314
  67.8 5.4 %collective-permute-start.18 = (bf16[512,256]{1,0:T(8,128)(2,1)}, bf16[512,256]{1,0:T(8,128)(2,1)S(1)}, u32[]{:S(2)}, u32[]{:S(2)}) collective-permute-start(bf16[512,256]{1,0:T(8,128)(2,1)} %collective-permute-done.16.refs_5_), channel_id=1, source_target_pairs={{8,0},{10,2},{16,8},{18,10},{24,16},{26,18},{28,24},{30,26},{20,28... | collective-permute-start | bytes 786440 | tf_op jit(solution)/shard_map/ppermute | solution.py:315
  84.3 17.0 %collective-permute-start.22 = (bf16[7,64,256]{2,1,0:T(8,128)(2,1)S(1)}, bf16[7,64,256]{2,1,0:T(8,128)(2,1)S(1)}, u32[]{:S(2)}, u32[]{:S(2)}) collective-permute-start(bf16[7,64,256]{2,1,0:T(8,128)(2,1)S(1)} %get-tuple-element.164), channel_id=1, source_target_pairs={{0,1},{1,0},{2,3},{3,2},{4,5},{5,4},{6,7},{7,6},{8,9},{9,8},{10,11... | collective-permute-start | bytes 688136 | tf_op jit(solution)/shard_map/ppermute | solution.py:468
  85.5 15.7 %collective-permute-start.23 = (bf16[7,64,256]{2,1,0:T(8,128)(2,1)S(1)}, bf16[7,64,256]{2,1,0:T(8,128)(2,1)S(1)}, u32[]{:S(2)}, u32[]{:S(2)}) collective-permute-start(bf16[7,64,256]{2,1,0:T(8,128)(2,1)S(1)} %get-tuple-element.165), channel_id=1, source_target_pairs={{0,2},{1,3},{2,0},{3,1},{4,6},{5,7},{6,4},{7,5},{8,10},{9,11},{10,... | collective-permute-start | bytes 688136 | tf_op jit(solution)/shard_map/ppermute | solution.py:468
  86.2 15.0 %collective-permute-start.24 = (bf16[7,64,256]{2,1,0:T(8,128)(2,1)S(1)}, bf16[7,64,256]{2,1,0:T(8,128)(2,1)S(1)}, u32[]{:S(2)}, u32[]{:S(2)}) collective-permute-start(bf16[7,64,256]{2,1,0:T(8,128)(2,1)S(1)} %get-tuple-element.166), channel_id=1, source_target_pairs={{0,3},{1,2},{2,1},{3,0},{4,7},{5,6},{6,5},{7,4},{8,11},{9,10},{10,... | collective-permute-start | bytes 688136 | tf_op jit(solution)/shard_map/ppermute | solution.py:468
  93.0 6.0 %collective-permute-start.26 = (bf16[1,64,256]{2,1,0:T(8,128)(2,1)S(1)}, bf16[1,64,256]{2,1,0:T(8,128)(2,1)S(1)}, u32[]{:S(2)}, u32[]{:S(2)}) collective-permute-start(bf16[1,64,256]{2,1,0:T(8,128)(2,1)S(1)} %get-tuple-element.169), channel_id=1, source_target_pairs={{0,2},{1,3},{2,0},{3,1},{4,6},{5,7},{6,4},{7,5},{8,10},{9,11},{10,... | collective-permute-start | bytes 98312 | tf_op jit(solution)/shard_map/ppermute | solution.py:468
  (14 other events, 99.0 us)

commit v17 on v16

--- a/solution.py
+++ b/solution.py
@@ -177,6 +177,8 @@
     orig_ref,
     kv_ref,
     out_ref,
+    sent_ref,
+    stats_ref,
 ):
     keys = kv_ref[:, :HD]
     values = kv_ref[:, HD:]
@@ -204,31 +206,34 @@
         top = jnp.max(scores, axis=-1, keepdims=True)
         expo = jnp.where(allowed, jnp.exp(scores - top), 0.0)
         total = jnp.sum(expo, axis=-1, keepdims=True)
-        out_ref[:, columns] = jnp.dot(
-            expo.astype(jnp.bfloat16), values, preferred_element_type=jnp.float32
-        )
+        product = jnp.dot(expo.astype(jnp.bfloat16), values, preferred_element_type=jnp.float32)
+        out_ref[:, columns] = product
+        sent_ref[:, columns] = product.astype(jnp.bfloat16)
         stats = jnp.where(lane == 2 * head, total, stats)
         stats = jnp.where(lane == 2 * head + 1, top, stats)
-    out_ref[:, HEAD_COLS:] = stats
-
-
-def output_kernel(groups, pieces_of, mine_ref, theirs_ref, *refs):
+    stats_ref[...] = stats
+
+
+def output_kernel(
+    groups, pieces_of, mine_ref, stats_ref, theirs_ref, their_stats_ref, *refs
+):
     weight_refs, out_refs = refs[:-groups], refs[-groups:]
     chip_rows = mine_ref.shape[0]
     half = chip_rows // 2
 
-    def swapped(columns):
-        return jnp.concatenate([theirs_ref[half:, columns], theirs_ref[:half, columns]], axis=0)
+    def swapped(ref, columns):
+        return jnp.concatenate([ref[half:, columns], ref[:half, columns]], axis=0)
 
     pieces = []
     for head in range(QH_DEV):
         columns = slice(head * HD, (head + 1) * HD)
-        at = HEAD_COLS + 2 * head
-        total, top = mine_ref[:, at : at + 1], mine_ref[:, at + 1 : at + 2]
-        other_total, other_top = swapped(slice(at, at + 1)), swapped(slice(at + 1, at + 2))
+        sums, tops = slice(2 * head, 2 * head + 1), slice(2 * head + 1, 2 * head + 2)
+        total, top = stats_ref[:, sums], stats_ref[:, tops]
+        other_total, other_top = swapped(their_stats_ref, sums), swapped(their_stats_ref, tops)
         peak = jnp.maximum(top, other_top)
         factor, other_factor = jnp.exp(top - peak), jnp.exp(other_top - peak)
-        product = mine_ref[:, columns] * factor + swapped(columns) * other_factor
+        other = swapped(theirs_ref, columns).astype(jnp.float32)
+        product = mine_ref[:, columns] * factor + other * other_factor
         pieces.append(
             (product / (total * factor + other_total * other_factor)).astype(jnp.bfloat16)
         )
@@ -423,11 +428,15 @@
     out_ring.step()
     (kv,) = ordered((kv,))
 
-    mixed = pl.pallas_call(
+    mixed, sent, stats = pl.pallas_call(
         attend_kernel,
-        out_shape=jax.ShapeDtypeStruct((2 * tokens_here, HEAD_COLS + HD), jnp.float32),
+        out_shape=[
+            jax.ShapeDtypeStruct((2 * tokens_here, HEAD_COLS), jnp.float32),
+            jax.ShapeDtypeStruct((2 * tokens_here, HEAD_COLS), jnp.bfloat16),
+            jax.ShapeDtypeStruct((2 * tokens_here, HD), jnp.float32),
+        ],
         in_specs=vmem_specs(8),
-        out_specs=vmem_specs(1)[0],
+        out_specs=vmem_specs(3),
         compiler_params=compute_params(),
         name="attend",
     )(
@@ -440,10 +449,11 @@
         key_orig,
         kv,
     )
+    sent, stats = ordered((sent, stats))
+    sent = lax.ppermute(sent, "context", sibling)
+    their_stats = lax.ppermute(stats, "context", sibling)
     while not out_ring.done():
         out_ring.step()
-    (mixed,) = ordered((mixed,))
-    mixed_theirs = lax.ppermute(mixed, "context", sibling)
 
     out_block = w_out.shape[1]
 
@@ -454,11 +464,11 @@
             functools.partial(output_kernel, groups, [len(pieces) for pieces in blocks]),
             out_shape=[jax.ShapeDtypeStruct((len(slots), rows_here, out_block), jnp.bfloat16)]
             * groups,
-            in_specs=vmem_specs(2 + len(flat)),
+            in_specs=vmem_specs(4 + len(flat)),
             out_specs=vmem_specs(groups),
             compiler_params=compute_params(),
             name=name,
-        )(mixed, mixed_theirs, *flat)
+        )(mixed, stats, sent, their_stats, *flat)
         parts = ordered(parts)
         arrived = []
         for e in range(2):

time: 103 us -> 96.6 us (0.938)
  waiting for transfers between devices: 44.1 us -> 39.8 us
  starting transfers between devices: 45.2 us -> 43 us
    ppermute x6, starting transfers between devices: 12.9 us -> 10.4 us  [step(): self.up.append(lax.ppermute(up, 'context', ahead))]
    ppermute x6, waiting for transfers between devices: 25.2 us -> 23 us  [step(): self.up.append(lax.ppermute(up, 'context', ahead))]
    ppermute x6, starting transfers between devices: 7.63 us -> 9.6 us  [output(): part = lax.ppermute(part, ('context', 'tensor'), member(e, -d))]
    ppermute x6, waiting for transfers between devices: 3.91 us -> 2.45 us  [output(): part = lax.ppermute(part, ('context', 'tensor'), member(e, -d))]
    ppermute x1 -> x2, starting transfers between devices: 3.66 us -> 2.59 us  [the longest x1 2.52 us: per_device(): sent = lax.ppermute(sent, 'context', sibling)]
  transfers between devices with their start and end apart: 29 -> 30, of which waited for: 17 -> 15; matrix products, arithmetic and copies ran while one was open for 0% -> 0% of each run, Pallas kernels for 3% -> 6%
where the time goes in v17:
time: 96.6 us; the launch traced here: 95.9 us
  starting transfers between devices  43 us (45%)
  waiting for transfers between devices  39.8 us (41%)
  Pallas kernels  10.2 us (11%)
  local copies, waits for them, and re-layouts  2.71 us (3%)
    ppermute x6, waiting for transfers between devices, step(): self.up.append(lax.ppermute(up, 'context', ahead))  23 us
    ppermute x6, starting transfers between devices, step(): self.up.append(lax.ppermute(up, 'context', ahead))  10.4 us
    ppermute x6, starting transfers between devices, output(): part = lax.ppermute(part, ('context', 'tensor'), member(e, -d))  9.6 us
    ppermute x1, starting transfers between devices, per_device(): theirs = lax.ppermute(theirs, 'context', sibling)  5.86 us
    ppermute x2, waiting for transfers between devices, step(): lax.ppermute(down[half:], 'context', back)  5.72 us
    ppermute x6, waiting for transfers between devices, step(): self.down.append(lax.ppermute(down, 'context', back))  5.62 us
    ppermute x2, starting transfers between devices, per_device(): normed += [lax.ppermute(rows, 'context', sibling) for rows in normed]  4.3 us
    all_to_all x1, starting transfers between devices, per_device(): lax.all_to_all(kv, 'context', split_axis=0, concat_axis=0, axis_index_gro...  3.56 us
  transfers between devices with their start and end apart: 30, of which 15 were waited for; matrix products, arithmetic and copies ran while one was open for 0% of the time, Pallas kernels for 6%

profile of v17, /device:TPU:1, one launch (start us, length us, event | category | flops | bytes accessed | tf_op | source)
XLA Modules:
  0.0 95.9 jit_solution(4418724698128709460)
XLA Ops:
  0.0 2.1 %collective-permute-start = (bf16[256,768]{1,0:T(8,128)(2,1)}, bf16[256,768]{1,0:T(8,128)(2,1)S(1)}, u32[]{:S(2)}, u32[]{:S(2)}) collective-permute-start(bf16[256,768]{1,0:T(8,128)(2,1)} %refs_4_), channel_id=1, source_target_pairs={{0,8},{2,10},{8,16},{10,18},{16,24},{18,26},{24,28},{26,30},{28,20... | collective-permute-start | bytes 1179656 | tf_op jit(solution)/shard_map/ppermute | solution.py:319
  4.2 1.4 %collective-permute-start.6 = (bf16[2,8,64,256]{3,2,1,0:T(8,128)(2,1)S(1)}, bf16[2,8,64,256]{3,2,1,0:T(8,128)(2,1)S(1)}, u32[]{:S(2)}, u32[]{:S(2)}) collective-permute-start(bf16[2,8,64,256]{3,2,1,0:T(8,128)(2,1)S(1)} %norm.1.refs_0_), channel_id=1, source_target_pairs={{0,1},{1,0},{2,3},{3,2},{4,5},{5,4},{6,7},{7,6},{8,9},{9,8},{10,11... | collective-permute-start | bytes 1572872 | tf_op jit(solution)/shard_map/ppermute | solution.py:381
  5.6 5.5 %collective-permute-done.refs_12_ = bf16[256,768]{1,0:T(8,128)(2,1)S(1)} collective-permute-done((bf16[256,768]{1,0:T(8,128)(2,1)}, bf16[256,768]{1,0:T(8,128)(2,1)S(1)}, u32[]{:S(2)}, u32[]{:S(2)}) %collective-permute-start) | collective-permute-done | bytes 393248 | tf_op jit(solution)/shard_map/ppermute | solution.py:319
  12.0 1.3 %collective-permute-start.2 = (bf16[256,768]{1,0:T(8,128)(2,1)S(1)}, bf16[256,768]{1,0:T(8,128)(2,1)S(1)}, u32[]{:S(2)}, u32[]{:S(2)}) collective-permute-start(bf16[256,768]{1,0:T(8,128)(2,1)S(1)} %collective-permute-done.refs_12_), channel_id=1, source_target_pairs={{0,8},{2,10},{8,16},{10,18},{16,24},{18,26},{24,28},{26,30},{28,20... | collective-permute-start | bytes 1179656 | tf_op jit(solution)/shard_map/ppermute | solution.py:319
  13.5 2.4 %collective-permute-start.7 = (bf16[2,8,64,256]{3,2,1,0:T(8,128)(2,1)S(1)}, bf16[2,8,64,256]{3,2,1,0:T(8,128)(2,1)S(1)}, u32[]{:S(2)}, u32[]{:S(2)}) collective-permute-start(bf16[2,8,64,256]{3,2,1,0:T(8,128)(2,1)S(1)} %norm.1.refs_0_), channel_id=1, source_target_pairs={{0,2},{2,0},{4,6},{6,4},{8,10},{10,8},{12,14},{14,12},{16,18},{18,... | collective-permute-start | bytes 1572872 | tf_op jit(solution)/shard_map/ppermute | solution.py:386
  16.7 1.9 %collective-permute-start.8 = (bf16[2,8,64,256]{3,2,1,0:T(8,128)(2,1)S(1)}, bf16[2,8,64,256]{3,2,1,0:T(8,128)(2,1)S(1)}, u32[]{:S(2)}, u32[]{:S(2)}) collective-permute-start(bf16[2,8,64,256]{3,2,1,0:T(8,128)(2,1)S(1)} %collective-permute-done.6.refs_1_), channel_id=1, source_target_pairs={{0,2},{2,0},{4,6},{6,4},{8,10},{10,8},{12,14},{14,12},{16,18},{18,... | collective-permute-start | bytes 1572872 | tf_op jit(solution)/shard_map/ppermute | solution.py:386
  23.2 6.1 %collective-permute-done.4.refs_10_ = bf16[256,768]{1,0:T(8,128)(2,1)S(1)} collective-permute-done((bf16[256,768]{1,0:T(8,128)(2,1)S(1)}, bf16[256,768]{1,0:T(8,128)(2,1)S(1)}, u32[]{:S(2)}, u32[]{:S(2)}) %collective-permute-start.4) | collective-permute-done | bytes 393248 | tf_op jit(solution)/shard_map/ppermute | solution.py:319
  33.4 2.6 %collective-permute-done.10.refs_9_ = bf16[128,768]{1,0:T(8,128)(2,1)S(1)} collective-permute-done((bf16[128,768]{1,0:T(8,128)(2,1)S(1)}, bf16[128,768]{1,0:T(8,128)(2,1)S(1)}, u32[]{:S(2)}, u32[]{:S(2)}) %collective-permute-start.10) | collective-permute-done | bytes 196640 | tf_op jit(solution)/shard_map/ppermute | solution.py:325
  37.1 5.9 %collective-permute-start.12 = (f32[128,256]{1,0:T(8,128)S(1)}, f32[128,256]{1,0:T(8,128)S(1)}, u32[]{:S(2)}, u32[]{:S(2)}) collective-permute-start(f32[128,256]{1,0:T(8,128)S(1)} %get-tuple-element.135), channel_id=1, source_target_pairs={{0,2},{2,0},{4,6},{6,4},{8,10},{10,8},{12,14},{14,12},{16,18},{18,... | collective-permute-start | bytes 393224 | tf_op jit(solution)/shard_map/ppermute | solution.py:412
  44.9 3.6 %all-to-all-start = ((bf16[8,128,256]{2,1,0:T(8,128)(2,1)}), bf16[8,128,256]{2,1,0:T(8,128)(2,1)S(1)}, u32[]{:S(2)}, u32[]{:S(2)}) async-start(bf16[8,128,256]{2,1,0:T(8,128)(2,1)} %bitcast.1), calls=%async_computation | async-start | bytes 1048576 | tf_op jit(solution)/shard_map/all_to_all | solution.py:425
  48.4 1.7 %collective-permute-start.11 = (f32[256,512]{1,0:T(8,128)S(1)}, f32[256,512]{1,0:T(8,128)S(1)}, u32[]{:S(2)}, u32[]{:S(2)}) collective-permute-start(f32[256,512]{1,0:T(8,128)S(1)} %get-tuple-element.128.mine_ref), channel_id=1, source_target_pairs={{0,2},{2,0},{4,6},{6,4},{8,10},{10,8},{12,14},{14,12},{16,18},{18,... | collective-permute-start | bytes 1572872 | tf_op jit(solution)/shard_map/ppermute | solution.py:413
  50.1 1.6 %collective-permute-start.15 = (bf16[512,256]{1,0:T(8,128)(2,1)S(1)}, bf16[512,256]{1,0:T(8,128)(2,1)S(1)}, u32[]{:S(2)}, u32[]{:S(2)}) collective-permute-start(bf16[512,256]{1,0:T(8,128)(2,1)S(1)} %collective-permute-done.13.refs_2_), channel_id=1, source_target_pairs={{0,8},{2,10},{8,16},{10,18},{16,24},{18,26},{24,28},{26,30},{28,20... | collective-permute-start | bytes 786440 | tf_op jit(solution)/shard_map/ppermute | solution.py:319
  51.7 10.5 %collective-permute-done.15.refs_1_ = bf16[512,256]{1,0:T(8,128)(2,1)S(1)} collective-permute-done((bf16[512,256]{1,0:T(8,128)(2,1)S(1)}, bf16[512,256]{1,0:T(8,128)(2,1)S(1)}, u32[]{:S(2)}, u32[]{:S(2)}) %collective-permute-start.15) | collective-permute-done | bytes 262176 | tf_op jit(solution)/shard_map/ppermute | solution.py:319
  62.2 2.7 %collective-permute-done.16.refs_5_ = bf16[512,256]{1,0:T(8,128)(2,1)} collective-permute-done((bf16[512,256]{1,0:T(8,128)(2,1)S(1)}, bf16[512,256]{1,0:T(8,128)(2,1)}, u32[]{:S(2)}, u32[]{:S(2)}) %collective-permute-start.16) | collective-permute-done | bytes 262176 | tf_op jit(solution)/shard_map/ppermute | solution.py:320
  64.9 2.9 %collective-permute-start.19 = (bf16[512,256]{1,0:T(8,128)(2,1)S(1)}, bf16[512,256]{1,0:T(8,128)(2,1)S(1)}, u32[]{:S(2)}, u32[]{:S(2)}) collective-permute-start(bf16[512,256]{1,0:T(8,128)(2,1)S(1)} %collective-permute-done.15.refs_1_), channel_id=1, source_target_pairs={{0,8},{2,10},{8,16},{10,18},{16,24},{18,26},{24,28},{26,30},{28,20... | collective-permute-start | bytes 786440 | tf_op jit(solution)/shard_map/ppermute | solution.py:319
  68.7 2.5 %attend.1 = (f32[256,512]{1,0:T(8,128)S(1)}, bf16[256,512]{1,0:T(8,128)(2,1)S(1)}, f32[256,128]{1,0:T(8,128)S(1)}) custom-call(f32[256,512]{1,0:T(8,128)S(1)} %get-tuple-element.128.mine_ref, f32[256,512]{1,0:T(8,128)S(1)} %collective-permute-done.11.theirs_ref, f32[256,128]{1,0:T(8,128)S(1)} %get-tuple-element.129.cosine_ref, ...), custom_call_target="tpu_custom_call" | custom-call | tf_op jit(solution)/shard_map/attend/pallas_call | solution.py:431
  71.2 2.5 %collective-permute-start.17 = (bf16[256,512]{1,0:T(8,128)(2,1)S(1)}, bf16[256,512]{1,0:T(8,128)(2,1)S(1)}, u32[]{:S(2)}, u32[]{:S(2)}) collective-permute-start(bf16[256,512]{1,0:T(8,128)(2,1)S(1)} %get-tuple-element.154), channel_id=1, source_target_pairs={{0,2},{2,0},{4,6},{6,4},{8,10},{10,8},{12,14},{14,12},{16,18},{18,... | collective-permute-start | bytes 786440 | tf_op jit(solution)/shard_map/ppermute | solution.py:453
  75.1 2.2 %output_near.1 = (bf16[7,64,256]{2,1,0:T(8,128)(2,1)S(1)}, bf16[7,64,256]{2,1,0:T(8,128)(2,1)S(1)}, bf16[7,64,256]{2,1,0:T(8,128)(2,1)S(1)}, bf16[7,64,256]{2,1,0:T(8,128)(2,1)S(1)}) custom-call(f32[256,512]{1,0:T(8,128)S(1)} %get-tuple-element.149.mine_ref, f32[256,128]{1,0:T(8,128)S(1)} %get-tuple-element.153.stats_ref, ...), custom_call_target="tpu_custom_call" | custom-call | tf_op jit(solution)/shard_map/output_near/pallas_call | solution.py:463
  78.6 2.0 %collective-permute-start.24 = (bf16[7,64,256]{2,1,0:T(8,128)(2,1)S(1)}, bf16[7,64,256]{2,1,0:T(8,128)(2,1)S(1)}, u32[]{:S(2)}, u32[]{:S(2)}) collective-permute-start(bf16[7,64,256]{2,1,0:T(8,128)(2,1)S(1)} %get-tuple-element.173), channel_id=1, source_target_pairs={{0,2},{1,3},{2,0},{3,1},{4,6},{5,7},{6,4},{7,5},{8,10},{9,11},{10,... | collective-permute-start | bytes 688136 | tf_op jit(solution)/shard_map/ppermute | solution.py:478
  80.8 1.5 %collective-permute-start.21 = (bf16[256,256]{1,0:T(8,128)(2,1)S(1)}, bf16[256,256]{1,0:T(8,128)(2,1)S(1)}, u32[]{:S(2)}, u32[]{:S(2)}) collective-permute-start(bf16[256,256]{1,0:T(8,128)(2,1)S(1)} %slice.14), channel_id=1, source_target_pairs={{0,8},{2,10},{8,16},{10,18},{16,24},{18,26},{24,28},{26,30},{28,20... | collective-permute-start | bytes 393224 | tf_op jit(solution)/shard_map/ppermute | solution.py:324
  82.3 3.1 %collective-permute-done.22.refs_1_ = bf16[256,256]{1,0:T(8,128)(2,1)S(1)} collective-permute-done((bf16[256,256]{1,0:T(8,128)(2,1)S(1)}, bf16[256,256]{1,0:T(8,128)(2,1)S(1)}, u32[]{:S(2)}, u32[]{:S(2)}) %collective-permute-start.22) | collective-permute-done | bytes 131104 | tf_op jit(solution)/shard_map/ppermute | solution.py:325
  87.4 1.7 %collective-permute-start.27 = (bf16[1,64,256]{2,1,0:T(8,128)(2,1)S(1)}, bf16[1,64,256]{2,1,0:T(8,128)(2,1)S(1)}, u32[]{:S(2)}, u32[]{:S(2)}) collective-permute-start(bf16[1,64,256]{2,1,0:T(8,128)(2,1)S(1)} %get-tuple-element.177), channel_id=1, source_target_pairs={{0,2},{1,3},{2,0},{3,1},{4,6},{5,7},{6,4},{7,5},{8,10},{9,11},{10,... | collective-permute-start | bytes 98312 | tf_op jit(solution)/shard_map/ppermute | solution.py:478
  89.4 3.2 %collective-permute-start.28 = (bf16[1,64,256]{2,1,0:T(8,128)(2,1)S(1)}, bf16[1,64,256]{2,1,0:T(8,128)(2,1)S(1)}, u32[]{:S(2)}, u32[]{:S(2)}) collective-permute-start(bf16[1,64,256]{2,1,0:T(8,128)(2,1)S(1)} %get-tuple-element.178), channel_id=1, source_target_pairs={{0,3},{1,2},{2,1},{3,0},{4,7},{5,6},{6,5},{7,4},{8,11},{9,10},{10,... | collective-permute-start | bytes 98312 | tf_op jit(solution)/shard_map/ppermute | solution.py:478
  92.6 2.2 %collective-permute-done.28.refs_7_ = bf16[1,64,256]{2,1,0:T(8,128)(2,1)S(1)} collective-permute-done((bf16[1,64,256]{2,1,0:T(8,128)(2,1)S(1)}, bf16[1,64,256]{2,1,0:T(8,128)(2,1)S(1)}, u32[]{:S(2)}, u32[]{:S(2)}) %collective-permute-start.28) | collective-permute-done | bytes 32800 | tf_op jit(solution)/shard_map/ppermute | solution.py:478
  (66 shorter events, 22.7 us)
Async XLA Ops:
  0.0 11.1 %collective-permute-start = (bf16[256,768]{1,0:T(8,128)(2,1)}, bf16[256,768]{1,0:T(8,128)(2,1)S(1)}, u32[]{:S(2)}, u32[]{:S(2)}) collective-permute-start(bf16[256,768]{1,0:T(8,128)(2,1)} %refs_4_), channel_id=1, source_target_pairs={{0,8},{2,10},{8,16},{10,18},{16,24},{18,26},{24,28},{26,30},{28,20... | collective-permute-start | bytes 1179656 | tf_op jit(solution)/shard_map/ppermute | solution.py:319
  2.1 9.9 %collective-permute-start.1 = (bf16[256,768]{1,0:T(8,128)(2,1)}, bf16[256,768]{1,0:T(8,128)(2,1)S(1)}, u32[]{:S(2)}, u32[]{:S(2)}) collective-permute-start(bf16[256,768]{1,0:T(8,128)(2,1)} %refs_4_), channel_id=1, source_target_pairs={{8,0},{10,2},{16,8},{18,10},{24,16},{26,18},{28,24},{30,26},{20,28... | collective-permute-start | bytes 1179656 | tf_op jit(solution)/shard_map/ppermute | solution.py:320
  4.2 12.5 %collective-permute-start.6 = (bf16[2,8,64,256]{3,2,1,0:T(8,128)(2,1)S(1)}, bf16[2,8,64,256]{3,2,1,0:T(8,128)(2,1)S(1)}, u32[]{:S(2)}, u32[]{:S(2)}) collective-permute-start(bf16[2,8,64,256]{3,2,1,0:T(8,128)(2,1)S(1)} %norm.1.refs_0_), channel_id=1, source_target_pairs={{0,1},{1,0},{2,3},{3,2},{4,5},{5,4},{6,7},{7,6},{8,9},{9,8},{10,11... | collective-permute-start | bytes 1572872 | tf_op jit(solution)/shard_map/ppermute | solution.py:381
  12.0 8.7 %collective-permute-start.2 = (bf16[256,768]{1,0:T(8,128)(2,1)S(1)}, bf16[256,768]{1,0:T(8,128)(2,1)S(1)}, u32[]{:S(2)}, u32[]{:S(2)}) collective-permute-start(bf16[256,768]{1,0:T(8,128)(2,1)S(1)} %collective-permute-done.refs_12_), channel_id=1, source_target_pairs={{0,8},{2,10},{8,16},{10,18},{16,24},{18,26},{24,28},{26,30},{28,20... | collective-permute-start | bytes 1179656 | tf_op jit(solution)/shard_map/ppermute | solution.py:319
  13.3 8.5 %collective-permute-start.3 = (bf16[256,768]{1,0:T(8,128)(2,1)S(1)}, bf16[256,768]{1,0:T(8,128)(2,1)S(1)}, u32[]{:S(2)}, u32[]{:S(2)}) collective-permute-start(bf16[256,768]{1,0:T(8,128)(2,1)S(1)} %collective-permute-done.1.refs_5_), channel_id=1, source_target_pairs={{8,0},{10,2},{16,8},{18,10},{24,16},{26,18},{28,24},{30,26},{20,28... | collective-permute-start | bytes 1179656 | tf_op jit(solution)/shard_map/ppermute | solution.py:320
  13.5 9.8 %collective-permute-start.7 = (bf16[2,8,64,256]{3,2,1,0:T(8,128)(2,1)S(1)}, bf16[2,8,64,256]{3,2,1,0:T(8,128)(2,1)S(1)}, u32[]{:S(2)}, u32[]{:S(2)}) collective-permute-start(bf16[2,8,64,256]{3,2,1,0:T(8,128)(2,1)S(1)} %norm.1.refs_0_), channel_id=1, source_target_pairs={{0,2},{2,0},{4,6},{6,4},{8,10},{10,8},{12,14},{14,12},{16,18},{18,... | collective-permute-start | bytes 1572872 | tf_op jit(solution)/shard_map/ppermute | solution.py:386
  16.7 6.5 %collective-permute-start.8 = (bf16[2,8,64,256]{3,2,1,0:T(8,128)(2,1)S(1)}, bf16[2,8,64,256]{3,2,1,0:T(8,128)(2,1)S(1)}, u32[]{:S(2)}, u32[]{:S(2)}) collective-permute-start(bf16[2,8,64,256]{3,2,1,0:T(8,128)(2,1)S(1)} %collective-permute-done.6.refs_1_), channel_id=1, source_target_pairs={{0,2},{2,0},{4,6},{6,4},{8,10},{10,8},{12,14},{14,12},{16,18},{18,... | collective-permute-start | bytes 1572872 | tf_op jit(solution)/shard_map/ppermute | solution.py:386
  21.8 7.5 %collective-permute-start.4 = (bf16[256,768]{1,0:T(8,128)(2,1)S(1)}, bf16[256,768]{1,0:T(8,128)(2,1)S(1)}, u32[]{:S(2)}, u32[]{:S(2)}) collective-permute-start(bf16[256,768]{1,0:T(8,128)(2,1)S(1)} %collective-permute-done.2.refs_11_), channel_id=1, source_target_pairs={{0,8},{2,10},{8,16},{10,18},{16,24},{18,26},{24,28},{26,30},{28,20... | collective-permute-start | bytes 1179656 | tf_op jit(solution)/shard_map/ppermute | solution.py:319
  23.1 7.3 %collective-permute-start.5 = (bf16[256,768]{1,0:T(8,128)(2,1)S(1)}, bf16[256,768]{1,0:T(8,128)(2,1)S(1)}, u32[]{:S(2)}, u32[]{:S(2)}) collective-permute-start(bf16[256,768]{1,0:T(8,128)(2,1)S(1)} %collective-permute-done.3.refs_6_), channel_id=1, source_target_pairs={{8,0},{10,2},{16,8},{18,10},{24,16},{26,18},{28,24},{30,26},{20,28... | collective-permute-start | bytes 1179656 | tf_op jit(solution)/shard_map/ppermute | solution.py:320
  30.4 5.6 %collective-permute-start.10 = (bf16[128,768]{1,0:T(8,128)(2,1)S(1)}, bf16[128,768]{1,0:T(8,128)(2,1)S(1)}, u32[]{:S(2)}, u32[]{:S(2)}) collective-permute-start(bf16[128,768]{1,0:T(8,128)(2,1)S(1)} %slice.13), channel_id=1, source_target_pairs={{8,0},{10,2},{16,8},{18,10},{24,16},{26,18},{28,24},{30,26},{20,28... | collective-permute-start | bytes 589832 | tf_op jit(solution)/shard_map/ppermute | solution.py:325
  30.6 5.4 %collective-permute-start.9 = (bf16[128,768]{1,0:T(8,128)(2,1)S(1)}, bf16[128,768]{1,0:T(8,128)(2,1)S(1)}, u32[]{:S(2)}, u32[]{:S(2)}) collective-permute-start(bf16[128,768]{1,0:T(8,128)(2,1)S(1)} %slice.12), channel_id=1, source_target_pairs={{0,8},{2,10},{8,16},{10,18},{16,24},{18,26},{24,28},{26,30},{28,20... | collective-permute-start | bytes 589832 | tf_op jit(solution)/shard_map/ppermute | solution.py:324
  31.9 11.1 %collective-permute-start.13 = (bf16[512,256]{1,0:T(8,128)(2,1)S(1)}, bf16[512,256]{1,0:T(8,128)(2,1)S(1)}, u32[]{:S(2)}, u32[]{:S(2)}) collective-permute-start(bf16[512,256]{1,0:T(8,128)(2,1)S(1)} %copy-done.2), channel_id=1, source_target_pairs={{0,8},{2,10},{8,16},{10,18},{16,24},{18,26},{24,28},{26,30},{28,20... | collective-permute-start | bytes 786440 | tf_op jit(solution)/shard_map/ppermute | solution.py:319
  33.1 9.8 %collective-permute-start.14 = (bf16[512,256]{1,0:T(8,128)(2,1)S(1)}, bf16[512,256]{1,0:T(8,128)(2,1)S(1)}, u32[]{:S(2)}, u32[]{:S(2)}) collective-permute-start(bf16[512,256]{1,0:T(8,128)(2,1)S(1)} %copy-done.2), channel_id=1, source_target_pairs={{8,0},{10,2},{16,8},{18,10},{24,16},{26,18},{28,24},{30,26},{20,28... | collective-permute-start | bytes 786440 | tf_op jit(solution)/shard_map/ppermute | solution.py:320
  37.1 6.8 %collective-permute-start.12 = (f32[128,256]{1,0:T(8,128)S(1)}, f32[128,256]{1,0:T(8,128)S(1)}, u32[]{:S(2)}, u32[]{:S(2)}) collective-permute-start(f32[128,256]{1,0:T(8,128)S(1)} %get-tuple-element.135), channel_id=1, source_target_pairs={{0,2},{2,0},{4,6},{6,4},{8,10},{10,8},{12,14},{14,12},{16,18},{18,... | collective-permute-start | bytes 393224 | tf_op jit(solution)/shard_map/ppermute | solution.py:412
  44.9 22.9 %all-to-all-start = ((bf16[8,128,256]{2,1,0:T(8,128)(2,1)}), bf16[8,128,256]{2,1,0:T(8,128)(2,1)S(1)}, u32[]{:S(2)}, u32[]{:S(2)}) async-start(bf16[8,128,256]{2,1,0:T(8,128)(2,1)} %bitcast.1), calls=%async_computation | async-start | bytes 1048576 | tf_op jit(solution)/shard_map/all_to_all | solution.py:425
  48.4 19.3 %collective-permute-start.11 = (f32[256,512]{1,0:T(8,128)S(1)}, f32[256,512]{1,0:T(8,128)S(1)}, u32[]{:S(2)}, u32[]{:S(2)}) collective-permute-start(f32[256,512]{1,0:T(8,128)S(1)} %get-tuple-element.128.mine_ref), channel_id=1, source_target_pairs={{0,2},{2,0},{4,6},{6,4},{8,10},{10,8},{12,14},{14,12},{16,18},{18,... | collective-permute-start | bytes 1572872 | tf_op jit(solution)/shard_map/ppermute | solution.py:413
  50.1 12.1 %collective-permute-start.15 = (bf16[512,256]{1,0:T(8,128)(2,1)S(1)}, bf16[512,256]{1,0:T(8,128)(2,1)S(1)}, u32[]{:S(2)}, u32[]{:S(2)}) collective-permute-start(bf16[512,256]{1,0:T(8,128)(2,1)S(1)} %collective-permute-done.13.refs_2_), channel_id=1, source_target_pairs={{0,8},{2,10},{8,16},{10,18},{16,24},{18,26},{24,28},{26,30},{28,20... | collective-permute-start | bytes 786440 | tf_op jit(solution)/shard_map/ppermute | solution.py:319
  51.7 13.2 %collective-permute-start.16 = (bf16[512,256]{1,0:T(8,128)(2,1)S(1)}, bf16[512,256]{1,0:T(8,128)(2,1)}, u32[]{:S(2)}, u32[]{:S(2)}) collective-permute-start(bf16[512,256]{1,0:T(8,128)(2,1)S(1)} %collective-permute-done.14.refs_4_), channel_id=1, source_target_pairs={{8,0},{10,2},{16,8},{18,10},{24,16},{26,18},{28,24},{30,26},{20,28... | collective-permute-start | bytes 786440 | tf_op jit(solution)/shard_map/ppermute | solution.py:320
  64.9 8.9 %collective-permute-start.19 = (bf16[512,256]{1,0:T(8,128)(2,1)S(1)}, bf16[512,256]{1,0:T(8,128)(2,1)S(1)}, u32[]{:S(2)}, u32[]{:S(2)}) collective-permute-start(bf16[512,256]{1,0:T(8,128)(2,1)S(1)} %collective-permute-done.15.refs_1_), channel_id=1, source_target_pairs={{0,8},{2,10},{8,16},{10,18},{16,24},{18,26},{24,28},{26,30},{28,20... | collective-permute-start | bytes 786440 | tf_op jit(solution)/shard_map/ppermute | solution.py:319
  67.8 6.1 %collective-permute-start.20 = (bf16[512,256]{1,0:T(8,128)(2,1)}, bf16[512,256]{1,0:T(8,128)(2,1)S(1)}, u32[]{:S(2)}, u32[]{:S(2)}) collective-permute-start(bf16[512,256]{1,0:T(8,128)(2,1)} %collective-permute-done.16.refs_5_), channel_id=1, source_target_pairs={{8,0},{10,2},{16,8},{18,10},{24,16},{26,18},{28,24},{30,26},{20,28... | collective-permute-start | bytes 786440 | tf_op jit(solution)/shard_map/ppermute | solution.py:320
  77.3 17.5 %collective-permute-start.23 = (bf16[7,64,256]{2,1,0:T(8,128)(2,1)S(1)}, bf16[7,64,256]{2,1,0:T(8,128)(2,1)S(1)}, u32[]{:S(2)}, u32[]{:S(2)}) collective-permute-start(bf16[7,64,256]{2,1,0:T(8,128)(2,1)S(1)} %get-tuple-element.172), channel_id=1, source_target_pairs={{0,1},{1,0},{2,3},{3,2},{4,5},{5,4},{6,7},{7,6},{8,9},{9,8},{10,11... | collective-permute-start | bytes 688136 | tf_op jit(solution)/shard_map/ppermute | solution.py:478
  78.6 16.2 %collective-permute-start.24 = (bf16[7,64,256]{2,1,0:T(8,128)(2,1)S(1)}, bf16[7,64,256]{2,1,0:T(8,128)(2,1)S(1)}, u32[]{:S(2)}, u32[]{:S(2)}) collective-permute-start(bf16[7,64,256]{2,1,0:T(8,128)(2,1)S(1)} %get-tuple-element.173), channel_id=1, source_target_pairs={{0,2},{1,3},{2,0},{3,1},{4,6},{5,7},{6,4},{7,5},{8,10},{9,11},{10,... | collective-permute-start | bytes 688136 | tf_op jit(solution)/shard_map/ppermute | solution.py:478
  80.6 14.2 %collective-permute-start.25 = (bf16[7,64,256]{2,1,0:T(8,128)(2,1)S(1)}, bf16[7,64,256]{2,1,0:T(8,128)(2,1)S(1)}, u32[]{:S(2)}, u32[]{:S(2)}) collective-permute-start(bf16[7,64,256]{2,1,0:T(8,128)(2,1)S(1)} %get-tuple-element.174), channel_id=1, source_target_pairs={{0,3},{1,2},{2,1},{3,0},{4,7},{5,6},{6,5},{7,4},{8,11},{9,10},{10,... | collective-permute-start | bytes 688136 | tf_op jit(solution)/shard_map/ppermute | solution.py:478
  89.4 5.4 %collective-permute-start.28 = (bf16[1,64,256]{2,1,0:T(8,128)(2,1)S(1)}, bf16[1,64,256]{2,1,0:T(8,128)(2,1)S(1)}, u32[]{:S(2)}, u32[]{:S(2)}) collective-permute-start(bf16[1,64,256]{2,1,0:T(8,128)(2,1)S(1)} %get-tuple-element.178), channel_id=1, source_target_pairs={{0,3},{1,2},{2,1},{3,0},{4,7},{5,6},{6,5},{7,4},{8,11},{9,10},{10,... | collective-permute-start | bytes 98312 | tf_op jit(solution)/shard_map/ppermute | solution.py:478
  (15 other events, 97.8 us)

commit v18 on v14

--- a/solution.py
+++ b/solution.py
@@ -90,6 +90,12 @@
         orig_ref[:, chip * rows : (chip + 1) * rows] = initial(owner, inside)
 
 
+def slot_of(place, chip, side, at):
+    chips = len(place)
+    ahead = place[chip] - at if side == 0 else at - place[chip]
+    return lax.rem(ahead + chips, chips)
+
+
 def norm_kernel(place, chips, hidden_ref, gain_ref, out_ref):
     at, core = place_of(place)
     wide = hidden_ref[...].astype(jnp.float32)
@@ -112,8 +118,8 @@
         @pl.when(core == even)
         def _():
             for chip in range(chips):
-                slot = lax.rem(place[chip] + chips - at, chips)
                 for side in range(2):
+                    slot = slot_of(place, chip, side, at)
                     column = (2 * chip + side) * block
                     out_ref[side ^ even, slot] = normed[:, column : column + block]
 
@@ -273,8 +279,8 @@
         @pl.when(core == even)
         def _():
             for chip in range(chips):
-                slot = lax.rem(place[chip] + chips - at, chips)
                 for side in range(2):
+                    slot = slot_of(place, chip, side, at)
                     column = (2 * chip + side) * block
                     out_ref[:, column : column + block] = added(side ^ even, slot)
 
@@ -290,7 +296,9 @@
     context = lax.axis_index("context")
     tensor = lax.axis_index("tensor")
     ahead = [
-        (ring[i] * 2 + k, ring[(i + 1) % chips] * 2 + k) for i in range(chips) for k in range(2)
+        (ring[i] * 2 + k, ring[(i + 1 - 2 * k) % chips] * 2 + k)
+        for i in range(chips)
+        for k in range(2)
     ]
     back = [(b, a) for a, b in ahead]
     sibling = [(c, c ^ 1) for c in range(n_context)]
@@ -381,6 +389,9 @@
     normed += [lax.ppermute(rows, "context", sibling) for rows in normed]
 
     qkv_ring.step()
+    cosine, sine, query_start, query_orig, key_orig = ordered(
+        (cosine, sine, query_start, query_orig, key_orig)
+    )
     qkv_ring.step()
     normed = qkv_ring.step(normed)
     while not qkv_ring.done():

time: 95.7 us -> 100 us (1.045)
  waiting for transfers between devices: 44.3 us -> 53.9 us
  starting transfers between devices: 39.8 us -> 34.8 us
    ppermute x6, waiting for transfers between devices: 26.5 us -> 33.1 us  [step(): self.up.append(lax.ppermute(up, 'context', ahead))]
    ppermute x1, starting transfers between devices: 6.09 us -> 1.78 us  [per_device(): theirs = lax.ppermute(theirs, 'context', sibling)]
    ppermute x2, waiting for transfers between devices: 1.64 us -> 4.23 us  [step(): lax.ppermute(up[:half], 'context', ahead)]
    ppermute x6, starting transfers between devices: 1.81 us -> 4.13 us  [step(): self.down.append(lax.ppermute(down, 'context', back))]
    ppermute x2, starting transfers between devices: 4.3 us -> 2.39 us  [per_device(): normed += [lax.ppermute(rows, 'context', sibling) for rows in normed]]
    ppermute x6, starting transfers between devices: 10.3 us -> 8.7 us  [step(): self.up.append(lax.ppermute(up, 'context', ahead))]
    ppermute x6, waiting for transfers between devices: 9.32 us -> 8.24 us  [step(): self.down.append(lax.ppermute(down, 'context', back))]
  transfers between devices with their start and end apart: 29 -> 29, of which waited for: 19 -> 17; matrix products, arithmetic and copies ran while one was open for 0% -> 0% of each run, Pallas kernels for 5% -> 5%
where the time goes in v18:
time: 100 us; the launch traced here: 99.9 us
  waiting for transfers between devices  53.9 us (54%)
  starting transfers between devices  34.8 us (35%)
  Pallas kernels  9.22 us (9%)
  local copies, waits for them, and re-layouts  1.81 us (2%)
    ppermute x6, waiting for transfers between devices, step(): self.up.append(lax.ppermute(up, 'context', ahead))  33.1 us
    ppermute x6, starting transfers between devices, step(): self.up.append(lax.ppermute(up, 'context', ahead))  8.7 us
    ppermute x6, waiting for transfers between devices, step(): self.down.append(lax.ppermute(down, 'context', back))  8.24 us
    ppermute x6, starting transfers between devices, output(): part = lax.ppermute(part, ('context', 'tensor'), member(e, -d))  6.74 us
    ppermute x6, waiting for transfers between devices, output(): part = lax.ppermute(part, ('context', 'tensor'), member(e, -d))  4.4 us
    ppermute x2, waiting for transfers between devices, step(): lax.ppermute(up[:half], 'context', ahead)  4.23 us
    ppermute x6, starting transfers between devices, step(): self.down.append(lax.ppermute(down, 'context', back))  4.13 us
    all_to_all x1, starting transfers between devices, per_device(): lax.all_to_all(kv, 'context', split_axis=0, concat_axis=0, axis_index_gro...  3.8 us
  transfers between devices with their start and end apart: 29, of which 17 were waited for; matrix products, arithmetic and copies ran while one was open for 0% of the time, Pallas kernels for 5%

profile of v18, /device:TPU:1, one launch (start us, length us, event | category | flops | bytes accessed | tf_op | source)
XLA Modules:
  0.0 99.9 jit_solution(9527568917818888965)
XLA Ops:
  0.0 2.1 %collective-permute-start = (bf16[256,768]{1,0:T(8,128)(2,1)}, bf16[256,768]{1,0:T(8,128)(2,1)S(1)}, u32[]{:S(2)}, u32[]{:S(2)}) collective-permute-start(bf16[256,768]{1,0:T(8,128)(2,1)} %refs_4_), channel_id=1, source_target_pairs={{0,8},{2,6},{8,16},{10,2},{16,24},{18,10},{24,28},{26,18},{28,20},... | collective-permute-start | bytes 1179656 | tf_op jit(solution)/shard_map/ppermute | solution.py:322
  5.6 4.5 %collective-permute-done.refs_12_ = bf16[256,768]{1,0:T(8,128)(2,1)S(1)} collective-permute-done((bf16[256,768]{1,0:T(8,128)(2,1)}, bf16[256,768]{1,0:T(8,128)(2,1)S(1)}, u32[]{:S(2)}, u32[]{:S(2)}) %collective-permute-start) | collective-permute-done | bytes 393248 | tf_op jit(solution)/shard_map/ppermute | solution.py:322
  10.1 2.7 %collective-permute-done.1.refs_5_ = bf16[256,768]{1,0:T(8,128)(2,1)S(1)} collective-permute-done((bf16[256,768]{1,0:T(8,128)(2,1)}, bf16[256,768]{1,0:T(8,128)(2,1)S(1)}, u32[]{:S(2)}, u32[]{:S(2)}) %collective-permute-start.1) | collective-permute-done | bytes 393248 | tf_op jit(solution)/shard_map/ppermute | solution.py:323
  12.8 1.7 %collective-permute-start.2 = (bf16[256,768]{1,0:T(8,128)(2,1)S(1)}, bf16[256,768]{1,0:T(8,128)(2,1)S(1)}, u32[]{:S(2)}, u32[]{:S(2)}) collective-permute-start(bf16[256,768]{1,0:T(8,128)(2,1)S(1)} %collective-permute-done.refs_12_), channel_id=1, source_target_pairs={{0,8},{2,6},{8,16},{10,2},{16,24},{18,10},{24,28},{26,18},{28,20},... | collective-permute-start | bytes 1179656 | tf_op jit(solution)/shard_map/ppermute | solution.py:322
  16.7 1.9 %collective-permute-start.8 = (bf16[2,8,64,256]{3,2,1,0:T(8,128)(2,1)S(1)}, bf16[2,8,64,256]{3,2,1,0:T(8,128)(2,1)S(1)}, u32[]{:S(2)}, u32[]{:S(2)}) collective-permute-start(bf16[2,8,64,256]{3,2,1,0:T(8,128)(2,1)S(1)} %collective-permute-done.6.refs_1_), channel_id=1, source_target_pairs={{0,2},{2,0},{4,6},{6,4},{8,10},{10,8},{12,14},{14,12},{16,18},{18,... | collective-permute-start | bytes 1572872 | tf_op jit(solution)/shard_map/ppermute | solution.py:389
  19.8 3.0 %collective-permute-done.2.refs_11_ = bf16[256,768]{1,0:T(8,128)(2,1)S(1)} collective-permute-done((bf16[256,768]{1,0:T(8,128)(2,1)S(1)}, bf16[256,768]{1,0:T(8,128)(2,1)S(1)}, u32[]{:S(2)}, u32[]{:S(2)}) %collective-permute-start.2) | collective-permute-done | bytes 393248 | tf_op jit(solution)/shard_map/ppermute | solution.py:322
  24.3 1.7 %collective-permute-start.4 = (bf16[256,768]{1,0:T(8,128)(2,1)S(1)}, bf16[256,768]{1,0:T(8,128)(2,1)S(1)}, u32[]{:S(2)}, u32[]{:S(2)}) collective-permute-start(bf16[256,768]{1,0:T(8,128)(2,1)S(1)} %collective-permute-done.2.refs_11_), channel_id=1, source_target_pairs={{0,8},{2,6},{8,16},{10,2},{16,24},{18,10},{24,28},{26,18},{28,20},... | collective-permute-start | bytes 1179656 | tf_op jit(solution)/shard_map/ppermute | solution.py:322
  26.1 8.4 %collective-permute-done.4.refs_10_ = bf16[256,768]{1,0:T(8,128)(2,1)S(1)} collective-permute-done((bf16[256,768]{1,0:T(8,128)(2,1)S(1)}, bf16[256,768]{1,0:T(8,128)(2,1)S(1)}, u32[]{:S(2)}, u32[]{:S(2)}) %collective-permute-start.4) | collective-permute-done | bytes 393248 | tf_op jit(solution)/shard_map/ppermute | solution.py:322
  39.2 1.9 %collective-permute-done.10.refs_9_ = bf16[128,768]{1,0:T(8,128)(2,1)S(1)} collective-permute-done((bf16[128,768]{1,0:T(8,128)(2,1)S(1)}, bf16[128,768]{1,0:T(8,128)(2,1)S(1)}, u32[]{:S(2)}, u32[]{:S(2)}) %collective-permute-start.10) | collective-permute-done | bytes 196640 | tf_op jit(solution)/shard_map/ppermute | solution.py:328
  41.0 2.4 %collective-permute-done.9.refs_8_ = bf16[128,768]{1,0:T(8,128)(2,1)S(1)} collective-permute-done((bf16[128,768]{1,0:T(8,128)(2,1)S(1)}, bf16[128,768]{1,0:T(8,128)(2,1)S(1)}, u32[]{:S(2)}, u32[]{:S(2)}) %collective-permute-start.9) | collective-permute-done | bytes 196640 | tf_op jit(solution)/shard_map/ppermute | solution.py:327
  44.6 1.8 %collective-permute-start.12 = (f32[128,256]{1,0:T(8,128)S(1)}, f32[128,256]{1,0:T(8,128)S(1)}, u32[]{:S(2)}, u32[]{:S(2)}) collective-permute-start(f32[128,256]{1,0:T(8,128)S(1)} %get-tuple-element.131), channel_id=1, source_target_pairs={{0,2},{2,0},{4,6},{6,4},{8,10},{10,8},{12,14},{14,12},{16,18},{18,... | collective-permute-start | bytes 393224 | tf_op jit(solution)/shard_map/ppermute | solution.py:415
  46.3 2.6 %collective-permute-done.13.refs_1_ = bf16[512,256]{1,0:T(8,128)(2,1)S(1)} collective-permute-done((bf16[512,256]{1,0:T(8,128)(2,1)S(1)}, bf16[512,256]{1,0:T(8,128)(2,1)S(1)}, u32[]{:S(2)}, u32[]{:S(2)}) %collective-permute-start.13) | collective-permute-done | bytes 262176 | tf_op jit(solution)/shard_map/ppermute | solution.py:322
  49.8 3.8 %all-to-all-start = ((bf16[8,128,256]{2,1,0:T(8,128)(2,1)}), bf16[8,128,256]{2,1,0:T(8,128)(2,1)S(1)}, u32[]{:S(2)}, u32[]{:S(2)}) async-start(bf16[8,128,256]{2,1,0:T(8,128)(2,1)} %bitcast.1), calls=%async_computation | async-start | bytes 1048576 | tf_op jit(solution)/shard_map/all_to_all | solution.py:428
  54.2 1.7 %collective-permute-start.15 = (bf16[512,256]{1,0:T(8,128)(2,1)S(1)}, bf16[512,256]{1,0:T(8,128)(2,1)S(1)}, u32[]{:S(2)}, u32[]{:S(2)}) collective-permute-start(bf16[512,256]{1,0:T(8,128)(2,1)S(1)} %collective-permute-done.13.refs_1_), channel_id=1, source_target_pairs={{0,8},{2,6},{8,16},{10,2},{16,24},{18,10},{24,28},{26,18},{28,20},... | collective-permute-start | bytes 786440 | tf_op jit(solution)/shard_map/ppermute | solution.py:322
  56.0 13.2 %collective-permute-done.15.refs_0_ = bf16[512,256]{1,0:T(8,128)(2,1)S(1)} collective-permute-done((bf16[512,256]{1,0:T(8,128)(2,1)S(1)}, bf16[512,256]{1,0:T(8,128)(2,1)S(1)}, u32[]{:S(2)}, u32[]{:S(2)}) %collective-permute-start.15) | collective-permute-done | bytes 262176 | tf_op jit(solution)/shard_map/ppermute | solution.py:322
  69.2 2.5 %attend.1.mine_ref = f32[256,640]{1,0:T(8,128)S(1)} custom-call(f32[256,512]{1,0:T(8,128)S(1)} %get-tuple-element.124.mine_ref, f32[256,512]{1,0:T(8,128)S(1)} %collective-permute-done.11.theirs_ref, f32[256,128]{1,0:T(8,128)S(1)} %get-tuple-element.125.cosine_ref, f32[256,128]{1,0:T(8,128)S(1)} %get-tuple-element.126.sine_ref, ...), custom_call_target="tpu_custom_call" | custom-call | tf_op jit(solution)/shard_map/attend/pallas_call | solution.py:434
  71.7 1.8 %collective-permute-start.17 = (f32[256,640]{1,0:T(8,128)S(1)}, f32[256,640]{1,0:T(8,128)S(1)}, u32[]{:S(2)}, u32[]{:S(2)}) collective-permute-start(f32[256,640]{1,0:T(8,128)S(1)} %attend.1.mine_ref), channel_id=1, source_target_pairs={{0,2},{2,0},{4,6},{6,4},{8,10},{10,8},{12,14},{14,12},{16,18},{18,... | collective-permute-start | bytes 1966088 | tf_op jit(solution)/shard_map/ppermute | solution.py:452
  73.6 4.0 %collective-permute-start.18 = (bf16[512,256]{1,0:T(8,128)(2,1)S(1)}, bf16[512,256]{1,0:T(8,128)(2,1)S(1)}, u32[]{:S(2)}, u32[]{:S(2)}) collective-permute-start(bf16[512,256]{1,0:T(8,128)(2,1)S(1)} %collective-permute-done.16.refs_4_), channel_id=1, source_target_pairs={{8,0},{6,2},{16,8},{2,10},{24,16},{10,18},{28,24},{18,26},{20,28},... | collective-permute-start | bytes 786440 | tf_op jit(solution)/shard_map/ppermute | solution.py:323
  78.7 1.8 %collective-permute-start.22 = (bf16[5,64,256]{2,1,0:T(8,128)(2,1)S(1)}, bf16[5,64,256]{2,1,0:T(8,128)(2,1)S(1)}, u32[]{:S(2)}, u32[]{:S(2)}) collective-permute-start(bf16[5,64,256]{2,1,0:T(8,128)(2,1)S(1)} %get-tuple-element.164), channel_id=1, source_target_pairs={{0,1},{1,0},{2,3},{3,2},{4,5},{5,4},{6,7},{7,6},{8,9},{9,8},{10,11... | collective-permute-start | bytes 491528 | tf_op jit(solution)/shard_map/ppermute | solution.py:474
  80.5 2.6 %collective-permute-done.18.refs_0_ = bf16[512,256]{1,0:T(8,128)(2,1)S(1)} collective-permute-done((bf16[512,256]{1,0:T(8,128)(2,1)S(1)}, bf16[512,256]{1,0:T(8,128)(2,1)S(1)}, u32[]{:S(2)}, u32[]{:S(2)}) %collective-permute-start.18) | collective-permute-done | bytes 262176 | tf_op jit(solution)/shard_map/ppermute | solution.py:323
  86.8 1.6 %collective-permute-start.24 = (bf16[5,64,256]{2,1,0:T(8,128)(2,1)S(1)}, bf16[5,64,256]{2,1,0:T(8,128)(2,1)S(1)}, u32[]{:S(2)}, u32[]{:S(2)}) collective-permute-start(bf16[5,64,256]{2,1,0:T(8,128)(2,1)S(1)} %get-tuple-element.166), channel_id=1, source_target_pairs={{0,3},{1,2},{2,1},{3,0},{4,7},{5,6},{6,5},{7,4},{8,11},{9,10},{10,... | collective-permute-start | bytes 491528 | tf_op jit(solution)/shard_map/ppermute | solution.py:474
  88.9 1.8 %collective-permute-done.20.refs_1_ = bf16[256,256]{1,0:T(8,128)(2,1)S(1)} collective-permute-done((bf16[256,256]{1,0:T(8,128)(2,1)S(1)}, bf16[256,256]{1,0:T(8,128)(2,1)S(1)}, u32[]{:S(2)}, u32[]{:S(2)}) %collective-permute-start.20) | collective-permute-done | bytes 131104 | tf_op jit(solution)/shard_map/ppermute | solution.py:327
  91.6 1.8 %collective-permute-start.25 = (bf16[3,64,256]{2,1,0:T(8,128)(2,1)S(1)}, bf16[3,64,256]{2,1,0:T(8,128)(2,1)S(1)}, u32[]{:S(2)}, u32[]{:S(2)}) collective-permute-start(bf16[3,64,256]{2,1,0:T(8,128)(2,1)S(1)} %get-tuple-element.168), channel_id=1, source_target_pairs={{0,1},{1,0},{2,3},{3,2},{4,5},{5,4},{6,7},{7,6},{8,9},{9,8},{10,11... | collective-permute-start | bytes 294920 | tf_op jit(solution)/shard_map/ppermute | solution.py:474
  96.0 2.8 %collective-permute-done.27.refs_7_ = bf16[3,64,256]{2,1,0:T(8,128)(2,1)S(1)} collective-permute-done((bf16[3,64,256]{2,1,0:T(8,128)(2,1)S(1)}, bf16[3,64,256]{2,1,0:T(8,128)(2,1)S(1)}, u32[]{:S(2)}, u32[]{:S(2)}) %collective-permute-start.27) | collective-permute-done | bytes 98336 | tf_op jit(solution)/shard_map/ppermute | solution.py:474
  (60 shorter events, 25.6 us)
Async XLA Ops:
  0.0 10.1 %collective-permute-start = (bf16[256,768]{1,0:T(8,128)(2,1)}, bf16[256,768]{1,0:T(8,128)(2,1)S(1)}, u32[]{:S(2)}, u32[]{:S(2)}) collective-permute-start(bf16[256,768]{1,0:T(8,128)(2,1)} %refs_4_), channel_id=1, source_target_pairs={{0,8},{2,6},{8,16},{10,2},{16,24},{18,10},{24,28},{26,18},{28,20},... | collective-permute-start | bytes 1179656 | tf_op jit(solution)/shard_map/ppermute | solution.py:322
  2.1 10.7 %collective-permute-start.1 = (bf16[256,768]{1,0:T(8,128)(2,1)}, bf16[256,768]{1,0:T(8,128)(2,1)S(1)}, u32[]{:S(2)}, u32[]{:S(2)}) collective-permute-start(bf16[256,768]{1,0:T(8,128)(2,1)} %refs_4_), channel_id=1, source_target_pairs={{8,0},{6,2},{16,8},{2,10},{24,16},{10,18},{28,24},{18,26},{20,28},... | collective-permute-start | bytes 1179656 | tf_op jit(solution)/shard_map/ppermute | solution.py:323
  4.2 12.5 %collective-permute-start.6 = (bf16[2,8,64,256]{3,2,1,0:T(8,128)(2,1)S(1)}, bf16[2,8,64,256]{3,2,1,0:T(8,128)(2,1)S(1)}, u32[]{:S(2)}, u32[]{:S(2)}) collective-permute-start(bf16[2,8,64,256]{3,2,1,0:T(8,128)(2,1)S(1)} %norm.1.refs_0_), channel_id=1, source_target_pairs={{0,1},{1,0},{2,3},{3,2},{4,5},{5,4},{6,7},{7,6},{8,9},{9,8},{10,11... | collective-permute-start | bytes 1572872 | tf_op jit(solution)/shard_map/ppermute | solution.py:384
  12.8 10.0 %collective-permute-start.2 = (bf16[256,768]{1,0:T(8,128)(2,1)S(1)}, bf16[256,768]{1,0:T(8,128)(2,1)S(1)}, u32[]{:S(2)}, u32[]{:S(2)}) collective-permute-start(bf16[256,768]{1,0:T(8,128)(2,1)S(1)} %collective-permute-done.refs_12_), channel_id=1, source_target_pairs={{0,8},{2,6},{8,16},{10,2},{16,24},{18,10},{24,28},{26,18},{28,20},... | collective-permute-start | bytes 1179656 | tf_op jit(solution)/shard_map/ppermute | solution.py:322
  14.6 9.8 %collective-permute-start.3 = (bf16[256,768]{1,0:T(8,128)(2,1)S(1)}, bf16[256,768]{1,0:T(8,128)(2,1)S(1)}, u32[]{:S(2)}, u32[]{:S(2)}) collective-permute-start(bf16[256,768]{1,0:T(8,128)(2,1)S(1)} %collective-permute-done.1.refs_5_), channel_id=1, source_target_pairs={{8,0},{6,2},{16,8},{2,10},{24,16},{10,18},{28,24},{18,26},{20,28},... | collective-permute-start | bytes 1179656 | tf_op jit(solution)/shard_map/ppermute | solution.py:323
  14.6 11.5 %collective-permute-start.7 = (bf16[2,8,64,256]{3,2,1,0:T(8,128)(2,1)S(1)}, bf16[2,8,64,256]{3,2,1,0:T(8,128)(2,1)S(1)}, u32[]{:S(2)}, u32[]{:S(2)}) collective-permute-start(bf16[2,8,64,256]{3,2,1,0:T(8,128)(2,1)S(1)} %norm.1.refs_0_), channel_id=1, source_target_pairs={{0,2},{2,0},{4,6},{6,4},{8,10},{10,8},{12,14},{14,12},{16,18},{18,... | collective-permute-start | bytes 1572872 | tf_op jit(solution)/shard_map/ppermute | solution.py:389
  16.7 9.4 %collective-permute-start.8 = (bf16[2,8,64,256]{3,2,1,0:T(8,128)(2,1)S(1)}, bf16[2,8,64,256]{3,2,1,0:T(8,128)(2,1)S(1)}, u32[]{:S(2)}, u32[]{:S(2)}) collective-permute-start(bf16[2,8,64,256]{3,2,1,0:T(8,128)(2,1)S(1)} %collective-permute-done.6.refs_1_), channel_id=1, source_target_pairs={{0,2},{2,0},{4,6},{6,4},{8,10},{10,8},{12,14},{14,12},{16,18},{18,... | collective-permute-start | bytes 1572872 | tf_op jit(solution)/shard_map/ppermute | solution.py:389
  24.3 10.1 %collective-permute-start.4 = (bf16[256,768]{1,0:T(8,128)(2,1)S(1)}, bf16[256,768]{1,0:T(8,128)(2,1)S(1)}, u32[]{:S(2)}, u32[]{:S(2)}) collective-permute-start(bf16[256,768]{1,0:T(8,128)(2,1)S(1)} %collective-permute-done.2.refs_11_), channel_id=1, source_target_pairs={{0,8},{2,6},{8,16},{10,2},{16,24},{18,10},{24,28},{26,18},{28,20},... | collective-permute-start | bytes 1179656 | tf_op jit(solution)/shard_map/ppermute | solution.py:322
  26.1 9.7 %collective-permute-start.5 = (bf16[256,768]{1,0:T(8,128)(2,1)S(1)}, bf16[256,768]{1,0:T(8,128)(2,1)S(1)}, u32[]{:S(2)}, u32[]{:S(2)}) collective-permute-start(bf16[256,768]{1,0:T(8,128)(2,1)S(1)} %collective-permute-done.3.refs_6_), channel_id=1, source_target_pairs={{8,0},{6,2},{16,8},{2,10},{24,16},{10,18},{28,24},{18,26},{20,28},... | collective-permute-start | bytes 1179656 | tf_op jit(solution)/shard_map/ppermute | solution.py:323
  35.8 5.2 %collective-permute-start.10 = (bf16[128,768]{1,0:T(8,128)(2,1)S(1)}, bf16[128,768]{1,0:T(8,128)(2,1)S(1)}, u32[]{:S(2)}, u32[]{:S(2)}) collective-permute-start(bf16[128,768]{1,0:T(8,128)(2,1)S(1)} %slice.13), channel_id=1, source_target_pairs={{8,0},{6,2},{16,8},{2,10},{24,16},{10,18},{28,24},{18,26},{20,28},... | collective-permute-start | bytes 589832 | tf_op jit(solution)/shard_map/ppermute | solution.py:328
  37.3 6.2 %collective-permute-start.9 = (bf16[128,768]{1,0:T(8,128)(2,1)S(1)}, bf16[128,768]{1,0:T(8,128)(2,1)S(1)}, u32[]{:S(2)}, u32[]{:S(2)}) collective-permute-start(bf16[128,768]{1,0:T(8,128)(2,1)S(1)} %slice.12), channel_id=1, source_target_pairs={{0,8},{2,6},{8,16},{10,2},{16,24},{18,10},{24,28},{26,18},{28,20},... | collective-permute-start | bytes 589832 | tf_op jit(solution)/shard_map/ppermute | solution.py:327
  37.7 11.2 %collective-permute-start.13 = (bf16[512,256]{1,0:T(8,128)(2,1)S(1)}, bf16[512,256]{1,0:T(8,128)(2,1)S(1)}, u32[]{:S(2)}, u32[]{:S(2)}) collective-permute-start(bf16[512,256]{1,0:T(8,128)(2,1)S(1)} %copy-done.2), channel_id=1, source_target_pairs={{0,8},{2,6},{8,16},{10,2},{16,24},{18,10},{24,28},{26,18},{28,20},... | collective-permute-start | bytes 786440 | tf_op jit(solution)/shard_map/ppermute | solution.py:322
  39.1 9.8 %collective-permute-start.14 = (bf16[512,256]{1,0:T(8,128)(2,1)S(1)}, bf16[512,256]{1,0:T(8,128)(2,1)S(1)}, u32[]{:S(2)}, u32[]{:S(2)}) collective-permute-start(bf16[512,256]{1,0:T(8,128)(2,1)S(1)} %copy-done.2), channel_id=1, source_target_pairs={{8,0},{6,2},{16,8},{2,10},{24,16},{10,18},{28,24},{18,26},{20,28},... | collective-permute-start | bytes 786440 | tf_op jit(solution)/shard_map/ppermute | solution.py:323
  49.8 19.4 %all-to-all-start = ((bf16[8,128,256]{2,1,0:T(8,128)(2,1)}), bf16[8,128,256]{2,1,0:T(8,128)(2,1)S(1)}, u32[]{:S(2)}, u32[]{:S(2)}) async-start(bf16[8,128,256]{2,1,0:T(8,128)(2,1)} %bitcast.1), calls=%async_computation | async-start | bytes 1048576 | tf_op jit(solution)/shard_map/all_to_all | solution.py:428
  53.6 15.6 %collective-permute-start.11 = (f32[256,512]{1,0:T(8,128)S(1)}, f32[256,512]{1,0:T(8,128)S(1)}, u32[]{:S(2)}, u32[]{:S(2)}) collective-permute-start(f32[256,512]{1,0:T(8,128)S(1)} %get-tuple-element.124.mine_ref), channel_id=1, source_target_pairs={{0,2},{2,0},{4,6},{6,4},{8,10},{10,8},{12,14},{14,12},{16,18},{18,... | collective-permute-start | bytes 1572872 | tf_op jit(solution)/shard_map/ppermute | solution.py:416
  54.2 14.9 %collective-permute-start.15 = (bf16[512,256]{1,0:T(8,128)(2,1)S(1)}, bf16[512,256]{1,0:T(8,128)(2,1)S(1)}, u32[]{:S(2)}, u32[]{:S(2)}) collective-permute-start(bf16[512,256]{1,0:T(8,128)(2,1)S(1)} %collective-permute-done.13.refs_1_), channel_id=1, source_target_pairs={{0,8},{2,6},{8,16},{10,2},{16,24},{18,10},{24,28},{26,18},{28,20},... | collective-permute-start | bytes 786440 | tf_op jit(solution)/shard_map/ppermute | solution.py:322
  56.0 13.2 %collective-permute-start.16 = (bf16[512,256]{1,0:T(8,128)(2,1)S(1)}, bf16[512,256]{1,0:T(8,128)(2,1)S(1)}, u32[]{:S(2)}, u32[]{:S(2)}) collective-permute-start(bf16[512,256]{1,0:T(8,128)(2,1)S(1)} %collective-permute-done.14.refs_3_), channel_id=1, source_target_pairs={{8,0},{6,2},{16,8},{2,10},{24,16},{10,18},{28,24},{18,26},{20,28},... | collective-permute-start | bytes 786440 | tf_op jit(solution)/shard_map/ppermute | solution.py:323
  71.7 5.8 %collective-permute-start.17 = (f32[256,640]{1,0:T(8,128)S(1)}, f32[256,640]{1,0:T(8,128)S(1)}, u32[]{:S(2)}, u32[]{:S(2)}) collective-permute-start(f32[256,640]{1,0:T(8,128)S(1)} %attend.1.mine_ref), channel_id=1, source_target_pairs={{0,2},{2,0},{4,6},{6,4},{8,10},{10,8},{12,14},{14,12},{16,18},{18,... | collective-permute-start | bytes 1966088 | tf_op jit(solution)/shard_map/ppermute | solution.py:452
  73.6 9.6 %collective-permute-start.18 = (bf16[512,256]{1,0:T(8,128)(2,1)S(1)}, bf16[512,256]{1,0:T(8,128)(2,1)S(1)}, u32[]{:S(2)}, u32[]{:S(2)}) collective-permute-start(bf16[512,256]{1,0:T(8,128)(2,1)S(1)} %collective-permute-done.16.refs_4_), channel_id=1, source_target_pairs={{8,0},{6,2},{16,8},{2,10},{24,16},{10,18},{28,24},{18,26},{20,28},... | collective-permute-start | bytes 786440 | tf_op jit(solution)/shard_map/ppermute | solution.py:323
  77.6 7.1 %collective-permute-start.19 = (bf16[512,256]{1,0:T(8,128)(2,1)S(1)}, bf16[512,256]{1,0:T(8,128)(2,1)S(1)}, u32[]{:S(2)}, u32[]{:S(2)}) collective-permute-start(bf16[512,256]{1,0:T(8,128)(2,1)S(1)} %collective-permute-done.15.refs_0_), channel_id=1, source_target_pairs={{0,8},{2,6},{8,16},{10,2},{16,24},{18,10},{24,28},{26,18},{28,20},... | collective-permute-start | bytes 786440 | tf_op jit(solution)/shard_map/ppermute | solution.py:322
  78.7 15.7 %collective-permute-start.22 = (bf16[5,64,256]{2,1,0:T(8,128)(2,1)S(1)}, bf16[5,64,256]{2,1,0:T(8,128)(2,1)S(1)}, u32[]{:S(2)}, u32[]{:S(2)}) collective-permute-start(bf16[5,64,256]{2,1,0:T(8,128)(2,1)S(1)} %get-tuple-element.164), channel_id=1, source_target_pairs={{0,1},{1,0},{2,3},{3,2},{4,5},{5,4},{6,7},{7,6},{8,9},{9,8},{10,11... | collective-permute-start | bytes 491528 | tf_op jit(solution)/shard_map/ppermute | solution.py:474
  85.6 5.0 %collective-permute-start.20 = (bf16[256,256]{1,0:T(8,128)(2,1)S(1)}, bf16[256,256]{1,0:T(8,128)(2,1)S(1)}, u32[]{:S(2)}, u32[]{:S(2)}) collective-permute-start(bf16[256,256]{1,0:T(8,128)(2,1)S(1)} %slice.14), channel_id=1, source_target_pairs={{0,8},{2,6},{8,16},{10,2},{16,24},{18,10},{24,28},{26,18},{28,20},... | collective-permute-start | bytes 393224 | tf_op jit(solution)/shard_map/ppermute | solution.py:327
  86.2 8.2 %collective-permute-start.23 = (bf16[5,64,256]{2,1,0:T(8,128)(2,1)S(1)}, bf16[5,64,256]{2,1,0:T(8,128)(2,1)S(1)}, u32[]{:S(2)}, u32[]{:S(2)}) collective-permute-start(bf16[5,64,256]{2,1,0:T(8,128)(2,1)S(1)} %get-tuple-element.165), channel_id=1, source_target_pairs={{0,2},{1,3},{2,0},{3,1},{4,6},{5,7},{6,4},{7,5},{8,10},{9,11},{10,... | collective-permute-start | bytes 491528 | tf_op jit(solution)/shard_map/ppermute | solution.py:474
  86.8 7.6 %collective-permute-start.24 = (bf16[5,64,256]{2,1,0:T(8,128)(2,1)S(1)}, bf16[5,64,256]{2,1,0:T(8,128)(2,1)S(1)}, u32[]{:S(2)}, u32[]{:S(2)}) collective-permute-start(bf16[5,64,256]{2,1,0:T(8,128)(2,1)S(1)} %get-tuple-element.166), channel_id=1, source_target_pairs={{0,3},{1,2},{2,1},{3,0},{4,7},{5,6},{6,5},{7,4},{8,11},{9,10},{10,... | collective-permute-start | bytes 491528 | tf_op jit(solution)/shard_map/ppermute | solution.py:474
  (12 other events, 91.2 us)

commit v19 on v14

--- a/solution.py
+++ b/solution.py
@@ -90,7 +90,7 @@
         orig_ref[:, chip * rows : (chip + 1) * rows] = initial(owner, inside)
 
 
-def norm_kernel(place, chips, hidden_ref, gain_ref, out_ref):
+def norm_kernel(place, chips, hidden_ref, gain_ref, own_ref, other_ref):
     at, core = place_of(place)
     wide = hidden_ref[...].astype(jnp.float32)
     meansq = jnp.mean(wide * wide, axis=-1, keepdims=True)
@@ -106,7 +106,7 @@
         ],
         axis=1,
     )
-    block = out_ref.shape[3]
+    block = own_ref.shape[2]
     for even in range(2):
 
         @pl.when(core == even)
@@ -115,7 +115,8 @@
                 slot = lax.rem(place[chip] + chips - at, chips)
                 for side in range(2):
                     column = (2 * chip + side) * block
-                    out_ref[side ^ even, slot] = normed[:, column : column + block]
+                    ref = own_ref if side == even else other_ref
+                    ref[slot] = normed[:, column : column + block]
 
 
 def take_ring(refs, chips):
@@ -131,13 +132,10 @@
 def project_kernel(chips, groups, *refs):
     rows_refs, refs = refs[:groups], refs[groups:]
     weight_refs, (mine_ref, theirs_ref, queries_ref) = refs[:-3], refs[-3:]
-    half = groups // 2
     weights = take_ring(weight_refs, chips)
     total = None
     for slot in range(chips):
-        rows = jnp.concatenate(
-            [ref[group // half, slot] for group, ref in enumerate(rows_refs)], axis=0
-        )
+        rows = jnp.concatenate([ref[slot] for ref in rows_refs], axis=0)
         start = 0
         for ref in weights[slot]:
             depth = ref.shape[0]
@@ -364,23 +362,29 @@
 
     qkv_ring = Ring(w_qkv)
     qkv_ring.step()
-    normed = pl.pallas_call(
+    own, other = pl.pallas_call(
         functools.partial(norm_kernel, place, chips),
-        out_shape=jax.ShapeDtypeStruct((2, chips, rows_here, block), jnp.bfloat16),
+        out_shape=[jax.ShapeDtypeStruct((chips, rows_here, block), jnp.bfloat16)] * 2,
         in_specs=vmem_specs(2),
-        out_specs=vmem_specs(1)[0],
+        out_specs=vmem_specs(2),
         compiler_params=compute_params(),
         name="norm",
     )(hidden_rows, norm_gain.reshape(-1, HD))
-    normed = [normed] + [
-        lax.ppermute(
-            normed, "tensor", [(t, (t - d) % n_tensor) for t in range(n_tensor)]
-        )
-        for d in range(1, n_tensor)
-    ]
-    normed += [lax.ppermute(rows, "context", sibling) for rows in normed]
+
+    def from_tensor(rows):
+        return [rows] + [
+            lax.ppermute(rows, "tensor", [(t, (t - d) % n_tensor) for t in range(n_tensor)])
+            for d in range(1, n_tensor)
+        ]
+
+    other = from_tensor(other)
+    normed = from_tensor(own)
+    normed += [lax.ppermute(rows, "context", sibling) for rows in other]
 
     qkv_ring.step()
+    cosine, sine, query_start, query_orig, key_orig = ordered(
+        (cosine, sine, query_start, query_orig, key_orig)
+    )
     qkv_ring.step()
     normed = qkv_ring.step(normed)
     while not qkv_ring.done():

time: 95.7 us -> 99.4 us (1.039)
  waiting for transfers between devices: 44.3 us -> 46.7 us
  starting transfers between devices: 39.8 us -> 41.1 us
    ppermute x3 -> x4, waiting for transfers between devices: 0.82 us -> 6.45 us  [the longest x2 6.44 us: from_tensor(): lax.ppermute(rows, 'tensor', [(t, (t - d) % n_tensor) for t in range(n_te...]
    ppermute x6, waiting for transfers between devices: 26.5 us -> 23.2 us  [step(): self.up.append(lax.ppermute(up, 'context', ahead))]
    ppermute x1, starting transfers between devices: 6.09 us -> 3.49 us  [per_device(): theirs = lax.ppermute(theirs, 'context', sibling)]
    ppermute x1, starting transfers between devices: 0.64 us -> 2.17 us  [per_device(): queries_theirs = lax.ppermute(queries, 'context', sibling)]
    ppermute x2, waiting for transfers between devices: 1.59 us -> 2.89 us  [step(): lax.ppermute(down[half:], 'context', back)]
    ppermute x1, starting transfers between devices: 1.14 us -> 2.27 us  [per_device(): mixed_theirs = lax.ppermute(mixed, 'context', sibling)]
    all_to_all x1, starting transfers between devices: 3.49 us -> 4.54 us  [per_device(): lax.all_to_all(kv, 'context', split_axis=0, concat_axis=0, axis_index_gro...]
    ppermute x3 -> x4, starting transfers between devices: 5.74 us -> 6.4 us  [the longest x2 3.91 us: per_device(): normed += [lax.ppermute(rows, 'context', sibling) for rows in other]]
  transfers between devices with their start and end apart: 29 -> 30, of which waited for: 19 -> 16; matrix products, arithmetic and copies ran while one was open for 0% -> 0% of each run, Pallas kernels for 5% -> 5%
where the time goes in v19:
time: 99.4 us; the launch traced here: 99 us
  waiting for transfers between devices  46.7 us (47%)
  starting transfers between devices  41.1 us (41%)
  Pallas kernels  9.22 us (9%)
  local copies, waits for them, and re-layouts  1.82 us (2%)
    ppermute x6, waiting for transfers between devices, step(): self.up.append(lax.ppermute(up, 'context', ahead))  23.2 us
    ppermute x6, starting transfers between devices, step(): self.up.append(lax.ppermute(up, 'context', ahead))  10.1 us
    ppermute x6, waiting for transfers between devices, step(): self.down.append(lax.ppermute(down, 'context', back))  8.68 us
    ppermute x6, starting transfers between devices, output(): part = lax.ppermute(part, ('context', 'tensor'), member(e, -d))  7.8 us
    ppermute x2, waiting for transfers between devices, from_tensor(): lax.ppermute(rows, 'tensor', [(t, (t - d) % n_tensor) for t in range(n_te...  6.44 us
    all_to_all x1, starting transfers between devices, per_device(): lax.all_to_all(kv, 'context', split_axis=0, concat_axis=0, axis_index_gro...  4.54 us
    ppermute x6, waiting for transfers between devices, output(): part = lax.ppermute(part, ('context', 'tensor'), member(e, -d))  4.39 us
    ppermute x2, starting transfers between devices, per_device(): normed += [lax.ppermute(rows, 'context', sibling) for rows in other]  3.91 us
  transfers between devices with their start and end apart: 30, of which 16 were waited for; matrix products, arithmetic and copies ran while one was open for 0% of the time, Pallas kernels for 5%

profile of v19, /device:TPU:1, one launch (start us, length us, event | category | flops | bytes accessed | tf_op | source)
XLA Modules:
  0.0 99.0 jit_solution(14582679821461643615)
XLA Ops:
  0.0 2.1 %collective-permute-start = (bf16[256,768]{1,0:T(8,128)(2,1)}, bf16[256,768]{1,0:T(8,128)(2,1)S(1)}, u32[]{:S(2)}, u32[]{:S(2)}) collective-permute-start(bf16[256,768]{1,0:T(8,128)(2,1)} %refs_4_), channel_id=1, source_target_pairs={{0,8},{2,10},{8,16},{10,18},{16,24},{18,26},{24,28},{26,30},{28,20... | collective-permute-start | bytes 1179656 | tf_op jit(solution)/shard_map/ppermute | solution.py:312
  2.1 9.0 %collective-permute-done.refs_12_ = bf16[256,768]{1,0:T(8,128)(2,1)S(1)} collective-permute-done((bf16[256,768]{1,0:T(8,128)(2,1)}, bf16[256,768]{1,0:T(8,128)(2,1)S(1)}, u32[]{:S(2)}, u32[]{:S(2)}) %collective-permute-start) | collective-permute-done | bytes 393248 | tf_op jit(solution)/shard_map/ppermute | solution.py:312
  12.0 1.3 %collective-permute-start.2 = (bf16[256,768]{1,0:T(8,128)(2,1)S(1)}, bf16[256,768]{1,0:T(8,128)(2,1)S(1)}, u32[]{:S(2)}, u32[]{:S(2)}) collective-permute-start(bf16[256,768]{1,0:T(8,128)(2,1)S(1)} %collective-permute-done.refs_12_), channel_id=1, source_target_pairs={{0,8},{2,10},{8,16},{10,18},{16,24},{18,26},{24,28},{26,30},{28,20... | collective-permute-start | bytes 1179656 | tf_op jit(solution)/shard_map/ppermute | solution.py:312
  18.1 2.7 %collective-permute-done.2.refs_11_ = bf16[256,768]{1,0:T(8,128)(2,1)S(1)} collective-permute-done((bf16[256,768]{1,0:T(8,128)(2,1)S(1)}, bf16[256,768]{1,0:T(8,128)(2,1)S(1)}, u32[]{:S(2)}, u32[]{:S(2)}) %collective-permute-start.2) | collective-permute-done | bytes 393248 | tf_op jit(solution)/shard_map/ppermute | solution.py:312
  21.8 1.3 %collective-permute-start.4 = (bf16[256,768]{1,0:T(8,128)(2,1)S(1)}, bf16[256,768]{1,0:T(8,128)(2,1)S(1)}, u32[]{:S(2)}, u32[]{:S(2)}) collective-permute-start(bf16[256,768]{1,0:T(8,128)(2,1)S(1)} %collective-permute-done.2.refs_11_), channel_id=1, source_target_pairs={{0,8},{2,10},{8,16},{10,18},{16,24},{18,26},{24,28},{26,30},{28,20... | collective-permute-start | bytes 1179656 | tf_op jit(solution)/shard_map/ppermute | solution.py:312
  23.2 3.6 %collective-permute-start.7 = (bf16[8,64,256]{2,1,0:T(8,128)(2,1)S(1)}, bf16[8,64,256]{2,1,0:T(8,128)(2,1)S(1)}, u32[]{:S(2)}, u32[]{:S(2)}) collective-permute-start(bf16[8,64,256]{2,1,0:T(8,128)(2,1)S(1)} %get-tuple-element.105), channel_id=1, source_target_pairs={{0,2},{2,0},{4,6},{6,4},{8,10},{10,8},{12,14},{14,12},{16,18},{18,... | collective-permute-start | bytes 786440 | tf_op jit(solution)/shard_map/ppermute | solution.py:382
  28.4 6.4 %collective-permute-done.6.refs_1_ = bf16[8,64,256]{2,1,0:T(8,128)(2,1)S(1)} collective-permute-done((bf16[8,64,256]{2,1,0:T(8,128)(2,1)S(1)}, bf16[8,64,256]{2,1,0:T(8,128)(2,1)S(1)}, u32[]{:S(2)}, u32[]{:S(2)}) %collective-permute-start.6) | collective-permute-done | bytes 262176 | tf_op jit(solution)/shard_map/ppermute | solution.py:376
  35.1 1.3 %collective-permute-start.10 = (bf16[128,768]{1,0:T(8,128)(2,1)S(1)}, bf16[128,768]{1,0:T(8,128)(2,1)S(1)}, u32[]{:S(2)}, u32[]{:S(2)}) collective-permute-start(bf16[128,768]{1,0:T(8,128)(2,1)S(1)} %slice.12), channel_id=1, source_target_pairs={{0,8},{2,10},{8,16},{10,18},{16,24},{18,26},{24,28},{26,30},{28,20... | collective-permute-start | bytes 589832 | tf_op jit(solution)/shard_map/ppermute | solution.py:317
  36.4 1.3 %collective-permute-start.14 = (bf16[512,256]{1,0:T(8,128)(2,1)S(1)}, bf16[512,256]{1,0:T(8,128)(2,1)S(1)}, u32[]{:S(2)}, u32[]{:S(2)}) collective-permute-start(bf16[512,256]{1,0:T(8,128)(2,1)S(1)} %copy-done.2), channel_id=1, source_target_pairs={{0,8},{2,10},{8,16},{10,18},{16,24},{18,26},{24,28},{26,30},{28,20... | collective-permute-start | bytes 786440 | tf_op jit(solution)/shard_map/ppermute | solution.py:312
  37.9 2.7 %collective-permute-done.11.refs_9_ = bf16[128,768]{1,0:T(8,128)(2,1)S(1)} collective-permute-done((bf16[128,768]{1,0:T(8,128)(2,1)S(1)}, bf16[128,768]{1,0:T(8,128)(2,1)S(1)}, u32[]{:S(2)}, u32[]{:S(2)}) %collective-permute-start.11) | collective-permute-done | bytes 196640 | tf_op jit(solution)/shard_map/ppermute | solution.py:318
  41.7 3.5 %collective-permute-start.13 = (f32[128,256]{1,0:T(8,128)S(1)}, f32[128,256]{1,0:T(8,128)S(1)}, u32[]{:S(2)}, u32[]{:S(2)}) collective-permute-start(f32[128,256]{1,0:T(8,128)S(1)} %get-tuple-element.135), channel_id=1, source_target_pairs={{0,2},{2,0},{4,6},{6,4},{8,10},{10,8},{12,14},{14,12},{16,18},{18,... | collective-permute-start | bytes 393224 | tf_op jit(solution)/shard_map/ppermute | solution.py:408
  47.1 4.5 %all-to-all-start = ((bf16[8,128,256]{2,1,0:T(8,128)(2,1)}), bf16[8,128,256]{2,1,0:T(8,128)(2,1)S(1)}, u32[]{:S(2)}, u32[]{:S(2)}) async-start(bf16[8,128,256]{2,1,0:T(8,128)(2,1)} %bitcast.1), calls=%async_computation | async-start | bytes 1048576 | tf_op jit(solution)/shard_map/all_to_all | solution.py:421
  51.6 2.2 %collective-permute-start.12 = (f32[256,512]{1,0:T(8,128)S(1)}, f32[256,512]{1,0:T(8,128)S(1)}, u32[]{:S(2)}, u32[]{:S(2)}) collective-permute-start(f32[256,512]{1,0:T(8,128)S(1)} %get-tuple-element.128.mine_ref), channel_id=1, source_target_pairs={{0,2},{2,0},{4,6},{6,4},{8,10},{10,8},{12,14},{14,12},{16,18},{18,... | collective-permute-start | bytes 1572872 | tf_op jit(solution)/shard_map/ppermute | solution.py:409
  53.8 1.7 %collective-permute-start.16 = (bf16[512,256]{1,0:T(8,128)(2,1)S(1)}, bf16[512,256]{1,0:T(8,128)(2,1)S(1)}, u32[]{:S(2)}, u32[]{:S(2)}) collective-permute-start(bf16[512,256]{1,0:T(8,128)(2,1)S(1)} %collective-permute-done.14.refs_1_), channel_id=1, source_target_pairs={{0,8},{2,10},{8,16},{10,18},{16,24},{18,26},{24,28},{26,30},{28,20... | collective-permute-start | bytes 786440 | tf_op jit(solution)/shard_map/ppermute | solution.py:312
  55.6 9.7 %collective-permute-done.16.refs_0_ = bf16[512,256]{1,0:T(8,128)(2,1)S(1)} collective-permute-done((bf16[512,256]{1,0:T(8,128)(2,1)S(1)}, bf16[512,256]{1,0:T(8,128)(2,1)S(1)}, u32[]{:S(2)}, u32[]{:S(2)}) %collective-permute-start.16) | collective-permute-done | bytes 262176 | tf_op jit(solution)/shard_map/ppermute | solution.py:312
  65.2 2.4 %collective-permute-done.17.refs_4_ = bf16[512,256]{1,0:T(8,128)(2,1)S(1)} collective-permute-done((bf16[512,256]{1,0:T(8,128)(2,1)S(1)}, bf16[512,256]{1,0:T(8,128)(2,1)S(1)}, u32[]{:S(2)}, u32[]{:S(2)}) %collective-permute-start.17) | collective-permute-done | bytes 262176 | tf_op jit(solution)/shard_map/ppermute | solution.py:313
  67.7 2.5 %attend.1.mine_ref = f32[256,640]{1,0:T(8,128)S(1)} custom-call(f32[256,512]{1,0:T(8,128)S(1)} %get-tuple-element.128.mine_ref, f32[256,512]{1,0:T(8,128)S(1)} %collective-permute-done.12.theirs_ref, f32[256,128]{1,0:T(8,128)S(1)} %get-tuple-element.129.cosine_ref, f32[256,128]{1,0:T(8,128)S(1)} %get-tuple-element.130.sine_ref, ...), custom_call_target="tpu_custom_call" | custom-call | tf_op jit(solution)/shard_map/attend/pallas_call | solution.py:427
  70.2 2.3 %collective-permute-start.18 = (f32[256,640]{1,0:T(8,128)S(1)}, f32[256,640]{1,0:T(8,128)S(1)}, u32[]{:S(2)}, u32[]{:S(2)}) collective-permute-start(f32[256,640]{1,0:T(8,128)S(1)} %attend.1.mine_ref), channel_id=1, source_target_pairs={{0,2},{2,0},{4,6},{6,4},{8,10},{10,8},{12,14},{14,12},{16,18},{18,... | collective-permute-start | bytes 1966088 | tf_op jit(solution)/shard_map/ppermute | solution.py:445
  73.2 2.4 %collective-permute-start.20 = (bf16[512,256]{1,0:T(8,128)(2,1)S(1)}, bf16[512,256]{1,0:T(8,128)(2,1)S(1)}, u32[]{:S(2)}, u32[]{:S(2)}) collective-permute-start(bf16[512,256]{1,0:T(8,128)(2,1)S(1)} %collective-permute-done.16.refs_0_), channel_id=1, source_target_pairs={{0,8},{2,10},{8,16},{10,18},{16,24},{18,26},{24,28},{26,30},{28,20... | collective-permute-start | bytes 786440 | tf_op jit(solution)/shard_map/ppermute | solution.py:312
  78.0 4.2 %collective-permute-done.19.refs_0_ = bf16[512,256]{1,0:T(8,128)(2,1)S(1)} collective-permute-done((bf16[512,256]{1,0:T(8,128)(2,1)S(1)}, bf16[512,256]{1,0:T(8,128)(2,1)S(1)}, u32[]{:S(2)}, u32[]{:S(2)}) %collective-permute-start.19) | collective-permute-done | bytes 262176 | tf_op jit(solution)/shard_map/ppermute | solution.py:313
  84.7 1.4 %collective-permute-start.24 = (bf16[5,64,256]{2,1,0:T(8,128)(2,1)S(1)}, bf16[5,64,256]{2,1,0:T(8,128)(2,1)S(1)}, u32[]{:S(2)}, u32[]{:S(2)}) collective-permute-start(bf16[5,64,256]{2,1,0:T(8,128)(2,1)S(1)} %get-tuple-element.169), channel_id=1, source_target_pairs={{0,2},{1,3},{2,0},{3,1},{4,6},{5,7},{6,4},{7,5},{8,10},{9,11},{10,... | collective-permute-start | bytes 491528 | tf_op jit(solution)/shard_map/ppermute | solution.py:467
  89.5 1.3 %collective-permute-start.26 = (bf16[3,64,256]{2,1,0:T(8,128)(2,1)S(1)}, bf16[3,64,256]{2,1,0:T(8,128)(2,1)S(1)}, u32[]{:S(2)}, u32[]{:S(2)}) collective-permute-start(bf16[3,64,256]{2,1,0:T(8,128)(2,1)S(1)} %get-tuple-element.172), channel_id=1, source_target_pairs={{0,1},{1,0},{2,3},{3,2},{4,5},{5,4},{6,7},{7,6},{8,9},{9,8},{10,11... | collective-permute-start | bytes 294920 | tf_op jit(solution)/shard_map/ppermute | solution.py:467
  90.8 2.6 %collective-permute-start.27 = (bf16[3,64,256]{2,1,0:T(8,128)(2,1)S(1)}, bf16[3,64,256]{2,1,0:T(8,128)(2,1)S(1)}, u32[]{:S(2)}, u32[]{:S(2)}) collective-permute-start(bf16[3,64,256]{2,1,0:T(8,128)(2,1)S(1)} %get-tuple-element.173), channel_id=1, source_target_pairs={{0,2},{1,3},{2,0},{3,1},{4,6},{5,7},{6,4},{7,5},{8,10},{9,11},{10,... | collective-permute-start | bytes 294920 | tf_op jit(solution)/shard_map/ppermute | solution.py:467
  94.3 3.6 %collective-permute-done.28.refs_7_ = bf16[3,64,256]{2,1,0:T(8,128)(2,1)S(1)} collective-permute-done((bf16[3,64,256]{2,1,0:T(8,128)(2,1)S(1)}, bf16[3,64,256]{2,1,0:T(8,128)(2,1)S(1)}, u32[]{:S(2)}, u32[]{:S(2)}) %collective-permute-start.28) | collective-permute-done | bytes 98336 | tf_op jit(solution)/shard_map/ppermute | solution.py:467
  (62 shorter events, 22.8 us)
Async XLA Ops:
  0.0 11.1 %collective-permute-start = (bf16[256,768]{1,0:T(8,128)(2,1)}, bf16[256,768]{1,0:T(8,128)(2,1)S(1)}, u32[]{:S(2)}, u32[]{:S(2)}) collective-permute-start(bf16[256,768]{1,0:T(8,128)(2,1)} %refs_4_), channel_id=1, source_target_pairs={{0,8},{2,10},{8,16},{10,18},{16,24},{18,26},{24,28},{26,30},{28,20... | collective-permute-start | bytes 1179656 | tf_op jit(solution)/shard_map/ppermute | solution.py:312
  2.1 9.9 %collective-permute-start.1 = (bf16[256,768]{1,0:T(8,128)(2,1)}, bf16[256,768]{1,0:T(8,128)(2,1)S(1)}, u32[]{:S(2)}, u32[]{:S(2)}) collective-permute-start(bf16[256,768]{1,0:T(8,128)(2,1)} %refs_4_), channel_id=1, source_target_pairs={{8,0},{10,2},{16,8},{18,10},{24,16},{26,18},{28,24},{30,26},{20,28... | collective-permute-start | bytes 1179656 | tf_op jit(solution)/shard_map/ppermute | solution.py:313
  12.0 8.7 %collective-permute-start.2 = (bf16[256,768]{1,0:T(8,128)(2,1)S(1)}, bf16[256,768]{1,0:T(8,128)(2,1)S(1)}, u32[]{:S(2)}, u32[]{:S(2)}) collective-permute-start(bf16[256,768]{1,0:T(8,128)(2,1)S(1)} %collective-permute-done.refs_12_), channel_id=1, source_target_pairs={{0,8},{2,10},{8,16},{10,18},{16,24},{18,26},{24,28},{26,30},{28,20... | collective-permute-start | bytes 1179656 | tf_op jit(solution)/shard_map/ppermute | solution.py:312
  13.3 8.5 %collective-permute-start.3 = (bf16[256,768]{1,0:T(8,128)(2,1)S(1)}, bf16[256,768]{1,0:T(8,128)(2,1)S(1)}, u32[]{:S(2)}, u32[]{:S(2)}) collective-permute-start(bf16[256,768]{1,0:T(8,128)(2,1)S(1)} %collective-permute-done.1.refs_5_), channel_id=1, source_target_pairs={{8,0},{10,2},{16,8},{18,10},{24,16},{26,18},{28,24},{30,26},{20,28... | collective-permute-start | bytes 1179656 | tf_op jit(solution)/shard_map/ppermute | solution.py:313
  15.5 12.5 %collective-permute-start.8 = (bf16[8,64,256]{2,1,0:T(8,128)(2,1)S(1)}, bf16[8,64,256]{2,1,0:T(8,128)(2,1)S(1)}, u32[]{:S(2)}, u32[]{:S(2)}) collective-permute-start(bf16[8,64,256]{2,1,0:T(8,128)(2,1)S(1)} %get-tuple-element.105), channel_id=1, source_target_pairs={{0,1},{1,0},{2,3},{3,2},{4,5},{5,4},{6,7},{7,6},{8,9},{9,8},{10,11... | collective-permute-start | bytes 786440 | tf_op jit(solution)/shard_map/ppermute | solution.py:376
  21.8 13.0 %collective-permute-start.4 = (bf16[256,768]{1,0:T(8,128)(2,1)S(1)}, bf16[256,768]{1,0:T(8,128)(2,1)S(1)}, u32[]{:S(2)}, u32[]{:S(2)}) collective-permute-start(bf16[256,768]{1,0:T(8,128)(2,1)S(1)} %collective-permute-done.2.refs_11_), channel_id=1, source_target_pairs={{0,8},{2,10},{8,16},{10,18},{16,24},{18,26},{24,28},{26,30},{28,20... | collective-permute-start | bytes 1179656 | tf_op jit(solution)/shard_map/ppermute | solution.py:312
  23.1 11.8 %collective-permute-start.5 = (bf16[256,768]{1,0:T(8,128)(2,1)S(1)}, bf16[256,768]{1,0:T(8,128)(2,1)S(1)}, u32[]{:S(2)}, u32[]{:S(2)}) collective-permute-start(bf16[256,768]{1,0:T(8,128)(2,1)S(1)} %collective-permute-done.3.refs_6_), channel_id=1, source_target_pairs={{8,0},{10,2},{16,8},{18,10},{24,16},{26,18},{28,24},{30,26},{20,28... | collective-permute-start | bytes 1179656 | tf_op jit(solution)/shard_map/ppermute | solution.py:313
  23.2 11.6 %collective-permute-start.7 = (bf16[8,64,256]{2,1,0:T(8,128)(2,1)S(1)}, bf16[8,64,256]{2,1,0:T(8,128)(2,1)S(1)}, u32[]{:S(2)}, u32[]{:S(2)}) collective-permute-start(bf16[8,64,256]{2,1,0:T(8,128)(2,1)S(1)} %get-tuple-element.105), channel_id=1, source_target_pairs={{0,2},{2,0},{4,6},{6,4},{8,10},{10,8},{12,14},{14,12},{16,18},{18,... | collective-permute-start | bytes 786440 | tf_op jit(solution)/shard_map/ppermute | solution.py:382
  26.9 7.9 %collective-permute-start.6 = (bf16[8,64,256]{2,1,0:T(8,128)(2,1)S(1)}, bf16[8,64,256]{2,1,0:T(8,128)(2,1)S(1)}, u32[]{:S(2)}, u32[]{:S(2)}) collective-permute-start(bf16[8,64,256]{2,1,0:T(8,128)(2,1)S(1)} %get-tuple-element.115.refs_0_), channel_id=1, source_target_pairs={{0,1},{1,0},{2,3},{3,2},{4,5},{5,4},{6,7},{7,6},{8,9},{9,8},{10,11... | collective-permute-start | bytes 786440 | tf_op jit(solution)/shard_map/ppermute | solution.py:376
  28.1 6.7 %collective-permute-start.9 = (bf16[8,64,256]{2,1,0:T(8,128)(2,1)S(1)}, bf16[8,64,256]{2,1,0:T(8,128)(2,1)S(1)}, u32[]{:S(2)}, u32[]{:S(2)}) collective-permute-start(bf16[8,64,256]{2,1,0:T(8,128)(2,1)S(1)} %collective-permute-done.8), channel_id=1, source_target_pairs={{0,2},{2,0},{4,6},{6,4},{8,10},{10,8},{12,14},{14,12},{16,18},{18,... | collective-permute-start | bytes 786440 | tf_op jit(solution)/shard_map/ppermute | solution.py:382
  34.9 5.7 %collective-permute-start.11 = (bf16[128,768]{1,0:T(8,128)(2,1)S(1)}, bf16[128,768]{1,0:T(8,128)(2,1)S(1)}, u32[]{:S(2)}, u32[]{:S(2)}) collective-permute-start(bf16[128,768]{1,0:T(8,128)(2,1)S(1)} %slice.13), channel_id=1, source_target_pairs={{8,0},{10,2},{16,8},{18,10},{24,16},{26,18},{28,24},{30,26},{20,28... | collective-permute-start | bytes 589832 | tf_op jit(solution)/shard_map/ppermute | solution.py:318
  35.1 5.5 %collective-permute-start.10 = (bf16[128,768]{1,0:T(8,128)(2,1)S(1)}, bf16[128,768]{1,0:T(8,128)(2,1)S(1)}, u32[]{:S(2)}, u32[]{:S(2)}) collective-permute-start(bf16[128,768]{1,0:T(8,128)(2,1)S(1)} %slice.12), channel_id=1, source_target_pairs={{0,8},{2,10},{8,16},{10,18},{16,24},{18,26},{24,28},{26,30},{28,20... | collective-permute-start | bytes 589832 | tf_op jit(solution)/shard_map/ppermute | solution.py:317
  36.4 9.6 %collective-permute-start.14 = (bf16[512,256]{1,0:T(8,128)(2,1)S(1)}, bf16[512,256]{1,0:T(8,128)(2,1)S(1)}, u32[]{:S(2)}, u32[]{:S(2)}) collective-permute-start(bf16[512,256]{1,0:T(8,128)(2,1)S(1)} %copy-done.2), channel_id=1, source_target_pairs={{0,8},{2,10},{8,16},{10,18},{16,24},{18,26},{24,28},{26,30},{28,20... | collective-permute-start | bytes 786440 | tf_op jit(solution)/shard_map/ppermute | solution.py:312
  37.7 8.5 %collective-permute-start.15 = (bf16[512,256]{1,0:T(8,128)(2,1)S(1)}, bf16[512,256]{1,0:T(8,128)(2,1)S(1)}, u32[]{:S(2)}, u32[]{:S(2)}) collective-permute-start(bf16[512,256]{1,0:T(8,128)(2,1)S(1)} %copy-done.2), channel_id=1, source_target_pairs={{8,0},{10,2},{16,8},{18,10},{24,16},{26,18},{28,24},{30,26},{20,28... | collective-permute-start | bytes 786440 | tf_op jit(solution)/shard_map/ppermute | solution.py:313
  47.1 20.6 %all-to-all-start = ((bf16[8,128,256]{2,1,0:T(8,128)(2,1)}), bf16[8,128,256]{2,1,0:T(8,128)(2,1)S(1)}, u32[]{:S(2)}, u32[]{:S(2)}) async-start(bf16[8,128,256]{2,1,0:T(8,128)(2,1)} %bitcast.1), calls=%async_computation | async-start | bytes 1048576 | tf_op jit(solution)/shard_map/all_to_all | solution.py:421
  51.6 16.1 %collective-permute-start.12 = (f32[256,512]{1,0:T(8,128)S(1)}, f32[256,512]{1,0:T(8,128)S(1)}, u32[]{:S(2)}, u32[]{:S(2)}) collective-permute-start(f32[256,512]{1,0:T(8,128)S(1)} %get-tuple-element.128.mine_ref), channel_id=1, source_target_pairs={{0,2},{2,0},{4,6},{6,4},{8,10},{10,8},{12,14},{14,12},{16,18},{18,... | collective-permute-start | bytes 1572872 | tf_op jit(solution)/shard_map/ppermute | solution.py:409
  53.8 11.4 %collective-permute-start.16 = (bf16[512,256]{1,0:T(8,128)(2,1)S(1)}, bf16[512,256]{1,0:T(8,128)(2,1)S(1)}, u32[]{:S(2)}, u32[]{:S(2)}) collective-permute-start(bf16[512,256]{1,0:T(8,128)(2,1)S(1)} %collective-permute-done.14.refs_1_), channel_id=1, source_target_pairs={{0,8},{2,10},{8,16},{10,18},{16,24},{18,26},{24,28},{26,30},{28,20... | collective-permute-start | bytes 786440 | tf_op jit(solution)/shard_map/ppermute | solution.py:312
  55.5 12.1 %collective-permute-start.17 = (bf16[512,256]{1,0:T(8,128)(2,1)S(1)}, bf16[512,256]{1,0:T(8,128)(2,1)S(1)}, u32[]{:S(2)}, u32[]{:S(2)}) collective-permute-start(bf16[512,256]{1,0:T(8,128)(2,1)S(1)} %collective-permute-done.15.refs_3_), channel_id=1, source_target_pairs={{8,0},{10,2},{16,8},{18,10},{24,16},{26,18},{28,24},{30,26},{20,28... | collective-permute-start | bytes 786440 | tf_op jit(solution)/shard_map/ppermute | solution.py:313
  70.2 5.4 %collective-permute-start.18 = (f32[256,640]{1,0:T(8,128)S(1)}, f32[256,640]{1,0:T(8,128)S(1)}, u32[]{:S(2)}, u32[]{:S(2)}) collective-permute-start(f32[256,640]{1,0:T(8,128)S(1)} %attend.1.mine_ref), channel_id=1, source_target_pairs={{0,2},{2,0},{4,6},{6,4},{8,10},{10,8},{12,14},{14,12},{16,18},{18,... | collective-permute-start | bytes 1966088 | tf_op jit(solution)/shard_map/ppermute | solution.py:445
  72.5 9.7 %collective-permute-start.19 = (bf16[512,256]{1,0:T(8,128)(2,1)S(1)}, bf16[512,256]{1,0:T(8,128)(2,1)S(1)}, u32[]{:S(2)}, u32[]{:S(2)}) collective-permute-start(bf16[512,256]{1,0:T(8,128)(2,1)S(1)} %collective-permute-done.17.refs_4_), channel_id=1, source_target_pairs={{8,0},{10,2},{16,8},{18,10},{24,16},{26,18},{28,24},{30,26},{20,28... | collective-permute-start | bytes 786440 | tf_op jit(solution)/shard_map/ppermute | solution.py:313
  73.2 10.0 %collective-permute-start.20 = (bf16[512,256]{1,0:T(8,128)(2,1)S(1)}, bf16[512,256]{1,0:T(8,128)(2,1)S(1)}, u32[]{:S(2)}, u32[]{:S(2)}) collective-permute-start(bf16[512,256]{1,0:T(8,128)(2,1)S(1)} %collective-permute-done.16.refs_0_), channel_id=1, source_target_pairs={{0,8},{2,10},{8,16},{10,18},{16,24},{18,26},{24,28},{26,30},{28,20... | collective-permute-start | bytes 786440 | tf_op jit(solution)/shard_map/ppermute | solution.py:312
  76.7 16.7 %collective-permute-start.23 = (bf16[5,64,256]{2,1,0:T(8,128)(2,1)S(1)}, bf16[5,64,256]{2,1,0:T(8,128)(2,1)S(1)}, u32[]{:S(2)}, u32[]{:S(2)}) collective-permute-start(bf16[5,64,256]{2,1,0:T(8,128)(2,1)S(1)} %get-tuple-element.168), channel_id=1, source_target_pairs={{0,1},{1,0},{2,3},{3,2},{4,5},{5,4},{6,7},{7,6},{8,9},{9,8},{10,11... | collective-permute-start | bytes 491528 | tf_op jit(solution)/shard_map/ppermute | solution.py:467
  84.7 8.8 %collective-permute-start.24 = (bf16[5,64,256]{2,1,0:T(8,128)(2,1)S(1)}, bf16[5,64,256]{2,1,0:T(8,128)(2,1)S(1)}, u32[]{:S(2)}, u32[]{:S(2)}) collective-permute-start(bf16[5,64,256]{2,1,0:T(8,128)(2,1)S(1)} %get-tuple-element.169), channel_id=1, source_target_pairs={{0,2},{1,3},{2,0},{3,1},{4,6},{5,7},{6,4},{7,5},{8,10},{9,11},{10,... | collective-permute-start | bytes 491528 | tf_op jit(solution)/shard_map/ppermute | solution.py:467
  86.1 7.4 %collective-permute-start.25 = (bf16[5,64,256]{2,1,0:T(8,128)(2,1)S(1)}, bf16[5,64,256]{2,1,0:T(8,128)(2,1)S(1)}, u32[]{:S(2)}, u32[]{:S(2)}) collective-permute-start(bf16[5,64,256]{2,1,0:T(8,128)(2,1)S(1)} %get-tuple-element.170), channel_id=1, source_target_pairs={{0,3},{1,2},{2,1},{3,0},{4,7},{5,6},{6,5},{7,4},{8,11},{9,10},{10,... | collective-permute-start | bytes 491528 | tf_op jit(solution)/shard_map/ppermute | solution.py:467
  (13 other events, 45.9 us)

commit v20 on v14

--- a/solution.py
+++ b/solution.py
@@ -381,6 +381,9 @@
     normed += [lax.ppermute(rows, "context", sibling) for rows in normed]
 
     qkv_ring.step()
+    cosine, sine, query_start, query_orig, key_orig = ordered(
+        (cosine, sine, query_start, query_orig, key_orig)
+    )
     qkv_ring.step()
     normed = qkv_ring.step(normed)
     while not qkv_ring.done():
@@ -403,7 +406,6 @@
     )(*ordered((*normed, *blocks)))
     theirs = lax.ppermute(theirs, "context", sibling)
     queries_theirs = lax.ppermute(queries, "context", sibling)
-    out_ring.step()
     mine, theirs = ordered((mine, theirs))
     kv = pl.pallas_call(
         functools.partial(keys_kernel, chips),
@@ -417,7 +419,6 @@
     kv = lax.all_to_all(
         kv, "context", split_axis=0, concat_axis=0, axis_index_groups=same_core, tiled=True
     )
-    out_ring.step()
     (kv,) = ordered((kv,))
 
     mixed = pl.pallas_call(
@@ -437,6 +438,7 @@
         key_orig,
         kv,
     )
+    out_ring.step()
     (mixed,) = ordered((mixed,))
     mixed_theirs = lax.ppermute(mixed, "context", sibling)
 

time: 95.7 us -> 105 us (1.097)
  waiting for transfers between devices: 44.3 us -> 51.7 us
  starting transfers between devices: 39.8 us -> 42.2 us
    all_to_all x1, waiting for transfers between devices: 0.01 us -> 11.2 us  [per_device(): lax.all_to_all(kv, 'context', split_axis=0, concat_axis=0, axis_index_gro...]
    ppermute x6, waiting for transfers between devices: 26.5 us -> 18.9 us  [step(): self.up.append(lax.ppermute(up, 'context', ahead))]
    ppermute x2, waiting for transfers between devices: 1.59 us -> 4.13 us  [step(): lax.ppermute(down[half:], 'context', back)]
    ppermute x6, starting transfers between devices: 7.47 us -> 9.81 us  [output(): part = lax.ppermute(part, ('context', 'tensor'), member(e, -d))]
    ppermute x6, waiting for transfers between devices: 9.32 us -> 11.1 us  [step(): self.down.append(lax.ppermute(down, 'context', back))]
    ppermute x2, waiting for transfers between devices: 1.64 us -> 0.12 us  [step(): lax.ppermute(up[:half], 'context', ahead)]
    ppermute x6, starting transfers between devices: 10.3 us -> 11.6 us  [step(): self.up.append(lax.ppermute(up, 'context', ahead))]
    ppermute x6, starting transfers between devices: 1.81 us -> 0.73 us  [step(): self.down.append(lax.ppermute(down, 'context', back))]
  transfers between devices with their start and end apart: 29 -> 29, of which waited for: 19 -> 19; matrix products, arithmetic and copies ran while one was open for 0% -> 0% of each run, Pallas kernels for 5% -> 2%
where the time goes in v20:
time: 105 us
  waiting for transfers between devices  51.7 us (49%)
  starting transfers between devices  42.2 us (40%)
  Pallas kernels  9.21 us (9%)
  local copies, waits for them, and re-layouts  1.81 us (2%)
    ppermute x6, waiting for transfers between devices, step(): self.up.append(lax.ppermute(up, 'context', ahead))  18.9 us
    ppermute x6, starting transfers between devices, step(): self.up.append(lax.ppermute(up, 'context', ahead))  11.6 us
    all_to_all x1, waiting for transfers between devices, per_device(): lax.all_to_all(kv, 'context', split_axis=0, concat_axis=0, axis_index_gro...  11.2 us
    ppermute x6, waiting for transfers between devices, step(): self.down.append(lax.ppermute(down, 'context', back))  11.1 us
    ppermute x6, starting transfers between devices, output(): part = lax.ppermute(part, ('context', 'tensor'), member(e, -d))  9.81 us
    ppermute x1, starting transfers between devices, per_device(): theirs = lax.ppermute(theirs, 'context', sibling)  5.86 us
    ppermute x6, waiting for transfers between devices, output(): part = lax.ppermute(part, ('context', 'tensor'), member(e, -d))  4.39 us
    ppermute x2, starting transfers between devices, per_device(): normed += [lax.ppermute(rows, 'context', sibling) for rows in normed]  4.3 us
  transfers between devices with their start and end apart: 29, of which 19 were waited for; matrix products, arithmetic and copies ran while one was open for 0% of the time, Pallas kernels for 2%

profile of v20, /device:TPU:1, one launch (start us, length us, event | category | flops | bytes accessed | tf_op | source)
XLA Modules:
  0.0 105.0 jit_solution(11116675900106532425)
XLA Ops:
  0.0 2.1 %collective-permute-start = (bf16[256,768]{1,0:T(8,128)(2,1)}, bf16[256,768]{1,0:T(8,128)(2,1)S(1)}, u32[]{:S(2)}, u32[]{:S(2)}) collective-permute-start(bf16[256,768]{1,0:T(8,128)(2,1)} %refs_4_), channel_id=1, source_target_pairs={{0,8},{2,10},{8,16},{10,18},{16,24},{18,26},{24,28},{26,30},{28,20... | collective-permute-start | bytes 1179656 | tf_op jit(solution)/shard_map/ppermute | solution.py:314
  4.2 1.4 %collective-permute-start.6 = (bf16[2,8,64,256]{3,2,1,0:T(8,128)(2,1)S(1)}, bf16[2,8,64,256]{3,2,1,0:T(8,128)(2,1)S(1)}, u32[]{:S(2)}, u32[]{:S(2)}) collective-permute-start(bf16[2,8,64,256]{3,2,1,0:T(8,128)(2,1)S(1)} %norm.1.refs_0_), channel_id=1, source_target_pairs={{0,1},{1,0},{2,3},{3,2},{4,5},{5,4},{6,7},{7,6},{8,9},{9,8},{10,11... | collective-permute-start | bytes 1572872 | tf_op jit(solution)/shard_map/ppermute | solution.py:376
  5.6 5.5 %collective-permute-done.refs_12_ = bf16[256,768]{1,0:T(8,128)(2,1)S(1)} collective-permute-done((bf16[256,768]{1,0:T(8,128)(2,1)}, bf16[256,768]{1,0:T(8,128)(2,1)S(1)}, u32[]{:S(2)}, u32[]{:S(2)}) %collective-permute-start) | collective-permute-done | bytes 393248 | tf_op jit(solution)/shard_map/ppermute | solution.py:314
  12.0 1.3 %collective-permute-start.2 = (bf16[256,768]{1,0:T(8,128)(2,1)S(1)}, bf16[256,768]{1,0:T(8,128)(2,1)S(1)}, u32[]{:S(2)}, u32[]{:S(2)}) collective-permute-start(bf16[256,768]{1,0:T(8,128)(2,1)S(1)} %collective-permute-done.refs_12_), channel_id=1, source_target_pairs={{0,8},{2,10},{8,16},{10,18},{16,24},{18,26},{24,28},{26,30},{28,20... | collective-permute-start | bytes 1179656 | tf_op jit(solution)/shard_map/ppermute | solution.py:314
  13.5 2.4 %collective-permute-start.7 = (bf16[2,8,64,256]{3,2,1,0:T(8,128)(2,1)S(1)}, bf16[2,8,64,256]{3,2,1,0:T(8,128)(2,1)S(1)}, u32[]{:S(2)}, u32[]{:S(2)}) collective-permute-start(bf16[2,8,64,256]{3,2,1,0:T(8,128)(2,1)S(1)} %norm.1.refs_0_), channel_id=1, source_target_pairs={{0,2},{2,0},{4,6},{6,4},{8,10},{10,8},{12,14},{14,12},{16,18},{18,... | collective-permute-start | bytes 1572872 | tf_op jit(solution)/shard_map/ppermute | solution.py:381
  16.7 1.9 %collective-permute-start.8 = (bf16[2,8,64,256]{3,2,1,0:T(8,128)(2,1)S(1)}, bf16[2,8,64,256]{3,2,1,0:T(8,128)(2,1)S(1)}, u32[]{:S(2)}, u32[]{:S(2)}) collective-permute-start(bf16[2,8,64,256]{3,2,1,0:T(8,128)(2,1)S(1)} %collective-permute-done.6.refs_1_), channel_id=1, source_target_pairs={{0,2},{2,0},{4,6},{6,4},{8,10},{10,8},{12,14},{14,12},{16,18},{18,... | collective-permute-start | bytes 1572872 | tf_op jit(solution)/shard_map/ppermute | solution.py:381
  21.8 1.3 %collective-permute-start.4 = (bf16[256,768]{1,0:T(8,128)(2,1)S(1)}, bf16[256,768]{1,0:T(8,128)(2,1)S(1)}, u32[]{:S(2)}, u32[]{:S(2)}) collective-permute-start(bf16[256,768]{1,0:T(8,128)(2,1)S(1)} %collective-permute-done.2.refs_11_), channel_id=1, source_target_pairs={{0,8},{2,10},{8,16},{10,18},{16,24},{18,26},{24,28},{26,30},{28,20... | collective-permute-start | bytes 1179656 | tf_op jit(solution)/shard_map/ppermute | solution.py:314
  23.2 6.1 %collective-permute-done.4.refs_10_ = bf16[256,768]{1,0:T(8,128)(2,1)S(1)} collective-permute-done((bf16[256,768]{1,0:T(8,128)(2,1)S(1)}, bf16[256,768]{1,0:T(8,128)(2,1)S(1)}, u32[]{:S(2)}, u32[]{:S(2)}) %collective-permute-start.4) | collective-permute-done | bytes 393248 | tf_op jit(solution)/shard_map/ppermute | solution.py:314
  30.6 1.3 %collective-permute-start.9 = (bf16[128,768]{1,0:T(8,128)(2,1)S(1)}, bf16[128,768]{1,0:T(8,128)(2,1)S(1)}, u32[]{:S(2)}, u32[]{:S(2)}) collective-permute-start(bf16[128,768]{1,0:T(8,128)(2,1)S(1)} %slice.12), channel_id=1, source_target_pairs={{0,8},{2,10},{8,16},{10,18},{16,24},{18,26},{24,28},{26,30},{28,20... | collective-permute-start | bytes 589832 | tf_op jit(solution)/shard_map/ppermute | solution.py:319
  31.9 4.1 %collective-permute-done.10.refs_9_ = bf16[128,768]{1,0:T(8,128)(2,1)S(1)} collective-permute-done((bf16[128,768]{1,0:T(8,128)(2,1)S(1)}, bf16[128,768]{1,0:T(8,128)(2,1)S(1)}, u32[]{:S(2)}, u32[]{:S(2)}) %collective-permute-start.10) | collective-permute-done | bytes 196640 | tf_op jit(solution)/shard_map/ppermute | solution.py:320
  37.1 5.9 %collective-permute-start.12 = (f32[128,256]{1,0:T(8,128)S(1)}, f32[128,256]{1,0:T(8,128)S(1)}, u32[]{:S(2)}, u32[]{:S(2)}) collective-permute-start(f32[128,256]{1,0:T(8,128)S(1)} %get-tuple-element.131), channel_id=1, source_target_pairs={{0,2},{2,0},{4,6},{6,4},{8,10},{10,8},{12,14},{14,12},{16,18},{18,... | collective-permute-start | bytes 393224 | tf_op jit(solution)/shard_map/ppermute | solution.py:407
  44.9 3.7 %all-to-all-start = ((bf16[8,128,256]{2,1,0:T(8,128)(2,1)}), bf16[8,128,256]{2,1,0:T(8,128)(2,1)S(1)}, u32[]{:S(2)}, u32[]{:S(2)}) async-start(bf16[8,128,256]{2,1,0:T(8,128)(2,1)} %bitcast.1), calls=%async_computation | async-start | bytes 1048576 | tf_op jit(solution)/shard_map/all_to_all | solution.py:419
  49.2 1.7 %collective-permute-start.13 = (bf16[512,256]{1,0:T(8,128)(2,1)S(1)}, bf16[512,256]{1,0:T(8,128)(2,1)S(1)}, u32[]{:S(2)}, u32[]{:S(2)}) collective-permute-start(bf16[512,256]{1,0:T(8,128)(2,1)S(1)} %copy-done.2), channel_id=1, source_target_pairs={{0,8},{2,10},{8,16},{10,18},{16,24},{18,26},{24,28},{26,30},{28,20... | collective-permute-start | bytes 786440 | tf_op jit(solution)/shard_map/ppermute | solution.py:314
  50.9 11.2 %all-to-all-done = bf16[8,128,256]{2,1,0:T(8,128)(2,1)S(1)} async-done(((bf16[8,128,256]{2,1,0:T(8,128)(2,1)}), bf16[8,128,256]{2,1,0:T(8,128)(2,1)S(1)}, u32[]{:S(2)}, u32[]{:S(2)}) %all-to-all-start) | async-done | bytes 524320 | tf_op jit(solution)/shard_map/all_to_all | solution.py:419
  62.5 2.4 %collective-permute-done.14.refs_3_ = bf16[512,256]{1,0:T(8,128)(2,1)S(1)} collective-permute-done((bf16[512,256]{1,0:T(8,128)(2,1)S(1)}, bf16[512,256]{1,0:T(8,128)(2,1)S(1)}, u32[]{:S(2)}, u32[]{:S(2)}) %collective-permute-start.14) | collective-permute-done | bytes 262176 | tf_op jit(solution)/shard_map/ppermute | solution.py:315
  64.9 2.5 %attend.1.mine_ref = f32[256,640]{1,0:T(8,128)S(1)} custom-call(f32[256,512]{1,0:T(8,128)S(1)} %get-tuple-element.124.mine_ref, f32[256,512]{1,0:T(8,128)S(1)} %collective-permute-done.11.theirs_ref, f32[256,128]{1,0:T(8,128)S(1)} %get-tuple-element.125.cosine_ref, f32[256,128]{1,0:T(8,128)S(1)} %get-tuple-element.126.sine_ref, ...), custom_call_target="tpu_custom_call" | custom-call | tf_op jit(solution)/shard_map/attend/pallas_call | solution.py:424
  68.5 4.0 %collective-permute-start.16 = (bf16[512,256]{1,0:T(8,128)(2,1)S(1)}, bf16[512,256]{1,0:T(8,128)(2,1)S(1)}, u32[]{:S(2)}, u32[]{:S(2)}) collective-permute-start(bf16[512,256]{1,0:T(8,128)(2,1)S(1)} %collective-permute-done.13.refs_1_), channel_id=1, source_target_pairs={{0,8},{2,10},{8,16},{10,18},{16,24},{18,26},{24,28},{26,30},{28,20... | collective-permute-start | bytes 786440 | tf_op jit(solution)/shard_map/ppermute | solution.py:314
  72.5 5.7 %collective-permute-done.16.refs_0_ = bf16[512,256]{1,0:T(8,128)(2,1)S(1)} collective-permute-done((bf16[512,256]{1,0:T(8,128)(2,1)S(1)}, bf16[512,256]{1,0:T(8,128)(2,1)S(1)}, u32[]{:S(2)}, u32[]{:S(2)}) %collective-permute-start.16) | collective-permute-done | bytes 262176 | tf_op jit(solution)/shard_map/ppermute | solution.py:314
  78.2 1.9 %collective-permute-done.17.refs_4_ = bf16[512,256]{1,0:T(8,128)(2,1)S(1)} collective-permute-done((bf16[512,256]{1,0:T(8,128)(2,1)S(1)}, bf16[512,256]{1,0:T(8,128)(2,1)S(1)}, u32[]{:S(2)}, u32[]{:S(2)}) %collective-permute-start.17) | collective-permute-done | bytes 262176 | tf_op jit(solution)/shard_map/ppermute | solution.py:315
  83.9 3.9 %collective-permute-done.18.refs_0_ = bf16[512,256]{1,0:T(8,128)(2,1)S(1)} collective-permute-done((bf16[512,256]{1,0:T(8,128)(2,1)S(1)}, bf16[512,256]{1,0:T(8,128)(2,1)S(1)}, u32[]{:S(2)}, u32[]{:S(2)}) %collective-permute-start.18) | collective-permute-done | bytes 262176 | tf_op jit(solution)/shard_map/ppermute | solution.py:315
  89.8 2.6 %collective-permute-start.23 = (bf16[5,64,256]{2,1,0:T(8,128)(2,1)S(1)}, bf16[5,64,256]{2,1,0:T(8,128)(2,1)S(1)}, u32[]{:S(2)}, u32[]{:S(2)}) collective-permute-start(bf16[5,64,256]{2,1,0:T(8,128)(2,1)S(1)} %get-tuple-element.165), channel_id=1, source_target_pairs={{0,2},{1,3},{2,0},{3,1},{4,6},{5,7},{6,4},{7,5},{8,10},{9,11},{10,... | collective-permute-start | bytes 491528 | tf_op jit(solution)/shard_map/ppermute | solution.py:465
  94.6 1.3 %collective-permute-start.25 = (bf16[3,64,256]{2,1,0:T(8,128)(2,1)S(1)}, bf16[3,64,256]{2,1,0:T(8,128)(2,1)S(1)}, u32[]{:S(2)}, u32[]{:S(2)}) collective-permute-start(bf16[3,64,256]{2,1,0:T(8,128)(2,1)S(1)} %get-tuple-element.168), channel_id=1, source_target_pairs={{0,1},{1,0},{2,3},{3,2},{4,5},{5,4},{6,7},{7,6},{8,9},{9,8},{10,11... | collective-permute-start | bytes 294920 | tf_op jit(solution)/shard_map/ppermute | solution.py:465
  95.9 3.5 %collective-permute-start.26 = (bf16[3,64,256]{2,1,0:T(8,128)(2,1)S(1)}, bf16[3,64,256]{2,1,0:T(8,128)(2,1)S(1)}, u32[]{:S(2)}, u32[]{:S(2)}) collective-permute-start(bf16[3,64,256]{2,1,0:T(8,128)(2,1)S(1)} %get-tuple-element.169), channel_id=1, source_target_pairs={{0,2},{1,3},{2,0},{3,1},{4,6},{5,7},{6,4},{7,5},{8,10},{9,11},{10,... | collective-permute-start | bytes 294920 | tf_op jit(solution)/shard_map/ppermute | solution.py:465
  100.3 3.6 %collective-permute-done.27.refs_7_ = bf16[3,64,256]{2,1,0:T(8,128)(2,1)S(1)} collective-permute-done((bf16[3,64,256]{2,1,0:T(8,128)(2,1)S(1)}, bf16[3,64,256]{2,1,0:T(8,128)(2,1)S(1)}, u32[]{:S(2)}, u32[]{:S(2)}) %collective-permute-start.27) | collective-permute-done | bytes 98336 | tf_op jit(solution)/shard_map/ppermute | solution.py:465
  (60 shorter events, 23.5 us)
Async XLA Ops:
  0.0 11.1 %collective-permute-start = (bf16[256,768]{1,0:T(8,128)(2,1)}, bf16[256,768]{1,0:T(8,128)(2,1)S(1)}, u32[]{:S(2)}, u32[]{:S(2)}) collective-permute-start(bf16[256,768]{1,0:T(8,128)(2,1)} %refs_4_), channel_id=1, source_target_pairs={{0,8},{2,10},{8,16},{10,18},{16,24},{18,26},{24,28},{26,30},{28,20... | collective-permute-start | bytes 1179656 | tf_op jit(solution)/shard_map/ppermute | solution.py:314
  2.1 9.9 %collective-permute-start.1 = (bf16[256,768]{1,0:T(8,128)(2,1)}, bf16[256,768]{1,0:T(8,128)(2,1)S(1)}, u32[]{:S(2)}, u32[]{:S(2)}) collective-permute-start(bf16[256,768]{1,0:T(8,128)(2,1)} %refs_4_), channel_id=1, source_target_pairs={{8,0},{10,2},{16,8},{18,10},{24,16},{26,18},{28,24},{30,26},{20,28... | collective-permute-start | bytes 1179656 | tf_op jit(solution)/shard_map/ppermute | solution.py:315
  4.2 12.5 %collective-permute-start.6 = (bf16[2,8,64,256]{3,2,1,0:T(8,128)(2,1)S(1)}, bf16[2,8,64,256]{3,2,1,0:T(8,128)(2,1)S(1)}, u32[]{:S(2)}, u32[]{:S(2)}) collective-permute-start(bf16[2,8,64,256]{3,2,1,0:T(8,128)(2,1)S(1)} %norm.1.refs_0_), channel_id=1, source_target_pairs={{0,1},{1,0},{2,3},{3,2},{4,5},{5,4},{6,7},{7,6},{8,9},{9,8},{10,11... | collective-permute-start | bytes 1572872 | tf_op jit(solution)/shard_map/ppermute | solution.py:376
  12.0 8.7 %collective-permute-start.2 = (bf16[256,768]{1,0:T(8,128)(2,1)S(1)}, bf16[256,768]{1,0:T(8,128)(2,1)S(1)}, u32[]{:S(2)}, u32[]{:S(2)}) collective-permute-start(bf16[256,768]{1,0:T(8,128)(2,1)S(1)} %collective-permute-done.refs_12_), channel_id=1, source_target_pairs={{0,8},{2,10},{8,16},{10,18},{16,24},{18,26},{24,28},{26,30},{28,20... | collective-permute-start | bytes 1179656 | tf_op jit(solution)/shard_map/ppermute | solution.py:314
  13.3 8.5 %collective-permute-start.3 = (bf16[256,768]{1,0:T(8,128)(2,1)S(1)}, bf16[256,768]{1,0:T(8,128)(2,1)S(1)}, u32[]{:S(2)}, u32[]{:S(2)}) collective-permute-start(bf16[256,768]{1,0:T(8,128)(2,1)S(1)} %collective-permute-done.1.refs_5_), channel_id=1, source_target_pairs={{8,0},{10,2},{16,8},{18,10},{24,16},{26,18},{28,24},{30,26},{20,28... | collective-permute-start | bytes 1179656 | tf_op jit(solution)/shard_map/ppermute | solution.py:315
  13.5 9.8 %collective-permute-start.7 = (bf16[2,8,64,256]{3,2,1,0:T(8,128)(2,1)S(1)}, bf16[2,8,64,256]{3,2,1,0:T(8,128)(2,1)S(1)}, u32[]{:S(2)}, u32[]{:S(2)}) collective-permute-start(bf16[2,8,64,256]{3,2,1,0:T(8,128)(2,1)S(1)} %norm.1.refs_0_), channel_id=1, source_target_pairs={{0,2},{2,0},{4,6},{6,4},{8,10},{10,8},{12,14},{14,12},{16,18},{18,... | collective-permute-start | bytes 1572872 | tf_op jit(solution)/shard_map/ppermute | solution.py:381
  16.7 6.5 %collective-permute-start.8 = (bf16[2,8,64,256]{3,2,1,0:T(8,128)(2,1)S(1)}, bf16[2,8,64,256]{3,2,1,0:T(8,128)(2,1)S(1)}, u32[]{:S(2)}, u32[]{:S(2)}) collective-permute-start(bf16[2,8,64,256]{3,2,1,0:T(8,128)(2,1)S(1)} %collective-permute-done.6.refs_1_), channel_id=1, source_target_pairs={{0,2},{2,0},{4,6},{6,4},{8,10},{10,8},{12,14},{14,12},{16,18},{18,... | collective-permute-start | bytes 1572872 | tf_op jit(solution)/shard_map/ppermute | solution.py:381
  21.8 7.5 %collective-permute-start.4 = (bf16[256,768]{1,0:T(8,128)(2,1)S(1)}, bf16[256,768]{1,0:T(8,128)(2,1)S(1)}, u32[]{:S(2)}, u32[]{:S(2)}) collective-permute-start(bf16[256,768]{1,0:T(8,128)(2,1)S(1)} %collective-permute-done.2.refs_11_), channel_id=1, source_target_pairs={{0,8},{2,10},{8,16},{10,18},{16,24},{18,26},{24,28},{26,30},{28,20... | collective-permute-start | bytes 1179656 | tf_op jit(solution)/shard_map/ppermute | solution.py:314
  23.1 7.3 %collective-permute-start.5 = (bf16[256,768]{1,0:T(8,128)(2,1)S(1)}, bf16[256,768]{1,0:T(8,128)(2,1)S(1)}, u32[]{:S(2)}, u32[]{:S(2)}) collective-permute-start(bf16[256,768]{1,0:T(8,128)(2,1)S(1)} %collective-permute-done.3.refs_6_), channel_id=1, source_target_pairs={{8,0},{10,2},{16,8},{18,10},{24,16},{26,18},{28,24},{30,26},{20,28... | collective-permute-start | bytes 1179656 | tf_op jit(solution)/shard_map/ppermute | solution.py:315
  30.4 5.6 %collective-permute-start.10 = (bf16[128,768]{1,0:T(8,128)(2,1)S(1)}, bf16[128,768]{1,0:T(8,128)(2,1)S(1)}, u32[]{:S(2)}, u32[]{:S(2)}) collective-permute-start(bf16[128,768]{1,0:T(8,128)(2,1)S(1)} %slice.13), channel_id=1, source_target_pairs={{8,0},{10,2},{16,8},{18,10},{24,16},{26,18},{28,24},{30,26},{20,28... | collective-permute-start | bytes 589832 | tf_op jit(solution)/shard_map/ppermute | solution.py:320
  30.6 5.4 %collective-permute-start.9 = (bf16[128,768]{1,0:T(8,128)(2,1)S(1)}, bf16[128,768]{1,0:T(8,128)(2,1)S(1)}, u32[]{:S(2)}, u32[]{:S(2)}) collective-permute-start(bf16[128,768]{1,0:T(8,128)(2,1)S(1)} %slice.12), channel_id=1, source_target_pairs={{0,8},{2,10},{8,16},{10,18},{16,24},{18,26},{24,28},{26,30},{28,20... | collective-permute-start | bytes 589832 | tf_op jit(solution)/shard_map/ppermute | solution.py:319
  37.1 6.8 %collective-permute-start.12 = (f32[128,256]{1,0:T(8,128)S(1)}, f32[128,256]{1,0:T(8,128)S(1)}, u32[]{:S(2)}, u32[]{:S(2)}) collective-permute-start(f32[128,256]{1,0:T(8,128)S(1)} %get-tuple-element.131), channel_id=1, source_target_pairs={{0,2},{2,0},{4,6},{6,4},{8,10},{10,8},{12,14},{14,12},{16,18},{18,... | collective-permute-start | bytes 393224 | tf_op jit(solution)/shard_map/ppermute | solution.py:407
  44.9 17.3 %all-to-all-start = ((bf16[8,128,256]{2,1,0:T(8,128)(2,1)}), bf16[8,128,256]{2,1,0:T(8,128)(2,1)S(1)}, u32[]{:S(2)}, u32[]{:S(2)}) async-start(bf16[8,128,256]{2,1,0:T(8,128)(2,1)} %bitcast.1), calls=%async_computation | async-start | bytes 1048576 | tf_op jit(solution)/shard_map/all_to_all | solution.py:419
  48.6 16.3 %collective-permute-start.11 = (f32[256,512]{1,0:T(8,128)S(1)}, f32[256,512]{1,0:T(8,128)S(1)}, u32[]{:S(2)}, u32[]{:S(2)}) collective-permute-start(f32[256,512]{1,0:T(8,128)S(1)} %get-tuple-element.124.mine_ref), channel_id=1, source_target_pairs={{0,2},{2,0},{4,6},{6,4},{8,10},{10,8},{12,14},{14,12},{16,18},{18,... | collective-permute-start | bytes 1572872 | tf_op jit(solution)/shard_map/ppermute | solution.py:408
  49.2 13.3 %collective-permute-start.13 = (bf16[512,256]{1,0:T(8,128)(2,1)S(1)}, bf16[512,256]{1,0:T(8,128)(2,1)S(1)}, u32[]{:S(2)}, u32[]{:S(2)}) collective-permute-start(bf16[512,256]{1,0:T(8,128)(2,1)S(1)} %copy-done.2), channel_id=1, source_target_pairs={{0,8},{2,10},{8,16},{10,18},{16,24},{18,26},{24,28},{26,30},{28,20... | collective-permute-start | bytes 786440 | tf_op jit(solution)/shard_map/ppermute | solution.py:314
  50.9 14.0 %collective-permute-start.14 = (bf16[512,256]{1,0:T(8,128)(2,1)S(1)}, bf16[512,256]{1,0:T(8,128)(2,1)S(1)}, u32[]{:S(2)}, u32[]{:S(2)}) collective-permute-start(bf16[512,256]{1,0:T(8,128)(2,1)S(1)} %copy-done.2), channel_id=1, source_target_pairs={{8,0},{10,2},{16,8},{18,10},{24,16},{26,18},{28,24},{30,26},{20,28... | collective-permute-start | bytes 786440 | tf_op jit(solution)/shard_map/ppermute | solution.py:315
  67.4 12.6 %collective-permute-start.15 = (f32[256,640]{1,0:T(8,128)S(1)}, f32[256,640]{1,0:T(8,128)S(1)}, u32[]{:S(2)}, u32[]{:S(2)}) collective-permute-start(f32[256,640]{1,0:T(8,128)S(1)} %attend.1.mine_ref), channel_id=1, source_target_pairs={{0,2},{2,0},{4,6},{6,4},{8,10},{10,8},{12,14},{14,12},{16,18},{18,... | collective-permute-start | bytes 1966088 | tf_op jit(solution)/shard_map/ppermute | solution.py:443
  68.5 9.7 %collective-permute-start.16 = (bf16[512,256]{1,0:T(8,128)(2,1)S(1)}, bf16[512,256]{1,0:T(8,128)(2,1)S(1)}, u32[]{:S(2)}, u32[]{:S(2)}) collective-permute-start(bf16[512,256]{1,0:T(8,128)(2,1)S(1)} %collective-permute-done.13.refs_1_), channel_id=1, source_target_pairs={{0,8},{2,10},{8,16},{10,18},{16,24},{18,26},{24,28},{26,30},{28,20... | collective-permute-start | bytes 786440 | tf_op jit(solution)/shard_map/ppermute | solution.py:314
  72.5 7.5 %collective-permute-start.17 = (bf16[512,256]{1,0:T(8,128)(2,1)S(1)}, bf16[512,256]{1,0:T(8,128)(2,1)S(1)}, u32[]{:S(2)}, u32[]{:S(2)}) collective-permute-start(bf16[512,256]{1,0:T(8,128)(2,1)S(1)} %collective-permute-done.14.refs_3_), channel_id=1, source_target_pairs={{8,0},{10,2},{16,8},{18,10},{24,16},{26,18},{28,24},{30,26},{20,28... | collective-permute-start | bytes 786440 | tf_op jit(solution)/shard_map/ppermute | solution.py:315
  81.2 6.7 %collective-permute-start.18 = (bf16[512,256]{1,0:T(8,128)(2,1)S(1)}, bf16[512,256]{1,0:T(8,128)(2,1)S(1)}, u32[]{:S(2)}, u32[]{:S(2)}) collective-permute-start(bf16[512,256]{1,0:T(8,128)(2,1)S(1)} %collective-permute-done.17.refs_4_), channel_id=1, source_target_pairs={{8,0},{10,2},{16,8},{18,10},{24,16},{26,18},{28,24},{30,26},{20,28... | collective-permute-start | bytes 786440 | tf_op jit(solution)/shard_map/ppermute | solution.py:315
  81.6 6.7 %collective-permute-start.19 = (bf16[512,256]{1,0:T(8,128)(2,1)S(1)}, bf16[512,256]{1,0:T(8,128)(2,1)S(1)}, u32[]{:S(2)}, u32[]{:S(2)}) collective-permute-start(bf16[512,256]{1,0:T(8,128)(2,1)S(1)} %collective-permute-done.16.refs_0_), channel_id=1, source_target_pairs={{0,8},{2,10},{8,16},{10,18},{16,24},{18,26},{24,28},{26,30},{28,20... | collective-permute-start | bytes 786440 | tf_op jit(solution)/shard_map/ppermute | solution.py:314
  82.7 16.6 %collective-permute-start.22 = (bf16[5,64,256]{2,1,0:T(8,128)(2,1)S(1)}, bf16[5,64,256]{2,1,0:T(8,128)(2,1)S(1)}, u32[]{:S(2)}, u32[]{:S(2)}) collective-permute-start(bf16[5,64,256]{2,1,0:T(8,128)(2,1)S(1)} %get-tuple-element.164), channel_id=1, source_target_pairs={{0,1},{1,0},{2,3},{3,2},{4,5},{5,4},{6,7},{7,6},{8,9},{9,8},{10,11... | collective-permute-start | bytes 491528 | tf_op jit(solution)/shard_map/ppermute | solution.py:465
  89.8 9.7 %collective-permute-start.23 = (bf16[5,64,256]{2,1,0:T(8,128)(2,1)S(1)}, bf16[5,64,256]{2,1,0:T(8,128)(2,1)S(1)}, u32[]{:S(2)}, u32[]{:S(2)}) collective-permute-start(bf16[5,64,256]{2,1,0:T(8,128)(2,1)S(1)} %get-tuple-element.165), channel_id=1, source_target_pairs={{0,2},{1,3},{2,0},{3,1},{4,6},{5,7},{6,4},{7,5},{8,10},{9,11},{10,... | collective-permute-start | bytes 491528 | tf_op jit(solution)/shard_map/ppermute | solution.py:465
  92.4 7.1 %collective-permute-start.24 = (bf16[5,64,256]{2,1,0:T(8,128)(2,1)S(1)}, bf16[5,64,256]{2,1,0:T(8,128)(2,1)S(1)}, u32[]{:S(2)}, u32[]{:S(2)}) collective-permute-start(bf16[5,64,256]{2,1,0:T(8,128)(2,1)S(1)} %get-tuple-element.166), channel_id=1, source_target_pairs={{0,3},{1,2},{2,1},{3,0},{4,7},{5,6},{6,5},{7,4},{8,11},{9,10},{10,... | collective-permute-start | bytes 491528 | tf_op jit(solution)/shard_map/ppermute | solution.py:465
  (12 other events, 89.6 us)

commit v21 on v15

--- a/solution.py
+++ b/solution.py
@@ -231,8 +231,9 @@
     out_ref[:, HEAD_COLS:] = stats
 
 
-def output_kernel(groups, pieces_of, mine_ref, theirs_ref, *refs):
+def output_kernel(chips, groups, mine_ref, theirs_ref, *refs):
     weight_refs, out_refs = refs[:-groups], refs[-groups:]
+    weights = take_ring(weight_refs, chips)
     chip_rows = mine_ref.shape[0]
     half = chip_rows // 2
 
@@ -253,11 +254,9 @@
         )
     mixed = jnp.concatenate(pieces, axis=1)
     rows = chip_rows // groups
-    weight_refs = iter(weight_refs)
-    for slot, pieces in enumerate(pieces_of):
+    for slot in range(chips):
         start, total = 0, None
-        for _ in range(pieces):
-            ref = next(weight_refs)
+        for ref in weights[slot]:
             depth = ref.shape[0]
             part = jnp.dot(
                 mixed[:, start : start + depth], ref[...], preferred_element_type=jnp.float32
@@ -269,22 +268,16 @@
             out_refs[group][slot] = total[group * rows : (group + 1) * rows]
 
 
-def sum_kernel(place, chips, groups, near, token_ref, *refs):
-    near_refs, far_refs, out_ref = refs[:groups], refs[groups : 2 * groups], refs[2 * groups]
+def sum_kernel(place, chips, groups, token_ref, *refs):
+    part_refs, out_ref = refs[:groups], refs[groups]
     at, core = place_of(place)
-    block = near_refs[0].shape[2]
+    block = part_refs[0].shape[2]
     half = groups // 2
 
     def added(part, slot):
-        turn_at = lax.rem(slot + near // 2, chips)
-        total = None
-        for group in range(part * half, (part + 1) * half):
-            rows = jnp.where(
-                turn_at < near,
-                near_refs[group][jnp.minimum(turn_at, near - 1)].astype(jnp.float32),
-                far_refs[group][jnp.maximum(turn_at - near, 0)].astype(jnp.float32),
-            )
-            total = rows if total is None else total + rows
+        total = part_refs[part * half][slot].astype(jnp.float32)
+        for ref in part_refs[part * half + 1 : (part + 1) * half]:
+            total += ref[slot].astype(jnp.float32)
         return total.astype(jnp.bfloat16)
 
     for even in range(2):
@@ -346,12 +339,6 @@
             while not self.done():
                 self.step()
             return self.down + self.middle + self.up[:0:-1]
-
-        def block(self, slot):
-            slot %= chips
-            if chips % 2 == 0 and slot == chips // 2:
-                return tuple(self.middle)
-            return (self.down[slot] if slot <= chips // 2 else self.up[chips - slot],)
 
     def member(e, d):
         return [
@@ -462,42 +449,31 @@
         key_orig,
         *kv_blocks,
     )
-    (mixed,) = ordered((mixed,))
+    mixed, *out_ring.middle = ordered((mixed, *out_ring.middle))
     mixed_theirs = lax.ppermute(mixed, "context", sibling)
 
     out_block = w_out.shape[1]
 
-    def output(slots, name):
-        blocks = [out_ring.block(slot) for slot in slots]
-        flat = [piece for pieces in blocks for piece in pieces]
-        parts = pl.pallas_call(
-            functools.partial(output_kernel, groups, [len(pieces) for pieces in blocks]),
-            out_shape=[jax.ShapeDtypeStruct((len(slots), rows_here, out_block), jnp.bfloat16)]
-            * groups,
-            in_specs=vmem_specs(2 + len(flat)),
-            out_specs=vmem_specs(groups),
-            compiler_params=compute_params(),
-            name=name,
-        )(mixed, mixed_theirs, *flat)
-        parts = ordered(parts)
-        arrived = []
-        for e in range(2):
-            for d in range(n_tensor):
-                part = parts[e * n_tensor + d]
-                if e or d:
-                    part = lax.ppermute(part, ("context", "tensor"), member(e, -d))
-                arrived.append(part)
-        return arrived
-
-    reach = (chips - 1) // 2
-    near = 2 * reach + 1
-    arrived = output(list(range(-reach, reach + 1)), "output_near")
-    if near < chips:
-        arrived += output(list(range(reach + 1, chips - reach)), "output_far")
+    blocks = out_ring.finish()
+    parts = pl.pallas_call(
+        functools.partial(output_kernel, chips, groups),
+        out_shape=[jax.ShapeDtypeStruct((chips, rows_here, out_block), jnp.bfloat16)] * groups,
+        in_specs=vmem_specs(2 + len(blocks)),
+        out_specs=vmem_specs(groups),
+        compiler_params=compute_params(),
+        name="output",
+    )(mixed, mixed_theirs, *blocks)
+    arrived = []
+    for e in range(2):
+        for d in range(n_tensor):
+            part = parts[e * n_tensor + d]
+            if e or d:
+                part = lax.ppermute(part, ("context", "tensor"), member(e, -d))
+            arrived.append(part)
     return pl.pallas_call(
-        functools.partial(sum_kernel, place, chips, groups, near),
+        functools.partial(sum_kernel, place, chips, groups),
         out_shape=jax.ShapeDtypeStruct((rows_here, n_context * out_block), jnp.bfloat16),
-        in_specs=[pl.BlockSpec(memory_space=pl.ANY)] + vmem_specs(2 * groups),
+        in_specs=[pl.BlockSpec(memory_space=pl.ANY)] + vmem_specs(groups),
         out_specs=vmem_specs(1)[0],
         compiler_params=compute_params(),
         name="sum",

time: 98.3 us -> 97.3 us (0.990)
  waiting for transfers between devices: 41.9 us -> 46.8 us
  starting transfers between devices: 45.5 us -> 40.8 us
    ppermute x6 -> x3, waiting for transfers between devices: 3.88 us -> 11.6 us  [per_device(): part = lax.ppermute(part, ('context', 'tensor'), member(e, -d))]
    ppermute x6 -> x3, starting transfers between devices: 7.61 us -> 2.08 us  [per_device(): part = lax.ppermute(part, ('context', 'tensor'), member(e, -d))]
    ppermute x3, waiting for transfers between devices: 7.48 us -> 4.58 us  [step(): lax.ppermute(down[half:], 'context', back)]
    ppermute x1, starting transfers between devices: 5.47 us -> 6.47 us  [per_device(): mixed_theirs = lax.ppermute(mixed, 'context', sibling)]
    pallas_call x3 -> x2, Pallas kernels: 3.18 us -> 2.26 us  [the longest x1 1.33 us: per_device(): pl.pallas_call(functools.partial(output_kernel, chips, groups), out_shape...]
  transfers between devices with their start and end apart: 36 -> 33, of which waited for: 18 -> 18; matrix products, arithmetic and copies ran while one was open for 0% -> 0% of each run, Pallas kernels for 4% -> 5%
where the time goes in v21:
time: 97.3 us; the launch traced here: 97.1 us
  waiting for transfers between devices  46.8 us (48%)
  starting transfers between devices  40.8 us (42%)
  Pallas kernels  7.55 us (8%)
  local copies, waits for them, and re-layouts  1.82 us (2%)
    ppermute x9, waiting for transfers between devices, step(): self.down.append(lax.ppermute(down, 'context', back))  14.2 us
    ppermute x9, waiting for transfers between devices, step(): self.up.append(lax.ppermute(up, 'context', ahead))  12.7 us
    ppermute x9, starting transfers between devices, step(): self.up.append(lax.ppermute(up, 'context', ahead))  12.5 us
    ppermute x3, waiting for transfers between devices, per_device(): part = lax.ppermute(part, ('context', 'tensor'), member(e, -d))  11.6 us
    ppermute x1, starting transfers between devices, per_device(): mixed_theirs = lax.ppermute(mixed, 'context', sibling)  6.47 us
    ppermute x1, starting transfers between devices, per_device(): theirs = lax.ppermute(theirs, 'context', sibling)  5.86 us
    ppermute x3, waiting for transfers between devices, step(): lax.ppermute(down[half:], 'context', back)  4.58 us
    ppermute x2, starting transfers between devices, per_device(): normed += [lax.ppermute(rows, 'context', sibling) for rows in normed]  4.3 us
  transfers between devices with their start and end apart: 33, of which 18 were waited for; matrix products, arithmetic and copies ran while one was open for 0% of the time, Pallas kernels for 5%

profile of v21, /device:TPU:1, one launch (start us, length us, event | category | flops | bytes accessed | tf_op | source)
XLA Modules:
  0.0 97.1 jit_solution(3874037785403603292)
XLA Ops:
  0.0 2.1 %collective-permute-start = (bf16[256,768]{1,0:T(8,128)(2,1)}, bf16[256,768]{1,0:T(8,128)(2,1)S(1)}, u32[]{:S(2)}, u32[]{:S(2)}) collective-permute-start(bf16[256,768]{1,0:T(8,128)(2,1)} %refs_4_), channel_id=1, source_target_pairs={{0,8},{2,10},{8,16},{10,18},{16,24},{18,26},{24,28},{26,30},{28,20... | collective-permute-start | bytes 1179656 | tf_op jit(solution)/shard_map/ppermute | solution.py:325
  4.2 1.4 %collective-permute-start.6 = (bf16[2,8,64,256]{3,2,1,0:T(8,128)(2,1)S(1)}, bf16[2,8,64,256]{3,2,1,0:T(8,128)(2,1)S(1)}, u32[]{:S(2)}, u32[]{:S(2)}) collective-permute-start(bf16[2,8,64,256]{3,2,1,0:T(8,128)(2,1)S(1)} %norm.1.refs_0_), channel_id=1, source_target_pairs={{0,1},{1,0},{2,3},{3,2},{4,5},{5,4},{6,7},{7,6},{8,9},{9,8},{10,11... | collective-permute-start | bytes 1572872 | tf_op jit(solution)/shard_map/ppermute | solution.py:381
  5.6 5.5 %collective-permute-done.refs_12_ = bf16[256,768]{1,0:T(8,128)(2,1)S(1)} collective-permute-done((bf16[256,768]{1,0:T(8,128)(2,1)}, bf16[256,768]{1,0:T(8,128)(2,1)S(1)}, u32[]{:S(2)}, u32[]{:S(2)}) %collective-permute-start) | collective-permute-done | bytes 393248 | tf_op jit(solution)/shard_map/ppermute | solution.py:325
  13.5 2.4 %collective-permute-start.7 = (bf16[2,8,64,256]{3,2,1,0:T(8,128)(2,1)S(1)}, bf16[2,8,64,256]{3,2,1,0:T(8,128)(2,1)S(1)}, u32[]{:S(2)}, u32[]{:S(2)}) collective-permute-start(bf16[2,8,64,256]{3,2,1,0:T(8,128)(2,1)S(1)} %norm.1.refs_0_), channel_id=1, source_target_pairs={{0,2},{2,0},{4,6},{6,4},{8,10},{10,8},{12,14},{14,12},{16,18},{18,... | collective-permute-start | bytes 1572872 | tf_op jit(solution)/shard_map/ppermute | solution.py:386
  16.7 1.9 %collective-permute-start.8 = (bf16[2,8,64,256]{3,2,1,0:T(8,128)(2,1)S(1)}, bf16[2,8,64,256]{3,2,1,0:T(8,128)(2,1)S(1)}, u32[]{:S(2)}, u32[]{:S(2)}) collective-permute-start(bf16[2,8,64,256]{3,2,1,0:T(8,128)(2,1)S(1)} %collective-permute-done.6.refs_1_), channel_id=1, source_target_pairs={{0,2},{2,0},{4,6},{6,4},{8,10},{10,8},{12,14},{14,12},{16,18},{18,... | collective-permute-start | bytes 1572872 | tf_op jit(solution)/shard_map/ppermute | solution.py:386
  23.2 6.1 %collective-permute-done.4.refs_10_ = bf16[256,768]{1,0:T(8,128)(2,1)S(1)} collective-permute-done((bf16[256,768]{1,0:T(8,128)(2,1)S(1)}, bf16[256,768]{1,0:T(8,128)(2,1)S(1)}, u32[]{:S(2)}, u32[]{:S(2)}) %collective-permute-start.4) | collective-permute-done | bytes 393248 | tf_op jit(solution)/shard_map/ppermute | solution.py:325
  33.4 2.6 %collective-permute-done.10.refs_9_ = bf16[128,768]{1,0:T(8,128)(2,1)S(1)} collective-permute-done((bf16[128,768]{1,0:T(8,128)(2,1)S(1)}, bf16[128,768]{1,0:T(8,128)(2,1)S(1)}, u32[]{:S(2)}, u32[]{:S(2)}) %collective-permute-start.10) | collective-permute-done | bytes 196640 | tf_op jit(solution)/shard_map/ppermute | solution.py:331
  37.1 5.9 %collective-permute-start.12 = (f32[128,256]{1,0:T(8,128)S(1)}, f32[128,256]{1,0:T(8,128)S(1)}, u32[]{:S(2)}, u32[]{:S(2)}) collective-permute-start(f32[128,256]{1,0:T(8,128)S(1)} %get-tuple-element.137), channel_id=1, source_target_pairs={{0,2},{2,0},{4,6},{6,4},{8,10},{10,8},{12,14},{14,12},{16,18},{18,... | collective-permute-start | bytes 393224 | tf_op jit(solution)/shard_map/ppermute | solution.py:412
  44.0 1.3 %collective-permute-start.19 = (bf16[512,256]{1,0:T(8,128)(2,1)S(1)}, bf16[512,256]{1,0:T(8,128)(2,1)S(1)}, u32[]{:S(2)}, u32[]{:S(2)}) collective-permute-start(bf16[512,256]{1,0:T(8,128)(2,1)S(1)} %collective-permute-done.13.refs_8_), channel_id=1, source_target_pairs={{0,8},{2,10},{8,16},{10,18},{16,24},{18,26},{24,28},{26,30},{28,20... | collective-permute-start | bytes 786440 | tf_op jit(solution)/shard_map/ppermute | solution.py:325
  45.4 2.2 %collective-permute-start.11 = (f32[256,512]{1,0:T(8,128)S(1)}, f32[256,512]{1,0:T(8,128)S(1)}, u32[]{:S(2)}, u32[]{:S(2)}) collective-permute-start(f32[256,512]{1,0:T(8,128)S(1)} %get-tuple-element.130.mine_ref), channel_id=1, source_target_pairs={{0,2},{2,0},{4,6},{6,4},{8,10},{10,8},{12,14},{14,12},{16,18},{18,... | collective-permute-start | bytes 1572872 | tf_op jit(solution)/shard_map/ppermute | solution.py:413
  49.3 4.3 %collective-permute-done.15.refs_1_ = bf16[128,256]{1,0:T(8,128)(2,1)S(1)} collective-permute-done((bf16[128,256]{1,0:T(8,128)(2,1)S(1)}, bf16[128,256]{1,0:T(8,128)(2,1)S(1)}, u32[]{:S(2)}, u32[]{:S(2)}) %collective-permute-start.15) | collective-permute-done | bytes 65568 | tf_op jit(solution)/shard_map/ppermute | solution.py:326
  53.5 1.3 %collective-permute-start.25 = (bf16[512,256]{1,0:T(8,128)(2,1)S(1)}, bf16[512,256]{1,0:T(8,128)(2,1)S(1)}, u32[]{:S(2)}, u32[]{:S(2)}) collective-permute-start(bf16[512,256]{1,0:T(8,128)(2,1)S(1)} %collective-permute-done.19.refs_7_), channel_id=1, source_target_pairs={{0,8},{2,10},{8,16},{10,18},{16,24},{18,26},{24,28},{26,30},{28,20... | collective-permute-start | bytes 786440 | tf_op jit(solution)/shard_map/ppermute | solution.py:325
  55.1 1.4 %collective-permute-start.18 = (bf16[128,256]{1,0:T(8,128)(2,1)S(1)}, bf16[128,256]{1,0:T(8,128)(2,1)S(1)}, u32[]{:S(2)}, u32[]{:S(2)}) collective-permute-start(bf16[128,256]{1,0:T(8,128)(2,1)S(1)} %collective-permute-done.16.refs_8_), channel_id=1, source_target_pairs={{0,8},{2,10},{8,16},{10,18},{16,24},{18,26},{24,28},{26,30},{28,20... | collective-permute-start | bytes 196616 | tf_op jit(solution)/shard_map/ppermute | solution.py:325
  56.5 5.4 %collective-permute-done.17.refs_2_ = bf16[128,256]{1,0:T(8,128)(2,1)S(1)} collective-permute-done((bf16[128,256]{1,0:T(8,128)(2,1)S(1)}, bf16[128,256]{1,0:T(8,128)(2,1)S(1)}, u32[]{:S(2)}, u32[]{:S(2)}) %collective-permute-start.17) | collective-permute-done | bytes 65568 | tf_op jit(solution)/shard_map/ppermute | solution.py:326
  63.4 1.6 %collective-permute-done.21.refs_3_ = bf16[128,256]{1,0:T(8,128)(2,1)S(1)} collective-permute-done((bf16[128,256]{1,0:T(8,128)(2,1)S(1)}, bf16[128,256]{1,0:T(8,128)(2,1)S(1)}, u32[]{:S(2)}, u32[]{:S(2)}) %collective-permute-start.21) | collective-permute-done | bytes 65568 | tf_op jit(solution)/shard_map/ppermute | solution.py:326
  65.4 1.5 %collective-permute-start.27 = (bf16[256,256]{1,0:T(8,128)(2,1)S(1)}, bf16[256,256]{1,0:T(8,128)(2,1)S(1)}, u32[]{:S(2)}, u32[]{:S(2)}) collective-permute-start(bf16[256,256]{1,0:T(8,128)(2,1)S(1)} %slice.22), channel_id=1, source_target_pairs={{0,8},{2,10},{8,16},{10,18},{16,24},{18,26},{24,28},{26,30},{28,20... | collective-permute-start | bytes 393224 | tf_op jit(solution)/shard_map/ppermute | solution.py:330
  66.9 1.4 %collective-permute-start.23 = (bf16[64,256]{1,0:T(8,128)(2,1)S(1)}, bf16[64,256]{1,0:T(8,128)(2,1)S(1)}, u32[]{:S(2)}, u32[]{:S(2)}) collective-permute-start(bf16[64,256]{1,0:T(8,128)(2,1)S(1)} %slice.20), channel_id=1, source_target_pairs={{0,8},{2,10},{8,16},{10,18},{16,24},{18,26},{24,28},{26,30},{28,20... | collective-permute-start | bytes 98312 | tf_op jit(solution)/shard_map/ppermute | solution.py:330
  68.3 1.9 %collective-permute-done.24.refs_5_ = bf16[64,256]{1,0:T(8,128)(2,1)S(1)} collective-permute-done((bf16[64,256]{1,0:T(8,128)(2,1)S(1)}, bf16[64,256]{1,0:T(8,128)(2,1)S(1)}, u32[]{:S(2)}, u32[]{:S(2)}) %collective-permute-start.24) | collective-permute-done | bytes 32800 | tf_op jit(solution)/shard_map/ppermute | solution.py:331
  70.3 2.6 %attend.1.mine_ref = f32[256,640]{1,0:T(8,128)S(1)} custom-call(f32[256,512]{1,0:T(8,128)S(1)} %get-tuple-element.130.mine_ref, f32[256,512]{1,0:T(8,128)S(1)} %collective-permute-done.11.theirs_ref, f32[256,128]{1,0:T(8,128)S(1)} %get-tuple-element.131.cosine_ref, f32[256,128]{1,0:T(8,128)S(1)} %get-tuple-element.132.sine_ref, ...), custom_call_target="tpu_custom_call" | custom-call | tf_op jit(solution)/shard_map/attend/pallas_call | solution.py:434
  72.9 6.5 %collective-permute-start.29 = (f32[256,640]{1,0:T(8,128)S(1)}, f32[256,640]{1,0:T(8,128)S(1)}, u32[]{:S(2)}, u32[]{:S(2)}) collective-permute-start(f32[256,640]{1,0:T(8,128)S(1)} %attend.1.mine_ref), channel_id=1, source_target_pairs={{0,2},{2,0},{4,6},{6,4},{8,10},{10,8},{12,14},{14,12},{16,18},{18,... | collective-permute-start | bytes 1966088 | tf_op jit(solution)/shard_map/ppermute | solution.py:453
  79.4 1.7 %collective-permute-done.29.theirs_ref = f32[256,640]{1,0:T(8,128)S(1)} collective-permute-done((f32[256,640]{1,0:T(8,128)S(1)}, f32[256,640]{1,0:T(8,128)S(1)}, u32[]{:S(2)}, u32[]{:S(2)}) %collective-permute-start.29) | collective-permute-done | bytes 655392 | tf_op jit(solution)/shard_map/ppermute | solution.py:453
  81.1 1.3 %output.1 = (bf16[8,64,256]{2,1,0:T(8,128)(2,1)S(1)}, bf16[8,64,256]{2,1,0:T(8,128)(2,1)S(1)}, bf16[8,64,256]{2,1,0:T(8,128)(2,1)S(1)}, bf16[8,64,256]{2,1,0:T(8,128)(2,1)S(1)}) custom-call(f32[256,640]{1,0:T(8,128)S(1)} %attend.1.mine_ref, f32[256,640]{1,0:T(8,128)S(1)} %collective-permute-done.29.theirs_ref, bf16[512,256]{1,0:T(8,128)(2,1)S(1)} %copy-done.2, ...), custom_call_target="tpu_custom_call" | custom-call | tf_op jit(solution)/shard_map/output/pallas_call | solution.py:458
  84.5 5.5 %collective-permute-done.30.refs_1_ = bf16[8,64,256]{2,1,0:T(8,128)(2,1)S(1)} collective-permute-done((bf16[8,64,256]{2,1,0:T(8,128)(2,1)S(1)}, bf16[8,64,256]{2,1,0:T(8,128)(2,1)S(1)}, u32[]{:S(2)}, u32[]{:S(2)}) %collective-permute-start.30) | collective-permute-done | bytes 262176 | tf_op jit(solution)/shard_map/ppermute | solution.py:471
  90.0 6.1 %collective-permute-done.32.refs_3_ = bf16[8,64,256]{2,1,0:T(8,128)(2,1)S(1)} collective-permute-done((bf16[8,64,256]{2,1,0:T(8,128)(2,1)S(1)}, bf16[8,64,256]{2,1,0:T(8,128)(2,1)S(1)}, u32[]{:S(2)}, u32[]{:S(2)}) %collective-permute-start.32) | collective-permute-done | bytes 262176 | tf_op jit(solution)/shard_map/ppermute | solution.py:471
  (69 shorter events, 22.9 us)
Async XLA Ops:
  0.0 11.1 %collective-permute-start = (bf16[256,768]{1,0:T(8,128)(2,1)}, bf16[256,768]{1,0:T(8,128)(2,1)S(1)}, u32[]{:S(2)}, u32[]{:S(2)}) collective-permute-start(bf16[256,768]{1,0:T(8,128)(2,1)} %refs_4_), channel_id=1, source_target_pairs={{0,8},{2,10},{8,16},{10,18},{16,24},{18,26},{24,28},{26,30},{28,20... | collective-permute-start | bytes 1179656 | tf_op jit(solution)/shard_map/ppermute | solution.py:325
  2.1 9.9 %collective-permute-start.1 = (bf16[256,768]{1,0:T(8,128)(2,1)}, bf16[256,768]{1,0:T(8,128)(2,1)S(1)}, u32[]{:S(2)}, u32[]{:S(2)}) collective-permute-start(bf16[256,768]{1,0:T(8,128)(2,1)} %refs_4_), channel_id=1, source_target_pairs={{8,0},{10,2},{16,8},{18,10},{24,16},{26,18},{28,24},{30,26},{20,28... | collective-permute-start | bytes 1179656 | tf_op jit(solution)/shard_map/ppermute | solution.py:326
  4.2 12.5 %collective-permute-start.6 = (bf16[2,8,64,256]{3,2,1,0:T(8,128)(2,1)S(1)}, bf16[2,8,64,256]{3,2,1,0:T(8,128)(2,1)S(1)}, u32[]{:S(2)}, u32[]{:S(2)}) collective-permute-start(bf16[2,8,64,256]{3,2,1,0:T(8,128)(2,1)S(1)} %norm.1.refs_0_), channel_id=1, source_target_pairs={{0,1},{1,0},{2,3},{3,2},{4,5},{5,4},{6,7},{7,6},{8,9},{9,8},{10,11... | collective-permute-start | bytes 1572872 | tf_op jit(solution)/shard_map/ppermute | solution.py:381
  12.0 8.7 %collective-permute-start.2 = (bf16[256,768]{1,0:T(8,128)(2,1)S(1)}, bf16[256,768]{1,0:T(8,128)(2,1)S(1)}, u32[]{:S(2)}, u32[]{:S(2)}) collective-permute-start(bf16[256,768]{1,0:T(8,128)(2,1)S(1)} %collective-permute-done.refs_12_), channel_id=1, source_target_pairs={{0,8},{2,10},{8,16},{10,18},{16,24},{18,26},{24,28},{26,30},{28,20... | collective-permute-start | bytes 1179656 | tf_op jit(solution)/shard_map/ppermute | solution.py:325
  13.3 8.5 %collective-permute-start.3 = (bf16[256,768]{1,0:T(8,128)(2,1)S(1)}, bf16[256,768]{1,0:T(8,128)(2,1)S(1)}, u32[]{:S(2)}, u32[]{:S(2)}) collective-permute-start(bf16[256,768]{1,0:T(8,128)(2,1)S(1)} %collective-permute-done.1.refs_5_), channel_id=1, source_target_pairs={{8,0},{10,2},{16,8},{18,10},{24,16},{26,18},{28,24},{30,26},{20,28... | collective-permute-start | bytes 1179656 | tf_op jit(solution)/shard_map/ppermute | solution.py:326
  13.5 9.8 %collective-permute-start.7 = (bf16[2,8,64,256]{3,2,1,0:T(8,128)(2,1)S(1)}, bf16[2,8,64,256]{3,2,1,0:T(8,128)(2,1)S(1)}, u32[]{:S(2)}, u32[]{:S(2)}) collective-permute-start(bf16[2,8,64,256]{3,2,1,0:T(8,128)(2,1)S(1)} %norm.1.refs_0_), channel_id=1, source_target_pairs={{0,2},{2,0},{4,6},{6,4},{8,10},{10,8},{12,14},{14,12},{16,18},{18,... | collective-permute-start | bytes 1572872 | tf_op jit(solution)/shard_map/ppermute | solution.py:386
  16.7 6.5 %collective-permute-start.8 = (bf16[2,8,64,256]{3,2,1,0:T(8,128)(2,1)S(1)}, bf16[2,8,64,256]{3,2,1,0:T(8,128)(2,1)S(1)}, u32[]{:S(2)}, u32[]{:S(2)}) collective-permute-start(bf16[2,8,64,256]{3,2,1,0:T(8,128)(2,1)S(1)} %collective-permute-done.6.refs_1_), channel_id=1, source_target_pairs={{0,2},{2,0},{4,6},{6,4},{8,10},{10,8},{12,14},{14,12},{16,18},{18,... | collective-permute-start | bytes 1572872 | tf_op jit(solution)/shard_map/ppermute | solution.py:386
  21.8 7.5 %collective-permute-start.4 = (bf16[256,768]{1,0:T(8,128)(2,1)S(1)}, bf16[256,768]{1,0:T(8,128)(2,1)S(1)}, u32[]{:S(2)}, u32[]{:S(2)}) collective-permute-start(bf16[256,768]{1,0:T(8,128)(2,1)S(1)} %collective-permute-done.2.refs_11_), channel_id=1, source_target_pairs={{0,8},{2,10},{8,16},{10,18},{16,24},{18,26},{24,28},{26,30},{28,20... | collective-permute-start | bytes 1179656 | tf_op jit(solution)/shard_map/ppermute | solution.py:325
  23.1 7.3 %collective-permute-start.5 = (bf16[256,768]{1,0:T(8,128)(2,1)S(1)}, bf16[256,768]{1,0:T(8,128)(2,1)S(1)}, u32[]{:S(2)}, u32[]{:S(2)}) collective-permute-start(bf16[256,768]{1,0:T(8,128)(2,1)S(1)} %collective-permute-done.3.refs_6_), channel_id=1, source_target_pairs={{8,0},{10,2},{16,8},{18,10},{24,16},{26,18},{28,24},{30,26},{20,28... | collective-permute-start | bytes 1179656 | tf_op jit(solution)/shard_map/ppermute | solution.py:326
  31.9 12.1 %collective-permute-start.13 = (bf16[512,256]{1,0:T(8,128)(2,1)S(1)}, bf16[512,256]{1,0:T(8,128)(2,1)S(1)}, u32[]{:S(2)}, u32[]{:S(2)}) collective-permute-start(bf16[512,256]{1,0:T(8,128)(2,1)S(1)} %copy-done.2), channel_id=1, source_target_pairs={{0,8},{2,10},{8,16},{10,18},{16,24},{18,26},{24,28},{26,30},{28,20... | collective-permute-start | bytes 786440 | tf_op jit(solution)/shard_map/ppermute | solution.py:325
  33.1 10.8 %collective-permute-start.14 = (bf16[512,256]{1,0:T(8,128)(2,1)S(1)}, bf16[512,256]{1,0:T(8,128)(2,1)S(1)}, u32[]{:S(2)}, u32[]{:S(2)}) collective-permute-start(bf16[512,256]{1,0:T(8,128)(2,1)S(1)} %copy-done.2), channel_id=1, source_target_pairs={{8,0},{10,2},{16,8},{18,10},{24,16},{26,18},{28,24},{30,26},{20,28... | collective-permute-start | bytes 786440 | tf_op jit(solution)/shard_map/ppermute | solution.py:326
  37.1 6.8 %collective-permute-start.12 = (f32[128,256]{1,0:T(8,128)S(1)}, f32[128,256]{1,0:T(8,128)S(1)}, u32[]{:S(2)}, u32[]{:S(2)}) collective-permute-start(f32[128,256]{1,0:T(8,128)S(1)} %get-tuple-element.137), channel_id=1, source_target_pairs={{0,2},{2,0},{4,6},{6,4},{8,10},{10,8},{12,14},{14,12},{16,18},{18,... | collective-permute-start | bytes 393224 | tf_op jit(solution)/shard_map/ppermute | solution.py:412
  44.0 9.6 %collective-permute-start.19 = (bf16[512,256]{1,0:T(8,128)(2,1)S(1)}, bf16[512,256]{1,0:T(8,128)(2,1)S(1)}, u32[]{:S(2)}, u32[]{:S(2)}) collective-permute-start(bf16[512,256]{1,0:T(8,128)(2,1)S(1)} %collective-permute-done.13.refs_8_), channel_id=1, source_target_pairs={{0,8},{2,10},{8,16},{10,18},{16,24},{18,26},{24,28},{26,30},{28,20... | collective-permute-start | bytes 786440 | tf_op jit(solution)/shard_map/ppermute | solution.py:325
  45.3 8.3 %collective-permute-start.20 = (bf16[512,256]{1,0:T(8,128)(2,1)S(1)}, bf16[512,256]{1,0:T(8,128)(2,1)S(1)}, u32[]{:S(2)}, u32[]{:S(2)}) collective-permute-start(bf16[512,256]{1,0:T(8,128)(2,1)S(1)} %collective-permute-done.14.refs_1_), channel_id=1, source_target_pairs={{8,0},{10,2},{16,8},{18,10},{24,16},{26,18},{28,24},{30,26},{20,28... | collective-permute-start | bytes 786440 | tf_op jit(solution)/shard_map/ppermute | solution.py:326
  45.4 24.8 %collective-permute-start.11 = (f32[256,512]{1,0:T(8,128)S(1)}, f32[256,512]{1,0:T(8,128)S(1)}, u32[]{:S(2)}, u32[]{:S(2)}) collective-permute-start(f32[256,512]{1,0:T(8,128)S(1)} %get-tuple-element.130.mine_ref), channel_id=1, source_target_pairs={{0,2},{2,0},{4,6},{6,4},{8,10},{10,8},{12,14},{14,12},{16,18},{18,... | collective-permute-start | bytes 1572872 | tf_op jit(solution)/shard_map/ppermute | solution.py:413
  53.5 11.7 %collective-permute-start.25 = (bf16[512,256]{1,0:T(8,128)(2,1)S(1)}, bf16[512,256]{1,0:T(8,128)(2,1)S(1)}, u32[]{:S(2)}, u32[]{:S(2)}) collective-permute-start(bf16[512,256]{1,0:T(8,128)(2,1)S(1)} %collective-permute-done.19.refs_7_), channel_id=1, source_target_pairs={{0,8},{2,10},{8,16},{10,18},{16,24},{18,26},{24,28},{26,30},{28,20... | collective-permute-start | bytes 786440 | tf_op jit(solution)/shard_map/ppermute | solution.py:325
  54.8 10.4 %collective-permute-start.26 = (bf16[512,256]{1,0:T(8,128)(2,1)S(1)}, bf16[512,256]{1,0:T(8,128)(2,1)S(1)}, u32[]{:S(2)}, u32[]{:S(2)}) collective-permute-start(bf16[512,256]{1,0:T(8,128)(2,1)S(1)} %collective-permute-done.20.refs_2_), channel_id=1, source_target_pairs={{8,0},{10,2},{16,8},{18,10},{24,16},{26,18},{28,24},{30,26},{20,28... | collective-permute-start | bytes 786440 | tf_op jit(solution)/shard_map/ppermute | solution.py:326
  55.1 6.9 %collective-permute-start.17 = (bf16[128,256]{1,0:T(8,128)(2,1)S(1)}, bf16[128,256]{1,0:T(8,128)(2,1)S(1)}, u32[]{:S(2)}, u32[]{:S(2)}) collective-permute-start(bf16[128,256]{1,0:T(8,128)(2,1)S(1)} %collective-permute-done.15.refs_1_), channel_id=1, source_target_pairs={{8,0},{10,2},{16,8},{18,10},{24,16},{26,18},{28,24},{30,26},{20,28... | collective-permute-start | bytes 196616 | tf_op jit(solution)/shard_map/ppermute | solution.py:326
  55.1 6.8 %collective-permute-start.18 = (bf16[128,256]{1,0:T(8,128)(2,1)S(1)}, bf16[128,256]{1,0:T(8,128)(2,1)S(1)}, u32[]{:S(2)}, u32[]{:S(2)}) collective-permute-start(bf16[128,256]{1,0:T(8,128)(2,1)S(1)} %collective-permute-done.16.refs_8_), channel_id=1, source_target_pairs={{0,8},{2,10},{8,16},{10,18},{16,24},{18,26},{24,28},{26,30},{28,20... | collective-permute-start | bytes 196616 | tf_op jit(solution)/shard_map/ppermute | solution.py:325
  65.3 7.6 %collective-permute-start.28 = (bf16[256,256]{1,0:T(8,128)(2,1)S(1)}, bf16[256,256]{1,0:T(8,128)(2,1)S(1)}, u32[]{:S(2)}, u32[]{:S(2)}) collective-permute-start(bf16[256,256]{1,0:T(8,128)(2,1)S(1)} %slice.23), channel_id=1, source_target_pairs={{8,0},{10,2},{16,8},{18,10},{24,16},{26,18},{28,24},{30,26},{20,28... | collective-permute-start | bytes 393224 | tf_op jit(solution)/shard_map/ppermute | solution.py:331
  65.4 7.5 %collective-permute-start.27 = (bf16[256,256]{1,0:T(8,128)(2,1)S(1)}, bf16[256,256]{1,0:T(8,128)(2,1)S(1)}, u32[]{:S(2)}, u32[]{:S(2)}) collective-permute-start(bf16[256,256]{1,0:T(8,128)(2,1)S(1)} %slice.22), channel_id=1, source_target_pairs={{0,8},{2,10},{8,16},{10,18},{16,24},{18,26},{24,28},{26,30},{28,20... | collective-permute-start | bytes 393224 | tf_op jit(solution)/shard_map/ppermute | solution.py:330
  72.9 8.2 %collective-permute-start.29 = (f32[256,640]{1,0:T(8,128)S(1)}, f32[256,640]{1,0:T(8,128)S(1)}, u32[]{:S(2)}, u32[]{:S(2)}) collective-permute-start(f32[256,640]{1,0:T(8,128)S(1)} %attend.1.mine_ref), channel_id=1, source_target_pairs={{0,2},{2,0},{4,6},{6,4},{8,10},{10,8},{12,14},{14,12},{16,18},{18,... | collective-permute-start | bytes 1966088 | tf_op jit(solution)/shard_map/ppermute | solution.py:453
  82.4 7.6 %collective-permute-start.30 = (bf16[8,64,256]{2,1,0:T(8,128)(2,1)S(1)}, bf16[8,64,256]{2,1,0:T(8,128)(2,1)S(1)}, u32[]{:S(2)}, u32[]{:S(2)}) collective-permute-start(bf16[8,64,256]{2,1,0:T(8,128)(2,1)S(1)} %get-tuple-element.180), channel_id=1, source_target_pairs={{0,1},{1,0},{2,3},{3,2},{4,5},{5,4},{6,7},{7,6},{8,9},{9,8},{10,11... | collective-permute-start | bytes 786440 | tf_op jit(solution)/shard_map/ppermute | solution.py:471
  84.4 11.8 %collective-permute-start.32 = (bf16[8,64,256]{2,1,0:T(8,128)(2,1)S(1)}, bf16[8,64,256]{2,1,0:T(8,128)(2,1)S(1)}, u32[]{:S(2)}, u32[]{:S(2)}) collective-permute-start(bf16[8,64,256]{2,1,0:T(8,128)(2,1)S(1)} %get-tuple-element.182), channel_id=1, source_target_pairs={{0,3},{1,2},{2,1},{3,0},{4,7},{5,6},{6,5},{7,4},{8,11},{9,10},{10,... | collective-permute-start | bytes 786440 | tf_op jit(solution)/shard_map/ppermute | solution.py:471
  (16 other events, 105.3 us)

commit v22 on v21

--- a/solution.py
+++ b/solution.py
@@ -412,7 +412,6 @@
     theirs = lax.ppermute(theirs, "context", sibling)
     queries_theirs = lax.ppermute(queries, "context", sibling)
     mine, theirs = ordered((mine, theirs))
-    out_ring.step()
     kv = pl.pallas_call(
         keys_kernel,
         out_shape=jax.ShapeDtypeStruct((tokens_here, 2 * HD), jnp.bfloat16),
@@ -427,9 +426,11 @@
     out_ring.step()
     while not kv_ring.done():
         kv_ring.step()
+    while len(out_ring.up) <= (chips - 1) // 2:
+        out_ring.step()
+    kv_blocks = ordered(kv_ring.finish())
     while not out_ring.done():
         out_ring.step()
-    kv_blocks = ordered(kv_ring.finish())
 
     mixed = pl.pallas_call(
         attend_kernel,

time: 97.3 us -> 97.7 us (level)
  starting transfers between devices: 40.8 us -> 42.2 us
  waiting for transfers between devices: 46.8 us -> 45.8 us
    ppermute x9, waiting for transfers between devices: 14.2 us -> 9.4 us  [step(): self.down.append(lax.ppermute(down, 'context', back))]
    ppermute x3, waiting for transfers between devices: 4.58 us -> 8.03 us  [step(): lax.ppermute(down[half:], 'context', back)]
    ppermute x1, starting transfers between devices: 6.47 us -> 7.49 us  [per_device(): mixed_theirs = lax.ppermute(mixed, 'context', sibling)]
  transfers between devices with their start and end apart: 33 -> 33, of which waited for: 18 -> 20; matrix products, arithmetic and copies ran while one was open for 0% -> 0% of each run, Pallas kernels for 5% -> 5%
where the time goes in v22:
time: 97.7 us; the launch traced here: 97.5 us
  waiting for transfers between devices  45.8 us (47%)
  starting transfers between devices  42.2 us (43%)
  Pallas kernels  7.55 us (8%)
  local copies, waits for them, and re-layouts  1.82 us (2%)
    ppermute x9, waiting for transfers between devices, step(): self.up.append(lax.ppermute(up, 'context', ahead))  13.1 us
    ppermute x9, starting transfers between devices, step(): self.up.append(lax.ppermute(up, 'context', ahead))  12.5 us
    ppermute x3, waiting for transfers between devices, per_device(): part = lax.ppermute(part, ('context', 'tensor'), member(e, -d))  11.6 us
    ppermute x9, waiting for transfers between devices, step(): self.down.append(lax.ppermute(down, 'context', back))  9.4 us
    ppermute x3, waiting for transfers between devices, step(): lax.ppermute(down[half:], 'context', back)  8.03 us
    ppermute x1, starting transfers between devices, per_device(): mixed_theirs = lax.ppermute(mixed, 'context', sibling)  7.49 us
    ppermute x1, starting transfers between devices, per_device(): theirs = lax.ppermute(theirs, 'context', sibling)  5.86 us
    ppermute x2, starting transfers between devices, per_device(): normed += [lax.ppermute(rows, 'context', sibling) for rows in normed]  4.3 us
  transfers between devices with their start and end apart: 33, of which 20 were waited for; matrix products, arithmetic and copies ran while one was open for 0% of the time, Pallas kernels for 5%

profile of v22, /device:TPU:1, one launch (start us, length us, event | category | flops | bytes accessed | tf_op | source)
XLA Modules:
  0.0 97.5 jit_solution(7042942531135003214)
XLA Ops:
  0.0 2.1 %collective-permute-start = (bf16[256,768]{1,0:T(8,128)(2,1)}, bf16[256,768]{1,0:T(8,128)(2,1)S(1)}, u32[]{:S(2)}, u32[]{:S(2)}) collective-permute-start(bf16[256,768]{1,0:T(8,128)(2,1)} %refs_4_), channel_id=1, source_target_pairs={{0,8},{2,10},{8,16},{10,18},{16,24},{18,26},{24,28},{26,30},{28,20... | collective-permute-start | bytes 1179656 | tf_op jit(solution)/shard_map/ppermute | solution.py:325
  4.2 1.4 %collective-permute-start.6 = (bf16[2,8,64,256]{3,2,1,0:T(8,128)(2,1)S(1)}, bf16[2,8,64,256]{3,2,1,0:T(8,128)(2,1)S(1)}, u32[]{:S(2)}, u32[]{:S(2)}) collective-permute-start(bf16[2,8,64,256]{3,2,1,0:T(8,128)(2,1)S(1)} %norm.1.refs_0_), channel_id=1, source_target_pairs={{0,1},{1,0},{2,3},{3,2},{4,5},{5,4},{6,7},{7,6},{8,9},{9,8},{10,11... | collective-permute-start | bytes 1572872 | tf_op jit(solution)/shard_map/ppermute | solution.py:381
  5.6 5.5 %collective-permute-done.refs_12_ = bf16[256,768]{1,0:T(8,128)(2,1)S(1)} collective-permute-done((bf16[256,768]{1,0:T(8,128)(2,1)}, bf16[256,768]{1,0:T(8,128)(2,1)S(1)}, u32[]{:S(2)}, u32[]{:S(2)}) %collective-permute-start) | collective-permute-done | bytes 393248 | tf_op jit(solution)/shard_map/ppermute | solution.py:325
  13.5 2.4 %collective-permute-start.7 = (bf16[2,8,64,256]{3,2,1,0:T(8,128)(2,1)S(1)}, bf16[2,8,64,256]{3,2,1,0:T(8,128)(2,1)S(1)}, u32[]{:S(2)}, u32[]{:S(2)}) collective-permute-start(bf16[2,8,64,256]{3,2,1,0:T(8,128)(2,1)S(1)} %norm.1.refs_0_), channel_id=1, source_target_pairs={{0,2},{2,0},{4,6},{6,4},{8,10},{10,8},{12,14},{14,12},{16,18},{18,... | collective-permute-start | bytes 1572872 | tf_op jit(solution)/shard_map/ppermute | solution.py:386
  16.7 1.9 %collective-permute-start.8 = (bf16[2,8,64,256]{3,2,1,0:T(8,128)(2,1)S(1)}, bf16[2,8,64,256]{3,2,1,0:T(8,128)(2,1)S(1)}, u32[]{:S(2)}, u32[]{:S(2)}) collective-permute-start(bf16[2,8,64,256]{3,2,1,0:T(8,128)(2,1)S(1)} %collective-permute-done.6.refs_1_), channel_id=1, source_target_pairs={{0,2},{2,0},{4,6},{6,4},{8,10},{10,8},{12,14},{14,12},{16,18},{18,... | collective-permute-start | bytes 1572872 | tf_op jit(solution)/shard_map/ppermute | solution.py:386
  23.2 6.1 %collective-permute-done.4.refs_10_ = bf16[256,768]{1,0:T(8,128)(2,1)S(1)} collective-permute-done((bf16[256,768]{1,0:T(8,128)(2,1)S(1)}, bf16[256,768]{1,0:T(8,128)(2,1)S(1)}, u32[]{:S(2)}, u32[]{:S(2)}) %collective-permute-start.4) | collective-permute-done | bytes 393248 | tf_op jit(solution)/shard_map/ppermute | solution.py:325
  33.4 2.6 %collective-permute-done.10.refs_9_ = bf16[128,768]{1,0:T(8,128)(2,1)S(1)} collective-permute-done((bf16[128,768]{1,0:T(8,128)(2,1)S(1)}, bf16[128,768]{1,0:T(8,128)(2,1)S(1)}, u32[]{:S(2)}, u32[]{:S(2)}) %collective-permute-start.10) | collective-permute-done | bytes 196640 | tf_op jit(solution)/shard_map/ppermute | solution.py:331
  37.1 5.9 %collective-permute-start.12 = (f32[128,256]{1,0:T(8,128)S(1)}, f32[128,256]{1,0:T(8,128)S(1)}, u32[]{:S(2)}, u32[]{:S(2)}) collective-permute-start(f32[128,256]{1,0:T(8,128)S(1)} %get-tuple-element.137), channel_id=1, source_target_pairs={{0,2},{2,0},{4,6},{6,4},{8,10},{10,8},{12,14},{14,12},{16,18},{18,... | collective-permute-start | bytes 393224 | tf_op jit(solution)/shard_map/ppermute | solution.py:412
  45.6 1.6 %collective-permute-done.13.refs_1_ = bf16[128,256]{1,0:T(8,128)(2,1)S(1)} collective-permute-done((bf16[128,256]{1,0:T(8,128)(2,1)S(1)}, bf16[128,256]{1,0:T(8,128)(2,1)S(1)}, u32[]{:S(2)}, u32[]{:S(2)}) %collective-permute-start.13) | collective-permute-done | bytes 65568 | tf_op jit(solution)/shard_map/ppermute | solution.py:326
  47.7 1.3 %collective-permute-start.23 = (bf16[512,256]{1,0:T(8,128)(2,1)S(1)}, bf16[512,256]{1,0:T(8,128)(2,1)S(1)}, u32[]{:S(2)}, u32[]{:S(2)}) collective-permute-start(bf16[512,256]{1,0:T(8,128)(2,1)S(1)} %collective-permute-done.17.refs_8_), channel_id=1, source_target_pairs={{0,8},{2,10},{8,16},{10,18},{16,24},{18,26},{24,28},{26,30},{28,20... | collective-permute-start | bytes 786440 | tf_op jit(solution)/shard_map/ppermute | solution.py:325
  49.3 1.3 %collective-permute-start.16 = (bf16[128,256]{1,0:T(8,128)(2,1)S(1)}, bf16[128,256]{1,0:T(8,128)(2,1)S(1)}, u32[]{:S(2)}, u32[]{:S(2)}) collective-permute-start(bf16[128,256]{1,0:T(8,128)(2,1)S(1)} %collective-permute-done.14.refs_8_), channel_id=1, source_target_pairs={{0,8},{2,10},{8,16},{10,18},{16,24},{18,26},{24,28},{26,30},{28,20... | collective-permute-start | bytes 196616 | tf_op jit(solution)/shard_map/ppermute | solution.py:325
  50.6 2.6 %collective-permute-start.11 = (f32[256,512]{1,0:T(8,128)S(1)}, f32[256,512]{1,0:T(8,128)S(1)}, u32[]{:S(2)}, u32[]{:S(2)}) collective-permute-start(f32[256,512]{1,0:T(8,128)S(1)} %get-tuple-element.130.mine_ref), channel_id=1, source_target_pairs={{0,2},{2,0},{4,6},{6,4},{8,10},{10,8},{12,14},{14,12},{16,18},{18,... | collective-permute-start | bytes 1572872 | tf_op jit(solution)/shard_map/ppermute | solution.py:413
  53.2 3.2 %collective-permute-done.15.refs_2_ = bf16[128,256]{1,0:T(8,128)(2,1)S(1)} collective-permute-done((bf16[128,256]{1,0:T(8,128)(2,1)S(1)}, bf16[128,256]{1,0:T(8,128)(2,1)S(1)}, u32[]{:S(2)}, u32[]{:S(2)}) %collective-permute-start.15) | collective-permute-done | bytes 65568 | tf_op jit(solution)/shard_map/ppermute | solution.py:326
  57.9 1.6 %collective-permute-done.19.refs_3_ = bf16[128,256]{1,0:T(8,128)(2,1)S(1)} collective-permute-done((bf16[128,256]{1,0:T(8,128)(2,1)S(1)}, bf16[128,256]{1,0:T(8,128)(2,1)S(1)}, u32[]{:S(2)}, u32[]{:S(2)}) %collective-permute-start.19) | collective-permute-done | bytes 65568 | tf_op jit(solution)/shard_map/ppermute | solution.py:326
  59.7 1.3 %collective-permute-start.25 = (bf16[512,256]{1,0:T(8,128)(2,1)S(1)}, bf16[512,256]{1,0:T(8,128)(2,1)S(1)}, u32[]{:S(2)}, u32[]{:S(2)}) collective-permute-start(bf16[512,256]{1,0:T(8,128)(2,1)S(1)} %collective-permute-done.23.refs_7_), channel_id=1, source_target_pairs={{0,8},{2,10},{8,16},{10,18},{16,24},{18,26},{24,28},{26,30},{28,20... | collective-permute-start | bytes 786440 | tf_op jit(solution)/shard_map/ppermute | solution.py:325
  61.4 1.3 %collective-permute-start.21 = (bf16[64,256]{1,0:T(8,128)(2,1)S(1)}, bf16[64,256]{1,0:T(8,128)(2,1)S(1)}, u32[]{:S(2)}, u32[]{:S(2)}) collective-permute-start(bf16[64,256]{1,0:T(8,128)(2,1)S(1)} %slice.20), channel_id=1, source_target_pairs={{0,8},{2,10},{8,16},{10,18},{16,24},{18,26},{24,28},{26,30},{28,20... | collective-permute-start | bytes 98312 | tf_op jit(solution)/shard_map/ppermute | solution.py:330
  62.7 3.9 %collective-permute-done.22.refs_5_ = bf16[64,256]{1,0:T(8,128)(2,1)S(1)} collective-permute-done((bf16[64,256]{1,0:T(8,128)(2,1)S(1)}, bf16[64,256]{1,0:T(8,128)(2,1)S(1)}, u32[]{:S(2)}, u32[]{:S(2)}) %collective-permute-start.22) | collective-permute-done | bytes 32800 | tf_op jit(solution)/shard_map/ppermute | solution.py:331
  68.2 2.6 %attend.1.mine_ref = f32[256,640]{1,0:T(8,128)S(1)} custom-call(f32[256,512]{1,0:T(8,128)S(1)} %get-tuple-element.130.mine_ref, f32[256,512]{1,0:T(8,128)S(1)} %collective-permute-done.11.theirs_ref, f32[256,128]{1,0:T(8,128)S(1)} %get-tuple-element.131.cosine_ref, f32[256,128]{1,0:T(8,128)S(1)} %get-tuple-element.132.sine_ref, ...), custom_call_target="tpu_custom_call" | custom-call | tf_op jit(solution)/shard_map/attend/pallas_call | solution.py:435
  70.8 1.5 %collective-permute-done.28.refs_5_ = bf16[256,256]{1,0:T(8,128)(2,1)S(1)} collective-permute-done((bf16[256,256]{1,0:T(8,128)(2,1)S(1)}, bf16[256,256]{1,0:T(8,128)(2,1)S(1)}, u32[]{:S(2)}, u32[]{:S(2)}) %collective-permute-start.28) | collective-permute-done | bytes 131104 | tf_op jit(solution)/shard_map/ppermute | solution.py:331
  72.3 7.5 %collective-permute-start.29 = (f32[256,640]{1,0:T(8,128)S(1)}, f32[256,640]{1,0:T(8,128)S(1)}, u32[]{:S(2)}, u32[]{:S(2)}) collective-permute-start(f32[256,640]{1,0:T(8,128)S(1)} %attend.1.mine_ref), channel_id=1, source_target_pairs={{0,2},{2,0},{4,6},{6,4},{8,10},{10,8},{12,14},{14,12},{16,18},{18,... | collective-permute-start | bytes 1966088 | tf_op jit(solution)/shard_map/ppermute | solution.py:454
  79.8 1.7 %collective-permute-done.29.theirs_ref = f32[256,640]{1,0:T(8,128)S(1)} collective-permute-done((f32[256,640]{1,0:T(8,128)S(1)}, f32[256,640]{1,0:T(8,128)S(1)}, u32[]{:S(2)}, u32[]{:S(2)}) %collective-permute-start.29) | collective-permute-done | bytes 655392 | tf_op jit(solution)/shard_map/ppermute | solution.py:454
  81.5 1.3 %output.1 = (bf16[8,64,256]{2,1,0:T(8,128)(2,1)S(1)}, bf16[8,64,256]{2,1,0:T(8,128)(2,1)S(1)}, bf16[8,64,256]{2,1,0:T(8,128)(2,1)S(1)}, bf16[8,64,256]{2,1,0:T(8,128)(2,1)S(1)}) custom-call(f32[256,640]{1,0:T(8,128)S(1)} %attend.1.mine_ref, f32[256,640]{1,0:T(8,128)S(1)} %collective-permute-done.29.theirs_ref, bf16[512,256]{1,0:T(8,128)(2,1)S(1)} %copy-done.2, ...), custom_call_target="tpu_custom_call" | custom-call | tf_op jit(solution)/shard_map/output/pallas_call | solution.py:459
  84.9 5.5 %collective-permute-done.30.refs_1_ = bf16[8,64,256]{2,1,0:T(8,128)(2,1)S(1)} collective-permute-done((bf16[8,64,256]{2,1,0:T(8,128)(2,1)S(1)}, bf16[8,64,256]{2,1,0:T(8,128)(2,1)S(1)}, u32[]{:S(2)}, u32[]{:S(2)}) %collective-permute-start.30) | collective-permute-done | bytes 262176 | tf_op jit(solution)/shard_map/ppermute | solution.py:472
  90.4 6.1 %collective-permute-done.32.refs_3_ = bf16[8,64,256]{2,1,0:T(8,128)(2,1)S(1)} collective-permute-done((bf16[8,64,256]{2,1,0:T(8,128)(2,1)S(1)}, bf16[8,64,256]{2,1,0:T(8,128)(2,1)S(1)}, u32[]{:S(2)}, u32[]{:S(2)}) %collective-permute-start.32) | collective-permute-done | bytes 262176 | tf_op jit(solution)/shard_map/ppermute | solution.py:472
  (69 shorter events, 24.9 us)
Async XLA Ops:
  0.0 11.1 %collective-permute-start = (bf16[256,768]{1,0:T(8,128)(2,1)}, bf16[256,768]{1,0:T(8,128)(2,1)S(1)}, u32[]{:S(2)}, u32[]{:S(2)}) collective-permute-start(bf16[256,768]{1,0:T(8,128)(2,1)} %refs_4_), channel_id=1, source_target_pairs={{0,8},{2,10},{8,16},{10,18},{16,24},{18,26},{24,28},{26,30},{28,20... | collective-permute-start | bytes 1179656 | tf_op jit(solution)/shard_map/ppermute | solution.py:325
  2.1 9.9 %collective-permute-start.1 = (bf16[256,768]{1,0:T(8,128)(2,1)}, bf16[256,768]{1,0:T(8,128)(2,1)S(1)}, u32[]{:S(2)}, u32[]{:S(2)}) collective-permute-start(bf16[256,768]{1,0:T(8,128)(2,1)} %refs_4_), channel_id=1, source_target_pairs={{8,0},{10,2},{16,8},{18,10},{24,16},{26,18},{28,24},{30,26},{20,28... | collective-permute-start | bytes 1179656 | tf_op jit(solution)/shard_map/ppermute | solution.py:326
  4.2 12.5 %collective-permute-start.6 = (bf16[2,8,64,256]{3,2,1,0:T(8,128)(2,1)S(1)}, bf16[2,8,64,256]{3,2,1,0:T(8,128)(2,1)S(1)}, u32[]{:S(2)}, u32[]{:S(2)}) collective-permute-start(bf16[2,8,64,256]{3,2,1,0:T(8,128)(2,1)S(1)} %norm.1.refs_0_), channel_id=1, source_target_pairs={{0,1},{1,0},{2,3},{3,2},{4,5},{5,4},{6,7},{7,6},{8,9},{9,8},{10,11... | collective-permute-start | bytes 1572872 | tf_op jit(solution)/shard_map/ppermute | solution.py:381
  12.0 8.7 %collective-permute-start.2 = (bf16[256,768]{1,0:T(8,128)(2,1)S(1)}, bf16[256,768]{1,0:T(8,128)(2,1)S(1)}, u32[]{:S(2)}, u32[]{:S(2)}) collective-permute-start(bf16[256,768]{1,0:T(8,128)(2,1)S(1)} %collective-permute-done.refs_12_), channel_id=1, source_target_pairs={{0,8},{2,10},{8,16},{10,18},{16,24},{18,26},{24,28},{26,30},{28,20... | collective-permute-start | bytes 1179656 | tf_op jit(solution)/shard_map/ppermute | solution.py:325
  13.3 8.5 %collective-permute-start.3 = (bf16[256,768]{1,0:T(8,128)(2,1)S(1)}, bf16[256,768]{1,0:T(8,128)(2,1)S(1)}, u32[]{:S(2)}, u32[]{:S(2)}) collective-permute-start(bf16[256,768]{1,0:T(8,128)(2,1)S(1)} %collective-permute-done.1.refs_5_), channel_id=1, source_target_pairs={{8,0},{10,2},{16,8},{18,10},{24,16},{26,18},{28,24},{30,26},{20,28... | collective-permute-start | bytes 1179656 | tf_op jit(solution)/shard_map/ppermute | solution.py:326
  13.5 9.8 %collective-permute-start.7 = (bf16[2,8,64,256]{3,2,1,0:T(8,128)(2,1)S(1)}, bf16[2,8,64,256]{3,2,1,0:T(8,128)(2,1)S(1)}, u32[]{:S(2)}, u32[]{:S(2)}) collective-permute-start(bf16[2,8,64,256]{3,2,1,0:T(8,128)(2,1)S(1)} %norm.1.refs_0_), channel_id=1, source_target_pairs={{0,2},{2,0},{4,6},{6,4},{8,10},{10,8},{12,14},{14,12},{16,18},{18,... | collective-permute-start | bytes 1572872 | tf_op jit(solution)/shard_map/ppermute | solution.py:386
  16.7 6.5 %collective-permute-start.8 = (bf16[2,8,64,256]{3,2,1,0:T(8,128)(2,1)S(1)}, bf16[2,8,64,256]{3,2,1,0:T(8,128)(2,1)S(1)}, u32[]{:S(2)}, u32[]{:S(2)}) collective-permute-start(bf16[2,8,64,256]{3,2,1,0:T(8,128)(2,1)S(1)} %collective-permute-done.6.refs_1_), channel_id=1, source_target_pairs={{0,2},{2,0},{4,6},{6,4},{8,10},{10,8},{12,14},{14,12},{16,18},{18,... | collective-permute-start | bytes 1572872 | tf_op jit(solution)/shard_map/ppermute | solution.py:386
  21.8 7.5 %collective-permute-start.4 = (bf16[256,768]{1,0:T(8,128)(2,1)S(1)}, bf16[256,768]{1,0:T(8,128)(2,1)S(1)}, u32[]{:S(2)}, u32[]{:S(2)}) collective-permute-start(bf16[256,768]{1,0:T(8,128)(2,1)S(1)} %collective-permute-done.2.refs_11_), channel_id=1, source_target_pairs={{0,8},{2,10},{8,16},{10,18},{16,24},{18,26},{24,28},{26,30},{28,20... | collective-permute-start | bytes 1179656 | tf_op jit(solution)/shard_map/ppermute | solution.py:325
  23.1 7.3 %collective-permute-start.5 = (bf16[256,768]{1,0:T(8,128)(2,1)S(1)}, bf16[256,768]{1,0:T(8,128)(2,1)S(1)}, u32[]{:S(2)}, u32[]{:S(2)}) collective-permute-start(bf16[256,768]{1,0:T(8,128)(2,1)S(1)} %collective-permute-done.3.refs_6_), channel_id=1, source_target_pairs={{8,0},{10,2},{16,8},{18,10},{24,16},{26,18},{28,24},{30,26},{20,28... | collective-permute-start | bytes 1179656 | tf_op jit(solution)/shard_map/ppermute | solution.py:326
  30.4 5.6 %collective-permute-start.10 = (bf16[128,768]{1,0:T(8,128)(2,1)S(1)}, bf16[128,768]{1,0:T(8,128)(2,1)S(1)}, u32[]{:S(2)}, u32[]{:S(2)}) collective-permute-start(bf16[128,768]{1,0:T(8,128)(2,1)S(1)} %slice.19), channel_id=1, source_target_pairs={{8,0},{10,2},{16,8},{18,10},{24,16},{26,18},{28,24},{30,26},{20,28... | collective-permute-start | bytes 589832 | tf_op jit(solution)/shard_map/ppermute | solution.py:331
  31.9 15.8 %collective-permute-start.17 = (bf16[512,256]{1,0:T(8,128)(2,1)S(1)}, bf16[512,256]{1,0:T(8,128)(2,1)S(1)}, u32[]{:S(2)}, u32[]{:S(2)}) collective-permute-start(bf16[512,256]{1,0:T(8,128)(2,1)S(1)} %copy-done.2), channel_id=1, source_target_pairs={{0,8},{2,10},{8,16},{10,18},{16,24},{18,26},{24,28},{26,30},{28,20... | collective-permute-start | bytes 786440 | tf_op jit(solution)/shard_map/ppermute | solution.py:325
  33.1 14.6 %collective-permute-start.18 = (bf16[512,256]{1,0:T(8,128)(2,1)S(1)}, bf16[512,256]{1,0:T(8,128)(2,1)S(1)}, u32[]{:S(2)}, u32[]{:S(2)}) collective-permute-start(bf16[512,256]{1,0:T(8,128)(2,1)S(1)} %copy-done.2), channel_id=1, source_target_pairs={{8,0},{10,2},{16,8},{18,10},{24,16},{26,18},{28,24},{30,26},{20,28... | collective-permute-start | bytes 786440 | tf_op jit(solution)/shard_map/ppermute | solution.py:326
  37.1 6.8 %collective-permute-start.12 = (f32[128,256]{1,0:T(8,128)S(1)}, f32[128,256]{1,0:T(8,128)S(1)}, u32[]{:S(2)}, u32[]{:S(2)}) collective-permute-start(f32[128,256]{1,0:T(8,128)S(1)} %get-tuple-element.137), channel_id=1, source_target_pairs={{0,2},{2,0},{4,6},{6,4},{8,10},{10,8},{12,14},{14,12},{16,18},{18,... | collective-permute-start | bytes 393224 | tf_op jit(solution)/shard_map/ppermute | solution.py:412
  47.7 12.0 %collective-permute-start.23 = (bf16[512,256]{1,0:T(8,128)(2,1)S(1)}, bf16[512,256]{1,0:T(8,128)(2,1)S(1)}, u32[]{:S(2)}, u32[]{:S(2)}) collective-permute-start(bf16[512,256]{1,0:T(8,128)(2,1)S(1)} %collective-permute-done.17.refs_8_), channel_id=1, source_target_pairs={{0,8},{2,10},{8,16},{10,18},{16,24},{18,26},{24,28},{26,30},{28,20... | collective-permute-start | bytes 786440 | tf_op jit(solution)/shard_map/ppermute | solution.py:325
  49.0 10.7 %collective-permute-start.24 = (bf16[512,256]{1,0:T(8,128)(2,1)S(1)}, bf16[512,256]{1,0:T(8,128)(2,1)S(1)}, u32[]{:S(2)}, u32[]{:S(2)}) collective-permute-start(bf16[512,256]{1,0:T(8,128)(2,1)S(1)} %collective-permute-done.18.refs_1_), channel_id=1, source_target_pairs={{8,0},{10,2},{16,8},{18,10},{24,16},{26,18},{28,24},{30,26},{20,28... | collective-permute-start | bytes 786440 | tf_op jit(solution)/shard_map/ppermute | solution.py:326
  49.2 7.3 %collective-permute-start.15 = (bf16[128,256]{1,0:T(8,128)(2,1)S(1)}, bf16[128,256]{1,0:T(8,128)(2,1)S(1)}, u32[]{:S(2)}, u32[]{:S(2)}) collective-permute-start(bf16[128,256]{1,0:T(8,128)(2,1)S(1)} %collective-permute-done.13.refs_1_), channel_id=1, source_target_pairs={{8,0},{10,2},{16,8},{18,10},{24,16},{26,18},{28,24},{30,26},{20,28... | collective-permute-start | bytes 196616 | tf_op jit(solution)/shard_map/ppermute | solution.py:326
  49.3 7.1 %collective-permute-start.16 = (bf16[128,256]{1,0:T(8,128)(2,1)S(1)}, bf16[128,256]{1,0:T(8,128)(2,1)S(1)}, u32[]{:S(2)}, u32[]{:S(2)}) collective-permute-start(bf16[128,256]{1,0:T(8,128)(2,1)S(1)} %collective-permute-done.14.refs_8_), channel_id=1, source_target_pairs={{0,8},{2,10},{8,16},{10,18},{16,24},{18,26},{24,28},{26,30},{28,20... | collective-permute-start | bytes 196616 | tf_op jit(solution)/shard_map/ppermute | solution.py:325
  50.6 17.5 %collective-permute-start.11 = (f32[256,512]{1,0:T(8,128)S(1)}, f32[256,512]{1,0:T(8,128)S(1)}, u32[]{:S(2)}, u32[]{:S(2)}) collective-permute-start(f32[256,512]{1,0:T(8,128)S(1)} %get-tuple-element.130.mine_ref), channel_id=1, source_target_pairs={{0,2},{2,0},{4,6},{6,4},{8,10},{10,8},{12,14},{14,12},{16,18},{18,... | collective-permute-start | bytes 1572872 | tf_op jit(solution)/shard_map/ppermute | solution.py:413
  59.7 6.9 %collective-permute-start.25 = (bf16[512,256]{1,0:T(8,128)(2,1)S(1)}, bf16[512,256]{1,0:T(8,128)(2,1)S(1)}, u32[]{:S(2)}, u32[]{:S(2)}) collective-permute-start(bf16[512,256]{1,0:T(8,128)(2,1)S(1)} %collective-permute-done.23.refs_7_), channel_id=1, source_target_pairs={{0,8},{2,10},{8,16},{10,18},{16,24},{18,26},{24,28},{26,30},{28,20... | collective-permute-start | bytes 786440 | tf_op jit(solution)/shard_map/ppermute | solution.py:325
  61.0 5.6 %collective-permute-start.26 = (bf16[512,256]{1,0:T(8,128)(2,1)S(1)}, bf16[512,256]{1,0:T(8,128)(2,1)S(1)}, u32[]{:S(2)}, u32[]{:S(2)}) collective-permute-start(bf16[512,256]{1,0:T(8,128)(2,1)S(1)} %collective-permute-done.24.refs_2_), channel_id=1, source_target_pairs={{8,0},{10,2},{16,8},{18,10},{24,16},{26,18},{28,24},{30,26},{20,28... | collective-permute-start | bytes 786440 | tf_op jit(solution)/shard_map/ppermute | solution.py:326
  72.3 9.2 %collective-permute-start.29 = (f32[256,640]{1,0:T(8,128)S(1)}, f32[256,640]{1,0:T(8,128)S(1)}, u32[]{:S(2)}, u32[]{:S(2)}) collective-permute-start(f32[256,640]{1,0:T(8,128)S(1)} %attend.1.mine_ref), channel_id=1, source_target_pairs={{0,2},{2,0},{4,6},{6,4},{8,10},{10,8},{12,14},{14,12},{16,18},{18,... | collective-permute-start | bytes 1966088 | tf_op jit(solution)/shard_map/ppermute | solution.py:454
  82.8 7.6 %collective-permute-start.30 = (bf16[8,64,256]{2,1,0:T(8,128)(2,1)S(1)}, bf16[8,64,256]{2,1,0:T(8,128)(2,1)S(1)}, u32[]{:S(2)}, u32[]{:S(2)}) collective-permute-start(bf16[8,64,256]{2,1,0:T(8,128)(2,1)S(1)} %get-tuple-element.180), channel_id=1, source_target_pairs={{0,1},{1,0},{2,3},{3,2},{4,5},{5,4},{6,7},{7,6},{8,9},{9,8},{10,11... | collective-permute-start | bytes 786440 | tf_op jit(solution)/shard_map/ppermute | solution.py:472
  84.1 6.3 %collective-permute-start.31 = (bf16[8,64,256]{2,1,0:T(8,128)(2,1)S(1)}, bf16[8,64,256]{2,1,0:T(8,128)(2,1)S(1)}, u32[]{:S(2)}, u32[]{:S(2)}) collective-permute-start(bf16[8,64,256]{2,1,0:T(8,128)(2,1)S(1)} %get-tuple-element.181), channel_id=1, source_target_pairs={{0,2},{1,3},{2,0},{3,1},{4,6},{5,7},{6,4},{7,5},{8,10},{9,11},{10,... | collective-permute-start | bytes 786440 | tf_op jit(solution)/shard_map/ppermute | solution.py:472
  84.8 11.8 %collective-permute-start.32 = (bf16[8,64,256]{2,1,0:T(8,128)(2,1)S(1)}, bf16[8,64,256]{2,1,0:T(8,128)(2,1)S(1)}, u32[]{:S(2)}, u32[]{:S(2)}) collective-permute-start(bf16[8,64,256]{2,1,0:T(8,128)(2,1)S(1)} %get-tuple-element.182), channel_id=1, source_target_pairs={{0,3},{1,2},{2,1},{3,0},{4,7},{5,6},{6,5},{7,4},{8,11},{9,10},{10,... | collective-permute-start | bytes 786440 | tf_op jit(solution)/shard_map/ppermute | solution.py:472
  (16 other events, 103.4 us)

commit v23 on v20

--- a/solution.py
+++ b/solution.py
@@ -419,6 +419,8 @@
     kv = lax.all_to_all(
         kv, "context", split_axis=0, concat_axis=0, axis_index_groups=same_core, tiled=True
     )
+    out_ring.step()
+    out_ring.step()
     (kv,) = ordered((kv,))
 
     mixed = pl.pallas_call(
@@ -438,7 +440,6 @@
         key_orig,
         kv,
     )
-    out_ring.step()
     (mixed,) = ordered((mixed,))
     mixed_theirs = lax.ppermute(mixed, "context", sibling)
 

time: 105 us -> 104 us (level)
  waiting for transfers between devices: 51.7 us -> 49.6 us
    all_to_all x1, waiting for transfers between devices: 11.2 us -> 0.01 us  [per_device(): lax.all_to_all(kv, 'context', split_axis=0, concat_axis=0, axis_index_gro...]
    ppermute x6, waiting for transfers between devices: 18.9 us -> 27.8 us  [step(): self.up.append(lax.ppermute(up, 'context', ahead))]
    ppermute x6, starting transfers between devices: 9.81 us -> 7.79 us  [output(): part = lax.ppermute(part, ('context', 'tensor'), member(e, -d))]
    ppermute x1, starting transfers between devices: 1.08 us -> 2.77 us  [per_device(): mixed_theirs = lax.ppermute(mixed, 'context', sibling)]
  transfers between devices with their start and end apart: 29 -> 29, of which waited for: 19 -> 19; matrix products, arithmetic and copies ran while one was open for 0% -> 0% of each run, Pallas kernels for 2% -> 4%
where the time goes in v23:
time: 104 us; the launch traced here: 103 us
  waiting for transfers between devices  49.6 us (48%)
  starting transfers between devices  42.5 us (41%)
  Pallas kernels  9.21 us (9%)
  local copies, waits for them, and re-layouts  1.81 us (2%)
    ppermute x6, waiting for transfers between devices, step(): self.up.append(lax.ppermute(up, 'context', ahead))  27.8 us
    ppermute x6, starting transfers between devices, step(): self.up.append(lax.ppermute(up, 'context', ahead))  12 us
    ppermute x6, waiting for transfers between devices, step(): self.down.append(lax.ppermute(down, 'context', back))  10.1 us
    ppermute x6, starting transfers between devices, output(): part = lax.ppermute(part, ('context', 'tensor'), member(e, -d))  7.79 us
    ppermute x1, starting transfers between devices, per_device(): theirs = lax.ppermute(theirs, 'context', sibling)  5.86 us
    ppermute x6, waiting for transfers between devices, output(): part = lax.ppermute(part, ('context', 'tensor'), member(e, -d))  4.39 us
    ppermute x2, waiting for transfers between devices, step(): lax.ppermute(down[half:], 'context', back)  4.32 us
    ppermute x2, starting transfers between devices, per_device(): normed += [lax.ppermute(rows, 'context', sibling) for rows in normed]  4.3 us
  transfers between devices with their start and end apart: 29, of which 19 were waited for; matrix products, arithmetic and copies ran while one was open for 0% of the time, Pallas kernels for 4%

profile of v23, /device:TPU:1, one launch (start us, length us, event | category | flops | bytes accessed | tf_op | source)
XLA Modules:
  0.0 103.2 jit_solution(11398466885068728617)
XLA Ops:
  0.0 2.1 %collective-permute-start = (bf16[256,768]{1,0:T(8,128)(2,1)}, bf16[256,768]{1,0:T(8,128)(2,1)S(1)}, u32[]{:S(2)}, u32[]{:S(2)}) collective-permute-start(bf16[256,768]{1,0:T(8,128)(2,1)} %refs_4_), channel_id=1, source_target_pairs={{0,8},{2,10},{8,16},{10,18},{16,24},{18,26},{24,28},{26,30},{28,20... | collective-permute-start | bytes 1179656 | tf_op jit(solution)/shard_map/ppermute | solution.py:314
  4.2 1.4 %collective-permute-start.6 = (bf16[2,8,64,256]{3,2,1,0:T(8,128)(2,1)S(1)}, bf16[2,8,64,256]{3,2,1,0:T(8,128)(2,1)S(1)}, u32[]{:S(2)}, u32[]{:S(2)}) collective-permute-start(bf16[2,8,64,256]{3,2,1,0:T(8,128)(2,1)S(1)} %norm.1.refs_0_), channel_id=1, source_target_pairs={{0,1},{1,0},{2,3},{3,2},{4,5},{5,4},{6,7},{7,6},{8,9},{9,8},{10,11... | collective-permute-start | bytes 1572872 | tf_op jit(solution)/shard_map/ppermute | solution.py:376
  5.6 5.5 %collective-permute-done.refs_12_ = bf16[256,768]{1,0:T(8,128)(2,1)S(1)} collective-permute-done((bf16[256,768]{1,0:T(8,128)(2,1)}, bf16[256,768]{1,0:T(8,128)(2,1)S(1)}, u32[]{:S(2)}, u32[]{:S(2)}) %collective-permute-start) | collective-permute-done | bytes 393248 | tf_op jit(solution)/shard_map/ppermute | solution.py:314
  12.0 1.3 %collective-permute-start.2 = (bf16[256,768]{1,0:T(8,128)(2,1)S(1)}, bf16[256,768]{1,0:T(8,128)(2,1)S(1)}, u32[]{:S(2)}, u32[]{:S(2)}) collective-permute-start(bf16[256,768]{1,0:T(8,128)(2,1)S(1)} %collective-permute-done.refs_12_), channel_id=1, source_target_pairs={{0,8},{2,10},{8,16},{10,18},{16,24},{18,26},{24,28},{26,30},{28,20... | collective-permute-start | bytes 1179656 | tf_op jit(solution)/shard_map/ppermute | solution.py:314
  13.5 2.4 %collective-permute-start.7 = (bf16[2,8,64,256]{3,2,1,0:T(8,128)(2,1)S(1)}, bf16[2,8,64,256]{3,2,1,0:T(8,128)(2,1)S(1)}, u32[]{:S(2)}, u32[]{:S(2)}) collective-permute-start(bf16[2,8,64,256]{3,2,1,0:T(8,128)(2,1)S(1)} %norm.1.refs_0_), channel_id=1, source_target_pairs={{0,2},{2,0},{4,6},{6,4},{8,10},{10,8},{12,14},{14,12},{16,18},{18,... | collective-permute-start | bytes 1572872 | tf_op jit(solution)/shard_map/ppermute | solution.py:381
  16.7 1.9 %collective-permute-start.8 = (bf16[2,8,64,256]{3,2,1,0:T(8,128)(2,1)S(1)}, bf16[2,8,64,256]{3,2,1,0:T(8,128)(2,1)S(1)}, u32[]{:S(2)}, u32[]{:S(2)}) collective-permute-start(bf16[2,8,64,256]{3,2,1,0:T(8,128)(2,1)S(1)} %collective-permute-done.6.refs_1_), channel_id=1, source_target_pairs={{0,2},{2,0},{4,6},{6,4},{8,10},{10,8},{12,14},{14,12},{16,18},{18,... | collective-permute-start | bytes 1572872 | tf_op jit(solution)/shard_map/ppermute | solution.py:381
  21.8 1.3 %collective-permute-start.4 = (bf16[256,768]{1,0:T(8,128)(2,1)S(1)}, bf16[256,768]{1,0:T(8,128)(2,1)S(1)}, u32[]{:S(2)}, u32[]{:S(2)}) collective-permute-start(bf16[256,768]{1,0:T(8,128)(2,1)S(1)} %collective-permute-done.2.refs_11_), channel_id=1, source_target_pairs={{0,8},{2,10},{8,16},{10,18},{16,24},{18,26},{24,28},{26,30},{28,20... | collective-permute-start | bytes 1179656 | tf_op jit(solution)/shard_map/ppermute | solution.py:314
  23.2 6.1 %collective-permute-done.4.refs_10_ = bf16[256,768]{1,0:T(8,128)(2,1)S(1)} collective-permute-done((bf16[256,768]{1,0:T(8,128)(2,1)S(1)}, bf16[256,768]{1,0:T(8,128)(2,1)S(1)}, u32[]{:S(2)}, u32[]{:S(2)}) %collective-permute-start.4) | collective-permute-done | bytes 393248 | tf_op jit(solution)/shard_map/ppermute | solution.py:314
  31.9 4.1 %collective-permute-done.10.refs_9_ = bf16[128,768]{1,0:T(8,128)(2,1)S(1)} collective-permute-done((bf16[128,768]{1,0:T(8,128)(2,1)S(1)}, bf16[128,768]{1,0:T(8,128)(2,1)S(1)}, u32[]{:S(2)}, u32[]{:S(2)}) %collective-permute-start.10) | collective-permute-done | bytes 196640 | tf_op jit(solution)/shard_map/ppermute | solution.py:320
  37.1 5.9 %collective-permute-start.12 = (f32[128,256]{1,0:T(8,128)S(1)}, f32[128,256]{1,0:T(8,128)S(1)}, u32[]{:S(2)}, u32[]{:S(2)}) collective-permute-start(f32[128,256]{1,0:T(8,128)S(1)} %get-tuple-element.131), channel_id=1, source_target_pairs={{0,2},{2,0},{4,6},{6,4},{8,10},{10,8},{12,14},{14,12},{16,18},{18,... | collective-permute-start | bytes 393224 | tf_op jit(solution)/shard_map/ppermute | solution.py:407
  44.9 3.7 %all-to-all-start = ((bf16[8,128,256]{2,1,0:T(8,128)(2,1)}), bf16[8,128,256]{2,1,0:T(8,128)(2,1)S(1)}, u32[]{:S(2)}, u32[]{:S(2)}) async-start(bf16[8,128,256]{2,1,0:T(8,128)(2,1)} %bitcast.1), calls=%async_computation | async-start | bytes 1048576 | tf_op jit(solution)/shard_map/all_to_all | solution.py:419
  48.6 1.5 %collective-permute-start.13 = (bf16[512,256]{1,0:T(8,128)(2,1)S(1)}, bf16[512,256]{1,0:T(8,128)(2,1)S(1)}, u32[]{:S(2)}, u32[]{:S(2)}) collective-permute-start(bf16[512,256]{1,0:T(8,128)(2,1)S(1)} %copy-done.2), channel_id=1, source_target_pairs={{0,8},{2,10},{8,16},{10,18},{16,24},{18,26},{24,28},{26,30},{28,20... | collective-permute-start | bytes 786440 | tf_op jit(solution)/shard_map/ppermute | solution.py:314
  51.3 11.2 %collective-permute-done.13.refs_1_ = bf16[512,256]{1,0:T(8,128)(2,1)S(1)} collective-permute-done((bf16[512,256]{1,0:T(8,128)(2,1)S(1)}, bf16[512,256]{1,0:T(8,128)(2,1)S(1)}, u32[]{:S(2)}, u32[]{:S(2)}) %collective-permute-start.13) | collective-permute-done | bytes 262176 | tf_op jit(solution)/shard_map/ppermute | solution.py:314
  62.5 1.6 %collective-permute-done.14.refs_3_ = bf16[512,256]{1,0:T(8,128)(2,1)S(1)} collective-permute-done((bf16[512,256]{1,0:T(8,128)(2,1)S(1)}, bf16[512,256]{1,0:T(8,128)(2,1)S(1)}, u32[]{:S(2)}, u32[]{:S(2)}) %collective-permute-start.14) | collective-permute-done | bytes 262176 | tf_op jit(solution)/shard_map/ppermute | solution.py:315
  64.1 4.3 %collective-permute-start.15 = (bf16[512,256]{1,0:T(8,128)(2,1)S(1)}, bf16[512,256]{1,0:T(8,128)(2,1)S(1)}, u32[]{:S(2)}, u32[]{:S(2)}) collective-permute-start(bf16[512,256]{1,0:T(8,128)(2,1)S(1)} %collective-permute-done.13.refs_1_), channel_id=1, source_target_pairs={{0,8},{2,10},{8,16},{10,18},{16,24},{18,26},{24,28},{26,30},{28,20... | collective-permute-start | bytes 786440 | tf_op jit(solution)/shard_map/ppermute | solution.py:314
  68.4 4.1 %collective-permute-done.15.refs_0_ = bf16[512,256]{1,0:T(8,128)(2,1)S(1)} collective-permute-done((bf16[512,256]{1,0:T(8,128)(2,1)S(1)}, bf16[512,256]{1,0:T(8,128)(2,1)S(1)}, u32[]{:S(2)}, u32[]{:S(2)}) %collective-permute-start.15) | collective-permute-done | bytes 262176 | tf_op jit(solution)/shard_map/ppermute | solution.py:314
  72.5 1.9 %collective-permute-done.16.refs_4_ = bf16[512,256]{1,0:T(8,128)(2,1)S(1)} collective-permute-done((bf16[512,256]{1,0:T(8,128)(2,1)S(1)}, bf16[512,256]{1,0:T(8,128)(2,1)S(1)}, u32[]{:S(2)}, u32[]{:S(2)}) %collective-permute-start.16) | collective-permute-done | bytes 262176 | tf_op jit(solution)/shard_map/ppermute | solution.py:315
  74.4 2.5 %attend.1.mine_ref = f32[256,640]{1,0:T(8,128)S(1)} custom-call(f32[256,512]{1,0:T(8,128)S(1)} %get-tuple-element.124.mine_ref, f32[256,512]{1,0:T(8,128)S(1)} %collective-permute-done.11.theirs_ref, f32[256,128]{1,0:T(8,128)S(1)} %get-tuple-element.125.cosine_ref, f32[256,128]{1,0:T(8,128)S(1)} %get-tuple-element.126.sine_ref, ...), custom_call_target="tpu_custom_call" | custom-call | tf_op jit(solution)/shard_map/attend/pallas_call | solution.py:426
  76.9 2.8 %collective-permute-start.17 = (f32[256,640]{1,0:T(8,128)S(1)}, f32[256,640]{1,0:T(8,128)S(1)}, u32[]{:S(2)}, u32[]{:S(2)}) collective-permute-start(f32[256,640]{1,0:T(8,128)S(1)} %attend.1.mine_ref), channel_id=1, source_target_pairs={{0,2},{2,0},{4,6},{6,4},{8,10},{10,8},{12,14},{14,12},{16,18},{18,... | collective-permute-start | bytes 1966088 | tf_op jit(solution)/shard_map/ppermute | solution.py:444
  79.7 1.5 %collective-permute-start.19 = (bf16[512,256]{1,0:T(8,128)(2,1)S(1)}, bf16[512,256]{1,0:T(8,128)(2,1)S(1)}, u32[]{:S(2)}, u32[]{:S(2)}) collective-permute-start(bf16[512,256]{1,0:T(8,128)(2,1)S(1)} %collective-permute-done.15.refs_0_), channel_id=1, source_target_pairs={{0,8},{2,10},{8,16},{10,18},{16,24},{18,26},{24,28},{26,30},{28,20... | collective-permute-start | bytes 786440 | tf_op jit(solution)/shard_map/ppermute | solution.py:314
  83.8 3.7 %collective-permute-done.18.refs_0_ = bf16[512,256]{1,0:T(8,128)(2,1)S(1)} collective-permute-done((bf16[512,256]{1,0:T(8,128)(2,1)S(1)}, bf16[512,256]{1,0:T(8,128)(2,1)S(1)}, u32[]{:S(2)}, u32[]{:S(2)}) %collective-permute-start.18) | collective-permute-done | bytes 262176 | tf_op jit(solution)/shard_map/ppermute | solution.py:315
  89.1 1.4 %collective-permute-start.23 = (bf16[5,64,256]{2,1,0:T(8,128)(2,1)S(1)}, bf16[5,64,256]{2,1,0:T(8,128)(2,1)S(1)}, u32[]{:S(2)}, u32[]{:S(2)}) collective-permute-start(bf16[5,64,256]{2,1,0:T(8,128)(2,1)S(1)} %get-tuple-element.165), channel_id=1, source_target_pairs={{0,2},{1,3},{2,0},{3,1},{4,6},{5,7},{6,4},{7,5},{8,10},{9,11},{10,... | collective-permute-start | bytes 491528 | tf_op jit(solution)/shard_map/ppermute | solution.py:466
  95.0 2.6 %collective-permute-start.26 = (bf16[3,64,256]{2,1,0:T(8,128)(2,1)S(1)}, bf16[3,64,256]{2,1,0:T(8,128)(2,1)S(1)}, u32[]{:S(2)}, u32[]{:S(2)}) collective-permute-start(bf16[3,64,256]{2,1,0:T(8,128)(2,1)S(1)} %get-tuple-element.169), channel_id=1, source_target_pairs={{0,2},{1,3},{2,0},{3,1},{4,6},{5,7},{6,4},{7,5},{8,10},{9,11},{10,... | collective-permute-start | bytes 294920 | tf_op jit(solution)/shard_map/ppermute | solution.py:466
  98.6 3.6 %collective-permute-done.27.refs_7_ = bf16[3,64,256]{2,1,0:T(8,128)(2,1)S(1)} collective-permute-done((bf16[3,64,256]{2,1,0:T(8,128)(2,1)S(1)}, bf16[3,64,256]{2,1,0:T(8,128)(2,1)S(1)}, u32[]{:S(2)}, u32[]{:S(2)}) %collective-permute-start.27) | collective-permute-done | bytes 98336 | tf_op jit(solution)/shard_map/ppermute | solution.py:466
  (60 shorter events, 24.7 us)
Async XLA Ops:
  0.0 11.1 %collective-permute-start = (bf16[256,768]{1,0:T(8,128)(2,1)}, bf16[256,768]{1,0:T(8,128)(2,1)S(1)}, u32[]{:S(2)}, u32[]{:S(2)}) collective-permute-start(bf16[256,768]{1,0:T(8,128)(2,1)} %refs_4_), channel_id=1, source_target_pairs={{0,8},{2,10},{8,16},{10,18},{16,24},{18,26},{24,28},{26,30},{28,20... | collective-permute-start | bytes 1179656 | tf_op jit(solution)/shard_map/ppermute | solution.py:314
  2.1 9.9 %collective-permute-start.1 = (bf16[256,768]{1,0:T(8,128)(2,1)}, bf16[256,768]{1,0:T(8,128)(2,1)S(1)}, u32[]{:S(2)}, u32[]{:S(2)}) collective-permute-start(bf16[256,768]{1,0:T(8,128)(2,1)} %refs_4_), channel_id=1, source_target_pairs={{8,0},{10,2},{16,8},{18,10},{24,16},{26,18},{28,24},{30,26},{20,28... | collective-permute-start | bytes 1179656 | tf_op jit(solution)/shard_map/ppermute | solution.py:315
  4.2 12.5 %collective-permute-start.6 = (bf16[2,8,64,256]{3,2,1,0:T(8,128)(2,1)S(1)}, bf16[2,8,64,256]{3,2,1,0:T(8,128)(2,1)S(1)}, u32[]{:S(2)}, u32[]{:S(2)}) collective-permute-start(bf16[2,8,64,256]{3,2,1,0:T(8,128)(2,1)S(1)} %norm.1.refs_0_), channel_id=1, source_target_pairs={{0,1},{1,0},{2,3},{3,2},{4,5},{5,4},{6,7},{7,6},{8,9},{9,8},{10,11... | collective-permute-start | bytes 1572872 | tf_op jit(solution)/shard_map/ppermute | solution.py:376
  12.0 8.7 %collective-permute-start.2 = (bf16[256,768]{1,0:T(8,128)(2,1)S(1)}, bf16[256,768]{1,0:T(8,128)(2,1)S(1)}, u32[]{:S(2)}, u32[]{:S(2)}) collective-permute-start(bf16[256,768]{1,0:T(8,128)(2,1)S(1)} %collective-permute-done.refs_12_), channel_id=1, source_target_pairs={{0,8},{2,10},{8,16},{10,18},{16,24},{18,26},{24,28},{26,30},{28,20... | collective-permute-start | bytes 1179656 | tf_op jit(solution)/shard_map/ppermute | solution.py:314
  13.3 8.5 %collective-permute-start.3 = (bf16[256,768]{1,0:T(8,128)(2,1)S(1)}, bf16[256,768]{1,0:T(8,128)(2,1)S(1)}, u32[]{:S(2)}, u32[]{:S(2)}) collective-permute-start(bf16[256,768]{1,0:T(8,128)(2,1)S(1)} %collective-permute-done.1.refs_5_), channel_id=1, source_target_pairs={{8,0},{10,2},{16,8},{18,10},{24,16},{26,18},{28,24},{30,26},{20,28... | collective-permute-start | bytes 1179656 | tf_op jit(solution)/shard_map/ppermute | solution.py:315
  13.5 9.8 %collective-permute-start.7 = (bf16[2,8,64,256]{3,2,1,0:T(8,128)(2,1)S(1)}, bf16[2,8,64,256]{3,2,1,0:T(8,128)(2,1)S(1)}, u32[]{:S(2)}, u32[]{:S(2)}) collective-permute-start(bf16[2,8,64,256]{3,2,1,0:T(8,128)(2,1)S(1)} %norm.1.refs_0_), channel_id=1, source_target_pairs={{0,2},{2,0},{4,6},{6,4},{8,10},{10,8},{12,14},{14,12},{16,18},{18,... | collective-permute-start | bytes 1572872 | tf_op jit(solution)/shard_map/ppermute | solution.py:381
  16.7 6.5 %collective-permute-start.8 = (bf16[2,8,64,256]{3,2,1,0:T(8,128)(2,1)S(1)}, bf16[2,8,64,256]{3,2,1,0:T(8,128)(2,1)S(1)}, u32[]{:S(2)}, u32[]{:S(2)}) collective-permute-start(bf16[2,8,64,256]{3,2,1,0:T(8,128)(2,1)S(1)} %collective-permute-done.6.refs_1_), channel_id=1, source_target_pairs={{0,2},{2,0},{4,6},{6,4},{8,10},{10,8},{12,14},{14,12},{16,18},{18,... | collective-permute-start | bytes 1572872 | tf_op jit(solution)/shard_map/ppermute | solution.py:381
  21.8 7.5 %collective-permute-start.4 = (bf16[256,768]{1,0:T(8,128)(2,1)S(1)}, bf16[256,768]{1,0:T(8,128)(2,1)S(1)}, u32[]{:S(2)}, u32[]{:S(2)}) collective-permute-start(bf16[256,768]{1,0:T(8,128)(2,1)S(1)} %collective-permute-done.2.refs_11_), channel_id=1, source_target_pairs={{0,8},{2,10},{8,16},{10,18},{16,24},{18,26},{24,28},{26,30},{28,20... | collective-permute-start | bytes 1179656 | tf_op jit(solution)/shard_map/ppermute | solution.py:314
  23.1 7.3 %collective-permute-start.5 = (bf16[256,768]{1,0:T(8,128)(2,1)S(1)}, bf16[256,768]{1,0:T(8,128)(2,1)S(1)}, u32[]{:S(2)}, u32[]{:S(2)}) collective-permute-start(bf16[256,768]{1,0:T(8,128)(2,1)S(1)} %collective-permute-done.3.refs_6_), channel_id=1, source_target_pairs={{8,0},{10,2},{16,8},{18,10},{24,16},{26,18},{28,24},{30,26},{20,28... | collective-permute-start | bytes 1179656 | tf_op jit(solution)/shard_map/ppermute | solution.py:315
  30.4 5.6 %collective-permute-start.10 = (bf16[128,768]{1,0:T(8,128)(2,1)S(1)}, bf16[128,768]{1,0:T(8,128)(2,1)S(1)}, u32[]{:S(2)}, u32[]{:S(2)}) collective-permute-start(bf16[128,768]{1,0:T(8,128)(2,1)S(1)} %slice.13), channel_id=1, source_target_pairs={{8,0},{10,2},{16,8},{18,10},{24,16},{26,18},{28,24},{30,26},{20,28... | collective-permute-start | bytes 589832 | tf_op jit(solution)/shard_map/ppermute | solution.py:320
  30.6 5.4 %collective-permute-start.9 = (bf16[128,768]{1,0:T(8,128)(2,1)S(1)}, bf16[128,768]{1,0:T(8,128)(2,1)S(1)}, u32[]{:S(2)}, u32[]{:S(2)}) collective-permute-start(bf16[128,768]{1,0:T(8,128)(2,1)S(1)} %slice.12), channel_id=1, source_target_pairs={{0,8},{2,10},{8,16},{10,18},{16,24},{18,26},{24,28},{26,30},{28,20... | collective-permute-start | bytes 589832 | tf_op jit(solution)/shard_map/ppermute | solution.py:319
  37.1 6.8 %collective-permute-start.12 = (f32[128,256]{1,0:T(8,128)S(1)}, f32[128,256]{1,0:T(8,128)S(1)}, u32[]{:S(2)}, u32[]{:S(2)}) collective-permute-start(f32[128,256]{1,0:T(8,128)S(1)} %get-tuple-element.131), channel_id=1, source_target_pairs={{0,2},{2,0},{4,6},{6,4},{8,10},{10,8},{12,14},{14,12},{16,18},{18,... | collective-permute-start | bytes 393224 | tf_op jit(solution)/shard_map/ppermute | solution.py:407
  44.9 29.5 %all-to-all-start = ((bf16[8,128,256]{2,1,0:T(8,128)(2,1)}), bf16[8,128,256]{2,1,0:T(8,128)(2,1)S(1)}, u32[]{:S(2)}, u32[]{:S(2)}) async-start(bf16[8,128,256]{2,1,0:T(8,128)(2,1)} %bitcast.1), calls=%async_computation | async-start | bytes 1048576 | tf_op jit(solution)/shard_map/all_to_all | solution.py:419
  48.6 14.0 %collective-permute-start.13 = (bf16[512,256]{1,0:T(8,128)(2,1)S(1)}, bf16[512,256]{1,0:T(8,128)(2,1)S(1)}, u32[]{:S(2)}, u32[]{:S(2)}) collective-permute-start(bf16[512,256]{1,0:T(8,128)(2,1)S(1)} %copy-done.2), channel_id=1, source_target_pairs={{0,8},{2,10},{8,16},{10,18},{16,24},{18,26},{24,28},{26,30},{28,20... | collective-permute-start | bytes 786440 | tf_op jit(solution)/shard_map/ppermute | solution.py:314
  50.0 14.1 %collective-permute-start.14 = (bf16[512,256]{1,0:T(8,128)(2,1)S(1)}, bf16[512,256]{1,0:T(8,128)(2,1)S(1)}, u32[]{:S(2)}, u32[]{:S(2)}) collective-permute-start(bf16[512,256]{1,0:T(8,128)(2,1)S(1)} %copy-done.2), channel_id=1, source_target_pairs={{8,0},{10,2},{16,8},{18,10},{24,16},{26,18},{28,24},{30,26},{20,28... | collective-permute-start | bytes 786440 | tf_op jit(solution)/shard_map/ppermute | solution.py:315
  50.1 24.3 %collective-permute-start.11 = (f32[256,512]{1,0:T(8,128)S(1)}, f32[256,512]{1,0:T(8,128)S(1)}, u32[]{:S(2)}, u32[]{:S(2)}) collective-permute-start(f32[256,512]{1,0:T(8,128)S(1)} %get-tuple-element.124.mine_ref), channel_id=1, source_target_pairs={{0,2},{2,0},{4,6},{6,4},{8,10},{10,8},{12,14},{14,12},{16,18},{18,... | collective-permute-start | bytes 1572872 | tf_op jit(solution)/shard_map/ppermute | solution.py:408
  64.1 8.4 %collective-permute-start.15 = (bf16[512,256]{1,0:T(8,128)(2,1)S(1)}, bf16[512,256]{1,0:T(8,128)(2,1)S(1)}, u32[]{:S(2)}, u32[]{:S(2)}) collective-permute-start(bf16[512,256]{1,0:T(8,128)(2,1)S(1)} %collective-permute-done.13.refs_1_), channel_id=1, source_target_pairs={{0,8},{2,10},{8,16},{10,18},{16,24},{18,26},{24,28},{26,30},{28,20... | collective-permute-start | bytes 786440 | tf_op jit(solution)/shard_map/ppermute | solution.py:314
  68.4 6.0 %collective-permute-start.16 = (bf16[512,256]{1,0:T(8,128)(2,1)S(1)}, bf16[512,256]{1,0:T(8,128)(2,1)S(1)}, u32[]{:S(2)}, u32[]{:S(2)}) collective-permute-start(bf16[512,256]{1,0:T(8,128)(2,1)S(1)} %collective-permute-done.14.refs_3_), channel_id=1, source_target_pairs={{8,0},{10,2},{16,8},{18,10},{24,16},{26,18},{28,24},{30,26},{20,28... | collective-permute-start | bytes 786440 | tf_op jit(solution)/shard_map/ppermute | solution.py:315
  79.7 7.9 %collective-permute-start.18 = (bf16[512,256]{1,0:T(8,128)(2,1)S(1)}, bf16[512,256]{1,0:T(8,128)(2,1)S(1)}, u32[]{:S(2)}, u32[]{:S(2)}) collective-permute-start(bf16[512,256]{1,0:T(8,128)(2,1)S(1)} %collective-permute-done.16.refs_4_), channel_id=1, source_target_pairs={{8,0},{10,2},{16,8},{18,10},{24,16},{26,18},{28,24},{30,26},{20,28... | collective-permute-start | bytes 786440 | tf_op jit(solution)/shard_map/ppermute | solution.py:315
  79.7 7.9 %collective-permute-start.19 = (bf16[512,256]{1,0:T(8,128)(2,1)S(1)}, bf16[512,256]{1,0:T(8,128)(2,1)S(1)}, u32[]{:S(2)}, u32[]{:S(2)}) collective-permute-start(bf16[512,256]{1,0:T(8,128)(2,1)S(1)} %collective-permute-done.15.refs_0_), channel_id=1, source_target_pairs={{0,8},{2,10},{8,16},{10,18},{16,24},{18,26},{24,28},{26,30},{28,20... | collective-permute-start | bytes 786440 | tf_op jit(solution)/shard_map/ppermute | solution.py:314
  82.6 15.0 %collective-permute-start.22 = (bf16[5,64,256]{2,1,0:T(8,128)(2,1)S(1)}, bf16[5,64,256]{2,1,0:T(8,128)(2,1)S(1)}, u32[]{:S(2)}, u32[]{:S(2)}) collective-permute-start(bf16[5,64,256]{2,1,0:T(8,128)(2,1)S(1)} %get-tuple-element.164), channel_id=1, source_target_pairs={{0,1},{1,0},{2,3},{3,2},{4,5},{5,4},{6,7},{7,6},{8,9},{9,8},{10,11... | collective-permute-start | bytes 491528 | tf_op jit(solution)/shard_map/ppermute | solution.py:466
  89.1 8.6 %collective-permute-start.23 = (bf16[5,64,256]{2,1,0:T(8,128)(2,1)S(1)}, bf16[5,64,256]{2,1,0:T(8,128)(2,1)S(1)}, u32[]{:S(2)}, u32[]{:S(2)}) collective-permute-start(bf16[5,64,256]{2,1,0:T(8,128)(2,1)S(1)} %get-tuple-element.165), channel_id=1, source_target_pairs={{0,2},{1,3},{2,0},{3,1},{4,6},{5,7},{6,4},{7,5},{8,10},{9,11},{10,... | collective-permute-start | bytes 491528 | tf_op jit(solution)/shard_map/ppermute | solution.py:466
  90.6 7.2 %collective-permute-start.24 = (bf16[5,64,256]{2,1,0:T(8,128)(2,1)S(1)}, bf16[5,64,256]{2,1,0:T(8,128)(2,1)S(1)}, u32[]{:S(2)}, u32[]{:S(2)}) collective-permute-start(bf16[5,64,256]{2,1,0:T(8,128)(2,1)S(1)} %get-tuple-element.166), channel_id=1, source_target_pairs={{0,3},{1,2},{2,1},{3,0},{4,7},{5,6},{6,5},{7,4},{8,11},{9,10},{10,... | collective-permute-start | bytes 491528 | tf_op jit(solution)/shard_map/ppermute | solution.py:466
  97.6 4.5 %collective-permute-start.27 = (bf16[3,64,256]{2,1,0:T(8,128)(2,1)S(1)}, bf16[3,64,256]{2,1,0:T(8,128)(2,1)S(1)}, u32[]{:S(2)}, u32[]{:S(2)}) collective-permute-start(bf16[3,64,256]{2,1,0:T(8,128)(2,1)S(1)} %get-tuple-element.170), channel_id=1, source_target_pairs={{0,3},{1,2},{2,1},{3,0},{4,7},{5,6},{6,5},{7,4},{8,11},{9,10},{10,... | collective-permute-start | bytes 294920 | tf_op jit(solution)/shard_map/ppermute | solution.py:466
  (12 other events, 86.1 us)

commit v24 on v17

--- a/solution.py
+++ b/solution.py
@@ -469,7 +469,8 @@
             compiler_params=compute_params(),
             name=name,
         )(mixed, stats, sent, their_stats, *flat)
-        parts = ordered(parts)
+        held = ordered((*parts, *out_ring.middle))
+        parts, out_ring.middle = held[: len(parts)], held[len(parts) :]
         arrived = []
         for e in range(2):
             for d in range(n_tensor):

time: 96.6 us -> 101 us (1.046)
  waiting for transfers between devices: 39.8 us -> 42.9 us
  starting transfers between devices: 43 us -> 44.1 us
    ppermute x6, waiting for transfers between devices: 2.45 us -> 8.47 us  [output(): part = lax.ppermute(part, ('context', 'tensor'), member(e, -d))]
    ppermute x1, starting transfers between devices: 0.08 us -> 3.05 us  [per_device(): their_stats = lax.ppermute(stats, 'context', sibling)]
    ppermute x6, starting transfers between devices: 9.6 us -> 7.66 us  [output(): part = lax.ppermute(part, ('context', 'tensor'), member(e, -d))]
    ppermute x2, waiting for transfers between devices: 5.72 us -> 4.05 us  [step(): lax.ppermute(down[half:], 'context', back)]
    ppermute x1, waiting for transfers between devices: 1.26 us -> 0.01 us  [per_device(): their_stats = lax.ppermute(stats, 'context', sibling)]
  transfers between devices with their start and end apart: 30 -> 30, of which waited for: 15 -> 14; matrix products, arithmetic and copies ran while one was open for 0% -> 0% of each run, Pallas kernels for 6% -> 8%
where the time goes in v24:
time: 101 us; the launch traced here: 100 us
  starting transfers between devices  44.1 us (44%)
  waiting for transfers between devices  42.9 us (42%)
  Pallas kernels  10.2 us (10%)
  local copies, waits for them, and re-layouts  2.71 us (3%)
    ppermute x6, waiting for transfers between devices, step(): self.up.append(lax.ppermute(up, 'context', ahead))  23 us
    ppermute x6, starting transfers between devices, step(): self.up.append(lax.ppermute(up, 'context', ahead))  10.4 us
    ppermute x6, waiting for transfers between devices, output(): part = lax.ppermute(part, ('context', 'tensor'), member(e, -d))  8.47 us
    ppermute x6, starting transfers between devices, output(): part = lax.ppermute(part, ('context', 'tensor'), member(e, -d))  7.66 us
    ppermute x1, starting transfers between devices, per_device(): theirs = lax.ppermute(theirs, 'context', sibling)  5.86 us
    ppermute x6, waiting for transfers between devices, step(): self.down.append(lax.ppermute(down, 'context', back))  5.62 us
    ppermute x2, starting transfers between devices, per_device(): normed += [lax.ppermute(rows, 'context', sibling) for rows in normed]  4.3 us
    ppermute x2, waiting for transfers between devices, step(): lax.ppermute(down[half:], 'context', back)  4.05 us
  transfers between devices with their start and end apart: 30, of which 14 were waited for; matrix products, arithmetic and copies ran while one was open for 0% of the time, Pallas kernels for 8%

profile of v24, /device:TPU:1, one launch (start us, length us, event | category | flops | bytes accessed | tf_op | source)
XLA Modules:
  0.0 100.0 jit_solution(13574135573854078613)
XLA Ops:
  0.0 2.1 %collective-permute-start = (bf16[256,768]{1,0:T(8,128)(2,1)}, bf16[256,768]{1,0:T(8,128)(2,1)S(1)}, u32[]{:S(2)}, u32[]{:S(2)}) collective-permute-start(bf16[256,768]{1,0:T(8,128)(2,1)} %refs_4_), channel_id=1, source_target_pairs={{0,8},{2,10},{8,16},{10,18},{16,24},{18,26},{24,28},{26,30},{28,20... | collective-permute-start | bytes 1179656 | tf_op jit(solution)/shard_map/ppermute | solution.py:319
  4.2 1.4 %collective-permute-start.6 = (bf16[2,8,64,256]{3,2,1,0:T(8,128)(2,1)S(1)}, bf16[2,8,64,256]{3,2,1,0:T(8,128)(2,1)S(1)}, u32[]{:S(2)}, u32[]{:S(2)}) collective-permute-start(bf16[2,8,64,256]{3,2,1,0:T(8,128)(2,1)S(1)} %norm.1.refs_0_), channel_id=1, source_target_pairs={{0,1},{1,0},{2,3},{3,2},{4,5},{5,4},{6,7},{7,6},{8,9},{9,8},{10,11... | collective-permute-start | bytes 1572872 | tf_op jit(solution)/shard_map/ppermute | solution.py:381
  5.6 5.5 %collective-permute-done.refs_12_ = bf16[256,768]{1,0:T(8,128)(2,1)S(1)} collective-permute-done((bf16[256,768]{1,0:T(8,128)(2,1)}, bf16[256,768]{1,0:T(8,128)(2,1)S(1)}, u32[]{:S(2)}, u32[]{:S(2)}) %collective-permute-start) | collective-permute-done | bytes 393248 | tf_op jit(solution)/shard_map/ppermute | solution.py:319
  12.0 1.3 %collective-permute-start.2 = (bf16[256,768]{1,0:T(8,128)(2,1)S(1)}, bf16[256,768]{1,0:T(8,128)(2,1)S(1)}, u32[]{:S(2)}, u32[]{:S(2)}) collective-permute-start(bf16[256,768]{1,0:T(8,128)(2,1)S(1)} %collective-permute-done.refs_12_), channel_id=1, source_target_pairs={{0,8},{2,10},{8,16},{10,18},{16,24},{18,26},{24,28},{26,30},{28,20... | collective-permute-start | bytes 1179656 | tf_op jit(solution)/shard_map/ppermute | solution.py:319
  13.5 2.4 %collective-permute-start.7 = (bf16[2,8,64,256]{3,2,1,0:T(8,128)(2,1)S(1)}, bf16[2,8,64,256]{3,2,1,0:T(8,128)(2,1)S(1)}, u32[]{:S(2)}, u32[]{:S(2)}) collective-permute-start(bf16[2,8,64,256]{3,2,1,0:T(8,128)(2,1)S(1)} %norm.1.refs_0_), channel_id=1, source_target_pairs={{0,2},{2,0},{4,6},{6,4},{8,10},{10,8},{12,14},{14,12},{16,18},{18,... | collective-permute-start | bytes 1572872 | tf_op jit(solution)/shard_map/ppermute | solution.py:386
  16.7 1.9 %collective-permute-start.8 = (bf16[2,8,64,256]{3,2,1,0:T(8,128)(2,1)S(1)}, bf16[2,8,64,256]{3,2,1,0:T(8,128)(2,1)S(1)}, u32[]{:S(2)}, u32[]{:S(2)}) collective-permute-start(bf16[2,8,64,256]{3,2,1,0:T(8,128)(2,1)S(1)} %collective-permute-done.6.refs_1_), channel_id=1, source_target_pairs={{0,2},{2,0},{4,6},{6,4},{8,10},{10,8},{12,14},{14,12},{16,18},{18,... | collective-permute-start | bytes 1572872 | tf_op jit(solution)/shard_map/ppermute | solution.py:386
  23.2 6.1 %collective-permute-done.4.refs_10_ = bf16[256,768]{1,0:T(8,128)(2,1)S(1)} collective-permute-done((bf16[256,768]{1,0:T(8,128)(2,1)S(1)}, bf16[256,768]{1,0:T(8,128)(2,1)S(1)}, u32[]{:S(2)}, u32[]{:S(2)}) %collective-permute-start.4) | collective-permute-done | bytes 393248 | tf_op jit(solution)/shard_map/ppermute | solution.py:319
  33.4 2.6 %collective-permute-done.10.refs_9_ = bf16[128,768]{1,0:T(8,128)(2,1)S(1)} collective-permute-done((bf16[128,768]{1,0:T(8,128)(2,1)S(1)}, bf16[128,768]{1,0:T(8,128)(2,1)S(1)}, u32[]{:S(2)}, u32[]{:S(2)}) %collective-permute-start.10) | collective-permute-done | bytes 196640 | tf_op jit(solution)/shard_map/ppermute | solution.py:325
  37.1 5.9 %collective-permute-start.12 = (f32[128,256]{1,0:T(8,128)S(1)}, f32[128,256]{1,0:T(8,128)S(1)}, u32[]{:S(2)}, u32[]{:S(2)}) collective-permute-start(f32[128,256]{1,0:T(8,128)S(1)} %get-tuple-element.137), channel_id=1, source_target_pairs={{0,2},{2,0},{4,6},{6,4},{8,10},{10,8},{12,14},{14,12},{16,18},{18,... | collective-permute-start | bytes 393224 | tf_op jit(solution)/shard_map/ppermute | solution.py:412
  44.9 3.6 %all-to-all-start = ((bf16[8,128,256]{2,1,0:T(8,128)(2,1)}), bf16[8,128,256]{2,1,0:T(8,128)(2,1)S(1)}, u32[]{:S(2)}, u32[]{:S(2)}) async-start(bf16[8,128,256]{2,1,0:T(8,128)(2,1)} %bitcast.1), calls=%async_computation | async-start | bytes 1048576 | tf_op jit(solution)/shard_map/all_to_all | solution.py:425
  48.4 1.7 %collective-permute-start.11 = (f32[256,512]{1,0:T(8,128)S(1)}, f32[256,512]{1,0:T(8,128)S(1)}, u32[]{:S(2)}, u32[]{:S(2)}) collective-permute-start(f32[256,512]{1,0:T(8,128)S(1)} %get-tuple-element.130.mine_ref), channel_id=1, source_target_pairs={{0,2},{2,0},{4,6},{6,4},{8,10},{10,8},{12,14},{14,12},{16,18},{18,... | collective-permute-start | bytes 1572872 | tf_op jit(solution)/shard_map/ppermute | solution.py:413
  50.1 1.6 %collective-permute-start.15 = (bf16[512,256]{1,0:T(8,128)(2,1)S(1)}, bf16[512,256]{1,0:T(8,128)(2,1)S(1)}, u32[]{:S(2)}, u32[]{:S(2)}) collective-permute-start(bf16[512,256]{1,0:T(8,128)(2,1)S(1)} %collective-permute-done.13.refs_2_), channel_id=1, source_target_pairs={{0,8},{2,10},{8,16},{10,18},{16,24},{18,26},{24,28},{26,30},{28,20... | collective-permute-start | bytes 786440 | tf_op jit(solution)/shard_map/ppermute | solution.py:319
  51.7 10.5 %collective-permute-done.15.refs_1_ = bf16[512,256]{1,0:T(8,128)(2,1)S(1)} collective-permute-done((bf16[512,256]{1,0:T(8,128)(2,1)S(1)}, bf16[512,256]{1,0:T(8,128)(2,1)S(1)}, u32[]{:S(2)}, u32[]{:S(2)}) %collective-permute-start.15) | collective-permute-done | bytes 262176 | tf_op jit(solution)/shard_map/ppermute | solution.py:319
  62.2 2.7 %collective-permute-done.16.refs_5_ = bf16[512,256]{1,0:T(8,128)(2,1)} collective-permute-done((bf16[512,256]{1,0:T(8,128)(2,1)S(1)}, bf16[512,256]{1,0:T(8,128)(2,1)}, u32[]{:S(2)}, u32[]{:S(2)}) %collective-permute-start.16) | collective-permute-done | bytes 262176 | tf_op jit(solution)/shard_map/ppermute | solution.py:320
  64.9 2.9 %collective-permute-start.19 = (bf16[512,256]{1,0:T(8,128)(2,1)S(1)}, bf16[512,256]{1,0:T(8,128)(2,1)S(1)}, u32[]{:S(2)}, u32[]{:S(2)}) collective-permute-start(bf16[512,256]{1,0:T(8,128)(2,1)S(1)} %collective-permute-done.15.refs_1_), channel_id=1, source_target_pairs={{0,8},{2,10},{8,16},{10,18},{16,24},{18,26},{24,28},{26,30},{28,20... | collective-permute-start | bytes 786440 | tf_op jit(solution)/shard_map/ppermute | solution.py:319
  68.7 2.5 %attend.1 = (f32[256,512]{1,0:T(8,128)S(1)}, bf16[256,512]{1,0:T(8,128)(2,1)S(1)}, f32[256,128]{1,0:T(8,128)S(1)}) custom-call(f32[256,512]{1,0:T(8,128)S(1)} %get-tuple-element.130.mine_ref, f32[256,512]{1,0:T(8,128)S(1)} %collective-permute-done.11.theirs_ref, f32[256,128]{1,0:T(8,128)S(1)} %get-tuple-element.131.cosine_ref, ...), custom_call_target="tpu_custom_call" | custom-call | tf_op jit(solution)/shard_map/attend/pallas_call | solution.py:431
  71.2 2.5 %collective-permute-start.17 = (bf16[256,512]{1,0:T(8,128)(2,1)S(1)}, bf16[256,512]{1,0:T(8,128)(2,1)S(1)}, u32[]{:S(2)}, u32[]{:S(2)}) collective-permute-start(bf16[256,512]{1,0:T(8,128)(2,1)S(1)} %get-tuple-element.156), channel_id=1, source_target_pairs={{0,2},{2,0},{4,6},{6,4},{8,10},{10,8},{12,14},{14,12},{16,18},{18,... | collective-permute-start | bytes 786440 | tf_op jit(solution)/shard_map/ppermute | solution.py:453
  73.7 3.0 %collective-permute-start.18 = (f32[256,128]{1,0:T(8,128)S(1)}, f32[256,128]{1,0:T(8,128)S(1)}, u32[]{:S(2)}, u32[]{:S(2)}) collective-permute-start(f32[256,128]{1,0:T(8,128)S(1)} %get-tuple-element.155.stats_ref), channel_id=1, source_target_pairs={{0,2},{2,0},{4,6},{6,4},{8,10},{10,8},{12,14},{14,12},{16,18},{18,... | collective-permute-start | bytes 393224 | tf_op jit(solution)/shard_map/ppermute | solution.py:454
  76.9 1.5 %collective-permute-start.21 = (bf16[256,256]{1,0:T(8,128)(2,1)S(1)}, bf16[256,256]{1,0:T(8,128)(2,1)S(1)}, u32[]{:S(2)}, u32[]{:S(2)}) collective-permute-start(bf16[256,256]{1,0:T(8,128)(2,1)S(1)} %slice.14), channel_id=1, source_target_pairs={{0,8},{2,10},{8,16},{10,18},{16,24},{18,26},{24,28},{26,30},{28,20... | collective-permute-start | bytes 393224 | tf_op jit(solution)/shard_map/ppermute | solution.py:324
  78.3 2.2 %output_near.1 = (bf16[7,64,256]{2,1,0:T(8,128)(2,1)S(1)}, bf16[7,64,256]{2,1,0:T(8,128)(2,1)S(1)}, bf16[7,64,256]{2,1,0:T(8,128)(2,1)S(1)}, bf16[7,64,256]{2,1,0:T(8,128)(2,1)S(1)}) custom-call(f32[256,512]{1,0:T(8,128)S(1)} %get-tuple-element.151.mine_ref, f32[256,128]{1,0:T(8,128)S(1)} %get-tuple-element.155.stats_ref, ...), custom_call_target="tpu_custom_call" | custom-call | tf_op jit(solution)/shard_map/output_near/pallas_call | solution.py:463
  80.6 1.4 %collective-permute-done.22.refs_1_ = bf16[256,256]{1,0:T(8,128)(2,1)S(1)} collective-permute-done((bf16[256,256]{1,0:T(8,128)(2,1)S(1)}, bf16[256,256]{1,0:T(8,128)(2,1)S(1)}, u32[]{:S(2)}, u32[]{:S(2)}) %collective-permute-start.22) | collective-permute-done | bytes 131104 | tf_op jit(solution)/shard_map/ppermute | solution.py:325
  87.3 6.3 %collective-permute-done.26.refs_5_ = bf16[1,64,256]{2,1,0:T(8,128)(2,1)S(1)} collective-permute-done((bf16[1,64,256]{2,1,0:T(8,128)(2,1)S(1)}, bf16[1,64,256]{2,1,0:T(8,128)(2,1)S(1)}, u32[]{:S(2)}, u32[]{:S(2)}) %collective-permute-start.26) | collective-permute-done | bytes 32800 | tf_op jit(solution)/shard_map/ppermute | solution.py:479
  93.6 3.1 %collective-permute-start.28 = (bf16[1,64,256]{2,1,0:T(8,128)(2,1)S(1)}, bf16[1,64,256]{2,1,0:T(8,128)(2,1)S(1)}, u32[]{:S(2)}, u32[]{:S(2)}) collective-permute-start(bf16[1,64,256]{2,1,0:T(8,128)(2,1)S(1)} %get-tuple-element.182), channel_id=1, source_target_pairs={{0,3},{1,2},{2,1},{3,0},{4,7},{5,6},{6,5},{7,4},{8,11},{9,10},{10,... | collective-permute-start | bytes 98312 | tf_op jit(solution)/shard_map/ppermute | solution.py:479
  96.7 2.2 %collective-permute-done.28.refs_7_ = bf16[1,64,256]{2,1,0:T(8,128)(2,1)S(1)} collective-permute-done((bf16[1,64,256]{2,1,0:T(8,128)(2,1)S(1)}, bf16[1,64,256]{2,1,0:T(8,128)(2,1)S(1)}, u32[]{:S(2)}, u32[]{:S(2)}) %collective-permute-start.28) | collective-permute-done | bytes 32800 | tf_op jit(solution)/shard_map/ppermute | solution.py:479
  (66 shorter events, 23.0 us)
Async XLA Ops:
  0.0 11.1 %collective-permute-start = (bf16[256,768]{1,0:T(8,128)(2,1)}, bf16[256,768]{1,0:T(8,128)(2,1)S(1)}, u32[]{:S(2)}, u32[]{:S(2)}) collective-permute-start(bf16[256,768]{1,0:T(8,128)(2,1)} %refs_4_), channel_id=1, source_target_pairs={{0,8},{2,10},{8,16},{10,18},{16,24},{18,26},{24,28},{26,30},{28,20... | collective-permute-start | bytes 1179656 | tf_op jit(solution)/shard_map/ppermute | solution.py:319
  2.1 9.9 %collective-permute-start.1 = (bf16[256,768]{1,0:T(8,128)(2,1)}, bf16[256,768]{1,0:T(8,128)(2,1)S(1)}, u32[]{:S(2)}, u32[]{:S(2)}) collective-permute-start(bf16[256,768]{1,0:T(8,128)(2,1)} %refs_4_), channel_id=1, source_target_pairs={{8,0},{10,2},{16,8},{18,10},{24,16},{26,18},{28,24},{30,26},{20,28... | collective-permute-start | bytes 1179656 | tf_op jit(solution)/shard_map/ppermute | solution.py:320
  4.2 12.5 %collective-permute-start.6 = (bf16[2,8,64,256]{3,2,1,0:T(8,128)(2,1)S(1)}, bf16[2,8,64,256]{3,2,1,0:T(8,128)(2,1)S(1)}, u32[]{:S(2)}, u32[]{:S(2)}) collective-permute-start(bf16[2,8,64,256]{3,2,1,0:T(8,128)(2,1)S(1)} %norm.1.refs_0_), channel_id=1, source_target_pairs={{0,1},{1,0},{2,3},{3,2},{4,5},{5,4},{6,7},{7,6},{8,9},{9,8},{10,11... | collective-permute-start | bytes 1572872 | tf_op jit(solution)/shard_map/ppermute | solution.py:381
  12.0 8.7 %collective-permute-start.2 = (bf16[256,768]{1,0:T(8,128)(2,1)S(1)}, bf16[256,768]{1,0:T(8,128)(2,1)S(1)}, u32[]{:S(2)}, u32[]{:S(2)}) collective-permute-start(bf16[256,768]{1,0:T(8,128)(2,1)S(1)} %collective-permute-done.refs_12_), channel_id=1, source_target_pairs={{0,8},{2,10},{8,16},{10,18},{16,24},{18,26},{24,28},{26,30},{28,20... | collective-permute-start | bytes 1179656 | tf_op jit(solution)/shard_map/ppermute | solution.py:319
  13.3 8.5 %collective-permute-start.3 = (bf16[256,768]{1,0:T(8,128)(2,1)S(1)}, bf16[256,768]{1,0:T(8,128)(2,1)S(1)}, u32[]{:S(2)}, u32[]{:S(2)}) collective-permute-start(bf16[256,768]{1,0:T(8,128)(2,1)S(1)} %collective-permute-done.1.refs_5_), channel_id=1, source_target_pairs={{8,0},{10,2},{16,8},{18,10},{24,16},{26,18},{28,24},{30,26},{20,28... | collective-permute-start | bytes 1179656 | tf_op jit(solution)/shard_map/ppermute | solution.py:320
  13.5 9.8 %collective-permute-start.7 = (bf16[2,8,64,256]{3,2,1,0:T(8,128)(2,1)S(1)}, bf16[2,8,64,256]{3,2,1,0:T(8,128)(2,1)S(1)}, u32[]{:S(2)}, u32[]{:S(2)}) collective-permute-start(bf16[2,8,64,256]{3,2,1,0:T(8,128)(2,1)S(1)} %norm.1.refs_0_), channel_id=1, source_target_pairs={{0,2},{2,0},{4,6},{6,4},{8,10},{10,8},{12,14},{14,12},{16,18},{18,... | collective-permute-start | bytes 1572872 | tf_op jit(solution)/shard_map/ppermute | solution.py:386
  16.7 6.5 %collective-permute-start.8 = (bf16[2,8,64,256]{3,2,1,0:T(8,128)(2,1)S(1)}, bf16[2,8,64,256]{3,2,1,0:T(8,128)(2,1)S(1)}, u32[]{:S(2)}, u32[]{:S(2)}) collective-permute-start(bf16[2,8,64,256]{3,2,1,0:T(8,128)(2,1)S(1)} %collective-permute-done.6.refs_1_), channel_id=1, source_target_pairs={{0,2},{2,0},{4,6},{6,4},{8,10},{10,8},{12,14},{14,12},{16,18},{18,... | collective-permute-start | bytes 1572872 | tf_op jit(solution)/shard_map/ppermute | solution.py:386
  21.8 7.5 %collective-permute-start.4 = (bf16[256,768]{1,0:T(8,128)(2,1)S(1)}, bf16[256,768]{1,0:T(8,128)(2,1)S(1)}, u32[]{:S(2)}, u32[]{:S(2)}) collective-permute-start(bf16[256,768]{1,0:T(8,128)(2,1)S(1)} %collective-permute-done.2.refs_11_), channel_id=1, source_target_pairs={{0,8},{2,10},{8,16},{10,18},{16,24},{18,26},{24,28},{26,30},{28,20... | collective-permute-start | bytes 1179656 | tf_op jit(solution)/shard_map/ppermute | solution.py:319
  23.1 7.3 %collective-permute-start.5 = (bf16[256,768]{1,0:T(8,128)(2,1)S(1)}, bf16[256,768]{1,0:T(8,128)(2,1)S(1)}, u32[]{:S(2)}, u32[]{:S(2)}) collective-permute-start(bf16[256,768]{1,0:T(8,128)(2,1)S(1)} %collective-permute-done.3.refs_6_), channel_id=1, source_target_pairs={{8,0},{10,2},{16,8},{18,10},{24,16},{26,18},{28,24},{30,26},{20,28... | collective-permute-start | bytes 1179656 | tf_op jit(solution)/shard_map/ppermute | solution.py:320
  31.9 11.1 %collective-permute-start.13 = (bf16[512,256]{1,0:T(8,128)(2,1)S(1)}, bf16[512,256]{1,0:T(8,128)(2,1)S(1)}, u32[]{:S(2)}, u32[]{:S(2)}) collective-permute-start(bf16[512,256]{1,0:T(8,128)(2,1)S(1)} %copy-done.2), channel_id=1, source_target_pairs={{0,8},{2,10},{8,16},{10,18},{16,24},{18,26},{24,28},{26,30},{28,20... | collective-permute-start | bytes 786440 | tf_op jit(solution)/shard_map/ppermute | solution.py:319
  33.1 9.8 %collective-permute-start.14 = (bf16[512,256]{1,0:T(8,128)(2,1)S(1)}, bf16[512,256]{1,0:T(8,128)(2,1)S(1)}, u32[]{:S(2)}, u32[]{:S(2)}) collective-permute-start(bf16[512,256]{1,0:T(8,128)(2,1)S(1)} %copy-done.2), channel_id=1, source_target_pairs={{8,0},{10,2},{16,8},{18,10},{24,16},{26,18},{28,24},{30,26},{20,28... | collective-permute-start | bytes 786440 | tf_op jit(solution)/shard_map/ppermute | solution.py:320
  37.1 6.8 %collective-permute-start.12 = (f32[128,256]{1,0:T(8,128)S(1)}, f32[128,256]{1,0:T(8,128)S(1)}, u32[]{:S(2)}, u32[]{:S(2)}) collective-permute-start(f32[128,256]{1,0:T(8,128)S(1)} %get-tuple-element.137), channel_id=1, source_target_pairs={{0,2},{2,0},{4,6},{6,4},{8,10},{10,8},{12,14},{14,12},{16,18},{18,... | collective-permute-start | bytes 393224 | tf_op jit(solution)/shard_map/ppermute | solution.py:412
  44.9 22.9 %all-to-all-start = ((bf16[8,128,256]{2,1,0:T(8,128)(2,1)}), bf16[8,128,256]{2,1,0:T(8,128)(2,1)S(1)}, u32[]{:S(2)}, u32[]{:S(2)}) async-start(bf16[8,128,256]{2,1,0:T(8,128)(2,1)} %bitcast.1), calls=%async_computation | async-start | bytes 1048576 | tf_op jit(solution)/shard_map/all_to_all | solution.py:425
  48.4 19.3 %collective-permute-start.11 = (f32[256,512]{1,0:T(8,128)S(1)}, f32[256,512]{1,0:T(8,128)S(1)}, u32[]{:S(2)}, u32[]{:S(2)}) collective-permute-start(f32[256,512]{1,0:T(8,128)S(1)} %get-tuple-element.130.mine_ref), channel_id=1, source_target_pairs={{0,2},{2,0},{4,6},{6,4},{8,10},{10,8},{12,14},{14,12},{16,18},{18,... | collective-permute-start | bytes 1572872 | tf_op jit(solution)/shard_map/ppermute | solution.py:413
  50.1 12.1 %collective-permute-start.15 = (bf16[512,256]{1,0:T(8,128)(2,1)S(1)}, bf16[512,256]{1,0:T(8,128)(2,1)S(1)}, u32[]{:S(2)}, u32[]{:S(2)}) collective-permute-start(bf16[512,256]{1,0:T(8,128)(2,1)S(1)} %collective-permute-done.13.refs_2_), channel_id=1, source_target_pairs={{0,8},{2,10},{8,16},{10,18},{16,24},{18,26},{24,28},{26,30},{28,20... | collective-permute-start | bytes 786440 | tf_op jit(solution)/shard_map/ppermute | solution.py:319
  51.7 13.2 %collective-permute-start.16 = (bf16[512,256]{1,0:T(8,128)(2,1)S(1)}, bf16[512,256]{1,0:T(8,128)(2,1)}, u32[]{:S(2)}, u32[]{:S(2)}) collective-permute-start(bf16[512,256]{1,0:T(8,128)(2,1)S(1)} %collective-permute-done.14.refs_4_), channel_id=1, source_target_pairs={{8,0},{10,2},{16,8},{18,10},{24,16},{26,18},{28,24},{30,26},{20,28... | collective-permute-start | bytes 786440 | tf_op jit(solution)/shard_map/ppermute | solution.py:320
  64.9 8.9 %collective-permute-start.19 = (bf16[512,256]{1,0:T(8,128)(2,1)S(1)}, bf16[512,256]{1,0:T(8,128)(2,1)S(1)}, u32[]{:S(2)}, u32[]{:S(2)}) collective-permute-start(bf16[512,256]{1,0:T(8,128)(2,1)S(1)} %collective-permute-done.15.refs_1_), channel_id=1, source_target_pairs={{0,8},{2,10},{8,16},{10,18},{16,24},{18,26},{24,28},{26,30},{28,20... | collective-permute-start | bytes 786440 | tf_op jit(solution)/shard_map/ppermute | solution.py:319
  67.8 6.0 %collective-permute-start.20 = (bf16[512,256]{1,0:T(8,128)(2,1)}, bf16[512,256]{1,0:T(8,128)(2,1)S(1)}, u32[]{:S(2)}, u32[]{:S(2)}) collective-permute-start(bf16[512,256]{1,0:T(8,128)(2,1)} %collective-permute-done.16.refs_5_), channel_id=1, source_target_pairs={{8,0},{10,2},{16,8},{18,10},{24,16},{26,18},{28,24},{30,26},{20,28... | collective-permute-start | bytes 786440 | tf_op jit(solution)/shard_map/ppermute | solution.py:320
  71.2 7.1 %collective-permute-start.17 = (bf16[256,512]{1,0:T(8,128)(2,1)S(1)}, bf16[256,512]{1,0:T(8,128)(2,1)S(1)}, u32[]{:S(2)}, u32[]{:S(2)}) collective-permute-start(bf16[256,512]{1,0:T(8,128)(2,1)S(1)} %get-tuple-element.156), channel_id=1, source_target_pairs={{0,2},{2,0},{4,6},{6,4},{8,10},{10,8},{12,14},{14,12},{16,18},{18,... | collective-permute-start | bytes 786440 | tf_op jit(solution)/shard_map/ppermute | solution.py:453
  82.0 16.9 %collective-permute-start.23 = (bf16[7,64,256]{2,1,0:T(8,128)(2,1)S(1)}, bf16[7,64,256]{2,1,0:T(8,128)(2,1)S(1)}, u32[]{:S(2)}, u32[]{:S(2)}) collective-permute-start(bf16[7,64,256]{2,1,0:T(8,128)(2,1)S(1)} %get-tuple-element.176), channel_id=1, source_target_pairs={{0,1},{1,0},{2,3},{3,2},{4,5},{5,4},{6,7},{7,6},{8,9},{9,8},{10,11... | collective-permute-start | bytes 688136 | tf_op jit(solution)/shard_map/ppermute | solution.py:479
  83.2 15.7 %collective-permute-start.24 = (bf16[7,64,256]{2,1,0:T(8,128)(2,1)S(1)}, bf16[7,64,256]{2,1,0:T(8,128)(2,1)S(1)}, u32[]{:S(2)}, u32[]{:S(2)}) collective-permute-start(bf16[7,64,256]{2,1,0:T(8,128)(2,1)S(1)} %get-tuple-element.177), channel_id=1, source_target_pairs={{0,2},{1,3},{2,0},{3,1},{4,6},{5,7},{6,4},{7,5},{8,10},{9,11},{10,... | collective-permute-start | bytes 688136 | tf_op jit(solution)/shard_map/ppermute | solution.py:479
  84.3 14.6 %collective-permute-start.25 = (bf16[7,64,256]{2,1,0:T(8,128)(2,1)S(1)}, bf16[7,64,256]{2,1,0:T(8,128)(2,1)S(1)}, u32[]{:S(2)}, u32[]{:S(2)}) collective-permute-start(bf16[7,64,256]{2,1,0:T(8,128)(2,1)S(1)} %get-tuple-element.178), channel_id=1, source_target_pairs={{0,3},{1,2},{2,1},{3,0},{4,7},{5,6},{6,5},{7,4},{8,11},{9,10},{10,... | collective-permute-start | bytes 688136 | tf_op jit(solution)/shard_map/ppermute | solution.py:479
  85.3 8.3 %collective-permute-start.26 = (bf16[1,64,256]{2,1,0:T(8,128)(2,1)S(1)}, bf16[1,64,256]{2,1,0:T(8,128)(2,1)S(1)}, u32[]{:S(2)}, u32[]{:S(2)}) collective-permute-start(bf16[1,64,256]{2,1,0:T(8,128)(2,1)S(1)} %get-tuple-element.180), channel_id=1, source_target_pairs={{0,1},{1,0},{2,3},{3,2},{4,5},{5,4},{6,7},{7,6},{8,9},{9,8},{10,11... | collective-permute-start | bytes 98312 | tf_op jit(solution)/shard_map/ppermute | solution.py:479
  86.5 10.2 %collective-permute-start.27 = (bf16[1,64,256]{2,1,0:T(8,128)(2,1)S(1)}, bf16[1,64,256]{2,1,0:T(8,128)(2,1)S(1)}, u32[]{:S(2)}, u32[]{:S(2)}) collective-permute-start(bf16[1,64,256]{2,1,0:T(8,128)(2,1)S(1)} %get-tuple-element.181), channel_id=1, source_target_pairs={{0,2},{1,3},{2,0},{3,1},{4,6},{5,7},{6,4},{7,5},{8,10},{9,11},{10,... | collective-permute-start | bytes 98312 | tf_op jit(solution)/shard_map/ppermute | solution.py:479
  (15 other events, 106.2 us)

commit v25 on v23

--- a/solution.py
+++ b/solution.py
@@ -406,6 +406,7 @@
     )(*ordered((*normed, *blocks)))
     theirs = lax.ppermute(theirs, "context", sibling)
     queries_theirs = lax.ppermute(queries, "context", sibling)
+    out_ring.step()
     mine, theirs = ordered((mine, theirs))
     kv = pl.pallas_call(
         functools.partial(keys_kernel, chips),
@@ -419,7 +420,6 @@
     kv = lax.all_to_all(
         kv, "context", split_axis=0, concat_axis=0, axis_index_groups=same_core, tiled=True
     )
-    out_ring.step()
     out_ring.step()
     (kv,) = ordered((kv,))
 

time: 104 us -> 96.2 us (0.925)
  waiting for transfers between devices: 49.6 us -> 43.7 us
  starting transfers between devices: 42.5 us -> 40.9 us
    ppermute x6, waiting for transfers between devices: 27.8 us -> 23.8 us  [step(): self.up.append(lax.ppermute(up, 'context', ahead))]
    ppermute x6, starting transfers between devices: 12 us -> 10.3 us  [step(): self.up.append(lax.ppermute(up, 'context', ahead))]
    ppermute x2, waiting for transfers between devices: 4.32 us -> 2.83 us  [step(): lax.ppermute(down[half:], 'context', back)]
    ppermute x1, starting transfers between devices: 2.77 us -> 1.67 us  [per_device(): mixed_theirs = lax.ppermute(mixed, 'context', sibling)]
  transfers between devices with their start and end apart: 29 -> 29, of which waited for: 19 -> 17; matrix products, arithmetic and copies ran while one was open for 0% -> 0% of each run, Pallas kernels for 4% -> 5%
where the time goes in v25:
time: 96.2 us; the launch traced here: 95.8 us
  waiting for transfers between devices  43.7 us (45%)
  starting transfers between devices  40.9 us (43%)
  Pallas kernels  9.22 us (10%)
  local copies, waits for them, and re-layouts  1.81 us (2%)
    ppermute x6, waiting for transfers between devices, step(): self.up.append(lax.ppermute(up, 'context', ahead))  23.8 us
    ppermute x6, starting transfers between devices, step(): self.up.append(lax.ppermute(up, 'context', ahead))  10.3 us
    ppermute x6, waiting for transfers between devices, step(): self.down.append(lax.ppermute(down, 'context', back))  9.81 us
    ppermute x6, starting transfers between devices, output(): part = lax.ppermute(part, ('context', 'tensor'), member(e, -d))  7.8 us
    ppermute x1, starting transfers between devices, per_device(): theirs = lax.ppermute(theirs, 'context', sibling)  5.86 us
    ppermute x6, waiting for transfers between devices, output(): part = lax.ppermute(part, ('context', 'tensor'), member(e, -d))  4.39 us
    ppermute x2, starting transfers between devices, per_device(): normed += [lax.ppermute(rows, 'context', sibling) for rows in normed]  4.3 us
    all_to_all x1, starting transfers between devices, per_device(): lax.all_to_all(kv, 'context', split_axis=0, concat_axis=0, axis_index_gro...  3.56 us
  transfers between devices with their start and end apart: 29, of which 17 were waited for; matrix products, arithmetic and copies ran while one was open for 0% of the time, Pallas kernels for 5%

profile of v25, /device:TPU:1, one launch (start us, length us, event | category | flops | bytes accessed | tf_op | source)
XLA Modules:
  0.0 95.8 jit_solution(17929728602725080203)
XLA Ops:
  0.0 2.1 %collective-permute-start = (bf16[256,768]{1,0:T(8,128)(2,1)}, bf16[256,768]{1,0:T(8,128)(2,1)S(1)}, u32[]{:S(2)}, u32[]{:S(2)}) collective-permute-start(bf16[256,768]{1,0:T(8,128)(2,1)} %refs_4_), channel_id=1, source_target_pairs={{0,8},{2,10},{8,16},{10,18},{16,24},{18,26},{24,28},{26,30},{28,20... | collective-permute-start | bytes 1179656 | tf_op jit(solution)/shard_map/ppermute | solution.py:314
  4.2 1.4 %collective-permute-start.6 = (bf16[2,8,64,256]{3,2,1,0:T(8,128)(2,1)S(1)}, bf16[2,8,64,256]{3,2,1,0:T(8,128)(2,1)S(1)}, u32[]{:S(2)}, u32[]{:S(2)}) collective-permute-start(bf16[2,8,64,256]{3,2,1,0:T(8,128)(2,1)S(1)} %norm.1.refs_0_), channel_id=1, source_target_pairs={{0,1},{1,0},{2,3},{3,2},{4,5},{5,4},{6,7},{7,6},{8,9},{9,8},{10,11... | collective-permute-start | bytes 1572872 | tf_op jit(solution)/shard_map/ppermute | solution.py:376
  5.6 5.5 %collective-permute-done.refs_12_ = bf16[256,768]{1,0:T(8,128)(2,1)S(1)} collective-permute-done((bf16[256,768]{1,0:T(8,128)(2,1)}, bf16[256,768]{1,0:T(8,128)(2,1)S(1)}, u32[]{:S(2)}, u32[]{:S(2)}) %collective-permute-start) | collective-permute-done | bytes 393248 | tf_op jit(solution)/shard_map/ppermute | solution.py:314
  12.0 1.3 %collective-permute-start.2 = (bf16[256,768]{1,0:T(8,128)(2,1)S(1)}, bf16[256,768]{1,0:T(8,128)(2,1)S(1)}, u32[]{:S(2)}, u32[]{:S(2)}) collective-permute-start(bf16[256,768]{1,0:T(8,128)(2,1)S(1)} %collective-permute-done.refs_12_), channel_id=1, source_target_pairs={{0,8},{2,10},{8,16},{10,18},{16,24},{18,26},{24,28},{26,30},{28,20... | collective-permute-start | bytes 1179656 | tf_op jit(solution)/shard_map/ppermute | solution.py:314
  13.5 2.4 %collective-permute-start.7 = (bf16[2,8,64,256]{3,2,1,0:T(8,128)(2,1)S(1)}, bf16[2,8,64,256]{3,2,1,0:T(8,128)(2,1)S(1)}, u32[]{:S(2)}, u32[]{:S(2)}) collective-permute-start(bf16[2,8,64,256]{3,2,1,0:T(8,128)(2,1)S(1)} %norm.1.refs_0_), channel_id=1, source_target_pairs={{0,2},{2,0},{4,6},{6,4},{8,10},{10,8},{12,14},{14,12},{16,18},{18,... | collective-permute-start | bytes 1572872 | tf_op jit(solution)/shard_map/ppermute | solution.py:381
  16.7 1.9 %collective-permute-start.8 = (bf16[2,8,64,256]{3,2,1,0:T(8,128)(2,1)S(1)}, bf16[2,8,64,256]{3,2,1,0:T(8,128)(2,1)S(1)}, u32[]{:S(2)}, u32[]{:S(2)}) collective-permute-start(bf16[2,8,64,256]{3,2,1,0:T(8,128)(2,1)S(1)} %collective-permute-done.6.refs_1_), channel_id=1, source_target_pairs={{0,2},{2,0},{4,6},{6,4},{8,10},{10,8},{12,14},{14,12},{16,18},{18,... | collective-permute-start | bytes 1572872 | tf_op jit(solution)/shard_map/ppermute | solution.py:381
  21.8 1.3 %collective-permute-start.4 = (bf16[256,768]{1,0:T(8,128)(2,1)S(1)}, bf16[256,768]{1,0:T(8,128)(2,1)S(1)}, u32[]{:S(2)}, u32[]{:S(2)}) collective-permute-start(bf16[256,768]{1,0:T(8,128)(2,1)S(1)} %collective-permute-done.2.refs_11_), channel_id=1, source_target_pairs={{0,8},{2,10},{8,16},{10,18},{16,24},{18,26},{24,28},{26,30},{28,20... | collective-permute-start | bytes 1179656 | tf_op jit(solution)/shard_map/ppermute | solution.py:314
  23.2 6.1 %collective-permute-done.4.refs_10_ = bf16[256,768]{1,0:T(8,128)(2,1)S(1)} collective-permute-done((bf16[256,768]{1,0:T(8,128)(2,1)S(1)}, bf16[256,768]{1,0:T(8,128)(2,1)S(1)}, u32[]{:S(2)}, u32[]{:S(2)}) %collective-permute-start.4) | collective-permute-done | bytes 393248 | tf_op jit(solution)/shard_map/ppermute | solution.py:314
  30.6 1.3 %collective-permute-start.9 = (bf16[128,768]{1,0:T(8,128)(2,1)S(1)}, bf16[128,768]{1,0:T(8,128)(2,1)S(1)}, u32[]{:S(2)}, u32[]{:S(2)}) collective-permute-start(bf16[128,768]{1,0:T(8,128)(2,1)S(1)} %slice.12), channel_id=1, source_target_pairs={{0,8},{2,10},{8,16},{10,18},{16,24},{18,26},{24,28},{26,30},{28,20... | collective-permute-start | bytes 589832 | tf_op jit(solution)/shard_map/ppermute | solution.py:319
  33.4 2.6 %collective-permute-done.10.refs_9_ = bf16[128,768]{1,0:T(8,128)(2,1)S(1)} collective-permute-done((bf16[128,768]{1,0:T(8,128)(2,1)S(1)}, bf16[128,768]{1,0:T(8,128)(2,1)S(1)}, u32[]{:S(2)}, u32[]{:S(2)}) %collective-permute-start.10) | collective-permute-done | bytes 196640 | tf_op jit(solution)/shard_map/ppermute | solution.py:320
  37.1 5.9 %collective-permute-start.12 = (f32[128,256]{1,0:T(8,128)S(1)}, f32[128,256]{1,0:T(8,128)S(1)}, u32[]{:S(2)}, u32[]{:S(2)}) collective-permute-start(f32[128,256]{1,0:T(8,128)S(1)} %get-tuple-element.131), channel_id=1, source_target_pairs={{0,2},{2,0},{4,6},{6,4},{8,10},{10,8},{12,14},{14,12},{16,18},{18,... | collective-permute-start | bytes 393224 | tf_op jit(solution)/shard_map/ppermute | solution.py:407
  44.9 3.6 %all-to-all-start = ((bf16[8,128,256]{2,1,0:T(8,128)(2,1)}), bf16[8,128,256]{2,1,0:T(8,128)(2,1)S(1)}, u32[]{:S(2)}, u32[]{:S(2)}) async-start(bf16[8,128,256]{2,1,0:T(8,128)(2,1)} %bitcast.1), calls=%async_computation | async-start | bytes 1048576 | tf_op jit(solution)/shard_map/all_to_all | solution.py:420
  48.4 1.7 %collective-permute-start.11 = (f32[256,512]{1,0:T(8,128)S(1)}, f32[256,512]{1,0:T(8,128)S(1)}, u32[]{:S(2)}, u32[]{:S(2)}) collective-permute-start(f32[256,512]{1,0:T(8,128)S(1)} %get-tuple-element.124.mine_ref), channel_id=1, source_target_pairs={{0,2},{2,0},{4,6},{6,4},{8,10},{10,8},{12,14},{14,12},{16,18},{18,... | collective-permute-start | bytes 1572872 | tf_op jit(solution)/shard_map/ppermute | solution.py:408
  50.1 1.6 %collective-permute-start.15 = (bf16[512,256]{1,0:T(8,128)(2,1)S(1)}, bf16[512,256]{1,0:T(8,128)(2,1)S(1)}, u32[]{:S(2)}, u32[]{:S(2)}) collective-permute-start(bf16[512,256]{1,0:T(8,128)(2,1)S(1)} %collective-permute-done.13.refs_1_), channel_id=1, source_target_pairs={{0,8},{2,10},{8,16},{10,18},{16,24},{18,26},{24,28},{26,30},{28,20... | collective-permute-start | bytes 786440 | tf_op jit(solution)/shard_map/ppermute | solution.py:314
  51.7 10.4 %collective-permute-done.15.refs_0_ = bf16[512,256]{1,0:T(8,128)(2,1)S(1)} collective-permute-done((bf16[512,256]{1,0:T(8,128)(2,1)S(1)}, bf16[512,256]{1,0:T(8,128)(2,1)S(1)}, u32[]{:S(2)}, u32[]{:S(2)}) %collective-permute-start.15) | collective-permute-done | bytes 262176 | tf_op jit(solution)/shard_map/ppermute | solution.py:314
  62.1 2.7 %collective-permute-done.16.refs_4_ = bf16[512,256]{1,0:T(8,128)(2,1)S(1)} collective-permute-done((bf16[512,256]{1,0:T(8,128)(2,1)S(1)}, bf16[512,256]{1,0:T(8,128)(2,1)S(1)}, u32[]{:S(2)}, u32[]{:S(2)}) %collective-permute-start.16) | collective-permute-done | bytes 262176 | tf_op jit(solution)/shard_map/ppermute | solution.py:315
  64.8 2.5 %attend.1.mine_ref = f32[256,640]{1,0:T(8,128)S(1)} custom-call(f32[256,512]{1,0:T(8,128)S(1)} %get-tuple-element.124.mine_ref, f32[256,512]{1,0:T(8,128)S(1)} %collective-permute-done.11.theirs_ref, f32[256,128]{1,0:T(8,128)S(1)} %get-tuple-element.125.cosine_ref, f32[256,128]{1,0:T(8,128)S(1)} %get-tuple-element.126.sine_ref, ...), custom_call_target="tpu_custom_call" | custom-call | tf_op jit(solution)/shard_map/attend/pallas_call | solution.py:426
  67.3 1.7 %collective-permute-start.17 = (f32[256,640]{1,0:T(8,128)S(1)}, f32[256,640]{1,0:T(8,128)S(1)}, u32[]{:S(2)}, u32[]{:S(2)}) collective-permute-start(f32[256,640]{1,0:T(8,128)S(1)} %attend.1.mine_ref), channel_id=1, source_target_pairs={{0,2},{2,0},{4,6},{6,4},{8,10},{10,8},{12,14},{14,12},{16,18},{18,... | collective-permute-start | bytes 1966088 | tf_op jit(solution)/shard_map/ppermute | solution.py:444
  69.6 2.8 %collective-permute-start.19 = (bf16[512,256]{1,0:T(8,128)(2,1)S(1)}, bf16[512,256]{1,0:T(8,128)(2,1)S(1)}, u32[]{:S(2)}, u32[]{:S(2)}) collective-permute-start(bf16[512,256]{1,0:T(8,128)(2,1)S(1)} %collective-permute-done.15.refs_0_), channel_id=1, source_target_pairs={{0,8},{2,10},{8,16},{10,18},{16,24},{18,26},{24,28},{26,30},{28,20... | collective-permute-start | bytes 786440 | tf_op jit(solution)/shard_map/ppermute | solution.py:314
  73.6 1.3 %collective-permute-start.22 = (bf16[5,64,256]{2,1,0:T(8,128)(2,1)S(1)}, bf16[5,64,256]{2,1,0:T(8,128)(2,1)S(1)}, u32[]{:S(2)}, u32[]{:S(2)}) collective-permute-start(bf16[5,64,256]{2,1,0:T(8,128)(2,1)S(1)} %get-tuple-element.164), channel_id=1, source_target_pairs={{0,1},{1,0},{2,3},{3,2},{4,5},{5,4},{6,7},{7,6},{8,9},{9,8},{10,11... | collective-permute-start | bytes 491528 | tf_op jit(solution)/shard_map/ppermute | solution.py:466
  74.8 4.2 %collective-permute-done.18.refs_0_ = bf16[512,256]{1,0:T(8,128)(2,1)S(1)} collective-permute-done((bf16[512,256]{1,0:T(8,128)(2,1)S(1)}, bf16[512,256]{1,0:T(8,128)(2,1)S(1)}, u32[]{:S(2)}, u32[]{:S(2)}) %collective-permute-start.18) | collective-permute-done | bytes 262176 | tf_op jit(solution)/shard_map/ppermute | solution.py:315
  81.5 1.4 %collective-permute-start.23 = (bf16[5,64,256]{2,1,0:T(8,128)(2,1)S(1)}, bf16[5,64,256]{2,1,0:T(8,128)(2,1)S(1)}, u32[]{:S(2)}, u32[]{:S(2)}) collective-permute-start(bf16[5,64,256]{2,1,0:T(8,128)(2,1)S(1)} %get-tuple-element.165), channel_id=1, source_target_pairs={{0,2},{1,3},{2,0},{3,1},{4,6},{5,7},{6,4},{7,5},{8,10},{9,11},{10,... | collective-permute-start | bytes 491528 | tf_op jit(solution)/shard_map/ppermute | solution.py:466
  87.6 2.6 %collective-permute-start.26 = (bf16[3,64,256]{2,1,0:T(8,128)(2,1)S(1)}, bf16[3,64,256]{2,1,0:T(8,128)(2,1)S(1)}, u32[]{:S(2)}, u32[]{:S(2)}) collective-permute-start(bf16[3,64,256]{2,1,0:T(8,128)(2,1)S(1)} %get-tuple-element.169), channel_id=1, source_target_pairs={{0,2},{1,3},{2,0},{3,1},{4,6},{5,7},{6,4},{7,5},{8,10},{9,11},{10,... | collective-permute-start | bytes 294920 | tf_op jit(solution)/shard_map/ppermute | solution.py:466
  91.1 3.6 %collective-permute-done.27.refs_7_ = bf16[3,64,256]{2,1,0:T(8,128)(2,1)S(1)} collective-permute-done((bf16[3,64,256]{2,1,0:T(8,128)(2,1)S(1)}, bf16[3,64,256]{2,1,0:T(8,128)(2,1)S(1)}, u32[]{:S(2)}, u32[]{:S(2)}) %collective-permute-start.27) | collective-permute-done | bytes 98336 | tf_op jit(solution)/shard_map/ppermute | solution.py:466
  (60 shorter events, 23.8 us)
Async XLA Ops:
  0.0 11.1 %collective-permute-start = (bf16[256,768]{1,0:T(8,128)(2,1)}, bf16[256,768]{1,0:T(8,128)(2,1)S(1)}, u32[]{:S(2)}, u32[]{:S(2)}) collective-permute-start(bf16[256,768]{1,0:T(8,128)(2,1)} %refs_4_), channel_id=1, source_target_pairs={{0,8},{2,10},{8,16},{10,18},{16,24},{18,26},{24,28},{26,30},{28,20... | collective-permute-start | bytes 1179656 | tf_op jit(solution)/shard_map/ppermute | solution.py:314
  2.1 9.9 %collective-permute-start.1 = (bf16[256,768]{1,0:T(8,128)(2,1)}, bf16[256,768]{1,0:T(8,128)(2,1)S(1)}, u32[]{:S(2)}, u32[]{:S(2)}) collective-permute-start(bf16[256,768]{1,0:T(8,128)(2,1)} %refs_4_), channel_id=1, source_target_pairs={{8,0},{10,2},{16,8},{18,10},{24,16},{26,18},{28,24},{30,26},{20,28... | collective-permute-start | bytes 1179656 | tf_op jit(solution)/shard_map/ppermute | solution.py:315
  4.2 12.5 %collective-permute-start.6 = (bf16[2,8,64,256]{3,2,1,0:T(8,128)(2,1)S(1)}, bf16[2,8,64,256]{3,2,1,0:T(8,128)(2,1)S(1)}, u32[]{:S(2)}, u32[]{:S(2)}) collective-permute-start(bf16[2,8,64,256]{3,2,1,0:T(8,128)(2,1)S(1)} %norm.1.refs_0_), channel_id=1, source_target_pairs={{0,1},{1,0},{2,3},{3,2},{4,5},{5,4},{6,7},{7,6},{8,9},{9,8},{10,11... | collective-permute-start | bytes 1572872 | tf_op jit(solution)/shard_map/ppermute | solution.py:376
  12.0 8.7 %collective-permute-start.2 = (bf16[256,768]{1,0:T(8,128)(2,1)S(1)}, bf16[256,768]{1,0:T(8,128)(2,1)S(1)}, u32[]{:S(2)}, u32[]{:S(2)}) collective-permute-start(bf16[256,768]{1,0:T(8,128)(2,1)S(1)} %collective-permute-done.refs_12_), channel_id=1, source_target_pairs={{0,8},{2,10},{8,16},{10,18},{16,24},{18,26},{24,28},{26,30},{28,20... | collective-permute-start | bytes 1179656 | tf_op jit(solution)/shard_map/ppermute | solution.py:314
  13.3 8.5 %collective-permute-start.3 = (bf16[256,768]{1,0:T(8,128)(2,1)S(1)}, bf16[256,768]{1,0:T(8,128)(2,1)S(1)}, u32[]{:S(2)}, u32[]{:S(2)}) collective-permute-start(bf16[256,768]{1,0:T(8,128)(2,1)S(1)} %collective-permute-done.1.refs_5_), channel_id=1, source_target_pairs={{8,0},{10,2},{16,8},{18,10},{24,16},{26,18},{28,24},{30,26},{20,28... | collective-permute-start | bytes 1179656 | tf_op jit(solution)/shard_map/ppermute | solution.py:315
  13.5 9.8 %collective-permute-start.7 = (bf16[2,8,64,256]{3,2,1,0:T(8,128)(2,1)S(1)}, bf16[2,8,64,256]{3,2,1,0:T(8,128)(2,1)S(1)}, u32[]{:S(2)}, u32[]{:S(2)}) collective-permute-start(bf16[2,8,64,256]{3,2,1,0:T(8,128)(2,1)S(1)} %norm.1.refs_0_), channel_id=1, source_target_pairs={{0,2},{2,0},{4,6},{6,4},{8,10},{10,8},{12,14},{14,12},{16,18},{18,... | collective-permute-start | bytes 1572872 | tf_op jit(solution)/shard_map/ppermute | solution.py:381
  16.7 6.5 %collective-permute-start.8 = (bf16[2,8,64,256]{3,2,1,0:T(8,128)(2,1)S(1)}, bf16[2,8,64,256]{3,2,1,0:T(8,128)(2,1)S(1)}, u32[]{:S(2)}, u32[]{:S(2)}) collective-permute-start(bf16[2,8,64,256]{3,2,1,0:T(8,128)(2,1)S(1)} %collective-permute-done.6.refs_1_), channel_id=1, source_target_pairs={{0,2},{2,0},{4,6},{6,4},{8,10},{10,8},{12,14},{14,12},{16,18},{18,... | collective-permute-start | bytes 1572872 | tf_op jit(solution)/shard_map/ppermute | solution.py:381
  21.8 7.5 %collective-permute-start.4 = (bf16[256,768]{1,0:T(8,128)(2,1)S(1)}, bf16[256,768]{1,0:T(8,128)(2,1)S(1)}, u32[]{:S(2)}, u32[]{:S(2)}) collective-permute-start(bf16[256,768]{1,0:T(8,128)(2,1)S(1)} %collective-permute-done.2.refs_11_), channel_id=1, source_target_pairs={{0,8},{2,10},{8,16},{10,18},{16,24},{18,26},{24,28},{26,30},{28,20... | collective-permute-start | bytes 1179656 | tf_op jit(solution)/shard_map/ppermute | solution.py:314
  23.1 7.3 %collective-permute-start.5 = (bf16[256,768]{1,0:T(8,128)(2,1)S(1)}, bf16[256,768]{1,0:T(8,128)(2,1)S(1)}, u32[]{:S(2)}, u32[]{:S(2)}) collective-permute-start(bf16[256,768]{1,0:T(8,128)(2,1)S(1)} %collective-permute-done.3.refs_6_), channel_id=1, source_target_pairs={{8,0},{10,2},{16,8},{18,10},{24,16},{26,18},{28,24},{30,26},{20,28... | collective-permute-start | bytes 1179656 | tf_op jit(solution)/shard_map/ppermute | solution.py:315
  30.4 5.6 %collective-permute-start.10 = (bf16[128,768]{1,0:T(8,128)(2,1)S(1)}, bf16[128,768]{1,0:T(8,128)(2,1)S(1)}, u32[]{:S(2)}, u32[]{:S(2)}) collective-permute-start(bf16[128,768]{1,0:T(8,128)(2,1)S(1)} %slice.13), channel_id=1, source_target_pairs={{8,0},{10,2},{16,8},{18,10},{24,16},{26,18},{28,24},{30,26},{20,28... | collective-permute-start | bytes 589832 | tf_op jit(solution)/shard_map/ppermute | solution.py:320
  30.6 5.4 %collective-permute-start.9 = (bf16[128,768]{1,0:T(8,128)(2,1)S(1)}, bf16[128,768]{1,0:T(8,128)(2,1)S(1)}, u32[]{:S(2)}, u32[]{:S(2)}) collective-permute-start(bf16[128,768]{1,0:T(8,128)(2,1)S(1)} %slice.12), channel_id=1, source_target_pairs={{0,8},{2,10},{8,16},{10,18},{16,24},{18,26},{24,28},{26,30},{28,20... | collective-permute-start | bytes 589832 | tf_op jit(solution)/shard_map/ppermute | solution.py:319
  31.9 11.1 %collective-permute-start.13 = (bf16[512,256]{1,0:T(8,128)(2,1)S(1)}, bf16[512,256]{1,0:T(8,128)(2,1)S(1)}, u32[]{:S(2)}, u32[]{:S(2)}) collective-permute-start(bf16[512,256]{1,0:T(8,128)(2,1)S(1)} %copy-done.2), channel_id=1, source_target_pairs={{0,8},{2,10},{8,16},{10,18},{16,24},{18,26},{24,28},{26,30},{28,20... | collective-permute-start | bytes 786440 | tf_op jit(solution)/shard_map/ppermute | solution.py:314
  33.1 9.8 %collective-permute-start.14 = (bf16[512,256]{1,0:T(8,128)(2,1)S(1)}, bf16[512,256]{1,0:T(8,128)(2,1)S(1)}, u32[]{:S(2)}, u32[]{:S(2)}) collective-permute-start(bf16[512,256]{1,0:T(8,128)(2,1)S(1)} %copy-done.2), channel_id=1, source_target_pairs={{8,0},{10,2},{16,8},{18,10},{24,16},{26,18},{28,24},{30,26},{20,28... | collective-permute-start | bytes 786440 | tf_op jit(solution)/shard_map/ppermute | solution.py:315
  37.1 6.8 %collective-permute-start.12 = (f32[128,256]{1,0:T(8,128)S(1)}, f32[128,256]{1,0:T(8,128)S(1)}, u32[]{:S(2)}, u32[]{:S(2)}) collective-permute-start(f32[128,256]{1,0:T(8,128)S(1)} %get-tuple-element.131), channel_id=1, source_target_pairs={{0,2},{2,0},{4,6},{6,4},{8,10},{10,8},{12,14},{14,12},{16,18},{18,... | collective-permute-start | bytes 393224 | tf_op jit(solution)/shard_map/ppermute | solution.py:407
  44.9 19.9 %all-to-all-start = ((bf16[8,128,256]{2,1,0:T(8,128)(2,1)}), bf16[8,128,256]{2,1,0:T(8,128)(2,1)S(1)}, u32[]{:S(2)}, u32[]{:S(2)}) async-start(bf16[8,128,256]{2,1,0:T(8,128)(2,1)} %bitcast.1), calls=%async_computation | async-start | bytes 1048576 | tf_op jit(solution)/shard_map/all_to_all | solution.py:420
  48.4 16.3 %collective-permute-start.11 = (f32[256,512]{1,0:T(8,128)S(1)}, f32[256,512]{1,0:T(8,128)S(1)}, u32[]{:S(2)}, u32[]{:S(2)}) collective-permute-start(f32[256,512]{1,0:T(8,128)S(1)} %get-tuple-element.124.mine_ref), channel_id=1, source_target_pairs={{0,2},{2,0},{4,6},{6,4},{8,10},{10,8},{12,14},{14,12},{16,18},{18,... | collective-permute-start | bytes 1572872 | tf_op jit(solution)/shard_map/ppermute | solution.py:408
  50.1 12.0 %collective-permute-start.15 = (bf16[512,256]{1,0:T(8,128)(2,1)S(1)}, bf16[512,256]{1,0:T(8,128)(2,1)S(1)}, u32[]{:S(2)}, u32[]{:S(2)}) collective-permute-start(bf16[512,256]{1,0:T(8,128)(2,1)S(1)} %collective-permute-done.13.refs_1_), channel_id=1, source_target_pairs={{0,8},{2,10},{8,16},{10,18},{16,24},{18,26},{24,28},{26,30},{28,20... | collective-permute-start | bytes 786440 | tf_op jit(solution)/shard_map/ppermute | solution.py:314
  51.7 13.1 %collective-permute-start.16 = (bf16[512,256]{1,0:T(8,128)(2,1)S(1)}, bf16[512,256]{1,0:T(8,128)(2,1)S(1)}, u32[]{:S(2)}, u32[]{:S(2)}) collective-permute-start(bf16[512,256]{1,0:T(8,128)(2,1)S(1)} %collective-permute-done.14.refs_3_), channel_id=1, source_target_pairs={{8,0},{10,2},{16,8},{18,10},{24,16},{26,18},{28,24},{30,26},{20,28... | collective-permute-start | bytes 786440 | tf_op jit(solution)/shard_map/ppermute | solution.py:315
  67.3 5.1 %collective-permute-start.17 = (f32[256,640]{1,0:T(8,128)S(1)}, f32[256,640]{1,0:T(8,128)S(1)}, u32[]{:S(2)}, u32[]{:S(2)}) collective-permute-start(f32[256,640]{1,0:T(8,128)S(1)} %attend.1.mine_ref), channel_id=1, source_target_pairs={{0,2},{2,0},{4,6},{6,4},{8,10},{10,8},{12,14},{14,12},{16,18},{18,... | collective-permute-start | bytes 1966088 | tf_op jit(solution)/shard_map/ppermute | solution.py:444
  69.0 10.0 %collective-permute-start.18 = (bf16[512,256]{1,0:T(8,128)(2,1)S(1)}, bf16[512,256]{1,0:T(8,128)(2,1)S(1)}, u32[]{:S(2)}, u32[]{:S(2)}) collective-permute-start(bf16[512,256]{1,0:T(8,128)(2,1)S(1)} %collective-permute-done.16.refs_4_), channel_id=1, source_target_pairs={{8,0},{10,2},{16,8},{18,10},{24,16},{26,18},{28,24},{30,26},{20,28... | collective-permute-start | bytes 786440 | tf_op jit(solution)/shard_map/ppermute | solution.py:315
  69.6 10.3 %collective-permute-start.19 = (bf16[512,256]{1,0:T(8,128)(2,1)S(1)}, bf16[512,256]{1,0:T(8,128)(2,1)S(1)}, u32[]{:S(2)}, u32[]{:S(2)}) collective-permute-start(bf16[512,256]{1,0:T(8,128)(2,1)S(1)} %collective-permute-done.15.refs_0_), channel_id=1, source_target_pairs={{0,8},{2,10},{8,16},{10,18},{16,24},{18,26},{24,28},{26,30},{28,20... | collective-permute-start | bytes 786440 | tf_op jit(solution)/shard_map/ppermute | solution.py:314
  73.6 16.6 %collective-permute-start.22 = (bf16[5,64,256]{2,1,0:T(8,128)(2,1)S(1)}, bf16[5,64,256]{2,1,0:T(8,128)(2,1)S(1)}, u32[]{:S(2)}, u32[]{:S(2)}) collective-permute-start(bf16[5,64,256]{2,1,0:T(8,128)(2,1)S(1)} %get-tuple-element.164), channel_id=1, source_target_pairs={{0,1},{1,0},{2,3},{3,2},{4,5},{5,4},{6,7},{7,6},{8,9},{9,8},{10,11... | collective-permute-start | bytes 491528 | tf_op jit(solution)/shard_map/ppermute | solution.py:466
  81.5 8.8 %collective-permute-start.23 = (bf16[5,64,256]{2,1,0:T(8,128)(2,1)S(1)}, bf16[5,64,256]{2,1,0:T(8,128)(2,1)S(1)}, u32[]{:S(2)}, u32[]{:S(2)}) collective-permute-start(bf16[5,64,256]{2,1,0:T(8,128)(2,1)S(1)} %get-tuple-element.165), channel_id=1, source_target_pairs={{0,2},{1,3},{2,0},{3,1},{4,6},{5,7},{6,4},{7,5},{8,10},{9,11},{10,... | collective-permute-start | bytes 491528 | tf_op jit(solution)/shard_map/ppermute | solution.py:466
  82.9 7.4 %collective-permute-start.24 = (bf16[5,64,256]{2,1,0:T(8,128)(2,1)S(1)}, bf16[5,64,256]{2,1,0:T(8,128)(2,1)S(1)}, u32[]{:S(2)}, u32[]{:S(2)}) collective-permute-start(bf16[5,64,256]{2,1,0:T(8,128)(2,1)S(1)} %get-tuple-element.166), channel_id=1, source_target_pairs={{0,3},{1,2},{2,1},{3,0},{4,7},{5,6},{6,5},{7,4},{8,11},{9,10},{10,... | collective-permute-start | bytes 491528 | tf_op jit(solution)/shard_map/ppermute | solution.py:466
  (12 other events, 84.0 us)
